TPU v7x, 32 devices: a whole 2x2x4 slice. The times are simulated.
32 devices in a mesh: groups: 2 (over y), dp: 8 (over z, x), tensor: 2 (over core).
Axes of the slice: x: 2, y: 2, z: 4, core: 2. Of those that a mesh axis runs over, the one named last changes fastest.
Arguments:
- prefix_kv: bfloat16 [128, 256, 512], P(('groups', 'dp'), None, 'tensor'), parts along dimension 0, may hold values from -4.5 to 4.5
- move_ids: int32 [8192], P(('groups', 'dp')), parts along dimension 0, may hold values from 0 to 1023
- move_board: int32 [8192, 1], P(('groups', 'dp')), parts along dimension 0, may hold values from 0 to 63; in each aligned block of 512 rows (0 to 511, 512 to 1023, ...) at most 16 rows name the same one
- move_table: bfloat16 [1024, 4096], replicated, may hold values from -4.5 to 4.5
- norm_gain: bfloat16 [4096], replicated, may hold values from 0.25 to 1.75
- w_query: bfloat16 [4096, 2048], P('dp', 'tensor'), may hold values from -0.0625 to 0.0625
- w_keyval: bfloat16 [4096, 512], P('dp', 'tensor'), may hold values from -0.09375 to 0.09375
- w_score: bfloat16 [2048], P('tensor'), may hold values from -3 to 3
Outputs:
- move_logprob: float32 [8192], P(('groups', 'dp')), parts along dimension 0
There are 2 independent parts, one for each index of `groups`. A program takes and returns all parts, laid end to end along the dimension named above; an argument that names none is the same for every part. Nothing has to cross between parts.
Inputs may be any that keep to these rules, and one draw needn't show every extreme that they name: `move_board`: within the rows of one device, at most 16 rows name one board, a bound that some block reaches; every board is named by some row.
All inputs are finite; a program needn't handle non-finite values.
Results may differ from a plain program's by a relative error of at most 0.003.
Values may be sent and summed in bfloat16 or wider, within the bound.
No kernel may reach another device: no remote copies, remote signals or barrier semaphores. Data moves between devices by JAX's collectives and lax.ppermute only.
A program may use at most 128 MiB of HBM per device.

v0:
```python
import math

import jax
import jax.numpy as jnp
from jax import lax
from jax.sharding import PartitionSpec as P

HD = 128


EPS = 1e-06
THETA = 5000000.0


def rotate(block, position):
    full_width = block.shape[-1]
    half_width = full_width // 2
    frequency = THETA ** (-2.0 * jnp.arange(half_width, dtype=jnp.float32) / full_width)
    angles = position * frequency
    cosine = jnp.cos(angles)
    sin_part = jnp.sin(angles)
    first_half = block[..., :half_width]
    second = block[..., half_width:]
    return jnp.concatenate(
        [first_half * cosine - second * sin_part, second * cosine + first_half * sin_part], axis=-1
    )


def normalize(embedded, norm_gain):
    raw_values = embedded.astype(jnp.float32)
    inverse = lax.rsqrt(jnp.mean(raw_values * raw_values, axis=-1, keepdims=True) + EPS)
    return (raw_values * inverse * norm_gain.astype(jnp.float32)).astype(jnp.bfloat16)


def finish_rows(query_rows, keyval, position):
    row_count = query_rows.shape[0]
    head_count = query_rows.shape[1] // HD
    group_count = keyval.shape[1] // (2 * HD)
    query_rows = rotate(query_rows.reshape(row_count, head_count, HD), position)
    query_rows = query_rows.astype(jnp.bfloat16).reshape(row_count, head_count * HD)
    keyval = keyval.reshape(row_count, group_count, 2, HD)
    own_key = rotate(keyval[:, :, 0], position)
    own_rows = jnp.stack([own_key, keyval[:, :, 1]], axis=2).astype(jnp.bfloat16)
    return (query_rows, own_rows.reshape(row_count, group_count * 2 * HD))


def project_rows(normed, w_query, w_keyval, position):
    query_rows = jnp.dot(
        normed,
        lax.all_gather(w_query, "dp", axis=0, tiled=True),
        preferred_element_type=jnp.float32,
    )
    keyval = jnp.dot(
        normed,
        lax.all_gather(w_keyval, "dp", axis=0, tiled=True),
        preferred_element_type=jnp.float32,
    )
    return finish_rows(query_rows, keyval, position)


def make_rows(ids, move_table, norm_gain, w_query, w_keyval, position):
    normed = normalize(jnp.take(move_table, ids, axis=0), norm_gain)
    return project_rows(normed, w_query, w_keyval, position)


def score_boards(query_rows, own_rows, live_mask, prefix_kv, w_score):
    peer_count, boards_here, capacity = live_mask.shape
    prefix_len = prefix_kv.shape[1]
    group_count = own_rows.shape[-1] // (2 * HD)
    group_size = query_rows.shape[-1] // HD // group_count
    inv_root = 1.0 / math.sqrt(HD)
    prefix_split = prefix_kv.reshape(boards_here, prefix_len, group_count, 2, HD)
    grouped = query_rows.reshape(peer_count, boards_here, capacity, group_count, group_size, HD)
    own_split = own_rows.reshape(peer_count, boards_here, capacity, group_count, 2, HD)
    logit_prefix = (
        jnp.einsum(
            "sbckgd,bpkd->sbckgp",
            grouped,
            prefix_split[:, :, :, 0],
            preferred_element_type=jnp.float32,
        )
        * inv_root
    )
    logit_own = (
        jnp.einsum(
            "sbckgd,sbckd->sbckg", grouped, own_split[..., 0, :], preferred_element_type=jnp.float32
        )
        * inv_root
    )
    peak = jnp.maximum(jnp.max(logit_prefix, axis=-1), logit_own)
    exp_prefix = jnp.exp(logit_prefix - peak[..., None])
    exp_own = jnp.exp(logit_own - peak)
    denom = jnp.sum(exp_prefix, axis=-1) + exp_own
    weight_prefix = (exp_prefix / denom[..., None]).astype(jnp.bfloat16)
    weight_own = (exp_own / denom).astype(jnp.bfloat16)
    context = jnp.einsum(
        "sbckgp,bpkd->sbckgd",
        weight_prefix,
        prefix_split[:, :, :, 1],
        preferred_element_type=jnp.float32,
    )
    context = (
        context
        + weight_own.astype(jnp.float32)[..., None]
        * own_split[..., 1, :].astype(jnp.float32)[..., None, :]
    )
    context = context.astype(jnp.bfloat16).reshape(
        peer_count, boards_here, capacity, group_count * group_size * HD
    )
    partial_value = jnp.einsum("sbcf,f->sbc", context, w_score, preferred_element_type=jnp.float32)
    scores_all = lax.psum(partial_value, "tensor")
    is_live = live_mask > 0.5
    peak_board = jnp.max(jnp.where(is_live, scores_all, -1e30), axis=(0, 2))
    shifted = jnp.where(is_live, jnp.exp(scores_all - peak_board[None, :, None]), 0.0)
    denom_board = jnp.sum(shifted, axis=(0, 2))
    return scores_all - peak_board[None, :, None] - jnp.log(denom_board)[None, :, None]


def per_device(prefix_kv, move_ids, move_board, move_table, norm_gain, w_query, w_keyval, w_score):
    row_count = move_ids.shape[0]
    boards_here = prefix_kv.shape[0]
    prefix_len = prefix_kv.shape[1]
    peer_count = lax.axis_size("dp")
    board_total = boards_here * peer_count
    capacity = max(2, (2 * row_count + board_total - 1) // board_total)
    board_of = move_board[:, 0]
    positions = jnp.arange(row_count)
    ahead = (board_of[:, None] == board_of[None, :]) & (positions[None, :] < positions[:, None])
    rank_in = jnp.sum(ahead.astype(jnp.int32), axis=1)
    slot_of = board_of * capacity + rank_in
    slot_total = board_total * capacity
    query_rows, own_rows = make_rows(move_ids, move_table, norm_gain, w_query, w_keyval, prefix_len)
    query_cols = query_rows.shape[1]
    payload = jnp.concatenate([query_rows, own_rows], axis=1)
    outgoing = jnp.zeros((slot_total, payload.shape[1]), jnp.bfloat16).at[slot_of].set(payload)
    markers = jnp.zeros((slot_total,), jnp.bfloat16).at[slot_of].set(1.0)
    arrived, markers_in = (
        lax.all_to_all(
            outgoing.reshape(peer_count, boards_here * capacity, payload.shape[1]),
            "dp",
            split_axis=0,
            concat_axis=0,
            tiled=True,
        ),
        lax.all_to_all(
            markers.reshape(peer_count, boards_here * capacity),
            "dp",
            split_axis=0,
            concat_axis=0,
            tiled=True,
        ),
    )
    arrived = arrived.reshape(peer_count, boards_here, capacity, payload.shape[1])
    query_rows = arrived[..., :query_cols]
    own_rows = arrived[..., query_cols:]
    live_mask = markers_in.astype(jnp.float32).reshape(peer_count, boards_here, capacity)
    logprob = score_boards(query_rows, own_rows, live_mask, prefix_kv, w_score)
    returned = lax.all_to_all(
        logprob.reshape(peer_count, boards_here * capacity),
        "dp",
        split_axis=0,
        concat_axis=0,
        tiled=True,
    )
    return jnp.take(returned.reshape(slot_total), slot_of, axis=0)


def solution(mesh):
    placed = (
        P(("groups", "dp"), None, "tensor"),
        P(("groups", "dp")),
        P(("groups", "dp"), None),
        P(),
        P(),
        P("dp", "tensor"),
        P("dp", "tensor"),
        P("tensor"),
    )
    return jax.shard_map(
        per_device, mesh=mesh, in_specs=placed, out_specs=P(("groups", "dp")), check_vma=False
    )
```

profile of v0, /device:TPU:0, one launch (start us, length us, event | category | flops | bytes accessed | tf_op | source)
XLA Modules:
  0.0 307.9 jit_solution(4011202950417739300)
XLA Ops:
  8.0 1.0 convert_reduce_fusion
  9.7 3.8 %scatter_custom_fusion.1 = bf16[1024]{0:T(1024)(128)(2,1)S(1)} fusion(s32[512]{0:T(512)S(1)} %bitcast.134, bf16[512]{0:T(512)(128)(2,1)S(1)} %broadcast.92, bf16[]{:T(256)} %constant.22.clone.1), kind=kCustom, calls=%fused_computation.69 | custom fusion | bytes 2050 | tf_op jit(solution)/shard_map/scatter | solution.py:136
  14.1 7.3 %all-to-all-start.1 = ((bf16[8,1,128]{2,1,0:T(2,128)(2,1)}), bf16[8,1,128]{2,1,0:T(2,128)(2,1)S(1)}, u32[]{:S(2)}, u32[]{:S(2)}) async-start(bf16[8,1,128]{2,1,0:T(2,128)(2,1)} %copy.41), calls=%async_computation.1 | async-start | bytes 8192 | tf_op jit(solution)/shard_map/all_to_all | solution.py:145
  22.7 13.0 %gather_fusion = bf16[512,4096]{1,0:T(8,128)(2,1)} fusion(bf16[1024,4096]{1,0:T(8,128)(2,1)} %param.11, s32[1024]{0:T(1024)S(1)} %pad_clamp_fusion.1), kind=kCustom, calls=%fused_computation | custom fusion | bytes 8390656 | tf_op jit(solution)/shard_map/jit(_take)/gather | solution.py:62
  35.9 3.4 %fusion = f32[512]{0:T(512)S(1)} fusion(bf16[512,4096]{1,0:T(8,128)(2,1)} %gather_fusion, pred[512]{0:T(512)(128)(4,1)S(1)} %compare_and_fusion), kind=kLoop, calls=%fused_computation.6 | loop fusion | flops 8388096 | bytes 4196864 | tf_op jit(solution)/shard_map/reduce_sum | solution.py:31
  39.3 22.2 %all-gather.5.cloned.1.call-done = bf16[4096,256]{1,0:T(8,128)(2,1)} async-done(((bf16[512,256]{1,0:T(8,128)(2,1)}), bf16[4096,256]{1,0:T(8,128)(2,1)}) %all-gather.5.cloned.1.call-update) | async-done | bytes 2097168 | tf_op jit(solution)/shard_map/all_gather | solution.py:55
  61.5 4.8 %fusion.33 = f32[512,256]{0,1:T(8,128)S(1)} fusion(bf16[4096,256]{1,0:T(8,128)(2,1)} %all-gather.5.cloned.1.call-done, f32[4096]{0:T(1024)S(1)} %convert_element_type.49, f32[512]{0:T(512)S(1)} %add_rsqrt_fusion, bf16[512,4096]{1,0:T(8,128)(2,1)} %gather_fusion, pred[512]{0:T(512)(128)(4,1)S(1)} %compare_and_fusion), kind=kOutput, calls=%fused_computation.75 | convolution fusion | flops 1084227584 | bytes 6834688 | tf_op jit(solution)/shard_map/dot_general | solution.py:53
  66.7 120.4 %all-gather.3.cloned.1.call-done = bf16[4096,1024]{1,0:T(8,128)(2,1)} async-done(((bf16[512,1024]{1,0:T(8,128)(2,1)}), bf16[4096,1024]{1,0:T(8,128)(2,1)}) %all-gather.3.cloned.1.call-update) | async-done | bytes 8388624 | tf_op jit(solution)/shard_map/all_gather | solution.py:50
  187.1 8.5 %convolution_bitcast_fusion = f32[64,8,8,128]{3,1,2,0:T(8,128)S(1)} fusion(bf16[4096,1024]{1,0:T(8,128)(2,1)} %all-gather.3.cloned.1.call-done, f32[4096]{0:T(1024)S(1)} %convert_element_type.49, f32[512]{0:T(512)S(1)} %add_rsqrt_fusion, bf16[512,4096]{1,0:T(8,128)(2,1)} %gather_fusion, pred[512]{0:T(512)(128)(4,1)S(1)} %compare_and_fusion), kind=kOutput, calls=%fused_computation.26 | convolution fusion | flops 4305453056 | bytes 14699008 | tf_op jit(solution)/shard_map/dot_general | solution.py:48
  196.1 0.7 subtract_convert_fusion
  197.7 4.7 %scatter_custom_fusion = bf16[1024,1280]{1,0:T(8,128)(2,1)} fusion(s32[512]{0:T(512)S(1)} %bitcast.135, bf16[512,256]{1,0:T(8,128)(2,1)S(1)} %copy.34, bf16[]{:T(256)} %constant.69, bf16[512,1024]{1,0:T(8,128)(2,1)S(1)} %bitcast.123, bf16[]{:T(256)} %constant.22.clone.1), kind=kCustom, calls=%fused_computation.27 | custom fusion | flops 2621440 | bytes 3932164 | tf_op jit(solution)/shard_map/scatter | solution.py:135
  202.4 3.8 %all-to-all-start = ((bf16[8,128,1280]{2,1,0:T(8,128)(2,1)}), bf16[8,128,1280]{2,1,0:T(8,128)(2,1)S(1)}, u32[]{:S(2)}, u32[]{:S(2)}) async-start(bf16[8,128,1280]{2,1,0:T(8,128)(2,1)} %bitcast.7), calls=%async_computation | async-start | bytes 5242880 | tf_op jit(solution)/shard_map/all_to_all | solution.py:138
  206.1 2.3 copy.36
  208.5 56.9 %all-to-all-done = bf16[8,128,1280]{2,1,0:T(8,128)(2,1)S(1)} async-done(((bf16[8,128,1280]{2,1,0:T(8,128)(2,1)}), bf16[8,128,1280]{2,1,0:T(8,128)(2,1)S(1)}, u32[]{:S(2)}, u32[]{:S(2)}) %all-to-all-start) | async-done | bytes 2621472 | tf_op jit(solution)/shard_map/all_to_all | solution.py:138
  267.3 1.2 fusion.21
  268.5 1.4 bitcast_reduce_fusion
  270.0 2.8 fusion.4
  273.0 4.1 %fusion.5 = bf16[8,8,16,1,8,128]{5,4,2,0,1,3:T(8,128)(2,1)S(1)} fusion(f32[8,8,16,128]{3,2,0,1:T(8,128)S(1)} %fusion.25, f32[8,8,16,8]{3,2,0,1:T(8,128)S(1)} %get-tuple-element.10, f32[8,8,16,8]{3,2,0,1:T(8,128)S(1)} %get-tuple-element.9, f32[8,8,16,8]{3,2,0,1:T(8,128)S(1)} %fusion.23, f32[8,8,16,8,256]{4,3,2,1,0:T(8,128)S(1)} %get-tuple-element.16, ...), kind=kOutput, calls=%fused_computation.15 | convolution fusion | flops 548405248 | bytes 13107200 | tf_op jit(solution)/shard_map/sbckgp,bpkd->sbckgd/dot_general | solution.py:96
  277.2 2.3 reshape.156
  279.5 4.1 %fusion.11 = f32[1,8,8,16]{3,0,2,1:T(1,128)S(1)} fusion(bf16[8,8,16,1024]{3,2,0,1:T(8,128)(2,1)} %reshape.156, bf16[1024,1,1,1]{0,1,2,3:T(2,128)(2,1)S(1)} %reshape.196), kind=kOutput, calls=%fused_computation.22 | convolution fusion | flops 2097152 | bytes 2103296 | tf_op jit(solution)/shard_map/sbcf,f->sbc/dot_general | solution.py:110
  283.6 3.4 %psum.7 = f32[8,8,16]{2,1,0:T(8,128)S(1)} all-reduce(f32[8,8,16]{2,1,0:T(8,128)S(1)} %bitcast.131), channel_id=1, replica_groups=mesh['groups'=2,'dp'=8,'tensor'=2] {'tensor'}, use_global_device_ids=true, to_apply=%region_5.6 | all-reduce | flops 1024 | bytes 8192 | tf_op jit(solution)/shard_map/psum | solution.py:111
  288.1 3.6 %all-to-all-start.2 = ((f32[8,1,128]{2,1,0:T(1,128)}), f32[8,1,128]{2,1,0:T(1,128)S(1)}, u32[]{:S(2)}, u32[]{:S(2)}) async-start(f32[8,1,128]{2,1,0:T(1,128)} %bitcast.33), calls=%async_computation.2 | async-start | bytes 8192 | tf_op jit(solution)/shard_map/all_to_all | solution.py:158
  291.8 6.5 %all-to-all-done.2 = f32[8,1,128]{2,1,0:T(1,128)S(1)} async-done(((f32[8,1,128]{2,1,0:T(1,128)}), f32[8,1,128]{2,1,0:T(1,128)S(1)}, u32[]{:S(2)}, u32[]{:S(2)}) %all-to-all-start.2) | async-done | bytes 4128 | tf_op jit(solution)/shard_map/all_to_all | solution.py:158
  298.2 2.3 gather_fusion.1
  (48 shorter events, 9.8 us)
Async XLA Ops:
  6.5 55.0 %all-gather.5.cloned.1.call-start = ((), (), s32[]{:S(2)}) async-start(), calls=%async_computation.4 | async-start | bytes 2359296 | tf_op jit(solution)/shard_map/all_gather | solution.py:55
  7.3 179.9 %all-gather.3.cloned.1.call-start = ((), (), s32[]{:S(2)}) async-start(), calls=%async_computation.3 | async-start | bytes 9437184 | tf_op jit(solution)/shard_map/all_gather | solution.py:50
  14.1 188.3 %all-to-all-start.1 = ((bf16[8,1,128]{2,1,0:T(2,128)(2,1)}), bf16[8,1,128]{2,1,0:T(2,128)(2,1)S(1)}, u32[]{:S(2)}, u32[]{:S(2)}) async-start(bf16[8,1,128]{2,1,0:T(2,128)(2,1)} %copy.41), calls=%async_computation.1 | async-start | bytes 8192 | tf_op jit(solution)/shard_map/all_to_all | solution.py:145
  22.7 13.1 %copy-start.1 = (s32[512]{0:T(512)S(1)}, s32[512]{0:T(512)}, u32[]{:S(2)}) copy-start(s32[512]{0:T(512)} %param.9) | copy-start | bytes 6148
  202.4 6.0 %copy-start.2 = (bf16[1024]{0:T(1024)(128)(2,1)S(1)}, bf16[1024]{0:T(1024)(128)(2,1)}, u32[]{:S(2)}) copy-start(bf16[1024]{0:T(1024)(128)(2,1)} %param.15) | copy-start | bytes 6148
  202.4 63.0 %all-to-all-start = ((bf16[8,128,1280]{2,1,0:T(8,128)(2,1)}), bf16[8,128,1280]{2,1,0:T(8,128)(2,1)S(1)}, u32[]{:S(2)}, u32[]{:S(2)}) async-start(bf16[8,128,1280]{2,1,0:T(8,128)(2,1)} %bitcast.7), calls=%async_computation | async-start | bytes 5242880 | tf_op jit(solution)/shard_map/all_to_all | solution.py:138
  266.5 2.0 copy-start
  288.1 10.1 %all-to-all-start.2 = ((f32[8,1,128]{2,1,0:T(1,128)}), f32[8,1,128]{2,1,0:T(1,128)S(1)}, u32[]{:S(2)}, u32[]{:S(2)}) async-start(f32[8,1,128]{2,1,0:T(1,128)} %bitcast.33), calls=%async_computation.2 | async-start | bytes 8192 | tf_op jit(solution)/shard_map/all_to_all | solution.py:158
Sparse Core Ops, SparseCore 0:
  9.5 52.0 all-gather.4
  63.7 123.4 all-gather.2
where the time goes:
time: 308 us
  waiting for transfers between devices  207 us (67%)
  local copies, waits for them, and re-layouts  27.8 us (9%)
  matrix products  24.1 us (8%)
  other arithmetic  16.8 us (5%)
  starting transfers between devices  14.7 us (5%)
  between operations  13.7 us (4%)
  blocking collectives  3.41 us (1%)
    all_gather x1, waiting for transfers between devices, project_rows(): lax.all_gather(w_query, 'dp', axis=0, tiled=True)  120 us
    all_to_all x1, waiting for transfers between devices, per_device(): lax.all_to_all(outgoing.reshape(peer_count, boards_here * capacity, paylo...  56.9 us
    all_gather x1, waiting for transfers between devices, project_rows(): lax.all_gather(w_keyval, 'dp', axis=0, tiled=True)  22.2 us
    gather x1, local copies, waits for them, and re-layouts, make_rows(): normed = normalize(jnp.take(move_table, ids, axis=0), norm_gain)  13 us
    dot_general x1, matrix products, project_rows(): jnp.dot(normed, lax.all_gather(w_query, 'dp', axis=0, tiled=True), prefer...  8.48 us
    all_to_all x1, starting transfers between devices, per_device(): lax.all_to_all(markers.reshape(peer_count, boards_here * capacity), 'dp',...  7.25 us
    all_to_all x1, waiting for transfers between devices, per_device(): lax.all_to_all(logprob.reshape(peer_count, boards_here * capacity), 'dp',...  6.46 us
  transfers between devices with their start and end apart: 5, of which 4 were waited for; matrix products, arithmetic and copies ran while one was open for 15% of the time, Pallas kernels for 0%

commit v1 on v0

v1 whole, which is shorter than its diff:
```python
import functools
import math

import jax
import jax.numpy as jnp
import numpy as np
from jax import lax
from jax.experimental import pallas as pl
from jax.experimental.pallas import tpu as pltpu
from jax.sharding import Mesh
from jax.sharding import PartitionSpec as P

HD = 128
HALF = HD // 2
EPS = 1e-06
THETA = 5000000.0
DEAD = -1e30

F32 = jnp.float32
BF16 = jnp.bfloat16

NN = (((1,), (0,)), ((), ()))
NT = (((1,), (1,)), ((), ()))
TN = (((0,), (0,)), ((), ()))


def matmul(a, b, dims=NN):
    return lax.dot_general(a, b, dims, preferred_element_type=F32)


def limits(mib):
    return pltpu.CompilerParams(vmem_limit_bytes=mib * 1024 * 1024)


class Plan:
    def __init__(self, groups, line, pair, heads, capacity):
        self.groups, self.line, self.pair = groups, line, pair
        self.peers = line * pair
        self.slab = groups * pair
        self.heads = heads
        self.mine = heads // self.slab
        self.pairs = HALF // line
        self.q_rows = self.mine * 2 * self.pairs
        self.k_rows = HD // (groups * self.peers)
        self.fold_rows = 2 * self.mine
        used = self.q_rows + self.k_rows + self.fold_rows
        self.rows = -(-used // 16) * 16
        self.capacity = capacity
        self.slots = self.peers * capacity


def pack_weights(plan, at_ref, wq_ref, wkv_ref, ws_ref, out_ref, pick):
    group = at_ref[0]
    rows, half_cols = plan.rows, wq_ref.shape[1]
    r = lax.broadcasted_iota(jnp.int32, (rows, 1), 0)
    part = r // (plan.mine * plan.pairs)
    head = (r // plan.pairs) % plan.mine
    entry = r % plan.pairs
    is_q = r < plan.q_rows
    k_at = r - plan.q_rows
    is_k = (k_at >= 0) & (k_at < plan.k_rows)
    f_at = k_at - plan.k_rows
    is_f = (f_at >= 0) & (f_at < plan.fold_rows)
    f_head = f_at // 2
    q_lane = lax.broadcasted_iota(jnp.int32, (rows, half_cols), 1)
    k_lane = lax.broadcasted_iota(jnp.int32, (rows, HD), 1)

    ws = ws_ref[...].astype(F32)

    def fill(peer, carry):
        line, pair = peer // plan.pair, peer % plan.pair
        column = (pair * plan.mine + head) * HD + part * HALF + line * plan.pairs + entry
        column = jnp.where(is_q, column, -1)
        at = pl.ds(pl.multiple_of(peer * rows, 16), rows)
        pick[at, :half_cols] = jnp.where(q_lane == column, 1.0, 0.0).astype(BF16)
        k_column = jnp.where(is_k, (group * plan.peers + peer) * plan.k_rows + k_at, -1)
        pick[at, half_cols : half_cols + HD] = jnp.where(k_lane == k_column, 1.0, 0.0).astype(BF16)
        fold = jnp.zeros((rows, HD), F32)
        my_head = jnp.where(is_f, (group * plan.pair + pair) * plan.mine + f_head, -1)
        for h in range(plan.heads):
            fold = jnp.where(my_head == h, ws[h : h + 1], fold)
        pick[at, half_cols + HD :] = fold.astype(BF16)
        return carry

    lax.fori_loop(0, plan.peers, fill, 0, unroll=plan.peers <= 8)
    total = matmul(pick[:, :half_cols], wq_ref[...], NT) + matmul(pick[:, half_cols:], wkv_ref[...], NT)
    rounded = total.astype(BF16)
    rest = (total - rounded.astype(F32)).astype(BF16)
    is_rest = is_f & (f_at % 2 == 1)
    for peer in range(plan.peers):
        at = slice(peer * rows, (peer + 1) * rows)
        out_ref[peer] = jnp.where(is_rest, rest[at].astype(F32), rounded[at].astype(F32)).astype(BF16)


def normalize(table_ref, gain_ref, out_ref):
    raw = table_ref[...].astype(F32)
    inverse = lax.rsqrt(jnp.mean(raw * raw, axis=-1, keepdims=True) + EPS)
    out_ref[...] = (raw * inverse * gain_ref[...].astype(F32)).astype(BF16)


def project(plan, w_ref, normed_ref, turn_ref, q_ref, k_ref, vo_ref):
    if len(w_ref.shape) == 3:
        depth = w_ref.shape[2]
        total = sum(
            matmul(w_ref[s], normed_ref[:, s * depth : (s + 1) * depth], NT) for s in range(w_ref.shape[0])
        )
    else:
        total = matmul(w_ref[...], normed_ref[...], NT)
    half = plan.q_rows // 2
    first, second = total[:half], total[half : 2 * half]
    cosine, sine = turn_ref[:, 0:1], turn_ref[:, 1:2]
    q = jnp.concatenate([first * cosine - second * sine, second * cosine + first * sine], axis=0).astype(BF16)
    for copy in range(q_ref.shape[0]):
        q_ref[copy] = q
    k = total[plan.q_rows : plan.q_rows + plan.k_rows].astype(BF16)
    for copy in range(k_ref.shape[0]):
        k_ref[copy] = k
    base = plan.q_rows + plan.k_rows
    for h in range(plan.mine):
        vo_ref[h : h + 1, :] = total[base + 2 * h : base + 2 * h + 1] + total[base + 2 * h + 1 : base + 2 * h + 2]


def pack_prefix(prefix_ref, ws_ref, out_ref):
    prefix_len = prefix_ref.shape[1]
    heads = ws_ref.shape[0]
    for board in range(prefix_ref.shape[0]):
        out_ref[board, :prefix_len] = prefix_ref[board, :, :HD]
        fold = matmul(ws_ref[...], prefix_ref[board, :, HD:], NT)
        rounded = fold.astype(BF16)
        rest = fold - rounded.astype(F32)
        both = jnp.concatenate([rounded.astype(F32), rest], axis=0).astype(BF16)
        for piece in range(prefix_len // HD):
            at = prefix_len + piece * 2 * heads
            out_ref[board, at : at + 2 * heads] = both[:, piece * HD : (piece + 1) * HD]


def list_moves(plan, at_ref, board_col_ref, board_row_ref, ids_ref, out_ref, slot_ref):
    count = board_col_ref.shape[0]
    same = board_col_ref[...] == board_row_ref[...]
    other = lax.broadcasted_iota(jnp.int32, (count, count), 0)
    own = lax.broadcasted_iota(jnp.int32, (count, count), 1)
    rank = jnp.sum(jnp.where(same & (other < own), 1.0, 0.0), axis=0, keepdims=True)
    slot = rank.astype(jnp.int32) + at_ref[0] * plan.capacity
    slot_ref[...] = slot
    slots_in = lax.broadcasted_iota(jnp.int32, (plan.slots, count), 0) == slot
    boards = plan.line * out_ref.shape[3]
    member = lax.broadcasted_iota(jnp.int32, (boards, count), 0) == board_row_ref[...]
    move = ids_ref[...] + 1
    high, low = (move // 64).astype(F32), (move % 64).astype(F32)
    slots_in = jnp.where(slots_in, 1.0, 0.0).astype(BF16)
    listed = 64.0 * matmul(jnp.where(member, high, 0.0).astype(BF16), slots_in, NT)
    listed = listed + matmul(jnp.where(member, low, 0.0).astype(BF16), slots_in, NT)
    share = boards // plan.line
    for line in range(plan.line):
        for g in range(plan.groups):
            for p in range(plan.pair):
                out_ref[g, line, p] = listed[line * share : (line + 1) * share]


def attend(plan, at_ref, q_ref, order_ref, k_ref, turn_ref, vo_ref, own_ref, *rest):
    peers = rest[: plan.slab - 1]
    moves_ref, out_ref, table, extra, scores = rest[plan.slab - 1 :]
    payloads = (own_ref, *peers)
    here = at_ref[0]
    mine, heads, slots = plan.mine, plan.heads, plan.slots
    moves = q_ref.shape[1]
    boards = own_ref.shape[0]
    prefix_len = own_ref.shape[1] - 2 * heads * (256 // HD)
    query_rows = mine * HD

    table[:query_rows] = matmul(order_ref[...], q_ref[...]).astype(BF16)
    key = k_ref[...].astype(F32)
    first, second = key[:HALF], key[HALF:]
    cosine, sine = turn_ref[:, 0:1], turn_ref[:, 1:2]
    key_first, key_second = first * cosine - second * sine, second * cosine + first * sine
    extra[...] = jnp.zeros_like(extra)
    for h in range(mine):
        q_first = table[h * HD : h * HD + HALF].astype(F32)
        q_second = table[h * HD + HALF : (h + 1) * HD].astype(F32)
        own_logit = jnp.sum(q_first * key_first + q_second * key_second, axis=0, keepdims=True)
        for place, value in ((0, own_logit), (2 * mine, vo_ref[h : h + 1, :])):
            rounded = value.astype(BF16).astype(F32)
            extra[place + h : place + h + 1] = rounded
            extra[place + mine + h : place + mine + h + 1] = value - rounded
    table[query_rows:] = extra[...].astype(BF16)

    scale = math.log2(math.e) / math.sqrt(HD)
    move_at = lax.broadcasted_iota(jnp.int32, (moves, slots), 0) + 1
    lanes = mine * slots
    fold_at = lax.broadcasted_iota(jnp.int32, (2 * heads, lanes), 0)
    fold_head = here * mine + lax.broadcasted_iota(jnp.int32, (2 * heads, lanes), 1) // slots
    fold_mine = (fold_at == fold_head) | (fold_at == fold_head + heads)

    def per_head(x, base):
        pieces = [x[base + h : base + h + 1] + x[base + mine + h : base + mine + h + 1] for h in range(mine)]
        return jnp.concatenate(pieces, axis=1)

    def step(board, carry):
        listed = []
        for j in range(plan.slab):
            owner = here ^ j
            listed.append(moves_ref[owner, pl.ds(board, 1), :])
        chosen = [jnp.where(move_at == row, 1.0, 0.0).astype(BF16) for row in listed]
        taken = matmul(table[...], jnp.concatenate(chosen, axis=1))
        for j in range(plan.slab):
            owner = here ^ j
            x = taken[:, j * slots : (j + 1) * slots]
            q = jnp.concatenate([x[h * HD : (h + 1) * HD].astype(BF16) for h in range(mine)], axis=1)
            logits = matmul(payloads[j][board, :prefix_len], q)
            own_logit = per_head(x, query_rows)
            own_value = per_head(x, query_rows + 2 * mine)
            peak = jnp.maximum(jnp.max(logits, axis=0, keepdims=True), own_logit)
            weight = jnp.exp2((logits - peak) * scale)
            own_weight = jnp.exp2((own_logit - peak) * scale)
            denom = jnp.sum(weight, axis=0, keepdims=True) + own_weight
            fold = jnp.concatenate(
                [
                    payloads[j][board, prefix_len + p * 2 * heads : prefix_len + (p + 1) * 2 * heads]
                    for p in range(prefix_len // HD)
                ],
                axis=1,
            )
            value = matmul(fold, weight.astype(BF16))
            value = jnp.sum(jnp.where(fold_mine, value, 0.0), axis=0, keepdims=True)
            value = (value + own_value * own_weight) / denom
            score = sum(value[:, h * slots : (h + 1) * slots] for h in range(mine))
            scores[owner, pl.ds(board, 1), :] = jnp.where(listed[j] > 0, score, DEAD)
        return carry

    lax.fori_loop(0, boards, step, 0)
    for g in range(plan.groups):
        mine_all = jnp.concatenate([scores[g * plan.pair + p] for p in range(plan.pair)], axis=0)
        for copy in range(out_ref.shape[1]):
            out_ref[g, copy] = mine_all


def finish(plan, parts_ref, board_ref, slot_ref, out_ref):
    line = parts_ref.shape[1]
    columns = []
    for at in range(line):
        total = None
        for g in range(parts_ref.shape[0]):
            for p in range(parts_ref.shape[2]):
                term = parts_ref[g, at, p]
                total = term if total is None else total + term
        columns.append(total)
    scores = jnp.concatenate(columns, axis=0)
    live = scores > 0.5 * DEAD
    peak = jnp.max(scores, axis=1, keepdims=True)
    denom = jnp.sum(jnp.where(live, jnp.exp(scores - peak), 0.0), axis=1, keepdims=True)
    logprob = jnp.where(live, scores - peak - jnp.log(denom), 0.0)
    count = board_ref.shape[1]
    member = lax.broadcasted_iota(jnp.int32, (scores.shape[0], count), 0) == board_ref[...]
    member = jnp.where(member, 1.0, 0.0).astype(BF16)
    found = jnp.zeros((plan.slots, count), F32)
    for _ in range(3):
        rounded = logprob.astype(BF16)
        found = found + matmul(rounded, member, TN)
        logprob = logprob - rounded.astype(F32)
    at = lax.broadcasted_iota(jnp.int32, (plan.slots, count), 0) == slot_ref[...]
    out_ref[...] = jnp.sum(jnp.where(at, found, 0.0), axis=0, keepdims=True)


def scalar_call(kernel, at, args, outs, scratch, mib, cost=None, specs=None):
    whole = lambda x: pl.BlockSpec(x.shape, lambda i, at, n=len(x.shape): (0,) * n)
    specs = specs or {}
    return pl.pallas_call(
        kernel,
        out_shape=outs,
        grid_spec=pltpu.PrefetchScalarGridSpec(
            num_scalar_prefetch=1,
            grid=(1,),
            in_specs=[specs.get(i, whole(x)) for i, x in enumerate(args)],
            out_specs=jax.tree.map(whole, outs),
            scratch_shapes=scratch,
        ),
        compiler_params=limits(mib),
        cost_estimate=cost,
    )(at, *args)


def shape(dims, dtype):
    return jax.ShapeDtypeStruct(tuple(dims), dtype)


def turn_table(position):
    frequency = THETA ** (-2.0 * np.arange(HALF, dtype=np.float32) / HD)
    angles = np.float32(position) * frequency.astype(np.float32)
    return np.stack([np.cos(angles), np.sin(angles)], axis=1).astype(np.float32)


def entry_order(plan):
    order = np.zeros((plan.mine * HD, plan.mine * HD), np.float32)
    for head in range(plan.mine):
        for part in range(2):
            for entry in range(HALF):
                line, at = divmod(entry, plan.pairs)
                source = line * plan.q_rows + (part * plan.mine + head) * plan.pairs + at
                order[head * HD + part * HALF + entry, source] = 1.0
    return order


def per_device(prefix_kv, move_ids, move_board, move_table, norm_gain, w_query, w_keyval, w_score):
    row_count = move_ids.shape[0]
    boards_here, prefix_len, _ = prefix_kv.shape
    moves, width = move_table.shape
    groups, line, pair = lax.axis_size("groups"), lax.axis_size("line"), lax.axis_size("pair")
    board_total = boards_here * line * pair
    capacity = max(2, (2 * row_count + board_total - 1) // board_total)
    heads = w_query.shape[1] // HD
    plan = Plan(groups, line, pair, heads, capacity)
    depth = w_query.shape[0]
    group_at = lax.axis_index("groups").astype(jnp.int32)
    line_at = lax.axis_index("line").astype(jnp.int32)
    pair_at = lax.axis_index("pair").astype(jnp.int32)
    slab_at = group_at * pair + pair_at
    as_index = lambda x: x.reshape(1)
    ws = w_score.reshape(heads, HD)

    half_cols = w_query.shape[1] // groups
    packed = scalar_call(
        functools.partial(pack_weights, plan),
        as_index(group_at),
        (w_query, w_keyval, ws),
        shape((plan.peers, plan.rows, depth), BF16),
        [pltpu.VMEM((plan.peers * plan.rows, half_cols + 2 * HD), BF16)],
        32,
        specs={0: pl.BlockSpec((depth, half_cols), lambda i, at: (0, at[0]))},
    )
    weights = lax.all_to_all(packed, ("line", "pair"), split_axis=0, concat_axis=0, tiled=True)

    board_row = move_board.reshape(1, row_count)
    share = pair * boards_here
    listed, slot_row = scalar_call(
        functools.partial(list_moves, plan),
        as_index(line_at * pair + pair_at),
        (move_board, board_row, move_ids.reshape(1, row_count)),
        (shape((groups, line, pair, share, plan.slots), F32), shape((1, row_count), jnp.int32)),
        [],
        32,
    )
    everywhere = ("groups", "line", "pair")
    listed = lax.all_to_all(
        listed.reshape(groups * plan.peers, share, plan.slots), everywhere, split_axis=0, concat_axis=0, tiled=True
    )
    listed = jnp.sum(listed.reshape(groups, plan.peers, share, plan.slots), axis=1)
    listed = listed.astype(jnp.int32).reshape(plan.slab, boards_here, plan.slots)

    pieces = prefix_len // HD
    payload = pl.pallas_call(
        pack_prefix,
        out_shape=shape((boards_here, prefix_len + pieces * 2 * heads, HD), BF16),
        compiler_params=limits(32),
    )(prefix_kv, ws)
    payloads = [payload]
    for step in range(1, plan.slab):
        swap = [(at, at ^ step) for at in range(plan.slab)]
        payloads.append(lax.ppermute(payload, ("groups", "pair"), swap))

    block = min(moves, 128)
    normed = pl.pallas_call(
        normalize,
        out_shape=shape((moves, width), BF16),
        grid=(moves // block,),
        in_specs=[pl.BlockSpec((block, width), lambda i: (i, 0)), pl.BlockSpec((1, width), lambda i: (0, 0))],
        out_specs=pl.BlockSpec((block, width), lambda i: (i, 0)),
        compiler_params=limits(32),
    )(move_table, norm_gain.reshape(1, width))
    turns = jnp.asarray(turn_table(prefix_len))
    my_turns = jnp.tile(lax.dynamic_slice_in_dim(turns, line_at * plan.pairs, plan.pairs, axis=0), (plan.mine, 1))
    if depth % HD:
        weights = weights.transpose(1, 0, 2).reshape(plan.rows, width)
    block = min(moves, 256)
    queries, keys, own_values = pl.pallas_call(
        functools.partial(project, plan),
        out_shape=(
            shape((line, plan.q_rows, moves), BF16),
            shape((groups * plan.peers, plan.k_rows, moves), BF16),
            shape((plan.mine, moves), F32),
        ),
        grid=(moves // block,),
        in_specs=[
            pl.BlockSpec(weights.shape, lambda i, n=weights.ndim: (0,) * n),
            pl.BlockSpec((block, width), lambda i: (i, 0)),
            pl.BlockSpec(my_turns.shape, lambda i: (0, 0)),
        ],
        out_specs=(
            pl.BlockSpec((line, plan.q_rows, block), lambda i: (0, 0, i)),
            pl.BlockSpec((groups * plan.peers, plan.k_rows, block), lambda i: (0, 0, i)),
            pl.BlockSpec((plan.mine, block), lambda i: (0, i)),
        ),
        compiler_params=limits(40),
    )(weights, normed, my_turns)
    queries = lax.all_to_all(queries, "line", split_axis=0, concat_axis=0, tiled=True)
    keys = lax.all_to_all(keys, everywhere, split_axis=0, concat_axis=0, tiled=True)

    query_rows = plan.mine * HD
    back = plan.peers * lax.axis_size("tensor")
    parts = scalar_call(
        functools.partial(attend, plan),
        as_index(slab_at),
        (
            queries.reshape(query_rows, moves),
            jnp.asarray(entry_order(plan), BF16),
            keys.reshape(HD, moves),
            turns,
            own_values,
            *payloads,
            listed,
        ),
        shape((groups, back, share, plan.slots), F32),
        [
            pltpu.VMEM((query_rows + 16, moves), BF16),
            pltpu.VMEM((16, moves), F32),
            pltpu.VMEM((plan.slab, boards_here, plan.slots), F32),
        ],
        48,
    )
    parts = lax.all_to_all(
        parts.reshape(groups * back, share, plan.slots),
        ("groups", "line", "pair", "tensor"),
        split_axis=0,
        concat_axis=0,
        tiled=True,
    )
    parts = parts.reshape(groups, line, back // line, share, plan.slots)
    logprob = pl.pallas_call(
        functools.partial(finish, plan), out_shape=shape((1, row_count), F32), compiler_params=limits(32)
    )(parts, board_row, slot_row)
    return logprob.reshape(row_count)


def solution(mesh):
    order = ("groups", "dp", "tensor")
    assert mesh.axis_names == order
    pair = 2
    groups, peers, tensor = (mesh.shape[name] for name in order)
    fine = Mesh(mesh.devices.reshape(groups, peers // pair, pair, tensor), ("groups", "line", "pair", "tensor"))
    rows = ("groups", "line", "pair")
    placed = (
        P(rows, None, "tensor"),
        P(rows),
        P(rows, None),
        P(),
        P(),
        P(("line", "pair"), "tensor"),
        P(("line", "pair"), "tensor"),
        P("tensor"),
    )
    return jax.shard_map(per_device, mesh=fine, in_specs=placed, out_specs=P(rows), check_vma=False)
```

time: 308 us -> 124 us (0.40)
  waiting for transfers between devices: 207 us -> 37.3 us
  blocking collectives: 3.41 us -> 31.1 us
  Pallas kernels: 0 us -> 27.1 us
  matrix products: 24.1 us -> 0 us
  local copies, waits for them, and re-layouts: 27.8 us -> 9.16 us
  other arithmetic: 16.8 us -> 0.02 us
  between operations: 13.7 us -> 0.17 us
  starting transfers between devices: 14.7 us -> 19 us
    all_gather x2 -> x0, waiting for transfers between devices: 143 us -> none  [the longest x1 120 us: project_rows(): lax.all_gather(w_query, 'dp', axis=0, tiled=True)]
    all_to_all x3, waiting for transfers between devices: 63.3 us -> 14.1 us  [the longest x1 14.1 us: per_device(): lax.all_to_all(packed, ('line', 'pair'), split_axis=0, concat_axis=0, til...]
    all_to_all x0 -> x2, blocking collectives: none -> 31.1 us  [the longest x1 16.2 us: per_device(): lax.all_to_all(keys, everywhere, split_axis=0, concat_axis=0, tiled=True)]
    pallas_call x0 -> x7, Pallas kernels: none -> 27.1 us  [the longest x3 17.2 us: scalar_call(): pl.pallas_call(kernel, out_shape=outs, grid_spec=pltpu.PrefetchScalarGrid...]
    dot_general x6 -> x0, matrix products: 24.1 us -> none  [the longest x1 8.48 us: project_rows(): jnp.dot(normed, lax.all_gather(w_query, 'dp', axis=0, tiled=True), prefer...]
    ppermute x0 -> x3, waiting for transfers between devices: none -> 23.2 us  [per_device(): payloads.append(lax.ppermute(payload, ('groups', 'pair'), swap))]
    gather x2 -> x0, local copies, waits for them, and re-layouts: 15.3 us -> none  [the longest x1 13 us: make_rows(): normed = normalize(jnp.take(move_table, ids, axis=0), norm_gain)]
    reduce_sum x4 -> x1, other arithmetic: 7.42 us -> 0.01 us  [per_device(): jnp.sum(listed.reshape(groups, plan.peers, share, plan.slots), axis=1)]
  transfers between devices with their start and end apart: 5 -> 6, of which waited for: 4 -> 3; matrix products, arithmetic and copies ran while one was open for 15% -> 1% of each run, Pallas kernels for 0% -> 8%
where the time goes in v1:
time: 124 us
  waiting for transfers between devices  37.3 us (30%)
  blocking collectives  31.1 us (25%)
  Pallas kernels  27.1 us (22%)
  starting transfers between devices  19 us (15%)
  local copies, waits for them, and re-layouts  9.16 us (7%)
    ppermute x3, waiting for transfers between devices, per_device(): payloads.append(lax.ppermute(payload, ('groups', 'pair'), swap))  23.2 us
    pallas_call x3, Pallas kernels, scalar_call(): pl.pallas_call(kernel, out_shape=outs, grid_spec=pltpu.PrefetchScalarGrid...  17.2 us
    all_to_all x1, blocking collectives, per_device(): lax.all_to_all(keys, everywhere, split_axis=0, concat_axis=0, tiled=True)  16.2 us
    all_to_all x1, blocking collectives, per_device(): lax.all_to_all(parts.reshape(groups * back, share, plan.slots), ('groups'...  14.9 us
    all_to_all x1, waiting for transfers between devices, per_device(): lax.all_to_all(packed, ('line', 'pair'), split_axis=0, concat_axis=0, til...  14.1 us
    unnamed x23, local copies, waits for them, and re-layouts  8.44 us
    all_to_all x1, starting transfers between devices, per_device(): lax.all_to_all(packed, ('line', 'pair'), split_axis=0, concat_axis=0, til...  7.25 us
    pallas_call x1, Pallas kernels, per_device(): pl.pallas_call(normalize, out_shape=shape((moves, width), BF16), grid=(mo...  4.78 us
  transfers between devices with their start and end apart: 6, of which 3 were waited for; matrix products, arithmetic and copies ran while one was open for 1% of the time, Pallas kernels for 8%

profile of v1, /device:TPU:0, one launch (start us, length us, event | category | flops | bytes accessed | tf_op | source)
XLA Modules:
  0.0 123.8 jit_solution(3019683609280857925)
XLA Ops:
  0.0 1.2 copy-done.1
  1.2 0.9 copy-done.3
  2.2 0.7 copy-done.8
  2.9 1.6 %shard_map.100 = bf16[8,80,512]{2,1,0:T(8,128)(2,1)} custom-call(s32[1]{0:T(128)} %bitcast.1.at_ref, bf16[512,1024]{1,0:T(8,128)(2,1)S(1)} %copy-done.1, bf16[512,256]{1,0:T(8,128)(2,1)S(1)} %copy-done.3, bf16[8,128]{1,0:T(8,128)(2,1)S(1)} %bitcast.24), custom_call_target="tpu_custom_call" | custom-call | tf_op jit(solution)/shard_map/pallas_call | solution.py:267
  4.4 7.3 %all-to-all-start = ((bf16[8,80,512]{2,1,0:T(8,128)(2,1)}), bf16[8,80,512]{2,1,0:T(8,128)(2,1)S(1)}, u32[]{:S(2)}, u32[]{:S(2)}) async-start(bf16[8,80,512]{2,1,0:T(8,128)(2,1)} %shard_map.100), calls=%async_computation | async-start | bytes 1310720 | tf_op jit(solution)/shard_map/all_to_all | solution.py:330
  11.7 0.8 copy.13.board_col_ref
  13.2 0.7 copy-done.10
  13.9 1.0 shard_map.104
  14.9 14.1 %all-to-all-done.w_ref = bf16[8,80,512]{2,1,0:T(8,128)(2,1)S(1)} async-done(((bf16[8,80,512]{2,1,0:T(8,128)(2,1)}), bf16[8,80,512]{2,1,0:T(8,128)(2,1)S(1)}, u32[]{:S(2)}, u32[]{:S(2)}) %all-to-all-start) | async-done | bytes 655392 | tf_op jit(solution)/shard_map/all_to_all | solution.py:330
  29.0 4.7 %all-to-all-start.3 = ((f32[16,16,128]{2,1,0:T(8,128)}), f32[16,16,128]{2,1,0:T(8,128)S(1)}, u32[]{:S(2)}, u32[]{:S(2)}) async-start(f32[16,16,128]{2,1,0:T(8,128)} %bitcast.9), calls=%async_computation.3 | async-start | bytes 262144 | tf_op jit(solution)/shard_map/all_to_all | solution.py:343
  33.7 0.7 reshape.52.gain_ref
  34.4 3.4 %copy-done = bf16[1024,4096]{1,0:T(8,128)(2,1)S(1)} copy-done((bf16[1024,4096]{1,0:T(8,128)(2,1)S(1)}, bf16[1024,4096]{1,0:T(8,128)(2,1)}, u32[]{:S(2)}) %copy-start) | copy-done | bytes 8388632
  37.8 4.8 %shard_map.101.normed_ref = bf16[1024,4096]{1,0:T(8,128)(2,1)S(1)} custom-call(bf16[1024,4096]{1,0:T(8,128)(2,1)S(1)} %copy-done, bf16[1,4096]{1,0:T(2,128)(2,1)S(1)} %reshape.52.gain_ref), custom_call_target="tpu_custom_call" | custom-call | tf_op jit(solution)/shard_map/pallas_call | solution.py:361
  42.7 3.8 %shard_map.102 = (bf16[4,64,1024]{2,1,0:T(8,128)(2,1)}, bf16[16,8,1024]{2,1,0:T(8,128)(2,1)S(1)}, f32[2,1024]{1,0:T(2,128)S(1)}) custom-call(bf16[8,80,512]{2,1,0:T(8,128)(2,1)S(1)} %all-to-all-done.w_ref, bf16[1024,4096]{1,0:T(8,128)(2,1)S(1)} %shard_map.101.normed_ref, f32[32,2]{1,0:T(8,128)S(1)} %bitcast.21), custom_call_target="tpu_custom_call" | custom-call | tf_op jit(solution)/shard_map/pallas_call | solution.py:374
  46.5 16.2 %all_to_all.25 = bf16[16,8,1024]{2,1,0:T(8,128)(2,1)S(1)} all-to-all(bf16[16,8,1024]{2,1,0:T(8,128)(2,1)S(1)} %get-tuple-element.11), channel_id=1, replica_groups=mesh['groups'=2,'line'=4,'pair'=2,'tensor'=2] {'groups','line','pair'}, dimensions={0} | all-to-all | bytes 524288 | tf_op jit(solution)/shard_map/all_to_all | solution.py:395
  62.7 3.5 %all-to-all-start.1 = ((bf16[4,64,1024]{2,1,0:T(8,128)(2,1)}), bf16[4,64,1024]{2,1,0:T(8,128)(2,1)S(1)}, u32[]{:S(2)}, u32[]{:S(2)}) async-start(bf16[4,64,1024]{2,1,0:T(8,128)(2,1)} %get-tuple-element.10), calls=%async_computation.1 | async-start | bytes 1048576 | tf_op jit(solution)/shard_map/all_to_all | solution.py:394
  66.4 0.8 collective-permute-start
  67.3 0.9 collective-permute-start.1
  68.2 1.8 %collective-permute-start.2 = (bf16[8,288,128]{2,1,0:T(8,128)(2,1)S(1)}, bf16[8,288,128]{2,1,0:T(8,128)(2,1)}, u32[]{:S(2)}, u32[]{:S(2)}) collective-permute-start(bf16[8,288,128]{2,1,0:T(8,128)(2,1)S(1)} %shard_map.103.own_ref), channel_id=1, source_target_pairs={{0,18},{2,16},{16,2},{18,0},{1,19},{3,17},{17,3},{19,1},{4,22},{6,... | collective-permute-start | bytes 1769480 | tf_op jit(solution)/shard_map/ppermute | solution.py:358
  70.0 12.7 %collective-permute-done.rest_0_ = bf16[8,288,128]{2,1,0:T(8,128)(2,1)S(1)} collective-permute-done((bf16[8,288,128]{2,1,0:T(8,128)(2,1)S(1)}, bf16[8,288,128]{2,1,0:T(8,128)(2,1)S(1)}, u32[]{:S(2)}, u32[]{:S(2)}) %collective-permute-start) | collective-permute-done | bytes 589856 | tf_op jit(solution)/shard_map/ppermute | solution.py:358
  82.8 10.4 %collective-permute-done.1.rest_1_ = bf16[8,288,128]{2,1,0:T(8,128)(2,1)S(1)} collective-permute-done((bf16[8,288,128]{2,1,0:T(8,128)(2,1)S(1)}, bf16[8,288,128]{2,1,0:T(8,128)(2,1)S(1)}, u32[]{:S(2)}, u32[]{:S(2)}) %collective-permute-start.1) | collective-permute-done | bytes 589856 | tf_op jit(solution)/shard_map/ppermute | solution.py:358
  93.2 14.6 %shard_map.105 = f32[2,16,16,128]{3,2,1,0:T(8,128)S(1)} custom-call(s32[1]{0:T(128)} %bitcast.at_ref, bf16[256,1024]{1,0:T(8,128)(2,1)S(1)} %bitcast.16, bf16[256,256]{1,0:T(8,128)(2,1)S(1)} %copy-done.4, bf16[128,1024]{1,0:T(8,128)(2,1)S(1)} %bitcast.18, f32[64,2]{1,0:T(8,128)S(1)} %copy-done.5, f32[2,1024]{1,0:T(2,128)S(1)} %get-tuple-element.12.vo_ref, ...), custom_call_target="tpu_custom_call" | custom-call | tf_op jit(solution)/shard_map/pallas_call | solution.py:267
  107.8 14.9 %all_to_all.26 = f32[32,16,128]{2,1,0:T(8,128)S(1)} all-to-all(f32[32,16,128]{2,1,0:T(8,128)S(1)} %bitcast.19), channel_id=1, replica_groups=mesh['groups'=2,'line'=4,'pair'=2,'tensor'=2] {'groups','line','pair','t..., dimensions={0} | all-to-all | bytes 524288 | tf_op jit(solution)/shard_map/all_to_all | solution.py:419
  122.7 1.1 shard_map.106
  (25 shorter events, 1.0 us)
Async XLA Ops:
  0.0 1.2 copy-start.1
  1.2 0.9 copy-start.3
  2.2 0.7 copy-start.8
  4.4 24.5 %all-to-all-start = ((bf16[8,80,512]{2,1,0:T(8,128)(2,1)}), bf16[8,80,512]{2,1,0:T(8,128)(2,1)S(1)}, u32[]{:S(2)}, u32[]{:S(2)}) async-start(bf16[8,80,512]{2,1,0:T(8,128)(2,1)} %shard_map.100), calls=%async_computation | async-start | bytes 1310720 | tf_op jit(solution)/shard_map/all_to_all | solution.py:330
  12.5 0.7 copy-start.6
  13.2 0.7 copy-start.10
  29.0 17.5 %all-to-all-start.3 = ((f32[16,16,128]{2,1,0:T(8,128)}), f32[16,16,128]{2,1,0:T(8,128)S(1)}, u32[]{:S(2)}, u32[]{:S(2)}) async-start(f32[16,16,128]{2,1,0:T(8,128)} %bitcast.9), calls=%async_computation.3 | async-start | bytes 262144 | tf_op jit(solution)/shard_map/all_to_all | solution.py:343
  34.4 3.4 %copy-start = (bf16[1024,4096]{1,0:T(8,128)(2,1)S(1)}, bf16[1024,4096]{1,0:T(8,128)(2,1)}, u32[]{:S(2)}) copy-start(bf16[1024,4096]{1,0:T(8,128)(2,1)} %table_ref.1) | copy-start | bytes 25165828
  37.8 4.8 %copy-start.5 = (f32[64,2]{1,0:T(8,128)S(1)}, f32[64,2]{1,0:T(8,128)}, u32[]{:S(2)}) copy-start(f32[64,2]{1,0:T(8,128)} %constant.27.clone.turn_ref) | copy-start | bytes 1540
  42.6 23.6 %copy-start.2 = (bf16[8,256,256]{2,1,0:T(8,128)(2,1)S(1)}, bf16[8,256,256]{2,1,0:T(8,128)(2,1)}, u32[]{:S(2)}) copy-start(bf16[8,256,256]{2,1,0:T(8,128)(2,1)} %prefix_ref.1) | copy-start | bytes 3145732
  42.6 23.6 %copy-start.9 = (bf16[1024]{0:T(1024)(128)(2,1)S(1)}, bf16[1024]{0:T(1024)(128)(2,1)}, u32[]{:S(2)}) copy-start(bf16[1024]{0:T(1024)(128)(2,1)} %param.17) | copy-start | bytes 6148
  42.6 50.6 %copy-start.4 = (bf16[256,256]{1,0:T(8,128)(2,1)S(1)}, bf16[256,256]{1,0:T(8,128)(2,1)}, u32[]{:S(2)}) copy-start(bf16[256,256]{1,0:T(8,128)(2,1)} %constant.28.clone.order_ref) | copy-start | bytes 393220
  42.6 80.1 %copy-start.7 = (s32[512,1]{0,1:T(1,128)S(1)}, s32[512,1]{0,1:T(1,128)}, u32[]{:S(2)}) copy-start(s32[512,1]{0,1:T(1,128)} %param.12) | copy-start | bytes 6148
  62.7 30.5 %all-to-all-start.1 = ((bf16[4,64,1024]{2,1,0:T(8,128)(2,1)}), bf16[4,64,1024]{2,1,0:T(8,128)(2,1)S(1)}, u32[]{:S(2)}, u32[]{:S(2)}) async-start(bf16[4,64,1024]{2,1,0:T(8,128)(2,1)} %get-tuple-element.10), calls=%async_computation.1 | async-start | bytes 1048576 | tf_op jit(solution)/shard_map/all_to_all | solution.py:394
  66.4 16.3 %collective-permute-start = (bf16[8,288,128]{2,1,0:T(8,128)(2,1)S(1)}, bf16[8,288,128]{2,1,0:T(8,128)(2,1)S(1)}, u32[]{:S(2)}, u32[]{:S(2)}) collective-permute-start(bf16[8,288,128]{2,1,0:T(8,128)(2,1)S(1)} %shard_map.103.own_ref), channel_id=1, source_target_pairs={{0,2},{2,0},{16,18},{18,16},{1,3},{3,1},{17,19},{19,17},{4,6},{6,4... | collective-permute-start | bytes 1769480 | tf_op jit(solution)/shard_map/ppermute | solution.py:358
  67.3 25.9 %collective-permute-start.1 = (bf16[8,288,128]{2,1,0:T(8,128)(2,1)S(1)}, bf16[8,288,128]{2,1,0:T(8,128)(2,1)S(1)}, u32[]{:S(2)}, u32[]{:S(2)}) collective-permute-start(bf16[8,288,128]{2,1,0:T(8,128)(2,1)S(1)} %shard_map.103.own_ref), channel_id=1, source_target_pairs={{0,16},{2,18},{16,0},{18,2},{1,17},{3,19},{17,1},{19,3},{4,20},{6,... | collective-permute-start | bytes 1769480 | tf_op jit(solution)/shard_map/ppermute | solution.py:358
  68.2 25.0 %collective-permute-start.2 = (bf16[8,288,128]{2,1,0:T(8,128)(2,1)S(1)}, bf16[8,288,128]{2,1,0:T(8,128)(2,1)}, u32[]{:S(2)}, u32[]{:S(2)}) collective-permute-start(bf16[8,288,128]{2,1,0:T(8,128)(2,1)S(1)} %shard_map.103.own_ref), channel_id=1, source_target_pairs={{0,18},{2,16},{16,2},{18,0},{1,19},{3,17},{17,3},{19,1},{4,22},{6,... | collective-permute-start | bytes 1769480 | tf_op jit(solution)/shard_map/ppermute | solution.py:358

commit v2 on v1

--- a/solution.py
+++ b/solution.py
@@ -113,8 +113,7 @@
     for copy in range(q_ref.shape[0]):
         q_ref[copy] = q
     k = total[plan.q_rows : plan.q_rows + plan.k_rows].astype(BF16)
-    for copy in range(k_ref.shape[0]):
-        k_ref[copy] = k
+    k_ref[...] = k
     base = plan.q_rows + plan.k_rows
     for h in range(plan.mine):
         vo_ref[h : h + 1, :] = total[base + 2 * h : base + 2 * h + 1] + total[base + 2 * h + 1 : base + 2 * h + 2]
@@ -143,29 +142,22 @@
     slot = rank.astype(jnp.int32) + at_ref[0] * plan.capacity
     slot_ref[...] = slot
     slots_in = lax.broadcasted_iota(jnp.int32, (plan.slots, count), 0) == slot
-    boards = plan.line * out_ref.shape[3]
+    boards = out_ref.shape[0]
     member = lax.broadcasted_iota(jnp.int32, (boards, count), 0) == board_row_ref[...]
     move = ids_ref[...] + 1
     high, low = (move // 64).astype(F32), (move % 64).astype(F32)
     slots_in = jnp.where(slots_in, 1.0, 0.0).astype(BF16)
     listed = 64.0 * matmul(jnp.where(member, high, 0.0).astype(BF16), slots_in, NT)
     listed = listed + matmul(jnp.where(member, low, 0.0).astype(BF16), slots_in, NT)
-    share = boards // plan.line
-    for line in range(plan.line):
-        for g in range(plan.groups):
-            for p in range(plan.pair):
-                out_ref[g, line, p] = listed[line * share : (line + 1) * share]
-
-
-def attend(plan, at_ref, q_ref, order_ref, k_ref, turn_ref, vo_ref, own_ref, *rest):
-    peers = rest[: plan.slab - 1]
-    moves_ref, out_ref, table, extra, scores = rest[plan.slab - 1 :]
-    payloads = (own_ref, *peers)
+    out_ref[...] = listed
+
+
+def attend(plan, at_ref, q_ref, order_ref, k_ref, turn_ref, vo_ref, prefix_ref, moves_ref, out_ref, table, extra, scores):
     here = at_ref[0]
     mine, heads, slots = plan.mine, plan.heads, plan.slots
     moves = q_ref.shape[1]
-    boards = own_ref.shape[0]
-    prefix_len = own_ref.shape[1] - 2 * heads * (256 // HD)
+    boards = prefix_ref.shape[1]
+    prefix_len = prefix_ref.shape[2] * HD // (HD + 2 * heads)
     query_rows = mine * HD
 
     table[:query_rows] = matmul(order_ref[...], q_ref[...]).astype(BF16)
@@ -198,15 +190,13 @@
     def step(board, carry):
         listed = []
         for j in range(plan.slab):
-            owner = here ^ j
-            listed.append(moves_ref[owner, pl.ds(board, 1), :])
+            listed.append(moves_ref[j, pl.ds(board, 1), :])
         chosen = [jnp.where(move_at == row, 1.0, 0.0).astype(BF16) for row in listed]
         taken = matmul(table[...], jnp.concatenate(chosen, axis=1))
         for j in range(plan.slab):
-            owner = here ^ j
             x = taken[:, j * slots : (j + 1) * slots]
             q = jnp.concatenate([x[h * HD : (h + 1) * HD].astype(BF16) for h in range(mine)], axis=1)
-            logits = matmul(payloads[j][board, :prefix_len], q)
+            logits = matmul(prefix_ref[j, board, :prefix_len], q)
             own_logit = per_head(x, query_rows)
             own_value = per_head(x, query_rows + 2 * mine)
             peak = jnp.maximum(jnp.max(logits, axis=0, keepdims=True), own_logit)
@@ -215,7 +205,7 @@
             denom = jnp.sum(weight, axis=0, keepdims=True) + own_weight
             fold = jnp.concatenate(
                 [
-                    payloads[j][board, prefix_len + p * 2 * heads : prefix_len + (p + 1) * 2 * heads]
+                    prefix_ref[j, board, prefix_len + p * 2 * heads : prefix_len + (p + 1) * 2 * heads]
                     for p in range(prefix_len // HD)
                 ],
                 axis=1,
@@ -224,7 +214,7 @@
             value = jnp.sum(jnp.where(fold_mine, value, 0.0), axis=0, keepdims=True)
             value = (value + own_value * own_weight) / denom
             score = sum(value[:, h * slots : (h + 1) * slots] for h in range(mine))
-            scores[owner, pl.ds(board, 1), :] = jnp.where(listed[j] > 0, score, DEAD)
+            scores[j, pl.ds(board, 1), :] = jnp.where(listed[j] > 0, score, DEAD)
         return carry
 
     lax.fori_loop(0, boards, step, 0)
@@ -335,27 +325,25 @@
         functools.partial(list_moves, plan),
         as_index(line_at * pair + pair_at),
         (move_board, board_row, move_ids.reshape(1, row_count)),
-        (shape((groups, line, pair, share, plan.slots), F32), shape((1, row_count), jnp.int32)),
+        (shape((board_total, plan.slots), F32), shape((1, row_count), jnp.int32)),
         [],
         32,
+        pl.CostEstimate(flops=10**8, bytes_accessed=10**5, transcendentals=0),
     )
     everywhere = ("groups", "line", "pair")
-    listed = lax.all_to_all(
-        listed.reshape(groups * plan.peers, share, plan.slots), everywhere, split_axis=0, concat_axis=0, tiled=True
-    )
-    listed = jnp.sum(listed.reshape(groups, plan.peers, share, plan.slots), axis=1)
-    listed = listed.astype(jnp.int32).reshape(plan.slab, boards_here, plan.slots)
+    listed = lax.all_gather(listed, everywhere)
+    listed = listed.reshape(groups, plan.peers, line, share, plan.slots)
+    listed = lax.dynamic_index_in_dim(listed, line_at, axis=2, keepdims=False)
+    listed = jnp.sum(listed, axis=1).astype(jnp.int32).reshape(plan.slab, boards_here, plan.slots)
 
     pieces = prefix_len // HD
     payload = pl.pallas_call(
         pack_prefix,
         out_shape=shape((boards_here, prefix_len + pieces * 2 * heads, HD), BF16),
         compiler_params=limits(32),
+        cost_estimate=pl.CostEstimate(flops=10**8, bytes_accessed=2 * 10**6, transcendentals=0),
     )(prefix_kv, ws)
-    payloads = [payload]
-    for step in range(1, plan.slab):
-        swap = [(at, at ^ step) for at in range(plan.slab)]
-        payloads.append(lax.ppermute(payload, ("groups", "pair"), swap))
+    payloads = lax.all_gather(payload, ("groups", "pair"))
 
     block = min(moves, 128)
     normed = pl.pallas_call(
@@ -365,6 +353,9 @@
         in_specs=[pl.BlockSpec((block, width), lambda i: (i, 0)), pl.BlockSpec((1, width), lambda i: (0, 0))],
         out_specs=pl.BlockSpec((block, width), lambda i: (i, 0)),
         compiler_params=limits(32),
+        cost_estimate=pl.CostEstimate(
+            flops=8 * moves * width, bytes_accessed=4 * moves * width, transcendentals=moves
+        ),
     )(move_table, norm_gain.reshape(1, width))
     turns = jnp.asarray(turn_table(prefix_len))
     my_turns = jnp.tile(lax.dynamic_slice_in_dim(turns, line_at * plan.pairs, plan.pairs, axis=0), (plan.mine, 1))
@@ -375,7 +366,7 @@
         functools.partial(project, plan),
         out_shape=(
             shape((line, plan.q_rows, moves), BF16),
-            shape((groups * plan.peers, plan.k_rows, moves), BF16),
+            shape((plan.k_rows, moves), BF16),
             shape((plan.mine, moves), F32),
         ),
         grid=(moves // block,),
@@ -386,13 +377,16 @@
         ],
         out_specs=(
             pl.BlockSpec((line, plan.q_rows, block), lambda i: (0, 0, i)),
-            pl.BlockSpec((groups * plan.peers, plan.k_rows, block), lambda i: (0, 0, i)),
+            pl.BlockSpec((plan.k_rows, block), lambda i: (0, i)),
             pl.BlockSpec((plan.mine, block), lambda i: (0, i)),
         ),
         compiler_params=limits(40),
+        cost_estimate=pl.CostEstimate(
+            flops=2 * moves * width * 256, bytes_accessed=2 * moves * width, transcendentals=0
+        ),
     )(weights, normed, my_turns)
     queries = lax.all_to_all(queries, "line", split_axis=0, concat_axis=0, tiled=True)
-    keys = lax.all_to_all(keys, everywhere, split_axis=0, concat_axis=0, tiled=True)
+    keys = lax.all_gather(keys, everywhere)
 
     query_rows = plan.mine * HD
     back = plan.peers * lax.axis_size("tensor")
@@ -405,7 +399,7 @@
             keys.reshape(HD, moves),
             turns,
             own_values,
-            *payloads,
+            payloads,
             listed,
         ),
         shape((groups, back, share, plan.slots), F32),

time: 124 us -> 169 us (1.36)
  blocking collectives: 31.1 us -> 95.5 us
  waiting for transfers between devices: 37.3 us -> 5.18 us
  between operations: 0.17 us -> 13.5 us
  starting transfers between devices: 19 us -> 10.7 us
  local copies, waits for them, and re-layouts: 9.16 us -> 17.4 us
    all_gather x0 -> x2, blocking collectives: none -> 83.5 us  [the longest x1 44.2 us: per_device(): listed = lax.all_gather(listed, everywhere)]
    ppermute x3 -> x0, waiting for transfers between devices: 23.2 us -> none  [per_device(): payloads.append(lax.ppermute(payload, ('groups', 'pair'), swap))]
    all_to_all x1 -> x0, blocking collectives: 16.2 us -> none  [per_device(): lax.all_to_all(keys, everywhere, split_axis=0, concat_axis=0, tiled=True)]
    all_to_all x1, waiting for transfers between devices: 14.1 us -> 5.16 us  [per_device(): lax.all_to_all(packed, ('line', 'pair'), split_axis=0, concat_axis=0, til...]
    unnamed x23 -> x27, local copies, waits for them, and re-layouts: 8.44 us -> 16.7 us
    all_to_all x1 -> x0, starting transfers between devices: 4.69 us -> none  [per_device(): lax.all_to_all(listed.reshape(groups * plan.peers, share, plan.slots), ev...]
    ppermute x3 -> x0, starting transfers between devices: 3.54 us -> none  [per_device(): payloads.append(lax.ppermute(payload, ('groups', 'pair'), swap))]
    all_to_all x1, blocking collectives: 14.9 us -> 12 us  [per_device(): lax.all_to_all(parts.reshape(groups * back, share, plan.slots), ('groups'...]
  transfers between devices with their start and end apart: 6 -> 3, of which waited for: 3 -> 1; matrix products, arithmetic and copies ran while one was open for 1% -> 1% of each run, Pallas kernels for 8% -> 6%
where the time goes in v2:
time: 169 us; the launch traced here: 168 us
  blocking collectives  95.5 us (57%)
  Pallas kernels  26.1 us (15%)
  local copies, waits for them, and re-layouts  17.4 us (10%)
  between operations  13.5 us (8%)
  starting transfers between devices  10.7 us (6%)
  waiting for transfers between devices  5.18 us (3%)
    all_gather x1, blocking collectives, per_device(): listed = lax.all_gather(listed, everywhere)  44.2 us
    all_gather x1, blocking collectives, per_device(): keys = lax.all_gather(keys, everywhere)  39.3 us
    unnamed x27, local copies, waits for them, and re-layouts  16.7 us
    pallas_call x3, Pallas kernels, scalar_call(): pl.pallas_call(kernel, out_shape=outs, grid_spec=pltpu.PrefetchScalarGrid...  15.5 us
    all_to_all x1, blocking collectives, per_device(): lax.all_to_all(parts.reshape(groups * back, share, plan.slots), ('groups'...  12 us
    all_to_all x1, starting transfers between devices, per_device(): lax.all_to_all(packed, ('line', 'pair'), split_axis=0, concat_axis=0, til...  7.25 us
    all_to_all x1, waiting for transfers between devices, per_device(): lax.all_to_all(packed, ('line', 'pair'), split_axis=0, concat_axis=0, til...  5.16 us
    pallas_call x1, Pallas kernels, per_device(): pl.pallas_call(normalize, out_shape=shape((moves, width), BF16), grid=(mo...  4.78 us
  transfers between devices with their start and end apart: 3, of which 1 were waited for; matrix products, arithmetic and copies ran while one was open for 1% of the time, Pallas kernels for 6%

profile of v2, /device:TPU:0, one launch (start us, length us, event | category | flops | bytes accessed | tf_op | source)
XLA Modules:
  0.0 168.5 jit_solution(18339448029488010528)
XLA Ops:
  6.5 1.2 copy-done.4
  7.8 0.7 copy-done.9
  8.4 1.1 shard_map.103
  9.6 1.2 copy-done.5
  10.8 0.9 copy-done.6
  11.7 0.7 copy-done.10
  12.4 1.6 shard_map.100
  14.0 7.3 %all-to-all-start = ((bf16[8,80,512]{2,1,0:T(8,128)(2,1)}), bf16[8,80,512]{2,1,0:T(8,128)(2,1)S(1)}, u32[]{:S(2)}, u32[]{:S(2)}) async-start(bf16[8,80,512]{2,1,0:T(8,128)(2,1)} %shard_map.100), calls=%async_computation | async-start | bytes 1310720 | tf_op jit(solution)/shard_map/all_to_all | solution.py:320
  21.2 0.7 reshape.49.gain_ref
  22.0 3.4 %copy-done.2 = bf16[1024,4096]{1,0:T(8,128)(2,1)S(1)} copy-done((bf16[1024,4096]{1,0:T(8,128)(2,1)S(1)}, bf16[1024,4096]{1,0:T(8,128)(2,1)}, u32[]{:S(2)}) %copy-start.2) | copy-done | bytes 8388632
  25.3 4.8 %shard_map.101.normed_ref = bf16[1024,4096]{1,0:T(8,128)(2,1)S(1)} custom-call(bf16[1024,4096]{1,0:T(8,128)(2,1)S(1)} %copy-done.2, bf16[1,4096]{1,0:T(2,128)(2,1)S(1)} %reshape.49.gain_ref), custom_call_target="tpu_custom_call" | custom-call | flops 33554432 | bytes 16777216 | tf_op jit(solution)/shard_map/pallas_call | solution.py:349
  30.1 3.2 %copy-done = bf16[1024,4096]{1,0:T(8,128)(2,1)} copy-done((bf16[1024,4096]{1,0:T(8,128)(2,1)}, bf16[1024,4096]{1,0:T(8,128)(2,1)S(1)}, u32[]{:S(2)}) %copy-start) | copy-done | bytes 8388632
  33.4 5.2 %all-to-all-done.w_ref = bf16[8,80,512]{2,1,0:T(8,128)(2,1)S(1)} async-done(((bf16[8,80,512]{2,1,0:T(8,128)(2,1)}), bf16[8,80,512]{2,1,0:T(8,128)(2,1)S(1)}, u32[]{:S(2)}, u32[]{:S(2)}) %all-to-all-start) | async-done | bytes 655392 | tf_op jit(solution)/shard_map/all_to_all | solution.py:320
  38.5 3.5 %copy-done.1 = bf16[1024,4096]{1,0:T(8,128)(2,1)S(1)} copy-done((bf16[1024,4096]{1,0:T(8,128)(2,1)S(1)}, bf16[1024,4096]{1,0:T(8,128)(2,1)}, u32[]{:S(2)}) %copy-start.1) | copy-done | bytes 8388632
  42.0 3.8 %shard_map.102 = (bf16[4,64,1024]{2,1,0:T(8,128)(2,1)}, bf16[8,1024]{1,0:T(8,128)(2,1)S(1)}, f32[2,1024]{1,0:T(2,128)S(1)}) custom-call(bf16[8,80,512]{2,1,0:T(8,128)(2,1)S(1)} %all-to-all-done.w_ref, bf16[1024,4096]{1,0:T(8,128)(2,1)S(1)} %copy-done.1, f32[32,2]{1,0:T(8,128)S(1)} %bitcast.19), custom_call_target="tpu_custom_call" | custom-call | flops 2147483648 | bytes 8388608 | tf_op jit(solution)/shard_map/pallas_call | solution.py:365
  45.8 3.5 %all-to-all-start.1 = ((bf16[4,64,1024]{2,1,0:T(8,128)(2,1)}), bf16[4,64,1024]{2,1,0:T(8,128)(2,1)S(1)}, u32[]{:S(2)}, u32[]{:S(2)}) async-start(bf16[4,64,1024]{2,1,0:T(8,128)(2,1)} %get-tuple-element.10), calls=%async_computation.1 | async-start | bytes 1048576 | tf_op jit(solution)/shard_map/all_to_all | solution.py:388
  49.3 0.1 copy.16.board_col_ref
  49.5 0.3 shard_map.104
  49.8 44.2 %all-gather.2 = f32[1024,128]{1,0:T(8,128)S(1)} all-gather(f32[64,128]{1,0:T(8,128)S(1)} %get-tuple-element.13), channel_id=4, replica_groups=mesh['groups'=2,'line'=4,'pair'=2,'tensor'=2] {'groups','line','pair'}, dimensions={0}, use_global_device_ids=true | all-gather | bytes 557056 | tf_op jit(solution)/shard_map/all_gather | solution.py:334
  94.1 39.3 %all-gather.k_ref = bf16[128,1024]{1,0:T(8,128)(2,1)S(1)} all-gather(bf16[8,1024]{1,0:T(8,128)(2,1)S(1)} %get-tuple-element.11), channel_id=2, replica_groups=mesh['groups'=2,'line'=4,'pair'=2,'tensor'=2] {'groups','line','pair'}, dimensions={0}, use_global_device_ids=true | all-gather | bytes 278528 | tf_op jit(solution)/shard_map/all_gather | solution.py:389
  133.3 1.7 copy-done.3
  135.0 13.5 %shard_map.105 = f32[2,16,16,128]{3,2,1,0:T(8,128)S(1)} custom-call(s32[1]{0:T(128)} %bitcast.at_ref, bf16[256,1024]{1,0:T(8,128)(2,1)S(1)} %bitcast.15, bf16[256,256]{1,0:T(8,128)(2,1)S(1)} %copy-done.7, bf16[128,1024]{1,0:T(8,128)(2,1)S(1)} %all-gather.k_ref, f32[64,2]{1,0:T(8,128)S(1)} %copy-done.8, f32[2,1024]{1,0:T(2,128)S(1)} %get-tuple-element.12.vo_ref, ...), custom_call_target="tpu_custom_call" | custom-call | tf_op jit(solution)/shard_map/pallas_call | solution.py:257
  148.6 12.0 %all_to_all.15 = f32[32,16,128]{2,1,0:T(8,128)S(1)} all-to-all(f32[32,16,128]{2,1,0:T(8,128)S(1)} %bitcast.17), channel_id=1, replica_groups=mesh['groups'=2,'line'=4,'pair'=2,'tensor'=2] {'groups','line','pair','t..., dimensions={0} | all-to-all | bytes 524288 | tf_op jit(solution)/shard_map/all_to_all | solution.py:413
  160.6 1.1 shard_map.106
  (25 shorter events, 0.1 us)
Async XLA Ops:
  6.5 126.8 %all-gather.5.cloned.1.call-start = ((), (), s32[]{:S(2)}) async-start(), calls=%async_computation.3 | async-start | bytes 2949120 | tf_op jit(solution)/shard_map/all_gather | solution.py:346
  6.5 1.2 copy-start.4
  7.8 0.7 copy-start.9
  9.6 1.2 copy-start.5
  10.8 0.9 copy-start.6
  11.7 0.7 copy-start.10
  14.0 24.5 %all-to-all-start = ((bf16[8,80,512]{2,1,0:T(8,128)(2,1)}), bf16[8,80,512]{2,1,0:T(8,128)(2,1)S(1)}, u32[]{:S(2)}, u32[]{:S(2)}) async-start(bf16[8,80,512]{2,1,0:T(8,128)(2,1)} %shard_map.100), calls=%async_computation | async-start | bytes 1310720 | tf_op jit(solution)/shard_map/all_to_all | solution.py:320
  21.9 3.4 %copy-start.2 = (bf16[1024,4096]{1,0:T(8,128)(2,1)S(1)}, bf16[1024,4096]{1,0:T(8,128)(2,1)}, u32[]{:S(2)}) copy-start(bf16[1024,4096]{1,0:T(8,128)(2,1)} %table_ref.1) | copy-start | bytes 25165828
  25.3 8.0 %copy-start.8 = (f32[64,2]{1,0:T(8,128)S(1)}, f32[64,2]{1,0:T(8,128)}, u32[]{:S(2)}) copy-start(f32[64,2]{1,0:T(8,128)} %constant.32.clone.turn_ref) | copy-start | bytes 1540
  25.3 108.0 %copy-start.7 = (bf16[256,256]{1,0:T(8,128)(2,1)S(1)}, bf16[256,256]{1,0:T(8,128)(2,1)}, u32[]{:S(2)}) copy-start(bf16[256,256]{1,0:T(8,128)(2,1)} %constant.33.clone.order_ref) | copy-start | bytes 393220
  30.1 3.2 %copy-start = (bf16[1024,4096]{1,0:T(8,128)(2,1)}, bf16[1024,4096]{1,0:T(8,128)(2,1)S(1)}, u32[]{:S(2)}) copy-start(bf16[1024,4096]{1,0:T(8,128)(2,1)S(1)} %shard_map.101.normed_ref) | copy-start | bytes 25165828
  33.4 15.9 %copy-start.11 = (s32[512,1]{0,1:T(1,128)S(1)}, s32[512,1]{0,1:T(1,128)}, u32[]{:S(2)}) copy-start(s32[512,1]{0,1:T(1,128)} %param.12) | copy-start | bytes 6148
  33.4 16.1 %copy-start.12 = (s32[512]{0:T(512)S(1)}, s32[512]{0:T(512)}, u32[]{:S(2)}) copy-start(s32[512]{0:T(512)} %param.11) | copy-start | bytes 6148
  38.5 3.5 %copy-start.1 = (bf16[1024,4096]{1,0:T(8,128)(2,1)S(1)}, bf16[1024,4096]{1,0:T(8,128)(2,1)}, u32[]{:S(2)}) copy-start(bf16[1024,4096]{1,0:T(8,128)(2,1)} %copy-done) | copy-start | bytes 25165828
  45.8 87.5 %all-to-all-start.1 = ((bf16[4,64,1024]{2,1,0:T(8,128)(2,1)}), bf16[4,64,1024]{2,1,0:T(8,128)(2,1)S(1)}, u32[]{:S(2)}, u32[]{:S(2)}) async-start(bf16[4,64,1024]{2,1,0:T(8,128)(2,1)} %get-tuple-element.10), calls=%async_computation.1 | async-start | bytes 1048576 | tf_op jit(solution)/shard_map/all_to_all | solution.py:388
  133.3 1.7 copy-start.3
Sparse Core Ops, SparseCore 0:
  9.7 47.5 all-gather.4

commit v3 on v2

--- a/solution.py
+++ b/solution.py
@@ -15,6 +15,7 @@
 EPS = 1e-06
 THETA = 5000000.0
 DEAD = -1e30
+VMEM_MIB = 52
 
 F32 = jnp.float32
 BF16 = jnp.bfloat16
@@ -73,7 +74,8 @@
         column = jnp.where(is_q, column, -1)
         at = pl.ds(pl.multiple_of(peer * rows, 16), rows)
         pick[at, :half_cols] = jnp.where(q_lane == column, 1.0, 0.0).astype(BF16)
-        k_column = jnp.where(is_k, (group * plan.peers + peer) * plan.k_rows + k_at, -1)
+        chip = line * plan.slab + group * plan.pair + pair
+        k_column = jnp.where(is_k, chip * plan.k_rows + k_at, -1)
         pick[at, half_cols : half_cols + HD] = jnp.where(k_lane == k_column, 1.0, 0.0).astype(BF16)
         fold = jnp.zeros((rows, HD), F32)
         my_head = jnp.where(is_f, (group * plan.pair + pair) * plan.mine + f_head, -1)
@@ -92,13 +94,14 @@
         out_ref[peer] = jnp.where(is_rest, rest[at].astype(F32), rounded[at].astype(F32)).astype(BF16)
 
 
-def normalize(table_ref, gain_ref, out_ref):
+def normalize(table_ref, gain_ref, after_ref, out_ref):
     raw = table_ref[...].astype(F32)
     inverse = lax.rsqrt(jnp.mean(raw * raw, axis=-1, keepdims=True) + EPS)
     out_ref[...] = (raw * inverse * gain_ref[...].astype(F32)).astype(BF16)
 
 
-def project(plan, w_ref, normed_ref, turn_ref, q_ref, k_ref, vo_ref):
+def project(plan, w_ref, normed_ref, turn_ref, *rest):
+    q_ref, k_ref, vo_ref = rest[-3:]
     if len(w_ref.shape) == 3:
         depth = w_ref.shape[2]
         total = sum(
@@ -119,21 +122,24 @@
         vo_ref[h : h + 1, :] = total[base + 2 * h : base + 2 * h + 1] + total[base + 2 * h + 1 : base + 2 * h + 2]
 
 
-def pack_prefix(prefix_ref, ws_ref, out_ref):
-    prefix_len = prefix_ref.shape[1]
+def pack_prefix(prefix_ref, ws_ref, after_ref, out_ref):
+    boards = prefix_ref.shape[0]
     heads = ws_ref.shape[0]
-    for board in range(prefix_ref.shape[0]):
-        out_ref[board, :prefix_len] = prefix_ref[board, :, :HD]
-        fold = matmul(ws_ref[...], prefix_ref[board, :, HD:], NT)
-        rounded = fold.astype(BF16)
-        rest = fold - rounded.astype(F32)
-        both = jnp.concatenate([rounded.astype(F32), rest], axis=0).astype(BF16)
-        for piece in range(prefix_len // HD):
-            at = prefix_len + piece * 2 * heads
-            out_ref[board, at : at + 2 * heads] = both[:, piece * HD : (piece + 1) * HD]
-
-
-def list_moves(plan, at_ref, board_col_ref, board_row_ref, ids_ref, out_ref, slot_ref):
+    span = HD // boards
+    ws = jnp.concatenate([ws_ref[...].astype(F32)] * (HD // heads), axis=0)
+    row = lax.broadcasted_iota(jnp.int32, (HD, 1), 0)
+    fold = None
+    for board in range(boards):
+        out_ref[board] = prefix_ref[board, :, :HD]
+        keep = (row // span == board) & (row % span < 2 * heads)
+        term = matmul(prefix_ref[board, :, HD:], jnp.where(keep, ws, 0.0).astype(BF16), NT)
+        fold = term if fold is None else fold + term
+    rounded = fold.astype(BF16).astype(F32)
+    lane = lax.broadcasted_iota(jnp.int32, fold.shape, 1)
+    out_ref[boards] = jnp.where(lane % span < heads, rounded, fold - rounded).astype(BF16)
+
+
+def list_moves(plan, at_ref, board_col_ref, board_row_ref, ids_ref, after_ref, out_ref, slot_ref):
     count = board_col_ref.shape[0]
     same = board_col_ref[...] == board_row_ref[...]
     other = lax.broadcasted_iota(jnp.int32, (count, count), 0)
@@ -142,26 +148,30 @@
     slot = rank.astype(jnp.int32) + at_ref[0] * plan.capacity
     slot_ref[...] = slot
     slots_in = lax.broadcasted_iota(jnp.int32, (plan.slots, count), 0) == slot
-    boards = out_ref.shape[0]
+    boards = out_ref.shape[0] * out_ref.shape[1]
     member = lax.broadcasted_iota(jnp.int32, (boards, count), 0) == board_row_ref[...]
     move = ids_ref[...] + 1
     high, low = (move // 64).astype(F32), (move % 64).astype(F32)
     slots_in = jnp.where(slots_in, 1.0, 0.0).astype(BF16)
     listed = 64.0 * matmul(jnp.where(member, high, 0.0).astype(BF16), slots_in, NT)
     listed = listed + matmul(jnp.where(member, low, 0.0).astype(BF16), slots_in, NT)
-    out_ref[...] = listed
-
-
-def attend(plan, at_ref, q_ref, order_ref, k_ref, turn_ref, vo_ref, prefix_ref, moves_ref, out_ref, table, extra, scores):
-    here = at_ref[0]
+    out_ref[...] = listed.reshape(out_ref.shape)
+
+
+def attend(plan, at_ref, q_ref, order_ref, k_ref, turn_ref, vo_ref, *rest):
+    prefix_refs = rest[: plan.slab]
+    moves_ref, out_ref, table, extra, scores = rest[plan.slab :]
+    here, chip = at_ref[0], at_ref[1]
     mine, heads, slots = plan.mine, plan.heads, plan.slots
     moves = q_ref.shape[1]
-    boards = prefix_ref.shape[1]
-    prefix_len = prefix_ref.shape[2] * HD // (HD + 2 * heads)
+    boards = prefix_refs[0].shape[0] - 1
     query_rows = mine * HD
 
     table[:query_rows] = matmul(order_ref[...], q_ref[...]).astype(BF16)
-    key = k_ref[...].astype(F32)
+    row = lax.broadcasted_iota(jnp.int32, (HD, HD), 0)
+    source = ((row // plan.k_rows) ^ chip) * plan.k_rows + row % plan.k_rows
+    pick = jnp.where(lax.broadcasted_iota(jnp.int32, (HD, HD), 1) == source, 1.0, 0.0).astype(BF16)
+    key = matmul(pick, k_ref[...])
     first, second = key[:HALF], key[HALF:]
     cosine, sine = turn_ref[:, 0:1], turn_ref[:, 1:2]
     key_first, key_second = first * cosine - second * sine, second * cosine + first * sine
@@ -179,49 +189,41 @@
     scale = math.log2(math.e) / math.sqrt(HD)
     move_at = lax.broadcasted_iota(jnp.int32, (moves, slots), 0) + 1
     lanes = mine * slots
-    fold_at = lax.broadcasted_iota(jnp.int32, (2 * heads, lanes), 0)
-    fold_head = here * mine + lax.broadcasted_iota(jnp.int32, (2 * heads, lanes), 1) // slots
-    fold_mine = (fold_at == fold_head) | (fold_at == fold_head + heads)
+    span = HD // boards
+    fold_row = lax.broadcasted_iota(jnp.int32, (HD, lanes), 0)
+    fold_head = here * mine + lax.broadcasted_iota(jnp.int32, (HD, lanes), 1) // slots
 
     def per_head(x, base):
         pieces = [x[base + h : base + h + 1] + x[base + mine + h : base + mine + h + 1] for h in range(mine)]
         return jnp.concatenate(pieces, axis=1)
 
     def step(board, carry):
-        listed = []
-        for j in range(plan.slab):
-            listed.append(moves_ref[j, pl.ds(board, 1), :])
+        listed = [moves_ref[here ^ j, pl.ds(board, 1), :] for j in range(plan.slab)]
         chosen = [jnp.where(move_at == row, 1.0, 0.0).astype(BF16) for row in listed]
         taken = matmul(table[...], jnp.concatenate(chosen, axis=1))
+        at = fold_row - board * span
+        fold_pick = jnp.where((at == fold_head) | (at == fold_head + heads), 1.0, 0.0).astype(BF16)
         for j in range(plan.slab):
             x = taken[:, j * slots : (j + 1) * slots]
             q = jnp.concatenate([x[h * HD : (h + 1) * HD].astype(BF16) for h in range(mine)], axis=1)
-            logits = matmul(prefix_ref[j, board, :prefix_len], q)
+            logits = matmul(prefix_refs[j][board], q)
+            fold = matmul(prefix_refs[j][boards], fold_pick)
             own_logit = per_head(x, query_rows)
             own_value = per_head(x, query_rows + 2 * mine)
             peak = jnp.maximum(jnp.max(logits, axis=0, keepdims=True), own_logit)
             weight = jnp.exp2((logits - peak) * scale)
             own_weight = jnp.exp2((own_logit - peak) * scale)
             denom = jnp.sum(weight, axis=0, keepdims=True) + own_weight
-            fold = jnp.concatenate(
-                [
-                    prefix_ref[j, board, prefix_len + p * 2 * heads : prefix_len + (p + 1) * 2 * heads]
-                    for p in range(prefix_len // HD)
-                ],
-                axis=1,
-            )
-            value = matmul(fold, weight.astype(BF16))
-            value = jnp.sum(jnp.where(fold_mine, value, 0.0), axis=0, keepdims=True)
-            value = (value + own_value * own_weight) / denom
+            value = (jnp.sum(weight * fold, axis=0, keepdims=True) + own_value * own_weight) / denom
             score = sum(value[:, h * slots : (h + 1) * slots] for h in range(mine))
-            scores[j, pl.ds(board, 1), :] = jnp.where(listed[j] > 0, score, DEAD)
+            scores[here ^ j, pl.ds(board, 1), :] = jnp.where(listed[j] > 0, score, DEAD)
         return carry
 
     lax.fori_loop(0, boards, step, 0)
     for g in range(plan.groups):
-        mine_all = jnp.concatenate([scores[g * plan.pair + p] for p in range(plan.pair)], axis=0)
+        both = jnp.concatenate([scores[g * plan.pair + p] for p in range(plan.pair)], axis=0)
         for copy in range(out_ref.shape[1]):
-            out_ref[g, copy] = mine_all
+            out_ref[g, copy] = both
 
 
 def finish(plan, parts_ref, board_ref, slot_ref, out_ref):
@@ -251,7 +253,11 @@
     out_ref[...] = jnp.sum(jnp.where(at, found, 0.0), axis=0, keepdims=True)
 
 
-def scalar_call(kernel, at, args, outs, scratch, mib, cost=None, specs=None):
+def untouched():
+    return pl.BlockSpec(memory_space=pl.ANY)
+
+
+def scalar_call(kernel, at, args, outs, scratch, cost=None, specs=None):
     whole = lambda x: pl.BlockSpec(x.shape, lambda i, at, n=len(x.shape): (0,) * n)
     specs = specs or {}
     return pl.pallas_call(
@@ -264,9 +270,21 @@
             out_specs=jax.tree.map(whole, outs),
             scratch_shapes=scratch,
         ),
-        compiler_params=limits(mib),
+        compiler_params=limits(VMEM_MIB),
         cost_estimate=cost,
     )(at, *args)
+
+
+def cost(flops, nbytes):
+    return pl.CostEstimate(flops=int(flops), bytes_accessed=int(nbytes), transcendentals=0)
+
+
+def swap(x, names, size, step):
+    return lax.ppermute(x, names, [(at, at ^ step) for at in range(size)])
+
+
+def gather_near(x, names, size):
+    return jnp.concatenate([x] + [swap(x, names, size, step) for step in range(1, size)], axis=0)
 
 
 def shape(dims, dtype):
@@ -304,59 +322,70 @@
     line_at = lax.axis_index("line").astype(jnp.int32)
     pair_at = lax.axis_index("pair").astype(jnp.int32)
     slab_at = group_at * pair + pair_at
-    as_index = lambda x: x.reshape(1)
     ws = w_score.reshape(heads, HD)
+    slab_axes = ("groups", "pair")
 
     half_cols = w_query.shape[1] // groups
     packed = scalar_call(
         functools.partial(pack_weights, plan),
-        as_index(group_at),
+        group_at.reshape(1),
         (w_query, w_keyval, ws),
         shape((plan.peers, plan.rows, depth), BF16),
         [pltpu.VMEM((plan.peers * plan.rows, half_cols + 2 * HD), BF16)],
-        32,
-        specs={0: pl.BlockSpec((depth, half_cols), lambda i, at: (0, at[0]))},
+        cost(2 * plan.peers * plan.rows * half_cols * depth, 4 * w_query.size),
+        {0: pl.BlockSpec((depth, half_cols), lambda i, at: (0, at[0]))},
     )
     weights = lax.all_to_all(packed, ("line", "pair"), split_axis=0, concat_axis=0, tiled=True)
+
+    payload = pl.pallas_call(
+        pack_prefix,
+        out_shape=shape((boards_here + 1, prefix_len, HD), BF16),
+        in_specs=[pl.BlockSpec(memory_space=pltpu.VMEM), pl.BlockSpec(memory_space=pltpu.VMEM), untouched()],
+        compiler_params=limits(VMEM_MIB),
+        cost_estimate=cost(2 * prefix_len * HD * HD * boards_here, 2 * prefix_kv.size),
+    )(prefix_kv, ws, packed)
+    beside = swap(payload, slab_axes, plan.slab, 1)
+    across = swap(payload, slab_axes, plan.slab, 2)
 
     board_row = move_board.reshape(1, row_count)
     share = pair * boards_here
     listed, slot_row = scalar_call(
         functools.partial(list_moves, plan),
-        as_index(line_at * pair + pair_at),
-        (move_board, board_row, move_ids.reshape(1, row_count)),
-        (shape((board_total, plan.slots), F32), shape((1, row_count), jnp.int32)),
+        (line_at * pair + pair_at).reshape(1),
+        (move_board, board_row, move_ids.reshape(1, row_count), packed),
+        (shape((line, share, plan.slots), F32), shape((1, row_count), jnp.int32)),
         [],
-        32,
-        pl.CostEstimate(flops=10**8, bytes_accessed=10**5, transcendentals=0),
+        cost(8 * row_count * row_count, 4 * board_total * plan.slots),
+        {3: untouched()},
     )
-    everywhere = ("groups", "line", "pair")
-    listed = lax.all_gather(listed, everywhere)
-    listed = listed.reshape(groups, plan.peers, line, share, plan.slots)
-    listed = lax.dynamic_index_in_dim(listed, line_at, axis=2, keepdims=False)
-    listed = jnp.sum(listed, axis=1).astype(jnp.int32).reshape(plan.slab, boards_here, plan.slots)
-
-    pieces = prefix_len // HD
-    payload = pl.pallas_call(
-        pack_prefix,
-        out_shape=shape((boards_here, prefix_len + pieces * 2 * heads, HD), BF16),
-        compiler_params=limits(32),
-        cost_estimate=pl.CostEstimate(flops=10**8, bytes_accessed=2 * 10**6, transcendentals=0),
-    )(prefix_kv, ws)
-    payloads = lax.all_gather(payload, ("groups", "pair"))
+    remaining = line
+    while remaining > 1:
+        remaining //= 2
+        upper = (line_at // remaining) % 2
+        kept = lax.dynamic_slice_in_dim(listed, upper * remaining, remaining, axis=0)
+        given = lax.dynamic_slice_in_dim(listed, (1 - upper) * remaining, remaining, axis=0)
+        listed = kept + swap(given, "line", line, remaining)
+    listed = listed[0]
+    turned = [listed] + [swap(listed, slab_axes, plan.slab, step) for step in range(1, plan.slab)]
+    same = sum(turned[:pair])
+    other = sum(turned[pair:])
+    listed = jnp.where(group_at == 0, jnp.stack([same, other]), jnp.stack([other, same]))
+    listed = listed.astype(jnp.int32).reshape(plan.slab, boards_here, plan.slots)
 
     block = min(moves, 128)
     normed = pl.pallas_call(
         normalize,
         out_shape=shape((moves, width), BF16),
         grid=(moves // block,),
-        in_specs=[pl.BlockSpec((block, width), lambda i: (i, 0)), pl.BlockSpec((1, width), lambda i: (0, 0))],
+        in_specs=[
+            pl.BlockSpec((block, width), lambda i: (i, 0)),
+            pl.BlockSpec((1, width), lambda i: (0, 0)),
+            untouched(),
+        ],
         out_specs=pl.BlockSpec((block, width), lambda i: (i, 0)),
-        compiler_params=limits(32),
-        cost_estimate=pl.CostEstimate(
-            flops=8 * moves * width, bytes_accessed=4 * moves * width, transcendentals=moves
-        ),
-    )(move_table, norm_gain.reshape(1, width))
+        compiler_params=limits(VMEM_MIB),
+        cost_estimate=cost(8 * moves * width, 4 * moves * width),
+    )(move_table, norm_gain.reshape(1, width), packed)
     turns = jnp.asarray(turn_table(prefix_len))
     my_turns = jnp.tile(lax.dynamic_slice_in_dim(turns, line_at * plan.pairs, plan.pairs, axis=0), (plan.mine, 1))
     if depth % HD:
@@ -374,32 +403,42 @@
             pl.BlockSpec(weights.shape, lambda i, n=weights.ndim: (0,) * n),
             pl.BlockSpec((block, width), lambda i: (i, 0)),
             pl.BlockSpec(my_turns.shape, lambda i: (0, 0)),
+            untouched(),
+            untouched(),
+            untouched(),
         ],
         out_specs=(
             pl.BlockSpec((line, plan.q_rows, block), lambda i: (0, 0, i)),
             pl.BlockSpec((plan.k_rows, block), lambda i: (0, i)),
             pl.BlockSpec((plan.mine, block), lambda i: (0, i)),
         ),
-        compiler_params=limits(40),
-        cost_estimate=pl.CostEstimate(
-            flops=2 * moves * width * 256, bytes_accessed=2 * moves * width, transcendentals=0
-        ),
-    )(weights, normed, my_turns)
+        compiler_params=limits(VMEM_MIB),
+        cost_estimate=cost(2 * moves * width * 256, 2 * moves * width),
+    )(weights, normed, my_turns, beside, across, listed)
     queries = lax.all_to_all(queries, "line", split_axis=0, concat_axis=0, tiled=True)
-    keys = lax.all_gather(keys, everywhere)
+    diagonal = swap(beside, slab_axes, plan.slab, 2)
+    keys = gather_near(keys, slab_axes, plan.slab)
+    bit = 1
+    while bit < line:
+        size = min(4, line // bit)
+        keys = jnp.concatenate([keys] + [swap(keys, "line", line, at * bit) for at in range(1, size)], axis=0)
+        bit *= size
 
     query_rows = plan.mine * HD
     back = plan.peers * lax.axis_size("tensor")
     parts = scalar_call(
         functools.partial(attend, plan),
-        as_index(slab_at),
+        jnp.stack([slab_at, line_at * plan.slab + slab_at]),
         (
             queries.reshape(query_rows, moves),
             jnp.asarray(entry_order(plan), BF16),
-            keys.reshape(HD, moves),
+            keys,
             turns,
             own_values,
-            payloads,
+            payload,
+            beside,
+            across,
+            diagonal,
             listed,
         ),
         shape((groups, back, share, plan.slots), F32),
@@ -408,7 +447,7 @@
             pltpu.VMEM((16, moves), F32),
             pltpu.VMEM((plan.slab, boards_here, plan.slots), F32),
         ],
-        48,
+        cost(2 * 272 * moves * 4096, 4 * 10**6),
     )
     parts = lax.all_to_all(
         parts.reshape(groups * back, share, plan.slots),
@@ -419,7 +458,7 @@
     )
     parts = parts.reshape(groups, line, back // line, share, plan.slots)
     logprob = pl.pallas_call(
-        functools.partial(finish, plan), out_shape=shape((1, row_count), F32), compiler_params=limits(32)
+        functools.partial(finish, plan), out_shape=shape((1, row_count), F32), compiler_params=limits(VMEM_MIB)
     )(parts, board_row, slot_row)
     return logprob.reshape(row_count)
 

time: 169 us -> 103 us (0.61)
  blocking collectives: 95.5 us -> 12.8 us
  starting transfers between devices: 10.7 us -> 30.6 us
  between operations: 13.5 us -> 0.24 us
  waiting for transfers between devices: 5.18 us -> 18.1 us
  local copies, waits for them, and re-layouts: 17.4 us -> 8.11 us
  Pallas kernels: 26.1 us -> 32 us
    all_gather x2 -> x0, blocking collectives: 83.5 us -> none  [the longest x1 44.2 us: per_device(): listed = lax.all_gather(listed, everywhere)]
    ppermute x0 -> x14, starting transfers between devices: none -> 21.3 us  [swap(): return lax.ppermute(x, names, [(at, at ^ step) for at in range(size)])]
    ppermute x0 -> x14, waiting for transfers between devices: none -> 18.1 us  [swap(): return lax.ppermute(x, names, [(at, at ^ step) for at in range(size)])]
    unnamed x27 -> x30, local copies, waits for them, and re-layouts: 16.7 us -> 6.67 us
    pallas_call x1, Pallas kernels: 4.78 us -> 10.7 us  [per_device(): pl.pallas_call(normalize, out_shape=shape((moves, width), BF16), grid=(mo...]
    all_to_all x1, waiting for transfers between devices: 5.16 us -> 0.01 us  [per_device(): lax.all_to_all(packed, ('line', 'pair'), split_axis=0, concat_axis=0, til...]
    all_to_all x1, starting transfers between devices: 7.25 us -> 3.78 us  [per_device(): lax.all_to_all(packed, ('line', 'pair'), split_axis=0, concat_axis=0, til...]
    pallas_call x3, Pallas kernels: 15.5 us -> 12.1 us  [scalar_call(): pl.pallas_call(kernel, out_shape=outs, grid_spec=pltpu.PrefetchScalarGrid...]
  transfers between devices with their start and end apart: 3 -> 16, of which waited for: 1 -> 5; matrix products, arithmetic and copies ran while one was open for 1% -> 2% of each run, Pallas kernels for 6% -> 19%
where the time goes in v3:
time: 103 us; the launch traced here: 102 us
  Pallas kernels  32 us (31%)
  starting transfers between devices  30.6 us (30%)
  waiting for transfers between devices  18.1 us (18%)
  blocking collectives  12.8 us (12%)
  local copies, waits for them, and re-layouts  8.11 us (8%)
    ppermute x14, starting transfers between devices, swap(): return lax.ppermute(x, names, [(at, at ^ step) for at in range(size)])  21.3 us
    ppermute x14, waiting for transfers between devices, swap(): return lax.ppermute(x, names, [(at, at ^ step) for at in range(size)])  18.1 us
    all_to_all x1, blocking collectives, per_device(): lax.all_to_all(parts.reshape(groups * back, share, plan.slots), ('groups'...  12.8 us
    pallas_call x3, Pallas kernels, scalar_call(): pl.pallas_call(kernel, out_shape=outs, grid_spec=pltpu.PrefetchScalarGrid...  12.1 us
    pallas_call x1, Pallas kernels, per_device(): pl.pallas_call(normalize, out_shape=shape((moves, width), BF16), grid=(mo...  10.7 us
    unnamed x30, local copies, waits for them, and re-layouts  6.67 us
    pallas_call x1, Pallas kernels, per_device(): pl.pallas_call(functools.partial(project, plan), out_shape=(shape((line,...  6.54 us
    all_to_all x1, starting transfers between devices, per_device(): lax.all_to_all(queries, 'line', split_axis=0, concat_axis=0, tiled=True)  5.55 us
  transfers between devices with their start and end apart: 16, of which 5 were waited for; matrix products, arithmetic and copies ran while one was open for 2% of the time, Pallas kernels for 19%

profile of v3, /device:TPU:0, one launch (start us, length us, event | category | flops | bytes accessed | tf_op | source)
XLA Modules:
  0.0 102.0 jit_solution(9484676038224202580)
XLA Ops:
  0.8 1.2 %copy-done = bf16[512,1024]{1,0:T(8,128)(2,1)S(1)} copy-done((bf16[512,1024]{1,0:T(8,128)(2,1)S(1)}, bf16[512,1024]{1,0:T(8,128)(2,1)}, u32[]{:S(2)}) %copy-start) | copy-done | bytes 1048600
  3.7 1.6 %shard_map.100.after_ref = bf16[8,80,512]{2,1,0:T(8,128)(2,1)} custom-call(s32[1]{0:T(128)} %bitcast.2.at_ref, bf16[512,1024]{1,0:T(8,128)(2,1)S(1)} %copy-done, bf16[512,256]{1,0:T(8,128)(2,1)S(1)} %copy-done.3, bf16[8,128]{1,0:T(8,128)(2,1)S(1)} %bitcast.27), custom_call_target="tpu_custom_call" | custom-call | flops 335544320 | bytes 2097152 | tf_op jit(solution)/shard_map/pallas_call | solution.py:263
  7.1 4.1 %collective-permute-start.2 = (f32[2,16,128]{2,1,0:T(8,128)S(1)}, f32[2,16,128]{2,1,0:T(8,128)S(1)}, u32[]{:S(2)}, u32[]{:S(2)}) collective-permute-start(f32[2,16,128]{2,1,0:T(8,128)S(1)} %constant_dynamic-slice_fusion.1), channel_id=1, source_target_pairs={{0,8},{4,12},{8,0},{12,4},{1,9},{5,13},{9,1},{13,5},{2,10},{6,14},... | collective-permute-start | bytes 49160 | tf_op jit(solution)/shard_map/ppermute | solution.py:283
  11.2 3.8 %all-to-all-start = ((bf16[8,80,512]{2,1,0:T(8,128)(2,1)}), bf16[8,80,512]{2,1,0:T(8,128)(2,1)S(1)}, u32[]{:S(2)}, u32[]{:S(2)}) async-start(bf16[8,80,512]{2,1,0:T(8,128)(2,1)} %shard_map.100.after_ref), calls=%async_computation | async-start | bytes 1310720 | tf_op jit(solution)/shard_map/all_to_all | solution.py:338
  15.0 2.1 %collective-permute-start.3 = (f32[1,16,128]{2,1,0:T(8,128)S(1)}, f32[1,16,128]{2,1,0:T(8,128)S(1)}, u32[]{:S(2)}, u32[]{:S(2)}) collective-permute-start(f32[1,16,128]{2,1,0:T(8,128)S(1)} %constant_dynamic-slice_fusion), channel_id=1, source_target_pairs={{0,4},{4,0},{8,12},{12,8},{1,5},{5,1},{9,13},{13,9},{2,6},{6,2},{1... | collective-permute-start | bytes 24584 | tf_op jit(solution)/shard_map/ppermute | solution.py:283
  17.7 1.6 %shard_map.102.rest_0_ = bf16[9,256,128]{2,1,0:T(8,128)(2,1)S(1)} custom-call(bf16[8,256,256]{2,1,0:T(8,128)(2,1)} %prefix_ref.1, bf16[8,128]{1,0:T(8,128)(2,1)S(1)} %bitcast.28, bf16[8,80,512]{2,1,0:T(8,128)(2,1)} %shard_map.100.after_ref), custom_call_target="tpu_custom_call" | custom-call | flops 67108864 | bytes 1048576 | tf_op jit(solution)/shard_map/pallas_call | solution.py:340
  19.3 1.5 %collective-permute-start = (bf16[9,256,128]{2,1,0:T(8,128)(2,1)S(1)}, bf16[9,256,128]{2,1,0:T(8,128)(2,1)S(1)}, u32[]{:S(2)}, u32[]{:S(2)}) collective-permute-start(bf16[9,256,128]{2,1,0:T(8,128)(2,1)S(1)} %shard_map.102.rest_0_), channel_id=1, source_target_pairs={{0,2},{2,0},{16,18},{18,16},{1,3},{3,1},{17,19},{19,17},{4,6},{6,4... | collective-permute-start | bytes 1769480 | tf_op jit(solution)/shard_map/ppermute | solution.py:283
  20.9 1.5 %collective-permute-start.1 = (bf16[9,256,128]{2,1,0:T(8,128)(2,1)S(1)}, bf16[9,256,128]{2,1,0:T(8,128)(2,1)S(1)}, u32[]{:S(2)}, u32[]{:S(2)}) collective-permute-start(bf16[9,256,128]{2,1,0:T(8,128)(2,1)S(1)} %shard_map.102.rest_0_), channel_id=1, source_target_pairs={{0,16},{2,18},{16,0},{18,2},{1,17},{3,19},{17,1},{19,3},{4,20},{6,... | collective-permute-start | bytes 1769480 | tf_op jit(solution)/shard_map/ppermute | solution.py:283
  22.4 3.2 %collective-permute-done.3 = f32[1,16,128]{2,1,0:T(8,128)S(1)} collective-permute-done((f32[1,16,128]{2,1,0:T(8,128)S(1)}, f32[1,16,128]{2,1,0:T(8,128)S(1)}, u32[]{:S(2)}, u32[]{:S(2)}) %collective-permute-start.3) | collective-permute-done | bytes 8224 | tf_op jit(solution)/shard_map/ppermute | solution.py:283
  25.6 1.7 %collective-permute-start.4 = (f32[16,128]{1,0:T(8,128)S(1)}, f32[16,128]{1,0:T(8,128)S(1)}, u32[]{:S(2)}, u32[]{:S(2)}) collective-permute-start(f32[16,128]{1,0:T(8,128)S(1)} %add_bitcast_fusion.2), channel_id=1, source_target_pairs={{0,2},{2,0},{16,18},{18,16},{1,3},{3,1},{17,19},{19,17},{4,6},{6,4... | collective-permute-start | bytes 24584 | tf_op jit(solution)/shard_map/ppermute | solution.py:283
  28.8 10.7 %shard_map.101.normed_ref = bf16[1024,4096]{1,0:T(8,128)(2,1)} custom-call(bf16[1024,4096]{1,0:T(8,128)(2,1)} %table_ref.1, bf16[1,4096]{1,0:T(2,128)(2,1)S(1)} %reshape.42.gain_ref, bf16[8,80,512]{2,1,0:T(8,128)(2,1)} %shard_map.100.after_ref), custom_call_target="tpu_custom_call" | custom-call | flops 33554432 | bytes 16777216 | tf_op jit(solution)/shard_map/pallas_call | solution.py:376
  39.5 1.5 %collective-permute-start.5 = (f32[16,128]{1,0:T(8,128)S(1)}, f32[16,128]{1,0:T(8,128)S(1)}, u32[]{:S(2)}, u32[]{:S(2)}) collective-permute-start(f32[16,128]{1,0:T(8,128)S(1)} %add_bitcast_fusion.2), channel_id=1, source_target_pairs={{0,16},{2,18},{16,0},{18,2},{1,17},{3,19},{17,1},{19,3},{4,20},{6,... | collective-permute-start | bytes 24584 | tf_op jit(solution)/shard_map/ppermute | solution.py:283
  41.3 1.9 %collective-permute-done.5 = f32[16,128]{1,0:T(8,128)S(1)} collective-permute-done((f32[16,128]{1,0:T(8,128)S(1)}, f32[16,128]{1,0:T(8,128)S(1)}, u32[]{:S(2)}, u32[]{:S(2)}) %collective-permute-start.5) | collective-permute-done | bytes 8224 | tf_op jit(solution)/shard_map/ppermute | solution.py:283
  43.2 2.5 %collective-permute-done.6 = f32[16,128]{1,0:T(8,128)S(1)} collective-permute-done((f32[16,128]{1,0:T(8,128)S(1)}, f32[16,128]{1,0:T(8,128)S(1)}, u32[]{:S(2)}, u32[]{:S(2)}) %collective-permute-start.6) | collective-permute-done | bytes 8224 | tf_op jit(solution)/shard_map/ppermute | solution.py:283
  47.3 6.5 %shard_map.104 = (bf16[4,64,1024]{2,1,0:T(8,128)(2,1)}, bf16[8,1024]{1,0:T(8,128)(2,1)S(1)}, f32[2,1024]{1,0:T(2,128)S(1)}) custom-call(bf16[8,80,512]{2,1,0:T(8,128)(2,1)} %copy-done.11, bf16[1024,4096]{1,0:T(8,128)(2,1)} %shard_map.101.normed_ref, f32[32,2]{1,0:T(8,128)S(1)} %bitcast.24, bf16[9,256,128]{2,1,0:T(8,128)(2,1)S(1)} %collective-permute-done.rest_0_.rest_1_, ...), custom_call_target="tpu_custom_call" | custom-call | flops 2147483648 | bytes 8388608 | tf_op jit(solution)/shard_map/pallas_call | solution.py:394
  54.1 1.5 %collective-permute-start.8 = (bf16[8,1024]{1,0:T(8,128)(2,1)S(1)}, bf16[8,1024]{1,0:T(8,128)(2,1)S(1)}, u32[]{:S(2)}, u32[]{:S(2)}) collective-permute-start(bf16[8,1024]{1,0:T(8,128)(2,1)S(1)} %get-tuple-element.12), channel_id=1, source_target_pairs={{0,16},{2,18},{16,0},{18,2},{1,17},{3,19},{17,1},{19,3},{4,20},{6,... | collective-permute-start | bytes 49160 | tf_op jit(solution)/shard_map/ppermute | solution.py:283
  55.6 1.7 %collective-permute-start.9 = (bf16[8,1024]{1,0:T(8,128)(2,1)S(1)}, bf16[8,1024]{1,0:T(8,128)(2,1)S(1)}, u32[]{:S(2)}, u32[]{:S(2)}) collective-permute-start(bf16[8,1024]{1,0:T(8,128)(2,1)S(1)} %get-tuple-element.12), channel_id=1, source_target_pairs={{0,18},{2,16},{16,2},{18,0},{1,19},{3,17},{17,3},{19,1},{4,22},{6,... | collective-permute-start | bytes 49160 | tf_op jit(solution)/shard_map/ppermute | solution.py:283
  57.3 5.6 %all-to-all-start.1 = ((bf16[4,64,1024]{2,1,0:T(8,128)(2,1)}), bf16[4,64,1024]{2,1,0:T(8,128)(2,1)S(1)}, u32[]{:S(2)}, u32[]{:S(2)}) async-start(bf16[4,64,1024]{2,1,0:T(8,128)(2,1)} %get-tuple-element.11), calls=%async_computation.1 | async-start | bytes 1048576 | tf_op jit(solution)/shard_map/all_to_all | solution.py:418
  62.9 2.1 %collective-permute-start.10 = (bf16[32,1024]{1,0:T(8,128)(2,1)S(1)}, bf16[32,1024]{1,0:T(8,128)(2,1)S(1)}, u32[]{:S(2)}, u32[]{:S(2)}) collective-permute-start(bf16[32,1024]{1,0:T(8,128)(2,1)S(1)} %get-tuple-element.15), channel_id=1, source_target_pairs={{0,4},{4,0},{8,12},{12,8},{1,5},{5,1},{9,13},{13,9},{2,6},{6,2},{1... | collective-permute-start | bytes 196616 | tf_op jit(solution)/shard_map/ppermute | solution.py:283
  65.1 2.4 %collective-permute-start.11 = (bf16[32,1024]{1,0:T(8,128)(2,1)S(1)}, bf16[32,1024]{1,0:T(8,128)(2,1)S(1)}, u32[]{:S(2)}, u32[]{:S(2)}) collective-permute-start(bf16[32,1024]{1,0:T(8,128)(2,1)S(1)} %get-tuple-element.15), channel_id=1, source_target_pairs={{0,8},{4,12},{8,0},{12,4},{1,9},{5,13},{9,1},{13,5},{2,10},{6,14},... | collective-permute-start | bytes 196616 | tf_op jit(solution)/shard_map/ppermute | solution.py:283
  67.5 4.4 %collective-permute-done.10 = bf16[32,1024]{1,0:T(8,128)(2,1)S(1)} collective-permute-done((bf16[32,1024]{1,0:T(8,128)(2,1)S(1)}, bf16[32,1024]{1,0:T(8,128)(2,1)S(1)}, u32[]{:S(2)}, u32[]{:S(2)}) %collective-permute-start.10) | collective-permute-done | bytes 65568 | tf_op jit(solution)/shard_map/ppermute | solution.py:283
  71.9 6.0 %collective-permute-done.11 = bf16[32,1024]{1,0:T(8,128)(2,1)S(1)} collective-permute-done((bf16[32,1024]{1,0:T(8,128)(2,1)S(1)}, bf16[32,1024]{1,0:T(8,128)(2,1)S(1)}, u32[]{:S(2)}, u32[]{:S(2)}) %collective-permute-start.11) | collective-permute-done | bytes 65568 | tf_op jit(solution)/shard_map/ppermute | solution.py:283
  78.0 10.1 %shard_map.105 = f32[2,16,16,128]{3,2,1,0:T(8,128)S(1)} custom-call(s32[2]{0:T(128)S(1)} %pad_add_fusion.at_ref, bf16[256,1024]{1,0:T(8,128)(2,1)S(1)} %bitcast.20, bf16[256,256]{1,0:T(8,128)(2,1)S(1)} %copy-done.10, bf16[128,1024]{1,0:T(8,128)(2,1)S(1)} %constant_dynamic-update-slice_fusion.4.k_ref, f32[64,2]{1,0:T(8,128)S(1)} %copy-done.9, ...), custom_call_target="tpu_custom_call" | custom-call | flops 2281701376 | bytes 4000000 | tf_op jit(solution)/shard_map/pallas_call | solution.py:263
  88.1 12.8 %all_to_all.15 = f32[32,16,128]{2,1,0:T(8,128)S(1)} all-to-all(f32[32,16,128]{2,1,0:T(8,128)S(1)} %bitcast.21), channel_id=1, replica_groups=mesh['groups'=2,'line'=4,'pair'=2,'tensor'=2] {'groups','line','pair','t..., dimensions={0} | all-to-all | bytes 524288 | tf_op jit(solution)/shard_map/all_to_all | solution.py:452
  (59 shorter events, 9.6 us)
Async XLA Ops:
  0.8 1.2 %copy-start = (bf16[512,1024]{1,0:T(8,128)(2,1)S(1)}, bf16[512,1024]{1,0:T(8,128)(2,1)}, u32[]{:S(2)}) copy-start(bf16[512,1024]{1,0:T(8,128)(2,1)} %wq_ref.1) | copy-start | bytes 3145732
  2.1 0.9 copy-start.3
  7.1 7.9 %collective-permute-start.2 = (f32[2,16,128]{2,1,0:T(8,128)S(1)}, f32[2,16,128]{2,1,0:T(8,128)S(1)}, u32[]{:S(2)}, u32[]{:S(2)}) collective-permute-start(f32[2,16,128]{2,1,0:T(8,128)S(1)} %constant_dynamic-slice_fusion.1), channel_id=1, source_target_pairs={{0,8},{4,12},{8,0},{12,4},{1,9},{5,13},{9,1},{13,5},{2,10},{6,14},... | collective-permute-start | bytes 49160 | tf_op jit(solution)/shard_map/ppermute | solution.py:283
  11.2 35.2 %all-to-all-start = ((bf16[8,80,512]{2,1,0:T(8,128)(2,1)}), bf16[8,80,512]{2,1,0:T(8,128)(2,1)S(1)}, u32[]{:S(2)}, u32[]{:S(2)}) async-start(bf16[8,80,512]{2,1,0:T(8,128)(2,1)} %shard_map.100.after_ref), calls=%async_computation | async-start | bytes 1310720 | tf_op jit(solution)/shard_map/all_to_all | solution.py:338
  15.0 10.6 %collective-permute-start.3 = (f32[1,16,128]{2,1,0:T(8,128)S(1)}, f32[1,16,128]{2,1,0:T(8,128)S(1)}, u32[]{:S(2)}, u32[]{:S(2)}) collective-permute-start(f32[1,16,128]{2,1,0:T(8,128)S(1)} %constant_dynamic-slice_fusion), channel_id=1, source_target_pairs={{0,4},{4,0},{8,12},{12,8},{1,5},{5,1},{9,13},{13,9},{2,6},{6,2},{1... | collective-permute-start | bytes 24584 | tf_op jit(solution)/shard_map/ppermute | solution.py:283
  19.3 26.4 %collective-permute-start = (bf16[9,256,128]{2,1,0:T(8,128)(2,1)S(1)}, bf16[9,256,128]{2,1,0:T(8,128)(2,1)S(1)}, u32[]{:S(2)}, u32[]{:S(2)}) collective-permute-start(bf16[9,256,128]{2,1,0:T(8,128)(2,1)S(1)} %shard_map.102.rest_0_), channel_id=1, source_target_pairs={{0,2},{2,0},{16,18},{18,16},{1,3},{3,1},{17,19},{19,17},{4,6},{6,4... | collective-permute-start | bytes 1769480 | tf_op jit(solution)/shard_map/ppermute | solution.py:283
  20.9 25.5 %collective-permute-start.1 = (bf16[9,256,128]{2,1,0:T(8,128)(2,1)S(1)}, bf16[9,256,128]{2,1,0:T(8,128)(2,1)S(1)}, u32[]{:S(2)}, u32[]{:S(2)}) collective-permute-start(bf16[9,256,128]{2,1,0:T(8,128)(2,1)S(1)} %shard_map.102.rest_0_), channel_id=1, source_target_pairs={{0,16},{2,18},{16,0},{18,2},{1,17},{3,19},{17,1},{19,3},{4,20},{6,... | collective-permute-start | bytes 1769480 | tf_op jit(solution)/shard_map/ppermute | solution.py:283
  25.6 15.7 %collective-permute-start.4 = (f32[16,128]{1,0:T(8,128)S(1)}, f32[16,128]{1,0:T(8,128)S(1)}, u32[]{:S(2)}, u32[]{:S(2)}) collective-permute-start(f32[16,128]{1,0:T(8,128)S(1)} %add_bitcast_fusion.2), channel_id=1, source_target_pairs={{0,2},{2,0},{16,18},{18,16},{1,3},{3,1},{17,19},{19,17},{4,6},{6,4... | collective-permute-start | bytes 24584 | tf_op jit(solution)/shard_map/ppermute | solution.py:283
  39.5 38.4 %copy-start.9 = (f32[64,2]{1,0:T(8,128)S(1)}, f32[64,2]{1,0:T(8,128)}, u32[]{:S(2)}) copy-start(f32[64,2]{1,0:T(8,128)} %constant.63.clone.turn_ref) | copy-start | bytes 1540
  39.5 38.4 %copy-start.10 = (bf16[256,256]{1,0:T(8,128)(2,1)S(1)}, bf16[256,256]{1,0:T(8,128)(2,1)}, u32[]{:S(2)}) copy-start(bf16[256,256]{1,0:T(8,128)(2,1)} %constant.64.clone.order_ref) | copy-start | bytes 393220
  39.5 3.7 %collective-permute-start.5 = (f32[16,128]{1,0:T(8,128)S(1)}, f32[16,128]{1,0:T(8,128)S(1)}, u32[]{:S(2)}, u32[]{:S(2)}) collective-permute-start(f32[16,128]{1,0:T(8,128)S(1)} %add_bitcast_fusion.2), channel_id=1, source_target_pairs={{0,16},{2,18},{16,0},{18,2},{1,17},{3,19},{17,1},{19,3},{4,20},{6,... | collective-permute-start | bytes 24584 | tf_op jit(solution)/shard_map/ppermute | solution.py:283
  41.0 4.7 %collective-permute-start.6 = (f32[16,128]{1,0:T(8,128)S(1)}, f32[16,128]{1,0:T(8,128)S(1)}, u32[]{:S(2)}, u32[]{:S(2)}) collective-permute-start(f32[16,128]{1,0:T(8,128)S(1)} %add_bitcast_fusion.2), channel_id=1, source_target_pairs={{0,18},{2,16},{16,2},{18,0},{1,19},{3,17},{17,3},{19,1},{4,22},{6,... | collective-permute-start | bytes 24584 | tf_op jit(solution)/shard_map/ppermute | solution.py:283
  45.7 32.2 %copy-start.1 = (bf16[9,256,128]{2,1,0:T(8,128)(2,1)}, bf16[9,256,128]{2,1,0:T(8,128)(2,1)S(1)}, u32[]{:S(2)}) copy-start(bf16[9,256,128]{2,1,0:T(8,128)(2,1)S(1)} %collective-permute-done.rest_0_.rest_1_) | copy-start | bytes 1769476
  45.7 32.2 %collective-permute-start.13 = (bf16[9,256,128]{2,1,0:T(8,128)(2,1)S(1)}, bf16[9,256,128]{2,1,0:T(8,128)(2,1)}, u32[]{:S(2)}, u32[]{:S(2)}) collective-permute-start(bf16[9,256,128]{2,1,0:T(8,128)(2,1)S(1)} %collective-permute-done.rest_0_.rest_1_), channel_id=1, source_target_pairs={{0,16},{2,18},{16,0},{18,2},{1,17},{3,19},{17,1},{19,3},{4,20},{6,... | collective-permute-start | bytes 1769480 | tf_op jit(solution)/shard_map/ppermute | solution.py:283
  46.3 31.6 %copy-start.2 = (bf16[9,256,128]{2,1,0:T(8,128)(2,1)}, bf16[9,256,128]{2,1,0:T(8,128)(2,1)S(1)}, u32[]{:S(2)}) copy-start(bf16[9,256,128]{2,1,0:T(8,128)(2,1)S(1)} %collective-permute-done.1.rest_1_.rest_2_) | copy-start | bytes 1769476
  46.3 0.9 copy-start.11
  47.3 53.7 %copy-start.5 = (s32[512,1]{0,1:T(1,128)S(1)}, s32[512,1]{0,1:T(1,128)}, u32[]{:S(2)}) copy-start(s32[512,1]{0,1:T(1,128)} %param.12) | copy-start | bytes 6148
  53.8 9.0 %collective-permute-start.7 = (bf16[8,1024]{1,0:T(8,128)(2,1)S(1)}, bf16[8,1024]{1,0:T(8,128)(2,1)S(1)}, u32[]{:S(2)}, u32[]{:S(2)}) collective-permute-start(bf16[8,1024]{1,0:T(8,128)(2,1)S(1)} %get-tuple-element.12), channel_id=1, source_target_pairs={{0,2},{2,0},{16,18},{18,16},{1,3},{3,1},{17,19},{19,17},{4,6},{6,4... | collective-permute-start | bytes 49160 | tf_op jit(solution)/shard_map/ppermute | solution.py:283
  54.1 8.8 %collective-permute-start.8 = (bf16[8,1024]{1,0:T(8,128)(2,1)S(1)}, bf16[8,1024]{1,0:T(8,128)(2,1)S(1)}, u32[]{:S(2)}, u32[]{:S(2)}) collective-permute-start(bf16[8,1024]{1,0:T(8,128)(2,1)S(1)} %get-tuple-element.12), channel_id=1, source_target_pairs={{0,16},{2,18},{16,0},{18,2},{1,17},{3,19},{17,1},{19,3},{4,20},{6,... | collective-permute-start | bytes 49160 | tf_op jit(solution)/shard_map/ppermute | solution.py:283
  55.6 7.3 %collective-permute-start.9 = (bf16[8,1024]{1,0:T(8,128)(2,1)S(1)}, bf16[8,1024]{1,0:T(8,128)(2,1)S(1)}, u32[]{:S(2)}, u32[]{:S(2)}) collective-permute-start(bf16[8,1024]{1,0:T(8,128)(2,1)S(1)} %get-tuple-element.12), channel_id=1, source_target_pairs={{0,18},{2,16},{16,2},{18,0},{1,19},{3,17},{17,3},{19,1},{4,22},{6,... | collective-permute-start | bytes 49160 | tf_op jit(solution)/shard_map/ppermute | solution.py:283
  57.3 20.6 %all-to-all-start.1 = ((bf16[4,64,1024]{2,1,0:T(8,128)(2,1)}), bf16[4,64,1024]{2,1,0:T(8,128)(2,1)S(1)}, u32[]{:S(2)}, u32[]{:S(2)}) async-start(bf16[4,64,1024]{2,1,0:T(8,128)(2,1)} %get-tuple-element.11), calls=%async_computation.1 | async-start | bytes 1048576 | tf_op jit(solution)/shard_map/all_to_all | solution.py:418
  62.9 9.0 %collective-permute-start.10 = (bf16[32,1024]{1,0:T(8,128)(2,1)S(1)}, bf16[32,1024]{1,0:T(8,128)(2,1)S(1)}, u32[]{:S(2)}, u32[]{:S(2)}) collective-permute-start(bf16[32,1024]{1,0:T(8,128)(2,1)S(1)} %get-tuple-element.15), channel_id=1, source_target_pairs={{0,4},{4,0},{8,12},{12,8},{1,5},{5,1},{9,13},{13,9},{2,6},{6,2},{1... | collective-permute-start | bytes 196616 | tf_op jit(solution)/shard_map/ppermute | solution.py:283
  65.1 12.8 %collective-permute-start.11 = (bf16[32,1024]{1,0:T(8,128)(2,1)S(1)}, bf16[32,1024]{1,0:T(8,128)(2,1)S(1)}, u32[]{:S(2)}, u32[]{:S(2)}) collective-permute-start(bf16[32,1024]{1,0:T(8,128)(2,1)S(1)} %get-tuple-element.15), channel_id=1, source_target_pairs={{0,8},{4,12},{8,0},{12,4},{1,9},{5,13},{9,1},{13,5},{2,10},{6,14},... | collective-permute-start | bytes 196616 | tf_op jit(solution)/shard_map/ppermute | solution.py:283
  67.4 10.5 %collective-permute-start.12 = (bf16[32,1024]{1,0:T(8,128)(2,1)S(1)}, bf16[32,1024]{1,0:T(8,128)(2,1)S(1)}, u32[]{:S(2)}, u32[]{:S(2)}) collective-permute-start(bf16[32,1024]{1,0:T(8,128)(2,1)S(1)} %get-tuple-element.15), channel_id=1, source_target_pairs={{0,12},{4,8},{8,4},{12,0},{1,13},{5,9},{9,5},{13,1},{2,14},{6,10},... | collective-permute-start | bytes 196616 | tf_op jit(solution)/shard_map/ppermute | solution.py:283
  (4 other events, 2.7 us)

commit v4 on v3

v4 whole, which is shorter than its diff:
```python
import functools
import math

import jax
import jax.numpy as jnp
import numpy as np
from jax import lax
from jax.experimental import pallas as pl
from jax.experimental.pallas import tpu as pltpu
from jax.sharding import Mesh
from jax.sharding import PartitionSpec as P

HD = 128
HALF = HD // 2
EPS = 1e-06
THETA = 5000000.0
DEAD = -1e30
VMEM_MIB = 52

F32 = jnp.float32
BF16 = jnp.bfloat16

NN = (((1,), (0,)), ((), ()))
NT = (((1,), (1,)), ((), ()))
TN = (((0,), (0,)), ((), ()))


def matmul(a, b, dims=NN):
    return lax.dot_general(a, b, dims, preferred_element_type=F32)


def limits(mib):
    return pltpu.CompilerParams(vmem_limit_bytes=mib * 1024 * 1024)


class Plan:
    def __init__(self, groups, line, pair, heads, capacity, share):
        self.groups, self.line, self.pair = groups, line, pair
        self.peers = line * pair
        self.slab = groups * pair
        self.heads = heads
        self.mine = heads // self.slab
        self.pairs = HALF // line
        self.q_rows = self.mine * 2 * self.pairs
        self.k_rows = 2 * self.pairs
        self.fold_at = self.q_rows + self.k_rows
        self.list_at = self.fold_at + self.mine
        self.rows = -(-(self.list_at + 1) // 8) * 8
        self.line_rows = -(-(self.q_rows + 2 * self.mine) // 8) * 8
        self.capacity = capacity
        self.share = share
        self.slots = self.peers * capacity


def pack_weights(plan, at_ref, wq_hbm, wkv_hbm, ws_ref, board_ref, ids_ref, out_ref, wq, wkv, pick, sems):
    group = at_ref[0]
    rows, half_cols = plan.rows, wq.shape[1]
    columns_here = pl.ds(pl.multiple_of(group * half_cols, HD), half_cols)
    copies = (
        pltpu.make_async_copy(wq_hbm.at[:, columns_here], wq, sems.at[0]),
        pltpu.make_async_copy(wkv_hbm, wkv, sems.at[1]),
    )
    for copy in copies:
        copy.start()
    r = lax.broadcasted_iota(jnp.int32, (rows, 1), 0)
    part = r // (plan.mine * plan.pairs)
    head = (r // plan.pairs) % plan.mine
    entry = r % plan.pairs
    is_q = r < plan.q_rows
    k_at = r - plan.q_rows
    is_k = (k_at >= 0) & (k_at < plan.k_rows)
    f_at = r - plan.fold_at
    is_f = (f_at >= 0) & (f_at < plan.mine)
    q_lane = lax.broadcasted_iota(jnp.int32, (rows, half_cols), 1)
    k_lane = lax.broadcasted_iota(jnp.int32, (rows, HD), 1)
    ws = ws_ref[...].astype(F32)

    def fill(peer, carry):
        line, pair = peer // plan.pair, peer % plan.pair
        column = (pair * plan.mine + head) * HD + part * HALF + line * plan.pairs + entry
        column = jnp.where(is_q, column, -1)
        at = pl.ds(pl.multiple_of(peer * rows, 8), rows)
        pick[at, :half_cols] = jnp.where(q_lane == column, 1.0, 0.0)
        k_column = (k_at // plan.pairs) * HALF + line * plan.pairs + k_at % plan.pairs
        k_column = jnp.where(is_k, k_column, -1)
        pick[at, half_cols : half_cols + HD] = jnp.where(k_lane == k_column, 1.0, 0.0)
        fold = jnp.zeros((rows, HD), F32)
        my_head = jnp.where(is_f, (group * plan.pair + pair) * plan.mine + f_at, -1)
        for h in range(plan.heads):
            fold = jnp.where(my_head == h, ws[h : h + 1], fold)
        pick[at, half_cols + HD :] = fold
        return carry

    lax.fori_loop(0, plan.peers, fill, 0, unroll=plan.peers <= 8)

    count, depth = board_ref.shape[1], wq.shape[0]
    board_row = board_ref[...]
    board_col = jnp.broadcast_to(board_row.astype(F32), (8, count)).T[:, 0:1].astype(jnp.int32)
    own = lax.broadcasted_iota(jnp.int32, (count, count), 0)
    other = lax.broadcasted_iota(jnp.int32, (count, count), 1)
    ahead = jnp.where((board_col == board_row) & (other < own), 1.0, 0.0)
    rank = jnp.sum(ahead, axis=1, keepdims=True).astype(jnp.int32)
    key = board_col * plan.capacity + rank
    move = ids_ref[...] + 1
    parts = jnp.concatenate([(move // 64).astype(F32), (move % 64).astype(F32)], axis=0).astype(BF16)
    span = plan.share * plan.capacity
    lane = lax.broadcasted_iota(jnp.int32, (count, depth), 1)
    lane_row = lax.broadcasted_iota(jnp.int32, (1, depth), 1)
    lists = []
    for line in range(plan.line):
        place = jnp.where(lane < span, lane, lane - span) + line * span
        found = matmul(parts, jnp.where(key == place, 1.0, 0.0).astype(BF16))
        lists.append(jnp.where(lane_row < span, found[0:1], found[1:2]))

    for copy in copies:
        copy.wait()
    left = pick[...].astype(BF16)
    total = matmul(left[:, :half_cols], wq[...], NT) + matmul(left[:, half_cols:], wkv[...], NT)
    for peer in range(plan.peers):
        mine = total[peer * rows : (peer + 1) * rows]
        out_ref[peer] = jnp.where(r == plan.list_at, lists[peer // plan.pair], mine).astype(BF16)


def normalize(table_hbm, gain_ref, after_ref, out_ref, buffers, sems):
    held, block, width = buffers.shape
    steps = table_hbm.shape[0] // block

    def copy(step):
        at = step % held
        return pltpu.make_async_copy(table_hbm.at[pl.ds(step * block, block)], buffers.at[at], sems.at[at])

    for step in range(min(held - 1, steps)):
        copy(step).start()
    gain = gain_ref[...].astype(F32)
    for step in range(steps):
        if step + held - 1 < steps:
            copy(step + held - 1).start()
        copy(step).wait()

        def one(tile, carry):
            raw = buffers[step % held, pl.ds(pl.multiple_of(tile * 16, 16), 16)].astype(F32)
            inverse = lax.rsqrt(jnp.mean(raw * raw, axis=-1, keepdims=True) + EPS)
            at = pl.ds(pl.multiple_of(step * block + tile * 16, 16), 16)
            out_ref[at, :] = (raw * inverse * gain).astype(BF16)
            return carry

        lax.fori_loop(0, block // 16, one, 0)


def project(plan, w_ref, normed_ref, turn_ref, *rest):
    q_ref, vo_ref = rest[-2:]
    moves = normed_ref.shape[0]
    block = min(moves, 256)
    half, k_half = plan.q_rows // 2, plan.k_rows // 2
    cosine, sine = turn_ref[:, 0:1], turn_ref[:, 1:2]
    for start in range(0, moves, block):
        at = slice(start, start + block)
        if len(w_ref.shape) == 3:
            depth = w_ref.shape[2]
            total = None
            for s in range(w_ref.shape[0]):
                term = matmul(w_ref[s], normed_ref[at, s * depth : (s + 1) * depth], NT)
                total = term if total is None else total + term
        else:
            total = matmul(w_ref[...], normed_ref[at, :], NT)
        first, second = total[:half], total[half : 2 * half]
        q_first = (first * cosine - second * sine).astype(BF16)
        q_second = (second * cosine + first * sine).astype(BF16)
        first, second = total[plan.q_rows : plan.q_rows + k_half], total[plan.q_rows + k_half : plan.fold_at]
        cos_k, sin_k = cosine[:k_half], sine[:k_half]
        k_first = (first * cos_k - second * sin_k).astype(BF16).astype(F32)
        k_second = (second * cos_k + first * sin_k).astype(BF16).astype(F32)
        f_first, f_second = q_first.astype(F32), q_second.astype(F32)
        logits, tails = [], []
        for h in range(plan.mine):
            own = slice(h * k_half, (h + 1) * k_half)
            logit = jnp.sum(f_first[own] * k_first + f_second[own] * k_second, axis=0, keepdims=True)
            logits.append(logit.astype(BF16).astype(F32))
            tails.append(logit - logits[-1])
        pad = plan.line_rows - plan.q_rows - 2 * plan.mine
        pieces = [f_first, f_second, *logits, *tails]
        if pad:
            pieces.append(jnp.zeros((pad, block), F32))
        out = jnp.concatenate(pieces, axis=0).astype(BF16)
        for copy in range(q_ref.shape[0]):
            q_ref[copy, :, at] = out
        vo_ref[:, at] = total[plan.fold_at : plan.list_at]


def pack_prefix(prefix_ref, ws_ref, after_ref, out_ref):
    boards = prefix_ref.shape[0]
    heads = ws_ref.shape[0]
    span = HD // boards
    ws = jnp.concatenate([ws_ref[...].astype(F32)] * (HD // heads), axis=0)
    row = lax.broadcasted_iota(jnp.int32, (HD, 1), 0)
    fold = None
    for board in range(boards):
        out_ref[board] = prefix_ref[board, :, :HD]
        keep = (row // span == board) & (row % span < 2 * heads)
        term = matmul(prefix_ref[board, :, HD:], jnp.where(keep, ws, 0.0).astype(BF16), NT)
        fold = term if fold is None else fold + term
    rounded = fold.astype(BF16).astype(F32)
    lane = lax.broadcasted_iota(jnp.int32, fold.shape, 1)
    out_ref[boards] = jnp.where(lane % span < heads, rounded, fold - rounded).astype(BF16)


def find_slots(plan, at_ref, board_ref, after_ref, slot_ref):
    count = board_ref.shape[1]
    board_row = board_ref[...]
    board_col = jnp.broadcast_to(board_row.astype(F32), (8, count)).T[:, 0:1].astype(jnp.int32)
    other = lax.broadcasted_iota(jnp.int32, (count, count), 0)
    own = lax.broadcasted_iota(jnp.int32, (count, count), 1)
    rank = jnp.sum(jnp.where((board_col == board_row) & (other < own), 1.0, 0.0), axis=0, keepdims=True)
    slot_ref[...] = rank.astype(jnp.int32) + at_ref[0] * plan.capacity


def read_lists(plan, w_ref, out_ref):
    share, capacity, peers = plan.share, plan.capacity, plan.peers
    span = share * capacity
    rows = jnp.concatenate([w_ref[s].astype(F32)[plan.list_at : plan.list_at + 1] for s in range(peers)], axis=0)
    lane = lax.broadcasted_iota(jnp.int32, (share * peers, 2 * span), 1)
    row = lax.broadcasted_iota(jnp.int32, (share * peers, 2 * span), 0)
    lane = jnp.where(lane < span, lane, lane - span)
    spread = jnp.concatenate([rows] * share, axis=0)
    spread = jnp.where(lane // capacity == row // peers, spread, 0.0).astype(BF16)
    c = lax.broadcasted_iota(jnp.int32, (2 * span, plan.slots), 0)
    slot = lax.broadcasted_iota(jnp.int32, (2 * span, plan.slots), 1)
    scale = jnp.where(c < span, 64.0, 1.0)
    place = jnp.where(c % capacity == slot % capacity, scale, 0.0).astype(BF16)
    listed = matmul(spread, place)
    row = lax.broadcasted_iota(jnp.int32, listed.shape, 0)
    slot = lax.broadcasted_iota(jnp.int32, listed.shape, 1)
    listed = jnp.where(slot // capacity == row % peers, listed, 0.0)
    out_ref[...] = jnp.sum(listed.reshape(share, peers, plan.slots), axis=1)


def attend(plan, at_ref, q_ref, order_ref, vo_ref, *rest):
    prefix_refs = rest[: plan.slab]
    moves_ref, out_ref, table, extra, scores = rest[plan.slab :]
    here = at_ref[0]
    mine, heads, slots = plan.mine, plan.heads, plan.slots
    moves = q_ref.shape[1]
    boards = prefix_refs[0].shape[0] - 1
    query_rows = mine * HD

    mixed = matmul(order_ref[...], q_ref[...])
    table[:query_rows] = mixed[:query_rows].astype(BF16)
    extra[...] = jnp.zeros_like(extra)
    for place, value in ((0, mixed[query_rows : query_rows + mine]), (2 * mine, vo_ref[...])):
        rounded = value.astype(BF16).astype(F32)
        extra[place : place + mine] = rounded
        extra[place + mine : place + 2 * mine] = value - rounded
    table[query_rows:] = extra[...].astype(BF16)

    scale = math.log2(math.e) / math.sqrt(HD)
    move_at = lax.broadcasted_iota(jnp.int32, (moves, slots), 0) + 1
    lanes = mine * slots
    span = HD // boards
    fold_row = lax.broadcasted_iota(jnp.int32, (HD, lanes), 0)
    fold_head = here * mine + lax.broadcasted_iota(jnp.int32, (HD, lanes), 1) // slots

    def per_head(x, base):
        pieces = [x[base + h : base + h + 1] + x[base + mine + h : base + mine + h + 1] for h in range(mine)]
        return jnp.concatenate(pieces, axis=1)

    def step(board, carry):
        listed = [moves_ref[j // plan.pair, pl.ds(((here ^ j) % plan.pair) * boards + board, 1), :] for j in range(plan.slab)]
        chosen = [jnp.where(move_at == row, 1.0, 0.0).astype(BF16) for row in listed]
        taken = matmul(table[...], jnp.concatenate(chosen, axis=1))
        at = fold_row - board * span
        fold_pick = jnp.where((at == fold_head) | (at == fold_head + heads), 1.0, 0.0).astype(BF16)
        for j in range(plan.slab):
            x = taken[:, j * slots : (j + 1) * slots]
            q = jnp.concatenate([x[h * HD : (h + 1) * HD].astype(BF16) for h in range(mine)], axis=1)
            logits = matmul(prefix_refs[j][board], q)
            fold = matmul(prefix_refs[j][boards], fold_pick)
            own_logit = per_head(x, query_rows)
            own_value = per_head(x, query_rows + 2 * mine)
            peak = jnp.maximum(jnp.max(logits, axis=0, keepdims=True), own_logit)
            weight = jnp.exp2((logits - peak) * scale)
            own_weight = jnp.exp2((own_logit - peak) * scale)
            denom = jnp.sum(weight, axis=0, keepdims=True) + own_weight
            value = (jnp.sum(weight * fold, axis=0, keepdims=True) + own_value * own_weight) / denom
            score = sum(value[:, h * slots : (h + 1) * slots] for h in range(mine))
            scores[here ^ j, pl.ds(board, 1), :] = jnp.where(listed[j] > 0, score, DEAD)
        return carry

    lax.fori_loop(0, boards, step, 0)
    for g in range(plan.groups):
        both = jnp.concatenate([scores[g * plan.pair + p] for p in range(plan.pair)], axis=0)
        for copy in range(out_ref.shape[1]):
            out_ref[g, copy] = both


def finish(plan, parts_ref, board_ref, slot_ref, out_ref):
    line = parts_ref.shape[1]
    columns = []
    for at in range(line):
        total = None
        for g in range(parts_ref.shape[0]):
            for p in range(parts_ref.shape[2]):
                term = parts_ref[g, at, p]
                total = term if total is None else total + term
        columns.append(total)
    scores = jnp.concatenate(columns, axis=0)
    live = scores > 0.5 * DEAD
    peak = jnp.max(scores, axis=1, keepdims=True)
    denom = jnp.sum(jnp.where(live, jnp.exp(scores - peak), 0.0), axis=1, keepdims=True)
    logprob = jnp.where(live, scores - peak - jnp.log(denom), 0.0)
    count = board_ref.shape[1]
    member = lax.broadcasted_iota(jnp.int32, (scores.shape[0], count), 0) == board_ref[...]
    member = jnp.where(member, 1.0, 0.0).astype(BF16)
    found = jnp.zeros((plan.slots, count), F32)
    for _ in range(3):
        rounded = logprob.astype(BF16)
        found = found + matmul(rounded, member, TN)
        logprob = logprob - rounded.astype(F32)
    at = lax.broadcasted_iota(jnp.int32, (plan.slots, count), 0) == slot_ref[...]
    out_ref[...] = jnp.sum(jnp.where(at, found, 0.0), axis=0, keepdims=True)


def untouched():
    return pl.BlockSpec(memory_space=pl.ANY)


def scalar_call(kernel, at, args, outs, scratch, cost=None, specs=None):
    whole = lambda x: pl.BlockSpec(x.shape, lambda i, at, n=len(x.shape): (0,) * n)
    specs = specs or {}
    return pl.pallas_call(
        kernel,
        out_shape=outs,
        grid_spec=pltpu.PrefetchScalarGridSpec(
            num_scalar_prefetch=1,
            grid=(1,),
            in_specs=[specs.get(i, whole(x)) for i, x in enumerate(args)],
            out_specs=jax.tree.map(whole, outs),
            scratch_shapes=scratch,
        ),
        compiler_params=limits(VMEM_MIB),
        cost_estimate=cost,
    )(at, *args)


def cost(flops, nbytes):
    return pl.CostEstimate(flops=int(flops), bytes_accessed=int(nbytes), transcendentals=0)


def swap(x, names, size, step):
    return lax.ppermute(x, names, [(at, at ^ step) for at in range(size)])


def shape(dims, dtype):
    return jax.ShapeDtypeStruct(tuple(dims), dtype)


def turn_table(position):
    frequency = THETA ** (-2.0 * np.arange(HALF, dtype=np.float32) / HD)
    angles = np.float32(position) * frequency.astype(np.float32)
    return np.stack([np.cos(angles), np.sin(angles)], axis=1).astype(np.float32)


def entry_order(plan):
    order = np.zeros((plan.mine * HD + 16, plan.line * plan.line_rows), np.float32)
    for head in range(plan.mine):
        for part in range(2):
            for entry in range(HALF):
                line, at = divmod(entry, plan.pairs)
                source = line * plan.line_rows + (part * plan.mine + head) * plan.pairs + at
                order[head * HD + part * HALF + entry, source] = 1.0
        for line in range(plan.line):
            for piece in range(2):
                order[plan.mine * HD + head, line * plan.line_rows + plan.q_rows + piece * plan.mine + head] = 1.0
    return order


def per_device(prefix_kv, move_ids, move_board, move_table, norm_gain, w_query, w_keyval, w_score):
    row_count = move_ids.shape[0]
    boards_here, prefix_len, _ = prefix_kv.shape
    moves, width = move_table.shape
    groups, line, pair = lax.axis_size("groups"), lax.axis_size("line"), lax.axis_size("pair")
    board_total = boards_here * line * pair
    capacity = max(2, (2 * row_count + board_total - 1) // board_total)
    heads = w_query.shape[1] // HD
    plan = Plan(groups, line, pair, heads, capacity, pair * boards_here)
    depth = w_query.shape[0]
    group_at = lax.axis_index("groups").astype(jnp.int32)
    line_at = lax.axis_index("line").astype(jnp.int32)
    pair_at = lax.axis_index("pair").astype(jnp.int32)
    slab_at = group_at * pair + pair_at
    ws = w_score.reshape(heads, HD)
    slab_axes = ("groups", "pair")
    board_row = move_board.reshape(1, row_count)

    half_cols = w_query.shape[1] // groups
    packed = scalar_call(
        functools.partial(pack_weights, plan),
        group_at.reshape(1),
        (w_query, w_keyval, ws, board_row, move_ids.reshape(1, row_count)),
        shape((plan.peers, plan.rows, depth), BF16),
        [
            pltpu.VMEM((depth, half_cols), BF16),
            pltpu.VMEM((depth, 2 * HD), BF16),
            pltpu.VMEM((plan.peers * plan.rows, half_cols + 2 * HD), F32),
            pltpu.SemaphoreType.DMA((2,)),
        ],
        cost(2 * plan.peers * plan.rows * half_cols * depth, 4 * w_query.size),
        {0: untouched(), 1: untouched()},
    )
    weights = lax.all_to_all(packed, ("line", "pair"), split_axis=0, concat_axis=0, tiled=True)

    payload = pl.pallas_call(
        pack_prefix,
        out_shape=shape((boards_here + 1, prefix_len, HD), BF16),
        in_specs=[pl.BlockSpec(memory_space=pltpu.VMEM), pl.BlockSpec(memory_space=pltpu.VMEM), untouched()],
        compiler_params=limits(32),
        cost_estimate=cost(2 * prefix_len * HD * HD * boards_here, 2 * prefix_kv.size),
    )(prefix_kv, ws, packed)
    beside = swap(payload, slab_axes, plan.slab, 1)
    across = swap(payload, slab_axes, plan.slab, 2)
    slot_row = scalar_call(
        functools.partial(find_slots, plan),
        (line_at * pair + pair_at).reshape(1),
        (board_row, packed),
        shape((1, row_count), jnp.int32),
        [],
        cost(4 * row_count * row_count, 4 * row_count),
        {1: untouched()},
    )

    block = min(moves, 128)
    normed = pl.pallas_call(
        normalize,
        out_shape=shape((moves, width), BF16),
        in_specs=[untouched(), pl.BlockSpec(memory_space=pltpu.VMEM), untouched()],
        out_specs=pl.BlockSpec(memory_space=pltpu.VMEM),
        scratch_shapes=[pltpu.VMEM((3, block, width), BF16), pltpu.SemaphoreType.DMA((3,))],
        compiler_params=limits(32),
        cost_estimate=cost(8 * moves * width, 2 * moves * width),
    )(move_table, norm_gain.reshape(1, width), packed)
    turns = jnp.asarray(turn_table(prefix_len))
    my_turns = jnp.tile(lax.dynamic_slice_in_dim(turns, line_at * plan.pairs, plan.pairs, axis=0), (plan.mine, 1))
    flat = weights.transpose(1, 0, 2).reshape(plan.rows, width) if depth % HD else weights
    queries, own_values = pl.pallas_call(
        functools.partial(project, plan),
        out_shape=(shape((line, plan.line_rows, moves), BF16), shape((plan.mine, moves), F32)),
        in_specs=[pl.BlockSpec(memory_space=pltpu.VMEM)] * 3 + [untouched()] * 3,
        compiler_params=limits(32),
        cost_estimate=cost(2 * moves * width * 256, 2 * moves * width),
    )(flat, normed, my_turns, beside, across, slot_row)
    queries = lax.all_to_all(queries, "line", split_axis=0, concat_axis=0, tiled=True)
    diagonal = swap(beside, slab_axes, plan.slab, 2)
    listed = pl.pallas_call(
        functools.partial(read_lists, plan),
        out_shape=shape((plan.share, plan.slots), F32),
        compiler_params=limits(32),
        cost_estimate=cost(10**7, 10**6),
    )(weights)
    listed = jnp.stack([listed, swap(listed, slab_axes, plan.slab, pair)]).astype(jnp.int32)

    query_rows = plan.mine * HD
    back = plan.peers * lax.axis_size("tensor")
    parts = scalar_call(
        functools.partial(attend, plan),
        slab_at.reshape(1),
        (
            queries.reshape(line * plan.line_rows, moves),
            jnp.asarray(entry_order(plan), BF16),
            own_values,
            payload,
            beside,
            across,
            diagonal,
            listed,
        ),
        shape((groups, back, plan.share, plan.slots), F32),
        [
            pltpu.VMEM((query_rows + 16, moves), BF16),
            pltpu.VMEM((16, moves), F32),
            pltpu.VMEM((plan.slab, boards_here, plan.slots), F32),
        ],
        cost(2 * 272 * moves * 4096, 4 * 10**6),
    )
    parts = lax.all_to_all(
        parts.reshape(groups * back, plan.share, plan.slots),
        ("groups", "line", "pair", "tensor"),
        split_axis=0,
        concat_axis=0,
        tiled=True,
    )
    parts = parts.reshape(groups, line, back // line, plan.share, plan.slots)
    logprob = pl.pallas_call(
        functools.partial(finish, plan), out_shape=shape((1, row_count), F32), compiler_params=limits(VMEM_MIB)
    )(parts, board_row, slot_row)
    return logprob.reshape(row_count)


def solution(mesh):
    order = ("groups", "dp", "tensor")
    assert mesh.axis_names == order
    pair = 2
    groups, peers, tensor = (mesh.shape[name] for name in order)
    fine = Mesh(mesh.devices.reshape(groups, peers // pair, pair, tensor), ("groups", "line", "pair", "tensor"))
    rows = ("groups", "line", "pair")
    placed = (
        P(rows, None, "tensor"),
        P(rows),
        P(rows, None),
        P(),
        P(),
        P(("line", "pair"), "tensor"),
        P(("line", "pair"), "tensor"),
        P("tensor"),
    )
    return jax.shard_map(per_device, mesh=fine, in_specs=placed, out_specs=P(rows), check_vma=False)
```

time: 103 us -> 90.6 us (0.88)
  starting transfers between devices: 30.6 us -> 17.5 us
  local copies, waits for them, and re-layouts: 8.11 us -> 17.6 us
  waiting for transfers between devices: 18.1 us -> 12.5 us
  Pallas kernels: 32 us -> 28 us
  blocking collectives: 12.8 us -> 14.2 us
    ppermute x14 -> x4, starting transfers between devices: 21.3 us -> 5.69 us  [swap(): return lax.ppermute(x, names, [(at, at ^ step) for at in range(size)])]
    unnamed x30 -> x29, local copies, waits for them, and re-layouts: 6.67 us -> 16.1 us
    ppermute x14 -> x4, waiting for transfers between devices: 18.1 us -> 11.6 us  [swap(): return lax.ppermute(x, names, [(at, at ^ step) for at in range(size)])]
    all_to_all x1, starting transfers between devices: 3.78 us -> 7.26 us  [per_device(): lax.all_to_all(packed, ('line', 'pair'), split_axis=0, concat_axis=0, til...]
    pallas_call x1, Pallas kernels: 6.54 us -> 3.66 us  [per_device(): pl.pallas_call(functools.partial(project, plan), out_shape=(shape((line,...]
    all_to_all x1, blocking collectives: 12.8 us -> 14.2 us  [per_device(): lax.all_to_all(parts.reshape(groups * back, plan.share, plan.slots), ('gr...]
    pallas_call x1, Pallas kernels: 1.59 us -> 0.28 us  [per_device(): pl.pallas_call(pack_prefix, out_shape=shape((boards_here + 1, prefix_len,...]
    pallas_call x1 -> x2, Pallas kernels: 10.7 us -> 10.2 us  [the longest x1 10 us: per_device(): pl.pallas_call(normalize, out_shape=shape((moves, width), BF16), in_specs...]
  transfers between devices with their start and end apart: 16 -> 6, of which waited for: 5 -> 2; matrix products, arithmetic and copies ran while one was open for 2% -> 2% of each run, Pallas kernels for 19% -> 12%
where the time goes in v4:
time: 90.6 us; the launch traced here: 89.9 us
  Pallas kernels  28 us (31%)
  local copies, waits for them, and re-layouts  17.6 us (19%)
  starting transfers between devices  17.5 us (19%)
  blocking collectives  14.2 us (16%)
  waiting for transfers between devices  12.5 us (14%)
    unnamed x29, local copies, waits for them, and re-layouts  16.1 us
    all_to_all x1, blocking collectives, per_device(): lax.all_to_all(parts.reshape(groups * back, plan.share, plan.slots), ('gr...  14.2 us
    pallas_call x3, Pallas kernels, scalar_call(): pl.pallas_call(kernel, out_shape=outs, grid_spec=pltpu.PrefetchScalarGrid...  12.8 us
    ppermute x4, waiting for transfers between devices, swap(): return lax.ppermute(x, names, [(at, at ^ step) for at in range(size)])  11.6 us
    pallas_call x1, Pallas kernels, per_device(): pl.pallas_call(normalize, out_shape=shape((moves, width), BF16), in_specs...  10 us
    all_to_all x1, starting transfers between devices, per_device(): lax.all_to_all(packed, ('line', 'pair'), split_axis=0, concat_axis=0, til...  7.26 us
    ppermute x4, starting transfers between devices, swap(): return lax.ppermute(x, names, [(at, at ^ step) for at in range(size)])  5.69 us
    all_to_all x1, starting transfers between devices, per_device(): lax.all_to_all(queries, 'line', split_axis=0, concat_axis=0, tiled=True)  4.53 us
  transfers between devices with their start and end apart: 6, of which 2 were waited for; matrix products, arithmetic and copies ran while one was open for 2% of the time, Pallas kernels for 12%

profile of v4, /device:TPU:0, one launch (start us, length us, event | category | flops | bytes accessed | tf_op | source)
XLA Modules:
  0.0 89.9 jit_solution(4532558180873602254)
XLA Ops:
  0.0 0.9 %copy-done.6 = bf16[512,256]{1,0:T(8,128)(2,1)S(1)} copy-done((bf16[512,256]{1,0:T(8,128)(2,1)S(1)}, bf16[512,256]{1,0:T(8,128)(2,1)}, u32[]{:S(2)}) %copy-start.6) | copy-done | bytes 262168
  1.0 0.7 copy-done.7
  1.6 0.7 copy-done.10
  3.0 2.9 %shard_map.100.after_ref = bf16[8,104,512]{2,1,0:T(8,128)(2,1)} custom-call(s32[1]{0:T(128)} %bitcast.1.at_ref, bf16[512,1024]{1,0:T(8,128)(2,1)} %wq_hbm.1, bf16[512,256]{1,0:T(8,128)(2,1)S(1)} %copy-done.6, bf16[8,128]{1,0:T(8,128)(2,1)S(1)} %bitcast.21, s32[1,512]{1,0:T(1,128)S(1)} %bitcast.18, s32[1,512]{1,0:T(1,128)S(1)} %bitcast.23), custom_call_target="tpu_custom_call" | custom-call | flops 436207616 | bytes 2097152 | tf_op jit(solution)/shard_map/pallas_call | solution.py:329
  5.9 7.3 %all-to-all-start = ((bf16[8,104,512]{2,1,0:T(8,128)(2,1)}), bf16[8,104,512]{2,1,0:T(8,128)(2,1)S(1)}, u32[]{:S(2)}, u32[]{:S(2)}) async-start(bf16[8,104,512]{2,1,0:T(8,128)(2,1)} %shard_map.100.after_ref), calls=%async_computation | async-start | bytes 1703936 | tf_op jit(solution)/shard_map/all_to_all | solution.py:409
  13.2 1.2 %copy-done.3 = bf16[8,256,256]{2,1,0:T(8,128)(2,1)S(1)} copy-done((bf16[8,256,256]{2,1,0:T(8,128)(2,1)S(1)}, bf16[8,256,256]{2,1,0:T(8,128)(2,1)}, u32[]{:S(2)}) %copy-start.3) | copy-done | bytes 1048600
  14.4 0.7 copy-done.11
  15.4 2.1 %collective-permute-start = (bf16[9,256,128]{2,1,0:T(8,128)(2,1)S(1)}, bf16[9,256,128]{2,1,0:T(8,128)(2,1)S(1)}, u32[]{:S(2)}, u32[]{:S(2)}) collective-permute-start(bf16[9,256,128]{2,1,0:T(8,128)(2,1)S(1)} %shard_map.102.rest_0_), channel_id=1, source_target_pairs={{0,2},{2,0},{16,18},{18,16},{1,3},{3,1},{17,19},{19,17},{4,6},{6,4... | collective-permute-start | bytes 1769480 | tf_op jit(solution)/shard_map/ppermute | solution.py:349
  17.5 1.5 %collective-permute-start.1 = (bf16[9,256,128]{2,1,0:T(8,128)(2,1)S(1)}, bf16[9,256,128]{2,1,0:T(8,128)(2,1)S(1)}, u32[]{:S(2)}, u32[]{:S(2)}) collective-permute-start(bf16[9,256,128]{2,1,0:T(8,128)(2,1)S(1)} %shard_map.102.rest_0_), channel_id=1, source_target_pairs={{0,16},{2,18},{16,0},{18,2},{1,17},{3,19},{17,1},{19,3},{4,20},{6,... | collective-permute-start | bytes 1769480 | tf_op jit(solution)/shard_map/ppermute | solution.py:349
  19.0 0.7 reshape.42.gain_ref
  19.7 0.8 constant_dynamic-slice_fusion
  21.5 3.4 %copy-done.2 = bf16[1024,4096]{1,0:T(8,128)(2,1)S(1)} copy-done((bf16[1024,4096]{1,0:T(8,128)(2,1)S(1)}, bf16[1024,4096]{1,0:T(8,128)(2,1)}, u32[]{:S(2)}) %copy-start.2) | copy-done | bytes 8388632
  24.9 10.0 %shard_map.101.normed_ref = bf16[1024,4096]{1,0:T(8,128)(2,1)S(1)} custom-call(bf16[1024,4096]{1,0:T(8,128)(2,1)S(1)} %copy-done.2, bf16[1,4096]{1,0:T(2,128)(2,1)S(1)} %reshape.42.gain_ref, bf16[8,104,512]{2,1,0:T(8,128)(2,1)} %shard_map.100.after_ref), custom_call_target="tpu_custom_call" | custom-call | flops 33554432 | bytes 8388608 | tf_op jit(solution)/shard_map/pallas_call | solution.py:431
  34.9 3.2 %copy-done = bf16[1024,4096]{1,0:T(8,128)(2,1)} copy-done((bf16[1024,4096]{1,0:T(8,128)(2,1)}, bf16[1024,4096]{1,0:T(8,128)(2,1)S(1)}, u32[]{:S(2)}) %copy-start) | copy-done | bytes 8388632
  38.2 3.8 %copy-done.1 = bf16[1024,4096]{1,0:T(8,128)(2,1)S(1)} copy-done((bf16[1024,4096]{1,0:T(8,128)(2,1)S(1)}, bf16[1024,4096]{1,0:T(8,128)(2,1)}, u32[]{:S(2)}) %copy-start.1) | copy-done | bytes 8388632
  42.0 3.7 %shard_map.104 = (bf16[4,72,1024]{2,1,0:T(8,128)(2,1)}, f32[2,1024]{1,0:T(2,128)S(1)}) custom-call(bf16[8,104,512]{2,1,0:T(8,128)(2,1)S(1)} %all-to-all-done.w_ref, bf16[1024,4096]{1,0:T(8,128)(2,1)S(1)} %copy-done.1, f32[32,2]{1,0:T(8,128)S(1)} %bitcast.16, bf16[9,256,128]{2,1,0:T(8,128)(2,1)S(1)} %collective-permute-done.rest_0_.rest_1_, ...), custom_call_target="tpu_custom_call" | custom-call | flops 2147483648 | bytes 8388608 | tf_op jit(solution)/shard_map/pallas_call | solution.py:443
  45.7 4.5 %all-to-all-start.1 = ((bf16[4,72,1024]{2,1,0:T(8,128)(2,1)}), bf16[4,72,1024]{2,1,0:T(8,128)(2,1)S(1)}, u32[]{:S(2)}, u32[]{:S(2)}) async-start(bf16[4,72,1024]{2,1,0:T(8,128)(2,1)} %get-tuple-element.7), calls=%async_computation.1 | async-start | bytes 1179648 | tf_op jit(solution)/shard_map/all_to_all | solution.py:450
  50.2 0.7 collective-permute-start.2
  51.1 1.4 %collective-permute-start.3 = (f32[16,128]{1,0:T(8,128)S(1)}, f32[16,128]{1,0:T(8,128)S(1)}, u32[]{:S(2)}, u32[]{:S(2)}) collective-permute-start(f32[16,128]{1,0:T(8,128)S(1)} %shard_map.105), channel_id=1, source_target_pairs={{0,16},{2,18},{16,0},{18,2},{1,17},{3,19},{17,1},{19,3},{4,20},{6,... | collective-permute-start | bytes 24584 | tf_op jit(solution)/shard_map/ppermute | solution.py:349
  52.5 11.6 %collective-permute-done.3 = f32[16,128]{1,0:T(8,128)S(1)} collective-permute-done((f32[16,128]{1,0:T(8,128)S(1)}, f32[16,128]{1,0:T(8,128)S(1)}, u32[]{:S(2)}, u32[]{:S(2)}) %collective-permute-start.3) | collective-permute-done | bytes 8224 | tf_op jit(solution)/shard_map/ppermute | solution.py:349
  64.1 0.9 %all-to-all-done.1 = bf16[4,72,1024]{2,1,0:T(8,128)(2,1)S(1)} async-done(((bf16[4,72,1024]{2,1,0:T(8,128)(2,1)}), bf16[4,72,1024]{2,1,0:T(8,128)(2,1)S(1)}, u32[]{:S(2)}, u32[]{:S(2)}) %all-to-all-start.1) | async-done | bytes 589856 | tf_op jit(solution)/shard_map/all_to_all | solution.py:450
  65.0 9.6 %shard_map.106 = f32[2,16,16,128]{3,2,1,0:T(8,128)S(1)} custom-call(s32[1]{0:T(128)} %bitcast.at_ref, bf16[288,1024]{1,0:T(8,128)(2,1)S(1)} %bitcast.14, bf16[272,288]{1,0:T(8,128)(2,1)S(1)} %copy-done.13, f32[2,1024]{1,0:T(2,128)S(1)} %get-tuple-element.8.vo_ref, bf16[9,256,128]{2,1,0:T(8,128)(2,1)S(1)} %shard_map.102.rest_0_, ...), custom_call_target="tpu_custom_call" | custom-call | flops 2281701376 | bytes 4000000 | tf_op jit(solution)/shard_map/pallas_call | solution.py:329
  74.6 14.2 %all_to_all.15 = f32[32,16,128]{2,1,0:T(8,128)S(1)} all-to-all(f32[32,16,128]{2,1,0:T(8,128)S(1)} %bitcast.15), channel_id=1, replica_groups=mesh['groups'=2,'line'=4,'pair'=2,'tensor'=2] {'groups','line','pair','t..., dimensions={0} | all-to-all | bytes 524288 | tf_op jit(solution)/shard_map/all_to_all | solution.py:483
  88.9 1.1 %shard_map.107 = f32[1,512]{1,0:T(1,128)} custom-call(f32[2,4,4,16,128]{4,3,2,1,0:T(8,128)S(1)} %bitcast.13, s32[1,512]{1,0:T(1,128)S(1)} %bitcast.20, s32[1,512]{1,0:T(1,128)S(1)} %shard_map.103.rest_2_.slot_ref), custom_call_target="tpu_custom_call" | custom-call | tf_op jit(solution)/shard_map/pallas_call | solution.py:491
  (30 shorter events, 2.3 us)
Async XLA Ops:
  0.0 0.9 %copy-start.6 = (bf16[512,256]{1,0:T(8,128)(2,1)S(1)}, bf16[512,256]{1,0:T(8,128)(2,1)}, u32[]{:S(2)}) copy-start(bf16[512,256]{1,0:T(8,128)(2,1)} %wkv_hbm.1) | copy-start | bytes 786436
  1.0 0.7 copy-start.7
  1.6 0.7 copy-start.10
  2.3 0.7 copy-start.12
  5.9 32.3 %all-to-all-start = ((bf16[8,104,512]{2,1,0:T(8,128)(2,1)}), bf16[8,104,512]{2,1,0:T(8,128)(2,1)S(1)}, u32[]{:S(2)}, u32[]{:S(2)}) async-start(bf16[8,104,512]{2,1,0:T(8,128)(2,1)} %shard_map.100.after_ref), calls=%async_computation | async-start | bytes 1703936 | tf_op jit(solution)/shard_map/all_to_all | solution.py:409
  13.2 1.2 %copy-start.3 = (bf16[8,256,256]{2,1,0:T(8,128)(2,1)S(1)}, bf16[8,256,256]{2,1,0:T(8,128)(2,1)}, u32[]{:S(2)}) copy-start(bf16[8,256,256]{2,1,0:T(8,128)(2,1)} %prefix_ref.1) | copy-start | bytes 3145732
  14.4 0.7 copy-start.11
  15.4 22.8 %collective-permute-start = (bf16[9,256,128]{2,1,0:T(8,128)(2,1)S(1)}, bf16[9,256,128]{2,1,0:T(8,128)(2,1)S(1)}, u32[]{:S(2)}, u32[]{:S(2)}) collective-permute-start(bf16[9,256,128]{2,1,0:T(8,128)(2,1)S(1)} %shard_map.102.rest_0_), channel_id=1, source_target_pairs={{0,2},{2,0},{16,18},{18,16},{1,3},{3,1},{17,19},{19,17},{4,6},{6,4... | collective-permute-start | bytes 1769480 | tf_op jit(solution)/shard_map/ppermute | solution.py:349
  17.5 20.7 %collective-permute-start.1 = (bf16[9,256,128]{2,1,0:T(8,128)(2,1)S(1)}, bf16[9,256,128]{2,1,0:T(8,128)(2,1)S(1)}, u32[]{:S(2)}, u32[]{:S(2)}) collective-permute-start(bf16[9,256,128]{2,1,0:T(8,128)(2,1)S(1)} %shard_map.102.rest_0_), channel_id=1, source_target_pairs={{0,16},{2,18},{16,0},{18,2},{1,17},{3,19},{17,1},{19,3},{4,20},{6,... | collective-permute-start | bytes 1769480 | tf_op jit(solution)/shard_map/ppermute | solution.py:349
  20.6 0.7 copy-start.8
  21.5 3.4 %copy-start.2 = (bf16[1024,4096]{1,0:T(8,128)(2,1)S(1)}, bf16[1024,4096]{1,0:T(8,128)(2,1)}, u32[]{:S(2)}) copy-start(bf16[1024,4096]{1,0:T(8,128)(2,1)} %table_hbm.1) | copy-start | bytes 25165828
  24.9 40.1 %copy-start.13 = (bf16[272,288]{1,0:T(8,128)(2,1)S(1)}, bf16[272,288]{1,0:T(8,128)(2,1)}, u32[]{:S(2)}) copy-start(bf16[272,288]{1,0:T(8,128)(2,1)} %constant.26.clone.order_ref) | copy-start | bytes 470020
  34.9 3.3 %copy-start = (bf16[1024,4096]{1,0:T(8,128)(2,1)}, bf16[1024,4096]{1,0:T(8,128)(2,1)S(1)}, u32[]{:S(2)}) copy-start(bf16[1024,4096]{1,0:T(8,128)(2,1)S(1)} %shard_map.101.normed_ref) | copy-start | bytes 25165828
  38.2 26.8 %copy-start.4 = (bf16[9,256,128]{2,1,0:T(8,128)(2,1)}, bf16[9,256,128]{2,1,0:T(8,128)(2,1)S(1)}, u32[]{:S(2)}) copy-start(bf16[9,256,128]{2,1,0:T(8,128)(2,1)S(1)} %collective-permute-done.rest_0_.rest_1_) | copy-start | bytes 1769476
  38.2 26.8 %copy-start.5 = (bf16[9,256,128]{2,1,0:T(8,128)(2,1)}, bf16[9,256,128]{2,1,0:T(8,128)(2,1)S(1)}, u32[]{:S(2)}) copy-start(bf16[9,256,128]{2,1,0:T(8,128)(2,1)S(1)} %collective-permute-done.1.rest_1_.rest_2_) | copy-start | bytes 1769476
  38.2 3.8 %copy-start.1 = (bf16[1024,4096]{1,0:T(8,128)(2,1)S(1)}, bf16[1024,4096]{1,0:T(8,128)(2,1)}, u32[]{:S(2)}) copy-start(bf16[1024,4096]{1,0:T(8,128)(2,1)} %copy-done) | copy-start | bytes 25165828
  42.0 46.8 %copy-start.9 = (s32[512,1]{0,1:T(1,128)S(1)}, s32[512,1]{0,1:T(1,128)}, u32[]{:S(2)}) copy-start(s32[512,1]{0,1:T(1,128)} %param.12) | copy-start | bytes 6148
  45.7 19.3 %all-to-all-start.1 = ((bf16[4,72,1024]{2,1,0:T(8,128)(2,1)}), bf16[4,72,1024]{2,1,0:T(8,128)(2,1)S(1)}, u32[]{:S(2)}, u32[]{:S(2)}) async-start(bf16[4,72,1024]{2,1,0:T(8,128)(2,1)} %get-tuple-element.7), calls=%async_computation.1 | async-start | bytes 1179648 | tf_op jit(solution)/shard_map/all_to_all | solution.py:450
  50.2 13.9 %collective-permute-start.2 = (bf16[9,256,128]{2,1,0:T(8,128)(2,1)S(1)}, bf16[9,256,128]{2,1,0:T(8,128)(2,1)}, u32[]{:S(2)}, u32[]{:S(2)}) collective-permute-start(bf16[9,256,128]{2,1,0:T(8,128)(2,1)S(1)} %collective-permute-done.rest_0_.rest_1_), channel_id=1, source_target_pairs={{0,16},{2,18},{16,0},{18,2},{1,17},{3,19},{17,1},{19,3},{4,20},{6,... | collective-permute-start | bytes 1769480 | tf_op jit(solution)/shard_map/ppermute | solution.py:349
  51.1 12.9 %collective-permute-start.3 = (f32[16,128]{1,0:T(8,128)S(1)}, f32[16,128]{1,0:T(8,128)S(1)}, u32[]{:S(2)}, u32[]{:S(2)}) collective-permute-start(f32[16,128]{1,0:T(8,128)S(1)} %shard_map.105), channel_id=1, source_target_pairs={{0,16},{2,18},{16,0},{18,2},{1,17},{3,19},{17,1},{19,3},{4,20},{6,... | collective-permute-start | bytes 24584 | tf_op jit(solution)/shard_map/ppermute | solution.py:349

commit v5 on v4

--- a/solution.py
+++ b/solution.py
@@ -52,16 +52,22 @@
         self.slots = self.peers * capacity
 
 
-def pack_weights(plan, at_ref, wq_hbm, wkv_hbm, ws_ref, board_ref, ids_ref, out_ref, wq, wkv, pick, sems):
+def pack_weights(plan, at_ref, wq_hbm, wkv_hbm, ws_hbm, board_hbm, ids_hbm, out_ref, *scratch):
+    wq, wkv, ws_ref, board_ref, ids_ref, pick, sems = scratch
     group = at_ref[0]
     rows, half_cols = plan.rows, wq.shape[1]
     columns_here = pl.ds(pl.multiple_of(group * half_cols, HD), half_cols)
     copies = (
-        pltpu.make_async_copy(wq_hbm.at[:, columns_here], wq, sems.at[0]),
-        pltpu.make_async_copy(wkv_hbm, wkv, sems.at[1]),
+        pltpu.make_async_copy(ws_hbm, ws_ref, sems.at[0]),
+        pltpu.make_async_copy(board_hbm, board_ref, sems.at[1]),
+        pltpu.make_async_copy(ids_hbm, ids_ref, sems.at[2]),
+        pltpu.make_async_copy(wq_hbm.at[:, columns_here], wq, sems.at[3]),
+        pltpu.make_async_copy(wkv_hbm, wkv, sems.at[4]),
     )
     for copy in copies:
         copy.start()
+    for copy in copies[:3]:
+        copy.wait()
     r = lax.broadcasted_iota(jnp.int32, (rows, 1), 0)
     part = r // (plan.mine * plan.pairs)
     head = (r // plan.pairs) % plan.mine
@@ -112,7 +118,7 @@
         found = matmul(parts, jnp.where(key == place, 1.0, 0.0).astype(BF16))
         lists.append(jnp.where(lane_row < span, found[0:1], found[1:2]))
 
-    for copy in copies:
+    for copy in copies[3:]:
         copy.wait()
     left = pick[...].astype(BF16)
     total = matmul(left[:, :half_cols], wq[...], NT) + matmul(left[:, half_cols:], wkv[...], NT)
@@ -121,56 +127,45 @@
         out_ref[peer] = jnp.where(r == plan.list_at, lists[peer // plan.pair], mine).astype(BF16)
 
 
-def normalize(table_hbm, gain_ref, after_ref, out_ref, buffers, sems):
-    held, block, width = buffers.shape
-    steps = table_hbm.shape[0] // block
+def normalize(table_ref, gain_ref, after_ref, out_ref):
+    raw = table_ref[...].astype(F32)
+    inverse = lax.rsqrt(jnp.mean(raw * raw, axis=-1, keepdims=True) + EPS)
+    out_ref[...] = (raw * inverse * gain_ref[...].astype(F32)).astype(BF16)
+
+
+def project(plan, w_ref, normed_hbm, turn_ref, *rest):
+    q_ref, vo_ref, buffers, total_ref, sems = rest[-5:]
+    moves = normed_hbm.shape[0]
+    held, _, depth = buffers.shape
+    steps = normed_hbm.shape[1] // depth
 
     def copy(step):
         at = step % held
-        return pltpu.make_async_copy(table_hbm.at[pl.ds(step * block, block)], buffers.at[at], sems.at[at])
-
-    for step in range(min(held - 1, steps)):
+        return pltpu.make_async_copy(normed_hbm.at[:, step * depth : (step + 1) * depth], buffers.at[at], sems.at[at])
+
+    for step in range(min(held, steps)):
         copy(step).start()
-    gain = gain_ref[...].astype(F32)
     for step in range(steps):
-        if step + held - 1 < steps:
-            copy(step + held - 1).start()
         copy(step).wait()
-
-        def one(tile, carry):
-            raw = buffers[step % held, pl.ds(pl.multiple_of(tile * 16, 16), 16)].astype(F32)
-            inverse = lax.rsqrt(jnp.mean(raw * raw, axis=-1, keepdims=True) + EPS)
-            at = pl.ds(pl.multiple_of(step * block + tile * 16, 16), 16)
-            out_ref[at, :] = (raw * inverse * gain).astype(BF16)
-            return carry
-
-        lax.fori_loop(0, block // 16, one, 0)
-
-
-def project(plan, w_ref, normed_ref, turn_ref, *rest):
-    q_ref, vo_ref = rest[-2:]
-    moves = normed_ref.shape[0]
-    block = min(moves, 256)
+        w = w_ref[step] if len(w_ref.shape) == 3 else w_ref[:, step * depth : (step + 1) * depth]
+        term = matmul(w, buffers[step % held], NT)
+        total_ref[...] = term if step == 0 else total_ref[...] + term
+        if step + held < steps:
+            copy(step + held).start()
+
     half, k_half = plan.q_rows // 2, plan.k_rows // 2
     cosine, sine = turn_ref[:, 0:1], turn_ref[:, 1:2]
+    cos_k, sin_k = cosine[:k_half], sine[:k_half]
+    block = min(moves, 256)
     for start in range(0, moves, block):
         at = slice(start, start + block)
-        if len(w_ref.shape) == 3:
-            depth = w_ref.shape[2]
-            total = None
-            for s in range(w_ref.shape[0]):
-                term = matmul(w_ref[s], normed_ref[at, s * depth : (s + 1) * depth], NT)
-                total = term if total is None else total + term
-        else:
-            total = matmul(w_ref[...], normed_ref[at, :], NT)
+        total = total_ref[:, at]
         first, second = total[:half], total[half : 2 * half]
-        q_first = (first * cosine - second * sine).astype(BF16)
-        q_second = (second * cosine + first * sine).astype(BF16)
+        f_first = (first * cosine - second * sine).astype(BF16).astype(F32)
+        f_second = (second * cosine + first * sine).astype(BF16).astype(F32)
         first, second = total[plan.q_rows : plan.q_rows + k_half], total[plan.q_rows + k_half : plan.fold_at]
-        cos_k, sin_k = cosine[:k_half], sine[:k_half]
         k_first = (first * cos_k - second * sin_k).astype(BF16).astype(F32)
         k_second = (second * cos_k + first * sin_k).astype(BF16).astype(F32)
-        f_first, f_second = q_first.astype(F32), q_second.astype(F32)
         logits, tails = [], []
         for h in range(plan.mine):
             own = slice(h * k_half, (h + 1) * k_half)
@@ -182,8 +177,8 @@
         if pad:
             pieces.append(jnp.zeros((pad, block), F32))
         out = jnp.concatenate(pieces, axis=0).astype(BF16)
-        for copy in range(q_ref.shape[0]):
-            q_ref[copy, :, at] = out
+        for copy_at in range(q_ref.shape[0]):
+            q_ref[copy_at, :, at] = out
         vo_ref[:, at] = total[plan.fold_at : plan.list_at]
 
 
@@ -236,7 +231,7 @@
 
 def attend(plan, at_ref, q_ref, order_ref, vo_ref, *rest):
     prefix_refs = rest[: plan.slab]
-    moves_ref, out_ref, table, extra, scores = rest[plan.slab :]
+    moves_ref, out_ref, table, extra, scores, taken_even, taken_odd = rest[plan.slab :]
     here = at_ref[0]
     mine, heads, slots = plan.mine, plan.heads, plan.slots
     moves = q_ref.shape[1]
@@ -263,10 +258,17 @@
         pieces = [x[base + h : base + h + 1] + x[base + mine + h : base + mine + h + 1] for h in range(mine)]
         return jnp.concatenate(pieces, axis=1)
 
-    def step(board, carry):
-        listed = [moves_ref[j // plan.pair, pl.ds(((here ^ j) % plan.pair) * boards + board, 1), :] for j in range(plan.slab)]
-        chosen = [jnp.where(move_at == row, 1.0, 0.0).astype(BF16) for row in listed]
-        taken = matmul(table[...], jnp.concatenate(chosen, axis=1))
+    def moves_of(j, board):
+        place = ((here ^ j) % plan.pair) * boards + board
+        return moves_ref[j // plan.pair, pl.ds(place, 1), :]
+
+    def gather(board, taken):
+        chosen = [
+            jnp.where(move_at == moves_of(j, board), 1.0, 0.0).astype(BF16) for j in range(plan.slab)
+        ]
+        taken[...] = matmul(table[...], jnp.concatenate(chosen, axis=1))
+
+    def score_board(board, taken):
         at = fold_row - board * span
         fold_pick = jnp.where((at == fold_head) | (at == fold_head + heads), 1.0, 0.0).astype(BF16)
         for j in range(plan.slab):
@@ -282,10 +284,19 @@
             denom = jnp.sum(weight, axis=0, keepdims=True) + own_weight
             value = (jnp.sum(weight * fold, axis=0, keepdims=True) + own_value * own_weight) / denom
             score = sum(value[:, h * slots : (h + 1) * slots] for h in range(mine))
-            scores[here ^ j, pl.ds(board, 1), :] = jnp.where(listed[j] > 0, score, DEAD)
+            scores[here ^ j, pl.ds(board, 1), :] = jnp.where(moves_of(j, board) > 0, score, DEAD)
+
+    gather(0, taken_even)
+
+    def step(at, carry):
+        board = 2 * at
+        gather(jnp.minimum(board + 1, boards - 1), taken_odd)
+        score_board(board, taken_even)
+        gather(jnp.minimum(board + 2, boards - 1), taken_even)
+        score_board(jnp.minimum(board + 1, boards - 1), taken_odd)
         return carry
 
-    lax.fori_loop(0, boards, step, 0)
+    lax.fori_loop(0, -(-boards // 2), step, 0)
     for g in range(plan.groups):
         both = jnp.concatenate([scores[g * plan.pair + p] for p in range(plan.pair)], axis=0)
         for copy in range(out_ref.shape[1]):
@@ -323,7 +334,7 @@
     return pl.BlockSpec(memory_space=pl.ANY)
 
 
-def scalar_call(kernel, at, args, outs, scratch, cost=None, specs=None):
+def scalar_call(kernel, at, args, outs, scratch, cost=None, specs=None, mib=VMEM_MIB):
     whole = lambda x: pl.BlockSpec(x.shape, lambda i, at, n=len(x.shape): (0,) * n)
     specs = specs or {}
     return pl.pallas_call(
@@ -336,7 +347,7 @@
             out_specs=jax.tree.map(whole, outs),
             scratch_shapes=scratch,
         ),
-        compiler_params=limits(VMEM_MIB),
+        compiler_params=limits(mib),
         cost_estimate=cost,
     )(at, *args)
 
@@ -400,11 +411,15 @@
         [
             pltpu.VMEM((depth, half_cols), BF16),
             pltpu.VMEM((depth, 2 * HD), BF16),
+            pltpu.VMEM((heads, HD), BF16),
+            pltpu.VMEM((1, row_count), jnp.int32),
+            pltpu.VMEM((1, row_count), jnp.int32),
             pltpu.VMEM((plan.peers * plan.rows, half_cols + 2 * HD), F32),
-            pltpu.SemaphoreType.DMA((2,)),
+            pltpu.SemaphoreType.DMA((5,)),
         ],
         cost(2 * plan.peers * plan.rows * half_cols * depth, 4 * w_query.size),
-        {0: untouched(), 1: untouched()},
+        {at: untouched() for at in range(5)},
+        62,
     )
     weights = lax.all_to_all(packed, ("line", "pair"), split_axis=0, concat_axis=0, tiled=True)
 
@@ -431,20 +446,37 @@
     normed = pl.pallas_call(
         normalize,
         out_shape=shape((moves, width), BF16),
-        in_specs=[untouched(), pl.BlockSpec(memory_space=pltpu.VMEM), untouched()],
-        out_specs=pl.BlockSpec(memory_space=pltpu.VMEM),
-        scratch_shapes=[pltpu.VMEM((3, block, width), BF16), pltpu.SemaphoreType.DMA((3,))],
-        compiler_params=limits(32),
-        cost_estimate=cost(8 * moves * width, 2 * moves * width),
+        grid=(moves // block,),
+        in_specs=[
+            pl.BlockSpec((block, width), lambda i: (i, 0)),
+            pl.BlockSpec((1, width), lambda i: (0, 0)),
+            untouched(),
+        ],
+        out_specs=pl.BlockSpec((block, width), lambda i: (i, 0)),
+        compiler_params=limits(57),
+        cost_estimate=cost(8 * moves * width, 4 * moves * width),
     )(move_table, norm_gain.reshape(1, width), packed)
     turns = jnp.asarray(turn_table(prefix_len))
     my_turns = jnp.tile(lax.dynamic_slice_in_dim(turns, line_at * plan.pairs, plan.pairs, axis=0), (plan.mine, 1))
     flat = weights.transpose(1, 0, 2).reshape(plan.rows, width) if depth % HD else weights
+    chunk = width // 8 if depth % HD else depth
     queries, own_values = pl.pallas_call(
         functools.partial(project, plan),
         out_shape=(shape((line, plan.line_rows, moves), BF16), shape((plan.mine, moves), F32)),
-        in_specs=[pl.BlockSpec(memory_space=pltpu.VMEM)] * 3 + [untouched()] * 3,
-        compiler_params=limits(32),
+        in_specs=[
+            pl.BlockSpec(memory_space=pltpu.VMEM),
+            untouched(),
+            pl.BlockSpec(memory_space=pltpu.VMEM),
+            untouched(),
+            untouched(),
+            untouched(),
+        ],
+        scratch_shapes=[
+            pltpu.VMEM((4, moves, chunk), BF16),
+            pltpu.VMEM((plan.rows, moves), F32),
+            pltpu.SemaphoreType.DMA((4,)),
+        ],
+        compiler_params=limits(57),
         cost_estimate=cost(2 * moves * width * 256, 2 * moves * width),
     )(flat, normed, my_turns, beside, across, slot_row)
     queries = lax.all_to_all(queries, "line", split_axis=0, concat_axis=0, tiled=True)
@@ -477,6 +509,8 @@
             pltpu.VMEM((query_rows + 16, moves), BF16),
             pltpu.VMEM((16, moves), F32),
             pltpu.VMEM((plan.slab, boards_here, plan.slots), F32),
+            pltpu.VMEM((query_rows + 16, plan.slab * plan.slots), F32),
+            pltpu.VMEM((query_rows + 16, plan.slab * plan.slots), F32),
         ],
         cost(2 * 272 * moves * 4096, 4 * 10**6),
     )

time: 90.6 us -> 89.7 us (0.990)
  local copies, waits for them, and re-layouts: 17.6 us -> 11 us
  Pallas kernels: 28 us -> 31.3 us
  waiting for transfers between devices: 12.5 us -> 13.7 us
    unnamed x29 -> x31, local copies, waits for them, and re-layouts: 16.1 us -> 8.31 us
    pallas_call x1, Pallas kernels: 3.66 us -> 6.5 us  [per_device(): pl.pallas_call(functools.partial(project, plan), out_shape=(shape((line,...]
    ppermute x4, waiting for transfers between devices: 11.6 us -> 13 us  [swap(): return lax.ppermute(x, names, [(at, at ^ step) for at in range(size)])]
  transfers between devices with their start and end apart: 6 -> 6, of which waited for: 2 -> 3; matrix products, arithmetic and copies ran while one was open for 2% -> 2% of each run, Pallas kernels for 12% -> 13%
where the time goes in v5:
time: 89.7 us; the launch traced here: 88.8 us
  Pallas kernels  31.3 us (35%)
  starting transfers between devices  17.7 us (20%)
  blocking collectives  15 us (17%)
  waiting for transfers between devices  13.7 us (15%)
  local copies, waits for them, and re-layouts  11 us (12%)
    all_to_all x1, blocking collectives, per_device(): lax.all_to_all(parts.reshape(groups * back, plan.share, plan.slots), ('gr...  15 us
    ppermute x4, waiting for transfers between devices, swap(): return lax.ppermute(x, names, [(at, at ^ step) for at in range(size)])  13 us
    pallas_call x3, Pallas kernels, scalar_call(): pl.pallas_call(kernel, out_shape=outs, grid_spec=pltpu.PrefetchScalarGrid...  12.6 us
    pallas_call x1, Pallas kernels, per_device(): pl.pallas_call(normalize, out_shape=shape((moves, width), BF16), grid=(mo...  10.7 us
    unnamed x31, local copies, waits for them, and re-layouts  8.31 us
    all_to_all x1, starting transfers between devices, per_device(): lax.all_to_all(packed, ('line', 'pair'), split_axis=0, concat_axis=0, til...  7.27 us
    pallas_call x1, Pallas kernels, per_device(): pl.pallas_call(functools.partial(project, plan), out_shape=(shape((line,...  6.5 us
    ppermute x4, starting transfers between devices, swap(): return lax.ppermute(x, names, [(at, at ^ step) for at in range(size)])  5.7 us
  transfers between devices with their start and end apart: 6, of which 3 were waited for; matrix products, arithmetic and copies ran while one was open for 2% of the time, Pallas kernels for 13%

profile of v5, /device:TPU:0, one launch (start us, length us, event | category | flops | bytes accessed | tf_op | source)
XLA Modules:
  0.0 88.8 jit_solution(1779288529021080789)
XLA Ops:
  0.0 3.5 %shard_map.100.after_ref = bf16[8,104,512]{2,1,0:T(8,128)(2,1)} custom-call(s32[1]{0:T(128)} %bitcast.1.at_ref, bf16[512,1024]{1,0:T(8,128)(2,1)} %wq_hbm.1, bf16[512,256]{1,0:T(8,128)(2,1)} %wkv_hbm.1, bf16[8,128]{1,0:T(8,128)(2,1)} %bitcast.20, s32[1,512]{1,0:T(1,128)} %bitcast.17, s32[1,512]{1,0:T(1,128)} %bitcast.24), custom_call_target="tpu_custom_call" | custom-call | flops 436207616 | bytes 2097152 | tf_op jit(solution)/shard_map/pallas_call | solution.py:340
  3.5 7.3 %all-to-all-start = ((bf16[8,104,512]{2,1,0:T(8,128)(2,1)}), bf16[8,104,512]{2,1,0:T(8,128)(2,1)S(1)}, u32[]{:S(2)}, u32[]{:S(2)}) async-start(bf16[8,104,512]{2,1,0:T(8,128)(2,1)} %shard_map.100.after_ref), calls=%async_computation | async-start | bytes 1703936 | tf_op jit(solution)/shard_map/all_to_all | solution.py:424
  10.8 1.2 %copy-done = bf16[8,104,512]{2,1,0:T(8,128)(2,1)S(1)} copy-done((bf16[8,104,512]{2,1,0:T(8,128)(2,1)S(1)}, bf16[8,104,512]{2,1,0:T(8,128)(2,1)}, u32[]{:S(2)}) %copy-start) | copy-done | bytes 851992
  12.0 1.2 %copy-done.4 = bf16[8,256,256]{2,1,0:T(8,128)(2,1)S(1)} copy-done((bf16[8,256,256]{2,1,0:T(8,128)(2,1)S(1)}, bf16[8,256,256]{2,1,0:T(8,128)(2,1)}, u32[]{:S(2)}) %copy-start.4) | copy-done | bytes 1048600
  13.2 0.7 copy-done.9
  14.2 2.1 %collective-permute-start = (bf16[9,256,128]{2,1,0:T(8,128)(2,1)S(1)}, bf16[9,256,128]{2,1,0:T(8,128)(2,1)S(1)}, u32[]{:S(2)}, u32[]{:S(2)}) collective-permute-start(bf16[9,256,128]{2,1,0:T(8,128)(2,1)S(1)} %shard_map.102.rest_0_), channel_id=1, source_target_pairs={{0,2},{2,0},{16,18},{18,16},{1,3},{3,1},{17,19},{19,17},{4,6},{6,4... | collective-permute-start | bytes 1769480 | tf_op jit(solution)/shard_map/ppermute | solution.py:360
  16.3 1.5 %collective-permute-start.1 = (bf16[9,256,128]{2,1,0:T(8,128)(2,1)S(1)}, bf16[9,256,128]{2,1,0:T(8,128)(2,1)S(1)}, u32[]{:S(2)}, u32[]{:S(2)}) collective-permute-start(bf16[9,256,128]{2,1,0:T(8,128)(2,1)S(1)} %shard_map.102.rest_0_), channel_id=1, source_target_pairs={{0,16},{2,18},{16,0},{18,2},{1,17},{3,19},{17,1},{19,3},{4,20},{6,... | collective-permute-start | bytes 1769480 | tf_op jit(solution)/shard_map/ppermute | solution.py:360
  17.8 1.3 %reshape.42.gain_ref = bf16[1,4096]{1,0:T(2,128)(2,1)} reshape(bf16[4096]{0:T(1024)(128)(2,1)} %param.14) | data formatting | bytes 16384 | tf_op jit(solution)/shard_map/reshape | solution.py:458
  19.1 0.7 constant_dynamic-slice_fusion
  19.9 1.2 %copy-done.1 = bf16[8,104,512]{2,1,0:T(8,128)(2,1)S(1)} copy-done((bf16[8,104,512]{2,1,0:T(8,128)(2,1)S(1)}, bf16[8,104,512]{2,1,0:T(8,128)(2,1)}, u32[]{:S(2)}) %copy-start.1) | copy-done | bytes 851992
  21.1 0.7 copy-done.5
  22.6 10.7 %shard_map.101.normed_hbm = bf16[1024,4096]{1,0:T(8,128)(2,1)} custom-call(bf16[1024,4096]{1,0:T(8,128)(2,1)} %table_ref.1, bf16[1,4096]{1,0:T(2,128)(2,1)} %reshape.42.gain_ref, bf16[8,104,512]{2,1,0:T(8,128)(2,1)} %shard_map.100.after_ref), custom_call_target="tpu_custom_call" | custom-call | flops 33554432 | bytes 16777216 | tf_op jit(solution)/shard_map/pallas_call | solution.py:446
  33.4 1.8 %collective-permute-done.rest_0_.rest_1_ = bf16[9,256,128]{2,1,0:T(8,128)(2,1)S(1)} collective-permute-done((bf16[9,256,128]{2,1,0:T(8,128)(2,1)S(1)}, bf16[9,256,128]{2,1,0:T(8,128)(2,1)S(1)}, u32[]{:S(2)}, u32[]{:S(2)}) %collective-permute-start) | collective-permute-done | bytes 589856 | tf_op jit(solution)/shard_map/ppermute | solution.py:360
  35.2 0.6 tile.4.clone
  36.6 6.5 %shard_map.104 = (bf16[4,72,1024]{2,1,0:T(8,128)(2,1)}, f32[2,1024]{1,0:T(2,128)}) custom-call(bf16[8,104,512]{2,1,0:T(8,128)(2,1)} %copy-done.2, bf16[1024,4096]{1,0:T(8,128)(2,1)} %shard_map.101.normed_hbm, f32[32,2]{1,0:T(8,128)} %bitcast.22, bf16[9,256,128]{2,1,0:T(8,128)(2,1)} %copy-done.12, bf16[9,256,128]{2,1,0:T(8,128)(2,1)} %copy-done.13, ...), custom_call_target="tpu_custom_call" | custom-call | flops 2147483648 | bytes 8388608 | tf_op jit(solution)/shard_map/pallas_call | solution.py:463
  43.1 4.7 %all-to-all-start.1 = ((bf16[4,72,1024]{2,1,0:T(8,128)(2,1)}), bf16[4,72,1024]{2,1,0:T(8,128)(2,1)S(1)}, u32[]{:S(2)}, u32[]{:S(2)}) async-start(bf16[4,72,1024]{2,1,0:T(8,128)(2,1)} %get-tuple-element.7), calls=%async_computation.1 | async-start | bytes 1179648 | tf_op jit(solution)/shard_map/all_to_all | solution.py:482
  47.8 1.5 %collective-permute-start.2 = (bf16[9,256,128]{2,1,0:T(8,128)(2,1)}, bf16[9,256,128]{2,1,0:T(8,128)(2,1)S(1)}, u32[]{:S(2)}, u32[]{:S(2)}) collective-permute-start(bf16[9,256,128]{2,1,0:T(8,128)(2,1)} %copy-done.12), channel_id=1, source_target_pairs={{0,16},{2,18},{16,0},{18,2},{1,17},{3,19},{17,1},{19,3},{4,20},{6,... | collective-permute-start | bytes 1769480 | tf_op jit(solution)/shard_map/ppermute | solution.py:360
  49.3 1.2 %copy-done.3 = bf16[8,104,512]{2,1,0:T(8,128)(2,1)S(1)} copy-done((bf16[8,104,512]{2,1,0:T(8,128)(2,1)S(1)}, bf16[8,104,512]{2,1,0:T(8,128)(2,1)}, u32[]{:S(2)}) %copy-start.3) | copy-done | bytes 851992
  51.3 11.1 %collective-permute-done.3 = f32[16,128]{1,0:T(8,128)S(1)} collective-permute-done((f32[16,128]{1,0:T(8,128)S(1)}, f32[16,128]{1,0:T(8,128)S(1)}, u32[]{:S(2)}, u32[]{:S(2)}) %collective-permute-start.3) | collective-permute-done | bytes 8224 | tf_op jit(solution)/shard_map/ppermute | solution.py:360
  62.4 0.7 all-to-all-done.1
  63.2 0.7 copy-done.10
  63.9 8.8 %shard_map.106 = f32[2,16,16,128]{3,2,1,0:T(8,128)S(1)} custom-call(s32[1]{0:T(128)} %bitcast.at_ref, bf16[288,1024]{1,0:T(8,128)(2,1)S(1)} %bitcast.14, bf16[272,288]{1,0:T(8,128)(2,1)S(1)} %copy-done.11, f32[2,1024]{1,0:T(2,128)S(1)} %copy-done.10, bf16[9,256,128]{2,1,0:T(8,128)(2,1)S(1)} %shard_map.102.rest_0_, bf16[9,256,128]{2,1,0:T(8,128)(2,1)} %copy-done.12, ...), custom_call_target="tpu_custom_call" | custom-call | flops 2281701376 | bytes 4000000 | tf_op jit(solution)/shard_map/pallas_call | solution.py:340
  72.7 15.0 %all_to_all.15 = f32[32,16,128]{2,1,0:T(8,128)S(1)} all-to-all(f32[32,16,128]{2,1,0:T(8,128)S(1)} %bitcast.15), channel_id=1, replica_groups=mesh['groups'=2,'line'=4,'pair'=2,'tensor'=2] {'groups','line','pair','t..., dimensions={0} | all-to-all | bytes 524288 | tf_op jit(solution)/shard_map/all_to_all | solution.py:517
  87.8 1.1 %shard_map.107 = f32[1,512]{1,0:T(1,128)} custom-call(f32[2,4,4,16,128]{4,3,2,1,0:T(8,128)S(1)} %bitcast.13, s32[1,512]{1,0:T(1,128)S(1)} %bitcast.19, s32[1,512]{1,0:T(1,128)S(1)} %copy-done.8), custom_call_target="tpu_custom_call" | custom-call | tf_op jit(solution)/shard_map/pallas_call | solution.py:525
  (32 shorter events, 2.9 us)
Async XLA Ops:
  3.5 31.7 %all-to-all-start = ((bf16[8,104,512]{2,1,0:T(8,128)(2,1)}), bf16[8,104,512]{2,1,0:T(8,128)(2,1)S(1)}, u32[]{:S(2)}, u32[]{:S(2)}) async-start(bf16[8,104,512]{2,1,0:T(8,128)(2,1)} %shard_map.100.after_ref), calls=%async_computation | async-start | bytes 1703936 | tf_op jit(solution)/shard_map/all_to_all | solution.py:424
  10.8 1.2 %copy-start = (bf16[8,104,512]{2,1,0:T(8,128)(2,1)S(1)}, bf16[8,104,512]{2,1,0:T(8,128)(2,1)}, u32[]{:S(2)}) copy-start(bf16[8,104,512]{2,1,0:T(8,128)(2,1)} %shard_map.100.after_ref) | copy-start | bytes 2555908
  12.0 1.2 %copy-start.4 = (bf16[8,256,256]{2,1,0:T(8,128)(2,1)S(1)}, bf16[8,256,256]{2,1,0:T(8,128)(2,1)}, u32[]{:S(2)}) copy-start(bf16[8,256,256]{2,1,0:T(8,128)(2,1)} %prefix_ref.1) | copy-start | bytes 3145732
  13.2 0.7 copy-start.9
  14.2 21.0 %collective-permute-start = (bf16[9,256,128]{2,1,0:T(8,128)(2,1)S(1)}, bf16[9,256,128]{2,1,0:T(8,128)(2,1)S(1)}, u32[]{:S(2)}, u32[]{:S(2)}) collective-permute-start(bf16[9,256,128]{2,1,0:T(8,128)(2,1)S(1)} %shard_map.102.rest_0_), channel_id=1, source_target_pairs={{0,2},{2,0},{16,18},{18,16},{1,3},{3,1},{17,19},{19,17},{4,6},{6,4... | collective-permute-start | bytes 1769480 | tf_op jit(solution)/shard_map/ppermute | solution.py:360
  16.3 18.9 %collective-permute-start.1 = (bf16[9,256,128]{2,1,0:T(8,128)(2,1)S(1)}, bf16[9,256,128]{2,1,0:T(8,128)(2,1)S(1)}, u32[]{:S(2)}, u32[]{:S(2)}) collective-permute-start(bf16[9,256,128]{2,1,0:T(8,128)(2,1)S(1)} %shard_map.102.rest_0_), channel_id=1, source_target_pairs={{0,16},{2,18},{16,0},{18,2},{1,17},{3,19},{17,1},{19,3},{4,20},{6,... | collective-permute-start | bytes 1769480 | tf_op jit(solution)/shard_map/ppermute | solution.py:360
  19.9 1.2 %copy-start.1 = (bf16[8,104,512]{2,1,0:T(8,128)(2,1)S(1)}, bf16[8,104,512]{2,1,0:T(8,128)(2,1)}, u32[]{:S(2)}) copy-start(bf16[8,104,512]{2,1,0:T(8,128)(2,1)} %shard_map.100.after_ref) | copy-start | bytes 2555908
  21.1 0.7 copy-start.5
  22.0 0.6 copy-start.7
  33.4 29.9 %copy-start.11 = (bf16[272,288]{1,0:T(8,128)(2,1)S(1)}, bf16[272,288]{1,0:T(8,128)(2,1)}, u32[]{:S(2)}) copy-start(bf16[272,288]{1,0:T(8,128)(2,1)} %constant.26.clone.order_ref) | copy-start | bytes 470020
  35.2 0.8 copy-start.12
  35.2 1.0 %copy-start.13 = (bf16[9,256,128]{2,1,0:T(8,128)(2,1)}, bf16[9,256,128]{2,1,0:T(8,128)(2,1)S(1)}, u32[]{:S(2)}) copy-start(bf16[9,256,128]{2,1,0:T(8,128)(2,1)S(1)} %collective-permute-done.1.rest_1_.rest_2_) | copy-start | bytes 1769476
  35.2 1.4 %copy-start.2 = (bf16[8,104,512]{2,1,0:T(8,128)(2,1)}, bf16[8,104,512]{2,1,0:T(8,128)(2,1)S(1)}, u32[]{:S(2)}) copy-start(bf16[8,104,512]{2,1,0:T(8,128)(2,1)S(1)} %all-to-all-done.w_ref) | copy-start | bytes 2555908
  36.6 51.2 %copy-start.6 = (s32[512,1]{0,1:T(1,128)S(1)}, s32[512,1]{0,1:T(1,128)}, u32[]{:S(2)}) copy-start(s32[512,1]{0,1:T(1,128)} %param.12) | copy-start | bytes 6148
  36.6 51.2 %copy-start.8 = (s32[1,512]{1,0:T(1,128)S(1)}, s32[1,512]{1,0:T(1,128)}, u32[]{:S(2)}) copy-start(s32[1,512]{1,0:T(1,128)} %copy-done.7) | copy-start | bytes 6148
  43.1 20.0 %all-to-all-start.1 = ((bf16[4,72,1024]{2,1,0:T(8,128)(2,1)}), bf16[4,72,1024]{2,1,0:T(8,128)(2,1)S(1)}, u32[]{:S(2)}, u32[]{:S(2)}) async-start(bf16[4,72,1024]{2,1,0:T(8,128)(2,1)} %get-tuple-element.7), calls=%async_computation.1 | async-start | bytes 1179648 | tf_op jit(solution)/shard_map/all_to_all | solution.py:482
  47.8 14.6 %collective-permute-start.2 = (bf16[9,256,128]{2,1,0:T(8,128)(2,1)}, bf16[9,256,128]{2,1,0:T(8,128)(2,1)S(1)}, u32[]{:S(2)}, u32[]{:S(2)}) collective-permute-start(bf16[9,256,128]{2,1,0:T(8,128)(2,1)} %copy-done.12), channel_id=1, source_target_pairs={{0,16},{2,18},{16,0},{18,2},{1,17},{3,19},{17,1},{19,3},{4,20},{6,... | collective-permute-start | bytes 1769480 | tf_op jit(solution)/shard_map/ppermute | solution.py:360
  49.3 1.2 %copy-start.3 = (bf16[8,104,512]{2,1,0:T(8,128)(2,1)S(1)}, bf16[8,104,512]{2,1,0:T(8,128)(2,1)}, u32[]{:S(2)}) copy-start(bf16[8,104,512]{2,1,0:T(8,128)(2,1)} %copy-done.2) | copy-start | bytes 2555908
  50.7 11.7 %collective-permute-start.3 = (f32[16,128]{1,0:T(8,128)S(1)}, f32[16,128]{1,0:T(8,128)S(1)}, u32[]{:S(2)}, u32[]{:S(2)}) collective-permute-start(f32[16,128]{1,0:T(8,128)S(1)} %shard_map.105), channel_id=1, source_target_pairs={{0,16},{2,18},{16,0},{18,2},{1,17},{3,19},{17,1},{19,3},{4,20},{6,... | collective-permute-start | bytes 24584 | tf_op jit(solution)/shard_map/ppermute | solution.py:360
  62.4 0.8 copy-start.14
  63.2 0.7 copy-start.10

commit v6 on v5

--- a/solution.py
+++ b/solution.py
@@ -52,21 +52,22 @@
         self.slots = self.peers * capacity
 
 
-def pack_weights(plan, at_ref, wq_hbm, wkv_hbm, ws_hbm, board_hbm, ids_hbm, out_ref, *scratch):
-    wq, wkv, ws_ref, board_ref, ids_ref, pick, sems = scratch
-    group = at_ref[0]
+def pack_weights(plan, at_ref, wq_hbm, wkv_hbm, ws_hbm, board_hbm, ids_hbm, gain_hbm, out_ref, *scratch):
+    wq, wkv, ws_ref, board_ref, ids_ref, gain_ref, pick, sems = scratch
+    group, peer_at = at_ref[0], at_ref[1]
     rows, half_cols = plan.rows, wq.shape[1]
     columns_here = pl.ds(pl.multiple_of(group * half_cols, HD), half_cols)
     copies = (
         pltpu.make_async_copy(ws_hbm, ws_ref, sems.at[0]),
         pltpu.make_async_copy(board_hbm, board_ref, sems.at[1]),
         pltpu.make_async_copy(ids_hbm, ids_ref, sems.at[2]),
-        pltpu.make_async_copy(wq_hbm.at[:, columns_here], wq, sems.at[3]),
-        pltpu.make_async_copy(wkv_hbm, wkv, sems.at[4]),
+        pltpu.make_async_copy(gain_hbm, gain_ref, sems.at[3]),
+        pltpu.make_async_copy(wq_hbm.at[:, columns_here], wq, sems.at[4]),
+        pltpu.make_async_copy(wkv_hbm, wkv, sems.at[5]),
     )
     for copy in copies:
         copy.start()
-    for copy in copies[:3]:
+    for copy in copies[:4]:
         copy.wait()
     r = lax.broadcasted_iota(jnp.int32, (rows, 1), 0)
     part = r // (plan.mine * plan.pairs)
@@ -118,48 +119,58 @@
         found = matmul(parts, jnp.where(key == place, 1.0, 0.0).astype(BF16))
         lists.append(jnp.where(lane_row < span, found[0:1], found[1:2]))
 
-    for copy in copies[3:]:
+    count, depth = wq.shape
+    gain = gain_ref[...].astype(F32)
+    gain_row = lax.broadcasted_iota(jnp.int32, gain.shape, 0)
+    first = peer_at * (count // gain.shape[1]) if gain.shape[0] > 1 else 0
+    pieces = max(1, count // gain.shape[1])
+    gain = [jnp.sum(jnp.where(gain_row == first + p, gain, 0.0), axis=0, keepdims=True) for p in range(pieces)]
+    gain = jnp.concatenate(gain, axis=1)
+
+    for copy in copies[4:]:
         copy.wait()
     left = pick[...].astype(BF16)
     total = matmul(left[:, :half_cols], wq[...], NT) + matmul(left[:, half_cols:], wkv[...], NT)
     for peer in range(plan.peers):
-        mine = total[peer * rows : (peer + 1) * rows]
+        mine = total[peer * rows : (peer + 1) * rows] * gain
         out_ref[peer] = jnp.where(r == plan.list_at, lists[peer // plan.pair], mine).astype(BF16)
 
 
-def normalize(table_ref, gain_ref, after_ref, out_ref):
+def inverse_norms(table_ref, after_ref, out_ref):
     raw = table_ref[...].astype(F32)
+    count = raw.shape[0]
     inverse = lax.rsqrt(jnp.mean(raw * raw, axis=-1, keepdims=True) + EPS)
-    out_ref[...] = (raw * inverse * gain_ref[...].astype(F32)).astype(BF16)
-
-
-def project(plan, w_ref, normed_hbm, turn_ref, *rest):
-    q_ref, vo_ref, buffers, total_ref, sems = rest[-5:]
-    moves = normed_hbm.shape[0]
-    held, _, depth = buffers.shape
-    steps = normed_hbm.shape[1] // depth
+    out_ref[...] = jnp.broadcast_to(inverse, (count, count)).T[0:1]
+
+
+def project(plan, at_ref, w_ref, table_hbm, inverse_ref, turn_ref, *rest):
+    q_ref, vo_ref, table, sems = rest[-4:]
+    moves, width = table_hbm.shape
+    block = moves // sems.shape[0]
 
     def copy(step):
-        at = step % held
-        return pltpu.make_async_copy(normed_hbm.at[:, step * depth : (step + 1) * depth], buffers.at[at], sems.at[at])
-
-    for step in range(min(held, steps)):
+        at = pl.ds(step * block, block)
+        return pltpu.make_async_copy(table_hbm.at[at], table.at[at], sems.at[step])
+
+    for step in range(sems.shape[0]):
         copy(step).start()
-    for step in range(steps):
+
+    half, k_half = plan.q_rows // 2, plan.k_rows // 2
+    turns = turn_ref[at_ref[0]]
+    cosine, sine = turns[:, 0:1], turns[:, 1:2]
+    cos_k, sin_k = cosine[:k_half], sine[:k_half]
+    for step in range(sems.shape[0]):
         copy(step).wait()
-        w = w_ref[step] if len(w_ref.shape) == 3 else w_ref[:, step * depth : (step + 1) * depth]
-        term = matmul(w, buffers[step % held], NT)
-        total_ref[...] = term if step == 0 else total_ref[...] + term
-        if step + held < steps:
-            copy(step + held).start()
-
-    half, k_half = plan.q_rows // 2, plan.k_rows // 2
-    cosine, sine = turn_ref[:, 0:1], turn_ref[:, 1:2]
-    cos_k, sin_k = cosine[:k_half], sine[:k_half]
-    block = min(moves, 256)
-    for start in range(0, moves, block):
-        at = slice(start, start + block)
-        total = total_ref[:, at]
+        at = slice(step * block, (step + 1) * block)
+        if len(w_ref.shape) == 3:
+            depth = w_ref.shape[2]
+            total = None
+            for s in range(w_ref.shape[0]):
+                term = matmul(w_ref[s], table[at, s * depth : (s + 1) * depth], NT)
+                total = term if total is None else total + term
+        else:
+            total = matmul(w_ref[...], table[at, :], NT)
+        total = total * inverse_ref[:, at]
         first, second = total[:half], total[half : 2 * half]
         f_first = (first * cosine - second * sine).astype(BF16).astype(F32)
         f_second = (second * cosine + first * sine).astype(BF16).astype(F32)
@@ -182,24 +193,19 @@
         vo_ref[:, at] = total[plan.fold_at : plan.list_at]
 
 
-def pack_prefix(prefix_ref, ws_ref, after_ref, out_ref):
-    boards = prefix_ref.shape[0]
-    heads = ws_ref.shape[0]
-    span = HD // boards
-    ws = jnp.concatenate([ws_ref[...].astype(F32)] * (HD // heads), axis=0)
-    row = lax.broadcasted_iota(jnp.int32, (HD, 1), 0)
-    fold = None
-    for board in range(boards):
-        out_ref[board] = prefix_ref[board, :, :HD]
-        keep = (row // span == board) & (row % span < 2 * heads)
-        term = matmul(prefix_ref[board, :, HD:], jnp.where(keep, ws, 0.0).astype(BF16), NT)
-        fold = term if fold is None else fold + term
-    rounded = fold.astype(BF16).astype(F32)
-    lane = lax.broadcasted_iota(jnp.int32, fold.shape, 1)
-    out_ref[boards] = jnp.where(lane % span < heads, rounded, fold - rounded).astype(BF16)
-
-
-def find_slots(plan, at_ref, board_ref, after_ref, slot_ref):
+def pack_prefix(plan, at_ref, prefix_hbm, ws_hbm, board_hbm, after_ref, out_ref, slot_ref, *scratch):
+    values, ws_ref, board_ref, sems = scratch
+    boards = values.shape[0]
+    heads = plan.heads
+    copies = (
+        pltpu.make_async_copy(board_hbm, board_ref, sems.at[0]),
+        pltpu.make_async_copy(ws_hbm, ws_ref, sems.at[1]),
+        pltpu.make_async_copy(prefix_hbm.at[:, :, pl.ds(HD, HD)], values, sems.at[2]),
+        pltpu.make_async_copy(prefix_hbm.at[:, :, pl.ds(0, HD)], out_ref.at[pl.ds(0, boards)], sems.at[3]),
+    )
+    for copy in copies:
+        copy.start()
+    copies[0].wait()
     count = board_ref.shape[1]
     board_row = board_ref[...]
     board_col = jnp.broadcast_to(board_row.astype(F32), (8, count)).T[:, 0:1].astype(jnp.int32)
@@ -207,6 +213,21 @@
     own = lax.broadcasted_iota(jnp.int32, (count, count), 1)
     rank = jnp.sum(jnp.where((board_col == board_row) & (other < own), 1.0, 0.0), axis=0, keepdims=True)
     slot_ref[...] = rank.astype(jnp.int32) + at_ref[0] * plan.capacity
+
+    copies[1].wait()
+    span = HD // boards
+    ws = jnp.concatenate([ws_ref[...].astype(F32)] * (HD // heads), axis=0)
+    row = lax.broadcasted_iota(jnp.int32, (HD, 1), 0)
+    copies[2].wait()
+    fold = None
+    for board in range(boards):
+        keep = (row // span == board) & (row % span < 2 * heads)
+        term = matmul(values[board], jnp.where(keep, ws, 0.0).astype(BF16), NT)
+        fold = term if fold is None else fold + term
+    rounded = fold.astype(BF16).astype(F32)
+    lane = lax.broadcasted_iota(jnp.int32, fold.shape, 1)
+    out_ref[boards] = jnp.where(lane % span < heads, rounded, fold - rounded).astype(BF16)
+    copies[3].wait()
 
 
 def read_lists(plan, w_ref, out_ref):
@@ -402,11 +423,16 @@
     slab_axes = ("groups", "pair")
     board_row = move_board.reshape(1, row_count)
 
+    if depth % HD:
+        gain = lax.dynamic_slice_in_dim(norm_gain, (line_at * pair + pair_at) * depth, depth).reshape(1, depth)
+    else:
+        gain = norm_gain.reshape(width // HD, HD)
+
     half_cols = w_query.shape[1] // groups
     packed = scalar_call(
         functools.partial(pack_weights, plan),
-        group_at.reshape(1),
-        (w_query, w_keyval, ws, board_row, move_ids.reshape(1, row_count)),
+        jnp.stack([group_at, line_at * pair + pair_at]),
+        (w_query, w_keyval, ws, board_row, move_ids.reshape(1, row_count), gain),
         shape((plan.peers, plan.rows, depth), BF16),
         [
             pltpu.VMEM((depth, half_cols), BF16),
@@ -414,73 +440,58 @@
             pltpu.VMEM((heads, HD), BF16),
             pltpu.VMEM((1, row_count), jnp.int32),
             pltpu.VMEM((1, row_count), jnp.int32),
+            pltpu.VMEM(gain.shape, BF16),
             pltpu.VMEM((plan.peers * plan.rows, half_cols + 2 * HD), F32),
-            pltpu.SemaphoreType.DMA((5,)),
+            pltpu.SemaphoreType.DMA((6,)),
         ],
         cost(2 * plan.peers * plan.rows * half_cols * depth, 4 * w_query.size),
-        {at: untouched() for at in range(5)},
+        {at: untouched() for at in range(6)},
         62,
     )
     weights = lax.all_to_all(packed, ("line", "pair"), split_axis=0, concat_axis=0, tiled=True)
 
-    payload = pl.pallas_call(
-        pack_prefix,
-        out_shape=shape((boards_here + 1, prefix_len, HD), BF16),
-        in_specs=[pl.BlockSpec(memory_space=pltpu.VMEM), pl.BlockSpec(memory_space=pltpu.VMEM), untouched()],
-        compiler_params=limits(32),
-        cost_estimate=cost(2 * prefix_len * HD * HD * boards_here, 2 * prefix_kv.size),
-    )(prefix_kv, ws, packed)
+    payload, slot_row = scalar_call(
+        functools.partial(pack_prefix, plan),
+        (line_at * pair + pair_at).reshape(1),
+        (prefix_kv, ws, board_row, packed),
+        (shape((boards_here + 1, prefix_len, HD), BF16), shape((1, row_count), jnp.int32)),
+        [
+            pltpu.VMEM((boards_here, prefix_len, HD), BF16),
+            pltpu.VMEM((heads, HD), BF16),
+            pltpu.VMEM((1, row_count), jnp.int32),
+            pltpu.SemaphoreType.DMA((4,)),
+        ],
+        cost(2 * prefix_len * HD * HD * boards_here, 2 * prefix_kv.size),
+        {at: untouched() for at in range(4)},
+        62,
+    )
     beside = swap(payload, slab_axes, plan.slab, 1)
     across = swap(payload, slab_axes, plan.slab, 2)
-    slot_row = scalar_call(
-        functools.partial(find_slots, plan),
-        (line_at * pair + pair_at).reshape(1),
-        (board_row, packed),
-        shape((1, row_count), jnp.int32),
-        [],
-        cost(4 * row_count * row_count, 4 * row_count),
-        {1: untouched()},
-    )
 
     block = min(moves, 128)
-    normed = pl.pallas_call(
-        normalize,
-        out_shape=shape((moves, width), BF16),
+    inverse = pl.pallas_call(
+        inverse_norms,
+        out_shape=shape((1, moves), F32),
         grid=(moves // block,),
-        in_specs=[
-            pl.BlockSpec((block, width), lambda i: (i, 0)),
-            pl.BlockSpec((1, width), lambda i: (0, 0)),
-            untouched(),
-        ],
-        out_specs=pl.BlockSpec((block, width), lambda i: (i, 0)),
-        compiler_params=limits(57),
-        cost_estimate=cost(8 * moves * width, 4 * moves * width),
-    )(move_table, norm_gain.reshape(1, width), packed)
-    turns = jnp.asarray(turn_table(prefix_len))
-    my_turns = jnp.tile(lax.dynamic_slice_in_dim(turns, line_at * plan.pairs, plan.pairs, axis=0), (plan.mine, 1))
+        in_specs=[pl.BlockSpec((block, width), lambda i: (i, 0)), untouched()],
+        out_specs=pl.BlockSpec((1, block), lambda i: (0, i)),
+        compiler_params=limits(58),
+        cost_estimate=cost(8 * moves * width, 2 * moves * width),
+    )(move_table, packed)
+    turns = turn_table(prefix_len).reshape(line, 1, plan.pairs, 2)
+    turns = jnp.asarray(np.tile(turns, (1, plan.mine, 1, 1)).reshape(line, plan.mine * plan.pairs, 2))
     flat = weights.transpose(1, 0, 2).reshape(plan.rows, width) if depth % HD else weights
-    chunk = width // 8 if depth % HD else depth
-    queries, own_values = pl.pallas_call(
+    queries, own_values = scalar_call(
         functools.partial(project, plan),
-        out_shape=(shape((line, plan.line_rows, moves), BF16), shape((plan.mine, moves), F32)),
-        in_specs=[
-            pl.BlockSpec(memory_space=pltpu.VMEM),
-            untouched(),
-            pl.BlockSpec(memory_space=pltpu.VMEM),
-            untouched(),
-            untouched(),
-            untouched(),
-        ],
-        scratch_shapes=[
-            pltpu.VMEM((4, moves, chunk), BF16),
-            pltpu.VMEM((plan.rows, moves), F32),
-            pltpu.SemaphoreType.DMA((4,)),
-        ],
-        compiler_params=limits(57),
-        cost_estimate=cost(2 * moves * width * 256, 2 * moves * width),
-    )(flat, normed, my_turns, beside, across, slot_row)
+        line_at.reshape(1),
+        (flat, move_table, inverse, turns, beside, across),
+        (shape((line, plan.line_rows, moves), BF16), shape((plan.mine, moves), F32)),
+        [pltpu.VMEM((moves, width), BF16), pltpu.SemaphoreType.DMA((4,))],
+        cost(2 * moves * width * 256, 2 * moves * width),
+        {1: untouched(), 4: untouched(), 5: untouched()},
+        58,
+    )
     queries = lax.all_to_all(queries, "line", split_axis=0, concat_axis=0, tiled=True)
-    diagonal = swap(beside, slab_axes, plan.slab, 2)
     listed = pl.pallas_call(
         functools.partial(read_lists, plan),
         out_shape=shape((plan.share, plan.slots), F32),
@@ -488,6 +499,7 @@
         cost_estimate=cost(10**7, 10**6),
     )(weights)
     listed = jnp.stack([listed, swap(listed, slab_axes, plan.slab, pair)]).astype(jnp.int32)
+    diagonal = swap(beside, slab_axes, plan.slab, 2)
 
     query_rows = plan.mine * HD
     back = plan.peers * lax.axis_size("tensor")

time: 89.7 us -> 92.5 us (1.031)
  waiting for transfers between devices: 13.7 us -> 22.7 us
  local copies, waits for them, and re-layouts: 11 us -> 3.06 us
  Pallas kernels: 31.3 us -> 32.7 us
    pallas_call x3 -> x4, Pallas kernels: 12.6 us -> 23.9 us  [scalar_call(): pl.pallas_call(kernel, out_shape=outs, grid_spec=pltpu.PrefetchScalarGrid...]
    pallas_call x3 -> x1, Pallas kernels: 17.5 us -> 7.52 us  [per_device(): pl.pallas_call(inverse_norms, out_shape=shape((1, moves), F32), grid=(mov...]
    ppermute x4, waiting for transfers between devices: 13 us -> 22 us  [swap(): return lax.ppermute(x, names, [(at, at ^ step) for at in range(size)])]
    unnamed x31 -> x20, local copies, waits for them, and re-layouts: 8.31 us -> 3.06 us
    reshape x1 -> x0, local copies, waits for them, and re-layouts: 1.3 us -> none  [per_device(): norm_gain.reshape(1, width)]
  transfers between devices with their start and end apart: 6 -> 6, of which waited for: 3 -> 4; matrix products, arithmetic and copies ran while one was open for 2% -> 0% of each run, Pallas kernels for 13% -> 11%
where the time goes in v6:
time: 92.5 us; the launch traced here: 91.9 us
  Pallas kernels  32.7 us (35%)
  waiting for transfers between devices  22.7 us (25%)
  starting transfers between devices  17.7 us (19%)
  blocking collectives  15.1 us (16%)
  local copies, waits for them, and re-layouts  3.06 us (3%)
    pallas_call x4, Pallas kernels, scalar_call(): pl.pallas_call(kernel, out_shape=outs, grid_spec=pltpu.PrefetchScalarGrid...  23.9 us
    ppermute x4, waiting for transfers between devices, swap(): return lax.ppermute(x, names, [(at, at ^ step) for at in range(size)])  22 us
    all_to_all x1, blocking collectives, per_device(): lax.all_to_all(parts.reshape(groups * back, plan.share, plan.slots), ('gr...  15.1 us
    pallas_call x1, Pallas kernels, per_device(): pl.pallas_call(inverse_norms, out_shape=shape((1, moves), F32), grid=(mov...  7.52 us
    all_to_all x1, starting transfers between devices, per_device(): lax.all_to_all(packed, ('line', 'pair'), split_axis=0, concat_axis=0, til...  7.27 us
    ppermute x4, starting transfers between devices, swap(): return lax.ppermute(x, names, [(at, at ^ step) for at in range(size)])  5.69 us
    all_to_all x1, starting transfers between devices, per_device(): lax.all_to_all(queries, 'line', split_axis=0, concat_axis=0, tiled=True)  4.79 us
    unnamed x20, local copies, waits for them, and re-layouts  3.06 us
  transfers between devices with their start and end apart: 6, of which 4 were waited for; matrix products, arithmetic and copies ran while one was open for 0% of the time, Pallas kernels for 11%

profile of v6, /device:TPU:0, one launch (start us, length us, event | category | flops | bytes accessed | tf_op | source)
XLA Modules:
  0.0 91.9 jit_solution(2876744918835639424)
XLA Ops:
  0.0 0.6 pad_add_fusion.at_ref
  0.6 4.1 %shard_map.100.after_ref = bf16[8,104,512]{2,1,0:T(8,128)(2,1)} custom-call(s32[2]{0:T(128)} %pad_add_fusion.at_ref, bf16[512,1024]{1,0:T(8,128)(2,1)} %wq_hbm.1, bf16[512,256]{1,0:T(8,128)(2,1)} %wkv_hbm.1, bf16[8,128]{1,0:T(8,128)(2,1)} %bitcast.23, s32[1,512]{1,0:T(1,128)} %bitcast.18, s32[1,512]{1,0:T(1,128)} %bitcast.25, bf16[32,128]{1,0:T(8,128)(2,1)} %bitcast.21), custom_call_target="tpu_custom_call" | custom-call | flops 436207616 | bytes 2097152 | tf_op jit(solution)/shard_map/pallas_call | solution.py:361
  4.7 7.3 %all-to-all-start = ((bf16[8,104,512]{2,1,0:T(8,128)(2,1)}), bf16[8,104,512]{2,1,0:T(8,128)(2,1)S(1)}, u32[]{:S(2)}, u32[]{:S(2)}) async-start(bf16[8,104,512]{2,1,0:T(8,128)(2,1)} %shard_map.100.after_ref), calls=%async_computation | async-start | bytes 1703936 | tf_op jit(solution)/shard_map/all_to_all | solution.py:451
  12.0 2.2 %shard_map.102 = (bf16[9,256,128]{2,1,0:T(8,128)(2,1)}, s32[1,512]{1,0:T(1,128)}) custom-call(s32[1]{0:T(128)} %bitcast.3.at_ref, bf16[8,256,256]{2,1,0:T(8,128)(2,1)} %prefix_hbm.1, bf16[8,128]{1,0:T(8,128)(2,1)} %bitcast.24, s32[1,512]{1,0:T(1,128)} %bitcast.19, bf16[8,104,512]{2,1,0:T(8,128)(2,1)} %shard_map.100.after_ref), custom_call_target="tpu_custom_call" | custom-call | flops 67108864 | bytes 1048576 | tf_op jit(solution)/shard_map/pallas_call | solution.py:361
  14.3 1.6 %collective-permute-start.1 = (bf16[9,256,128]{2,1,0:T(8,128)(2,1)}, bf16[9,256,128]{2,1,0:T(8,128)(2,1)S(1)}, u32[]{:S(2)}, u32[]{:S(2)}) collective-permute-start(bf16[9,256,128]{2,1,0:T(8,128)(2,1)} %get-tuple-element.9.rest_0_), channel_id=1, source_target_pairs={{0,16},{2,18},{16,0},{18,2},{1,17},{3,19},{17,1},{19,3},{4,20},{6,... | collective-permute-start | bytes 1769480 | tf_op jit(solution)/shard_map/ppermute | solution.py:381
  15.8 2.0 %collective-permute-start = (bf16[9,256,128]{2,1,0:T(8,128)(2,1)}, bf16[9,256,128]{2,1,0:T(8,128)(2,1)S(1)}, u32[]{:S(2)}, u32[]{:S(2)}) collective-permute-start(bf16[9,256,128]{2,1,0:T(8,128)(2,1)} %get-tuple-element.9.rest_0_), channel_id=1, source_target_pairs={{0,2},{2,0},{16,18},{18,16},{1,3},{3,1},{17,19},{19,17},{4,6},{6,4... | collective-permute-start | bytes 1769480 | tf_op jit(solution)/shard_map/ppermute | solution.py:381
  17.9 7.5 %shard_map.101.inverse_ref = f32[1,1024]{1,0:T(1,128)} custom-call(bf16[1024,4096]{1,0:T(8,128)(2,1)} %table_hbm.1, bf16[8,104,512]{2,1,0:T(8,128)(2,1)} %shard_map.100.after_ref), custom_call_target="tpu_custom_call" | custom-call | flops 33554432 | bytes 8388608 | tf_op jit(solution)/shard_map/pallas_call | solution.py:472
  25.4 3.9 %collective-permute-done.1.rest_1_.rest_2_ = bf16[9,256,128]{2,1,0:T(8,128)(2,1)S(1)} collective-permute-done((bf16[9,256,128]{2,1,0:T(8,128)(2,1)}, bf16[9,256,128]{2,1,0:T(8,128)(2,1)S(1)}, u32[]{:S(2)}, u32[]{:S(2)}) %collective-permute-start.1) | collective-permute-done | bytes 589856 | tf_op jit(solution)/shard_map/ppermute | solution.py:381
  29.3 7.1 %collective-permute-done.rest_0_.rest_1_ = bf16[9,256,128]{2,1,0:T(8,128)(2,1)S(1)} collective-permute-done((bf16[9,256,128]{2,1,0:T(8,128)(2,1)}, bf16[9,256,128]{2,1,0:T(8,128)(2,1)S(1)}, u32[]{:S(2)}, u32[]{:S(2)}) %collective-permute-start) | collective-permute-done | bytes 589856 | tf_op jit(solution)/shard_map/ppermute | solution.py:381
  36.4 0.8 copy-done.8
  37.2 0.3 copy-done
  37.5 8.8 %shard_map.103 = (bf16[4,72,1024]{2,1,0:T(8,128)(2,1)}, f32[2,1024]{1,0:T(2,128)}) custom-call(s32[1]{0:T(128)} %bitcast.1.at_ref, bf16[8,104,512]{2,1,0:T(8,128)(2,1)} %copy-done, bf16[1024,4096]{1,0:T(8,128)(2,1)} %table_hbm.1, f32[1,1024]{1,0:T(1,128)} %shard_map.101.inverse_ref, f32[4,32,2]{2,1,0:T(8,128)} %constant.19.clone.turn_ref, ...), custom_call_target="tpu_custom_call" | custom-call | flops 2147483648 | bytes 8388608 | tf_op jit(solution)/shard_map/pallas_call | solution.py:361
  46.3 4.8 %all-to-all-start.1 = ((bf16[4,72,1024]{2,1,0:T(8,128)(2,1)}), bf16[4,72,1024]{2,1,0:T(8,128)(2,1)S(1)}, u32[]{:S(2)}, u32[]{:S(2)}) async-start(bf16[4,72,1024]{2,1,0:T(8,128)(2,1)} %get-tuple-element.10), calls=%async_computation.1 | async-start | bytes 1179648 | tf_op jit(solution)/shard_map/all_to_all | solution.py:494
  51.0 1.1 %collective-permute-start.2 = (bf16[9,256,128]{2,1,0:T(8,128)(2,1)}, bf16[9,256,128]{2,1,0:T(8,128)(2,1)S(1)}, u32[]{:S(2)}, u32[]{:S(2)}) collective-permute-start(bf16[9,256,128]{2,1,0:T(8,128)(2,1)} %copy-done.8), channel_id=1, source_target_pairs={{0,16},{2,18},{16,0},{18,2},{1,17},{3,19},{17,1},{19,3},{4,20},{6,... | collective-permute-start | bytes 1769480 | tf_op jit(solution)/shard_map/ppermute | solution.py:381
  52.1 1.2 %copy-done.1 = bf16[8,104,512]{2,1,0:T(8,128)(2,1)S(1)} copy-done((bf16[8,104,512]{2,1,0:T(8,128)(2,1)S(1)}, bf16[8,104,512]{2,1,0:T(8,128)(2,1)}, u32[]{:S(2)}) %copy-start.1) | copy-done | bytes 851992
  53.3 0.2 shard_map.104
  53.5 1.0 %collective-permute-start.3 = (f32[16,128]{1,0:T(8,128)S(1)}, f32[16,128]{1,0:T(8,128)S(1)}, u32[]{:S(2)}, u32[]{:S(2)}) collective-permute-start(f32[16,128]{1,0:T(8,128)S(1)} %shard_map.104), channel_id=1, source_target_pairs={{0,16},{2,18},{16,0},{18,2},{1,17},{3,19},{17,1},{19,3},{4,20},{6,... | collective-permute-start | bytes 24584 | tf_op jit(solution)/shard_map/ppermute | solution.py:381
  54.5 10.9 %collective-permute-done.3 = f32[16,128]{1,0:T(8,128)S(1)} collective-permute-done((f32[16,128]{1,0:T(8,128)S(1)}, f32[16,128]{1,0:T(8,128)S(1)}, u32[]{:S(2)}, u32[]{:S(2)}) %collective-permute-start.3) | collective-permute-done | bytes 8224 | tf_op jit(solution)/shard_map/ppermute | solution.py:381
  65.5 0.7 all-to-all-done.1
  66.2 0.1 copy-done.9
  66.3 0.7 copy-done.5
  67.0 8.8 %shard_map.105 = f32[2,16,16,128]{3,2,1,0:T(8,128)S(1)} custom-call(s32[1]{0:T(128)} %bitcast.at_ref, bf16[288,1024]{1,0:T(8,128)(2,1)S(1)} %bitcast.15, bf16[272,288]{1,0:T(8,128)(2,1)S(1)} %copy-done.6, f32[2,1024]{1,0:T(2,128)S(1)} %copy-done.5, bf16[9,256,128]{2,1,0:T(8,128)(2,1)S(1)} %copy-done.4, bf16[9,256,128]{2,1,0:T(8,128)(2,1)} %copy-done.8, ...), custom_call_target="tpu_custom_call" | custom-call | flops 2281701376 | bytes 4000000 | tf_op jit(solution)/shard_map/pallas_call | solution.py:361
  75.8 15.1 %all_to_all.15 = f32[32,16,128]{2,1,0:T(8,128)S(1)} all-to-all(f32[32,16,128]{2,1,0:T(8,128)S(1)} %bitcast.16), channel_id=1, replica_groups=mesh['groups'=2,'line'=4,'pair'=2,'tensor'=2] {'groups','line','pair','t..., dimensions={0} | all-to-all | bytes 524288 | tf_op jit(solution)/shard_map/all_to_all | solution.py:529
  90.9 1.1 %shard_map.106 = f32[1,512]{1,0:T(1,128)} custom-call(f32[2,4,4,16,128]{4,3,2,1,0:T(8,128)S(1)} %bitcast.14, s32[1,512]{1,0:T(1,128)S(1)} %bitcast.20, s32[1,512]{1,0:T(1,128)S(1)} %copy-done.3), custom_call_target="tpu_custom_call" | custom-call | tf_op jit(solution)/shard_map/pallas_call | solution.py:537
  (18 shorter events, 0.0 us)
Async XLA Ops:
  4.7 31.7 %all-to-all-start = ((bf16[8,104,512]{2,1,0:T(8,128)(2,1)}), bf16[8,104,512]{2,1,0:T(8,128)(2,1)S(1)}, u32[]{:S(2)}, u32[]{:S(2)}) async-start(bf16[8,104,512]{2,1,0:T(8,128)(2,1)} %shard_map.100.after_ref), calls=%async_computation | async-start | bytes 1703936 | tf_op jit(solution)/shard_map/all_to_all | solution.py:451
  14.3 15.1 %collective-permute-start.1 = (bf16[9,256,128]{2,1,0:T(8,128)(2,1)}, bf16[9,256,128]{2,1,0:T(8,128)(2,1)S(1)}, u32[]{:S(2)}, u32[]{:S(2)}) collective-permute-start(bf16[9,256,128]{2,1,0:T(8,128)(2,1)} %get-tuple-element.9.rest_0_), channel_id=1, source_target_pairs={{0,16},{2,18},{16,0},{18,2},{1,17},{3,19},{17,1},{19,3},{4,20},{6,... | collective-permute-start | bytes 1769480 | tf_op jit(solution)/shard_map/ppermute | solution.py:381
  15.8 20.6 %collective-permute-start = (bf16[9,256,128]{2,1,0:T(8,128)(2,1)}, bf16[9,256,128]{2,1,0:T(8,128)(2,1)S(1)}, u32[]{:S(2)}, u32[]{:S(2)}) collective-permute-start(bf16[9,256,128]{2,1,0:T(8,128)(2,1)} %get-tuple-element.9.rest_0_), channel_id=1, source_target_pairs={{0,2},{2,0},{16,18},{18,16},{1,3},{3,1},{17,19},{19,17},{4,6},{6,4... | collective-permute-start | bytes 1769480 | tf_op jit(solution)/shard_map/ppermute | solution.py:381
  25.4 40.9 %copy-start.4 = (bf16[9,256,128]{2,1,0:T(8,128)(2,1)S(1)}, bf16[9,256,128]{2,1,0:T(8,128)(2,1)}, u32[]{:S(2)}) copy-start(bf16[9,256,128]{2,1,0:T(8,128)(2,1)} %get-tuple-element.9.rest_0_) | copy-start | bytes 1769476
  25.4 40.9 %copy-start.6 = (bf16[272,288]{1,0:T(8,128)(2,1)S(1)}, bf16[272,288]{1,0:T(8,128)(2,1)}, u32[]{:S(2)}) copy-start(bf16[272,288]{1,0:T(8,128)(2,1)} %constant.20.clone.order_ref) | copy-start | bytes 470020
  29.3 7.1 %copy-start.7 = (bf16[9,256,128]{2,1,0:T(8,128)(2,1)}, bf16[9,256,128]{2,1,0:T(8,128)(2,1)S(1)}, u32[]{:S(2)}) copy-start(bf16[9,256,128]{2,1,0:T(8,128)(2,1)S(1)} %collective-permute-done.1.rest_1_.rest_2_) | copy-start | bytes 1769476
  36.4 0.8 copy-start.8
  36.4 1.1 %copy-start = (bf16[8,104,512]{2,1,0:T(8,128)(2,1)}, bf16[8,104,512]{2,1,0:T(8,128)(2,1)S(1)}, u32[]{:S(2)}) copy-start(bf16[8,104,512]{2,1,0:T(8,128)(2,1)S(1)} %all-to-all-done.w_ref) | copy-start | bytes 2555908
  37.5 53.4 %copy-start.2 = (s32[512,1]{0,1:T(1,128)S(1)}, s32[512,1]{0,1:T(1,128)}, u32[]{:S(2)}) copy-start(s32[512,1]{0,1:T(1,128)} %param.12) | copy-start | bytes 6148
  37.5 53.4 %copy-start.3 = (s32[1,512]{1,0:T(1,128)S(1)}, s32[1,512]{1,0:T(1,128)}, u32[]{:S(2)}) copy-start(s32[1,512]{1,0:T(1,128)} %get-tuple-element.12.slot_ref) | copy-start | bytes 6148
  46.3 19.9 %all-to-all-start.1 = ((bf16[4,72,1024]{2,1,0:T(8,128)(2,1)}), bf16[4,72,1024]{2,1,0:T(8,128)(2,1)S(1)}, u32[]{:S(2)}, u32[]{:S(2)}) async-start(bf16[4,72,1024]{2,1,0:T(8,128)(2,1)} %get-tuple-element.10), calls=%async_computation.1 | async-start | bytes 1179648 | tf_op jit(solution)/shard_map/all_to_all | solution.py:494
  51.0 14.4 %collective-permute-start.2 = (bf16[9,256,128]{2,1,0:T(8,128)(2,1)}, bf16[9,256,128]{2,1,0:T(8,128)(2,1)S(1)}, u32[]{:S(2)}, u32[]{:S(2)}) collective-permute-start(bf16[9,256,128]{2,1,0:T(8,128)(2,1)} %copy-done.8), channel_id=1, source_target_pairs={{0,16},{2,18},{16,0},{18,2},{1,17},{3,19},{17,1},{19,3},{4,20},{6,... | collective-permute-start | bytes 1769480 | tf_op jit(solution)/shard_map/ppermute | solution.py:381
  52.1 1.2 %copy-start.1 = (bf16[8,104,512]{2,1,0:T(8,128)(2,1)S(1)}, bf16[8,104,512]{2,1,0:T(8,128)(2,1)}, u32[]{:S(2)}) copy-start(bf16[8,104,512]{2,1,0:T(8,128)(2,1)} %copy-done) | copy-start | bytes 2555908
  53.5 12.0 %collective-permute-start.3 = (f32[16,128]{1,0:T(8,128)S(1)}, f32[16,128]{1,0:T(8,128)S(1)}, u32[]{:S(2)}, u32[]{:S(2)}) collective-permute-start(f32[16,128]{1,0:T(8,128)S(1)} %shard_map.104), channel_id=1, source_target_pairs={{0,16},{2,18},{16,0},{18,2},{1,17},{3,19},{17,1},{19,3},{4,20},{6,... | collective-permute-start | bytes 24584 | tf_op jit(solution)/shard_map/ppermute | solution.py:381
  65.5 0.8 copy-start.9
  66.3 0.7 copy-start.5

commit v7 on v6

--- a/solution.py
+++ b/solution.py
@@ -52,22 +52,21 @@
         self.slots = self.peers * capacity
 
 
-def pack_weights(plan, at_ref, wq_hbm, wkv_hbm, ws_hbm, board_hbm, ids_hbm, gain_hbm, out_ref, *scratch):
-    wq, wkv, ws_ref, board_ref, ids_ref, gain_ref, pick, sems = scratch
-    group, peer_at = at_ref[0], at_ref[1]
+def pack_weights(plan, at_ref, wq_hbm, wkv_hbm, ws_hbm, board_hbm, ids_hbm, out_ref, *scratch):
+    wq, wkv, ws_ref, board_ref, ids_ref, pick, sems = scratch
+    group = at_ref[0]
     rows, half_cols = plan.rows, wq.shape[1]
     columns_here = pl.ds(pl.multiple_of(group * half_cols, HD), half_cols)
     copies = (
         pltpu.make_async_copy(ws_hbm, ws_ref, sems.at[0]),
         pltpu.make_async_copy(board_hbm, board_ref, sems.at[1]),
         pltpu.make_async_copy(ids_hbm, ids_ref, sems.at[2]),
-        pltpu.make_async_copy(gain_hbm, gain_ref, sems.at[3]),
-        pltpu.make_async_copy(wq_hbm.at[:, columns_here], wq, sems.at[4]),
-        pltpu.make_async_copy(wkv_hbm, wkv, sems.at[5]),
+        pltpu.make_async_copy(wq_hbm.at[:, columns_here], wq, sems.at[3]),
+        pltpu.make_async_copy(wkv_hbm, wkv, sems.at[4]),
     )
     for copy in copies:
         copy.start()
-    for copy in copies[:4]:
+    for copy in copies[:3]:
         copy.wait()
     r = lax.broadcasted_iota(jnp.int32, (rows, 1), 0)
     part = r // (plan.mine * plan.pairs)
@@ -119,58 +118,63 @@
         found = matmul(parts, jnp.where(key == place, 1.0, 0.0).astype(BF16))
         lists.append(jnp.where(lane_row < span, found[0:1], found[1:2]))
 
-    count, depth = wq.shape
-    gain = gain_ref[...].astype(F32)
-    gain_row = lax.broadcasted_iota(jnp.int32, gain.shape, 0)
-    first = peer_at * (count // gain.shape[1]) if gain.shape[0] > 1 else 0
-    pieces = max(1, count // gain.shape[1])
-    gain = [jnp.sum(jnp.where(gain_row == first + p, gain, 0.0), axis=0, keepdims=True) for p in range(pieces)]
-    gain = jnp.concatenate(gain, axis=1)
-
-    for copy in copies[4:]:
+    for copy in copies[3:]:
         copy.wait()
     left = pick[...].astype(BF16)
     total = matmul(left[:, :half_cols], wq[...], NT) + matmul(left[:, half_cols:], wkv[...], NT)
     for peer in range(plan.peers):
-        mine = total[peer * rows : (peer + 1) * rows] * gain
+        mine = total[peer * rows : (peer + 1) * rows]
         out_ref[peer] = jnp.where(r == plan.list_at, lists[peer // plan.pair], mine).astype(BF16)
 
 
-def inverse_norms(table_ref, after_ref, out_ref):
-    raw = table_ref[...].astype(F32)
-    count = raw.shape[0]
-    inverse = lax.rsqrt(jnp.mean(raw * raw, axis=-1, keepdims=True) + EPS)
-    out_ref[...] = jnp.broadcast_to(inverse, (count, count)).T[0:1]
-
-
-def project(plan, at_ref, w_ref, table_hbm, inverse_ref, turn_ref, *rest):
-    q_ref, vo_ref, table, sems = rest[-4:]
-    moves, width = table_hbm.shape
-    block = moves // sems.shape[0]
+def normalize(table_ref, gain_ref, after_ref, out_ref, gain):
+    @pl.when(pl.program_id(0) == 0)
+    def _():
+        rows = gain_ref[...].astype(F32)
+        gain[...] = jnp.concatenate([rows[r : r + 1] for r in range(rows.shape[0])], axis=1)
+
+    half = table_ref.shape[0] // 2
+    for at in (slice(0, half), slice(half, 2 * half)):
+        raw = table_ref[at].astype(F32)
+        inverse = lax.rsqrt(jnp.mean(raw * raw, axis=-1, keepdims=True) + EPS)
+        out_ref[at] = (raw * inverse * gain[...]).astype(BF16)
+
+
+def project(plan, at_ref, w_ref, normed_hbm, turn_ref, *rest):
+    q_ref, vo_ref, buffers, sems = rest[-4:]
+    moves, width = normed_hbm.shape
+    held, block, _ = buffers.shape
+    steps = moves // block
 
     def copy(step):
-        at = pl.ds(step * block, block)
-        return pltpu.make_async_copy(table_hbm.at[at], table.at[at], sems.at[step])
-
-    for step in range(sems.shape[0]):
+        at = step % held
+        return pltpu.make_async_copy(normed_hbm.at[pl.ds(step * block, block)], buffers.at[at], sems.at[at])
+
+    for step in range(min(held, steps)):
         copy(step).start()
 
     half, k_half = plan.q_rows // 2, plan.k_rows // 2
     turns = turn_ref[at_ref[0]]
     cosine, sine = turns[:, 0:1], turns[:, 1:2]
     cos_k, sin_k = cosine[:k_half], sine[:k_half]
-    for step in range(sems.shape[0]):
+    for step in range(steps):
         copy(step).wait()
         at = slice(step * block, (step + 1) * block)
+        held_at = step % held
         if len(w_ref.shape) == 3:
             depth = w_ref.shape[2]
             total = None
             for s in range(w_ref.shape[0]):
-                term = matmul(w_ref[s], table[at, s * depth : (s + 1) * depth], NT)
+                term = matmul(buffers[held_at, :, s * depth : (s + 1) * depth], w_ref[s], NT)
                 total = term if total is None else total + term
         else:
-            total = matmul(w_ref[...], table[at, :], NT)
-        total = total * inverse_ref[:, at]
+            total = matmul(buffers[held_at], w_ref[...], NT)
+        if step + held < steps:
+            copy(step + held).start()
+        pad = -total.shape[1] % HD
+        if pad:
+            total = jnp.concatenate([total, jnp.zeros((block, pad), F32)], axis=1)
+        total = total.T
         first, second = total[:half], total[half : 2 * half]
         f_first = (first * cosine - second * sine).astype(BF16).astype(F32)
         f_second = (second * cosine + first * sine).astype(BF16).astype(F32)
@@ -193,6 +197,10 @@
         vo_ref[:, at] = total[plan.fold_at : plan.list_at]
 
 
+def tie(x_ref, beside_ref, across_ref, out_ref):
+    pass
+
+
 def pack_prefix(plan, at_ref, prefix_hbm, ws_hbm, board_hbm, after_ref, out_ref, slot_ref, *scratch):
     values, ws_ref, board_ref, sems = scratch
     boards = values.shape[0]
@@ -319,21 +327,13 @@
 
     lax.fori_loop(0, -(-boards // 2), step, 0)
     for g in range(plan.groups):
-        both = jnp.concatenate([scores[g * plan.pair + p] for p in range(plan.pair)], axis=0)
-        for copy in range(out_ref.shape[1]):
-            out_ref[g, copy] = both
+        out_ref[g] = jnp.concatenate([scores[g * plan.pair + p] for p in range(plan.pair)], axis=0)
 
 
 def finish(plan, parts_ref, board_ref, slot_ref, out_ref):
-    line = parts_ref.shape[1]
     columns = []
-    for at in range(line):
-        total = None
-        for g in range(parts_ref.shape[0]):
-            for p in range(parts_ref.shape[2]):
-                term = parts_ref[g, at, p]
-                total = term if total is None else total + term
-        columns.append(total)
+    for at in range(plan.line):
+        columns.append(sum(parts_ref[at * plan.pair + p] for p in range(plan.pair)))
     scores = jnp.concatenate(columns, axis=0)
     live = scores > 0.5 * DEAD
     peak = jnp.max(scores, axis=1, keepdims=True)
@@ -423,16 +423,11 @@
     slab_axes = ("groups", "pair")
     board_row = move_board.reshape(1, row_count)
 
-    if depth % HD:
-        gain = lax.dynamic_slice_in_dim(norm_gain, (line_at * pair + pair_at) * depth, depth).reshape(1, depth)
-    else:
-        gain = norm_gain.reshape(width // HD, HD)
-
     half_cols = w_query.shape[1] // groups
     packed = scalar_call(
         functools.partial(pack_weights, plan),
-        jnp.stack([group_at, line_at * pair + pair_at]),
-        (w_query, w_keyval, ws, board_row, move_ids.reshape(1, row_count), gain),
+        group_at.reshape(1),
+        (w_query, w_keyval, ws, board_row, move_ids.reshape(1, row_count)),
         shape((plan.peers, plan.rows, depth), BF16),
         [
             pltpu.VMEM((depth, half_cols), BF16),
@@ -440,12 +435,11 @@
             pltpu.VMEM((heads, HD), BF16),
             pltpu.VMEM((1, row_count), jnp.int32),
             pltpu.VMEM((1, row_count), jnp.int32),
-            pltpu.VMEM(gain.shape, BF16),
             pltpu.VMEM((plan.peers * plan.rows, half_cols + 2 * HD), F32),
-            pltpu.SemaphoreType.DMA((6,)),
+            pltpu.SemaphoreType.DMA((5,)),
         ],
         cost(2 * plan.peers * plan.rows * half_cols * depth, 4 * w_query.size),
-        {at: untouched() for at in range(6)},
+        {at: untouched() for at in range(5)},
         62,
     )
     weights = lax.all_to_all(packed, ("line", "pair"), split_axis=0, concat_axis=0, tiled=True)
@@ -468,29 +462,42 @@
     beside = swap(payload, slab_axes, plan.slab, 1)
     across = swap(payload, slab_axes, plan.slab, 2)
 
-    block = min(moves, 128)
-    inverse = pl.pallas_call(
-        inverse_norms,
-        out_shape=shape((1, moves), F32),
+    block = min(moves, 256)
+    normed = pl.pallas_call(
+        normalize,
+        out_shape=shape((moves, width), BF16),
         grid=(moves // block,),
-        in_specs=[pl.BlockSpec((block, width), lambda i: (i, 0)), untouched()],
-        out_specs=pl.BlockSpec((1, block), lambda i: (0, i)),
+        in_specs=[
+            pl.BlockSpec((block, width), lambda i: (i, 0)),
+            pl.BlockSpec((width // HD, HD), lambda i: (0, 0)),
+            untouched(),
+        ],
+        out_specs=pl.BlockSpec((block, width), lambda i: (i, 0)),
+        scratch_shapes=[pltpu.VMEM((1, width), F32)],
         compiler_params=limits(58),
-        cost_estimate=cost(8 * moves * width, 2 * moves * width),
-    )(move_table, packed)
+        cost_estimate=cost(moves * width, moves * width // 4),
+    )(move_table, norm_gain.reshape(width // HD, HD), packed)
     turns = turn_table(prefix_len).reshape(line, 1, plan.pairs, 2)
     turns = jnp.asarray(np.tile(turns, (1, plan.mine, 1, 1)).reshape(line, plan.mine * plan.pairs, 2))
     flat = weights.transpose(1, 0, 2).reshape(plan.rows, width) if depth % HD else weights
     queries, own_values = scalar_call(
         functools.partial(project, plan),
         line_at.reshape(1),
-        (flat, move_table, inverse, turns, beside, across),
+        (flat, normed, turns),
         (shape((line, plan.line_rows, moves), BF16), shape((plan.mine, moves), F32)),
-        [pltpu.VMEM((moves, width), BF16), pltpu.SemaphoreType.DMA((4,))],
-        cost(2 * moves * width * 256, 2 * moves * width),
-        {1: untouched(), 4: untouched(), 5: untouched()},
+        [pltpu.VMEM((2, block, width), BF16), pltpu.SemaphoreType.DMA((2,))],
+        cost(moves * width, moves * width // 4),
+        {1: untouched()},
         58,
     )
+    queries = pl.pallas_call(
+        tie,
+        out_shape=shape(queries.shape, BF16),
+        in_specs=[untouched()] * 3,
+        out_specs=untouched(),
+        input_output_aliases={0: 0},
+        cost_estimate=cost(0, 0),
+    )(queries, beside, across)
     queries = lax.all_to_all(queries, "line", split_axis=0, concat_axis=0, tiled=True)
     listed = pl.pallas_call(
         functools.partial(read_lists, plan),
@@ -502,7 +509,6 @@
     diagonal = swap(beside, slab_axes, plan.slab, 2)
 
     query_rows = plan.mine * HD
-    back = plan.peers * lax.axis_size("tensor")
     parts = scalar_call(
         functools.partial(attend, plan),
         slab_at.reshape(1),
@@ -516,7 +522,7 @@
             diagonal,
             listed,
         ),
-        shape((groups, back, plan.share, plan.slots), F32),
+        shape((groups, plan.share, plan.slots), F32),
         [
             pltpu.VMEM((query_rows + 16, moves), BF16),
             pltpu.VMEM((16, moves), F32),
@@ -526,14 +532,10 @@
         ],
         cost(2 * 272 * moves * 4096, 4 * 10**6),
     )
-    parts = lax.all_to_all(
-        parts.reshape(groups * back, plan.share, plan.slots),
-        ("groups", "line", "pair", "tensor"),
-        split_axis=0,
-        concat_axis=0,
-        tiled=True,
-    )
-    parts = parts.reshape(groups, line, back // line, plan.share, plan.slots)
+    parts = lax.psum(parts, ("groups", "tensor"))
+    parts = lax.dynamic_index_in_dim(parts, group_at, axis=0)
+    parts = jnp.broadcast_to(parts, (plan.peers, plan.share, plan.slots))
+    parts = lax.all_to_all(parts, ("line", "pair"), split_axis=0, concat_axis=0, tiled=True)
     logprob = pl.pallas_call(
         functools.partial(finish, plan), out_shape=shape((1, row_count), F32), compiler_params=limits(VMEM_MIB)
     )(parts, board_row, slot_row)

time: 92.5 us -> 96.8 us (1.046)
  blocking collectives: 15.1 us -> 22.9 us
  waiting for transfers between devices: 22.7 us -> 17.7 us
  local copies, waits for them, and re-layouts: 3.06 us -> 5.21 us
  starting transfers between devices: 17.7 us -> 16.5 us
  Pallas kernels: 32.7 us -> 33.8 us
    ppermute x4, waiting for transfers between devices: 22 us -> 10.6 us  [swap(): return lax.ppermute(x, names, [(at, at ^ step) for at in range(size)])]
    psum x0 -> x1, blocking collectives: none -> 10.1 us  [per_device(): parts = lax.psum(parts, ('groups', 'tensor'))]
    all_to_all x1, waiting for transfers between devices: 0.01 us -> 6.42 us  [per_device(): lax.all_to_all(packed, ('line', 'pair'), split_axis=0, concat_axis=0, til...]
    all_to_all x1, blocking collectives: 15.1 us -> 12.8 us  [per_device(): lax.all_to_all(parts, ('line', 'pair'), split_axis=0, concat_axis=0, tile...]
    unnamed x20 -> x22, local copies, waits for them, and re-layouts: 3.06 us -> 5.19 us
    pallas_call x1 -> x2, Pallas kernels: 7.52 us -> 9.38 us  [the longest x1 9.38 us: per_device(): pl.pallas_call(normalize, out_shape=shape((moves, width), BF16), grid=(mo...]
    all_to_all x1, starting transfers between devices: 4.79 us -> 3.48 us  [per_device(): lax.all_to_all(queries, 'line', split_axis=0, concat_axis=0, tiled=True)]
  transfers between devices with their start and end apart: 6 -> 6, of which waited for: 4 -> 3; matrix products, arithmetic and copies ran while one was open for 0% -> 0% of each run, Pallas kernels for 11% -> 21%
where the time goes in v7:
time: 96.8 us; the launch traced here: 96.2 us
  Pallas kernels  33.8 us (35%)
  blocking collectives  22.9 us (24%)
  waiting for transfers between devices  17.7 us (18%)
  starting transfers between devices  16.5 us (17%)
  local copies, waits for them, and re-layouts  5.21 us (5%)
    pallas_call x4, Pallas kernels, scalar_call(): pl.pallas_call(kernel, out_shape=outs, grid_spec=pltpu.PrefetchScalarGrid...  23.2 us
    all_to_all x1, blocking collectives, per_device(): lax.all_to_all(parts, ('line', 'pair'), split_axis=0, concat_axis=0, tile...  12.8 us
    ppermute x4, waiting for transfers between devices, swap(): return lax.ppermute(x, names, [(at, at ^ step) for at in range(size)])  10.6 us
    psum x1, blocking collectives, per_device(): parts = lax.psum(parts, ('groups', 'tensor'))  10.1 us
    pallas_call x1, Pallas kernels, per_device(): pl.pallas_call(normalize, out_shape=shape((moves, width), BF16), grid=(mo...  9.38 us
    all_to_all x1, starting transfers between devices, per_device(): lax.all_to_all(packed, ('line', 'pair'), split_axis=0, concat_axis=0, til...  7.27 us
    all_to_all x1, waiting for transfers between devices, per_device(): lax.all_to_all(packed, ('line', 'pair'), split_axis=0, concat_axis=0, til...  6.42 us
    ppermute x4, starting transfers between devices, swap(): return lax.ppermute(x, names, [(at, at ^ step) for at in range(size)])  5.75 us
  transfers between devices with their start and end apart: 6, of which 3 were waited for; matrix products, arithmetic and copies ran while one was open for 0% of the time, Pallas kernels for 21%

profile of v7, /device:TPU:0, one launch (start us, length us, event | category | flops | bytes accessed | tf_op | source)
XLA Modules:
  0.0 96.2 jit_solution(17282375917430860667)
XLA Ops:
  0.0 3.5 %shard_map.100.after_ref = bf16[8,104,512]{2,1,0:T(8,128)(2,1)} custom-call(s32[1]{0:T(128)} %bitcast.2.at_ref, bf16[512,1024]{1,0:T(8,128)(2,1)} %wq_hbm.1, bf16[512,256]{1,0:T(8,128)(2,1)} %wkv_hbm.1, bf16[8,128]{1,0:T(8,128)(2,1)} %bitcast.21, s32[1,512]{1,0:T(1,128)} %bitcast.16, s32[1,512]{1,0:T(1,128)} %bitcast.23), custom_call_target="tpu_custom_call" | custom-call | flops 436207616 | bytes 2097152 | tf_op jit(solution)/shard_map/pallas_call | solution.py:361
  3.5 7.3 %all-to-all-start = ((bf16[8,104,512]{2,1,0:T(8,128)(2,1)}), bf16[8,104,512]{2,1,0:T(8,128)(2,1)S(1)}, u32[]{:S(2)}, u32[]{:S(2)}) async-start(bf16[8,104,512]{2,1,0:T(8,128)(2,1)} %shard_map.100.after_ref), calls=%async_computation | async-start | bytes 1703936 | tf_op jit(solution)/shard_map/all_to_all | solution.py:445
  10.8 2.2 %shard_map.103 = (bf16[9,256,128]{2,1,0:T(8,128)(2,1)}, s32[1,512]{1,0:T(1,128)}) custom-call(s32[1]{0:T(128)} %bitcast.7.at_ref, bf16[8,256,256]{2,1,0:T(8,128)(2,1)} %prefix_hbm.1, bf16[8,128]{1,0:T(8,128)(2,1)} %bitcast.22, s32[1,512]{1,0:T(1,128)} %bitcast.17, bf16[8,104,512]{2,1,0:T(8,128)(2,1)} %shard_map.100.after_ref), custom_call_target="tpu_custom_call" | custom-call | flops 67108864 | bytes 1048576 | tf_op jit(solution)/shard_map/pallas_call | solution.py:361
  13.0 2.1 %collective-permute-start = (bf16[9,256,128]{2,1,0:T(8,128)(2,1)}, bf16[9,256,128]{2,1,0:T(8,128)(2,1)S(1)}, u32[]{:S(2)}, u32[]{:S(2)}) collective-permute-start(bf16[9,256,128]{2,1,0:T(8,128)(2,1)} %get-tuple-element.10.rest_0_), channel_id=1, source_target_pairs={{0,2},{2,0},{16,18},{18,16},{1,3},{3,1},{17,19},{19,17},{4,6},{6,4... | collective-permute-start | bytes 1769480 | tf_op jit(solution)/shard_map/ppermute | solution.py:381
  15.1 1.5 %collective-permute-start.1 = (bf16[9,256,128]{2,1,0:T(8,128)(2,1)}, bf16[9,256,128]{2,1,0:T(8,128)(2,1)S(1)}, u32[]{:S(2)}, u32[]{:S(2)}) collective-permute-start(bf16[9,256,128]{2,1,0:T(8,128)(2,1)} %get-tuple-element.10.rest_0_), channel_id=1, source_target_pairs={{0,16},{2,18},{16,0},{18,2},{1,17},{3,19},{17,1},{19,3},{4,20},{6,... | collective-permute-start | bytes 1769480 | tf_op jit(solution)/shard_map/ppermute | solution.py:381
  16.6 9.4 %shard_map.101.normed_hbm = bf16[1024,4096]{1,0:T(8,128)(2,1)} custom-call(bf16[1024,4096]{1,0:T(8,128)(2,1)} %table_ref.1, bf16[32,128]{1,0:T(8,128)(2,1)} %bitcast.19, bf16[8,104,512]{2,1,0:T(8,128)(2,1)} %shard_map.100.after_ref), custom_call_target="tpu_custom_call" | custom-call | flops 4194304 | bytes 1048576 | tf_op jit(solution)/shard_map/pallas_call | solution.py:466
  26.0 6.4 %all-to-all-done.w_ref = bf16[8,104,512]{2,1,0:T(8,128)(2,1)S(1)} async-done(((bf16[8,104,512]{2,1,0:T(8,128)(2,1)}), bf16[8,104,512]{2,1,0:T(8,128)(2,1)S(1)}, u32[]{:S(2)}, u32[]{:S(2)}) %all-to-all-start) | async-done | bytes 852000 | tf_op jit(solution)/shard_map/all_to_all | solution.py:445
  32.4 1.0 %copy-done = bf16[8,104,512]{2,1,0:T(8,128)(2,1)} copy-done((bf16[8,104,512]{2,1,0:T(8,128)(2,1)}, bf16[8,104,512]{2,1,0:T(8,128)(2,1)S(1)}, u32[]{:S(2)}) %copy-start) | copy-done | bytes 851992
  33.4 8.9 %shard_map.102 = (bf16[4,72,1024]{2,1,0:T(8,128)(2,1)}, f32[2,1024]{1,0:T(2,128)}) custom-call(s32[1]{0:T(128)} %bitcast.1.at_ref, bf16[8,104,512]{2,1,0:T(8,128)(2,1)} %copy-done, bf16[1024,4096]{1,0:T(8,128)(2,1)} %shard_map.101.normed_hbm, f32[4,32,2]{2,1,0:T(8,128)} %constant.24.clone.turn_ref), custom_call_target="tpu_custom_call" | custom-call | flops 4194304 | bytes 1048576 | tf_op jit(solution)/shard_map/pallas_call | solution.py:361
  42.4 0.8 copy-done.2
  43.2 0.2 copy-done.9
  43.4 3.5 %all-to-all-start.1 = ((bf16[4,72,1024]{2,1,0:T(8,128)(2,1)}), bf16[4,72,1024]{2,1,0:T(8,128)(2,1)S(1)}, u32[]{:S(2)}, u32[]{:S(2)}) async-start(bf16[4,72,1024]{2,1,0:T(8,128)(2,1)} %shard_map.104), calls=%async_computation.1 | async-start | bytes 1179648 | tf_op jit(solution)/shard_map/all_to_all | solution.py:501
  46.9 1.6 %collective-permute-start.2 = (bf16[9,256,128]{2,1,0:T(8,128)(2,1)}, bf16[9,256,128]{2,1,0:T(8,128)(2,1)S(1)}, u32[]{:S(2)}, u32[]{:S(2)}) collective-permute-start(bf16[9,256,128]{2,1,0:T(8,128)(2,1)} %copy-done.2), channel_id=1, source_target_pairs={{0,16},{2,18},{16,0},{18,2},{1,17},{3,19},{17,1},{19,3},{4,20},{6,... | collective-permute-start | bytes 1769480 | tf_op jit(solution)/shard_map/ppermute | solution.py:381
  48.4 1.2 %copy-done.1 = bf16[8,104,512]{2,1,0:T(8,128)(2,1)S(1)} copy-done((bf16[8,104,512]{2,1,0:T(8,128)(2,1)S(1)}, bf16[8,104,512]{2,1,0:T(8,128)(2,1)}, u32[]{:S(2)}) %copy-start.1) | copy-done | bytes 851992
  49.8 0.6 collective-permute-start.3
  50.4 10.6 %collective-permute-done.3 = f32[16,128]{1,0:T(8,128)S(1)} collective-permute-done((f32[16,128]{1,0:T(8,128)S(1)}, f32[16,128]{1,0:T(8,128)S(1)}, u32[]{:S(2)}, u32[]{:S(2)}) %collective-permute-start.3) | collective-permute-done | bytes 8224 | tf_op jit(solution)/shard_map/ppermute | solution.py:381
  61.0 0.6 all-to-all-done.1
  61.6 0.2 copy-done.10
  61.9 1.1 %copy-done.3 = bf16[9,256,128]{2,1,0:T(8,128)(2,1)S(1)} copy-done((bf16[9,256,128]{2,1,0:T(8,128)(2,1)S(1)}, bf16[9,256,128]{2,1,0:T(8,128)(2,1)}, u32[]{:S(2)}) %copy-start.3) | copy-done | bytes 589848
  63.0 0.7 copy-done.7
  63.6 8.6 %shard_map.106 = f32[2,16,128]{2,1,0:T(8,128)S(1)} custom-call(s32[1]{0:T(128)} %bitcast.at_ref, bf16[288,1024]{1,0:T(8,128)(2,1)S(1)} %bitcast.14, bf16[272,288]{1,0:T(8,128)(2,1)S(1)} %copy-done.8, f32[2,1024]{1,0:T(2,128)S(1)} %copy-done.7, bf16[9,256,128]{2,1,0:T(8,128)(2,1)S(1)} %copy-done.6, bf16[9,256,128]{2,1,0:T(8,128)(2,1)S(1)} %copy-done.3, ...), custom_call_target="tpu_custom_call" | custom-call | flops 2281701376 | bytes 4000000 | tf_op jit(solution)/shard_map/pallas_call | solution.py:361
  72.2 10.1 %psum.7 = f32[2,16,128]{2,1,0:T(8,128)S(1)} all-reduce(f32[2,16,128]{2,1,0:T(8,128)S(1)} %shard_map.106), channel_id=1, replica_groups=mesh['groups'=2,'line'=4,'pair'=2,'tensor'=2] {'groups','tensor'}, use_global_device_ids=true, to_apply=%region_0.0 | all-reduce | flops 4096 | bytes 32768 | tf_op jit(solution)/shard_map/psum | solution.py:535
  82.4 12.8 %all_to_all.15.parts_ref = f32[8,16,128]{2,1,0:T(8,128)S(1)} all-to-all(f32[8,16,128]{2,1,0:T(8,128)S(1)} %broadcast_in_dim.8), channel_id=1, replica_groups=mesh['groups'=2,'line'=4,'pair'=2,'tensor'=2] {'line','pair'}, dimensions={0} | all-to-all | bytes 131072 | tf_op jit(solution)/shard_map/all_to_all | solution.py:538
  95.1 1.1 %shard_map.107 = f32[1,512]{1,0:T(1,128)} custom-call(f32[8,16,128]{2,1,0:T(8,128)S(1)} %all_to_all.15.parts_ref, s32[1,512]{1,0:T(1,128)S(1)} %bitcast.18, s32[1,512]{1,0:T(1,128)S(1)} %copy-done.5), custom_call_target="tpu_custom_call" | custom-call | tf_op jit(solution)/shard_map/pallas_call | solution.py:539
  (23 shorter events, 0.3 us)
Async XLA Ops:
  3.5 28.9 %all-to-all-start = ((bf16[8,104,512]{2,1,0:T(8,128)(2,1)}), bf16[8,104,512]{2,1,0:T(8,128)(2,1)S(1)}, u32[]{:S(2)}, u32[]{:S(2)}) async-start(bf16[8,104,512]{2,1,0:T(8,128)(2,1)} %shard_map.100.after_ref), calls=%async_computation | async-start | bytes 1703936 | tf_op jit(solution)/shard_map/all_to_all | solution.py:445
  13.0 29.3 %collective-permute-start = (bf16[9,256,128]{2,1,0:T(8,128)(2,1)}, bf16[9,256,128]{2,1,0:T(8,128)(2,1)S(1)}, u32[]{:S(2)}, u32[]{:S(2)}) collective-permute-start(bf16[9,256,128]{2,1,0:T(8,128)(2,1)} %get-tuple-element.10.rest_0_), channel_id=1, source_target_pairs={{0,2},{2,0},{16,18},{18,16},{1,3},{3,1},{17,19},{19,17},{4,6},{6,4... | collective-permute-start | bytes 1769480 | tf_op jit(solution)/shard_map/ppermute | solution.py:381
  15.1 27.2 %collective-permute-start.1 = (bf16[9,256,128]{2,1,0:T(8,128)(2,1)}, bf16[9,256,128]{2,1,0:T(8,128)(2,1)S(1)}, u32[]{:S(2)}, u32[]{:S(2)}) collective-permute-start(bf16[9,256,128]{2,1,0:T(8,128)(2,1)} %get-tuple-element.10.rest_0_), channel_id=1, source_target_pairs={{0,16},{2,18},{16,0},{18,2},{1,17},{3,19},{17,1},{19,3},{4,20},{6,... | collective-permute-start | bytes 1769480 | tf_op jit(solution)/shard_map/ppermute | solution.py:381
  26.0 35.9 %copy-start.6 = (bf16[9,256,128]{2,1,0:T(8,128)(2,1)S(1)}, bf16[9,256,128]{2,1,0:T(8,128)(2,1)}, u32[]{:S(2)}) copy-start(bf16[9,256,128]{2,1,0:T(8,128)(2,1)} %get-tuple-element.10.rest_0_) | copy-start | bytes 1769476
  26.0 35.9 %copy-start.8 = (bf16[272,288]{1,0:T(8,128)(2,1)S(1)}, bf16[272,288]{1,0:T(8,128)(2,1)}, u32[]{:S(2)}) copy-start(bf16[272,288]{1,0:T(8,128)(2,1)} %constant.25.clone.order_ref) | copy-start | bytes 470020
  32.4 1.0 %copy-start = (bf16[8,104,512]{2,1,0:T(8,128)(2,1)}, bf16[8,104,512]{2,1,0:T(8,128)(2,1)S(1)}, u32[]{:S(2)}) copy-start(bf16[8,104,512]{2,1,0:T(8,128)(2,1)S(1)} %all-to-all-done.w_ref) | copy-start | bytes 2555908
  42.3 52.8 %copy-start.4 = (s32[512,1]{0,1:T(1,128)S(1)}, s32[512,1]{0,1:T(1,128)}, u32[]{:S(2)}) copy-start(s32[512,1]{0,1:T(1,128)} %param.12) | copy-start | bytes 6148
  42.3 52.8 %copy-start.5 = (s32[1,512]{1,0:T(1,128)S(1)}, s32[1,512]{1,0:T(1,128)}, u32[]{:S(2)}) copy-start(s32[1,512]{1,0:T(1,128)} %get-tuple-element.12.slot_ref) | copy-start | bytes 6148
  42.3 0.8 copy-start.2
  42.3 1.0 %copy-start.9 = (bf16[9,256,128]{2,1,0:T(8,128)(2,1)}, bf16[9,256,128]{2,1,0:T(8,128)(2,1)S(1)}, u32[]{:S(2)}) copy-start(bf16[9,256,128]{2,1,0:T(8,128)(2,1)S(1)} %collective-permute-done.1.across_ref.rest_2_) | copy-start | bytes 1769476
  43.4 18.3 %all-to-all-start.1 = ((bf16[4,72,1024]{2,1,0:T(8,128)(2,1)}), bf16[4,72,1024]{2,1,0:T(8,128)(2,1)S(1)}, u32[]{:S(2)}, u32[]{:S(2)}) async-start(bf16[4,72,1024]{2,1,0:T(8,128)(2,1)} %shard_map.104), calls=%async_computation.1 | async-start | bytes 1179648 | tf_op jit(solution)/shard_map/all_to_all | solution.py:501
  46.9 14.2 %collective-permute-start.2 = (bf16[9,256,128]{2,1,0:T(8,128)(2,1)}, bf16[9,256,128]{2,1,0:T(8,128)(2,1)S(1)}, u32[]{:S(2)}, u32[]{:S(2)}) collective-permute-start(bf16[9,256,128]{2,1,0:T(8,128)(2,1)} %copy-done.2), channel_id=1, source_target_pairs={{0,16},{2,18},{16,0},{18,2},{1,17},{3,19},{17,1},{19,3},{4,20},{6,... | collective-permute-start | bytes 1769480 | tf_op jit(solution)/shard_map/ppermute | solution.py:381
  48.4 1.2 %copy-start.1 = (bf16[8,104,512]{2,1,0:T(8,128)(2,1)S(1)}, bf16[8,104,512]{2,1,0:T(8,128)(2,1)}, u32[]{:S(2)}) copy-start(bf16[8,104,512]{2,1,0:T(8,128)(2,1)} %copy-done) | copy-start | bytes 2555908
  49.8 11.2 %collective-permute-start.3 = (f32[16,128]{1,0:T(8,128)S(1)}, f32[16,128]{1,0:T(8,128)S(1)}, u32[]{:S(2)}, u32[]{:S(2)}) collective-permute-start(f32[16,128]{1,0:T(8,128)S(1)} %shard_map.105), channel_id=1, source_target_pairs={{0,16},{2,18},{16,0},{18,2},{1,17},{3,19},{17,1},{19,3},{4,20},{6,... | collective-permute-start | bytes 24584 | tf_op jit(solution)/shard_map/ppermute | solution.py:381
  61.0 0.9 copy-start.10
  61.9 1.1 %copy-start.3 = (bf16[9,256,128]{2,1,0:T(8,128)(2,1)S(1)}, bf16[9,256,128]{2,1,0:T(8,128)(2,1)}, u32[]{:S(2)}) copy-start(bf16[9,256,128]{2,1,0:T(8,128)(2,1)} %copy-done.2) | copy-start | bytes 1769476
  63.0 0.7 copy-start.7

commit v8 on v7

--- a/solution.py
+++ b/solution.py
@@ -127,7 +127,7 @@
         out_ref[peer] = jnp.where(r == plan.list_at, lists[peer // plan.pair], mine).astype(BF16)
 
 
-def normalize(table_ref, gain_ref, after_ref, out_ref, gain):
+def normalize(table_ref, gain_ref, after_ref, late_ref, out_ref, late_out_ref, gain):
     @pl.when(pl.program_id(0) == 0)
     def _():
         rows = gain_ref[...].astype(F32)
@@ -141,36 +141,34 @@
 
 
 def project(plan, at_ref, w_ref, normed_hbm, turn_ref, *rest):
-    q_ref, vo_ref, buffers, sems = rest[-4:]
-    moves, width = normed_hbm.shape
-    held, block, _ = buffers.shape
-    steps = moves // block
-
-    def copy(step):
-        at = step % held
-        return pltpu.make_async_copy(normed_hbm.at[pl.ds(step * block, block)], buffers.at[at], sems.at[at])
-
-    for step in range(min(held, steps)):
-        copy(step).start()
+    q_ref, vo_ref, table, sems = rest[-4:]
+    moves = normed_hbm.shape[0]
+    steps = sems.shape[0]
+    block = moves // steps
+    piece = math.gcd(block, 32)
+
+    def copy(start, rows, step):
+        at = pl.ds(start, rows)
+        return pltpu.make_async_copy(normed_hbm.at[at], table.at[at], sems.at[step])
+
+    for start in range(0, moves, piece):
+        copy(start, piece, start // block).start()
 
     half, k_half = plan.q_rows // 2, plan.k_rows // 2
     turns = turn_ref[at_ref[0]]
     cosine, sine = turns[:, 0:1], turns[:, 1:2]
     cos_k, sin_k = cosine[:k_half], sine[:k_half]
     for step in range(steps):
-        copy(step).wait()
+        copy(step * block, block, step).wait()
         at = slice(step * block, (step + 1) * block)
-        held_at = step % held
         if len(w_ref.shape) == 3:
             depth = w_ref.shape[2]
             total = None
             for s in range(w_ref.shape[0]):
-                term = matmul(buffers[held_at, :, s * depth : (s + 1) * depth], w_ref[s], NT)
+                term = matmul(table[at, s * depth : (s + 1) * depth], w_ref[s], NT)
                 total = term if total is None else total + term
         else:
-            total = matmul(buffers[held_at], w_ref[...], NT)
-        if step + held < steps:
-            copy(step + held).start()
+            total = matmul(table[at, :], w_ref[...], NT)
         pad = -total.shape[1] % HD
         if pad:
             total = jnp.concatenate([total, jnp.zeros((block, pad), F32)], axis=1)
@@ -197,11 +195,19 @@
         vo_ref[:, at] = total[plan.fold_at : plan.list_at]
 
 
-def tie(x_ref, beside_ref, across_ref, out_ref):
-    pass
-
-
-def pack_prefix(plan, at_ref, prefix_hbm, ws_hbm, board_hbm, after_ref, out_ref, slot_ref, *scratch):
+def tied(x, *others):
+    return pl.pallas_call(
+        lambda *refs: None,
+        out_shape=shape(x.shape, x.dtype),
+        in_specs=[untouched()] * (1 + len(others)),
+        out_specs=untouched(),
+        input_output_aliases={0: 0},
+        compiler_params=limits(62),
+        cost_estimate=cost(0, 0),
+    )(x, *others)
+
+
+def pack_prefix(plan, at_ref, prefix_hbm, ws_hbm, board_hbm, after_ref, out_ref, late_ref, slot_ref, *scratch):
     values, ws_ref, board_ref, sems = scratch
     boards = values.shape[0]
     heads = plan.heads
@@ -236,6 +242,7 @@
     lane = lax.broadcasted_iota(jnp.int32, fold.shape, 1)
     out_ref[boards] = jnp.where(lane % span < heads, rounded, fold - rounded).astype(BF16)
     copies[3].wait()
+    late_ref[...] = out_ref[...]
 
 
 def read_lists(plan, w_ref, out_ref):
@@ -327,13 +334,21 @@
 
     lax.fori_loop(0, -(-boards // 2), step, 0)
     for g in range(plan.groups):
-        out_ref[g] = jnp.concatenate([scores[g * plan.pair + p] for p in range(plan.pair)], axis=0)
+        both = jnp.concatenate([scores[g * plan.pair + p] for p in range(plan.pair)], axis=0)
+        for copy in range(out_ref.shape[1]):
+            out_ref[g, copy] = both
 
 
 def finish(plan, parts_ref, board_ref, slot_ref, out_ref):
+    line = parts_ref.shape[1]
     columns = []
-    for at in range(plan.line):
-        columns.append(sum(parts_ref[at * plan.pair + p] for p in range(plan.pair)))
+    for at in range(line):
+        total = None
+        for g in range(parts_ref.shape[0]):
+            for p in range(parts_ref.shape[2]):
+                term = parts_ref[g, at, p]
+                total = term if total is None else total + term
+        columns.append(total)
     scores = jnp.concatenate(columns, axis=0)
     live = scores > 0.5 * DEAD
     peak = jnp.max(scores, axis=1, keepdims=True)
@@ -444,11 +459,11 @@
     )
     weights = lax.all_to_all(packed, ("line", "pair"), split_axis=0, concat_axis=0, tiled=True)
 
-    payload, slot_row = scalar_call(
+    payload, late, slot_row = scalar_call(
         functools.partial(pack_prefix, plan),
         (line_at * pair + pair_at).reshape(1),
         (prefix_kv, ws, board_row, packed),
-        (shape((boards_here + 1, prefix_len, HD), BF16), shape((1, row_count), jnp.int32)),
+        (*[shape((boards_here + 1, prefix_len, HD), BF16)] * 2, shape((1, row_count), jnp.int32)),
         [
             pltpu.VMEM((boards_here, prefix_len, HD), BF16),
             pltpu.VMEM((heads, HD), BF16),
@@ -459,24 +474,26 @@
         {at: untouched() for at in range(4)},
         62,
     )
-    beside = swap(payload, slab_axes, plan.slab, 1)
     across = swap(payload, slab_axes, plan.slab, 2)
 
     block = min(moves, 256)
-    normed = pl.pallas_call(
+    normed, late = pl.pallas_call(
         normalize,
-        out_shape=shape((moves, width), BF16),
+        out_shape=(shape((moves, width), BF16), shape(late.shape, BF16)),
         grid=(moves // block,),
         in_specs=[
             pl.BlockSpec((block, width), lambda i: (i, 0)),
             pl.BlockSpec((width // HD, HD), lambda i: (0, 0)),
             untouched(),
+            untouched(),
         ],
-        out_specs=pl.BlockSpec((block, width), lambda i: (i, 0)),
+        out_specs=(pl.BlockSpec((block, width), lambda i: (i, 0)), untouched()),
         scratch_shapes=[pltpu.VMEM((1, width), F32)],
+        input_output_aliases={3: 1},
         compiler_params=limits(58),
         cost_estimate=cost(moves * width, moves * width // 4),
-    )(move_table, norm_gain.reshape(width // HD, HD), packed)
+    )(move_table, norm_gain.reshape(width // HD, HD), packed, late)
+    beside = swap(late, slab_axes, plan.slab, 1)
     turns = turn_table(prefix_len).reshape(line, 1, plan.pairs, 2)
     turns = jnp.asarray(np.tile(turns, (1, plan.mine, 1, 1)).reshape(line, plan.mine * plan.pairs, 2))
     flat = weights.transpose(1, 0, 2).reshape(plan.rows, width) if depth % HD else weights
@@ -485,19 +502,12 @@
         line_at.reshape(1),
         (flat, normed, turns),
         (shape((line, plan.line_rows, moves), BF16), shape((plan.mine, moves), F32)),
-        [pltpu.VMEM((2, block, width), BF16), pltpu.SemaphoreType.DMA((2,))],
+        [pltpu.VMEM((moves, width), BF16), pltpu.SemaphoreType.DMA((moves // block,))],
         cost(moves * width, moves * width // 4),
         {1: untouched()},
-        58,
-    )
-    queries = pl.pallas_call(
-        tie,
-        out_shape=shape(queries.shape, BF16),
-        in_specs=[untouched()] * 3,
-        out_specs=untouched(),
-        input_output_aliases={0: 0},
-        cost_estimate=cost(0, 0),
-    )(queries, beside, across)
+        57,
+    )
+    queries = tied(queries, beside, across)
     queries = lax.all_to_all(queries, "line", split_axis=0, concat_axis=0, tiled=True)
     listed = pl.pallas_call(
         functools.partial(read_lists, plan),
@@ -509,33 +519,40 @@
     diagonal = swap(beside, slab_axes, plan.slab, 2)
 
     query_rows = plan.mine * HD
-    parts = scalar_call(
+    back = plan.peers * lax.axis_size("tensor")
+    parts = pl.pallas_call(
         functools.partial(attend, plan),
-        slab_at.reshape(1),
-        (
-            queries.reshape(line * plan.line_rows, moves),
-            jnp.asarray(entry_order(plan), BF16),
-            own_values,
-            payload,
-            beside,
-            across,
-            diagonal,
-            listed,
-        ),
-        shape((groups, plan.share, plan.slots), F32),
-        [
+        out_shape=shape((groups, back, plan.share, plan.slots), F32),
+        in_specs=[pl.BlockSpec(memory_space=pltpu.SMEM)] + [pl.BlockSpec(memory_space=pltpu.VMEM)] * 8,
+        out_specs=pl.BlockSpec(memory_space=pltpu.VMEM),
+        scratch_shapes=[
             pltpu.VMEM((query_rows + 16, moves), BF16),
             pltpu.VMEM((16, moves), F32),
             pltpu.VMEM((plan.slab, boards_here, plan.slots), F32),
             pltpu.VMEM((query_rows + 16, plan.slab * plan.slots), F32),
             pltpu.VMEM((query_rows + 16, plan.slab * plan.slots), F32),
         ],
-        cost(2 * 272 * moves * 4096, 4 * 10**6),
-    )
-    parts = lax.psum(parts, ("groups", "tensor"))
-    parts = lax.dynamic_index_in_dim(parts, group_at, axis=0)
-    parts = jnp.broadcast_to(parts, (plan.peers, plan.share, plan.slots))
-    parts = lax.all_to_all(parts, ("line", "pair"), split_axis=0, concat_axis=0, tiled=True)
+        compiler_params=limits(24),
+        cost_estimate=cost(2 * 272 * moves * 4096, 4 * 10**6),
+    )(
+        slab_at.reshape(1),
+        queries.reshape(line * plan.line_rows, moves),
+        jnp.asarray(entry_order(plan), BF16),
+        own_values,
+        payload,
+        beside,
+        across,
+        diagonal,
+        listed,
+    )
+    parts = lax.all_to_all(
+        parts.reshape(groups * back, plan.share, plan.slots),
+        ("groups", "line", "pair", "tensor"),
+        split_axis=0,
+        concat_axis=0,
+        tiled=True,
+    )
+    parts = parts.reshape(groups, line, back // line, plan.share, plan.slots)
     logprob = pl.pallas_call(
         functools.partial(finish, plan), out_shape=shape((1, row_count), F32), compiler_params=limits(VMEM_MIB)
     )(parts, board_row, slot_row)

time: 96.8 us -> 91 us (0.940)
  blocking collectives: 22.9 us -> 15.6 us
  local copies, waits for them, and re-layouts: 5.21 us -> 8 us
  Pallas kernels: 33.8 us -> 32.8 us
    psum x1 -> x0, blocking collectives: 10.1 us -> none  [per_device(): parts = lax.psum(parts, ('groups', 'tensor'))]
    pallas_call x4 -> x3, Pallas kernels: 23.2 us -> 14.7 us  [scalar_call(): pl.pallas_call(kernel, out_shape=outs, grid_spec=pltpu.PrefetchScalarGrid...]
    pallas_call x2 -> x3, Pallas kernels: 9.38 us -> 16.8 us  [the longest x1 9.46 us: per_device(): pl.pallas_call(normalize, out_shape=(shape((moves, width), BF16), shape(l...]
    all_to_all x1, blocking collectives: 12.8 us -> 15.6 us  [per_device(): lax.all_to_all(parts.reshape(groups * back, plan.share, plan.slots), ('gr...]
    unnamed x22 -> x24, local copies, waits for them, and re-layouts: 5.19 us -> 8 us
  transfers between devices with their start and end apart: 6 -> 6, of which waited for: 3 -> 3; matrix products, arithmetic and copies ran while one was open for 0% -> 0% of each run, Pallas kernels for 21% -> 23%
where the time goes in v8:
time: 91 us; the launch traced here: 90.4 us
  Pallas kernels  32.8 us (36%)
  waiting for transfers between devices  17.4 us (19%)
  starting transfers between devices  16.4 us (18%)
  blocking collectives  15.6 us (17%)
  local copies, waits for them, and re-layouts  8 us (9%)
    all_to_all x1, blocking collectives, per_device(): lax.all_to_all(parts.reshape(groups * back, plan.share, plan.slots), ('gr...  15.6 us
    pallas_call x3, Pallas kernels, scalar_call(): pl.pallas_call(kernel, out_shape=outs, grid_spec=pltpu.PrefetchScalarGrid...  14.7 us
    ppermute x4, waiting for transfers between devices, swap(): return lax.ppermute(x, names, [(at, at ^ step) for at in range(size)])  10.6 us
    pallas_call x1, Pallas kernels, per_device(): pl.pallas_call(normalize, out_shape=(shape((moves, width), BF16), shape(l...  9.46 us
    unnamed x24, local copies, waits for them, and re-layouts  8 us
    pallas_call x1, Pallas kernels, per_device(): pl.pallas_call(functools.partial(attend, plan), out_shape=shape((groups,...  7.33 us
    all_to_all x1, starting transfers between devices, per_device(): lax.all_to_all(packed, ('line', 'pair'), split_axis=0, concat_axis=0, til...  7.27 us
    all_to_all x1, waiting for transfers between devices, per_device(): lax.all_to_all(packed, ('line', 'pair'), split_axis=0, concat_axis=0, til...  6.19 us
  transfers between devices with their start and end apart: 6, of which 3 were waited for; matrix products, arithmetic and copies ran while one was open for 0% of the time, Pallas kernels for 23%

profile of v8, /device:TPU:0, one launch (start us, length us, event | category | flops | bytes accessed | tf_op | source)
XLA Modules:
  0.0 90.4 jit_solution(15113949673248926934)
XLA Ops:
  0.0 3.5 %shard_map.100.after_ref = bf16[8,104,512]{2,1,0:T(8,128)(2,1)} custom-call(s32[1]{0:T(128)} %bitcast.2.at_ref, bf16[512,1024]{1,0:T(8,128)(2,1)} %wq_hbm.1, bf16[512,256]{1,0:T(8,128)(2,1)} %wkv_hbm.1, bf16[8,128]{1,0:T(8,128)(2,1)} %bitcast.23, s32[1,512]{1,0:T(1,128)} %bitcast.18, s32[1,512]{1,0:T(1,128)} %bitcast.25), custom_call_target="tpu_custom_call" | custom-call | flops 436207616 | bytes 2097152 | tf_op jit(solution)/shard_map/pallas_call | solution.py:376
  3.5 7.3 %all-to-all-start = ((bf16[8,104,512]{2,1,0:T(8,128)(2,1)}), bf16[8,104,512]{2,1,0:T(8,128)(2,1)S(1)}, u32[]{:S(2)}, u32[]{:S(2)}) async-start(bf16[8,104,512]{2,1,0:T(8,128)(2,1)} %shard_map.100.after_ref), calls=%async_computation | async-start | bytes 1703936 | tf_op jit(solution)/shard_map/all_to_all | solution.py:460
  10.8 2.4 %shard_map.101 = (bf16[9,256,128]{2,1,0:T(8,128)(2,1)}, bf16[9,256,128]{2,1,0:T(8,128)(2,1)}, s32[1,512]{1,0:T(1,128)}) custom-call(s32[1]{0:T(128)} %bitcast.7.at_ref, bf16[8,256,256]{2,1,0:T(8,128)(2,1)} %prefix_hbm.1, bf16[8,128]{1,0:T(8,128)(2,1)} %bitcast.24, s32[1,512]{1,0:T(1,128)} %bitcast.19, bf16[8,104,512]{2,1,0:T(8,128)(2,1)} %shard_map.100.after_ref), custom_call_target="tpu_custom_call" | custom-call | flops 67108864 | bytes 1048576 | tf_op jit(solution)/shard_map/pallas_call | solution.py:376
  13.3 9.5 %shard_map.102 = (bf16[1024,4096]{1,0:T(8,128)(2,1)}, bf16[9,256,128]{2,1,0:T(8,128)(2,1)}) custom-call(bf16[1024,4096]{1,0:T(8,128)(2,1)} %table_ref.1, bf16[32,128]{1,0:T(8,128)(2,1)} %bitcast.22, bf16[8,104,512]{2,1,0:T(8,128)(2,1)} %shard_map.100.after_ref, bf16[9,256,128]{2,1,0:T(8,128)(2,1)} %get-tuple-element.12.late_ref), custom_call_target="tpu_custom_call", output_to_operand_aliasing={{1}: (3, {})} | custom-call | flops 4194304 | bytes 1048576 | tf_op jit(solution)/shard_map/pallas_call | solution.py:480
  22.7 2.0 %collective-permute-start = (bf16[9,256,128]{2,1,0:T(8,128)(2,1)}, bf16[9,256,128]{2,1,0:T(8,128)(2,1)S(1)}, u32[]{:S(2)}, u32[]{:S(2)}) collective-permute-start(bf16[9,256,128]{2,1,0:T(8,128)(2,1)} %get-tuple-element.15), channel_id=1, source_target_pairs={{0,2},{2,0},{16,18},{18,16},{1,3},{3,1},{17,19},{19,17},{4,6},{6,4... | collective-permute-start | bytes 1769480 | tf_op jit(solution)/shard_map/ppermute | solution.py:396
  24.7 1.5 %collective-permute-start.1 = (bf16[9,256,128]{2,1,0:T(8,128)(2,1)S(1)}, bf16[9,256,128]{2,1,0:T(8,128)(2,1)S(1)}, u32[]{:S(2)}, u32[]{:S(2)}) collective-permute-start(bf16[9,256,128]{2,1,0:T(8,128)(2,1)S(1)} %copy-done.8), channel_id=1, source_target_pairs={{0,16},{2,18},{16,0},{18,2},{1,17},{3,19},{17,1},{19,3},{4,20},{6,... | collective-permute-start | bytes 1769480 | tf_op jit(solution)/shard_map/ppermute | solution.py:396
  26.2 6.2 %all-to-all-done.w_ref = bf16[8,104,512]{2,1,0:T(8,128)(2,1)S(1)} async-done(((bf16[8,104,512]{2,1,0:T(8,128)(2,1)}), bf16[8,104,512]{2,1,0:T(8,128)(2,1)S(1)}, u32[]{:S(2)}, u32[]{:S(2)}) %all-to-all-start) | async-done | bytes 852000 | tf_op jit(solution)/shard_map/all_to_all | solution.py:460
  32.4 1.0 %copy-done = bf16[8,104,512]{2,1,0:T(8,128)(2,1)} copy-done((bf16[8,104,512]{2,1,0:T(8,128)(2,1)}, bf16[8,104,512]{2,1,0:T(8,128)(2,1)S(1)}, u32[]{:S(2)}) %copy-start) | copy-done | bytes 851992
  33.4 8.8 %shard_map.103 = (bf16[4,72,1024]{2,1,0:T(8,128)(2,1)}, f32[2,1024]{1,0:T(2,128)}) custom-call(s32[1]{0:T(128)} %bitcast.1.at_ref, bf16[8,104,512]{2,1,0:T(8,128)(2,1)} %copy-done, bf16[1024,4096]{1,0:T(8,128)(2,1)} %get-tuple-element.13.normed_hbm, f32[4,32,2]{2,1,0:T(8,128)} %constant.19.clone.turn_ref), custom_call_target="tpu_custom_call" | custom-call | flops 4194304 | bytes 1048576 | tf_op jit(solution)/shard_map/pallas_call | solution.py:376
  42.3 0.8 copy-done.2
  43.3 3.5 %all-to-all-start.1 = ((bf16[4,72,1024]{2,1,0:T(8,128)(2,1)}), bf16[4,72,1024]{2,1,0:T(8,128)(2,1)S(1)}, u32[]{:S(2)}, u32[]{:S(2)}) async-start(bf16[4,72,1024]{2,1,0:T(8,128)(2,1)} %shard_map.104), calls=%async_computation.1 | async-start | bytes 1179648 | tf_op jit(solution)/shard_map/all_to_all | solution.py:511
  46.8 1.6 %collective-permute-start.2 = (bf16[9,256,128]{2,1,0:T(8,128)(2,1)}, bf16[9,256,128]{2,1,0:T(8,128)(2,1)S(1)}, u32[]{:S(2)}, u32[]{:S(2)}) collective-permute-start(bf16[9,256,128]{2,1,0:T(8,128)(2,1)} %copy-done.2), channel_id=1, source_target_pairs={{0,16},{2,18},{16,0},{18,2},{1,17},{3,19},{17,1},{19,3},{4,20},{6,... | collective-permute-start | bytes 1769480 | tf_op jit(solution)/shard_map/ppermute | solution.py:396
  48.3 1.2 %copy-done.1 = bf16[8,104,512]{2,1,0:T(8,128)(2,1)S(1)} copy-done((bf16[8,104,512]{2,1,0:T(8,128)(2,1)S(1)}, bf16[8,104,512]{2,1,0:T(8,128)(2,1)}, u32[]{:S(2)}) %copy-start.1) | copy-done | bytes 851992
  49.7 0.6 collective-permute-start.3
  50.3 10.6 %collective-permute-done.3 = f32[16,128]{1,0:T(8,128)S(1)} collective-permute-done((f32[16,128]{1,0:T(8,128)S(1)}, f32[16,128]{1,0:T(8,128)S(1)}, u32[]{:S(2)}, u32[]{:S(2)}) %collective-permute-start.3) | collective-permute-done | bytes 8224 | tf_op jit(solution)/shard_map/ppermute | solution.py:396
  60.9 0.6 all-to-all-done.1
  61.5 1.1 %copy-done.3 = bf16[9,256,128]{2,1,0:T(8,128)(2,1)S(1)} copy-done((bf16[9,256,128]{2,1,0:T(8,128)(2,1)S(1)}, bf16[9,256,128]{2,1,0:T(8,128)(2,1)}, u32[]{:S(2)}) %copy-start.3) | copy-done | bytes 589848
  62.6 1.1 %copy-done.5 = bf16[9,256,128]{2,1,0:T(8,128)(2,1)S(1)} copy-done((bf16[9,256,128]{2,1,0:T(8,128)(2,1)S(1)}, bf16[9,256,128]{2,1,0:T(8,128)(2,1)}, u32[]{:S(2)}) %copy-start.5) | copy-done | bytes 589848
  63.7 1.1 %copy-done.9 = bf16[9,256,128]{2,1,0:T(8,128)(2,1)S(1)} copy-done((bf16[9,256,128]{2,1,0:T(8,128)(2,1)S(1)}, bf16[9,256,128]{2,1,0:T(8,128)(2,1)}, u32[]{:S(2)}) %copy-start.9) | copy-done | bytes 589848
  64.7 0.7 copy-done.10
  65.4 0.9 %copy-done.11 = bf16[272,288]{1,0:T(8,128)(2,1)S(1)} copy-done((bf16[272,288]{1,0:T(8,128)(2,1)S(1)}, bf16[272,288]{1,0:T(8,128)(2,1)}, u32[]{:S(2)}) %copy-start.11) | copy-done | bytes 156696
  66.4 7.3 %shard_map.106 = f32[2,16,16,128]{3,2,1,0:T(8,128)S(1)} custom-call(s32[1]{0:T(128)} %bitcast.at_ref, bf16[288,1024]{1,0:T(8,128)(2,1)S(1)} %bitcast.15, bf16[272,288]{1,0:T(8,128)(2,1)S(1)} %copy-done.11, f32[2,1024]{1,0:T(2,128)S(1)} %copy-done.10, bf16[9,256,128]{2,1,0:T(8,128)(2,1)S(1)} %copy-done.9, bf16[9,256,128]{2,1,0:T(8,128)(2,1)S(1)} %copy-done.3, ...), custom_call_target="tpu_custom_call" | custom-call | flops 2281701376 | bytes 4000000 | tf_op jit(solution)/shard_map/pallas_call | solution.py:523
  73.7 15.6 %all_to_all.15 = f32[32,16,128]{2,1,0:T(8,128)S(1)} all-to-all(f32[32,16,128]{2,1,0:T(8,128)S(1)} %bitcast.16), channel_id=1, replica_groups=mesh['groups'=2,'line'=4,'pair'=2,'tensor'=2] {'groups','line','pair','t..., dimensions={0} | all-to-all | bytes 524288 | tf_op jit(solution)/shard_map/all_to_all | solution.py:548
  89.3 1.1 %shard_map.107 = f32[1,512]{1,0:T(1,128)} custom-call(f32[2,4,4,16,128]{4,3,2,1,0:T(8,128)S(1)} %bitcast.14, s32[1,512]{1,0:T(1,128)S(1)} %bitcast.20, s32[1,512]{1,0:T(1,128)S(1)} %copy-done.7), custom_call_target="tpu_custom_call" | custom-call | tf_op jit(solution)/shard_map/pallas_call | solution.py:556
  (22 shorter events, 0.5 us)
Async XLA Ops:
  3.5 28.9 %all-to-all-start = ((bf16[8,104,512]{2,1,0:T(8,128)(2,1)}), bf16[8,104,512]{2,1,0:T(8,128)(2,1)S(1)}, u32[]{:S(2)}, u32[]{:S(2)}) async-start(bf16[8,104,512]{2,1,0:T(8,128)(2,1)} %shard_map.100.after_ref), calls=%async_computation | async-start | bytes 1703936 | tf_op jit(solution)/shard_map/all_to_all | solution.py:460
  13.2 11.5 %copy-start.8 = (bf16[9,256,128]{2,1,0:T(8,128)(2,1)S(1)}, bf16[9,256,128]{2,1,0:T(8,128)(2,1)}, u32[]{:S(2)}) copy-start(bf16[9,256,128]{2,1,0:T(8,128)(2,1)} %get-tuple-element.16.rest_0_) | copy-start | bytes 1769476
  22.7 19.5 %collective-permute-start = (bf16[9,256,128]{2,1,0:T(8,128)(2,1)}, bf16[9,256,128]{2,1,0:T(8,128)(2,1)S(1)}, u32[]{:S(2)}, u32[]{:S(2)}) collective-permute-start(bf16[9,256,128]{2,1,0:T(8,128)(2,1)} %get-tuple-element.15), channel_id=1, source_target_pairs={{0,2},{2,0},{16,18},{18,16},{1,3},{3,1},{17,19},{19,17},{4,6},{6,4... | collective-permute-start | bytes 1769480 | tf_op jit(solution)/shard_map/ppermute | solution.py:396
  24.7 17.5 %collective-permute-start.1 = (bf16[9,256,128]{2,1,0:T(8,128)(2,1)S(1)}, bf16[9,256,128]{2,1,0:T(8,128)(2,1)S(1)}, u32[]{:S(2)}, u32[]{:S(2)}) collective-permute-start(bf16[9,256,128]{2,1,0:T(8,128)(2,1)S(1)} %copy-done.8), channel_id=1, source_target_pairs={{0,16},{2,18},{16,0},{18,2},{1,17},{3,19},{17,1},{19,3},{4,20},{6,... | collective-permute-start | bytes 1769480 | tf_op jit(solution)/shard_map/ppermute | solution.py:396
  32.4 1.0 %copy-start = (bf16[8,104,512]{2,1,0:T(8,128)(2,1)}, bf16[8,104,512]{2,1,0:T(8,128)(2,1)S(1)}, u32[]{:S(2)}) copy-start(bf16[8,104,512]{2,1,0:T(8,128)(2,1)S(1)} %all-to-all-done.w_ref) | copy-start | bytes 2555908
  42.2 47.1 %copy-start.6 = (s32[512,1]{0,1:T(1,128)S(1)}, s32[512,1]{0,1:T(1,128)}, u32[]{:S(2)}) copy-start(s32[512,1]{0,1:T(1,128)} %param.12) | copy-start | bytes 6148
  42.2 47.1 %copy-start.7 = (s32[1,512]{1,0:T(1,128)S(1)}, s32[1,512]{1,0:T(1,128)}, u32[]{:S(2)}) copy-start(s32[1,512]{1,0:T(1,128)} %get-tuple-element.18.slot_ref) | copy-start | bytes 6148
  42.2 0.8 copy-start.2
  42.3 1.0 %copy-start.4 = (bf16[9,256,128]{2,1,0:T(8,128)(2,1)}, bf16[9,256,128]{2,1,0:T(8,128)(2,1)S(1)}, u32[]{:S(2)}) copy-start(bf16[9,256,128]{2,1,0:T(8,128)(2,1)S(1)} %collective-permute-done.1.refs_2_.rest_2_) | copy-start | bytes 1769476
  43.3 18.3 %all-to-all-start.1 = ((bf16[4,72,1024]{2,1,0:T(8,128)(2,1)}), bf16[4,72,1024]{2,1,0:T(8,128)(2,1)S(1)}, u32[]{:S(2)}, u32[]{:S(2)}) async-start(bf16[4,72,1024]{2,1,0:T(8,128)(2,1)} %shard_map.104), calls=%async_computation.1 | async-start | bytes 1179648 | tf_op jit(solution)/shard_map/all_to_all | solution.py:511
  46.8 14.2 %collective-permute-start.2 = (bf16[9,256,128]{2,1,0:T(8,128)(2,1)}, bf16[9,256,128]{2,1,0:T(8,128)(2,1)S(1)}, u32[]{:S(2)}, u32[]{:S(2)}) collective-permute-start(bf16[9,256,128]{2,1,0:T(8,128)(2,1)} %copy-done.2), channel_id=1, source_target_pairs={{0,16},{2,18},{16,0},{18,2},{1,17},{3,19},{17,1},{19,3},{4,20},{6,... | collective-permute-start | bytes 1769480 | tf_op jit(solution)/shard_map/ppermute | solution.py:396
  48.3 1.2 %copy-start.1 = (bf16[8,104,512]{2,1,0:T(8,128)(2,1)S(1)}, bf16[8,104,512]{2,1,0:T(8,128)(2,1)}, u32[]{:S(2)}) copy-start(bf16[8,104,512]{2,1,0:T(8,128)(2,1)} %copy-done) | copy-start | bytes 2555908
  49.7 11.2 %collective-permute-start.3 = (f32[16,128]{1,0:T(8,128)S(1)}, f32[16,128]{1,0:T(8,128)S(1)}, u32[]{:S(2)}, u32[]{:S(2)}) collective-permute-start(f32[16,128]{1,0:T(8,128)S(1)} %shard_map.105), channel_id=1, source_target_pairs={{0,16},{2,18},{16,0},{18,2},{1,17},{3,19},{17,1},{19,3},{4,20},{6,... | collective-permute-start | bytes 24584 | tf_op jit(solution)/shard_map/ppermute | solution.py:396
  61.5 1.1 %copy-start.3 = (bf16[9,256,128]{2,1,0:T(8,128)(2,1)S(1)}, bf16[9,256,128]{2,1,0:T(8,128)(2,1)}, u32[]{:S(2)}) copy-start(bf16[9,256,128]{2,1,0:T(8,128)(2,1)} %copy-done.2) | copy-start | bytes 1769476
  62.6 1.1 %copy-start.5 = (bf16[9,256,128]{2,1,0:T(8,128)(2,1)S(1)}, bf16[9,256,128]{2,1,0:T(8,128)(2,1)}, u32[]{:S(2)}) copy-start(bf16[9,256,128]{2,1,0:T(8,128)(2,1)} %copy-done.4) | copy-start | bytes 1769476
  63.7 1.1 %copy-start.9 = (bf16[9,256,128]{2,1,0:T(8,128)(2,1)S(1)}, bf16[9,256,128]{2,1,0:T(8,128)(2,1)}, u32[]{:S(2)}) copy-start(bf16[9,256,128]{2,1,0:T(8,128)(2,1)} %get-tuple-element.16.rest_0_) | copy-start | bytes 1769476
  64.7 0.7 copy-start.10
  65.4 0.9 %copy-start.11 = (bf16[272,288]{1,0:T(8,128)(2,1)S(1)}, bf16[272,288]{1,0:T(8,128)(2,1)}, u32[]{:S(2)}) copy-start(bf16[272,288]{1,0:T(8,128)(2,1)} %constant.20.clone.order_ref) | copy-start | bytes 470020

commit v9 on v8

--- a/solution.py
+++ b/solution.py
@@ -16,6 +16,7 @@
 THETA = 5000000.0
 DEAD = -1e30
 VMEM_MIB = 52
+GROUP, LINE, PEER, SLAB = range(4)
 
 F32 = jnp.float32
 BF16 = jnp.bfloat16
@@ -50,11 +51,12 @@
         self.capacity = capacity
         self.share = share
         self.slots = self.peers * capacity
-
-
-def pack_weights(plan, at_ref, wq_hbm, wkv_hbm, ws_hbm, board_hbm, ids_hbm, out_ref, *scratch):
-    wq, wkv, ws_ref, board_ref, ids_ref, pick, sems = scratch
-    group = at_ref[0]
+        self.direct = line <= 4
+
+
+def pack_weights(plan, place_ref, wq_hbm, wkv_hbm, ws_hbm, board_hbm, ids_hbm, *rest):
+    out_ref, wq, wkv, ws_ref, board_ref, ids_ref, pick, sems = rest
+    group = place_ref[GROUP]
     rows, half_cols = plan.rows, wq.shape[1]
     columns_here = pl.ds(pl.multiple_of(group * half_cols, HD), half_cols)
     copies = (
@@ -127,7 +129,7 @@
         out_ref[peer] = jnp.where(r == plan.list_at, lists[peer // plan.pair], mine).astype(BF16)
 
 
-def normalize(table_ref, gain_ref, after_ref, late_ref, out_ref, late_out_ref, gain):
+def normalize(table_ref, gain_ref, after_ref, out_ref, gain):
     @pl.when(pl.program_id(0) == 0)
     def _():
         rows = gain_ref[...].astype(F32)
@@ -140,8 +142,7 @@
         out_ref[at] = (raw * inverse * gain[...]).astype(BF16)
 
 
-def project(plan, at_ref, w_ref, normed_hbm, turn_ref, *rest):
-    q_ref, vo_ref, table, sems = rest[-4:]
+def project(plan, place_ref, w_ref, normed_hbm, turn_hbm, q_ref, vo_ref, table, turns, sems, turn_sem):
     moves = normed_hbm.shape[0]
     steps = sems.shape[0]
     block = moves // steps
@@ -151,11 +152,13 @@
         at = pl.ds(start, rows)
         return pltpu.make_async_copy(normed_hbm.at[at], table.at[at], sems.at[step])
 
+    turn_copy = pltpu.make_async_copy(turn_hbm.at[place_ref[LINE]], turns, turn_sem)
+    turn_copy.start()
     for start in range(0, moves, piece):
         copy(start, piece, start // block).start()
+    turn_copy.wait()
 
     half, k_half = plan.q_rows // 2, plan.k_rows // 2
-    turns = turn_ref[at_ref[0]]
     cosine, sine = turns[:, 0:1], turns[:, 1:2]
     cos_k, sin_k = cosine[:k_half], sine[:k_half]
     for step in range(steps):
@@ -165,14 +168,10 @@
             depth = w_ref.shape[2]
             total = None
             for s in range(w_ref.shape[0]):
-                term = matmul(table[at, s * depth : (s + 1) * depth], w_ref[s], NT)
+                term = matmul(w_ref[s], table[at, s * depth : (s + 1) * depth], NT)
                 total = term if total is None else total + term
         else:
-            total = matmul(table[at, :], w_ref[...], NT)
-        pad = -total.shape[1] % HD
-        if pad:
-            total = jnp.concatenate([total, jnp.zeros((block, pad), F32)], axis=1)
-        total = total.T
+            total = matmul(w_ref[...], table[at, :], NT)
         first, second = total[:half], total[half : 2 * half]
         f_first = (first * cosine - second * sine).astype(BF16).astype(F32)
         f_second = (second * cosine + first * sine).astype(BF16).astype(F32)
@@ -190,8 +189,11 @@
         if pad:
             pieces.append(jnp.zeros((pad, block), F32))
         out = jnp.concatenate(pieces, axis=0).astype(BF16)
-        for copy_at in range(q_ref.shape[0]):
-            q_ref[copy_at, :, at] = out
+        if plan.direct:
+            q_ref[:, at] = out
+        else:
+            for line in range(plan.line):
+                q_ref[line, :, at] = out
         vo_ref[:, at] = total[plan.fold_at : plan.list_at]
 
 
@@ -202,12 +204,12 @@
         in_specs=[untouched()] * (1 + len(others)),
         out_specs=untouched(),
         input_output_aliases={0: 0},
-        compiler_params=limits(62),
+        compiler_params=limits(1),
         cost_estimate=cost(0, 0),
     )(x, *others)
 
 
-def pack_prefix(plan, at_ref, prefix_hbm, ws_hbm, board_hbm, after_ref, out_ref, late_ref, slot_ref, *scratch):
+def pack_prefix(plan, place_ref, prefix_hbm, ws_hbm, board_hbm, after_ref, out_ref, slot_ref, *scratch):
     values, ws_ref, board_ref, sems = scratch
     boards = values.shape[0]
     heads = plan.heads
@@ -226,7 +228,7 @@
     other = lax.broadcasted_iota(jnp.int32, (count, count), 0)
     own = lax.broadcasted_iota(jnp.int32, (count, count), 1)
     rank = jnp.sum(jnp.where((board_col == board_row) & (other < own), 1.0, 0.0), axis=0, keepdims=True)
-    slot_ref[...] = rank.astype(jnp.int32) + at_ref[0] * plan.capacity
+    slot_ref[...] = rank.astype(jnp.int32) + place_ref[PEER] * plan.capacity
 
     copies[1].wait()
     span = HD // boards
@@ -242,10 +244,10 @@
     lane = lax.broadcasted_iota(jnp.int32, fold.shape, 1)
     out_ref[boards] = jnp.where(lane % span < heads, rounded, fold - rounded).astype(BF16)
     copies[3].wait()
-    late_ref[...] = out_ref[...]
-
-
-def read_lists(plan, w_ref, out_ref):
+
+
+def read_lists(plan, place_ref, *refs):
+    w_ref, out_ref = refs
     share, capacity, peers = plan.share, plan.capacity, plan.peers
     span = share * capacity
     rows = jnp.concatenate([w_ref[s].astype(F32)[plan.list_at : plan.list_at + 1] for s in range(peers)], axis=0)
@@ -265,16 +267,26 @@
     out_ref[...] = jnp.sum(listed.reshape(share, peers, plan.slots), axis=1)
 
 
-def attend(plan, at_ref, q_ref, order_ref, vo_ref, *rest):
-    prefix_refs = rest[: plan.slab]
-    moves_ref, out_ref, table, extra, scores, taken_even, taken_odd = rest[plan.slab :]
-    here = at_ref[0]
+def attend(plan, place_ref, vo_ref, own_ref, other_ref, *rest):
+    prefix_refs, rest = rest[: plan.slab], rest[plan.slab :]
+    *q_refs, out_ref, table, extra, scores, taken_even, taken_odd = rest
+    here = place_ref[SLAB]
     mine, heads, slots = plan.mine, plan.heads, plan.slots
-    moves = q_ref.shape[1]
+    moves = vo_ref.shape[1]
     boards = prefix_refs[0].shape[0] - 1
     query_rows = mine * HD
 
-    mixed = matmul(order_ref[...], q_ref[...])
+    mixed = None
+    for step, q_ref in enumerate(q_refs):
+        r = lax.broadcasted_iota(jnp.int32, (query_rows + 8, q_ref.shape[0]), 0)
+        c = lax.broadcasted_iota(jnp.int32, (query_rows + 8, q_ref.shape[0]), 1)
+        line, at = (place_ref[LINE] ^ step, c) if plan.direct else (c // plan.line_rows, c % plan.line_rows)
+        part, head, entry = at // (mine * plan.pairs), (at // plan.pairs) % mine, at % plan.pairs
+        goes = jnp.where(at < plan.q_rows, head * HD + part * HALF + line * plan.pairs + entry, -1)
+        tail = at - plan.q_rows
+        goes = jnp.where((tail >= 0) & (tail < 2 * mine), query_rows + tail % mine, goes)
+        term = matmul(jnp.where(r == goes, 1.0, 0.0).astype(BF16), q_ref[...])
+        mixed = term if mixed is None else mixed + term
     table[:query_rows] = mixed[:query_rows].astype(BF16)
     extra[...] = jnp.zeros_like(extra)
     for place, value in ((0, mixed[query_rows : query_rows + mine]), (2 * mine, vo_ref[...])):
@@ -296,7 +308,7 @@
 
     def moves_of(j, board):
         place = ((here ^ j) % plan.pair) * boards + board
-        return moves_ref[j // plan.pair, pl.ds(place, 1), :]
+        return (own_ref, other_ref)[j // plan.pair][pl.ds(place, 1), :].astype(jnp.int32)
 
     def gather(board, taken):
         chosen = [
@@ -370,22 +382,18 @@
     return pl.BlockSpec(memory_space=pl.ANY)
 
 
-def scalar_call(kernel, at, args, outs, scratch, cost=None, specs=None, mib=VMEM_MIB):
-    whole = lambda x: pl.BlockSpec(x.shape, lambda i, at, n=len(x.shape): (0,) * n)
-    specs = specs or {}
+def local_call(kernel, place, args, outs, scratch=(), mib=40, copied=(), flops=0, nbytes=0):
+    vmem = pl.BlockSpec(memory_space=pltpu.VMEM)
     return pl.pallas_call(
         kernel,
         out_shape=outs,
-        grid_spec=pltpu.PrefetchScalarGridSpec(
-            num_scalar_prefetch=1,
-            grid=(1,),
-            in_specs=[specs.get(i, whole(x)) for i, x in enumerate(args)],
-            out_specs=jax.tree.map(whole, outs),
-            scratch_shapes=scratch,
-        ),
+        in_specs=[pl.BlockSpec(memory_space=pltpu.SMEM)]
+        + [untouched() if at in copied else vmem for at in range(len(args))],
+        out_specs=jax.tree.map(lambda x: vmem, outs),
+        scratch_shapes=scratch,
         compiler_params=limits(mib),
-        cost_estimate=cost,
-    )(at, *args)
+        cost_estimate=cost(flops, nbytes),
+    )(place, *args)
 
 
 def cost(flops, nbytes):
@@ -404,20 +412,6 @@
     frequency = THETA ** (-2.0 * np.arange(HALF, dtype=np.float32) / HD)
     angles = np.float32(position) * frequency.astype(np.float32)
     return np.stack([np.cos(angles), np.sin(angles)], axis=1).astype(np.float32)
-
-
-def entry_order(plan):
-    order = np.zeros((plan.mine * HD + 16, plan.line * plan.line_rows), np.float32)
-    for head in range(plan.mine):
-        for part in range(2):
-            for entry in range(HALF):
-                line, at = divmod(entry, plan.pairs)
-                source = line * plan.line_rows + (part * plan.mine + head) * plan.pairs + at
-                order[head * HD + part * HALF + entry, source] = 1.0
-        for line in range(plan.line):
-            for piece in range(2):
-                order[plan.mine * HD + head, line * plan.line_rows + plan.q_rows + piece * plan.mine + head] = 1.0
-    return order
 
 
 def per_device(prefix_kv, move_ids, move_board, move_table, norm_gain, w_query, w_keyval, w_score):
@@ -433,15 +427,15 @@
     group_at = lax.axis_index("groups").astype(jnp.int32)
     line_at = lax.axis_index("line").astype(jnp.int32)
     pair_at = lax.axis_index("pair").astype(jnp.int32)
-    slab_at = group_at * pair + pair_at
+    place = jnp.stack([group_at, line_at, line_at * pair + pair_at, group_at * pair + pair_at])
     ws = w_score.reshape(heads, HD)
     slab_axes = ("groups", "pair")
     board_row = move_board.reshape(1, row_count)
 
     half_cols = w_query.shape[1] // groups
-    packed = scalar_call(
+    packed = local_call(
         functools.partial(pack_weights, plan),
-        group_at.reshape(1),
+        place,
         (w_query, w_keyval, ws, board_row, move_ids.reshape(1, row_count)),
         shape((plan.peers, plan.rows, depth), BF16),
         [
@@ -453,97 +447,91 @@
             pltpu.VMEM((plan.peers * plan.rows, half_cols + 2 * HD), F32),
             pltpu.SemaphoreType.DMA((5,)),
         ],
-        cost(2 * plan.peers * plan.rows * half_cols * depth, 4 * w_query.size),
-        {at: untouched() for at in range(5)},
         62,
+        range(5),
     )
     weights = lax.all_to_all(packed, ("line", "pair"), split_axis=0, concat_axis=0, tiled=True)
 
-    payload, late, slot_row = scalar_call(
+    keys = shape((boards_here + 1, prefix_len, HD), BF16)
+    payload, slot_row = local_call(
         functools.partial(pack_prefix, plan),
-        (line_at * pair + pair_at).reshape(1),
+        place,
         (prefix_kv, ws, board_row, packed),
-        (*[shape((boards_here + 1, prefix_len, HD), BF16)] * 2, shape((1, row_count), jnp.int32)),
+        (keys, shape((1, row_count), jnp.int32)),
         [
             pltpu.VMEM((boards_here, prefix_len, HD), BF16),
             pltpu.VMEM((heads, HD), BF16),
             pltpu.VMEM((1, row_count), jnp.int32),
             pltpu.SemaphoreType.DMA((4,)),
         ],
-        cost(2 * prefix_len * HD * HD * boards_here, 2 * prefix_kv.size),
-        {at: untouched() for at in range(4)},
-        62,
-    )
+        56,
+        range(4),
+    )
+    beside = swap(payload, slab_axes, plan.slab, 1)
     across = swap(payload, slab_axes, plan.slab, 2)
 
     block = min(moves, 256)
-    normed, late = pl.pallas_call(
+    normed = pl.pallas_call(
         normalize,
-        out_shape=(shape((moves, width), BF16), shape(late.shape, BF16)),
+        out_shape=shape((moves, width), BF16),
         grid=(moves // block,),
         in_specs=[
             pl.BlockSpec((block, width), lambda i: (i, 0)),
             pl.BlockSpec((width // HD, HD), lambda i: (0, 0)),
             untouched(),
-            untouched(),
         ],
-        out_specs=(pl.BlockSpec((block, width), lambda i: (i, 0)), untouched()),
+        out_specs=pl.BlockSpec((block, width), lambda i: (i, 0)),
         scratch_shapes=[pltpu.VMEM((1, width), F32)],
-        input_output_aliases={3: 1},
         compiler_params=limits(58),
         cost_estimate=cost(moves * width, moves * width // 4),
-    )(move_table, norm_gain.reshape(width // HD, HD), packed, late)
-    beside = swap(late, slab_axes, plan.slab, 1)
+    )(move_table, norm_gain.reshape(width // HD, HD), packed)
     turns = turn_table(prefix_len).reshape(line, 1, plan.pairs, 2)
-    turns = jnp.asarray(np.tile(turns, (1, plan.mine, 1, 1)).reshape(line, plan.mine * plan.pairs, 2))
+    turns = np.tile(turns, (1, plan.mine, 1, 1)).reshape(line, plan.mine * plan.pairs, 2)
     flat = weights.transpose(1, 0, 2).reshape(plan.rows, width) if depth % HD else weights
-    queries, own_values = scalar_call(
+    sent = (plan.line_rows, moves)
+    queries, own_values = local_call(
         functools.partial(project, plan),
-        line_at.reshape(1),
-        (flat, normed, turns),
-        (shape((line, plan.line_rows, moves), BF16), shape((plan.mine, moves), F32)),
-        [pltpu.VMEM((moves, width), BF16), pltpu.SemaphoreType.DMA((moves // block,))],
-        cost(moves * width, moves * width // 4),
-        {1: untouched()},
-        57,
+        place,
+        (flat, normed, jnp.asarray(turns)),
+        (shape(sent if plan.direct else (line, *sent), BF16), shape((plan.mine, moves), F32)),
+        [
+            pltpu.VMEM((moves, width), BF16),
+            pltpu.VMEM(turns.shape[1:], F32),
+            pltpu.SemaphoreType.DMA((4,)),
+            pltpu.SemaphoreType.DMA,
+        ],
+        53,
+        (1, 2),
+        2 * moves * width * 256,
+        2 * moves * width,
     )
     queries = tied(queries, beside, across)
-    queries = lax.all_to_all(queries, "line", split_axis=0, concat_axis=0, tiled=True)
-    listed = pl.pallas_call(
-        functools.partial(read_lists, plan),
-        out_shape=shape((plan.share, plan.slots), F32),
-        compiler_params=limits(32),
-        cost_estimate=cost(10**7, 10**6),
-    )(weights)
-    listed = jnp.stack([listed, swap(listed, slab_axes, plan.slab, pair)]).astype(jnp.int32)
+    if plan.direct:
+        queries = [queries] + [swap(queries, "line", line, step) for step in range(1, line)]
+    else:
+        queries = lax.all_to_all(queries, "line", split_axis=0, concat_axis=0, tiled=True)
+        queries = [queries.reshape(line * plan.line_rows, moves)]
+    listed = local_call(
+        functools.partial(read_lists, plan), place, (weights,), shape((plan.share, plan.slots), F32)
+    )
+    other = swap(listed, slab_axes, plan.slab, pair)
     diagonal = swap(beside, slab_axes, plan.slab, 2)
 
     query_rows = plan.mine * HD
     back = plan.peers * lax.axis_size("tensor")
-    parts = pl.pallas_call(
+    parts = local_call(
         functools.partial(attend, plan),
-        out_shape=shape((groups, back, plan.share, plan.slots), F32),
-        in_specs=[pl.BlockSpec(memory_space=pltpu.SMEM)] + [pl.BlockSpec(memory_space=pltpu.VMEM)] * 8,
-        out_specs=pl.BlockSpec(memory_space=pltpu.VMEM),
-        scratch_shapes=[
+        place,
+        (own_values, listed, other, payload, beside, across, diagonal, *queries),
+        shape((groups, back, plan.share, plan.slots), F32),
+        [
             pltpu.VMEM((query_rows + 16, moves), BF16),
             pltpu.VMEM((16, moves), F32),
             pltpu.VMEM((plan.slab, boards_here, plan.slots), F32),
             pltpu.VMEM((query_rows + 16, plan.slab * plan.slots), F32),
             pltpu.VMEM((query_rows + 16, plan.slab * plan.slots), F32),
         ],
-        compiler_params=limits(24),
-        cost_estimate=cost(2 * 272 * moves * 4096, 4 * 10**6),
-    )(
-        slab_at.reshape(1),
-        queries.reshape(line * plan.line_rows, moves),
-        jnp.asarray(entry_order(plan), BF16),
-        own_values,
-        payload,
-        beside,
-        across,
-        diagonal,
-        listed,
+        24,
     )
     parts = lax.all_to_all(
         parts.reshape(groups * back, plan.share, plan.slots),

time: 91 us -> 94.3 us (1.036)
  waiting for transfers between devices: 17.4 us -> 26.1 us
  local copies, waits for them, and re-layouts: 8 us -> 2.15 us
  blocking collectives: 15.6 us -> 13.3 us
  Pallas kernels: 32.8 us -> 34.3 us
  starting transfers between devices: 16.4 us -> 17.4 us
    ppermute x4 -> x7, waiting for transfers between devices: 10.6 us -> 26.1 us  [swap(): return lax.ppermute(x, names, [(at, at ^ step) for at in range(size)])]
    all_to_all x1, waiting for transfers between devices: 6.19 us -> 0.01 us  [per_device(): lax.all_to_all(packed, ('line', 'pair'), split_axis=0, concat_axis=0, til...]
    unnamed x24 -> x14, local copies, waits for them, and re-layouts: 8 us -> 2.15 us
    ppermute x4 -> x7, starting transfers between devices: 5.69 us -> 10.1 us  [swap(): return lax.ppermute(x, names, [(at, at ^ step) for at in range(size)])]
    all_to_all x1 -> x0, starting transfers between devices: 3.48 us -> none  [per_device(): lax.all_to_all(queries, 'line', split_axis=0, concat_axis=0, tiled=True)]
    all_to_all x1, blocking collectives: 15.6 us -> 13.3 us  [per_device(): lax.all_to_all(parts.reshape(groups * back, plan.share, plan.slots), ('gr...]
    pallas_call x6, Pallas kernels: 31.7 us -> 33.2 us  [the longest x5 23.8 us: local_call(): pl.pallas_call(kernel, out_shape=outs, in_specs=[pl.BlockSpec(memory_spac...]
  transfers between devices with their start and end apart: 6 -> 8, of which waited for: 3 -> 3; matrix products, arithmetic and copies ran while one was open for 0% -> 0% of each run, Pallas kernels for 23% -> 22%
where the time goes in v9:
time: 94.3 us; the launch traced here: 93.9 us
  Pallas kernels  34.3 us (36%)
  waiting for transfers between devices  26.1 us (28%)
  starting transfers between devices  17.4 us (18%)
  blocking collectives  13.3 us (14%)
  local copies, waits for them, and re-layouts  2.15 us (2%)
    ppermute x7, waiting for transfers between devices, swap(): return lax.ppermute(x, names, [(at, at ^ step) for at in range(size)])  26.1 us
    pallas_call x5, Pallas kernels, local_call(): pl.pallas_call(kernel, out_shape=outs, in_specs=[pl.BlockSpec(memory_spac...  23.8 us
    all_to_all x1, blocking collectives, per_device(): lax.all_to_all(parts.reshape(groups * back, plan.share, plan.slots), ('gr...  13.3 us
    ppermute x7, starting transfers between devices, swap(): return lax.ppermute(x, names, [(at, at ^ step) for at in range(size)])  10.1 us
    pallas_call x1, Pallas kernels, per_device(): pl.pallas_call(normalize, out_shape=shape((moves, width), BF16), grid=(mo...  9.4 us
    all_to_all x1, starting transfers between devices, per_device(): lax.all_to_all(packed, ('line', 'pair'), split_axis=0, concat_axis=0, til...  7.26 us
    unnamed x14, local copies, waits for them, and re-layouts  2.15 us
  transfers between devices with their start and end apart: 8, of which 3 were waited for; matrix products, arithmetic and copies ran while one was open for 0% of the time, Pallas kernels for 22%

profile of v9, /device:TPU:0, one launch (start us, length us, event | category | flops | bytes accessed | tf_op | source)
XLA Modules:
  0.0 93.9 jit_solution(7199465814675127742)
XLA Ops:
  0.0 0.6 pad_add_fusion.place_ref
  0.6 4.2 %shard_map.91.after_ref = bf16[8,104,512]{2,1,0:T(8,128)(2,1)} custom-call(s32[4]{0:T(128)} %pad_add_fusion.place_ref, bf16[512,1024]{1,0:T(8,128)(2,1)} %wq_hbm.1, bf16[512,256]{1,0:T(8,128)(2,1)} %wkv_hbm.1, bf16[8,128]{1,0:T(8,128)(2,1)} %bitcast.17, s32[1,512]{1,0:T(1,128)} %bitcast.13, s32[1,512]{1,0:T(1,128)} %bitcast.19), custom_call_target="tpu_custom_call" | custom-call | tf_op jit(solution)/shard_map/pallas_call | solution.py:387
  4.8 7.3 %all-to-all-start = ((bf16[8,104,512]{2,1,0:T(8,128)(2,1)}), bf16[8,104,512]{2,1,0:T(8,128)(2,1)S(1)}, u32[]{:S(2)}, u32[]{:S(2)}) async-start(bf16[8,104,512]{2,1,0:T(8,128)(2,1)} %shard_map.91.after_ref), calls=%async_computation | async-start | bytes 1703936 | tf_op jit(solution)/shard_map/all_to_all | solution.py:453
  12.1 2.9 %shard_map.95 = (bf16[9,256,128]{2,1,0:T(8,128)(2,1)}, s32[1,512]{1,0:T(1,128)}) custom-call(s32[4]{0:T(128)} %pad_add_fusion.place_ref, bf16[8,256,256]{2,1,0:T(8,128)(2,1)} %prefix_hbm.1, bf16[8,128]{1,0:T(8,128)(2,1)} %bitcast.18, s32[1,512]{1,0:T(1,128)} %bitcast.14, bf16[8,104,512]{2,1,0:T(8,128)(2,1)} %shard_map.91.after_ref), custom_call_target="tpu_custom_call" | custom-call | tf_op jit(solution)/shard_map/pallas_call | solution.py:387
  14.9 2.1 %collective-permute-start.1 = (bf16[9,256,128]{2,1,0:T(8,128)(2,1)}, bf16[9,256,128]{2,1,0:T(8,128)(2,1)S(1)}, u32[]{:S(2)}, u32[]{:S(2)}) collective-permute-start(bf16[9,256,128]{2,1,0:T(8,128)(2,1)} %get-tuple-element.10.rest_0_), channel_id=1, source_target_pairs={{0,2},{2,0},{16,18},{18,16},{1,3},{3,1},{17,19},{19,17},{4,6},{6,4... | collective-permute-start | bytes 1769480 | tf_op jit(solution)/shard_map/ppermute | solution.py:404
  17.0 1.5 %collective-permute-start.2 = (bf16[9,256,128]{2,1,0:T(8,128)(2,1)}, bf16[9,256,128]{2,1,0:T(8,128)(2,1)S(1)}, u32[]{:S(2)}, u32[]{:S(2)}) collective-permute-start(bf16[9,256,128]{2,1,0:T(8,128)(2,1)} %get-tuple-element.10.rest_0_), channel_id=1, source_target_pairs={{0,16},{2,18},{16,0},{18,2},{1,17},{3,19},{17,1},{19,3},{4,20},{6,... | collective-permute-start | bytes 1769480 | tf_op jit(solution)/shard_map/ppermute | solution.py:404
  18.5 17.9 %collective-permute-done.1.refs_1_.rest_1_ = bf16[9,256,128]{2,1,0:T(8,128)(2,1)S(1)} collective-permute-done((bf16[9,256,128]{2,1,0:T(8,128)(2,1)}, bf16[9,256,128]{2,1,0:T(8,128)(2,1)S(1)}, u32[]{:S(2)}, u32[]{:S(2)}) %collective-permute-start.1) | collective-permute-done | bytes 589856 | tf_op jit(solution)/shard_map/ppermute | solution.py:404
  36.4 1.5 %collective-permute-start.3 = (bf16[9,256,128]{2,1,0:T(8,128)(2,1)S(1)}, bf16[9,256,128]{2,1,0:T(8,128)(2,1)S(1)}, u32[]{:S(2)}, u32[]{:S(2)}) collective-permute-start(bf16[9,256,128]{2,1,0:T(8,128)(2,1)S(1)} %collective-permute-done.1.refs_1_.rest_1_), channel_id=1, source_target_pairs={{0,16},{2,18},{16,0},{18,2},{1,17},{3,19},{17,1},{19,3},{4,20},{6,... | collective-permute-start | bytes 1769480 | tf_op jit(solution)/shard_map/ppermute | solution.py:404
  38.0 9.4 %shard_map.92.normed_hbm = bf16[1024,4096]{1,0:T(8,128)(2,1)} custom-call(bf16[1024,4096]{1,0:T(8,128)(2,1)} %table_ref.1, bf16[32,128]{1,0:T(8,128)(2,1)} %bitcast.16, bf16[8,104,512]{2,1,0:T(8,128)(2,1)} %shard_map.91.after_ref), custom_call_target="tpu_custom_call" | custom-call | flops 4194304 | bytes 1048576 | tf_op jit(solution)/shard_map/pallas_call | solution.py:474
  47.4 0.0 all-to-all-done.w_ref.refs_0_
  47.4 1.0 %copy-done = bf16[8,104,512]{2,1,0:T(8,128)(2,1)} copy-done((bf16[8,104,512]{2,1,0:T(8,128)(2,1)}, bf16[8,104,512]{2,1,0:T(8,128)(2,1)S(1)}, u32[]{:S(2)}) %copy-start) | copy-done | bytes 851992
  48.4 7.8 %shard_map.93 = (bf16[72,1024]{1,0:T(8,128)(2,1)S(1)}, f32[2,1024]{1,0:T(2,128)S(1)}) custom-call(s32[4]{0:T(128)S(1)} %copy-done.5, bf16[8,104,512]{2,1,0:T(8,128)(2,1)} %copy-done, bf16[1024,4096]{1,0:T(8,128)(2,1)} %shard_map.92.normed_hbm, f32[4,32,2]{2,1,0:T(8,128)S(1)} %copy-done.3), custom_call_target="tpu_custom_call" | custom-call | flops 2147483648 | bytes 8388608 | tf_op jit(solution)/shard_map/pallas_call | solution.py:387
  56.2 0.0 collective-permute-done.2.refs_2_.rest_2_
  56.3 1.5 %collective-permute-start.4 = (bf16[72,1024]{1,0:T(8,128)(2,1)S(1)}, bf16[72,1024]{1,0:T(8,128)(2,1)S(1)}, u32[]{:S(2)}, u32[]{:S(2)}) collective-permute-start(bf16[72,1024]{1,0:T(8,128)(2,1)S(1)} %shard_map.96.rest_4_), channel_id=1, source_target_pairs={{0,4},{4,0},{8,12},{12,8},{1,5},{5,1},{9,13},{13,9},{2,6},{6,2},{1... | collective-permute-start | bytes 442376 | tf_op jit(solution)/shard_map/ppermute | solution.py:404
  57.8 2.4 %collective-permute-start.5 = (bf16[72,1024]{1,0:T(8,128)(2,1)S(1)}, bf16[72,1024]{1,0:T(8,128)(2,1)S(1)}, u32[]{:S(2)}, u32[]{:S(2)}) collective-permute-start(bf16[72,1024]{1,0:T(8,128)(2,1)S(1)} %shard_map.96.rest_4_), channel_id=1, source_target_pairs={{0,8},{4,12},{8,0},{12,4},{1,9},{5,13},{9,1},{13,5},{2,10},{6,14},... | collective-permute-start | bytes 442376 | tf_op jit(solution)/shard_map/ppermute | solution.py:404
  60.2 0.5 collective-permute-start.6
  60.7 1.2 %copy-done.1 = bf16[8,104,512]{2,1,0:T(8,128)(2,1)S(1)} copy-done((bf16[8,104,512]{2,1,0:T(8,128)(2,1)S(1)}, bf16[8,104,512]{2,1,0:T(8,128)(2,1)}, u32[]{:S(2)}) %copy-start.1) | copy-done | bytes 851992
  61.9 0.7 shard_map.94.own_ref
  62.6 0.6 collective-permute-start
  63.2 3.1 %collective-permute-done.other_ref = f32[16,128]{1,0:T(8,128)S(1)} collective-permute-done((f32[16,128]{1,0:T(8,128)S(1)}, f32[16,128]{1,0:T(8,128)S(1)}, u32[]{:S(2)}, u32[]{:S(2)}) %collective-permute-start) | collective-permute-done | bytes 8224 | tf_op jit(solution)/shard_map/ppermute | solution.py:404
  66.3 5.0 %collective-permute-done.5.rest_6_ = bf16[72,1024]{1,0:T(8,128)(2,1)S(1)} collective-permute-done((bf16[72,1024]{1,0:T(8,128)(2,1)S(1)}, bf16[72,1024]{1,0:T(8,128)(2,1)S(1)}, u32[]{:S(2)}, u32[]{:S(2)}) %collective-permute-start.5) | collective-permute-done | bytes 147488 | tf_op jit(solution)/shard_map/ppermute | solution.py:404
  71.3 8.2 %shard_map.97 = f32[2,16,16,128]{3,2,1,0:T(8,128)S(1)} custom-call(s32[4]{0:T(128)S(1)} %copy-done.5, f32[2,1024]{1,0:T(2,128)S(1)} %get-tuple-element.9.vo_ref, f32[16,128]{1,0:T(8,128)S(1)} %shard_map.94.own_ref, f32[16,128]{1,0:T(8,128)S(1)} %collective-permute-done.other_ref, bf16[9,256,128]{2,1,0:T(8,128)(2,1)S(1)} %copy-done.2, ...), custom_call_target="tpu_custom_call" | custom-call | tf_op jit(solution)/shard_map/pallas_call | solution.py:387
  79.5 13.3 %all_to_all.10 = f32[32,16,128]{2,1,0:T(8,128)S(1)} all-to-all(f32[32,16,128]{2,1,0:T(8,128)S(1)} %bitcast.12), channel_id=1, replica_groups=mesh['groups'=2,'line'=4,'pair'=2,'tensor'=2] {'groups','line','pair','t..., dimensions={0} | all-to-all | bytes 524288 | tf_op jit(solution)/shard_map/all_to_all | solution.py:536
  92.9 1.1 %shard_map.98 = f32[1,512]{1,0:T(1,128)} custom-call(f32[2,4,4,16,128]{4,3,2,1,0:T(8,128)S(1)} %bitcast.11, s32[1,512]{1,0:T(1,128)S(1)} %bitcast.15, s32[1,512]{1,0:T(1,128)S(1)} %copy-done.6), custom_call_target="tpu_custom_call" | custom-call | tf_op jit(solution)/shard_map/pallas_call | solution.py:544
  (16 shorter events, 0.0 us)
Async XLA Ops:
  4.8 42.6 %all-to-all-start = ((bf16[8,104,512]{2,1,0:T(8,128)(2,1)}), bf16[8,104,512]{2,1,0:T(8,128)(2,1)S(1)}, u32[]{:S(2)}, u32[]{:S(2)}) async-start(bf16[8,104,512]{2,1,0:T(8,128)(2,1)} %shard_map.91.after_ref), calls=%async_computation | async-start | bytes 1703936 | tf_op jit(solution)/shard_map/all_to_all | solution.py:453
  14.9 21.5 %collective-permute-start.1 = (bf16[9,256,128]{2,1,0:T(8,128)(2,1)}, bf16[9,256,128]{2,1,0:T(8,128)(2,1)S(1)}, u32[]{:S(2)}, u32[]{:S(2)}) collective-permute-start(bf16[9,256,128]{2,1,0:T(8,128)(2,1)} %get-tuple-element.10.rest_0_), channel_id=1, source_target_pairs={{0,2},{2,0},{16,18},{18,16},{1,3},{3,1},{17,19},{19,17},{4,6},{6,4... | collective-permute-start | bytes 1769480 | tf_op jit(solution)/shard_map/ppermute | solution.py:404
  17.0 39.2 %collective-permute-start.2 = (bf16[9,256,128]{2,1,0:T(8,128)(2,1)}, bf16[9,256,128]{2,1,0:T(8,128)(2,1)S(1)}, u32[]{:S(2)}, u32[]{:S(2)}) collective-permute-start(bf16[9,256,128]{2,1,0:T(8,128)(2,1)} %get-tuple-element.10.rest_0_), channel_id=1, source_target_pairs={{0,16},{2,18},{16,0},{18,2},{1,17},{3,19},{17,1},{19,3},{4,20},{6,... | collective-permute-start | bytes 1769480 | tf_op jit(solution)/shard_map/ppermute | solution.py:404
  36.4 26.7 %collective-permute-start.3 = (bf16[9,256,128]{2,1,0:T(8,128)(2,1)S(1)}, bf16[9,256,128]{2,1,0:T(8,128)(2,1)S(1)}, u32[]{:S(2)}, u32[]{:S(2)}) collective-permute-start(bf16[9,256,128]{2,1,0:T(8,128)(2,1)S(1)} %collective-permute-done.1.refs_1_.rest_1_), channel_id=1, source_target_pairs={{0,16},{2,18},{16,0},{18,2},{1,17},{3,19},{17,1},{19,3},{4,20},{6,... | collective-permute-start | bytes 1769480 | tf_op jit(solution)/shard_map/ppermute | solution.py:404
  38.0 10.4 %copy-start.3 = (f32[4,32,2]{2,1,0:T(8,128)S(1)}, f32[4,32,2]{2,1,0:T(8,128)}, u32[]{:S(2)}) copy-start(f32[4,32,2]{2,1,0:T(8,128)} %constant.17.clone.turn_hbm) | copy-start | bytes 3076
  38.0 10.4 %copy-start.5 = (s32[4]{0:T(128)S(1)}, s32[4]{0:T(128)}, u32[]{:S(2)}) copy-start(s32[4]{0:T(128)} %pad_add_fusion.place_ref) | copy-start | bytes 52
  47.4 24.0 %copy-start.2 = (bf16[9,256,128]{2,1,0:T(8,128)(2,1)S(1)}, bf16[9,256,128]{2,1,0:T(8,128)(2,1)}, u32[]{:S(2)}) copy-start(bf16[9,256,128]{2,1,0:T(8,128)(2,1)} %get-tuple-element.10.rest_0_) | copy-start | bytes 1769476
  47.4 45.5 %copy-start.4 = (s32[512,1]{0,1:T(1,128)S(1)}, s32[512,1]{0,1:T(1,128)}, u32[]{:S(2)}) copy-start(s32[512,1]{0,1:T(1,128)} %param.11) | copy-start | bytes 6148
  47.4 45.5 %copy-start.6 = (s32[1,512]{1,0:T(1,128)S(1)}, s32[1,512]{1,0:T(1,128)}, u32[]{:S(2)}) copy-start(s32[1,512]{1,0:T(1,128)} %get-tuple-element.12.slot_ref) | copy-start | bytes 6148
  47.4 1.0 %copy-start = (bf16[8,104,512]{2,1,0:T(8,128)(2,1)}, bf16[8,104,512]{2,1,0:T(8,128)(2,1)S(1)}, u32[]{:S(2)}) copy-start(bf16[8,104,512]{2,1,0:T(8,128)(2,1)S(1)} %all-to-all-done.w_ref.refs_0_) | copy-start | bytes 2555908
  56.3 10.1 %collective-permute-start.4 = (bf16[72,1024]{1,0:T(8,128)(2,1)S(1)}, bf16[72,1024]{1,0:T(8,128)(2,1)S(1)}, u32[]{:S(2)}, u32[]{:S(2)}) collective-permute-start(bf16[72,1024]{1,0:T(8,128)(2,1)S(1)} %shard_map.96.rest_4_), channel_id=1, source_target_pairs={{0,4},{4,0},{8,12},{12,8},{1,5},{5,1},{9,13},{13,9},{2,6},{6,2},{1... | collective-permute-start | bytes 442376 | tf_op jit(solution)/shard_map/ppermute | solution.py:404
  57.8 13.6 %collective-permute-start.5 = (bf16[72,1024]{1,0:T(8,128)(2,1)S(1)}, bf16[72,1024]{1,0:T(8,128)(2,1)S(1)}, u32[]{:S(2)}, u32[]{:S(2)}) collective-permute-start(bf16[72,1024]{1,0:T(8,128)(2,1)S(1)} %shard_map.96.rest_4_), channel_id=1, source_target_pairs={{0,8},{4,12},{8,0},{12,4},{1,9},{5,13},{9,1},{13,5},{2,10},{6,14},... | collective-permute-start | bytes 442376 | tf_op jit(solution)/shard_map/ppermute | solution.py:404
  60.2 11.1 %collective-permute-start.6 = (bf16[72,1024]{1,0:T(8,128)(2,1)S(1)}, bf16[72,1024]{1,0:T(8,128)(2,1)S(1)}, u32[]{:S(2)}, u32[]{:S(2)}) collective-permute-start(bf16[72,1024]{1,0:T(8,128)(2,1)S(1)} %shard_map.96.rest_4_), channel_id=1, source_target_pairs={{0,12},{4,8},{8,4},{12,0},{1,13},{5,9},{9,5},{13,1},{2,14},{6,10},... | collective-permute-start | bytes 442376 | tf_op jit(solution)/shard_map/ppermute | solution.py:404
  60.7 1.2 %copy-start.1 = (bf16[8,104,512]{2,1,0:T(8,128)(2,1)S(1)}, bf16[8,104,512]{2,1,0:T(8,128)(2,1)}, u32[]{:S(2)}) copy-start(bf16[8,104,512]{2,1,0:T(8,128)(2,1)} %copy-done) | copy-start | bytes 2555908
  62.6 3.7 %collective-permute-start = (f32[16,128]{1,0:T(8,128)S(1)}, f32[16,128]{1,0:T(8,128)S(1)}, u32[]{:S(2)}, u32[]{:S(2)}) collective-permute-start(f32[16,128]{1,0:T(8,128)S(1)} %shard_map.94.own_ref), channel_id=1, source_target_pairs={{0,16},{2,18},{16,0},{18,2},{1,17},{3,19},{17,1},{19,3},{4,20},{6,... | collective-permute-start | bytes 24584 | tf_op jit(solution)/shard_map/ppermute | solution.py:404

commit v10 on v9

--- a/solution.py
+++ b/solution.py
@@ -56,7 +56,7 @@
 
 def pack_weights(plan, place_ref, wq_hbm, wkv_hbm, ws_hbm, board_hbm, ids_hbm, *rest):
     out_ref, wq, wkv, ws_ref, board_ref, ids_ref, pick, sems = rest
-    group = place_ref[GROUP]
+    group = place_ref[0]
     rows, half_cols = plan.rows, wq.shape[1]
     columns_here = pl.ds(pl.multiple_of(group * half_cols, HD), half_cols)
     copies = (
@@ -129,72 +129,74 @@
         out_ref[peer] = jnp.where(r == plan.list_at, lists[peer // plan.pair], mine).astype(BF16)
 
 
-def normalize(table_ref, gain_ref, after_ref, out_ref, gain):
-    @pl.when(pl.program_id(0) == 0)
+def normalize(table_ref, gain_ref, after_ref, *refs):
+    *outs, gain, held, sems = refs
+    here = pl.program_id(0)
+
+    @pl.when(here == 0)
     def _():
         rows = gain_ref[...].astype(F32)
         gain[...] = jnp.concatenate([rows[r : r + 1] for r in range(rows.shape[0])], axis=1)
 
-    half = table_ref.shape[0] // 2
-    for at in (slice(0, half), slice(half, 2 * half)):
-        raw = table_ref[at].astype(F32)
-        inverse = lax.rsqrt(jnp.mean(raw * raw, axis=-1, keepdims=True) + EPS)
-        out_ref[at] = (raw * inverse * gain[...]).astype(BF16)
-
-
-def project(plan, place_ref, w_ref, normed_hbm, turn_hbm, q_ref, vo_ref, table, turns, sems, turn_sem):
-    moves = normed_hbm.shape[0]
-    steps = sems.shape[0]
-    block = moves // steps
-    piece = math.gcd(block, 32)
-
-    def copy(start, rows, step):
-        at = pl.ds(start, rows)
-        return pltpu.make_async_copy(normed_hbm.at[at], table.at[at], sems.at[step])
-
-    turn_copy = pltpu.make_async_copy(turn_hbm.at[place_ref[LINE]], turns, turn_sem)
-    turn_copy.start()
-    for start in range(0, moves, piece):
-        copy(start, piece, start // block).start()
-    turn_copy.wait()
-
+    def copy(step):
+        return pltpu.make_async_copy(held.at[step % 2], outs[step], sems.at[step % 2])
+
+    def one(step):
+        if step >= 2:
+            copy(step - 2).wait()
+        half = table_ref.shape[0] // 2
+        for at in (slice(0, half), slice(half, 2 * half)):
+            raw = table_ref[at].astype(F32)
+            inverse = lax.rsqrt(jnp.mean(raw * raw, axis=-1, keepdims=True) + EPS)
+            held[step % 2, at] = (raw * inverse * gain[...]).astype(BF16)
+        copy(step).start()
+        if step == len(outs) - 1:
+            for last in range(max(0, step - 1), step + 1):
+                copy(last).wait()
+
+    for step in range(len(outs)):
+        pl.when(here == step)(functools.partial(one, step))
+
+
+def project(plan, at, place_ref, w_ref, normed_ref, turn_hbm, *refs):
+    q_ref, vo_ref, turns, turn_sem = refs[-4:]
+    copy = pltpu.make_async_copy(turn_hbm.at[place_ref[LINE]], turns, turn_sem)
+    copy.start()
+    if len(w_ref.shape) == 3:
+        depth = w_ref.shape[2]
+        total = None
+        for s in range(w_ref.shape[0]):
+            term = matmul(w_ref[s], normed_ref[:, s * depth : (s + 1) * depth], NT)
+            total = term if total is None else total + term
+    else:
+        total = matmul(w_ref[...], normed_ref[...], NT)
+    copy.wait()
     half, k_half = plan.q_rows // 2, plan.k_rows // 2
     cosine, sine = turns[:, 0:1], turns[:, 1:2]
     cos_k, sin_k = cosine[:k_half], sine[:k_half]
-    for step in range(steps):
-        copy(step * block, block, step).wait()
-        at = slice(step * block, (step + 1) * block)
-        if len(w_ref.shape) == 3:
-            depth = w_ref.shape[2]
-            total = None
-            for s in range(w_ref.shape[0]):
-                term = matmul(w_ref[s], table[at, s * depth : (s + 1) * depth], NT)
-                total = term if total is None else total + term
-        else:
-            total = matmul(w_ref[...], table[at, :], NT)
-        first, second = total[:half], total[half : 2 * half]
-        f_first = (first * cosine - second * sine).astype(BF16).astype(F32)
-        f_second = (second * cosine + first * sine).astype(BF16).astype(F32)
-        first, second = total[plan.q_rows : plan.q_rows + k_half], total[plan.q_rows + k_half : plan.fold_at]
-        k_first = (first * cos_k - second * sin_k).astype(BF16).astype(F32)
-        k_second = (second * cos_k + first * sin_k).astype(BF16).astype(F32)
-        logits, tails = [], []
-        for h in range(plan.mine):
-            own = slice(h * k_half, (h + 1) * k_half)
-            logit = jnp.sum(f_first[own] * k_first + f_second[own] * k_second, axis=0, keepdims=True)
-            logits.append(logit.astype(BF16).astype(F32))
-            tails.append(logit - logits[-1])
-        pad = plan.line_rows - plan.q_rows - 2 * plan.mine
-        pieces = [f_first, f_second, *logits, *tails]
-        if pad:
-            pieces.append(jnp.zeros((pad, block), F32))
-        out = jnp.concatenate(pieces, axis=0).astype(BF16)
-        if plan.direct:
-            q_ref[:, at] = out
-        else:
-            for line in range(plan.line):
-                q_ref[line, :, at] = out
-        vo_ref[:, at] = total[plan.fold_at : plan.list_at]
+    first, second = total[:half], total[half : 2 * half]
+    f_first = (first * cosine - second * sine).astype(BF16).astype(F32)
+    f_second = (second * cosine + first * sine).astype(BF16).astype(F32)
+    first, second = total[plan.q_rows : plan.q_rows + k_half], total[plan.q_rows + k_half : plan.fold_at]
+    k_first = (first * cos_k - second * sin_k).astype(BF16).astype(F32)
+    k_second = (second * cos_k + first * sin_k).astype(BF16).astype(F32)
+    logits, tails = [], []
+    for h in range(plan.mine):
+        own = slice(h * k_half, (h + 1) * k_half)
+        logit = jnp.sum(f_first[own] * k_first + f_second[own] * k_second, axis=0, keepdims=True)
+        logits.append(logit.astype(BF16).astype(F32))
+        tails.append(logit - logits[-1])
+    pad = plan.line_rows - plan.q_rows - 2 * plan.mine
+    pieces = [f_first, f_second, *logits, *tails]
+    if pad:
+        pieces.append(jnp.zeros((pad, total.shape[1]), F32))
+    out = jnp.concatenate(pieces, axis=0).astype(BF16)
+    if plan.direct:
+        q_ref[:, at] = out
+    else:
+        for line in range(plan.line):
+            q_ref[line, :, at] = out
+    vo_ref[:, at] = total[plan.fold_at : plan.list_at]
 
 
 def tied(x, *others):
@@ -382,7 +384,7 @@
     return pl.BlockSpec(memory_space=pl.ANY)
 
 
-def local_call(kernel, place, args, outs, scratch=(), mib=40, copied=(), flops=0, nbytes=0):
+def local_call(kernel, place, args, outs, scratch=(), mib=40, copied=(), flops=0, nbytes=0, aliases=None):
     vmem = pl.BlockSpec(memory_space=pltpu.VMEM)
     return pl.pallas_call(
         kernel,
@@ -391,6 +393,7 @@
         + [untouched() if at in copied else vmem for at in range(len(args))],
         out_specs=jax.tree.map(lambda x: vmem, outs),
         scratch_shapes=scratch,
+        input_output_aliases=aliases or {},
         compiler_params=limits(mib),
         cost_estimate=cost(flops, nbytes),
     )(place, *args)
@@ -435,7 +438,7 @@
     half_cols = w_query.shape[1] // groups
     packed = local_call(
         functools.partial(pack_weights, plan),
-        place,
+        group_at.reshape(1),
         (w_query, w_keyval, ws, board_row, move_ids.reshape(1, row_count)),
         shape((plan.peers, plan.rows, depth), BF16),
         [
@@ -471,17 +474,22 @@
     across = swap(payload, slab_axes, plan.slab, 2)
 
     block = min(moves, 256)
+    steps = moves // block
     normed = pl.pallas_call(
         normalize,
-        out_shape=shape((moves, width), BF16),
-        grid=(moves // block,),
+        out_shape=[shape((block, width), BF16)] * steps,
+        grid=(steps,),
         in_specs=[
             pl.BlockSpec((block, width), lambda i: (i, 0)),
             pl.BlockSpec((width // HD, HD), lambda i: (0, 0)),
             untouched(),
         ],
-        out_specs=pl.BlockSpec((block, width), lambda i: (i, 0)),
-        scratch_shapes=[pltpu.VMEM((1, width), F32)],
+        out_specs=[untouched()] * steps,
+        scratch_shapes=[
+            pltpu.VMEM((1, width), F32),
+            pltpu.VMEM((2, block, width), BF16),
+            pltpu.SemaphoreType.DMA((2,)),
+        ],
         compiler_params=limits(58),
         cost_estimate=cost(moves * width, moves * width // 4),
     )(move_table, norm_gain.reshape(width // HD, HD), packed)
@@ -489,23 +497,24 @@
     turns = np.tile(turns, (1, plan.mine, 1, 1)).reshape(line, plan.mine * plan.pairs, 2)
     flat = weights.transpose(1, 0, 2).reshape(plan.rows, width) if depth % HD else weights
     sent = (plan.line_rows, moves)
-    queries, own_values = local_call(
-        functools.partial(project, plan),
-        place,
-        (flat, normed, jnp.asarray(turns)),
-        (shape(sent if plan.direct else (line, *sent), BF16), shape((plan.mine, moves), F32)),
-        [
-            pltpu.VMEM((moves, width), BF16),
-            pltpu.VMEM(turns.shape[1:], F32),
-            pltpu.SemaphoreType.DMA((4,)),
-            pltpu.SemaphoreType.DMA,
-        ],
-        53,
-        (1, 2),
-        2 * moves * width * 256,
-        2 * moves * width,
-    )
+    outs = (shape(sent if plan.direct else (line, *sent), BF16), shape((plan.mine, moves), F32))
+    filled = ()
+    for step in range(steps):
+        filled = local_call(
+            functools.partial(project, plan, slice(step * block, (step + 1) * block)),
+            place,
+            (flat, normed[step], jnp.asarray(turns), *filled),
+            outs,
+            [pltpu.VMEM(turns.shape[1:], F32), pltpu.SemaphoreType.DMA],
+            16,
+            (2,),
+            2 * block * width * 1024,
+            block * width,
+            {4: 0, 5: 1} if filled else None,
+        )
+    queries, own_values = filled
     queries = tied(queries, beside, across)
+    beside = tied(beside, own_values)
     if plan.direct:
         queries = [queries] + [swap(queries, "line", line, step) for step in range(1, line)]
     else:

time: 94.3 us -> 79.3 us (0.84)
  waiting for transfers between devices: 26.1 us -> 12.1 us
  Pallas kernels: 34.3 us -> 31.7 us
  blocking collectives: 13.3 us -> 14.9 us
    ppermute x7, waiting for transfers between devices: 26.1 us -> 7.13 us  [swap(): return lax.ppermute(x, names, [(at, at ^ step) for at in range(size)])]
    all_to_all x1, waiting for transfers between devices: 0.01 us -> 5.01 us  [per_device(): lax.all_to_all(packed, ('line', 'pair'), split_axis=0, concat_axis=0, til...]
    pallas_call x5 -> x8, Pallas kernels: 23.8 us -> 21.2 us  [local_call(): pl.pallas_call(kernel, out_shape=outs, in_specs=[pl.BlockSpec(memory_spac...]
    all_to_all x1, blocking collectives: 13.3 us -> 14.9 us  [per_device(): lax.all_to_all(parts.reshape(groups * back, plan.share, plan.slots), ('gr...]
    unnamed x14 -> x18, local copies, waits for them, and re-layouts: 2.15 us -> 1.98 us
  transfers between devices with their start and end apart: 8 -> 8, of which waited for: 3 -> 3; matrix products, arithmetic and copies ran while one was open for 0% -> 1% of each run, Pallas kernels for 22% -> 24%
where the time goes in v10:
time: 79.3 us; the launch traced here: 78.9 us
  Pallas kernels  31.7 us (40%)
  starting transfers between devices  17.4 us (22%)
  blocking collectives  14.9 us (19%)
  waiting for transfers between devices  12.1 us (15%)
  local copies, waits for them, and re-layouts  1.98 us (2%)
    pallas_call x8, Pallas kernels, local_call(): pl.pallas_call(kernel, out_shape=outs, in_specs=[pl.BlockSpec(memory_spac...  21.2 us
    all_to_all x1, blocking collectives, per_device(): lax.all_to_all(parts.reshape(groups * back, plan.share, plan.slots), ('gr...  14.9 us
    ppermute x7, starting transfers between devices, swap(): return lax.ppermute(x, names, [(at, at ^ step) for at in range(size)])  10.1 us
    pallas_call x1, Pallas kernels, per_device(): pl.pallas_call(normalize, out_shape=[shape((block, width), BF16)] * steps...  9.47 us
    all_to_all x1, starting transfers between devices, per_device(): lax.all_to_all(packed, ('line', 'pair'), split_axis=0, concat_axis=0, til...  7.27 us
    ppermute x7, waiting for transfers between devices, swap(): return lax.ppermute(x, names, [(at, at ^ step) for at in range(size)])  7.13 us
    all_to_all x1, waiting for transfers between devices, per_device(): lax.all_to_all(packed, ('line', 'pair'), split_axis=0, concat_axis=0, til...  5.01 us
    unnamed x18, local copies, waits for them, and re-layouts  1.98 us
  transfers between devices with their start and end apart: 8, of which 3 were waited for; matrix products, arithmetic and copies ran while one was open for 1% of the time, Pallas kernels for 24%

profile of v10, /device:TPU:0, one launch (start us, length us, event | category | flops | bytes accessed | tf_op | source)
XLA Modules:
  0.0 78.9 jit_solution(7488802645977019695)
XLA Ops:
  0.0 3.5 %shard_map.91.after_ref = bf16[8,104,512]{2,1,0:T(8,128)(2,1)} custom-call(s32[1]{0:T(128)} %bitcast.place_ref, bf16[512,1024]{1,0:T(8,128)(2,1)} %wq_hbm.1, bf16[512,256]{1,0:T(8,128)(2,1)} %wkv_hbm.1, bf16[8,128]{1,0:T(8,128)(2,1)} %bitcast.17, s32[1,512]{1,0:T(1,128)} %bitcast.13, s32[1,512]{1,0:T(1,128)} %bitcast.19), custom_call_target="tpu_custom_call" | custom-call | tf_op jit(solution)/shard_map/pallas_call | solution.py:389
  3.5 7.3 %all-to-all-start = ((bf16[8,104,512]{2,1,0:T(8,128)(2,1)}), bf16[8,104,512]{2,1,0:T(8,128)(2,1)S(1)}, u32[]{:S(2)}, u32[]{:S(2)}) async-start(bf16[8,104,512]{2,1,0:T(8,128)(2,1)} %shard_map.91.after_ref), calls=%async_computation | async-start | bytes 1703936 | tf_op jit(solution)/shard_map/all_to_all | solution.py:456
  10.8 0.7 pad_add_fusion.place_ref
  11.5 2.9 %shard_map.98 = (bf16[9,256,128]{2,1,0:T(8,128)(2,1)}, s32[1,512]{1,0:T(1,128)}) custom-call(s32[4]{0:T(128)} %pad_add_fusion.place_ref, bf16[8,256,256]{2,1,0:T(8,128)(2,1)} %prefix_hbm.1, bf16[8,128]{1,0:T(8,128)(2,1)} %bitcast.18, s32[1,512]{1,0:T(1,128)} %bitcast.14, bf16[8,104,512]{2,1,0:T(8,128)(2,1)} %shard_map.91.after_ref), custom_call_target="tpu_custom_call" | custom-call | tf_op jit(solution)/shard_map/pallas_call | solution.py:389
  14.3 2.1 %collective-permute-start.1 = (bf16[9,256,128]{2,1,0:T(8,128)(2,1)}, bf16[9,256,128]{2,1,0:T(8,128)(2,1)S(1)}, u32[]{:S(2)}, u32[]{:S(2)}) collective-permute-start(bf16[9,256,128]{2,1,0:T(8,128)(2,1)} %get-tuple-element.30.rest_0_), channel_id=1, source_target_pairs={{0,2},{2,0},{16,18},{18,16},{1,3},{3,1},{17,19},{19,17},{4,6},{6,4... | collective-permute-start | bytes 1769480 | tf_op jit(solution)/shard_map/ppermute | solution.py:407
  16.4 1.5 %collective-permute-start.2 = (bf16[9,256,128]{2,1,0:T(8,128)(2,1)}, bf16[9,256,128]{2,1,0:T(8,128)(2,1)S(1)}, u32[]{:S(2)}, u32[]{:S(2)}) collective-permute-start(bf16[9,256,128]{2,1,0:T(8,128)(2,1)} %get-tuple-element.30.rest_0_), channel_id=1, source_target_pairs={{0,16},{2,18},{16,0},{18,2},{1,17},{3,19},{17,1},{19,3},{4,20},{6,... | collective-permute-start | bytes 1769480 | tf_op jit(solution)/shard_map/ppermute | solution.py:407
  17.9 9.5 %shard_map.92 = (bf16[256,4096]{1,0:T(8,128)(2,1)}, bf16[256,4096]{1,0:T(8,128)(2,1)}, bf16[256,4096]{1,0:T(8,128)(2,1)}, bf16[256,4096]{1,0:T(8,128)(2,1)}) custom-call(bf16[1024,4096]{1,0:T(8,128)(2,1)} %table_ref.1, bf16[32,128]{1,0:T(8,128)(2,1)} %bitcast.16, bf16[8,104,512]{2,1,0:T(8,128)(2,1)} %shard_map.91.after_ref), custom_call_target="tpu_custom_call" | custom-call | flops 4194304 | bytes 1048576 | tf_op jit(solution)/shard_map/pallas_call | solution.py:478
  27.4 5.0 %all-to-all-done.w_ref.refs_0_ = bf16[8,104,512]{2,1,0:T(8,128)(2,1)S(1)} async-done(((bf16[8,104,512]{2,1,0:T(8,128)(2,1)}), bf16[8,104,512]{2,1,0:T(8,128)(2,1)S(1)}, u32[]{:S(2)}, u32[]{:S(2)}) %all-to-all-start) | async-done | bytes 852000 | tf_op jit(solution)/shard_map/all_to_all | solution.py:456
  32.4 1.6 %copy-done.7 = bf16[256,4096]{1,0:T(8,128)(2,1)S(1)} copy-done((bf16[256,4096]{1,0:T(8,128)(2,1)S(1)}, bf16[256,4096]{1,0:T(8,128)(2,1)}, u32[]{:S(2)}) %copy-start.7) | copy-done | bytes 2097176
  34.0 1.5 %shard_map.93 = (bf16[72,1024]{1,0:T(8,128)(2,1)S(1)}, f32[2,1024]{1,0:T(2,128)S(1)}) custom-call(s32[4]{0:T(128)S(1)} %copy-done.2, bf16[8,104,512]{2,1,0:T(8,128)(2,1)S(1)} %all-to-all-done.w_ref.refs_0_, bf16[256,4096]{1,0:T(8,128)(2,1)S(1)} %copy-done.7, f32[4,32,2]{2,1,0:T(8,128)S(1)} %copy-done.8), custom_call_target="tpu_custom_call" | custom-call | flops 2147483648 | bytes 1048576 | tf_op jit(solution)/shard_map/pallas_call | solution.py:389
  35.5 0.1 copy-done.6
  35.6 1.5 %shard_map.94 = (bf16[72,1024]{1,0:T(8,128)(2,1)S(1)}, f32[2,1024]{1,0:T(2,128)S(1)}) custom-call(s32[4]{0:T(128)S(1)} %copy-done.2, bf16[8,104,512]{2,1,0:T(8,128)(2,1)S(1)} %all-to-all-done.w_ref.refs_0_, bf16[256,4096]{1,0:T(8,128)(2,1)S(1)} %copy-done.6, f32[4,32,2]{2,1,0:T(8,128)S(1)} %copy-done.8, ...), custom_call_target="tpu_custom_call", output_to_operand_aliasing={{0}: (4, {}), {1}: (5, {})} | custom-call | flops 2147483648 | bytes 1048576 | tf_op jit(solution)/shard_map/pallas_call | solution.py:389
  37.2 1.5 %shard_map.95 = (bf16[72,1024]{1,0:T(8,128)(2,1)S(1)}, f32[2,1024]{1,0:T(2,128)S(1)}) custom-call(s32[4]{0:T(128)S(1)} %copy-done.2, bf16[8,104,512]{2,1,0:T(8,128)(2,1)S(1)} %all-to-all-done.w_ref.refs_0_, bf16[256,4096]{1,0:T(8,128)(2,1)S(1)} %copy-done.5, f32[4,32,2]{2,1,0:T(8,128)S(1)} %copy-done.8, ...), custom_call_target="tpu_custom_call", output_to_operand_aliasing={{0}: (4, {}), {1}: (5, {})} | custom-call | flops 2147483648 | bytes 1048576 | tf_op jit(solution)/shard_map/pallas_call | solution.py:389
  38.8 1.5 %shard_map.96 = (bf16[72,1024]{1,0:T(8,128)(2,1)S(1)}, f32[2,1024]{1,0:T(2,128)S(1)}) custom-call(s32[4]{0:T(128)S(1)} %copy-done.2, bf16[8,104,512]{2,1,0:T(8,128)(2,1)S(1)} %all-to-all-done.w_ref.refs_0_, bf16[256,4096]{1,0:T(8,128)(2,1)S(1)} %copy-done.4, f32[4,32,2]{2,1,0:T(8,128)S(1)} %copy-done.8, ...), custom_call_target="tpu_custom_call", output_to_operand_aliasing={{0}: (4, {}), {1}: (5, {})} | custom-call | flops 2147483648 | bytes 1048576 | tf_op jit(solution)/shard_map/pallas_call | solution.py:389
  40.3 1.6 %collective-permute-start.3 = (bf16[9,256,128]{2,1,0:T(8,128)(2,1)S(1)}, bf16[9,256,128]{2,1,0:T(8,128)(2,1)S(1)}, u32[]{:S(2)}, u32[]{:S(2)}) collective-permute-start(bf16[9,256,128]{2,1,0:T(8,128)(2,1)S(1)} %shard_map.99.rest_1_), channel_id=1, source_target_pairs={{0,16},{2,18},{16,0},{18,2},{1,17},{3,19},{17,1},{19,3},{4,20},{6,... | collective-permute-start | bytes 1769480 | tf_op jit(solution)/shard_map/ppermute | solution.py:407
  42.0 1.6 %collective-permute-start.5 = (bf16[72,1024]{1,0:T(8,128)(2,1)S(1)}, bf16[72,1024]{1,0:T(8,128)(2,1)S(1)}, u32[]{:S(2)}, u32[]{:S(2)}) collective-permute-start(bf16[72,1024]{1,0:T(8,128)(2,1)S(1)} %shard_map.100.rest_4_), channel_id=1, source_target_pairs={{0,8},{4,12},{8,0},{12,4},{1,9},{5,13},{9,1},{13,5},{2,10},{6,14},... | collective-permute-start | bytes 442376 | tf_op jit(solution)/shard_map/ppermute | solution.py:407
  43.6 2.7 %collective-permute-start.6 = (bf16[72,1024]{1,0:T(8,128)(2,1)S(1)}, bf16[72,1024]{1,0:T(8,128)(2,1)S(1)}, u32[]{:S(2)}, u32[]{:S(2)}) collective-permute-start(bf16[72,1024]{1,0:T(8,128)(2,1)S(1)} %shard_map.100.rest_4_), channel_id=1, source_target_pairs={{0,12},{4,8},{8,4},{12,0},{1,13},{5,9},{9,5},{13,1},{2,14},{6,10},... | collective-permute-start | bytes 442376 | tf_op jit(solution)/shard_map/ppermute | solution.py:407
  46.3 0.7 shard_map.97.own_ref
  47.1 0.6 collective-permute-start
  47.6 6.6 %collective-permute-done.other_ref = f32[16,128]{1,0:T(8,128)S(1)} collective-permute-done((f32[16,128]{1,0:T(8,128)S(1)}, f32[16,128]{1,0:T(8,128)S(1)}, u32[]{:S(2)}, u32[]{:S(2)}) %collective-permute-start) | collective-permute-done | bytes 8224 | tf_op jit(solution)/shard_map/ppermute | solution.py:407
  54.3 0.5 collective-permute-done.5.rest_6_
  54.8 8.2 %shard_map.101 = f32[2,16,16,128]{3,2,1,0:T(8,128)S(1)} custom-call(s32[4]{0:T(128)S(1)} %copy-done.2, f32[2,1024]{1,0:T(2,128)S(1)} %get-tuple-element.29.refs_1_.vo_ref, f32[16,128]{1,0:T(8,128)S(1)} %shard_map.97.own_ref, f32[16,128]{1,0:T(8,128)S(1)} %collective-permute-done.other_ref, bf16[9,256,128]{2,1,0:T(8,128)(2,1)S(1)} %copy-done, ...), custom_call_target="tpu_custom_call" | custom-call | tf_op jit(solution)/shard_map/pallas_call | solution.py:389
  63.0 14.9 %all_to_all.10 = f32[32,16,128]{2,1,0:T(8,128)S(1)} all-to-all(f32[32,16,128]{2,1,0:T(8,128)S(1)} %bitcast.12), channel_id=1, replica_groups=mesh['groups'=2,'line'=4,'pair'=2,'tensor'=2] {'groups','line','pair','t..., dimensions={0} | all-to-all | bytes 524288 | tf_op jit(solution)/shard_map/all_to_all | solution.py:545
  77.9 1.1 %shard_map.102 = f32[1,512]{1,0:T(1,128)} custom-call(f32[2,4,4,16,128]{4,3,2,1,0:T(8,128)S(1)} %bitcast.11, s32[1,512]{1,0:T(1,128)S(1)} %bitcast.15, s32[1,512]{1,0:T(1,128)S(1)} %copy-done.3), custom_call_target="tpu_custom_call" | custom-call | tf_op jit(solution)/shard_map/pallas_call | solution.py:553
  (24 shorter events, 0.4 us)
Async XLA Ops:
  3.5 28.9 %all-to-all-start = ((bf16[8,104,512]{2,1,0:T(8,128)(2,1)}), bf16[8,104,512]{2,1,0:T(8,128)(2,1)S(1)}, u32[]{:S(2)}, u32[]{:S(2)}) async-start(bf16[8,104,512]{2,1,0:T(8,128)(2,1)} %shard_map.91.after_ref), calls=%async_computation | async-start | bytes 1703936 | tf_op jit(solution)/shard_map/all_to_all | solution.py:456
  14.3 25.9 %collective-permute-start.1 = (bf16[9,256,128]{2,1,0:T(8,128)(2,1)}, bf16[9,256,128]{2,1,0:T(8,128)(2,1)S(1)}, u32[]{:S(2)}, u32[]{:S(2)}) collective-permute-start(bf16[9,256,128]{2,1,0:T(8,128)(2,1)} %get-tuple-element.30.rest_0_), channel_id=1, source_target_pairs={{0,2},{2,0},{16,18},{18,16},{1,3},{3,1},{17,19},{19,17},{4,6},{6,4... | collective-permute-start | bytes 1769480 | tf_op jit(solution)/shard_map/ppermute | solution.py:407
  16.4 23.9 %collective-permute-start.2 = (bf16[9,256,128]{2,1,0:T(8,128)(2,1)}, bf16[9,256,128]{2,1,0:T(8,128)(2,1)S(1)}, u32[]{:S(2)}, u32[]{:S(2)}) collective-permute-start(bf16[9,256,128]{2,1,0:T(8,128)(2,1)} %get-tuple-element.30.rest_0_), channel_id=1, source_target_pairs={{0,16},{2,18},{16,0},{18,2},{1,17},{3,19},{17,1},{19,3},{4,20},{6,... | collective-permute-start | bytes 1769480 | tf_op jit(solution)/shard_map/ppermute | solution.py:407
  17.9 14.5 %copy-start.2 = (s32[4]{0:T(128)S(1)}, s32[4]{0:T(128)}, u32[]{:S(2)}) copy-start(s32[4]{0:T(128)} %pad_add_fusion.place_ref) | copy-start | bytes 52
  17.9 14.5 %copy-start.8 = (f32[4,32,2]{2,1,0:T(8,128)S(1)}, f32[4,32,2]{2,1,0:T(8,128)}, u32[]{:S(2)}) copy-start(f32[4,32,2]{2,1,0:T(8,128)} %constant.17.clone.turn_hbm) | copy-start | bytes 3076
  32.4 1.6 %copy-start.7 = (bf16[256,4096]{1,0:T(8,128)(2,1)S(1)}, bf16[256,4096]{1,0:T(8,128)(2,1)}, u32[]{:S(2)}) copy-start(bf16[256,4096]{1,0:T(8,128)(2,1)} %get-tuple-element.22.normed_ref) | copy-start | bytes 6291460
  34.0 1.6 %copy-start.6 = (bf16[256,4096]{1,0:T(8,128)(2,1)S(1)}, bf16[256,4096]{1,0:T(8,128)(2,1)}, u32[]{:S(2)}) copy-start(bf16[256,4096]{1,0:T(8,128)(2,1)} %get-tuple-element.21.normed_ref) | copy-start | bytes 6291460
  35.6 1.6 %copy-start.5 = (bf16[256,4096]{1,0:T(8,128)(2,1)S(1)}, bf16[256,4096]{1,0:T(8,128)(2,1)}, u32[]{:S(2)}) copy-start(bf16[256,4096]{1,0:T(8,128)(2,1)} %get-tuple-element.20.normed_ref) | copy-start | bytes 6291460
  37.2 1.6 %copy-start.4 = (bf16[256,4096]{1,0:T(8,128)(2,1)S(1)}, bf16[256,4096]{1,0:T(8,128)(2,1)}, u32[]{:S(2)}) copy-start(bf16[256,4096]{1,0:T(8,128)(2,1)} %get-tuple-element.19.normed_ref) | copy-start | bytes 6291460
  40.3 14.5 %copy-start = (bf16[9,256,128]{2,1,0:T(8,128)(2,1)S(1)}, bf16[9,256,128]{2,1,0:T(8,128)(2,1)}, u32[]{:S(2)}) copy-start(bf16[9,256,128]{2,1,0:T(8,128)(2,1)} %get-tuple-element.30.rest_0_) | copy-start | bytes 1769476
  40.3 14.4 %collective-permute-start.3 = (bf16[9,256,128]{2,1,0:T(8,128)(2,1)S(1)}, bf16[9,256,128]{2,1,0:T(8,128)(2,1)S(1)}, u32[]{:S(2)}, u32[]{:S(2)}) collective-permute-start(bf16[9,256,128]{2,1,0:T(8,128)(2,1)S(1)} %shard_map.99.rest_1_), channel_id=1, source_target_pairs={{0,16},{2,18},{16,0},{18,2},{1,17},{3,19},{17,1},{19,3},{4,20},{6,... | collective-permute-start | bytes 1769480 | tf_op jit(solution)/shard_map/ppermute | solution.py:407
  41.9 12.4 %collective-permute-start.4 = (bf16[72,1024]{1,0:T(8,128)(2,1)S(1)}, bf16[72,1024]{1,0:T(8,128)(2,1)S(1)}, u32[]{:S(2)}, u32[]{:S(2)}) collective-permute-start(bf16[72,1024]{1,0:T(8,128)(2,1)S(1)} %shard_map.100.rest_4_), channel_id=1, source_target_pairs={{0,4},{4,0},{8,12},{12,8},{1,5},{5,1},{9,13},{13,9},{2,6},{6,2},{1... | collective-permute-start | bytes 442376 | tf_op jit(solution)/shard_map/ppermute | solution.py:407
  42.0 12.7 %collective-permute-start.5 = (bf16[72,1024]{1,0:T(8,128)(2,1)S(1)}, bf16[72,1024]{1,0:T(8,128)(2,1)S(1)}, u32[]{:S(2)}, u32[]{:S(2)}) collective-permute-start(bf16[72,1024]{1,0:T(8,128)(2,1)S(1)} %shard_map.100.rest_4_), channel_id=1, source_target_pairs={{0,8},{4,12},{8,0},{12,4},{1,9},{5,13},{9,1},{13,5},{2,10},{6,14},... | collective-permute-start | bytes 442376 | tf_op jit(solution)/shard_map/ppermute | solution.py:407
  43.6 11.2 %collective-permute-start.6 = (bf16[72,1024]{1,0:T(8,128)(2,1)S(1)}, bf16[72,1024]{1,0:T(8,128)(2,1)S(1)}, u32[]{:S(2)}, u32[]{:S(2)}) collective-permute-start(bf16[72,1024]{1,0:T(8,128)(2,1)S(1)} %shard_map.100.rest_4_), channel_id=1, source_target_pairs={{0,12},{4,8},{8,4},{12,0},{1,13},{5,9},{9,5},{13,1},{2,14},{6,10},... | collective-permute-start | bytes 442376 | tf_op jit(solution)/shard_map/ppermute | solution.py:407
  47.0 30.8 %copy-start.1 = (s32[512,1]{0,1:T(1,128)S(1)}, s32[512,1]{0,1:T(1,128)}, u32[]{:S(2)}) copy-start(s32[512,1]{0,1:T(1,128)} %param.11) | copy-start | bytes 6148
  47.1 30.8 %copy-start.3 = (s32[1,512]{1,0:T(1,128)S(1)}, s32[1,512]{1,0:T(1,128)}, u32[]{:S(2)}) copy-start(s32[1,512]{1,0:T(1,128)} %get-tuple-element.32.slot_ref) | copy-start | bytes 6148
  47.1 7.2 %collective-permute-start = (f32[16,128]{1,0:T(8,128)S(1)}, f32[16,128]{1,0:T(8,128)S(1)}, u32[]{:S(2)}, u32[]{:S(2)}) collective-permute-start(f32[16,128]{1,0:T(8,128)S(1)} %shard_map.97.own_ref), channel_id=1, source_target_pairs={{0,16},{2,18},{16,0},{18,2},{1,17},{3,19},{17,1},{19,3},{4,20},{6,... | collective-permute-start | bytes 24584 | tf_op jit(solution)/shard_map/ppermute | solution.py:407

commit v11 on v10

--- a/solution.py
+++ b/solution.py
@@ -108,17 +108,22 @@
     other = lax.broadcasted_iota(jnp.int32, (count, count), 1)
     ahead = jnp.where((board_col == board_row) & (other < own), 1.0, 0.0)
     rank = jnp.sum(ahead, axis=1, keepdims=True).astype(jnp.int32)
-    key = board_col * plan.capacity + rank
     move = ids_ref[...] + 1
-    parts = jnp.concatenate([(move // 64).astype(F32), (move % 64).astype(F32)], axis=0).astype(BF16)
-    span = plan.share * plan.capacity
+    boards, span = plan.line * plan.share, plan.share * plan.capacity
+    member = lax.broadcasted_iota(jnp.int32, (boards, count), 0) == board_row
+    parts = [jnp.where(member, part.astype(F32), 0.0) for part in (move // 64, move % 64)]
     lane = lax.broadcasted_iota(jnp.int32, (count, depth), 1)
-    lane_row = lax.broadcasted_iota(jnp.int32, (1, depth), 1)
+    ranked = jnp.where(rank == (lane % span) % plan.capacity, 1.0, 0.0).astype(BF16)
+    found = matmul(jnp.concatenate(parts, axis=0).astype(BF16), ranked)
+    lane = lax.broadcasted_iota(jnp.int32, (2 * boards, depth), 1)
+    row = lax.broadcasted_iota(jnp.int32, (2 * boards, depth), 0)
+    keep = (row // boards == lane // span) & (row % plan.share == (lane % span) // plan.capacity)
+    found = jnp.where(keep, found, 0.0)
     lists = []
     for line in range(plan.line):
-        place = jnp.where(lane < span, lane, lane - span) + line * span
-        found = matmul(parts, jnp.where(key == place, 1.0, 0.0).astype(BF16))
-        lists.append(jnp.where(lane_row < span, found[0:1], found[1:2]))
+        at = line * plan.share
+        both = found[at : at + plan.share] + found[boards + at : boards + at + plan.share]
+        lists.append(jnp.sum(both, axis=0, keepdims=True))
 
     for copy in copies[3:]:
         copy.wait()
@@ -158,10 +163,11 @@
         pl.when(here == step)(functools.partial(one, step))
 
 
-def project(plan, at, place_ref, w_ref, normed_ref, turn_hbm, *refs):
-    q_ref, vo_ref, turns, turn_sem = refs[-4:]
-    copy = pltpu.make_async_copy(turn_hbm.at[place_ref[LINE]], turns, turn_sem)
-    copy.start()
+def project(plan, at, mark, place_ref, w_ref, normed_ref, turn_ref, *refs):
+    if mark:
+        *refs, mark_ref = refs
+        mark_ref[...] = jnp.zeros_like(mark_ref)
+    q_ref, vo_ref = refs[-2:]
     if len(w_ref.shape) == 3:
         depth = w_ref.shape[2]
         total = None
@@ -170,7 +176,7 @@
             total = term if total is None else total + term
     else:
         total = matmul(w_ref[...], normed_ref[...], NT)
-    copy.wait()
+    turns = turn_ref[place_ref[LINE]]
     half, k_half = plan.q_rows // 2, plan.k_rows // 2
     cosine, sine = turns[:, 0:1], turns[:, 1:2]
     cos_k, sin_k = cosine[:k_half], sine[:k_half]
@@ -249,7 +255,7 @@
 
 
 def read_lists(plan, place_ref, *refs):
-    w_ref, out_ref = refs
+    w_ref, _, out_ref = refs
     share, capacity, peers = plan.share, plan.capacity, plan.peers
     span = share * capacity
     rows = jnp.concatenate([w_ref[s].astype(F32)[plan.list_at : plan.list_at + 1] for s in range(peers)], axis=0)
@@ -269,7 +275,34 @@
     out_ref[...] = jnp.sum(listed.reshape(share, peers, plan.slots), axis=1)
 
 
-def attend(plan, place_ref, vo_ref, own_ref, other_ref, *rest):
+def fold_columns(plan, here, block, board, boards, heads):
+    lanes = plan.mine * plan.slots
+    row = lax.broadcasted_iota(jnp.int32, (HD, lanes), 0) - board * (HD // boards)
+    head = here * plan.mine + lax.broadcasted_iota(jnp.int32, (HD, lanes), 1) // plan.slots
+    pick = jnp.where((row == head) | (row == head + heads), 1.0, 0.0).astype(BF16)
+    return matmul(block, pick)
+
+
+def prepare(plan, place_ref, own_ref, other_ref, *rest):
+    *prefix_refs, chosen_ref, fold_ref = rest
+    here = place_ref[SLAB]
+    boards, moves = chosen_ref.shape[0], chosen_ref.shape[1]
+    move_at = lax.broadcasted_iota(jnp.int32, (moves, plan.slots), 0) + 1
+
+    def step(board, carry):
+        for j in range(plan.slab):
+            place = ((here ^ j) % plan.pair) * boards + board
+            row = (own_ref, other_ref)[j // plan.pair][pl.ds(place, 1), :].astype(jnp.int32)
+            at = slice(j * plan.slots, (j + 1) * plan.slots)
+            chosen_ref[board, :, at] = jnp.where(move_at == row, 1.0, 0.0).astype(BF16)
+        for j, prefix_ref in enumerate(prefix_refs):
+            fold_ref[j, board] = fold_columns(plan, here, prefix_ref[boards], board, boards, plan.heads)
+        return carry
+
+    lax.fori_loop(0, boards, step, 0)
+
+
+def attend(plan, place_ref, vo_ref, own_ref, other_ref, chosen_ref, fold_ref, *rest):
     prefix_refs, rest = rest[: plan.slab], rest[plan.slab :]
     *q_refs, out_ref, table, extra, scores, taken_even, taken_odd = rest
     here = place_ref[SLAB]
@@ -298,12 +331,6 @@
     table[query_rows:] = extra[...].astype(BF16)
 
     scale = math.log2(math.e) / math.sqrt(HD)
-    move_at = lax.broadcasted_iota(jnp.int32, (moves, slots), 0) + 1
-    lanes = mine * slots
-    span = HD // boards
-    fold_row = lax.broadcasted_iota(jnp.int32, (HD, lanes), 0)
-    fold_head = here * mine + lax.broadcasted_iota(jnp.int32, (HD, lanes), 1) // slots
-
     def per_head(x, base):
         pieces = [x[base + h : base + h + 1] + x[base + mine + h : base + mine + h + 1] for h in range(mine)]
         return jnp.concatenate(pieces, axis=1)
@@ -313,19 +340,17 @@
         return (own_ref, other_ref)[j // plan.pair][pl.ds(place, 1), :].astype(jnp.int32)
 
     def gather(board, taken):
-        chosen = [
-            jnp.where(move_at == moves_of(j, board), 1.0, 0.0).astype(BF16) for j in range(plan.slab)
-        ]
-        taken[...] = matmul(table[...], jnp.concatenate(chosen, axis=1))
+        taken[...] = matmul(table[...], chosen_ref[board])
 
     def score_board(board, taken):
-        at = fold_row - board * span
-        fold_pick = jnp.where((at == fold_head) | (at == fold_head + heads), 1.0, 0.0).astype(BF16)
         for j in range(plan.slab):
             x = taken[:, j * slots : (j + 1) * slots]
             q = jnp.concatenate([x[h * HD : (h + 1) * HD].astype(BF16) for h in range(mine)], axis=1)
             logits = matmul(prefix_refs[j][board], q)
-            fold = matmul(prefix_refs[j][boards], fold_pick)
+            if j < plan.slab - 1:
+                fold = fold_ref[j, board]
+            else:
+                fold = fold_columns(plan, here, prefix_refs[j][boards], board, boards, heads)
             own_logit = per_head(x, query_rows)
             own_value = per_head(x, query_rows + 2 * mine)
             peak = jnp.maximum(jnp.max(logits, axis=0, keepdims=True), own_logit)
@@ -498,40 +523,58 @@
     flat = weights.transpose(1, 0, 2).reshape(plan.rows, width) if depth % HD else weights
     sent = (plan.line_rows, moves)
     outs = (shape(sent if plan.direct else (line, *sent), BF16), shape((plan.mine, moves), F32))
-    filled = ()
+    filled, ready = (), None
     for step in range(steps):
-        filled = local_call(
-            functools.partial(project, plan, slice(step * block, (step + 1) * block)),
+        made = local_call(
+            functools.partial(project, plan, slice(step * block, (step + 1) * block), step == 0),
             place,
             (flat, normed[step], jnp.asarray(turns), *filled),
-            outs,
-            [pltpu.VMEM(turns.shape[1:], F32), pltpu.SemaphoreType.DMA],
+            [*outs, shape((8, HD), F32)] if step == 0 else list(outs),
+            (),
             16,
-            (2,),
+            (),
             2 * block * width * 1024,
             block * width,
             {4: 0, 5: 1} if filled else None,
         )
+        filled = made[:2]
+        ready = made[2] if step == 0 else ready
     queries, own_values = filled
+    listed = local_call(
+        functools.partial(read_lists, plan),
+        place,
+        (weights, ready),
+        shape((plan.share, plan.slots), F32),
+        copied=(1,),
+    )
+    other = swap(listed, slab_axes, plan.slab, pair)
+    beside = tied(beside, other)
     queries = tied(queries, beside, across)
-    beside = tied(beside, own_values)
     if plan.direct:
         queries = [queries] + [swap(queries, "line", line, step) for step in range(1, line)]
     else:
         queries = lax.all_to_all(queries, "line", split_axis=0, concat_axis=0, tiled=True)
         queries = [queries.reshape(line * plan.line_rows, moves)]
-    listed = local_call(
-        functools.partial(read_lists, plan), place, (weights,), shape((plan.share, plan.slots), F32)
-    )
-    other = swap(listed, slab_axes, plan.slab, pair)
     diagonal = swap(beside, slab_axes, plan.slab, 2)
 
     query_rows = plan.mine * HD
     back = plan.peers * lax.axis_size("tensor")
+    chosen, folds = local_call(
+        functools.partial(prepare, plan),
+        place,
+        (listed, other, payload, beside, across),
+        (
+            shape((boards_here, moves, plan.slab * plan.slots), BF16),
+            shape((plan.slab - 1, boards_here, prefix_len, plan.mine * plan.slots), F32),
+        ),
+        mib=20,
+        flops=10**9,
+        nbytes=10**6,
+    )
     parts = local_call(
         functools.partial(attend, plan),
         place,
-        (own_values, listed, other, payload, beside, across, diagonal, *queries),
+        (own_values, listed, other, chosen, folds, payload, beside, across, diagonal, *queries),
         shape((groups, back, plan.share, plan.slots), F32),
         [
             pltpu.VMEM((query_rows + 16, moves), BF16),

time: 79.3 us -> 87.5 us (1.10)
  waiting for transfers between devices: 12.1 us -> 17.3 us
  Pallas kernels: 31.7 us -> 34.6 us
    ppermute x7, waiting for transfers between devices: 7.13 us -> 10.7 us  [swap(): return lax.ppermute(x, names, [(at, at ^ step) for at in range(size)])]
    pallas_call x8 -> x9, Pallas kernels: 21.2 us -> 24.1 us  [local_call(): pl.pallas_call(kernel, out_shape=outs, in_specs=[pl.BlockSpec(memory_spac...]
    all_to_all x1, waiting for transfers between devices: 5.01 us -> 6.6 us  [per_device(): lax.all_to_all(packed, ('line', 'pair'), split_axis=0, concat_axis=0, til...]
  transfers between devices with their start and end apart: 8 -> 8, of which waited for: 3 -> 4; matrix products, arithmetic and copies ran while one was open for 1% -> 1% of each run, Pallas kernels for 24% -> 26%
where the time goes in v11:
time: 87.5 us; the launch traced here: 87.2 us
  Pallas kernels  34.6 us (40%)
  starting transfers between devices  17.4 us (20%)
  waiting for transfers between devices  17.3 us (20%)
  blocking collectives  15 us (17%)
  local copies, waits for them, and re-layouts  2.09 us (2%)
    pallas_call x9, Pallas kernels, local_call(): pl.pallas_call(kernel, out_shape=outs, in_specs=[pl.BlockSpec(memory_spac...  24.1 us
    all_to_all x1, blocking collectives, per_device(): lax.all_to_all(parts.reshape(groups * back, plan.share, plan.slots), ('gr...  15 us
    ppermute x7, waiting for transfers between devices, swap(): return lax.ppermute(x, names, [(at, at ^ step) for at in range(size)])  10.7 us
    ppermute x7, starting transfers between devices, swap(): return lax.ppermute(x, names, [(at, at ^ step) for at in range(size)])  10.1 us
    pallas_call x1, Pallas kernels, per_device(): pl.pallas_call(normalize, out_shape=[shape((block, width), BF16)] * steps...  9.43 us
    all_to_all x1, starting transfers between devices, per_device(): lax.all_to_all(packed, ('line', 'pair'), split_axis=0, concat_axis=0, til...  7.27 us
    all_to_all x1, waiting for transfers between devices, per_device(): lax.all_to_all(packed, ('line', 'pair'), split_axis=0, concat_axis=0, til...  6.6 us
    unnamed x18, local copies, waits for them, and re-layouts  2.09 us
  transfers between devices with their start and end apart: 8, of which 4 were waited for; matrix products, arithmetic and copies ran while one was open for 1% of the time, Pallas kernels for 26%

profile of v11, /device:TPU:0, one launch (start us, length us, event | category | flops | bytes accessed | tf_op | source)
XLA Modules:
  0.0 87.2 jit_solution(13014983605110276661)
XLA Ops:
  0.0 3.3 %shard_map.91.after_ref = bf16[8,104,512]{2,1,0:T(8,128)(2,1)} custom-call(s32[1]{0:T(128)} %bitcast.place_ref, bf16[512,1024]{1,0:T(8,128)(2,1)} %wq_hbm.1, bf16[512,256]{1,0:T(8,128)(2,1)} %wkv_hbm.1, bf16[8,128]{1,0:T(8,128)(2,1)} %bitcast.17, s32[1,512]{1,0:T(1,128)} %bitcast.13, s32[1,512]{1,0:T(1,128)} %bitcast.19), custom_call_target="tpu_custom_call" | custom-call | tf_op jit(solution)/shard_map/pallas_call | solution.py:414
  3.3 7.3 %all-to-all-start = ((bf16[8,104,512]{2,1,0:T(8,128)(2,1)}), bf16[8,104,512]{2,1,0:T(8,128)(2,1)S(1)}, u32[]{:S(2)}, u32[]{:S(2)}) async-start(bf16[8,104,512]{2,1,0:T(8,128)(2,1)} %shard_map.91.after_ref), calls=%async_computation | async-start | bytes 1703936 | tf_op jit(solution)/shard_map/all_to_all | solution.py:481
  10.6 0.6 pad_add_fusion.place_ref
  11.2 2.9 %shard_map.98 = (bf16[9,256,128]{2,1,0:T(8,128)(2,1)}, s32[1,512]{1,0:T(1,128)}) custom-call(s32[4]{0:T(128)} %pad_add_fusion.place_ref, bf16[8,256,256]{2,1,0:T(8,128)(2,1)} %prefix_hbm.1, bf16[8,128]{1,0:T(8,128)(2,1)} %bitcast.18, s32[1,512]{1,0:T(1,128)} %bitcast.14, bf16[8,104,512]{2,1,0:T(8,128)(2,1)} %shard_map.91.after_ref), custom_call_target="tpu_custom_call" | custom-call | tf_op jit(solution)/shard_map/pallas_call | solution.py:414
  14.1 2.1 %collective-permute-start.1 = (bf16[9,256,128]{2,1,0:T(8,128)(2,1)}, bf16[9,256,128]{2,1,0:T(8,128)(2,1)S(1)}, u32[]{:S(2)}, u32[]{:S(2)}) collective-permute-start(bf16[9,256,128]{2,1,0:T(8,128)(2,1)} %get-tuple-element.34.rest_0_), channel_id=1, source_target_pairs={{0,2},{2,0},{16,18},{18,16},{1,3},{3,1},{17,19},{19,17},{4,6},{6,4... | collective-permute-start | bytes 1769480 | tf_op jit(solution)/shard_map/ppermute | solution.py:432
  16.2 9.4 %shard_map.92 = (bf16[256,4096]{1,0:T(8,128)(2,1)}, bf16[256,4096]{1,0:T(8,128)(2,1)}, bf16[256,4096]{1,0:T(8,128)(2,1)}, bf16[256,4096]{1,0:T(8,128)(2,1)}) custom-call(bf16[1024,4096]{1,0:T(8,128)(2,1)} %table_ref.1, bf16[32,128]{1,0:T(8,128)(2,1)} %bitcast.16, bf16[8,104,512]{2,1,0:T(8,128)(2,1)} %shard_map.91.after_ref), custom_call_target="tpu_custom_call" | custom-call | flops 4194304 | bytes 1048576 | tf_op jit(solution)/shard_map/pallas_call | solution.py:503
  25.6 6.6 %all-to-all-done.w_ref.refs_0_ = bf16[8,104,512]{2,1,0:T(8,128)(2,1)S(1)} async-done(((bf16[8,104,512]{2,1,0:T(8,128)(2,1)}), bf16[8,104,512]{2,1,0:T(8,128)(2,1)S(1)}, u32[]{:S(2)}, u32[]{:S(2)}) %all-to-all-start) | async-done | bytes 852000 | tf_op jit(solution)/shard_map/all_to_all | solution.py:481
  32.2 1.6 %copy-done.7 = bf16[256,4096]{1,0:T(8,128)(2,1)S(1)} copy-done((bf16[256,4096]{1,0:T(8,128)(2,1)S(1)}, bf16[256,4096]{1,0:T(8,128)(2,1)}, u32[]{:S(2)}) %copy-start.7) | copy-done | bytes 2097176
  33.8 1.3 %shard_map.93 = (bf16[72,1024]{1,0:T(8,128)(2,1)S(1)}, f32[2,1024]{1,0:T(2,128)S(1)}, f32[8,128]{1,0:T(8,128)S(1)}) custom-call(s32[4]{0:T(128)S(1)} %copy-done.2, bf16[8,104,512]{2,1,0:T(8,128)(2,1)S(1)} %all-to-all-done.w_ref.refs_0_, bf16[256,4096]{1,0:T(8,128)(2,1)S(1)} %copy-done.7, f32[4,32,2]{2,1,0:T(8,128)S(1)} %copy-done.8), custom_call_target="tpu_custom_call" | custom-call | flops 2147483648 | bytes 1048576 | tf_op jit(solution)/shard_map/pallas_call | solution.py:414
  35.2 0.7 shard_map.97.own_ref
  35.9 1.6 %collective-permute-start = (f32[16,128]{1,0:T(8,128)S(1)}, f32[16,128]{1,0:T(8,128)S(1)}, u32[]{:S(2)}, u32[]{:S(2)}) collective-permute-start(f32[16,128]{1,0:T(8,128)S(1)} %shard_map.97.own_ref), channel_id=1, source_target_pairs={{0,16},{2,18},{16,0},{18,2},{1,17},{3,19},{17,1},{19,3},{4,20},{6,... | collective-permute-start | bytes 24584 | tf_op jit(solution)/shard_map/ppermute | solution.py:432
  38.0 1.7 %collective-permute-done.refs_1_.other_ref = f32[16,128]{1,0:T(8,128)S(1)} collective-permute-done((f32[16,128]{1,0:T(8,128)S(1)}, f32[16,128]{1,0:T(8,128)S(1)}, u32[]{:S(2)}, u32[]{:S(2)}) %collective-permute-start) | collective-permute-done | bytes 8224 | tf_op jit(solution)/shard_map/ppermute | solution.py:432
  39.8 1.5 %collective-permute-start.3 = (bf16[9,256,128]{2,1,0:T(8,128)(2,1)S(1)}, bf16[9,256,128]{2,1,0:T(8,128)(2,1)S(1)}, u32[]{:S(2)}, u32[]{:S(2)}) collective-permute-start(bf16[9,256,128]{2,1,0:T(8,128)(2,1)S(1)} %shard_map.99.rest_1_.refs_1_), channel_id=1, source_target_pairs={{0,16},{2,18},{16,0},{18,2},{1,17},{3,19},{17,1},{19,3},{4,20},{6,... | collective-permute-start | bytes 1769480 | tf_op jit(solution)/shard_map/ppermute | solution.py:432
  41.3 1.3 %shard_map.94 = (bf16[72,1024]{1,0:T(8,128)(2,1)S(1)}, f32[2,1024]{1,0:T(2,128)S(1)}) custom-call(s32[4]{0:T(128)S(1)} %copy-done.2, bf16[8,104,512]{2,1,0:T(8,128)(2,1)S(1)} %all-to-all-done.w_ref.refs_0_, bf16[256,4096]{1,0:T(8,128)(2,1)S(1)} %copy-done.6, f32[4,32,2]{2,1,0:T(8,128)S(1)} %copy-done.8, ...), custom_call_target="tpu_custom_call", output_to_operand_aliasing={{0}: (4, {}), {1}: (5, {})} | custom-call | flops 2147483648 | bytes 1048576 | tf_op jit(solution)/shard_map/pallas_call | solution.py:414
  42.9 1.3 %shard_map.95 = (bf16[72,1024]{1,0:T(8,128)(2,1)S(1)}, f32[2,1024]{1,0:T(2,128)S(1)}) custom-call(s32[4]{0:T(128)S(1)} %copy-done.2, bf16[8,104,512]{2,1,0:T(8,128)(2,1)S(1)} %all-to-all-done.w_ref.refs_0_, bf16[256,4096]{1,0:T(8,128)(2,1)S(1)} %copy-done.5, f32[4,32,2]{2,1,0:T(8,128)S(1)} %copy-done.8, ...), custom_call_target="tpu_custom_call", output_to_operand_aliasing={{0}: (4, {}), {1}: (5, {})} | custom-call | flops 2147483648 | bytes 1048576 | tf_op jit(solution)/shard_map/pallas_call | solution.py:414
  44.5 1.3 %shard_map.96 = (bf16[72,1024]{1,0:T(8,128)(2,1)S(1)}, f32[2,1024]{1,0:T(2,128)S(1)}) custom-call(s32[4]{0:T(128)S(1)} %copy-done.2, bf16[8,104,512]{2,1,0:T(8,128)(2,1)S(1)} %all-to-all-done.w_ref.refs_0_, bf16[256,4096]{1,0:T(8,128)(2,1)S(1)} %copy-done.4, f32[4,32,2]{2,1,0:T(8,128)S(1)} %copy-done.8, ...), custom_call_target="tpu_custom_call", output_to_operand_aliasing={{0}: (4, {}), {1}: (5, {})} | custom-call | flops 2147483648 | bytes 1048576 | tf_op jit(solution)/shard_map/pallas_call | solution.py:414
  45.8 7.9 %collective-permute-done.2.rest_2_.refs_2_ = bf16[9,256,128]{2,1,0:T(8,128)(2,1)S(1)} collective-permute-done((bf16[9,256,128]{2,1,0:T(8,128)(2,1)S(1)}, bf16[9,256,128]{2,1,0:T(8,128)(2,1)S(1)}, u32[]{:S(2)}, u32[]{:S(2)}) %collective-permute-start.2) | collective-permute-done | bytes 589856 | tf_op jit(solution)/shard_map/ppermute | solution.py:432
  53.8 1.1 %collective-permute-start.6 = (bf16[72,1024]{1,0:T(8,128)(2,1)S(1)}, bf16[72,1024]{1,0:T(8,128)(2,1)S(1)}, u32[]{:S(2)}, u32[]{:S(2)}) collective-permute-start(bf16[72,1024]{1,0:T(8,128)(2,1)S(1)} %shard_map.101.rest_4_), channel_id=1, source_target_pairs={{0,12},{4,8},{8,4},{12,0},{1,13},{5,9},{9,5},{13,1},{2,14},{6,10},... | collective-permute-start | bytes 442376 | tf_op jit(solution)/shard_map/ppermute | solution.py:432
  55.3 2.8 %collective-permute-start.4 = (bf16[72,1024]{1,0:T(8,128)(2,1)S(1)}, bf16[72,1024]{1,0:T(8,128)(2,1)S(1)}, u32[]{:S(2)}, u32[]{:S(2)}) collective-permute-start(bf16[72,1024]{1,0:T(8,128)(2,1)S(1)} %shard_map.101.rest_4_), channel_id=1, source_target_pairs={{0,4},{4,0},{8,12},{12,8},{1,5},{5,1},{9,13},{13,9},{2,6},{6,2},{1... | collective-permute-start | bytes 442376 | tf_op jit(solution)/shard_map/ppermute | solution.py:432
  58.2 4.6 %shard_map.100 = (bf16[8,1024,512]{2,1,0:T(8,128)(2,1)S(1)}, f32[3,8,256,256]{3,2,1,0:T(8,128)S(1)}) custom-call(s32[4]{0:T(128)S(1)} %copy-done.2, f32[16,128]{1,0:T(8,128)S(1)} %shard_map.97.own_ref, f32[16,128]{1,0:T(8,128)S(1)} %collective-permute-done.refs_1_.other_ref, bf16[9,256,128]{2,1,0:T(8,128)(2,1)S(1)} %copy-done, ...), custom_call_target="tpu_custom_call" | custom-call | flops 1000000000 | bytes 1000000 | tf_op jit(solution)/shard_map/pallas_call | solution.py:414
  62.8 1.1 %collective-permute-done.5.rest_6_ = bf16[72,1024]{1,0:T(8,128)(2,1)S(1)} collective-permute-done((bf16[72,1024]{1,0:T(8,128)(2,1)S(1)}, bf16[72,1024]{1,0:T(8,128)(2,1)S(1)}, u32[]{:S(2)}, u32[]{:S(2)}) %collective-permute-start.5) | collective-permute-done | bytes 147488 | tf_op jit(solution)/shard_map/ppermute | solution.py:432
  63.9 7.2 %shard_map.102 = f32[2,16,16,128]{3,2,1,0:T(8,128)S(1)} custom-call(s32[4]{0:T(128)S(1)} %copy-done.2, f32[2,1024]{1,0:T(2,128)S(1)} %get-tuple-element.32.vo_ref, f32[16,128]{1,0:T(8,128)S(1)} %shard_map.97.own_ref, f32[16,128]{1,0:T(8,128)S(1)} %collective-permute-done.refs_1_.other_ref, bf16[8,1024,512]{2,1,0:T(8,128)(2,1)S(1)} %get-tuple-element.35.chosen_ref, ...), custom_call_target="tpu_custom_call" | custom-call | tf_op jit(solution)/shard_map/pallas_call | solution.py:414
  71.1 15.0 %all_to_all.10 = f32[32,16,128]{2,1,0:T(8,128)S(1)} all-to-all(f32[32,16,128]{2,1,0:T(8,128)S(1)} %bitcast.11), channel_id=1, replica_groups=mesh['groups'=2,'line'=4,'pair'=2,'tensor'=2] {'groups','line','pair','t..., dimensions={0} | all-to-all | bytes 524288 | tf_op jit(solution)/shard_map/all_to_all | solution.py:588
  86.1 1.1 %shard_map.103 = f32[1,512]{1,0:T(1,128)} custom-call(f32[2,4,4,16,128]{4,3,2,1,0:T(8,128)S(1)} %bitcast.12, s32[1,512]{1,0:T(1,128)S(1)} %bitcast.15, s32[1,512]{1,0:T(1,128)S(1)} %copy-done.3), custom_call_target="tpu_custom_call" | custom-call | tf_op jit(solution)/shard_map/pallas_call | solution.py:596
  (25 shorter events, 1.5 us)
Async XLA Ops:
  3.3 28.9 %all-to-all-start = ((bf16[8,104,512]{2,1,0:T(8,128)(2,1)}), bf16[8,104,512]{2,1,0:T(8,128)(2,1)S(1)}, u32[]{:S(2)}, u32[]{:S(2)}) async-start(bf16[8,104,512]{2,1,0:T(8,128)(2,1)} %shard_map.91.after_ref), calls=%async_computation | async-start | bytes 1703936 | tf_op jit(solution)/shard_map/all_to_all | solution.py:481
  14.1 23.9 %collective-permute-start.1 = (bf16[9,256,128]{2,1,0:T(8,128)(2,1)}, bf16[9,256,128]{2,1,0:T(8,128)(2,1)S(1)}, u32[]{:S(2)}, u32[]{:S(2)}) collective-permute-start(bf16[9,256,128]{2,1,0:T(8,128)(2,1)} %get-tuple-element.34.rest_0_), channel_id=1, source_target_pairs={{0,2},{2,0},{16,18},{18,16},{1,3},{3,1},{17,19},{19,17},{4,6},{6,4... | collective-permute-start | bytes 1769480 | tf_op jit(solution)/shard_map/ppermute | solution.py:432
  16.2 16.0 %copy-start.2 = (s32[4]{0:T(128)S(1)}, s32[4]{0:T(128)}, u32[]{:S(2)}) copy-start(s32[4]{0:T(128)} %pad_add_fusion.place_ref) | copy-start | bytes 52
  16.2 16.0 %copy-start.8 = (f32[4,32,2]{2,1,0:T(8,128)S(1)}, f32[4,32,2]{2,1,0:T(8,128)}, u32[]{:S(2)}) copy-start(f32[4,32,2]{2,1,0:T(8,128)} %constant.17.clone.turn_ref) | copy-start | bytes 3076
  32.2 1.6 %copy-start.7 = (bf16[256,4096]{1,0:T(8,128)(2,1)S(1)}, bf16[256,4096]{1,0:T(8,128)(2,1)}, u32[]{:S(2)}) copy-start(bf16[256,4096]{1,0:T(8,128)(2,1)} %get-tuple-element.25.normed_ref) | copy-start | bytes 6291460
  33.8 3.7 %copy-start = (bf16[9,256,128]{2,1,0:T(8,128)(2,1)S(1)}, bf16[9,256,128]{2,1,0:T(8,128)(2,1)}, u32[]{:S(2)}) copy-start(bf16[9,256,128]{2,1,0:T(8,128)(2,1)} %get-tuple-element.34.rest_0_) | copy-start | bytes 1769476
  33.8 7.5 %copy-start.6 = (bf16[256,4096]{1,0:T(8,128)(2,1)S(1)}, bf16[256,4096]{1,0:T(8,128)(2,1)}, u32[]{:S(2)}) copy-start(bf16[256,4096]{1,0:T(8,128)(2,1)} %get-tuple-element.24.normed_ref) | copy-start | bytes 6291460
  35.9 3.8 %collective-permute-start = (f32[16,128]{1,0:T(8,128)S(1)}, f32[16,128]{1,0:T(8,128)S(1)}, u32[]{:S(2)}, u32[]{:S(2)}) collective-permute-start(f32[16,128]{1,0:T(8,128)S(1)} %shard_map.97.own_ref), channel_id=1, source_target_pairs={{0,16},{2,18},{16,0},{18,2},{1,17},{3,19},{17,1},{19,3},{4,20},{6,... | collective-permute-start | bytes 24584 | tf_op jit(solution)/shard_map/ppermute | solution.py:432
  37.5 16.3 %collective-permute-start.2 = (bf16[9,256,128]{2,1,0:T(8,128)(2,1)S(1)}, bf16[9,256,128]{2,1,0:T(8,128)(2,1)S(1)}, u32[]{:S(2)}, u32[]{:S(2)}) collective-permute-start(bf16[9,256,128]{2,1,0:T(8,128)(2,1)S(1)} %copy-done), channel_id=1, source_target_pairs={{0,16},{2,18},{16,0},{18,2},{1,17},{3,19},{17,1},{19,3},{4,20},{6,... | collective-permute-start | bytes 1769480 | tf_op jit(solution)/shard_map/ppermute | solution.py:432
  39.8 24.1 %collective-permute-start.3 = (bf16[9,256,128]{2,1,0:T(8,128)(2,1)S(1)}, bf16[9,256,128]{2,1,0:T(8,128)(2,1)S(1)}, u32[]{:S(2)}, u32[]{:S(2)}) collective-permute-start(bf16[9,256,128]{2,1,0:T(8,128)(2,1)S(1)} %shard_map.99.rest_1_.refs_1_), channel_id=1, source_target_pairs={{0,16},{2,18},{16,0},{18,2},{1,17},{3,19},{17,1},{19,3},{4,20},{6,... | collective-permute-start | bytes 1769480 | tf_op jit(solution)/shard_map/ppermute | solution.py:432
  41.3 1.6 %copy-start.5 = (bf16[256,4096]{1,0:T(8,128)(2,1)S(1)}, bf16[256,4096]{1,0:T(8,128)(2,1)}, u32[]{:S(2)}) copy-start(bf16[256,4096]{1,0:T(8,128)(2,1)} %get-tuple-element.23.normed_ref) | copy-start | bytes 6291460
  42.9 1.6 %copy-start.4 = (bf16[256,4096]{1,0:T(8,128)(2,1)S(1)}, bf16[256,4096]{1,0:T(8,128)(2,1)}, u32[]{:S(2)}) copy-start(bf16[256,4096]{1,0:T(8,128)(2,1)} %get-tuple-element.22.normed_ref) | copy-start | bytes 6291460
  53.8 9.0 %collective-permute-start.6 = (bf16[72,1024]{1,0:T(8,128)(2,1)S(1)}, bf16[72,1024]{1,0:T(8,128)(2,1)S(1)}, u32[]{:S(2)}, u32[]{:S(2)}) collective-permute-start(bf16[72,1024]{1,0:T(8,128)(2,1)S(1)} %shard_map.101.rest_4_), channel_id=1, source_target_pairs={{0,12},{4,8},{8,4},{12,0},{1,13},{5,9},{9,5},{13,1},{2,14},{6,10},... | collective-permute-start | bytes 442376 | tf_op jit(solution)/shard_map/ppermute | solution.py:432
  54.9 9.0 %collective-permute-start.5 = (bf16[72,1024]{1,0:T(8,128)(2,1)S(1)}, bf16[72,1024]{1,0:T(8,128)(2,1)S(1)}, u32[]{:S(2)}, u32[]{:S(2)}) collective-permute-start(bf16[72,1024]{1,0:T(8,128)(2,1)S(1)} %shard_map.101.rest_4_), channel_id=1, source_target_pairs={{0,8},{4,12},{8,0},{12,4},{1,9},{5,13},{9,1},{13,5},{2,10},{6,14},... | collective-permute-start | bytes 442376 | tf_op jit(solution)/shard_map/ppermute | solution.py:432
  55.3 8.6 %collective-permute-start.4 = (bf16[72,1024]{1,0:T(8,128)(2,1)S(1)}, bf16[72,1024]{1,0:T(8,128)(2,1)S(1)}, u32[]{:S(2)}, u32[]{:S(2)}) collective-permute-start(bf16[72,1024]{1,0:T(8,128)(2,1)S(1)} %shard_map.101.rest_4_), channel_id=1, source_target_pairs={{0,4},{4,0},{8,12},{12,8},{1,5},{5,1},{9,13},{13,9},{2,6},{6,2},{1... | collective-permute-start | bytes 442376 | tf_op jit(solution)/shard_map/ppermute | solution.py:432
  63.9 22.2 %copy-start.1 = (s32[512,1]{0,1:T(1,128)S(1)}, s32[512,1]{0,1:T(1,128)}, u32[]{:S(2)}) copy-start(s32[512,1]{0,1:T(1,128)} %param.11) | copy-start | bytes 6148
  63.9 22.2 %copy-start.3 = (s32[1,512]{1,0:T(1,128)S(1)}, s32[1,512]{1,0:T(1,128)}, u32[]{:S(2)}) copy-start(s32[1,512]{1,0:T(1,128)} %get-tuple-element.38.slot_ref) | copy-start | bytes 6148

commit v12 on v11

--- a/solution.py
+++ b/solution.py
@@ -163,10 +163,35 @@
         pl.when(here == step)(functools.partial(one, step))
 
 
-def project(plan, at, mark, place_ref, w_ref, normed_ref, turn_ref, *refs):
-    if mark:
-        *refs, mark_ref = refs
-        mark_ref[...] = jnp.zeros_like(mark_ref)
+def read_lists(plan, w_ref, out_ref):
+    share, capacity, peers = plan.share, plan.capacity, plan.peers
+    span = share * capacity
+    if len(w_ref.shape) == 3:
+        rows = [w_ref[s].astype(F32)[plan.list_at : plan.list_at + 1] for s in range(peers)]
+    else:
+        row = w_ref[...].astype(F32)[plan.list_at : plan.list_at + 1]
+        rows = [row[:, s * 2 * span : (s + 1) * 2 * span] for s in range(peers)]
+    rows = jnp.concatenate(rows, axis=0)
+    lane = lax.broadcasted_iota(jnp.int32, (share * peers, 2 * span), 1)
+    row = lax.broadcasted_iota(jnp.int32, (share * peers, 2 * span), 0)
+    lane = jnp.where(lane < span, lane, lane - span)
+    spread = jnp.concatenate([rows] * share, axis=0)
+    spread = jnp.where(lane // capacity == row // peers, spread, 0.0).astype(BF16)
+    c = lax.broadcasted_iota(jnp.int32, (2 * span, plan.slots), 0)
+    slot = lax.broadcasted_iota(jnp.int32, (2 * span, plan.slots), 1)
+    scale = jnp.where(c < span, 64.0, 1.0)
+    place = jnp.where(c % capacity == slot % capacity, scale, 0.0).astype(BF16)
+    listed = matmul(spread, place)
+    row = lax.broadcasted_iota(jnp.int32, listed.shape, 0)
+    slot = lax.broadcasted_iota(jnp.int32, listed.shape, 1)
+    listed = jnp.where(slot // capacity == row % peers, listed, 0.0)
+    out_ref[...] = jnp.sum(listed.reshape(share, peers, plan.slots), axis=1)
+
+
+def project(plan, at, lists, place_ref, w_ref, normed_ref, turn_ref, *refs):
+    if lists:
+        *refs, list_ref = refs
+        read_lists(plan, w_ref, list_ref)
     q_ref, vo_ref = refs[-2:]
     if len(w_ref.shape) == 3:
         depth = w_ref.shape[2]
@@ -254,27 +279,6 @@
     copies[3].wait()
 
 
-def read_lists(plan, place_ref, *refs):
-    w_ref, _, out_ref = refs
-    share, capacity, peers = plan.share, plan.capacity, plan.peers
-    span = share * capacity
-    rows = jnp.concatenate([w_ref[s].astype(F32)[plan.list_at : plan.list_at + 1] for s in range(peers)], axis=0)
-    lane = lax.broadcasted_iota(jnp.int32, (share * peers, 2 * span), 1)
-    row = lax.broadcasted_iota(jnp.int32, (share * peers, 2 * span), 0)
-    lane = jnp.where(lane < span, lane, lane - span)
-    spread = jnp.concatenate([rows] * share, axis=0)
-    spread = jnp.where(lane // capacity == row // peers, spread, 0.0).astype(BF16)
-    c = lax.broadcasted_iota(jnp.int32, (2 * span, plan.slots), 0)
-    slot = lax.broadcasted_iota(jnp.int32, (2 * span, plan.slots), 1)
-    scale = jnp.where(c < span, 64.0, 1.0)
-    place = jnp.where(c % capacity == slot % capacity, scale, 0.0).astype(BF16)
-    listed = matmul(spread, place)
-    row = lax.broadcasted_iota(jnp.int32, listed.shape, 0)
-    slot = lax.broadcasted_iota(jnp.int32, listed.shape, 1)
-    listed = jnp.where(slot // capacity == row % peers, listed, 0.0)
-    out_ref[...] = jnp.sum(listed.reshape(share, peers, plan.slots), axis=1)
-
-
 def fold_columns(plan, here, block, board, boards, heads):
     lanes = plan.mine * plan.slots
     row = lax.broadcasted_iota(jnp.int32, (HD, lanes), 0) - board * (HD // boards)
@@ -523,39 +527,35 @@
     flat = weights.transpose(1, 0, 2).reshape(plan.rows, width) if depth % HD else weights
     sent = (plan.line_rows, moves)
     outs = (shape(sent if plan.direct else (line, *sent), BF16), shape((plan.mine, moves), F32))
-    filled, ready = (), None
+    waits = {0: across, steps - 1: beside}
+    filled, listed = (), None
     for step in range(steps):
+        args = (flat, normed[step], jnp.asarray(turns), *filled)
+        more = (waits[step],) if step in waits else ()
+        lists = [shape((plan.share, plan.slots), F32)] if step == 0 else []
         made = local_call(
             functools.partial(project, plan, slice(step * block, (step + 1) * block), step == 0),
             place,
-            (flat, normed[step], jnp.asarray(turns), *filled),
-            [*outs, shape((8, HD), F32)] if step == 0 else list(outs),
+            (*args, *more),
+            [*outs, *lists],
             (),
             16,
-            (),
+            range(len(args), len(args) + len(more)),
             2 * block * width * 1024,
             block * width,
             {4: 0, 5: 1} if filled else None,
         )
         filled = made[:2]
-        ready = made[2] if step == 0 else ready
+        listed = made[2] if step == 0 else listed
     queries, own_values = filled
-    listed = local_call(
-        functools.partial(read_lists, plan),
-        place,
-        (weights, ready),
-        shape((plan.share, plan.slots), F32),
-        copied=(1,),
-    )
     other = swap(listed, slab_axes, plan.slab, pair)
-    beside = tied(beside, other)
-    queries = tied(queries, beside, across)
+    across = tied(across, listed)
+    diagonal = swap(across, slab_axes, plan.slab, 1)
     if plan.direct:
         queries = [queries] + [swap(queries, "line", line, step) for step in range(1, line)]
     else:
         queries = lax.all_to_all(queries, "line", split_axis=0, concat_axis=0, tiled=True)
         queries = [queries.reshape(line * plan.line_rows, moves)]
-    diagonal = swap(beside, slab_axes, plan.slab, 2)
 
     query_rows = plan.mine * HD
     back = plan.peers * lax.axis_size("tensor")

time: 87.5 us -> 76.6 us (0.88)
  waiting for transfers between devices: 17.3 us -> 7.68 us
  blocking collectives: 15 us -> 13.5 us
    ppermute x7, waiting for transfers between devices: 10.7 us -> 4.61 us  [swap(): return lax.ppermute(x, names, [(at, at ^ step) for at in range(size)])]
    all_to_all x1, waiting for transfers between devices: 6.6 us -> 3.07 us  [per_device(): lax.all_to_all(packed, ('line', 'pair'), split_axis=0, concat_axis=0, til...]
    all_to_all x1, blocking collectives: 15 us -> 13.5 us  [per_device(): lax.all_to_all(parts.reshape(groups * back, plan.share, plan.slots), ('gr...]
    pallas_call x9 -> x8, Pallas kernels: 24.1 us -> 23.4 us  [local_call(): pl.pallas_call(kernel, out_shape=outs, in_specs=[pl.BlockSpec(memory_spac...]
  transfers between devices with their start and end apart: 8 -> 8, of which waited for: 4 -> 4; matrix products, arithmetic and copies ran while one was open for 1% -> 1% of each run, Pallas kernels for 26% -> 29%
where the time goes in v12:
time: 76.6 us; the launch traced here: 76.2 us
  Pallas kernels  33.9 us (44%)
  starting transfers between devices  18.2 us (24%)
  blocking collectives  13.5 us (18%)
  waiting for transfers between devices  7.68 us (10%)
  local copies, waits for them, and re-layouts  2.08 us (3%)
    pallas_call x8, Pallas kernels, local_call(): pl.pallas_call(kernel, out_shape=outs, in_specs=[pl.BlockSpec(memory_spac...  23.4 us
    all_to_all x1, blocking collectives, per_device(): lax.all_to_all(parts.reshape(groups * back, plan.share, plan.slots), ('gr...  13.5 us
    ppermute x7, starting transfers between devices, swap(): return lax.ppermute(x, names, [(at, at ^ step) for at in range(size)])  11 us
    pallas_call x1, Pallas kernels, per_device(): pl.pallas_call(normalize, out_shape=[shape((block, width), BF16)] * steps...  9.46 us
    all_to_all x1, starting transfers between devices, per_device(): lax.all_to_all(packed, ('line', 'pair'), split_axis=0, concat_axis=0, til...  7.27 us
    ppermute x7, waiting for transfers between devices, swap(): return lax.ppermute(x, names, [(at, at ^ step) for at in range(size)])  4.61 us
    all_to_all x1, waiting for transfers between devices, per_device(): lax.all_to_all(packed, ('line', 'pair'), split_axis=0, concat_axis=0, til...  3.07 us
    unnamed x18, local copies, waits for them, and re-layouts  2.08 us
  transfers between devices with their start and end apart: 8, of which 4 were waited for; matrix products, arithmetic and copies ran while one was open for 1% of the time, Pallas kernels for 29%

profile of v12, /device:TPU:0, one launch (start us, length us, event | category | flops | bytes accessed | tf_op | source)
XLA Modules:
  0.0 76.2 jit_solution(16740460016318369250)
XLA Ops:
  0.0 3.3 %shard_map.91.after_ref = bf16[8,104,512]{2,1,0:T(8,128)(2,1)} custom-call(s32[1]{0:T(128)} %bitcast.place_ref, bf16[512,1024]{1,0:T(8,128)(2,1)} %wq_hbm.1, bf16[512,256]{1,0:T(8,128)(2,1)} %wkv_hbm.1, bf16[8,128]{1,0:T(8,128)(2,1)} %bitcast.17, s32[1,512]{1,0:T(1,128)} %bitcast.13, s32[1,512]{1,0:T(1,128)} %bitcast.19), custom_call_target="tpu_custom_call" | custom-call | tf_op jit(solution)/shard_map/pallas_call | solution.py:418
  3.3 7.3 %all-to-all-start = ((bf16[8,104,512]{2,1,0:T(8,128)(2,1)}), bf16[8,104,512]{2,1,0:T(8,128)(2,1)S(1)}, u32[]{:S(2)}, u32[]{:S(2)}) async-start(bf16[8,104,512]{2,1,0:T(8,128)(2,1)} %shard_map.91.after_ref), calls=%async_computation | async-start | bytes 1703936 | tf_op jit(solution)/shard_map/all_to_all | solution.py:485
  10.6 0.6 pad_add_fusion.place_ref
  11.2 2.9 %shard_map.93 = (bf16[9,256,128]{2,1,0:T(8,128)(2,1)}, s32[1,512]{1,0:T(1,128)}) custom-call(s32[4]{0:T(128)} %pad_add_fusion.place_ref, bf16[8,256,256]{2,1,0:T(8,128)(2,1)} %prefix_hbm.1, bf16[8,128]{1,0:T(8,128)(2,1)} %bitcast.18, s32[1,512]{1,0:T(1,128)} %bitcast.14, bf16[8,104,512]{2,1,0:T(8,128)(2,1)} %shard_map.91.after_ref), custom_call_target="tpu_custom_call" | custom-call | tf_op jit(solution)/shard_map/pallas_call | solution.py:418
  14.1 1.6 %collective-permute-start = (bf16[9,256,128]{2,1,0:T(8,128)(2,1)}, bf16[9,256,128]{2,1,0:T(8,128)(2,1)S(1)}, u32[]{:S(2)}, u32[]{:S(2)}) collective-permute-start(bf16[9,256,128]{2,1,0:T(8,128)(2,1)} %get-tuple-element.26.rest_0_), channel_id=1, source_target_pairs={{0,16},{2,18},{16,0},{18,2},{1,17},{3,19},{17,1},{19,3},{4,20},{6,... | collective-permute-start | bytes 1769480 | tf_op jit(solution)/shard_map/ppermute | solution.py:436
  15.7 2.0 %collective-permute-start.1 = (bf16[9,256,128]{2,1,0:T(8,128)(2,1)}, bf16[9,256,128]{2,1,0:T(8,128)(2,1)S(1)}, u32[]{:S(2)}, u32[]{:S(2)}) collective-permute-start(bf16[9,256,128]{2,1,0:T(8,128)(2,1)} %get-tuple-element.26.rest_0_), channel_id=1, source_target_pairs={{0,2},{2,0},{16,18},{18,16},{1,3},{3,1},{17,19},{19,17},{4,6},{6,4... | collective-permute-start | bytes 1769480 | tf_op jit(solution)/shard_map/ppermute | solution.py:436
  17.7 9.5 %shard_map.92 = (bf16[256,4096]{1,0:T(8,128)(2,1)}, bf16[256,4096]{1,0:T(8,128)(2,1)}, bf16[256,4096]{1,0:T(8,128)(2,1)}, bf16[256,4096]{1,0:T(8,128)(2,1)}) custom-call(bf16[1024,4096]{1,0:T(8,128)(2,1)} %table_ref.1, bf16[32,128]{1,0:T(8,128)(2,1)} %bitcast.16, bf16[8,104,512]{2,1,0:T(8,128)(2,1)} %shard_map.91.after_ref), custom_call_target="tpu_custom_call" | custom-call | flops 4194304 | bytes 1048576 | tf_op jit(solution)/shard_map/pallas_call | solution.py:507
  27.2 2.0 %collective-permute-done.refs_0_ = bf16[9,256,128]{2,1,0:T(8,128)(2,1)S(1)} collective-permute-done((bf16[9,256,128]{2,1,0:T(8,128)(2,1)}, bf16[9,256,128]{2,1,0:T(8,128)(2,1)S(1)}, u32[]{:S(2)}, u32[]{:S(2)}) %collective-permute-start) | collective-permute-done | bytes 589856 | tf_op jit(solution)/shard_map/ppermute | solution.py:436
  29.1 3.1 %all-to-all-done.w_ref = bf16[8,104,512]{2,1,0:T(8,128)(2,1)S(1)} async-done(((bf16[8,104,512]{2,1,0:T(8,128)(2,1)}), bf16[8,104,512]{2,1,0:T(8,128)(2,1)S(1)}, u32[]{:S(2)}, u32[]{:S(2)}) %all-to-all-start) | async-done | bytes 852000 | tf_op jit(solution)/shard_map/all_to_all | solution.py:485
  32.2 1.6 %copy-done.7 = bf16[256,4096]{1,0:T(8,128)(2,1)S(1)} copy-done((bf16[256,4096]{1,0:T(8,128)(2,1)S(1)}, bf16[256,4096]{1,0:T(8,128)(2,1)}, u32[]{:S(2)}) %copy-start.7) | copy-done | bytes 2097176
  33.8 1.4 %shard_map.94 = (bf16[72,1024]{1,0:T(8,128)(2,1)S(1)}, f32[2,1024]{1,0:T(2,128)S(1)}, f32[16,128]{1,0:T(8,128)S(1)}) custom-call(s32[4]{0:T(128)S(1)} %copy-done.2, bf16[8,104,512]{2,1,0:T(8,128)(2,1)S(1)} %all-to-all-done.w_ref, bf16[256,4096]{1,0:T(8,128)(2,1)S(1)} %copy-done.7, f32[4,32,2]{2,1,0:T(8,128)S(1)} %copy-done.8, ...), custom_call_target="tpu_custom_call" | custom-call | flops 2147483648 | bytes 1048576 | tf_op jit(solution)/shard_map/pallas_call | solution.py:418
  35.2 1.4 %collective-permute-start.3 = (bf16[9,256,128]{2,1,0:T(8,128)(2,1)S(1)}, bf16[9,256,128]{2,1,0:T(8,128)(2,1)S(1)}, u32[]{:S(2)}, u32[]{:S(2)}) collective-permute-start(bf16[9,256,128]{2,1,0:T(8,128)(2,1)S(1)} %shard_map.98.rest_2_), channel_id=1, source_target_pairs={{0,2},{2,0},{16,18},{18,16},{1,3},{3,1},{17,19},{19,17},{4,6},{6,4... | collective-permute-start | bytes 1769480 | tf_op jit(solution)/shard_map/ppermute | solution.py:436
  36.6 1.3 %shard_map.95 = (bf16[72,1024]{1,0:T(8,128)(2,1)S(1)}, f32[2,1024]{1,0:T(2,128)S(1)}) custom-call(s32[4]{0:T(128)S(1)} %copy-done.2, bf16[8,104,512]{2,1,0:T(8,128)(2,1)S(1)} %all-to-all-done.w_ref, bf16[256,4096]{1,0:T(8,128)(2,1)S(1)} %copy-done.6, f32[4,32,2]{2,1,0:T(8,128)S(1)} %copy-done.8, ...), custom_call_target="tpu_custom_call", output_to_operand_aliasing={{0}: (4, {}), {1}: (5, {})} | custom-call | flops 2147483648 | bytes 1048576 | tf_op jit(solution)/shard_map/pallas_call | solution.py:418
  38.2 1.3 %shard_map.96 = (bf16[72,1024]{1,0:T(8,128)(2,1)S(1)}, f32[2,1024]{1,0:T(2,128)S(1)}) custom-call(s32[4]{0:T(128)S(1)} %copy-done.2, bf16[8,104,512]{2,1,0:T(8,128)(2,1)S(1)} %all-to-all-done.w_ref, bf16[256,4096]{1,0:T(8,128)(2,1)S(1)} %copy-done.5, f32[4,32,2]{2,1,0:T(8,128)S(1)} %copy-done.8, ...), custom_call_target="tpu_custom_call", output_to_operand_aliasing={{0}: (4, {}), {1}: (5, {})} | custom-call | flops 2147483648 | bytes 1048576 | tf_op jit(solution)/shard_map/pallas_call | solution.py:418
  39.8 1.3 %shard_map.97 = (bf16[72,1024]{1,0:T(8,128)(2,1)S(1)}, f32[2,1024]{1,0:T(2,128)S(1)}) custom-call(s32[4]{0:T(128)S(1)} %copy-done.2, bf16[8,104,512]{2,1,0:T(8,128)(2,1)S(1)} %all-to-all-done.w_ref, bf16[256,4096]{1,0:T(8,128)(2,1)S(1)} %copy-done.4, f32[4,32,2]{2,1,0:T(8,128)S(1)} %copy-done.8, ...), custom_call_target="tpu_custom_call", output_to_operand_aliasing={{0}: (4, {}), {1}: (5, {})} | custom-call | flops 2147483648 | bytes 1048576 | tf_op jit(solution)/shard_map/pallas_call | solution.py:418
  41.2 1.6 %collective-permute-start.6 = (bf16[72,1024]{1,0:T(8,128)(2,1)S(1)}, bf16[72,1024]{1,0:T(8,128)(2,1)S(1)}, u32[]{:S(2)}, u32[]{:S(2)}) collective-permute-start(bf16[72,1024]{1,0:T(8,128)(2,1)S(1)} %get-tuple-element.37.rest_4_), channel_id=1, source_target_pairs={{0,12},{4,8},{8,4},{12,0},{1,13},{5,9},{9,5},{13,1},{2,14},{6,10},... | collective-permute-start | bytes 442376 | tf_op jit(solution)/shard_map/ppermute | solution.py:436
  42.7 2.9 %collective-permute-start.4 = (bf16[72,1024]{1,0:T(8,128)(2,1)S(1)}, bf16[72,1024]{1,0:T(8,128)(2,1)S(1)}, u32[]{:S(2)}, u32[]{:S(2)}) collective-permute-start(bf16[72,1024]{1,0:T(8,128)(2,1)S(1)} %get-tuple-element.37.rest_4_), channel_id=1, source_target_pairs={{0,4},{4,0},{8,12},{12,8},{1,5},{5,1},{9,13},{13,9},{2,6},{6,2},{1... | collective-permute-start | bytes 442376 | tf_op jit(solution)/shard_map/ppermute | solution.py:436
  45.6 1.5 %collective-permute-start.2 = (f32[16,128]{1,0:T(8,128)S(1)}, f32[16,128]{1,0:T(8,128)S(1)}, u32[]{:S(2)}, u32[]{:S(2)}) collective-permute-start(f32[16,128]{1,0:T(8,128)S(1)} %get-tuple-element.34.refs_1_.own_ref), channel_id=1, source_target_pairs={{0,16},{2,18},{16,0},{18,2},{1,17},{3,19},{17,1},{19,3},{4,20},{6,... | collective-permute-start | bytes 24584 | tf_op jit(solution)/shard_map/ppermute | solution.py:436
  47.2 2.1 %collective-permute-done.2.other_ref = f32[16,128]{1,0:T(8,128)S(1)} collective-permute-done((f32[16,128]{1,0:T(8,128)S(1)}, f32[16,128]{1,0:T(8,128)S(1)}, u32[]{:S(2)}, u32[]{:S(2)}) %collective-permute-start.2) | collective-permute-done | bytes 8224 | tf_op jit(solution)/shard_map/ppermute | solution.py:436
  49.3 4.6 %shard_map.99 = (bf16[8,1024,512]{2,1,0:T(8,128)(2,1)S(1)}, f32[3,8,256,256]{3,2,1,0:T(8,128)S(1)}) custom-call(s32[4]{0:T(128)S(1)} %copy-done.2, f32[16,128]{1,0:T(8,128)S(1)} %get-tuple-element.34.refs_1_.own_ref, f32[16,128]{1,0:T(8,128)S(1)} %collective-permute-done.2.other_ref, bf16[9,256,128]{2,1,0:T(8,128)(2,1)S(1)} %copy-done, ...), custom_call_target="tpu_custom_call" | custom-call | flops 1000000000 | bytes 1000000 | tf_op jit(solution)/shard_map/pallas_call | solution.py:418
  53.9 0.5 collective-permute-done.5.rest_6_
  54.5 7.2 %shard_map.100 = f32[2,16,16,128]{3,2,1,0:T(8,128)S(1)} custom-call(s32[4]{0:T(128)S(1)} %copy-done.2, f32[2,1024]{1,0:T(2,128)S(1)} %get-tuple-element.33.vo_ref, f32[16,128]{1,0:T(8,128)S(1)} %get-tuple-element.34.refs_1_.own_ref, f32[16,128]{1,0:T(8,128)S(1)} %collective-permute-done.2.other_ref, bf16[8,1024,512]{2,1,0:T(8,128)(2,1)S(1)} %get-tuple-element.35.chosen_ref, ...), custom_call_target="tpu_custom_call" | custom-call | tf_op jit(solution)/shard_map/pallas_call | solution.py:418
  61.6 13.5 %all_to_all.10 = f32[32,16,128]{2,1,0:T(8,128)S(1)} all-to-all(f32[32,16,128]{2,1,0:T(8,128)S(1)} %bitcast.11), channel_id=1, replica_groups=mesh['groups'=2,'line'=4,'pair'=2,'tensor'=2] {'groups','line','pair','t..., dimensions={0} | all-to-all | bytes 524288 | tf_op jit(solution)/shard_map/all_to_all | solution.py:588
  75.1 1.1 %shard_map.101 = f32[1,512]{1,0:T(1,128)} custom-call(f32[2,4,4,16,128]{4,3,2,1,0:T(8,128)S(1)} %bitcast.12, s32[1,512]{1,0:T(1,128)S(1)} %bitcast.15, s32[1,512]{1,0:T(1,128)S(1)} %copy-done.3), custom_call_target="tpu_custom_call" | custom-call | tf_op jit(solution)/shard_map/pallas_call | solution.py:596
  (23 shorter events, 0.5 us)
Async XLA Ops:
  3.3 28.9 %all-to-all-start = ((bf16[8,104,512]{2,1,0:T(8,128)(2,1)}), bf16[8,104,512]{2,1,0:T(8,128)(2,1)S(1)}, u32[]{:S(2)}, u32[]{:S(2)}) async-start(bf16[8,104,512]{2,1,0:T(8,128)(2,1)} %shard_map.91.after_ref), calls=%async_computation | async-start | bytes 1703936 | tf_op jit(solution)/shard_map/all_to_all | solution.py:485
  14.1 15.1 %collective-permute-start = (bf16[9,256,128]{2,1,0:T(8,128)(2,1)}, bf16[9,256,128]{2,1,0:T(8,128)(2,1)S(1)}, u32[]{:S(2)}, u32[]{:S(2)}) collective-permute-start(bf16[9,256,128]{2,1,0:T(8,128)(2,1)} %get-tuple-element.26.rest_0_), channel_id=1, source_target_pairs={{0,16},{2,18},{16,0},{18,2},{1,17},{3,19},{17,1},{19,3},{4,20},{6,... | collective-permute-start | bytes 1769480 | tf_op jit(solution)/shard_map/ppermute | solution.py:436
  15.7 23.9 %collective-permute-start.1 = (bf16[9,256,128]{2,1,0:T(8,128)(2,1)}, bf16[9,256,128]{2,1,0:T(8,128)(2,1)S(1)}, u32[]{:S(2)}, u32[]{:S(2)}) collective-permute-start(bf16[9,256,128]{2,1,0:T(8,128)(2,1)} %get-tuple-element.26.rest_0_), channel_id=1, source_target_pairs={{0,2},{2,0},{16,18},{18,16},{1,3},{3,1},{17,19},{19,17},{4,6},{6,4... | collective-permute-start | bytes 1769480 | tf_op jit(solution)/shard_map/ppermute | solution.py:436
  17.7 14.5 %copy-start.2 = (s32[4]{0:T(128)S(1)}, s32[4]{0:T(128)}, u32[]{:S(2)}) copy-start(s32[4]{0:T(128)} %pad_add_fusion.place_ref) | copy-start | bytes 52
  17.7 14.5 %copy-start.8 = (f32[4,32,2]{2,1,0:T(8,128)S(1)}, f32[4,32,2]{2,1,0:T(8,128)}, u32[]{:S(2)}) copy-start(f32[4,32,2]{2,1,0:T(8,128)} %constant.17.clone.turn_ref) | copy-start | bytes 3076
  32.2 1.6 %copy-start.7 = (bf16[256,4096]{1,0:T(8,128)(2,1)S(1)}, bf16[256,4096]{1,0:T(8,128)(2,1)}, u32[]{:S(2)}) copy-start(bf16[256,4096]{1,0:T(8,128)(2,1)} %get-tuple-element.25.normed_ref) | copy-start | bytes 6291460
  33.8 2.8 %copy-start.6 = (bf16[256,4096]{1,0:T(8,128)(2,1)S(1)}, bf16[256,4096]{1,0:T(8,128)(2,1)}, u32[]{:S(2)}) copy-start(bf16[256,4096]{1,0:T(8,128)(2,1)} %get-tuple-element.24.normed_ref) | copy-start | bytes 6291460
  35.2 19.2 %collective-permute-start.3 = (bf16[9,256,128]{2,1,0:T(8,128)(2,1)S(1)}, bf16[9,256,128]{2,1,0:T(8,128)(2,1)S(1)}, u32[]{:S(2)}, u32[]{:S(2)}) collective-permute-start(bf16[9,256,128]{2,1,0:T(8,128)(2,1)S(1)} %shard_map.98.rest_2_), channel_id=1, source_target_pairs={{0,2},{2,0},{16,18},{18,16},{1,3},{3,1},{17,19},{19,17},{4,6},{6,4... | collective-permute-start | bytes 1769480 | tf_op jit(solution)/shard_map/ppermute | solution.py:436
  36.6 1.6 %copy-start.5 = (bf16[256,4096]{1,0:T(8,128)(2,1)S(1)}, bf16[256,4096]{1,0:T(8,128)(2,1)}, u32[]{:S(2)}) copy-start(bf16[256,4096]{1,0:T(8,128)(2,1)} %get-tuple-element.23.normed_ref) | copy-start | bytes 6291460
  38.2 1.6 %copy-start.4 = (bf16[256,4096]{1,0:T(8,128)(2,1)S(1)}, bf16[256,4096]{1,0:T(8,128)(2,1)}, u32[]{:S(2)}) copy-start(bf16[256,4096]{1,0:T(8,128)(2,1)} %get-tuple-element.22.normed_ref) | copy-start | bytes 6291460
  39.8 9.5 %copy-start = (bf16[9,256,128]{2,1,0:T(8,128)(2,1)S(1)}, bf16[9,256,128]{2,1,0:T(8,128)(2,1)}, u32[]{:S(2)}) copy-start(bf16[9,256,128]{2,1,0:T(8,128)(2,1)} %get-tuple-element.26.rest_0_) | copy-start | bytes 1769476
  41.2 12.8 %collective-permute-start.6 = (bf16[72,1024]{1,0:T(8,128)(2,1)S(1)}, bf16[72,1024]{1,0:T(8,128)(2,1)S(1)}, u32[]{:S(2)}, u32[]{:S(2)}) collective-permute-start(bf16[72,1024]{1,0:T(8,128)(2,1)S(1)} %get-tuple-element.37.rest_4_), channel_id=1, source_target_pairs={{0,12},{4,8},{8,4},{12,0},{1,13},{5,9},{9,5},{13,1},{2,14},{6,10},... | collective-permute-start | bytes 442376 | tf_op jit(solution)/shard_map/ppermute | solution.py:436
  42.7 11.7 %collective-permute-start.5 = (bf16[72,1024]{1,0:T(8,128)(2,1)S(1)}, bf16[72,1024]{1,0:T(8,128)(2,1)S(1)}, u32[]{:S(2)}, u32[]{:S(2)}) collective-permute-start(bf16[72,1024]{1,0:T(8,128)(2,1)S(1)} %get-tuple-element.37.rest_4_), channel_id=1, source_target_pairs={{0,8},{4,12},{8,0},{12,4},{1,9},{5,13},{9,1},{13,5},{2,10},{6,14},... | collective-permute-start | bytes 442376 | tf_op jit(solution)/shard_map/ppermute | solution.py:436
  42.7 11.7 %collective-permute-start.4 = (bf16[72,1024]{1,0:T(8,128)(2,1)S(1)}, bf16[72,1024]{1,0:T(8,128)(2,1)S(1)}, u32[]{:S(2)}, u32[]{:S(2)}) collective-permute-start(bf16[72,1024]{1,0:T(8,128)(2,1)S(1)} %get-tuple-element.37.rest_4_), channel_id=1, source_target_pairs={{0,4},{4,0},{8,12},{12,8},{1,5},{5,1},{9,13},{13,9},{2,6},{6,2},{1... | collective-permute-start | bytes 442376 | tf_op jit(solution)/shard_map/ppermute | solution.py:436
  45.6 3.7 %collective-permute-start.2 = (f32[16,128]{1,0:T(8,128)S(1)}, f32[16,128]{1,0:T(8,128)S(1)}, u32[]{:S(2)}, u32[]{:S(2)}) collective-permute-start(f32[16,128]{1,0:T(8,128)S(1)} %get-tuple-element.34.refs_1_.own_ref), channel_id=1, source_target_pairs={{0,16},{2,18},{16,0},{18,2},{1,17},{3,19},{17,1},{19,3},{4,20},{6,... | collective-permute-start | bytes 24584 | tf_op jit(solution)/shard_map/ppermute | solution.py:436
  54.4 20.7 %copy-start.1 = (s32[512,1]{0,1:T(1,128)S(1)}, s32[512,1]{0,1:T(1,128)}, u32[]{:S(2)}) copy-start(s32[512,1]{0,1:T(1,128)} %param.11) | copy-start | bytes 6148
  54.4 20.7 %copy-start.3 = (s32[1,512]{1,0:T(1,128)S(1)}, s32[1,512]{1,0:T(1,128)}, u32[]{:S(2)}) copy-start(s32[1,512]{1,0:T(1,128)} %get-tuple-element.38.slot_ref) | copy-start | bytes 6148

commit v13 on v12

--- a/solution.py
+++ b/solution.py
@@ -57,7 +57,7 @@
 def pack_weights(plan, place_ref, wq_hbm, wkv_hbm, ws_hbm, board_hbm, ids_hbm, *rest):
     out_ref, wq, wkv, ws_ref, board_ref, ids_ref, pick, sems = rest
     group = place_ref[0]
-    rows, half_cols = plan.rows, wq.shape[1]
+    half_cols = wq.shape[1]
     columns_here = pl.ds(pl.multiple_of(group * half_cols, HD), half_cols)
     copies = (
         pltpu.make_async_copy(ws_hbm, ws_ref, sems.at[0]),
@@ -70,37 +70,6 @@
         copy.start()
     for copy in copies[:3]:
         copy.wait()
-    r = lax.broadcasted_iota(jnp.int32, (rows, 1), 0)
-    part = r // (plan.mine * plan.pairs)
-    head = (r // plan.pairs) % plan.mine
-    entry = r % plan.pairs
-    is_q = r < plan.q_rows
-    k_at = r - plan.q_rows
-    is_k = (k_at >= 0) & (k_at < plan.k_rows)
-    f_at = r - plan.fold_at
-    is_f = (f_at >= 0) & (f_at < plan.mine)
-    q_lane = lax.broadcasted_iota(jnp.int32, (rows, half_cols), 1)
-    k_lane = lax.broadcasted_iota(jnp.int32, (rows, HD), 1)
-    ws = ws_ref[...].astype(F32)
-
-    def fill(peer, carry):
-        line, pair = peer // plan.pair, peer % plan.pair
-        column = (pair * plan.mine + head) * HD + part * HALF + line * plan.pairs + entry
-        column = jnp.where(is_q, column, -1)
-        at = pl.ds(pl.multiple_of(peer * rows, 8), rows)
-        pick[at, :half_cols] = jnp.where(q_lane == column, 1.0, 0.0)
-        k_column = (k_at // plan.pairs) * HALF + line * plan.pairs + k_at % plan.pairs
-        k_column = jnp.where(is_k, k_column, -1)
-        pick[at, half_cols : half_cols + HD] = jnp.where(k_lane == k_column, 1.0, 0.0)
-        fold = jnp.zeros((rows, HD), F32)
-        my_head = jnp.where(is_f, (group * plan.pair + pair) * plan.mine + f_at, -1)
-        for h in range(plan.heads):
-            fold = jnp.where(my_head == h, ws[h : h + 1], fold)
-        pick[at, half_cols + HD :] = fold
-        return carry
-
-    lax.fori_loop(0, plan.peers, fill, 0, unroll=plan.peers <= 8)
-
     count, depth = board_ref.shape[1], wq.shape[0]
     board_row = board_ref[...]
     board_col = jnp.broadcast_to(board_row.astype(F32), (8, count)).T[:, 0:1].astype(jnp.int32)
@@ -125,7 +94,72 @@
         both = found[at : at + plan.share] + found[boards + at : boards + at + plan.share]
         lists.append(jnp.sum(both, axis=0, keepdims=True))
 
-    for copy in copies[3:]:
+    if plan.pairs % 16 == 0:
+        turn_weights(plan, group, lists, copies[3:], wq, wkv, ws_ref, out_ref)
+    else:
+        pick_weights(plan, group, lists, copies[3:], wq, wkv, ws_ref, out_ref, pick)
+
+
+def turn_weights(plan, group, lists, copies, wq, wkv, ws_ref, out_ref):
+    for copy in copies:
+        copy.wait()
+    q = wq[...].T
+    k = wkv[:, :HD].T
+    folds = matmul(ws_ref[...], wkv[:, HD:], NT)
+    row = lax.broadcasted_iota(jnp.int32, folds.shape, 0)
+    pairs = plan.pairs
+    zeros = jnp.zeros((plan.rows - plan.list_at - 1, folds.shape[1]), F32)
+    for pair in range(plan.pair):
+        first = (group * plan.pair + pair) * plan.mine
+        mine = [jnp.sum(jnp.where(row == first + h, folds, 0.0), axis=0, keepdims=True) for h in range(plan.mine)]
+        for line in range(plan.line):
+            peer = line * plan.pair + pair
+            for part in range(2):
+                entry = part * HALF + line * pairs
+                for h in range(plan.mine):
+                    at = (part * plan.mine + h) * pairs
+                    source = (pair * plan.mine + h) * HD + entry
+                    out_ref[peer, at : at + pairs] = q[source : source + pairs]
+                at = plan.q_rows + part * pairs
+                out_ref[peer, at : at + pairs] = k[entry : entry + pairs]
+            last = jnp.concatenate([*mine, lists[line], zeros], axis=0)
+            out_ref[peer, plan.fold_at :] = last.astype(BF16)
+
+
+def pick_weights(plan, group, lists, copies, wq, wkv, ws_ref, out_ref, pick):
+    rows, half_cols = plan.rows, wq.shape[1]
+    r = lax.broadcasted_iota(jnp.int32, (rows, 1), 0)
+    part = r // (plan.mine * plan.pairs)
+    head = (r // plan.pairs) % plan.mine
+    entry = r % plan.pairs
+    is_q = r < plan.q_rows
+    k_at = r - plan.q_rows
+    is_k = (k_at >= 0) & (k_at < plan.k_rows)
+    f_at = r - plan.fold_at
+    is_f = (f_at >= 0) & (f_at < plan.mine)
+    q_lane = lax.broadcasted_iota(jnp.int32, (rows, half_cols), 1)
+    k_lane = lax.broadcasted_iota(jnp.int32, (rows, HD), 1)
+    ws = ws_ref[...].astype(F32)
+
+    def fill(peer, carry):
+        line, pair = peer // plan.pair, peer % plan.pair
+        column = (pair * plan.mine + head) * HD + part * HALF + line * plan.pairs + entry
+        column = jnp.where(is_q, column, -1)
+        at = pl.ds(pl.multiple_of(peer * rows, 8), rows)
+        pick[at, :half_cols] = jnp.where(q_lane == column, 1.0, 0.0)
+        k_column = (k_at // plan.pairs) * HALF + line * plan.pairs + k_at % plan.pairs
+        k_column = jnp.where(is_k, k_column, -1)
+        pick[at, half_cols : half_cols + HD] = jnp.where(k_lane == k_column, 1.0, 0.0)
+        fold = jnp.zeros((rows, HD), F32)
+        my_head = jnp.where(is_f, (group * plan.pair + pair) * plan.mine + f_at, -1)
+        for h in range(plan.heads):
+            fold = jnp.where(my_head == h, ws[h : h + 1], fold)
+        pick[at, half_cols + HD :] = fold
+        return carry
+
+    lax.fori_loop(0, plan.peers, fill, 0, unroll=plan.peers <= 8)
+
+    for copy in copies:
         copy.wait()
     left = pick[...].astype(BF16)
     total = matmul(left[:, :half_cols], wq[...], NT) + matmul(left[:, half_cols:], wkv[...], NT)
@@ -135,31 +169,47 @@
 
 
 def normalize(table_ref, gain_ref, after_ref, *refs):
-    *outs, gain, held, sems = refs
+    *outs, mark_ref, gain, held, sems = refs
     here = pl.program_id(0)
+    block = table_ref.shape[0]
+    starts = np.cumsum([0] + [out.shape[0] for out in outs])
 
     @pl.when(here == 0)
     def _():
         rows = gain_ref[...].astype(F32)
         gain[...] = jnp.concatenate([rows[r : r + 1] for r in range(rows.shape[0])], axis=1)
-
-    def copy(step):
-        return pltpu.make_async_copy(held.at[step % 2], outs[step], sems.at[step % 2])
+        mark_ref[...] = jnp.zeros_like(mark_ref)
+
+    def copies(step):
+        found = []
+        for out, start in zip(outs, starts.tolist()):
+            low = max(step * block, start)
+            size = min((step + 1) * block, start + out.shape[0]) - low
+            if size > 0:
+                slot, place = step % 2, len(found)
+                source = held.at[slot, pl.ds(low - step * block, size)]
+                found.append(pltpu.make_async_copy(source, out.at[pl.ds(low - start, size)], sems.at[slot, place]))
+        return found
+
+    steps = int(starts[-1]) // block
 
     def one(step):
         if step >= 2:
-            copy(step - 2).wait()
-        half = table_ref.shape[0] // 2
+            for copy in copies(step - 2):
+                copy.wait()
+        half = block // 2
         for at in (slice(0, half), slice(half, 2 * half)):
             raw = table_ref[at].astype(F32)
             inverse = lax.rsqrt(jnp.mean(raw * raw, axis=-1, keepdims=True) + EPS)
             held[step % 2, at] = (raw * inverse * gain[...]).astype(BF16)
-        copy(step).start()
-        if step == len(outs) - 1:
+        for copy in copies(step):
+            copy.start()
+        if step == steps - 1:
             for last in range(max(0, step - 1), step + 1):
-                copy(last).wait()
-
-    for step in range(len(outs)):
+                for copy in copies(last):
+                    copy.wait()
+
+    for step in range(steps):
         pl.when(here == step)(functools.partial(one, step))
 
 
@@ -503,21 +553,21 @@
     across = swap(payload, slab_axes, plan.slab, 2)
 
     block = min(moves, 256)
-    steps = moves // block
-    normed = pl.pallas_call(
+    blocks = (moves // 4, moves * 3 // 8, moves * 3 // 8)
+    *normed, mark = pl.pallas_call(
         normalize,
-        out_shape=[shape((block, width), BF16)] * steps,
-        grid=(steps,),
+        out_shape=[*[shape((size, width), BF16) for size in blocks], shape((8, HD), F32)],
+        grid=(moves // block,),
         in_specs=[
             pl.BlockSpec((block, width), lambda i: (i, 0)),
             pl.BlockSpec((width // HD, HD), lambda i: (0, 0)),
             untouched(),
         ],
-        out_specs=[untouched()] * steps,
+        out_specs=[*[untouched()] * len(blocks), pl.BlockSpec((8, HD), lambda i: (0, 0))],
         scratch_shapes=[
             pltpu.VMEM((1, width), F32),
             pltpu.VMEM((2, block, width), BF16),
-            pltpu.SemaphoreType.DMA((2,)),
+            pltpu.SemaphoreType.DMA((2, 2)),
         ],
         compiler_params=limits(58),
         cost_estimate=cost(moves * width, moves * width // 4),
@@ -527,14 +577,16 @@
     flat = weights.transpose(1, 0, 2).reshape(plan.rows, width) if depth % HD else weights
     sent = (plan.line_rows, moves)
     outs = (shape(sent if plan.direct else (line, *sent), BF16), shape((plan.mine, moves), F32))
-    waits = {0: across, steps - 1: beside}
-    filled, listed = (), None
-    for step in range(steps):
+    across = tied(across, mark)
+    diagonal = swap(across, slab_axes, plan.slab, 1)
+    waits = {0: across, len(blocks) - 1: beside}
+    filled, listed, start = (), None, 0
+    for step, block in enumerate(blocks):
         args = (flat, normed[step], jnp.asarray(turns), *filled)
         more = (waits[step],) if step in waits else ()
         lists = [shape((plan.share, plan.slots), F32)] if step == 0 else []
         made = local_call(
-            functools.partial(project, plan, slice(step * block, (step + 1) * block), step == 0),
+            functools.partial(project, plan, slice(start, start + block), step == 0),
             place,
             (*args, *more),
             [*outs, *lists],
@@ -545,12 +597,10 @@
             block * width,
             {4: 0, 5: 1} if filled else None,
         )
-        filled = made[:2]
+        filled, start = made[:2], start + block
         listed = made[2] if step == 0 else listed
     queries, own_values = filled
     other = swap(listed, slab_axes, plan.slab, pair)
-    across = tied(across, listed)
-    diagonal = swap(across, slab_axes, plan.slab, 1)
     if plan.direct:
         queries = [queries] + [swap(queries, "line", line, step) for step in range(1, line)]
     else:

time: 76.6 us -> 75.5 us (0.986)
  waiting for transfers between devices: 7.68 us -> 5.34 us
  blocking collectives: 13.5 us -> 14.9 us
  Pallas kernels: 33.9 us -> 33 us
    all_to_all x1, waiting for transfers between devices: 3.07 us -> 0.51 us  [per_device(): lax.all_to_all(packed, ('line', 'pair'), split_axis=0, concat_axis=0, til...]
    pallas_call x8 -> x7, Pallas kernels: 23.4 us -> 21.9 us  [local_call(): pl.pallas_call(kernel, out_shape=outs, in_specs=[pl.BlockSpec(memory_spac...]
    all_to_all x1, blocking collectives: 13.5 us -> 14.9 us  [per_device(): lax.all_to_all(parts.reshape(groups * back, plan.share, plan.slots), ('gr...]
  transfers between devices with their start and end apart: 8 -> 8, of which waited for: 4 -> 4; matrix products, arithmetic and copies ran while one was open for 1% -> 1% of each run, Pallas kernels for 29% -> 30%
where the time goes in v13:
time: 75.5 us; the launch traced here: 75.2 us
  Pallas kernels  33 us (44%)
  starting transfers between devices  18.6 us (25%)
  blocking collectives  14.9 us (20%)
  waiting for transfers between devices  5.34 us (7%)
  local copies, waits for them, and re-layouts  2.67 us (4%)
    pallas_call x7, Pallas kernels, local_call(): pl.pallas_call(kernel, out_shape=outs, in_specs=[pl.BlockSpec(memory_spac...  21.9 us
    all_to_all x1, blocking collectives, per_device(): lax.all_to_all(parts.reshape(groups * back, plan.share, plan.slots), ('gr...  14.9 us
    ppermute x7, starting transfers between devices, swap(): return lax.ppermute(x, names, [(at, at ^ step) for at in range(size)])  11.3 us
    pallas_call x1, Pallas kernels, per_device(): pl.pallas_call(normalize, out_shape=[*[shape((size, width), BF16) for siz...  9.99 us
    all_to_all x1, starting transfers between devices, per_device(): lax.all_to_all(packed, ('line', 'pair'), split_axis=0, concat_axis=0, til...  7.26 us
    ppermute x7, waiting for transfers between devices, swap(): return lax.ppermute(x, names, [(at, at ^ step) for at in range(size)])  4.83 us
    unnamed x18, local copies, waits for them, and re-layouts  2.67 us
  transfers between devices with their start and end apart: 8, of which 4 were waited for; matrix products, arithmetic and copies ran while one was open for 1% of the time, Pallas kernels for 30%

profile of v13, /device:TPU:0, one launch (start us, length us, event | category | flops | bytes accessed | tf_op | source)
XLA Modules:
  0.0 75.2 jit_solution(2378237726584841406)
XLA Ops:
  0.0 2.6 %shard_map.91.after_ref = bf16[8,104,512]{2,1,0:T(8,128)(2,1)} custom-call(s32[1]{0:T(128)} %bitcast.place_ref, bf16[512,1024]{1,0:T(8,128)(2,1)} %wq_hbm.1, bf16[512,256]{1,0:T(8,128)(2,1)} %wkv_hbm.1, bf16[8,128]{1,0:T(8,128)(2,1)} %bitcast.17, s32[1,512]{1,0:T(1,128)} %bitcast.13, s32[1,512]{1,0:T(1,128)} %bitcast.19), custom_call_target="tpu_custom_call" | custom-call | tf_op jit(solution)/shard_map/pallas_call | solution.py:468
  2.7 7.3 %all-to-all-start = ((bf16[8,104,512]{2,1,0:T(8,128)(2,1)}), bf16[8,104,512]{2,1,0:T(8,128)(2,1)S(1)}, u32[]{:S(2)}, u32[]{:S(2)}) async-start(bf16[8,104,512]{2,1,0:T(8,128)(2,1)} %shard_map.91.after_ref), calls=%async_computation | async-start | bytes 1703936 | tf_op jit(solution)/shard_map/all_to_all | solution.py:535
  9.9 0.6 pad_add_fusion.place_ref
  10.5 3.0 %shard_map.93 = (bf16[9,256,128]{2,1,0:T(8,128)(2,1)}, s32[1,512]{1,0:T(1,128)}) custom-call(s32[4]{0:T(128)} %pad_add_fusion.place_ref, bf16[8,256,256]{2,1,0:T(8,128)(2,1)} %prefix_hbm.1, bf16[8,128]{1,0:T(8,128)(2,1)} %bitcast.18, s32[1,512]{1,0:T(1,128)} %bitcast.14, bf16[8,104,512]{2,1,0:T(8,128)(2,1)} %shard_map.91.after_ref), custom_call_target="tpu_custom_call" | custom-call | tf_op jit(solution)/shard_map/pallas_call | solution.py:468
  13.6 1.6 %collective-permute-start = (bf16[9,256,128]{2,1,0:T(8,128)(2,1)}, bf16[9,256,128]{2,1,0:T(8,128)(2,1)S(1)}, u32[]{:S(2)}, u32[]{:S(2)}) collective-permute-start(bf16[9,256,128]{2,1,0:T(8,128)(2,1)} %get-tuple-element.23.rest_0_), channel_id=1, source_target_pairs={{0,16},{2,18},{16,0},{18,2},{1,17},{3,19},{17,1},{19,3},{4,20},{6,... | collective-permute-start | bytes 1769480 | tf_op jit(solution)/shard_map/ppermute | solution.py:486
  15.1 2.0 %collective-permute-start.1 = (bf16[9,256,128]{2,1,0:T(8,128)(2,1)}, bf16[9,256,128]{2,1,0:T(8,128)(2,1)S(1)}, u32[]{:S(2)}, u32[]{:S(2)}) collective-permute-start(bf16[9,256,128]{2,1,0:T(8,128)(2,1)} %get-tuple-element.23.rest_0_), channel_id=1, source_target_pairs={{0,2},{2,0},{16,18},{18,16},{1,3},{3,1},{17,19},{19,17},{4,6},{6,4... | collective-permute-start | bytes 1769480 | tf_op jit(solution)/shard_map/ppermute | solution.py:486
  17.2 10.0 %shard_map.92 = (bf16[256,4096]{1,0:T(8,128)(2,1)}, bf16[384,4096]{1,0:T(8,128)(2,1)}, bf16[384,4096]{1,0:T(8,128)(2,1)}, f32[8,128]{1,0:T(8,128)}) custom-call(bf16[1024,4096]{1,0:T(8,128)(2,1)} %table_ref.1, bf16[32,128]{1,0:T(8,128)(2,1)} %bitcast.16, bf16[8,104,512]{2,1,0:T(8,128)(2,1)} %shard_map.91.after_ref), custom_call_target="tpu_custom_call" | custom-call | flops 4194304 | bytes 1048576 | tf_op jit(solution)/shard_map/pallas_call | solution.py:557
  27.2 1.5 %collective-permute-done.refs_0_ = bf16[9,256,128]{2,1,0:T(8,128)(2,1)S(1)} collective-permute-done((bf16[9,256,128]{2,1,0:T(8,128)(2,1)}, bf16[9,256,128]{2,1,0:T(8,128)(2,1)S(1)}, u32[]{:S(2)}, u32[]{:S(2)}) %collective-permute-start) | collective-permute-done | bytes 589856 | tf_op jit(solution)/shard_map/ppermute | solution.py:486
  28.6 0.7 copy-done.3
  29.3 1.7 %collective-permute-start.3 = (bf16[9,256,128]{2,1,0:T(8,128)(2,1)S(1)}, bf16[9,256,128]{2,1,0:T(8,128)(2,1)S(1)}, u32[]{:S(2)}, u32[]{:S(2)}) collective-permute-start(bf16[9,256,128]{2,1,0:T(8,128)(2,1)S(1)} %shard_map.94.refs_0_.rest_2_), channel_id=1, source_target_pairs={{0,2},{2,0},{16,18},{18,16},{1,3},{3,1},{17,19},{19,17},{4,6},{6,4... | collective-permute-start | bytes 1769480 | tf_op jit(solution)/shard_map/ppermute | solution.py:486
  31.0 0.5 all-to-all-done.w_ref
  31.6 1.7 %copy-done.7 = bf16[256,4096]{1,0:T(8,128)(2,1)S(1)} copy-done((bf16[256,4096]{1,0:T(8,128)(2,1)S(1)}, bf16[256,4096]{1,0:T(8,128)(2,1)}, u32[]{:S(2)}) %copy-start.7) | copy-done | bytes 2097176
  33.3 1.4 %shard_map.95 = (bf16[72,1024]{1,0:T(8,128)(2,1)S(1)}, f32[2,1024]{1,0:T(2,128)S(1)}, f32[16,128]{1,0:T(8,128)S(1)}) custom-call(s32[4]{0:T(128)S(1)} %copy-done.2, bf16[8,104,512]{2,1,0:T(8,128)(2,1)S(1)} %all-to-all-done.w_ref, bf16[256,4096]{1,0:T(8,128)(2,1)S(1)} %copy-done.7, f32[4,32,2]{2,1,0:T(8,128)S(1)} %copy-done.8, ...), custom_call_target="tpu_custom_call" | custom-call | flops 2147483648 | bytes 1048576 | tf_op jit(solution)/shard_map/pallas_call | solution.py:468
  34.7 1.6 %shard_map.96 = (bf16[72,1024]{1,0:T(8,128)(2,1)S(1)}, f32[2,1024]{1,0:T(2,128)S(1)}) custom-call(s32[4]{0:T(128)S(1)} %copy-done.2, bf16[8,104,512]{2,1,0:T(8,128)(2,1)S(1)} %all-to-all-done.w_ref, bf16[384,4096]{1,0:T(8,128)(2,1)S(1)} %copy-done.6, f32[4,32,2]{2,1,0:T(8,128)S(1)} %copy-done.8, ...), custom_call_target="tpu_custom_call", output_to_operand_aliasing={{0}: (4, {}), {1}: (5, {})} | custom-call | flops 3221225472 | bytes 1572864 | tf_op jit(solution)/shard_map/pallas_call | solution.py:468
  36.6 1.6 %shard_map.97 = (bf16[72,1024]{1,0:T(8,128)(2,1)S(1)}, f32[2,1024]{1,0:T(2,128)S(1)}) custom-call(s32[4]{0:T(128)S(1)} %copy-done.2, bf16[8,104,512]{2,1,0:T(8,128)(2,1)S(1)} %all-to-all-done.w_ref, bf16[384,4096]{1,0:T(8,128)(2,1)S(1)} %copy-done.5, f32[4,32,2]{2,1,0:T(8,128)S(1)} %copy-done.8, ...), custom_call_target="tpu_custom_call", output_to_operand_aliasing={{0}: (4, {}), {1}: (5, {})} | custom-call | flops 3221225472 | bytes 1572864 | tf_op jit(solution)/shard_map/pallas_call | solution.py:468
  38.2 2.8 %collective-permute-start.6 = (bf16[72,1024]{1,0:T(8,128)(2,1)S(1)}, bf16[72,1024]{1,0:T(8,128)(2,1)S(1)}, u32[]{:S(2)}, u32[]{:S(2)}) collective-permute-start(bf16[72,1024]{1,0:T(8,128)(2,1)S(1)} %get-tuple-element.33.rest_4_), channel_id=1, source_target_pairs={{0,12},{4,8},{8,4},{12,0},{1,13},{5,9},{9,5},{13,1},{2,14},{6,10},... | collective-permute-start | bytes 442376 | tf_op jit(solution)/shard_map/ppermute | solution.py:486
  41.3 1.3 %collective-permute-start.4 = (bf16[72,1024]{1,0:T(8,128)(2,1)S(1)}, bf16[72,1024]{1,0:T(8,128)(2,1)S(1)}, u32[]{:S(2)}, u32[]{:S(2)}) collective-permute-start(bf16[72,1024]{1,0:T(8,128)(2,1)S(1)} %get-tuple-element.33.rest_4_), channel_id=1, source_target_pairs={{0,4},{4,0},{8,12},{12,8},{1,5},{5,1},{9,13},{13,9},{2,6},{6,2},{1... | collective-permute-start | bytes 442376 | tf_op jit(solution)/shard_map/ppermute | solution.py:486
  42.7 1.5 %collective-permute-start.2 = (f32[16,128]{1,0:T(8,128)S(1)}, f32[16,128]{1,0:T(8,128)S(1)}, u32[]{:S(2)}, u32[]{:S(2)}) collective-permute-start(f32[16,128]{1,0:T(8,128)S(1)} %get-tuple-element.30.own_ref), channel_id=1, source_target_pairs={{0,16},{2,18},{16,0},{18,2},{1,17},{3,19},{17,1},{19,3},{4,20},{6,... | collective-permute-start | bytes 24584 | tf_op jit(solution)/shard_map/ppermute | solution.py:486
  44.2 2.1 %collective-permute-done.2.other_ref = f32[16,128]{1,0:T(8,128)S(1)} collective-permute-done((f32[16,128]{1,0:T(8,128)S(1)}, f32[16,128]{1,0:T(8,128)S(1)}, u32[]{:S(2)}, u32[]{:S(2)}) %collective-permute-start.2) | collective-permute-done | bytes 8224 | tf_op jit(solution)/shard_map/ppermute | solution.py:486
  46.3 4.6 %shard_map.98 = (bf16[8,1024,512]{2,1,0:T(8,128)(2,1)S(1)}, f32[3,8,256,256]{3,2,1,0:T(8,128)S(1)}) custom-call(s32[4]{0:T(128)S(1)} %copy-done.2, f32[16,128]{1,0:T(8,128)S(1)} %get-tuple-element.30.own_ref, f32[16,128]{1,0:T(8,128)S(1)} %collective-permute-done.2.other_ref, bf16[9,256,128]{2,1,0:T(8,128)(2,1)S(1)} %copy-done, ...), custom_call_target="tpu_custom_call" | custom-call | flops 1000000000 | bytes 1000000 | tf_op jit(solution)/shard_map/pallas_call | solution.py:468
  51.0 1.2 %collective-permute-done.5.rest_6_ = bf16[72,1024]{1,0:T(8,128)(2,1)S(1)} collective-permute-done((bf16[72,1024]{1,0:T(8,128)(2,1)S(1)}, bf16[72,1024]{1,0:T(8,128)(2,1)S(1)}, u32[]{:S(2)}, u32[]{:S(2)}) %collective-permute-start.5) | collective-permute-done | bytes 147488 | tf_op jit(solution)/shard_map/ppermute | solution.py:486
  52.2 7.0 %shard_map.99 = f32[2,16,16,128]{3,2,1,0:T(8,128)S(1)} custom-call(s32[4]{0:T(128)S(1)} %copy-done.2, f32[2,1024]{1,0:T(2,128)S(1)} %get-tuple-element.29.vo_ref, f32[16,128]{1,0:T(8,128)S(1)} %get-tuple-element.30.own_ref, f32[16,128]{1,0:T(8,128)S(1)} %collective-permute-done.2.other_ref, bf16[8,1024,512]{2,1,0:T(8,128)(2,1)S(1)} %get-tuple-element.31.chosen_ref, ...), custom_call_target="tpu_custom_call" | custom-call | tf_op jit(solution)/shard_map/pallas_call | solution.py:468
  59.2 14.9 %all_to_all.10 = f32[32,16,128]{2,1,0:T(8,128)S(1)} all-to-all(f32[32,16,128]{2,1,0:T(8,128)S(1)} %bitcast.11), channel_id=1, replica_groups=mesh['groups'=2,'line'=4,'pair'=2,'tensor'=2] {'groups','line','pair','t..., dimensions={0} | all-to-all | bytes 524288 | tf_op jit(solution)/shard_map/all_to_all | solution.py:638
  74.1 1.1 %shard_map.100 = f32[1,512]{1,0:T(1,128)} custom-call(f32[2,4,4,16,128]{4,3,2,1,0:T(8,128)S(1)} %bitcast.12, s32[1,512]{1,0:T(1,128)S(1)} %bitcast.15, s32[1,512]{1,0:T(1,128)S(1)} %copy-done.4), custom_call_target="tpu_custom_call" | custom-call | tf_op jit(solution)/shard_map/pallas_call | solution.py:646
  (22 shorter events, 0.5 us)
Async XLA Ops:
  2.7 28.9 %all-to-all-start = ((bf16[8,104,512]{2,1,0:T(8,128)(2,1)}), bf16[8,104,512]{2,1,0:T(8,128)(2,1)S(1)}, u32[]{:S(2)}, u32[]{:S(2)}) async-start(bf16[8,104,512]{2,1,0:T(8,128)(2,1)} %shard_map.91.after_ref), calls=%async_computation | async-start | bytes 1703936 | tf_op jit(solution)/shard_map/all_to_all | solution.py:535
  9.9 21.6 %copy-start.8 = (f32[4,32,2]{2,1,0:T(8,128)S(1)}, f32[4,32,2]{2,1,0:T(8,128)}, u32[]{:S(2)}) copy-start(f32[4,32,2]{2,1,0:T(8,128)} %constant.17.clone.turn_ref) | copy-start | bytes 3076
  10.5 21.0 %copy-start.2 = (s32[4]{0:T(128)S(1)}, s32[4]{0:T(128)}, u32[]{:S(2)}) copy-start(s32[4]{0:T(128)} %pad_add_fusion.place_ref) | copy-start | bytes 52
  13.6 15.1 %collective-permute-start = (bf16[9,256,128]{2,1,0:T(8,128)(2,1)}, bf16[9,256,128]{2,1,0:T(8,128)(2,1)S(1)}, u32[]{:S(2)}, u32[]{:S(2)}) collective-permute-start(bf16[9,256,128]{2,1,0:T(8,128)(2,1)} %get-tuple-element.23.rest_0_), channel_id=1, source_target_pairs={{0,16},{2,18},{16,0},{18,2},{1,17},{3,19},{17,1},{19,3},{4,20},{6,... | collective-permute-start | bytes 1769480 | tf_op jit(solution)/shard_map/ppermute | solution.py:486
  15.1 21.2 %collective-permute-start.1 = (bf16[9,256,128]{2,1,0:T(8,128)(2,1)}, bf16[9,256,128]{2,1,0:T(8,128)(2,1)S(1)}, u32[]{:S(2)}, u32[]{:S(2)}) collective-permute-start(bf16[9,256,128]{2,1,0:T(8,128)(2,1)} %get-tuple-element.23.rest_0_), channel_id=1, source_target_pairs={{0,2},{2,0},{16,18},{18,16},{1,3},{3,1},{17,19},{19,17},{4,6},{6,4... | collective-permute-start | bytes 1769480 | tf_op jit(solution)/shard_map/ppermute | solution.py:486
  28.6 0.7 copy-start.3
  29.3 21.7 %collective-permute-start.3 = (bf16[9,256,128]{2,1,0:T(8,128)(2,1)S(1)}, bf16[9,256,128]{2,1,0:T(8,128)(2,1)S(1)}, u32[]{:S(2)}, u32[]{:S(2)}) collective-permute-start(bf16[9,256,128]{2,1,0:T(8,128)(2,1)S(1)} %shard_map.94.refs_0_.rest_2_), channel_id=1, source_target_pairs={{0,2},{2,0},{16,18},{18,16},{1,3},{3,1},{17,19},{19,17},{4,6},{6,4... | collective-permute-start | bytes 1769480 | tf_op jit(solution)/shard_map/ppermute | solution.py:486
  31.6 3.2 %copy-start.6 = (bf16[384,4096]{1,0:T(8,128)(2,1)S(1)}, bf16[384,4096]{1,0:T(8,128)(2,1)}, u32[]{:S(2)}) copy-start(bf16[384,4096]{1,0:T(8,128)(2,1)} %get-tuple-element.21.normed_ref) | copy-start | bytes 9437188
  31.6 1.7 %copy-start.7 = (bf16[256,4096]{1,0:T(8,128)(2,1)S(1)}, bf16[256,4096]{1,0:T(8,128)(2,1)}, u32[]{:S(2)}) copy-start(bf16[256,4096]{1,0:T(8,128)(2,1)} %get-tuple-element.22.normed_ref) | copy-start | bytes 6291460
  34.7 1.9 %copy-start.5 = (bf16[384,4096]{1,0:T(8,128)(2,1)S(1)}, bf16[384,4096]{1,0:T(8,128)(2,1)}, u32[]{:S(2)}) copy-start(bf16[384,4096]{1,0:T(8,128)(2,1)} %get-tuple-element.20.normed_ref) | copy-start | bytes 9437188
  36.4 10.0 %copy-start = (bf16[9,256,128]{2,1,0:T(8,128)(2,1)S(1)}, bf16[9,256,128]{2,1,0:T(8,128)(2,1)}, u32[]{:S(2)}) copy-start(bf16[9,256,128]{2,1,0:T(8,128)(2,1)} %get-tuple-element.23.rest_0_) | copy-start | bytes 1769476
  38.2 12.8 %collective-permute-start.6 = (bf16[72,1024]{1,0:T(8,128)(2,1)S(1)}, bf16[72,1024]{1,0:T(8,128)(2,1)S(1)}, u32[]{:S(2)}, u32[]{:S(2)}) collective-permute-start(bf16[72,1024]{1,0:T(8,128)(2,1)S(1)} %get-tuple-element.33.rest_4_), channel_id=1, source_target_pairs={{0,12},{4,8},{8,4},{12,0},{1,13},{5,9},{9,5},{13,1},{2,14},{6,10},... | collective-permute-start | bytes 442376 | tf_op jit(solution)/shard_map/ppermute | solution.py:486
  41.1 11.2 %collective-permute-start.5 = (bf16[72,1024]{1,0:T(8,128)(2,1)S(1)}, bf16[72,1024]{1,0:T(8,128)(2,1)S(1)}, u32[]{:S(2)}, u32[]{:S(2)}) collective-permute-start(bf16[72,1024]{1,0:T(8,128)(2,1)S(1)} %get-tuple-element.33.rest_4_), channel_id=1, source_target_pairs={{0,8},{4,12},{8,0},{12,4},{1,9},{5,13},{9,1},{13,5},{2,10},{6,14},... | collective-permute-start | bytes 442376 | tf_op jit(solution)/shard_map/ppermute | solution.py:486
  41.3 10.9 %collective-permute-start.4 = (bf16[72,1024]{1,0:T(8,128)(2,1)S(1)}, bf16[72,1024]{1,0:T(8,128)(2,1)S(1)}, u32[]{:S(2)}, u32[]{:S(2)}) collective-permute-start(bf16[72,1024]{1,0:T(8,128)(2,1)S(1)} %get-tuple-element.33.rest_4_), channel_id=1, source_target_pairs={{0,4},{4,0},{8,12},{12,8},{1,5},{5,1},{9,13},{13,9},{2,6},{6,2},{1... | collective-permute-start | bytes 442376 | tf_op jit(solution)/shard_map/ppermute | solution.py:486
  42.7 3.7 %collective-permute-start.2 = (f32[16,128]{1,0:T(8,128)S(1)}, f32[16,128]{1,0:T(8,128)S(1)}, u32[]{:S(2)}, u32[]{:S(2)}) collective-permute-start(f32[16,128]{1,0:T(8,128)S(1)} %get-tuple-element.30.own_ref), channel_id=1, source_target_pairs={{0,16},{2,18},{16,0},{18,2},{1,17},{3,19},{17,1},{19,3},{4,20},{6,... | collective-permute-start | bytes 24584 | tf_op jit(solution)/shard_map/ppermute | solution.py:486
  52.2 21.9 %copy-start.1 = (s32[512,1]{0,1:T(1,128)S(1)}, s32[512,1]{0,1:T(1,128)}, u32[]{:S(2)}) copy-start(s32[512,1]{0,1:T(1,128)} %param.11) | copy-start | bytes 6148
  52.2 21.9 %copy-start.4 = (s32[1,512]{1,0:T(1,128)S(1)}, s32[1,512]{1,0:T(1,128)}, u32[]{:S(2)}) copy-start(s32[1,512]{1,0:T(1,128)} %get-tuple-element.34.slot_ref) | copy-start | bytes 6148

commit v14 on v13

--- a/solution.py
+++ b/solution.py
@@ -168,49 +168,26 @@
         out_ref[peer] = jnp.where(r == plan.list_at, lists[peer // plan.pair], mine).astype(BF16)
 
 
-def normalize(table_ref, gain_ref, after_ref, *refs):
-    *outs, mark_ref, gain, held, sems = refs
-    here = pl.program_id(0)
-    block = table_ref.shape[0]
-    starts = np.cumsum([0] + [out.shape[0] for out in outs])
-
-    @pl.when(here == 0)
-    def _():
-        rows = gain_ref[...].astype(F32)
-        gain[...] = jnp.concatenate([rows[r : r + 1] for r in range(rows.shape[0])], axis=1)
-        mark_ref[...] = jnp.zeros_like(mark_ref)
-
-    def copies(step):
-        found = []
-        for out, start in zip(outs, starts.tolist()):
-            low = max(step * block, start)
-            size = min((step + 1) * block, start + out.shape[0]) - low
-            if size > 0:
-                slot, place = step % 2, len(found)
-                source = held.at[slot, pl.ds(low - step * block, size)]
-                found.append(pltpu.make_async_copy(source, out.at[pl.ds(low - start, size)], sems.at[slot, place]))
-        return found
-
-    steps = int(starts[-1]) // block
-
-    def one(step):
-        if step >= 2:
-            for copy in copies(step - 2):
-                copy.wait()
-        half = block // 2
-        for at in (slice(0, half), slice(half, 2 * half)):
-            raw = table_ref[at].astype(F32)
-            inverse = lax.rsqrt(jnp.mean(raw * raw, axis=-1, keepdims=True) + EPS)
-            held[step % 2, at] = (raw * inverse * gain[...]).astype(BF16)
-        for copy in copies(step):
-            copy.start()
-        if step == steps - 1:
-            for last in range(max(0, step - 1), step + 1):
-                for copy in copies(last):
-                    copy.wait()
-
+def normalize(table_hbm, gain_ref, after_ref, out_ref, mark_ref, gain, buffers, sems):
+    mark_ref[...] = jnp.zeros_like(mark_ref)
+    held, block, _ = buffers.shape
+    steps = table_hbm.shape[0] // block
+
+    def copy(step):
+        source = table_hbm.at[pl.ds(step * block, block)]
+        return pltpu.make_async_copy(source, buffers.at[step % held], sems.at[step % held])
+
+    for step in range(min(held, steps)):
+        copy(step).start()
+    rows = gain_ref[...].astype(F32)
+    gain[...] = jnp.concatenate([rows[r : r + 1] for r in range(rows.shape[0])], axis=1)
     for step in range(steps):
-        pl.when(here == step)(functools.partial(one, step))
+        copy(step).wait()
+        raw = buffers[step % held].astype(F32)
+        inverse = lax.rsqrt(jnp.mean(raw * raw, axis=-1, keepdims=True) + EPS)
+        out_ref[step * block : (step + 1) * block] = (raw * inverse * gain[...]).astype(BF16)
+        if step + held < steps:
+            copy(step + held).start()
 
 
 def read_lists(plan, w_ref, out_ref):
@@ -238,46 +215,47 @@
     out_ref[...] = jnp.sum(listed.reshape(share, peers, plan.slots), axis=1)
 
 
-def project(plan, at, lists, place_ref, w_ref, normed_ref, turn_ref, *refs):
-    if lists:
-        *refs, list_ref = refs
-        read_lists(plan, w_ref, list_ref)
-    q_ref, vo_ref = refs[-2:]
-    if len(w_ref.shape) == 3:
-        depth = w_ref.shape[2]
-        total = None
-        for s in range(w_ref.shape[0]):
-            term = matmul(w_ref[s], normed_ref[:, s * depth : (s + 1) * depth], NT)
-            total = term if total is None else total + term
-    else:
-        total = matmul(w_ref[...], normed_ref[...], NT)
+def project(plan, place_ref, w_ref, normed_ref, turn_ref, after_ref, q_ref, vo_ref, list_ref):
+    read_lists(plan, w_ref, list_ref)
     turns = turn_ref[place_ref[LINE]]
     half, k_half = plan.q_rows // 2, plan.k_rows // 2
     cosine, sine = turns[:, 0:1], turns[:, 1:2]
     cos_k, sin_k = cosine[:k_half], sine[:k_half]
-    first, second = total[:half], total[half : 2 * half]
-    f_first = (first * cosine - second * sine).astype(BF16).astype(F32)
-    f_second = (second * cosine + first * sine).astype(BF16).astype(F32)
-    first, second = total[plan.q_rows : plan.q_rows + k_half], total[plan.q_rows + k_half : plan.fold_at]
-    k_first = (first * cos_k - second * sin_k).astype(BF16).astype(F32)
-    k_second = (second * cos_k + first * sin_k).astype(BF16).astype(F32)
-    logits, tails = [], []
-    for h in range(plan.mine):
-        own = slice(h * k_half, (h + 1) * k_half)
-        logit = jnp.sum(f_first[own] * k_first + f_second[own] * k_second, axis=0, keepdims=True)
-        logits.append(logit.astype(BF16).astype(F32))
-        tails.append(logit - logits[-1])
-    pad = plan.line_rows - plan.q_rows - 2 * plan.mine
-    pieces = [f_first, f_second, *logits, *tails]
-    if pad:
-        pieces.append(jnp.zeros((pad, total.shape[1]), F32))
-    out = jnp.concatenate(pieces, axis=0).astype(BF16)
-    if plan.direct:
-        q_ref[:, at] = out
-    else:
-        for line in range(plan.line):
-            q_ref[line, :, at] = out
-    vo_ref[:, at] = total[plan.fold_at : plan.list_at]
+    moves = normed_ref.shape[0]
+    block = min(moves, 512)
+    for start in range(0, moves, block):
+        at = slice(start, start + block)
+        if len(w_ref.shape) == 3:
+            depth = w_ref.shape[2]
+            total = None
+            for s in range(w_ref.shape[0]):
+                term = matmul(w_ref[s], normed_ref[at, s * depth : (s + 1) * depth], NT)
+                total = term if total is None else total + term
+        else:
+            total = matmul(w_ref[...], normed_ref[at, :], NT)
+        first, second = total[:half], total[half : 2 * half]
+        f_first = (first * cosine - second * sine).astype(BF16).astype(F32)
+        f_second = (second * cosine + first * sine).astype(BF16).astype(F32)
+        first, second = total[plan.q_rows : plan.q_rows + k_half], total[plan.q_rows + k_half : plan.fold_at]
+        k_first = (first * cos_k - second * sin_k).astype(BF16).astype(F32)
+        k_second = (second * cos_k + first * sin_k).astype(BF16).astype(F32)
+        logits, tails = [], []
+        for h in range(plan.mine):
+            own = slice(h * k_half, (h + 1) * k_half)
+            logit = jnp.sum(f_first[own] * k_first + f_second[own] * k_second, axis=0, keepdims=True)
+            logits.append(logit.astype(BF16).astype(F32))
+            tails.append(logit - logits[-1])
+        pad = plan.line_rows - plan.q_rows - 2 * plan.mine
+        pieces = [f_first, f_second, *logits, *tails]
+        if pad:
+            pieces.append(jnp.zeros((pad, block), F32))
+        out = jnp.concatenate(pieces, axis=0).astype(BF16)
+        if plan.direct:
+            q_ref[:, at] = out
+        else:
+            for line in range(plan.line):
+                q_ref[line, :, at] = out
+        vo_ref[:, at] = total[plan.fold_at : plan.list_at]
 
 
 def tied(x, *others):
@@ -552,24 +530,19 @@
     beside = swap(payload, slab_axes, plan.slab, 1)
     across = swap(payload, slab_axes, plan.slab, 2)
 
-    block = min(moves, 256)
-    blocks = (moves // 4, moves * 3 // 8, moves * 3 // 8)
-    *normed, mark = pl.pallas_call(
+    block = min(moves, 128)
+    vmem = pl.BlockSpec(memory_space=pltpu.VMEM)
+    normed, mark = pl.pallas_call(
         normalize,
-        out_shape=[*[shape((size, width), BF16) for size in blocks], shape((8, HD), F32)],
-        grid=(moves // block,),
-        in_specs=[
-            pl.BlockSpec((block, width), lambda i: (i, 0)),
-            pl.BlockSpec((width // HD, HD), lambda i: (0, 0)),
-            untouched(),
-        ],
-        out_specs=[*[untouched()] * len(blocks), pl.BlockSpec((8, HD), lambda i: (0, 0))],
+        out_shape=(pltpu.VMEM((moves, width), BF16), shape((8, HD), F32)),
+        in_specs=[untouched(), vmem, untouched()],
+        out_specs=(vmem, vmem),
         scratch_shapes=[
             pltpu.VMEM((1, width), F32),
-            pltpu.VMEM((2, block, width), BF16),
-            pltpu.SemaphoreType.DMA((2, 2)),
+            pltpu.VMEM((3, block, width), BF16),
+            pltpu.SemaphoreType.DMA((3,)),
         ],
-        compiler_params=limits(58),
+        compiler_params=limits(48),
         cost_estimate=cost(moves * width, moves * width // 4),
     )(move_table, norm_gain.reshape(width // HD, HD), packed)
     turns = turn_table(prefix_len).reshape(line, 1, plan.pairs, 2)
@@ -579,27 +552,18 @@
     outs = (shape(sent if plan.direct else (line, *sent), BF16), shape((plan.mine, moves), F32))
     across = tied(across, mark)
     diagonal = swap(across, slab_axes, plan.slab, 1)
-    waits = {0: across, len(blocks) - 1: beside}
-    filled, listed, start = (), None, 0
-    for step, block in enumerate(blocks):
-        args = (flat, normed[step], jnp.asarray(turns), *filled)
-        more = (waits[step],) if step in waits else ()
-        lists = [shape((plan.share, plan.slots), F32)] if step == 0 else []
-        made = local_call(
-            functools.partial(project, plan, slice(start, start + block), step == 0),
-            place,
-            (*args, *more),
-            [*outs, *lists],
-            (),
-            16,
-            range(len(args), len(args) + len(more)),
-            2 * block * width * 1024,
-            block * width,
-            {4: 0, 5: 1} if filled else None,
-        )
-        filled, start = made[:2], start + block
-        listed = made[2] if step == 0 else listed
-    queries, own_values = filled
+    queries, own_values, listed = local_call(
+        functools.partial(project, plan),
+        place,
+        (flat, normed, jnp.asarray(turns), across),
+        (*outs, shape((plan.share, plan.slots), F32)),
+        (),
+        20,
+        (3,),
+        2 * moves * width * 256,
+        2 * moves * width,
+    )
+    queries = tied(queries, beside)
     other = swap(listed, slab_axes, plan.slab, pair)
     if plan.direct:
         queries = [queries] + [swap(queries, "line", line, step) for step in range(1, line)]

time: 75.5 us -> 76 us (level)
  local copies, waits for them, and re-layouts: 2.67 us -> 7.3 us
  Pallas kernels: 33 us -> 28.9 us
    unnamed x18 -> x16, local copies, waits for them, and re-layouts: 2.67 us -> 7.3 us
    pallas_call x1, Pallas kernels: 9.99 us -> 6.73 us  [per_device(): pl.pallas_call(normalize, out_shape=(pltpu.VMEM((moves, width), BF16), sh...]
    pallas_call x7 -> x5, Pallas kernels: 21.9 us -> 21.1 us  [local_call(): pl.pallas_call(kernel, out_shape=outs, in_specs=[pl.BlockSpec(memory_spac...]
  transfers between devices with their start and end apart: 8 -> 8, of which waited for: 4 -> 4; matrix products, arithmetic and copies ran while one was open for 1% -> 1% of each run, Pallas kernels for 30% -> 23%
where the time goes in v14:
time: 76 us; the launch traced here: 75.7 us
  Pallas kernels  28.9 us (38%)
  starting transfers between devices  18.6 us (24%)
  blocking collectives  14.9 us (20%)
  local copies, waits for them, and re-layouts  7.3 us (10%)
  waiting for transfers between devices  5.28 us (7%)
    pallas_call x5, Pallas kernels, local_call(): pl.pallas_call(kernel, out_shape=outs, in_specs=[pl.BlockSpec(memory_spac...  21.1 us
    all_to_all x1, blocking collectives, per_device(): lax.all_to_all(parts.reshape(groups * back, plan.share, plan.slots), ('gr...  14.9 us
    ppermute x7, starting transfers between devices, swap(): return lax.ppermute(x, names, [(at, at ^ step) for at in range(size)])  11.3 us
    unnamed x16, local copies, waits for them, and re-layouts  7.3 us
    all_to_all x1, starting transfers between devices, per_device(): lax.all_to_all(packed, ('line', 'pair'), split_axis=0, concat_axis=0, til...  7.27 us
    pallas_call x1, Pallas kernels, per_device(): pl.pallas_call(normalize, out_shape=(pltpu.VMEM((moves, width), BF16), sh...  6.73 us
    ppermute x7, waiting for transfers between devices, swap(): return lax.ppermute(x, names, [(at, at ^ step) for at in range(size)])  4.82 us
  transfers between devices with their start and end apart: 8, of which 4 were waited for; matrix products, arithmetic and copies ran while one was open for 1% of the time, Pallas kernels for 23%

profile of v14, /device:TPU:0, one launch (start us, length us, event | category | flops | bytes accessed | tf_op | source)
XLA Modules:
  0.0 75.7 jit_solution(11829079485142746361)
XLA Ops:
  0.0 2.7 %shard_map.91.after_ref = bf16[8,104,512]{2,1,0:T(8,128)(2,1)} custom-call(s32[1]{0:T(128)} %bitcast.place_ref, bf16[512,1024]{1,0:T(8,128)(2,1)} %wq_hbm.1, bf16[512,256]{1,0:T(8,128)(2,1)} %wkv_hbm.1, bf16[8,128]{1,0:T(8,128)(2,1)} %bitcast.17, s32[1,512]{1,0:T(1,128)} %bitcast.13, s32[1,512]{1,0:T(1,128)} %bitcast.19), custom_call_target="tpu_custom_call" | custom-call | tf_op jit(solution)/shard_map/pallas_call | solution.py:446
  2.7 7.3 %all-to-all-start = ((bf16[8,104,512]{2,1,0:T(8,128)(2,1)}), bf16[8,104,512]{2,1,0:T(8,128)(2,1)S(1)}, u32[]{:S(2)}, u32[]{:S(2)}) async-start(bf16[8,104,512]{2,1,0:T(8,128)(2,1)} %shard_map.91.after_ref), calls=%async_computation | async-start | bytes 1703936 | tf_op jit(solution)/shard_map/all_to_all | solution.py:513
  10.0 0.7 pad_add_fusion.place_ref
  10.6 3.0 %shard_map.93 = (bf16[9,256,128]{2,1,0:T(8,128)(2,1)}, s32[1,512]{1,0:T(1,128)}) custom-call(s32[4]{0:T(128)} %pad_add_fusion.place_ref, bf16[8,256,256]{2,1,0:T(8,128)(2,1)} %prefix_hbm.1, bf16[8,128]{1,0:T(8,128)(2,1)} %bitcast.18, s32[1,512]{1,0:T(1,128)} %bitcast.14, bf16[8,104,512]{2,1,0:T(8,128)(2,1)} %shard_map.91.after_ref), custom_call_target="tpu_custom_call" | custom-call | tf_op jit(solution)/shard_map/pallas_call | solution.py:446
  13.6 1.6 %collective-permute-start = (bf16[9,256,128]{2,1,0:T(8,128)(2,1)}, bf16[9,256,128]{2,1,0:T(8,128)(2,1)S(1)}, u32[]{:S(2)}, u32[]{:S(2)}) collective-permute-start(bf16[9,256,128]{2,1,0:T(8,128)(2,1)} %get-tuple-element.15.rest_0_), channel_id=1, source_target_pairs={{0,16},{2,18},{16,0},{18,2},{1,17},{3,19},{17,1},{19,3},{4,20},{6,... | collective-permute-start | bytes 1769480 | tf_op jit(solution)/shard_map/ppermute | solution.py:464
  15.2 2.0 %collective-permute-start.2 = (bf16[9,256,128]{2,1,0:T(8,128)(2,1)}, bf16[9,256,128]{2,1,0:T(8,128)(2,1)S(1)}, u32[]{:S(2)}, u32[]{:S(2)}) collective-permute-start(bf16[9,256,128]{2,1,0:T(8,128)(2,1)} %get-tuple-element.15.rest_0_), channel_id=1, source_target_pairs={{0,2},{2,0},{16,18},{18,16},{1,3},{3,1},{17,19},{19,17},{4,6},{6,4... | collective-permute-start | bytes 1769480 | tf_op jit(solution)/shard_map/ppermute | solution.py:464
  17.3 6.7 %shard_map.92 = (bf16[1024,4096]{1,0:T(8,128)(2,1)S(1)}, f32[8,128]{1,0:T(8,128)}) custom-call(bf16[1024,4096]{1,0:T(8,128)(2,1)} %table_hbm.1, bf16[32,128]{1,0:T(8,128)(2,1)} %bitcast.16, bf16[8,104,512]{2,1,0:T(8,128)(2,1)} %shard_map.91.after_ref), custom_call_target="tpu_custom_call" | custom-call | flops 4194304 | bytes 1048576 | tf_op jit(solution)/shard_map/pallas_call | solution.py:535
  24.0 3.2 %copy-done = bf16[1024,4096]{1,0:T(8,128)(2,1)} copy-done((bf16[1024,4096]{1,0:T(8,128)(2,1)}, bf16[1024,4096]{1,0:T(8,128)(2,1)S(1)}, u32[]{:S(2)}) %copy-start) | copy-done | bytes 8388632
  27.2 1.5 %collective-permute-done.refs_0_ = bf16[9,256,128]{2,1,0:T(8,128)(2,1)S(1)} collective-permute-done((bf16[9,256,128]{2,1,0:T(8,128)(2,1)}, bf16[9,256,128]{2,1,0:T(8,128)(2,1)S(1)}, u32[]{:S(2)}, u32[]{:S(2)}) %collective-permute-start) | collective-permute-done | bytes 589856 | tf_op jit(solution)/shard_map/ppermute | solution.py:464
  28.7 0.7 copy-done.6
  29.4 1.7 %collective-permute-start.3 = (bf16[9,256,128]{2,1,0:T(8,128)(2,1)S(1)}, bf16[9,256,128]{2,1,0:T(8,128)(2,1)S(1)}, u32[]{:S(2)}, u32[]{:S(2)}) collective-permute-start(bf16[9,256,128]{2,1,0:T(8,128)(2,1)S(1)} %shard_map.94.after_ref.rest_2_), channel_id=1, source_target_pairs={{0,2},{2,0},{16,18},{18,16},{1,3},{3,1},{17,19},{19,17},{4,6},{6,4... | collective-permute-start | bytes 1769480 | tf_op jit(solution)/shard_map/ppermute | solution.py:464
  31.1 0.5 all-to-all-done.w_ref
  31.6 3.4 %copy-done.1 = bf16[1024,4096]{1,0:T(8,128)(2,1)S(1)} copy-done((bf16[1024,4096]{1,0:T(8,128)(2,1)S(1)}, bf16[1024,4096]{1,0:T(8,128)(2,1)}, u32[]{:S(2)}) %copy-start.1) | copy-done | bytes 8388632
  35.0 3.4 %shard_map.95 = (bf16[72,1024]{1,0:T(8,128)(2,1)S(1)}, f32[2,1024]{1,0:T(2,128)S(1)}, f32[16,128]{1,0:T(8,128)S(1)}) custom-call(s32[4]{0:T(128)S(1)} %copy-done.5, bf16[8,104,512]{2,1,0:T(8,128)(2,1)S(1)} %all-to-all-done.w_ref, bf16[1024,4096]{1,0:T(8,128)(2,1)S(1)} %copy-done.1, f32[4,32,2]{2,1,0:T(8,128)S(1)} %copy-done.3, ...), custom_call_target="tpu_custom_call" | custom-call | flops 2147483648 | bytes 8388608 | tf_op jit(solution)/shard_map/pallas_call | solution.py:446
  38.3 0.0 collective-permute-done.2.rest_1_.refs_1_
  38.4 2.9 %collective-permute-start.6 = (bf16[72,1024]{1,0:T(8,128)(2,1)S(1)}, bf16[72,1024]{1,0:T(8,128)(2,1)S(1)}, u32[]{:S(2)}, u32[]{:S(2)}) collective-permute-start(bf16[72,1024]{1,0:T(8,128)(2,1)S(1)} %shard_map.97.rest_4_), channel_id=1, source_target_pairs={{0,12},{4,8},{8,4},{12,0},{1,13},{5,9},{9,5},{13,1},{2,14},{6,10},... | collective-permute-start | bytes 442376 | tf_op jit(solution)/shard_map/ppermute | solution.py:464
  41.2 1.6 %collective-permute-start.4 = (bf16[72,1024]{1,0:T(8,128)(2,1)S(1)}, bf16[72,1024]{1,0:T(8,128)(2,1)S(1)}, u32[]{:S(2)}, u32[]{:S(2)}) collective-permute-start(bf16[72,1024]{1,0:T(8,128)(2,1)S(1)} %shard_map.97.rest_4_), channel_id=1, source_target_pairs={{0,4},{4,0},{8,12},{12,8},{1,5},{5,1},{9,13},{13,9},{2,6},{6,2},{1... | collective-permute-start | bytes 442376 | tf_op jit(solution)/shard_map/ppermute | solution.py:464
  42.8 1.5 %collective-permute-start.1 = (f32[16,128]{1,0:T(8,128)S(1)}, f32[16,128]{1,0:T(8,128)S(1)}, u32[]{:S(2)}, u32[]{:S(2)}) collective-permute-start(f32[16,128]{1,0:T(8,128)S(1)} %get-tuple-element.18.own_ref), channel_id=1, source_target_pairs={{0,16},{2,18},{16,0},{18,2},{1,17},{3,19},{17,1},{19,3},{4,20},{6,... | collective-permute-start | bytes 24584 | tf_op jit(solution)/shard_map/ppermute | solution.py:464
  44.3 2.1 %collective-permute-done.1.other_ref = f32[16,128]{1,0:T(8,128)S(1)} collective-permute-done((f32[16,128]{1,0:T(8,128)S(1)}, f32[16,128]{1,0:T(8,128)S(1)}, u32[]{:S(2)}, u32[]{:S(2)}) %collective-permute-start.1) | collective-permute-done | bytes 8224 | tf_op jit(solution)/shard_map/ppermute | solution.py:464
  46.5 4.7 %shard_map.96 = (bf16[8,1024,512]{2,1,0:T(8,128)(2,1)S(1)}, f32[3,8,256,256]{3,2,1,0:T(8,128)S(1)}) custom-call(s32[4]{0:T(128)S(1)} %copy-done.5, f32[16,128]{1,0:T(8,128)S(1)} %get-tuple-element.18.own_ref, f32[16,128]{1,0:T(8,128)S(1)} %collective-permute-done.1.other_ref, bf16[9,256,128]{2,1,0:T(8,128)(2,1)S(1)} %copy-done.2, ...), custom_call_target="tpu_custom_call" | custom-call | flops 1000000000 | bytes 1000000 | tf_op jit(solution)/shard_map/pallas_call | solution.py:446
  51.1 1.2 %collective-permute-done.5.rest_6_ = bf16[72,1024]{1,0:T(8,128)(2,1)S(1)} collective-permute-done((bf16[72,1024]{1,0:T(8,128)(2,1)S(1)}, bf16[72,1024]{1,0:T(8,128)(2,1)S(1)}, u32[]{:S(2)}, u32[]{:S(2)}) %collective-permute-start.5) | collective-permute-done | bytes 147488 | tf_op jit(solution)/shard_map/ppermute | solution.py:464
  52.4 7.4 %shard_map.98 = f32[2,16,16,128]{3,2,1,0:T(8,128)S(1)} custom-call(s32[4]{0:T(128)S(1)} %copy-done.5, f32[2,1024]{1,0:T(2,128)S(1)} %get-tuple-element.17.vo_ref, f32[16,128]{1,0:T(8,128)S(1)} %get-tuple-element.18.own_ref, f32[16,128]{1,0:T(8,128)S(1)} %collective-permute-done.1.other_ref, bf16[8,1024,512]{2,1,0:T(8,128)(2,1)S(1)} %get-tuple-element.19.chosen_ref, ...), custom_call_target="tpu_custom_call" | custom-call | tf_op jit(solution)/shard_map/pallas_call | solution.py:446
  59.8 14.9 %all_to_all.10 = f32[32,16,128]{2,1,0:T(8,128)S(1)} all-to-all(f32[32,16,128]{2,1,0:T(8,128)S(1)} %bitcast.11), channel_id=1, replica_groups=mesh['groups'=2,'line'=4,'pair'=2,'tensor'=2] {'groups','line','pair','t..., dimensions={0} | all-to-all | bytes 524288 | tf_op jit(solution)/shard_map/all_to_all | solution.py:602
  74.7 1.1 %shard_map.99 = f32[1,512]{1,0:T(1,128)} custom-call(f32[2,4,4,16,128]{4,3,2,1,0:T(8,128)S(1)} %bitcast.12, s32[1,512]{1,0:T(1,128)S(1)} %bitcast.15, s32[1,512]{1,0:T(1,128)S(1)} %copy-done.7), custom_call_target="tpu_custom_call" | custom-call | tf_op jit(solution)/shard_map/pallas_call | solution.py:610
  (19 shorter events, 0.0 us)
Async XLA Ops:
  0.0 31.6 %copy-start.3 = (f32[4,32,2]{2,1,0:T(8,128)S(1)}, f32[4,32,2]{2,1,0:T(8,128)}, u32[]{:S(2)}) copy-start(f32[4,32,2]{2,1,0:T(8,128)} %constant.17.clone.turn_ref) | copy-start | bytes 3076
  2.7 28.9 %all-to-all-start = ((bf16[8,104,512]{2,1,0:T(8,128)(2,1)}), bf16[8,104,512]{2,1,0:T(8,128)(2,1)S(1)}, u32[]{:S(2)}, u32[]{:S(2)}) async-start(bf16[8,104,512]{2,1,0:T(8,128)(2,1)} %shard_map.91.after_ref), calls=%async_computation | async-start | bytes 1703936 | tf_op jit(solution)/shard_map/all_to_all | solution.py:513
  10.6 21.0 %copy-start.5 = (s32[4]{0:T(128)S(1)}, s32[4]{0:T(128)}, u32[]{:S(2)}) copy-start(s32[4]{0:T(128)} %pad_add_fusion.place_ref) | copy-start | bytes 52
  13.6 15.1 %collective-permute-start = (bf16[9,256,128]{2,1,0:T(8,128)(2,1)}, bf16[9,256,128]{2,1,0:T(8,128)(2,1)S(1)}, u32[]{:S(2)}, u32[]{:S(2)}) collective-permute-start(bf16[9,256,128]{2,1,0:T(8,128)(2,1)} %get-tuple-element.15.rest_0_), channel_id=1, source_target_pairs={{0,16},{2,18},{16,0},{18,2},{1,17},{3,19},{17,1},{19,3},{4,20},{6,... | collective-permute-start | bytes 1769480 | tf_op jit(solution)/shard_map/ppermute | solution.py:464
  15.2 23.1 %collective-permute-start.2 = (bf16[9,256,128]{2,1,0:T(8,128)(2,1)}, bf16[9,256,128]{2,1,0:T(8,128)(2,1)S(1)}, u32[]{:S(2)}, u32[]{:S(2)}) collective-permute-start(bf16[9,256,128]{2,1,0:T(8,128)(2,1)} %get-tuple-element.15.rest_0_), channel_id=1, source_target_pairs={{0,2},{2,0},{16,18},{18,16},{1,3},{3,1},{17,19},{19,17},{4,6},{6,4... | collective-permute-start | bytes 1769480 | tf_op jit(solution)/shard_map/ppermute | solution.py:464
  17.3 29.2 %copy-start.2 = (bf16[9,256,128]{2,1,0:T(8,128)(2,1)S(1)}, bf16[9,256,128]{2,1,0:T(8,128)(2,1)}, u32[]{:S(2)}) copy-start(bf16[9,256,128]{2,1,0:T(8,128)(2,1)} %get-tuple-element.15.rest_0_) | copy-start | bytes 1769476
  24.0 3.2 %copy-start = (bf16[1024,4096]{1,0:T(8,128)(2,1)}, bf16[1024,4096]{1,0:T(8,128)(2,1)S(1)}, u32[]{:S(2)}) copy-start(bf16[1024,4096]{1,0:T(8,128)(2,1)S(1)} %get-tuple-element.14.normed_ref) | copy-start | bytes 25165828
  28.7 0.7 copy-start.6
  29.4 21.7 %collective-permute-start.3 = (bf16[9,256,128]{2,1,0:T(8,128)(2,1)S(1)}, bf16[9,256,128]{2,1,0:T(8,128)(2,1)S(1)}, u32[]{:S(2)}, u32[]{:S(2)}) collective-permute-start(bf16[9,256,128]{2,1,0:T(8,128)(2,1)S(1)} %shard_map.94.after_ref.rest_2_), channel_id=1, source_target_pairs={{0,2},{2,0},{16,18},{18,16},{1,3},{3,1},{17,19},{19,17},{4,6},{6,4... | collective-permute-start | bytes 1769480 | tf_op jit(solution)/shard_map/ppermute | solution.py:464
  31.6 3.4 %copy-start.1 = (bf16[1024,4096]{1,0:T(8,128)(2,1)S(1)}, bf16[1024,4096]{1,0:T(8,128)(2,1)}, u32[]{:S(2)}) copy-start(bf16[1024,4096]{1,0:T(8,128)(2,1)} %copy-done) | copy-start | bytes 25165828
  38.4 12.8 %collective-permute-start.6 = (bf16[72,1024]{1,0:T(8,128)(2,1)S(1)}, bf16[72,1024]{1,0:T(8,128)(2,1)S(1)}, u32[]{:S(2)}, u32[]{:S(2)}) collective-permute-start(bf16[72,1024]{1,0:T(8,128)(2,1)S(1)} %shard_map.97.rest_4_), channel_id=1, source_target_pairs={{0,12},{4,8},{8,4},{12,0},{1,13},{5,9},{9,5},{13,1},{2,14},{6,10},... | collective-permute-start | bytes 442376 | tf_op jit(solution)/shard_map/ppermute | solution.py:464
  41.2 11.1 %collective-permute-start.5 = (bf16[72,1024]{1,0:T(8,128)(2,1)S(1)}, bf16[72,1024]{1,0:T(8,128)(2,1)S(1)}, u32[]{:S(2)}, u32[]{:S(2)}) collective-permute-start(bf16[72,1024]{1,0:T(8,128)(2,1)S(1)} %shard_map.97.rest_4_), channel_id=1, source_target_pairs={{0,8},{4,12},{8,0},{12,4},{1,9},{5,13},{9,1},{13,5},{2,10},{6,14},... | collective-permute-start | bytes 442376 | tf_op jit(solution)/shard_map/ppermute | solution.py:464
  41.2 11.1 %collective-permute-start.4 = (bf16[72,1024]{1,0:T(8,128)(2,1)S(1)}, bf16[72,1024]{1,0:T(8,128)(2,1)S(1)}, u32[]{:S(2)}, u32[]{:S(2)}) collective-permute-start(bf16[72,1024]{1,0:T(8,128)(2,1)S(1)} %shard_map.97.rest_4_), channel_id=1, source_target_pairs={{0,4},{4,0},{8,12},{12,8},{1,5},{5,1},{9,13},{13,9},{2,6},{6,2},{1... | collective-permute-start | bytes 442376 | tf_op jit(solution)/shard_map/ppermute | solution.py:464
  42.8 3.7 %collective-permute-start.1 = (f32[16,128]{1,0:T(8,128)S(1)}, f32[16,128]{1,0:T(8,128)S(1)}, u32[]{:S(2)}, u32[]{:S(2)}) collective-permute-start(f32[16,128]{1,0:T(8,128)S(1)} %get-tuple-element.18.own_ref), channel_id=1, source_target_pairs={{0,16},{2,18},{16,0},{18,2},{1,17},{3,19},{17,1},{19,3},{4,20},{6,... | collective-permute-start | bytes 24584 | tf_op jit(solution)/shard_map/ppermute | solution.py:464
  52.4 22.3 %copy-start.4 = (s32[512,1]{0,1:T(1,128)S(1)}, s32[512,1]{0,1:T(1,128)}, u32[]{:S(2)}) copy-start(s32[512,1]{0,1:T(1,128)} %param.11) | copy-start | bytes 6148
  52.4 22.3 %copy-start.7 = (s32[1,512]{1,0:T(1,128)S(1)}, s32[1,512]{1,0:T(1,128)}, u32[]{:S(2)}) copy-start(s32[1,512]{1,0:T(1,128)} %get-tuple-element.22.slot_ref) | copy-start | bytes 6148

commit v15 on v14

--- a/solution.py
+++ b/solution.py
@@ -168,14 +168,20 @@
         out_ref[peer] = jnp.where(r == plan.list_at, lists[peer // plan.pair], mine).astype(BF16)
 
 
-def normalize(table_hbm, gain_ref, after_ref, out_ref, mark_ref, gain, buffers, sems):
+def normalize(table_hbm, gain_ref, after_ref, *refs):
+    *outs, mark_ref, gain, buffers, made, sems, out_sems = refs
     mark_ref[...] = jnp.zeros_like(mark_ref)
     held, block, _ = buffers.shape
     steps = table_hbm.shape[0] // block
+    each = outs[0].shape[0] // block
 
     def copy(step):
         source = table_hbm.at[pl.ds(step * block, block)]
         return pltpu.make_async_copy(source, buffers.at[step % held], sems.at[step % held])
+
+    def store(step):
+        target = outs[step // each].at[pl.ds(step % each * block, block)]
+        return pltpu.make_async_copy(made.at[step % held], target, out_sems.at[step % held])
 
     for step in range(min(held, steps)):
         copy(step).start()
@@ -183,11 +189,16 @@
     gain[...] = jnp.concatenate([rows[r : r + 1] for r in range(rows.shape[0])], axis=1)
     for step in range(steps):
         copy(step).wait()
+        if step >= held:
+            store(step - held).wait()
         raw = buffers[step % held].astype(F32)
         inverse = lax.rsqrt(jnp.mean(raw * raw, axis=-1, keepdims=True) + EPS)
-        out_ref[step * block : (step + 1) * block] = (raw * inverse * gain[...]).astype(BF16)
+        made[step % held] = (raw * inverse * gain[...]).astype(BF16)
+        store(step).start()
         if step + held < steps:
             copy(step + held).start()
+    for step in range(max(0, steps - held), steps):
+        store(step).wait()
 
 
 def read_lists(plan, w_ref, out_ref):
@@ -215,16 +226,19 @@
     out_ref[...] = jnp.sum(listed.reshape(share, peers, plan.slots), axis=1)
 
 
-def project(plan, place_ref, w_ref, normed_ref, turn_ref, after_ref, q_ref, vo_ref, list_ref):
-    read_lists(plan, w_ref, list_ref)
+def project(plan, place, lists, place_ref, w_ref, normed_ref, turn_ref, after_ref, *refs):
+    if lists:
+        *refs, list_ref = refs
+        read_lists(plan, w_ref, list_ref)
+    q_ref, vo_ref = refs[-2:]
     turns = turn_ref[place_ref[LINE]]
     half, k_half = plan.q_rows // 2, plan.k_rows // 2
     cosine, sine = turns[:, 0:1], turns[:, 1:2]
     cos_k, sin_k = cosine[:k_half], sine[:k_half]
     moves = normed_ref.shape[0]
-    block = min(moves, 512)
+    block = min(moves, 256)
     for start in range(0, moves, block):
-        at = slice(start, start + block)
+        at, to = slice(start, start + block), slice(place + start, place + start + block)
         if len(w_ref.shape) == 3:
             depth = w_ref.shape[2]
             total = None
@@ -251,11 +265,11 @@
             pieces.append(jnp.zeros((pad, block), F32))
         out = jnp.concatenate(pieces, axis=0).astype(BF16)
         if plan.direct:
-            q_ref[:, at] = out
+            q_ref[:, to] = out
         else:
             for line in range(plan.line):
-                q_ref[line, :, at] = out
-        vo_ref[:, at] = total[plan.fold_at : plan.list_at]
+                q_ref[line, :, to] = out
+        vo_ref[:, to] = total[plan.fold_at : plan.list_at]
 
 
 def tied(x, *others):
@@ -404,8 +418,12 @@
         return carry
 
     lax.fori_loop(0, -(-boards // 2), step, 0)
+    live = scores[...] > 0.5 * DEAD
+    count = jnp.sum(jnp.where(live, 1.0, 0.0), axis=2, keepdims=True)
+    mean = jnp.sum(jnp.where(live, scores[...], 0.0), axis=2, keepdims=True) / jnp.maximum(count, 1.0)
+    centered = jnp.where(live, scores[...] - mean, DEAD)
     for g in range(plan.groups):
-        both = jnp.concatenate([scores[g * plan.pair + p] for p in range(plan.pair)], axis=0)
+        both = jnp.concatenate([centered[g * plan.pair + p] for p in range(plan.pair)], axis=0).astype(BF16)
         for copy in range(out_ref.shape[1]):
             out_ref[g, copy] = both
 
@@ -417,7 +435,7 @@
         total = None
         for g in range(parts_ref.shape[0]):
             for p in range(parts_ref.shape[2]):
-                term = parts_ref[g, at, p]
+                term = parts_ref[g, at, p].astype(F32)
                 total = term if total is None else total + term
         columns.append(total)
     scores = jnp.concatenate(columns, axis=0)
@@ -532,17 +550,19 @@
 
     block = min(moves, 128)
     vmem = pl.BlockSpec(memory_space=pltpu.VMEM)
-    normed, mark = pl.pallas_call(
+    *normed, mark = pl.pallas_call(
         normalize,
-        out_shape=(pltpu.VMEM((moves, width), BF16), shape((8, HD), F32)),
+        out_shape=[*[shape((moves // 2, width), BF16)] * 2, shape((8, HD), F32)],
         in_specs=[untouched(), vmem, untouched()],
-        out_specs=(vmem, vmem),
+        out_specs=[untouched(), untouched(), vmem],
         scratch_shapes=[
             pltpu.VMEM((1, width), F32),
             pltpu.VMEM((3, block, width), BF16),
+            pltpu.VMEM((3, block, width), BF16),
+            pltpu.SemaphoreType.DMA((3,)),
             pltpu.SemaphoreType.DMA((3,)),
         ],
-        compiler_params=limits(48),
+        compiler_params=limits(58),
         cost_estimate=cost(moves * width, moves * width // 4),
     )(move_table, norm_gain.reshape(width // HD, HD), packed)
     turns = turn_table(prefix_len).reshape(line, 1, plan.pairs, 2)
@@ -552,18 +572,22 @@
     outs = (shape(sent if plan.direct else (line, *sent), BF16), shape((plan.mine, moves), F32))
     across = tied(across, mark)
     diagonal = swap(across, slab_axes, plan.slab, 1)
-    queries, own_values, listed = local_call(
-        functools.partial(project, plan),
-        place,
-        (flat, normed, jnp.asarray(turns), across),
-        (*outs, shape((plan.share, plan.slots), F32)),
-        (),
-        20,
-        (3,),
-        2 * moves * width * 256,
-        2 * moves * width,
-    )
-    queries = tied(queries, beside)
+    filled, listed = (), None
+    for step, after in enumerate((across, beside)):
+        made = local_call(
+            functools.partial(project, plan, step * moves // 2, step == 0),
+            place,
+            (flat, normed[step], jnp.asarray(turns), after, *filled),
+            [*outs, *([shape((plan.share, plan.slots), F32)] if step == 0 else [])],
+            (),
+            20,
+            (3,),
+            moves * width * 1024,
+            moves * width,
+            {5: 0, 6: 1} if filled else None,
+        )
+        filled, listed = made[:2], made[2] if step == 0 else listed
+    queries, own_values = filled
     other = swap(listed, slab_axes, plan.slab, pair)
     if plan.direct:
         queries = [queries] + [swap(queries, "line", line, step) for step in range(1, line)]
@@ -589,7 +613,7 @@
         functools.partial(attend, plan),
         place,
         (own_values, listed, other, chosen, folds, payload, beside, across, diagonal, *queries),
-        shape((groups, back, plan.share, plan.slots), F32),
+        shape((groups, back, plan.share, plan.slots), BF16),
         [
             pltpu.VMEM((query_rows + 16, moves), BF16),
             pltpu.VMEM((16, moves), F32),

time: 76 us -> 73.4 us (0.966)
  local copies, waits for them, and re-layouts: 7.3 us -> 2.99 us
  Pallas kernels: 28.9 us -> 31.4 us
  blocking collectives: 14.9 us -> 12.7 us
  waiting for transfers between devices: 5.28 us -> 6.54 us
    unnamed x16, local copies, waits for them, and re-layouts: 7.3 us -> 2.99 us
    all_to_all x1, blocking collectives: 14.9 us -> 12.7 us  [per_device(): lax.all_to_all(parts.reshape(groups * back, plan.share, plan.slots), ('gr...]
    pallas_call x1, Pallas kernels: 6.73 us -> 8.9 us  [per_device(): pl.pallas_call(normalize, out_shape=[*[shape((moves // 2, width), BF16)]...]
    ppermute x7, waiting for transfers between devices: 4.82 us -> 6.09 us  [swap(): return lax.ppermute(x, names, [(at, at ^ step) for at in range(size)])]
    pallas_call x5 -> x6, Pallas kernels: 21.1 us -> 21.5 us  [local_call(): pl.pallas_call(kernel, out_shape=outs, in_specs=[pl.BlockSpec(memory_spac...]
  transfers between devices with their start and end apart: 8 -> 8, of which waited for: 4 -> 4; matrix products, arithmetic and copies ran while one was open for 1% -> 1% of each run, Pallas kernels for 23% -> 28%
where the time goes in v15:
time: 73.4 us; the launch traced here: 73 us
  Pallas kernels  31.4 us (43%)
  starting transfers between devices  18.6 us (25%)
  blocking collectives  12.7 us (17%)
  waiting for transfers between devices  6.54 us (9%)
  local copies, waits for them, and re-layouts  2.99 us (4%)
    pallas_call x6, Pallas kernels, local_call(): pl.pallas_call(kernel, out_shape=outs, in_specs=[pl.BlockSpec(memory_spac...  21.5 us
    all_to_all x1, blocking collectives, per_device(): lax.all_to_all(parts.reshape(groups * back, plan.share, plan.slots), ('gr...  12.7 us
    ppermute x7, starting transfers between devices, swap(): return lax.ppermute(x, names, [(at, at ^ step) for at in range(size)])  11.3 us
    pallas_call x1, Pallas kernels, per_device(): pl.pallas_call(normalize, out_shape=[*[shape((moves // 2, width), BF16)]...  8.9 us
    all_to_all x1, starting transfers between devices, per_device(): lax.all_to_all(packed, ('line', 'pair'), split_axis=0, concat_axis=0, til...  7.26 us
    ppermute x7, waiting for transfers between devices, swap(): return lax.ppermute(x, names, [(at, at ^ step) for at in range(size)])  6.09 us
    unnamed x16, local copies, waits for them, and re-layouts  2.99 us
  transfers between devices with their start and end apart: 8, of which 4 were waited for; matrix products, arithmetic and copies ran while one was open for 1% of the time, Pallas kernels for 28%

profile of v15, /device:TPU:0, one launch (start us, length us, event | category | flops | bytes accessed | tf_op | source)
XLA Modules:
  0.0 73.0 jit_solution(17792779611440764755)
XLA Ops:
  0.0 2.6 %shard_map.91.after_ref = bf16[8,104,512]{2,1,0:T(8,128)(2,1)} custom-call(s32[1]{0:T(128)} %bitcast.place_ref, bf16[512,1024]{1,0:T(8,128)(2,1)} %wq_hbm.1, bf16[512,256]{1,0:T(8,128)(2,1)} %wkv_hbm.1, bf16[8,128]{1,0:T(8,128)(2,1)} %bitcast.17, s32[1,512]{1,0:T(1,128)} %bitcast.13, s32[1,512]{1,0:T(1,128)} %bitcast.19), custom_call_target="tpu_custom_call" | custom-call | tf_op jit(solution)/shard_map/pallas_call | solution.py:464
  2.7 7.3 %all-to-all-start = ((bf16[8,104,512]{2,1,0:T(8,128)(2,1)}), bf16[8,104,512]{2,1,0:T(8,128)(2,1)S(1)}, u32[]{:S(2)}, u32[]{:S(2)}) async-start(bf16[8,104,512]{2,1,0:T(8,128)(2,1)} %shard_map.91.after_ref), calls=%async_computation | async-start | bytes 1703936 | tf_op jit(solution)/shard_map/all_to_all | solution.py:531
  9.9 0.7 pad_add_fusion.place_ref
  10.6 3.0 %shard_map.93 = (bf16[9,256,128]{2,1,0:T(8,128)(2,1)}, s32[1,512]{1,0:T(1,128)}) custom-call(s32[4]{0:T(128)} %pad_add_fusion.place_ref, bf16[8,256,256]{2,1,0:T(8,128)(2,1)} %prefix_hbm.1, bf16[8,128]{1,0:T(8,128)(2,1)} %bitcast.18, s32[1,512]{1,0:T(1,128)} %bitcast.14, bf16[8,104,512]{2,1,0:T(8,128)(2,1)} %shard_map.91.after_ref), custom_call_target="tpu_custom_call" | custom-call | tf_op jit(solution)/shard_map/pallas_call | solution.py:464
  13.6 1.6 %collective-permute-start.1 = (bf16[9,256,128]{2,1,0:T(8,128)(2,1)}, bf16[9,256,128]{2,1,0:T(8,128)(2,1)S(1)}, u32[]{:S(2)}, u32[]{:S(2)}) collective-permute-start(bf16[9,256,128]{2,1,0:T(8,128)(2,1)} %get-tuple-element.18.rest_0_), channel_id=1, source_target_pairs={{0,16},{2,18},{16,0},{18,2},{1,17},{3,19},{17,1},{19,3},{4,20},{6,... | collective-permute-start | bytes 1769480 | tf_op jit(solution)/shard_map/ppermute | solution.py:482
  15.2 2.0 %collective-permute-start = (bf16[9,256,128]{2,1,0:T(8,128)(2,1)}, bf16[9,256,128]{2,1,0:T(8,128)(2,1)S(1)}, u32[]{:S(2)}, u32[]{:S(2)}) collective-permute-start(bf16[9,256,128]{2,1,0:T(8,128)(2,1)} %get-tuple-element.18.rest_0_), channel_id=1, source_target_pairs={{0,2},{2,0},{16,18},{18,16},{1,3},{3,1},{17,19},{19,17},{4,6},{6,4... | collective-permute-start | bytes 1769480 | tf_op jit(solution)/shard_map/ppermute | solution.py:482
  17.2 8.9 %shard_map.92 = (bf16[512,4096]{1,0:T(8,128)(2,1)}, bf16[512,4096]{1,0:T(8,128)(2,1)}, f32[8,128]{1,0:T(8,128)}) custom-call(bf16[1024,4096]{1,0:T(8,128)(2,1)} %table_hbm.1, bf16[32,128]{1,0:T(8,128)(2,1)} %bitcast.16, bf16[8,104,512]{2,1,0:T(8,128)(2,1)} %shard_map.91.after_ref), custom_call_target="tpu_custom_call" | custom-call | flops 4194304 | bytes 1048576 | tf_op jit(solution)/shard_map/pallas_call | solution.py:553
  26.1 2.6 %collective-permute-done.1.refs_0_ = bf16[9,256,128]{2,1,0:T(8,128)(2,1)S(1)} collective-permute-done((bf16[9,256,128]{2,1,0:T(8,128)(2,1)}, bf16[9,256,128]{2,1,0:T(8,128)(2,1)S(1)}, u32[]{:S(2)}, u32[]{:S(2)}) %collective-permute-start.1) | collective-permute-done | bytes 589856 | tf_op jit(solution)/shard_map/ppermute | solution.py:482
  28.7 0.7 copy-done.3
  29.4 1.7 %collective-permute-start.3 = (bf16[9,256,128]{2,1,0:T(8,128)(2,1)S(1)}, bf16[9,256,128]{2,1,0:T(8,128)(2,1)S(1)}, u32[]{:S(2)}, u32[]{:S(2)}) collective-permute-start(bf16[9,256,128]{2,1,0:T(8,128)(2,1)S(1)} %shard_map.94.after_ref.rest_2_), channel_id=1, source_target_pairs={{0,2},{2,0},{16,18},{18,16},{1,3},{3,1},{17,19},{19,17},{4,6},{6,4... | collective-permute-start | bytes 1769480 | tf_op jit(solution)/shard_map/ppermute | solution.py:482
  31.1 0.5 all-to-all-done.w_ref
  31.6 2.2 %copy-done.6 = bf16[512,4096]{1,0:T(8,128)(2,1)S(1)} copy-done((bf16[512,4096]{1,0:T(8,128)(2,1)S(1)}, bf16[512,4096]{1,0:T(8,128)(2,1)}, u32[]{:S(2)}) %copy-start.6) | copy-done | bytes 4194328
  33.7 2.1 %shard_map.95 = (bf16[72,1024]{1,0:T(8,128)(2,1)S(1)}, f32[2,1024]{1,0:T(2,128)S(1)}, f32[16,128]{1,0:T(8,128)S(1)}) custom-call(s32[4]{0:T(128)S(1)} %copy-done.2, bf16[8,104,512]{2,1,0:T(8,128)(2,1)S(1)} %all-to-all-done.w_ref, bf16[512,4096]{1,0:T(8,128)(2,1)S(1)} %copy-done.6, f32[4,32,2]{2,1,0:T(8,128)S(1)} %copy-done.7, ...), custom_call_target="tpu_custom_call" | custom-call | flops 4294967296 | bytes 4194304 | tf_op jit(solution)/shard_map/pallas_call | solution.py:464
  35.9 2.0 %shard_map.96 = (bf16[72,1024]{1,0:T(8,128)(2,1)S(1)}, f32[2,1024]{1,0:T(2,128)S(1)}) custom-call(s32[4]{0:T(128)S(1)} %copy-done.2, bf16[8,104,512]{2,1,0:T(8,128)(2,1)S(1)} %all-to-all-done.w_ref, bf16[512,4096]{1,0:T(8,128)(2,1)S(1)} %copy-done.5, f32[4,32,2]{2,1,0:T(8,128)S(1)} %copy-done.7, ...), custom_call_target="tpu_custom_call", output_to_operand_aliasing={{0}: (5, {}), {1}: (6, {})} | custom-call | flops 4294967296 | bytes 4194304 | tf_op jit(solution)/shard_map/pallas_call | solution.py:464
  38.0 3.2 %collective-permute-start.6 = (bf16[72,1024]{1,0:T(8,128)(2,1)S(1)}, bf16[72,1024]{1,0:T(8,128)(2,1)S(1)}, u32[]{:S(2)}, u32[]{:S(2)}) collective-permute-start(bf16[72,1024]{1,0:T(8,128)(2,1)S(1)} %get-tuple-element.27.rest_4_), channel_id=1, source_target_pairs={{0,12},{4,8},{8,4},{12,0},{1,13},{5,9},{9,5},{13,1},{2,14},{6,10},... | collective-permute-start | bytes 442376 | tf_op jit(solution)/shard_map/ppermute | solution.py:482
  41.2 0.6 collective-permute-start.5
  41.8 0.6 collective-permute-start.4
  42.4 1.5 %collective-permute-start.2 = (f32[16,128]{1,0:T(8,128)S(1)}, f32[16,128]{1,0:T(8,128)S(1)}, u32[]{:S(2)}, u32[]{:S(2)}) collective-permute-start(f32[16,128]{1,0:T(8,128)S(1)} %get-tuple-element.24.own_ref), channel_id=1, source_target_pairs={{0,16},{2,18},{16,0},{18,2},{1,17},{3,19},{17,1},{19,3},{4,20},{6,... | collective-permute-start | bytes 24584 | tf_op jit(solution)/shard_map/ppermute | solution.py:482
  43.9 2.1 %collective-permute-done.2.other_ref = f32[16,128]{1,0:T(8,128)S(1)} collective-permute-done((f32[16,128]{1,0:T(8,128)S(1)}, f32[16,128]{1,0:T(8,128)S(1)}, u32[]{:S(2)}, u32[]{:S(2)}) %collective-permute-start.2) | collective-permute-done | bytes 8224 | tf_op jit(solution)/shard_map/ppermute | solution.py:482
  46.1 4.6 %shard_map.97 = (bf16[8,1024,512]{2,1,0:T(8,128)(2,1)S(1)}, f32[3,8,256,256]{3,2,1,0:T(8,128)S(1)}) custom-call(s32[4]{0:T(128)S(1)} %copy-done.2, f32[16,128]{1,0:T(8,128)S(1)} %get-tuple-element.24.own_ref, f32[16,128]{1,0:T(8,128)S(1)} %collective-permute-done.2.other_ref, bf16[9,256,128]{2,1,0:T(8,128)(2,1)S(1)} %copy-done, ...), custom_call_target="tpu_custom_call" | custom-call | flops 1000000000 | bytes 1000000 | tf_op jit(solution)/shard_map/pallas_call | solution.py:464
  50.7 1.4 %collective-permute-done.5.rest_6_ = bf16[72,1024]{1,0:T(8,128)(2,1)S(1)} collective-permute-done((bf16[72,1024]{1,0:T(8,128)(2,1)S(1)}, bf16[72,1024]{1,0:T(8,128)(2,1)S(1)}, u32[]{:S(2)}, u32[]{:S(2)}) %collective-permute-start.5) | collective-permute-done | bytes 147488 | tf_op jit(solution)/shard_map/ppermute | solution.py:482
  52.1 7.1 %shard_map.98 = bf16[2,16,16,128]{3,2,1,0:T(8,128)(2,1)S(1)} custom-call(s32[4]{0:T(128)S(1)} %copy-done.2, f32[2,1024]{1,0:T(2,128)S(1)} %get-tuple-element.23.vo_ref, f32[16,128]{1,0:T(8,128)S(1)} %get-tuple-element.24.own_ref, f32[16,128]{1,0:T(8,128)S(1)} %collective-permute-done.2.other_ref, bf16[8,1024,512]{2,1,0:T(8,128)(2,1)S(1)} %get-tuple-element.25.chosen_ref, ...), custom_call_target="tpu_custom_call" | custom-call | tf_op jit(solution)/shard_map/pallas_call | solution.py:464
  59.2 12.7 %all_to_all.10 = bf16[32,16,128]{2,1,0:T(8,128)(2,1)S(1)} all-to-all(bf16[32,16,128]{2,1,0:T(8,128)(2,1)S(1)} %bitcast.11), channel_id=1, replica_groups=mesh['groups'=2,'line'=4,'pair'=2,'tensor'=2] {'groups','line','pair','t..., dimensions={0} | all-to-all | bytes 262144 | tf_op jit(solution)/shard_map/all_to_all | solution.py:626
  71.9 1.1 %shard_map.99 = f32[1,512]{1,0:T(1,128)} custom-call(bf16[2,4,4,16,128]{4,3,2,1,0:T(8,128)(2,1)S(1)} %bitcast.12, s32[1,512]{1,0:T(1,128)S(1)} %bitcast.15, s32[1,512]{1,0:T(1,128)S(1)} %copy-done.4), custom_call_target="tpu_custom_call" | custom-call | tf_op jit(solution)/shard_map/pallas_call | solution.py:634
  (19 shorter events, 0.1 us)
Async XLA Ops:
  2.7 28.9 %all-to-all-start = ((bf16[8,104,512]{2,1,0:T(8,128)(2,1)}), bf16[8,104,512]{2,1,0:T(8,128)(2,1)S(1)}, u32[]{:S(2)}, u32[]{:S(2)}) async-start(bf16[8,104,512]{2,1,0:T(8,128)(2,1)} %shard_map.91.after_ref), calls=%async_computation | async-start | bytes 1703936 | tf_op jit(solution)/shard_map/all_to_all | solution.py:531
  9.9 21.6 %copy-start.7 = (f32[4,32,2]{2,1,0:T(8,128)S(1)}, f32[4,32,2]{2,1,0:T(8,128)}, u32[]{:S(2)}) copy-start(f32[4,32,2]{2,1,0:T(8,128)} %constant.17.clone.turn_ref) | copy-start | bytes 3076
  10.6 21.0 %copy-start.2 = (s32[4]{0:T(128)S(1)}, s32[4]{0:T(128)}, u32[]{:S(2)}) copy-start(s32[4]{0:T(128)} %pad_add_fusion.place_ref) | copy-start | bytes 52
  13.6 15.1 %collective-permute-start.1 = (bf16[9,256,128]{2,1,0:T(8,128)(2,1)}, bf16[9,256,128]{2,1,0:T(8,128)(2,1)S(1)}, u32[]{:S(2)}, u32[]{:S(2)}) collective-permute-start(bf16[9,256,128]{2,1,0:T(8,128)(2,1)} %get-tuple-element.18.rest_0_), channel_id=1, source_target_pairs={{0,16},{2,18},{16,0},{18,2},{1,17},{3,19},{17,1},{19,3},{4,20},{6,... | collective-permute-start | bytes 1769480 | tf_op jit(solution)/shard_map/ppermute | solution.py:482
  15.2 20.6 %collective-permute-start = (bf16[9,256,128]{2,1,0:T(8,128)(2,1)}, bf16[9,256,128]{2,1,0:T(8,128)(2,1)S(1)}, u32[]{:S(2)}, u32[]{:S(2)}) collective-permute-start(bf16[9,256,128]{2,1,0:T(8,128)(2,1)} %get-tuple-element.18.rest_0_), channel_id=1, source_target_pairs={{0,2},{2,0},{16,18},{18,16},{1,3},{3,1},{17,19},{19,17},{4,6},{6,4... | collective-permute-start | bytes 1769480 | tf_op jit(solution)/shard_map/ppermute | solution.py:482
  28.7 0.7 copy-start.3
  29.4 21.3 %collective-permute-start.3 = (bf16[9,256,128]{2,1,0:T(8,128)(2,1)S(1)}, bf16[9,256,128]{2,1,0:T(8,128)(2,1)S(1)}, u32[]{:S(2)}, u32[]{:S(2)}) collective-permute-start(bf16[9,256,128]{2,1,0:T(8,128)(2,1)S(1)} %shard_map.94.after_ref.rest_2_), channel_id=1, source_target_pairs={{0,2},{2,0},{16,18},{18,16},{1,3},{3,1},{17,19},{19,17},{4,6},{6,4... | collective-permute-start | bytes 1769480 | tf_op jit(solution)/shard_map/ppermute | solution.py:482
  31.6 2.2 %copy-start.6 = (bf16[512,4096]{1,0:T(8,128)(2,1)S(1)}, bf16[512,4096]{1,0:T(8,128)(2,1)}, u32[]{:S(2)}) copy-start(bf16[512,4096]{1,0:T(8,128)(2,1)} %get-tuple-element.19.normed_ref) | copy-start | bytes 12582916
  33.7 2.2 %copy-start.5 = (bf16[512,4096]{1,0:T(8,128)(2,1)S(1)}, bf16[512,4096]{1,0:T(8,128)(2,1)}, u32[]{:S(2)}) copy-start(bf16[512,4096]{1,0:T(8,128)(2,1)} %get-tuple-element.17.normed_ref) | copy-start | bytes 12582916
  35.9 10.1 %copy-start = (bf16[9,256,128]{2,1,0:T(8,128)(2,1)S(1)}, bf16[9,256,128]{2,1,0:T(8,128)(2,1)}, u32[]{:S(2)}) copy-start(bf16[9,256,128]{2,1,0:T(8,128)(2,1)} %get-tuple-element.18.rest_0_) | copy-start | bytes 1769476
  38.0 12.8 %collective-permute-start.6 = (bf16[72,1024]{1,0:T(8,128)(2,1)S(1)}, bf16[72,1024]{1,0:T(8,128)(2,1)S(1)}, u32[]{:S(2)}, u32[]{:S(2)}) collective-permute-start(bf16[72,1024]{1,0:T(8,128)(2,1)S(1)} %get-tuple-element.27.rest_4_), channel_id=1, source_target_pairs={{0,12},{4,8},{8,4},{12,0},{1,13},{5,9},{9,5},{13,1},{2,14},{6,10},... | collective-permute-start | bytes 442376 | tf_op jit(solution)/shard_map/ppermute | solution.py:482
  41.2 10.9 %collective-permute-start.5 = (bf16[72,1024]{1,0:T(8,128)(2,1)S(1)}, bf16[72,1024]{1,0:T(8,128)(2,1)S(1)}, u32[]{:S(2)}, u32[]{:S(2)}) collective-permute-start(bf16[72,1024]{1,0:T(8,128)(2,1)S(1)} %get-tuple-element.27.rest_4_), channel_id=1, source_target_pairs={{0,8},{4,12},{8,0},{12,4},{1,9},{5,13},{9,1},{13,5},{2,10},{6,14},... | collective-permute-start | bytes 442376 | tf_op jit(solution)/shard_map/ppermute | solution.py:482
  41.8 10.3 %collective-permute-start.4 = (bf16[72,1024]{1,0:T(8,128)(2,1)S(1)}, bf16[72,1024]{1,0:T(8,128)(2,1)S(1)}, u32[]{:S(2)}, u32[]{:S(2)}) collective-permute-start(bf16[72,1024]{1,0:T(8,128)(2,1)S(1)} %get-tuple-element.27.rest_4_), channel_id=1, source_target_pairs={{0,4},{4,0},{8,12},{12,8},{1,5},{5,1},{9,13},{13,9},{2,6},{6,2},{1... | collective-permute-start | bytes 442376 | tf_op jit(solution)/shard_map/ppermute | solution.py:482
  42.4 3.7 %collective-permute-start.2 = (f32[16,128]{1,0:T(8,128)S(1)}, f32[16,128]{1,0:T(8,128)S(1)}, u32[]{:S(2)}, u32[]{:S(2)}) collective-permute-start(f32[16,128]{1,0:T(8,128)S(1)} %get-tuple-element.24.own_ref), channel_id=1, source_target_pairs={{0,16},{2,18},{16,0},{18,2},{1,17},{3,19},{17,1},{19,3},{4,20},{6,... | collective-permute-start | bytes 24584 | tf_op jit(solution)/shard_map/ppermute | solution.py:482
  52.1 19.8 %copy-start.1 = (s32[512,1]{0,1:T(1,128)S(1)}, s32[512,1]{0,1:T(1,128)}, u32[]{:S(2)}) copy-start(s32[512,1]{0,1:T(1,128)} %param.11) | copy-start | bytes 6148
  52.1 19.8 %copy-start.4 = (s32[1,512]{1,0:T(1,128)S(1)}, s32[1,512]{1,0:T(1,128)}, u32[]{:S(2)}) copy-start(s32[1,512]{1,0:T(1,128)} %get-tuple-element.28.slot_ref) | copy-start | bytes 6148

commit v16 on v15

--- a/solution.py
+++ b/solution.py
@@ -170,7 +170,6 @@
 
 def normalize(table_hbm, gain_ref, after_ref, *refs):
     *outs, mark_ref, gain, buffers, made, sems, out_sems = refs
-    mark_ref[...] = jnp.zeros_like(mark_ref)
     held, block, _ = buffers.shape
     steps = table_hbm.shape[0] // block
     each = outs[0].shape[0] // block
@@ -199,6 +198,9 @@
             copy(step + held).start()
     for step in range(max(0, steps - held), steps):
         store(step).wait()
+    mark = pltpu.make_async_copy(made.at[0, pl.ds(0, mark_ref.shape[0])], mark_ref, out_sems.at[0])
+    mark.start()
+    mark.wait()
 
 
 def read_lists(plan, w_ref, out_ref):
@@ -276,7 +278,7 @@
     return pl.pallas_call(
         lambda *refs: None,
         out_shape=shape(x.shape, x.dtype),
-        in_specs=[untouched()] * (1 + len(others)),
+        in_specs=[untouched()] + [pl.BlockSpec(memory_space=pltpu.HBM)] * len(others),
         out_specs=untouched(),
         input_output_aliases={0: 0},
         compiler_params=limits(1),
@@ -284,32 +286,22 @@
     )(x, *others)
 
 
-def pack_prefix(plan, place_ref, prefix_hbm, ws_hbm, board_hbm, after_ref, out_ref, slot_ref, *scratch):
-    values, ws_ref, board_ref, sems = scratch
+def pack_prefix(plan, prefix_hbm, ws_hbm, after_ref, out_ref, *scratch):
+    values, ws_ref, sems = scratch
     boards = values.shape[0]
     heads = plan.heads
     copies = (
-        pltpu.make_async_copy(board_hbm, board_ref, sems.at[0]),
-        pltpu.make_async_copy(ws_hbm, ws_ref, sems.at[1]),
-        pltpu.make_async_copy(prefix_hbm.at[:, :, pl.ds(HD, HD)], values, sems.at[2]),
-        pltpu.make_async_copy(prefix_hbm.at[:, :, pl.ds(0, HD)], out_ref.at[pl.ds(0, boards)], sems.at[3]),
+        pltpu.make_async_copy(ws_hbm, ws_ref, sems.at[0]),
+        pltpu.make_async_copy(prefix_hbm.at[:, :, pl.ds(HD, HD)], values, sems.at[1]),
+        pltpu.make_async_copy(prefix_hbm.at[:, :, pl.ds(0, HD)], out_ref.at[pl.ds(0, boards)], sems.at[2]),
     )
     for copy in copies:
         copy.start()
     copies[0].wait()
-    count = board_ref.shape[1]
-    board_row = board_ref[...]
-    board_col = jnp.broadcast_to(board_row.astype(F32), (8, count)).T[:, 0:1].astype(jnp.int32)
-    other = lax.broadcasted_iota(jnp.int32, (count, count), 0)
-    own = lax.broadcasted_iota(jnp.int32, (count, count), 1)
-    rank = jnp.sum(jnp.where((board_col == board_row) & (other < own), 1.0, 0.0), axis=0, keepdims=True)
-    slot_ref[...] = rank.astype(jnp.int32) + place_ref[PEER] * plan.capacity
-
-    copies[1].wait()
     span = HD // boards
     ws = jnp.concatenate([ws_ref[...].astype(F32)] * (HD // heads), axis=0)
     row = lax.broadcasted_iota(jnp.int32, (HD, 1), 0)
-    copies[2].wait()
+    copies[1].wait()
     fold = None
     for board in range(boards):
         keep = (row // span == board) & (row % span < 2 * heads)
@@ -318,7 +310,7 @@
     rounded = fold.astype(BF16).astype(F32)
     lane = lax.broadcasted_iota(jnp.int32, fold.shape, 1)
     out_ref[boards] = jnp.where(lane % span < heads, rounded, fold - rounded).astype(BF16)
-    copies[3].wait()
+    copies[2].wait()
 
 
 def fold_columns(plan, here, block, board, boards, heads):
@@ -329,8 +321,14 @@
     return matmul(block, pick)
 
 
-def prepare(plan, place_ref, own_ref, other_ref, *rest):
-    *prefix_refs, chosen_ref, fold_ref = rest
+def prepare(plan, place_ref, board_ref, own_ref, other_ref, *rest):
+    *prefix_refs, chosen_ref, fold_ref, slot_ref = rest
+    count = board_ref.shape[1]
+    board_row = board_ref[...]
+    board_col = jnp.broadcast_to(board_row.astype(F32), (8, count)).T[:, 0:1].astype(jnp.int32)
+    ahead = lax.broadcasted_iota(jnp.int32, (count, count), 0) < lax.broadcasted_iota(jnp.int32, (count, count), 1)
+    rank = jnp.sum(jnp.where((board_col == board_row) & ahead, 1.0, 0.0), axis=0, keepdims=True)
+    slot_ref[...] = rank.astype(jnp.int32) + place_ref[PEER] * plan.capacity
     here = place_ref[SLAB]
     boards, moves = chosen_ref.shape[0], chosen_ref.shape[1]
     move_at = lax.broadcasted_iota(jnp.int32, (moves, plan.slots), 0) + 1
@@ -530,21 +528,19 @@
     )
     weights = lax.all_to_all(packed, ("line", "pair"), split_axis=0, concat_axis=0, tiled=True)
 
-    keys = shape((boards_here + 1, prefix_len, HD), BF16)
-    payload, slot_row = local_call(
+    payload = pl.pallas_call(
         functools.partial(pack_prefix, plan),
-        place,
-        (prefix_kv, ws, board_row, packed),
-        (keys, shape((1, row_count), jnp.int32)),
-        [
+        out_shape=shape((boards_here + 1, prefix_len, HD), BF16),
+        in_specs=[untouched()] * 3,
+        out_specs=pl.BlockSpec(memory_space=pltpu.VMEM),
+        scratch_shapes=[
             pltpu.VMEM((boards_here, prefix_len, HD), BF16),
             pltpu.VMEM((heads, HD), BF16),
-            pltpu.VMEM((1, row_count), jnp.int32),
-            pltpu.SemaphoreType.DMA((4,)),
+            pltpu.SemaphoreType.DMA((3,)),
         ],
-        56,
-        range(4),
-    )
+        compiler_params=limits(56),
+        cost_estimate=cost(0, 0),
+    )(prefix_kv, ws, packed)
     beside = swap(payload, slab_axes, plan.slab, 1)
     across = swap(payload, slab_axes, plan.slab, 2)
 
@@ -552,9 +548,9 @@
     vmem = pl.BlockSpec(memory_space=pltpu.VMEM)
     *normed, mark = pl.pallas_call(
         normalize,
-        out_shape=[*[shape((moves // 2, width), BF16)] * 2, shape((8, HD), F32)],
+        out_shape=[*[shape((moves // 2, width), BF16)] * 2, pltpu.HBM((8, width), BF16)],
         in_specs=[untouched(), vmem, untouched()],
-        out_specs=[untouched(), untouched(), vmem],
+        out_specs=[untouched()] * 3,
         scratch_shapes=[
             pltpu.VMEM((1, width), F32),
             pltpu.VMEM((3, block, width), BF16),
@@ -597,13 +593,14 @@
 
     query_rows = plan.mine * HD
     back = plan.peers * lax.axis_size("tensor")
-    chosen, folds = local_call(
+    chosen, folds, slot_row = local_call(
         functools.partial(prepare, plan),
         place,
-        (listed, other, payload, beside, across),
+        (board_row, listed, other, payload, beside, across),
         (
             shape((boards_here, moves, plan.slab * plan.slots), BF16),
             shape((plan.slab - 1, boards_here, prefix_len, plan.mine * plan.slots), F32),
+            shape((1, row_count), jnp.int32),
         ),
         mib=20,
         flops=10**9,

time: 73.4 us -> 73 us (level)
  waiting for transfers between devices: 6.54 us -> 7.33 us
    pallas_call x6 -> x5, Pallas kernels: 21.5 us -> 18.7 us  [local_call(): pl.pallas_call(kernel, out_shape=outs, in_specs=[pl.BlockSpec(memory_spac...]
    pallas_call x0 -> x1, Pallas kernels: none -> 2.22 us  [per_device(): pl.pallas_call(functools.partial(pack_prefix, plan), out_shape=shape((boa...]
    all_to_all x1, waiting for transfers between devices: 0.46 us -> 1.76 us  [per_device(): lax.all_to_all(packed, ('line', 'pair'), split_axis=0, concat_axis=0, til...]
    unnamed x16 -> x12, local copies, waits for them, and re-layouts: 2.99 us -> 3.15 us
  transfers between devices with their start and end apart: 8 -> 8, of which waited for: 4 -> 4; matrix products, arithmetic and copies ran while one was open for 1% -> 0% of each run, Pallas kernels for 28% -> 28%
where the time goes in v16:
time: 73 us; the launch traced here: 72.5 us
  Pallas kernels  30.9 us (42%)
  starting transfers between devices  18.6 us (25%)
  blocking collectives  12.4 us (17%)
  waiting for transfers between devices  7.33 us (10%)
  local copies, waits for them, and re-layouts  3.15 us (4%)
    pallas_call x5, Pallas kernels, local_call(): pl.pallas_call(kernel, out_shape=outs, in_specs=[pl.BlockSpec(memory_spac...  18.7 us
    all_to_all x1, blocking collectives, per_device(): lax.all_to_all(parts.reshape(groups * back, plan.share, plan.slots), ('gr...  12.4 us
    ppermute x7, starting transfers between devices, swap(): return lax.ppermute(x, names, [(at, at ^ step) for at in range(size)])  11.3 us
    pallas_call x1, Pallas kernels, per_device(): pl.pallas_call(normalize, out_shape=[*[shape((moves // 2, width), BF16)]...  8.91 us
    all_to_all x1, starting transfers between devices, per_device(): lax.all_to_all(packed, ('line', 'pair'), split_axis=0, concat_axis=0, til...  7.26 us
    ppermute x7, waiting for transfers between devices, swap(): return lax.ppermute(x, names, [(at, at ^ step) for at in range(size)])  5.58 us
    unnamed x12, local copies, waits for them, and re-layouts  3.15 us
    pallas_call x1, Pallas kernels, per_device(): pl.pallas_call(functools.partial(pack_prefix, plan), out_shape=shape((boa...  2.22 us
  transfers between devices with their start and end apart: 8, of which 4 were waited for; matrix products, arithmetic and copies ran while one was open for 0% of the time, Pallas kernels for 28%

profile of v16, /device:TPU:0, one launch (start us, length us, event | category | flops | bytes accessed | tf_op | source)
XLA Modules:
  0.0 72.5 jit_solution(5584165585151752963)
XLA Ops:
  0.0 2.6 %shard_map.91.after_ref = bf16[8,104,512]{2,1,0:T(8,128)(2,1)} custom-call(s32[1]{0:T(128)} %bitcast.place_ref, bf16[512,1024]{1,0:T(8,128)(2,1)} %wq_hbm.1, bf16[512,256]{1,0:T(8,128)(2,1)} %wkv_hbm.1, bf16[8,128]{1,0:T(8,128)(2,1)} %bitcast.17, s32[1,512]{1,0:T(1,128)} %bitcast.13, s32[1,512]{1,0:T(1,128)} %bitcast.19), custom_call_target="tpu_custom_call" | custom-call | tf_op jit(solution)/shard_map/pallas_call | solution.py:462
  2.6 7.3 %all-to-all-start = ((bf16[8,104,512]{2,1,0:T(8,128)(2,1)}), bf16[8,104,512]{2,1,0:T(8,128)(2,1)S(1)}, u32[]{:S(2)}, u32[]{:S(2)}) async-start(bf16[8,104,512]{2,1,0:T(8,128)(2,1)} %shard_map.91.after_ref), calls=%async_computation | async-start | bytes 1703936 | tf_op jit(solution)/shard_map/all_to_all | solution.py:529
  9.9 2.2 %shard_map.93.rest_0_ = bf16[9,256,128]{2,1,0:T(8,128)(2,1)} custom-call(bf16[8,256,256]{2,1,0:T(8,128)(2,1)} %prefix_hbm.1, bf16[8,128]{1,0:T(8,128)(2,1)} %bitcast.18, bf16[8,104,512]{2,1,0:T(8,128)(2,1)} %shard_map.91.after_ref), custom_call_target="tpu_custom_call" | custom-call | tf_op jit(solution)/shard_map/pallas_call | solution.py:531
  12.1 1.6 %collective-permute-start.1 = (bf16[9,256,128]{2,1,0:T(8,128)(2,1)}, bf16[9,256,128]{2,1,0:T(8,128)(2,1)S(1)}, u32[]{:S(2)}, u32[]{:S(2)}) collective-permute-start(bf16[9,256,128]{2,1,0:T(8,128)(2,1)} %shard_map.93.rest_0_), channel_id=1, source_target_pairs={{0,16},{2,18},{16,0},{18,2},{1,17},{3,19},{17,1},{19,3},{4,20},{6,... | collective-permute-start | bytes 1769480 | tf_op jit(solution)/shard_map/ppermute | solution.py:480
  13.7 2.0 %collective-permute-start = (bf16[9,256,128]{2,1,0:T(8,128)(2,1)}, bf16[9,256,128]{2,1,0:T(8,128)(2,1)S(1)}, u32[]{:S(2)}, u32[]{:S(2)}) collective-permute-start(bf16[9,256,128]{2,1,0:T(8,128)(2,1)} %shard_map.93.rest_0_), channel_id=1, source_target_pairs={{0,2},{2,0},{16,18},{18,16},{1,3},{3,1},{17,19},{19,17},{4,6},{6,4... | collective-permute-start | bytes 1769480 | tf_op jit(solution)/shard_map/ppermute | solution.py:480
  15.7 8.9 %shard_map.92 = (bf16[512,4096]{1,0:T(8,128)(2,1)}, bf16[512,4096]{1,0:T(8,128)(2,1)}, bf16[8,4096]{1,0:T(8,128)(2,1)}) custom-call(bf16[1024,4096]{1,0:T(8,128)(2,1)} %table_hbm.1, bf16[32,128]{1,0:T(8,128)(2,1)} %bitcast.16, bf16[8,104,512]{2,1,0:T(8,128)(2,1)} %shard_map.91.after_ref), custom_call_target="tpu_custom_call" | custom-call | flops 4194304 | bytes 1048576 | tf_op jit(solution)/shard_map/pallas_call | solution.py:549
  24.7 0.1 pad_add_fusion.place_ref
  24.7 2.5 %collective-permute-done.1.refs_0_ = bf16[9,256,128]{2,1,0:T(8,128)(2,1)S(1)} collective-permute-done((bf16[9,256,128]{2,1,0:T(8,128)(2,1)}, bf16[9,256,128]{2,1,0:T(8,128)(2,1)S(1)}, u32[]{:S(2)}, u32[]{:S(2)}) %collective-permute-start.1) | collective-permute-done | bytes 589856 | tf_op jit(solution)/shard_map/ppermute | solution.py:480
  27.2 0.8 %copy-done.1 = bf16[8,4096]{1,0:T(8,128)(2,1)S(1)} copy-done((bf16[8,4096]{1,0:T(8,128)(2,1)S(1)}, bf16[8,4096]{1,0:T(8,128)(2,1)}, u32[]{:S(2)}) %copy-start.1) | copy-done | bytes 65560
  28.1 1.7 %collective-permute-start.3 = (bf16[9,256,128]{2,1,0:T(8,128)(2,1)S(1)}, bf16[9,256,128]{2,1,0:T(8,128)(2,1)S(1)}, u32[]{:S(2)}, u32[]{:S(2)}) collective-permute-start(bf16[9,256,128]{2,1,0:T(8,128)(2,1)S(1)} %shard_map.94.after_ref.rest_2_), channel_id=1, source_target_pairs={{0,2},{2,0},{16,18},{18,16},{1,3},{3,1},{17,19},{19,17},{4,6},{6,4... | collective-permute-start | bytes 1769480 | tf_op jit(solution)/shard_map/ppermute | solution.py:480
  29.8 1.8 %all-to-all-done.w_ref = bf16[8,104,512]{2,1,0:T(8,128)(2,1)S(1)} async-done(((bf16[8,104,512]{2,1,0:T(8,128)(2,1)}), bf16[8,104,512]{2,1,0:T(8,128)(2,1)S(1)}, u32[]{:S(2)}, u32[]{:S(2)}) %all-to-all-start) | async-done | bytes 852000 | tf_op jit(solution)/shard_map/all_to_all | solution.py:529
  31.5 2.2 %copy-done.4 = bf16[512,4096]{1,0:T(8,128)(2,1)S(1)} copy-done((bf16[512,4096]{1,0:T(8,128)(2,1)S(1)}, bf16[512,4096]{1,0:T(8,128)(2,1)}, u32[]{:S(2)}) %copy-start.4) | copy-done | bytes 4194328
  33.7 2.1 %shard_map.95 = (bf16[72,1024]{1,0:T(8,128)(2,1)S(1)}, f32[2,1024]{1,0:T(2,128)S(1)}, f32[16,128]{1,0:T(8,128)S(1)}) custom-call(s32[4]{0:T(128)S(1)} %pad_add_fusion.place_ref, bf16[8,104,512]{2,1,0:T(8,128)(2,1)S(1)} %all-to-all-done.w_ref, bf16[512,4096]{1,0:T(8,128)(2,1)S(1)} %copy-done.4, f32[4,32,2]{2,1,0:T(8,128)S(1)} %copy-done.5, ...), custom_call_target="tpu_custom_call" | custom-call | flops 4294967296 | bytes 4194304 | tf_op jit(solution)/shard_map/pallas_call | solution.py:462
  35.8 0.1 copy-done.3
  35.9 2.0 %shard_map.96 = (bf16[72,1024]{1,0:T(8,128)(2,1)S(1)}, f32[2,1024]{1,0:T(2,128)S(1)}) custom-call(s32[4]{0:T(128)S(1)} %pad_add_fusion.place_ref, bf16[8,104,512]{2,1,0:T(8,128)(2,1)S(1)} %all-to-all-done.w_ref, bf16[512,4096]{1,0:T(8,128)(2,1)S(1)} %copy-done.3, f32[4,32,2]{2,1,0:T(8,128)S(1)} %copy-done.5, ...), custom_call_target="tpu_custom_call", output_to_operand_aliasing={{0}: (5, {}), {1}: (6, {})} | custom-call | flops 4294967296 | bytes 4194304 | tf_op jit(solution)/shard_map/pallas_call | solution.py:462
  38.0 3.0 %collective-permute-start.6 = (bf16[72,1024]{1,0:T(8,128)(2,1)S(1)}, bf16[72,1024]{1,0:T(8,128)(2,1)S(1)}, u32[]{:S(2)}, u32[]{:S(2)}) collective-permute-start(bf16[72,1024]{1,0:T(8,128)(2,1)S(1)} %get-tuple-element.25.rest_4_), channel_id=1, source_target_pairs={{0,12},{4,8},{8,4},{12,0},{1,13},{5,9},{9,5},{13,1},{2,14},{6,10},... | collective-permute-start | bytes 442376 | tf_op jit(solution)/shard_map/ppermute | solution.py:480
  41.0 1.5 %collective-permute-start.4 = (bf16[72,1024]{1,0:T(8,128)(2,1)S(1)}, bf16[72,1024]{1,0:T(8,128)(2,1)S(1)}, u32[]{:S(2)}, u32[]{:S(2)}) collective-permute-start(bf16[72,1024]{1,0:T(8,128)(2,1)S(1)} %get-tuple-element.25.rest_4_), channel_id=1, source_target_pairs={{0,4},{4,0},{8,12},{12,8},{1,5},{5,1},{9,13},{13,9},{2,6},{6,2},{1... | collective-permute-start | bytes 442376 | tf_op jit(solution)/shard_map/ppermute | solution.py:480
  42.4 1.5 %collective-permute-start.2 = (f32[16,128]{1,0:T(8,128)S(1)}, f32[16,128]{1,0:T(8,128)S(1)}, u32[]{:S(2)}, u32[]{:S(2)}) collective-permute-start(f32[16,128]{1,0:T(8,128)S(1)} %get-tuple-element.22.own_ref), channel_id=1, source_target_pairs={{0,16},{2,18},{16,0},{18,2},{1,17},{3,19},{17,1},{19,3},{4,20},{6,... | collective-permute-start | bytes 24584 | tf_op jit(solution)/shard_map/ppermute | solution.py:480
  43.9 2.1 %collective-permute-done.2.other_ref = f32[16,128]{1,0:T(8,128)S(1)} collective-permute-done((f32[16,128]{1,0:T(8,128)S(1)}, f32[16,128]{1,0:T(8,128)S(1)}, u32[]{:S(2)}, u32[]{:S(2)}) %collective-permute-start.2) | collective-permute-done | bytes 8224 | tf_op jit(solution)/shard_map/ppermute | solution.py:480
  46.1 4.9 %shard_map.97 = (bf16[8,1024,512]{2,1,0:T(8,128)(2,1)S(1)}, f32[3,8,256,256]{3,2,1,0:T(8,128)S(1)}, s32[1,512]{1,0:T(1,128)S(1)}) custom-call(s32[4]{0:T(128)S(1)} %pad_add_fusion.place_ref, s32[1,512]{1,0:T(1,128)S(1)} %bitcast.14, f32[16,128]{1,0:T(8,128)S(1)} %get-tuple-element.22.own_ref, f32[16,128]{1,0:T(8,128)S(1)} %collective-permute-done.2.other_ref, ...), custom_call_target="tpu_custom_call" | custom-call | flops 1000000000 | bytes 1000000 | tf_op jit(solution)/shard_map/pallas_call | solution.py:462
  51.0 1.0 %collective-permute-done.5.rest_6_ = bf16[72,1024]{1,0:T(8,128)(2,1)S(1)} collective-permute-done((bf16[72,1024]{1,0:T(8,128)(2,1)S(1)}, bf16[72,1024]{1,0:T(8,128)(2,1)S(1)}, u32[]{:S(2)}, u32[]{:S(2)}) %collective-permute-start.5) | collective-permute-done | bytes 147488 | tf_op jit(solution)/shard_map/ppermute | solution.py:480
  52.0 7.1 %shard_map.98 = bf16[2,16,16,128]{3,2,1,0:T(8,128)(2,1)S(1)} custom-call(s32[4]{0:T(128)S(1)} %pad_add_fusion.place_ref, f32[2,1024]{1,0:T(2,128)S(1)} %get-tuple-element.21.vo_ref, f32[16,128]{1,0:T(8,128)S(1)} %get-tuple-element.22.own_ref, f32[16,128]{1,0:T(8,128)S(1)} %collective-permute-done.2.other_ref, ...), custom_call_target="tpu_custom_call" | custom-call | tf_op jit(solution)/shard_map/pallas_call | solution.py:462
  59.1 12.4 %all_to_all.10 = bf16[32,16,128]{2,1,0:T(8,128)(2,1)S(1)} all-to-all(bf16[32,16,128]{2,1,0:T(8,128)(2,1)S(1)} %bitcast.11), channel_id=1, replica_groups=mesh['groups'=2,'line'=4,'pair'=2,'tensor'=2] {'groups','line','pair','t..., dimensions={0} | all-to-all | bytes 262144 | tf_op jit(solution)/shard_map/all_to_all | solution.py:623
  71.5 1.1 %shard_map.99 = f32[1,512]{1,0:T(1,128)} custom-call(bf16[2,4,4,16,128]{4,3,2,1,0:T(8,128)(2,1)S(1)} %bitcast.12, s32[1,512]{1,0:T(1,128)S(1)} %bitcast.15, s32[1,512]{1,0:T(1,128)S(1)} %get-tuple-element.26.slot_ref), custom_call_target="tpu_custom_call" | custom-call | tf_op jit(solution)/shard_map/pallas_call | solution.py:631
  (15 shorter events, 0.0 us)
Async XLA Ops:
  2.6 28.9 %all-to-all-start = ((bf16[8,104,512]{2,1,0:T(8,128)(2,1)}), bf16[8,104,512]{2,1,0:T(8,128)(2,1)S(1)}, u32[]{:S(2)}, u32[]{:S(2)}) async-start(bf16[8,104,512]{2,1,0:T(8,128)(2,1)} %shard_map.91.after_ref), calls=%async_computation | async-start | bytes 1703936 | tf_op jit(solution)/shard_map/all_to_all | solution.py:529
  9.9 21.6 %copy-start.5 = (f32[4,32,2]{2,1,0:T(8,128)S(1)}, f32[4,32,2]{2,1,0:T(8,128)}, u32[]{:S(2)}) copy-start(f32[4,32,2]{2,1,0:T(8,128)} %constant.17.clone.turn_ref) | copy-start | bytes 3076
  12.1 15.1 %collective-permute-start.1 = (bf16[9,256,128]{2,1,0:T(8,128)(2,1)}, bf16[9,256,128]{2,1,0:T(8,128)(2,1)S(1)}, u32[]{:S(2)}, u32[]{:S(2)}) collective-permute-start(bf16[9,256,128]{2,1,0:T(8,128)(2,1)} %shard_map.93.rest_0_), channel_id=1, source_target_pairs={{0,16},{2,18},{16,0},{18,2},{1,17},{3,19},{17,1},{19,3},{4,20},{6,... | collective-permute-start | bytes 1769480 | tf_op jit(solution)/shard_map/ppermute | solution.py:480
  13.7 22.1 %collective-permute-start = (bf16[9,256,128]{2,1,0:T(8,128)(2,1)}, bf16[9,256,128]{2,1,0:T(8,128)(2,1)S(1)}, u32[]{:S(2)}, u32[]{:S(2)}) collective-permute-start(bf16[9,256,128]{2,1,0:T(8,128)(2,1)} %shard_map.93.rest_0_), channel_id=1, source_target_pairs={{0,2},{2,0},{16,18},{18,16},{1,3},{3,1},{17,19},{19,17},{4,6},{6,4... | collective-permute-start | bytes 1769480 | tf_op jit(solution)/shard_map/ppermute | solution.py:480
  27.2 0.8 %copy-start.1 = (bf16[8,4096]{1,0:T(8,128)(2,1)S(1)}, bf16[8,4096]{1,0:T(8,128)(2,1)}, u32[]{:S(2)}) copy-start(bf16[8,4096]{1,0:T(8,128)(2,1)} %get-tuple-element.18.refs_1_) | copy-start | bytes 196612
  28.1 22.9 %collective-permute-start.3 = (bf16[9,256,128]{2,1,0:T(8,128)(2,1)S(1)}, bf16[9,256,128]{2,1,0:T(8,128)(2,1)S(1)}, u32[]{:S(2)}, u32[]{:S(2)}) collective-permute-start(bf16[9,256,128]{2,1,0:T(8,128)(2,1)S(1)} %shard_map.94.after_ref.rest_2_), channel_id=1, source_target_pairs={{0,2},{2,0},{16,18},{18,16},{1,3},{3,1},{17,19},{19,17},{4,6},{6,4... | collective-permute-start | bytes 1769480 | tf_op jit(solution)/shard_map/ppermute | solution.py:480
  31.5 2.2 %copy-start.4 = (bf16[512,4096]{1,0:T(8,128)(2,1)S(1)}, bf16[512,4096]{1,0:T(8,128)(2,1)}, u32[]{:S(2)}) copy-start(bf16[512,4096]{1,0:T(8,128)(2,1)} %get-tuple-element.17.normed_ref) | copy-start | bytes 12582916
  33.7 2.2 %copy-start.3 = (bf16[512,4096]{1,0:T(8,128)(2,1)S(1)}, bf16[512,4096]{1,0:T(8,128)(2,1)}, u32[]{:S(2)}) copy-start(bf16[512,4096]{1,0:T(8,128)(2,1)} %get-tuple-element.16.normed_ref) | copy-start | bytes 12582916
  35.9 10.1 %copy-start = (bf16[9,256,128]{2,1,0:T(8,128)(2,1)S(1)}, bf16[9,256,128]{2,1,0:T(8,128)(2,1)}, u32[]{:S(2)}) copy-start(bf16[9,256,128]{2,1,0:T(8,128)(2,1)} %shard_map.93.rest_0_) | copy-start | bytes 1769476
  35.9 10.1 %copy-start.2 = (s32[512,1]{0,1:T(1,128)S(1)}, s32[512,1]{0,1:T(1,128)}, u32[]{:S(2)}) copy-start(s32[512,1]{0,1:T(1,128)} %param.11) | copy-start | bytes 6148
  38.0 13.0 %collective-permute-start.6 = (bf16[72,1024]{1,0:T(8,128)(2,1)S(1)}, bf16[72,1024]{1,0:T(8,128)(2,1)S(1)}, u32[]{:S(2)}, u32[]{:S(2)}) collective-permute-start(bf16[72,1024]{1,0:T(8,128)(2,1)S(1)} %get-tuple-element.25.rest_4_), channel_id=1, source_target_pairs={{0,12},{4,8},{8,4},{12,0},{1,13},{5,9},{9,5},{13,1},{2,14},{6,10},... | collective-permute-start | bytes 442376 | tf_op jit(solution)/shard_map/ppermute | solution.py:480
  41.0 11.0 %collective-permute-start.5 = (bf16[72,1024]{1,0:T(8,128)(2,1)S(1)}, bf16[72,1024]{1,0:T(8,128)(2,1)S(1)}, u32[]{:S(2)}, u32[]{:S(2)}) collective-permute-start(bf16[72,1024]{1,0:T(8,128)(2,1)S(1)} %get-tuple-element.25.rest_4_), channel_id=1, source_target_pairs={{0,8},{4,12},{8,0},{12,4},{1,9},{5,13},{9,1},{13,5},{2,10},{6,14},... | collective-permute-start | bytes 442376 | tf_op jit(solution)/shard_map/ppermute | solution.py:480
  41.0 11.0 %collective-permute-start.4 = (bf16[72,1024]{1,0:T(8,128)(2,1)S(1)}, bf16[72,1024]{1,0:T(8,128)(2,1)S(1)}, u32[]{:S(2)}, u32[]{:S(2)}) collective-permute-start(bf16[72,1024]{1,0:T(8,128)(2,1)S(1)} %get-tuple-element.25.rest_4_), channel_id=1, source_target_pairs={{0,4},{4,0},{8,12},{12,8},{1,5},{5,1},{9,13},{13,9},{2,6},{6,2},{1... | collective-permute-start | bytes 442376 | tf_op jit(solution)/shard_map/ppermute | solution.py:480
  42.4 3.7 %collective-permute-start.2 = (f32[16,128]{1,0:T(8,128)S(1)}, f32[16,128]{1,0:T(8,128)S(1)}, u32[]{:S(2)}, u32[]{:S(2)}) collective-permute-start(f32[16,128]{1,0:T(8,128)S(1)} %get-tuple-element.22.own_ref), channel_id=1, source_target_pairs={{0,16},{2,18},{16,0},{18,2},{1,17},{3,19},{17,1},{19,3},{4,20},{6,... | collective-permute-start | bytes 24584 | tf_op jit(solution)/shard_map/ppermute | solution.py:480

commit v17 on v16

--- a/solution.py
+++ b/solution.py
@@ -55,7 +55,7 @@
 
 
 def pack_weights(plan, place_ref, wq_hbm, wkv_hbm, ws_hbm, board_hbm, ids_hbm, *rest):
-    out_ref, wq, wkv, ws_ref, board_ref, ids_ref, pick, sems = rest
+    out_hbm, wq, wkv, ws_ref, board_ref, ids_ref, pick, made, sems, out_sems = rest
     group = place_ref[0]
     half_cols = wq.shape[1]
     columns_here = pl.ds(pl.multiple_of(group * half_cols, HD), half_cols)
@@ -94,13 +94,16 @@
         both = found[at : at + plan.share] + found[boards + at : boards + at + plan.share]
         lists.append(jnp.sum(both, axis=0, keepdims=True))
 
+    def send(peer):
+        return pltpu.make_async_copy(made.at[peer], out_hbm.at[peer], out_sems.at[peer])
+
     if plan.pairs % 16 == 0:
-        turn_weights(plan, group, lists, copies[3:], wq, wkv, ws_ref, out_ref)
+        turn_weights(plan, group, lists, copies[3:], wq, wkv, ws_ref, made, send)
     else:
-        pick_weights(plan, group, lists, copies[3:], wq, wkv, ws_ref, out_ref, pick)
-
-
-def turn_weights(plan, group, lists, copies, wq, wkv, ws_ref, out_ref):
+        pick_weights(plan, group, lists, copies[3:], wq, wkv, ws_ref, made, send, pick)
+
+
+def turn_weights(plan, group, lists, copies, wq, wkv, ws_ref, out_ref, send):
     for copy in copies:
         copy.wait()
     q = wq[...].T
@@ -124,9 +127,12 @@
                 out_ref[peer, at : at + pairs] = k[entry : entry + pairs]
             last = jnp.concatenate([*mine, lists[line], zeros], axis=0)
             out_ref[peer, plan.fold_at :] = last.astype(BF16)
-
-
-def pick_weights(plan, group, lists, copies, wq, wkv, ws_ref, out_ref, pick):
+            send(peer).start()
+    for peer in range(plan.peers):
+        send(peer).wait()
+
+
+def pick_weights(plan, group, lists, copies, wq, wkv, ws_ref, out_ref, send, pick):
     rows, half_cols = plan.rows, wq.shape[1]
     r = lax.broadcasted_iota(jnp.int32, (rows, 1), 0)
     part = r // (plan.mine * plan.pairs)
@@ -166,6 +172,9 @@
     for peer in range(plan.peers):
         mine = total[peer * rows : (peer + 1) * rows]
         out_ref[peer] = jnp.where(r == plan.list_at, lists[peer // plan.pair], mine).astype(BF16)
+        send(peer).start()
+    for peer in range(plan.peers):
+        send(peer).wait()
 
 
 def normalize(table_hbm, gain_ref, after_ref, *refs):
@@ -322,13 +331,23 @@
 
 
 def prepare(plan, place_ref, board_ref, own_ref, other_ref, *rest):
-    *prefix_refs, chosen_ref, fold_ref, slot_ref = rest
+    *prefix_refs, chosen_ref, fold_ref, slot_ref, order_ref = rest
     count = board_ref.shape[1]
     board_row = board_ref[...]
     board_col = jnp.broadcast_to(board_row.astype(F32), (8, count)).T[:, 0:1].astype(jnp.int32)
     ahead = lax.broadcasted_iota(jnp.int32, (count, count), 0) < lax.broadcasted_iota(jnp.int32, (count, count), 1)
     rank = jnp.sum(jnp.where((board_col == board_row) & ahead, 1.0, 0.0), axis=0, keepdims=True)
     slot_ref[...] = rank.astype(jnp.int32) + place_ref[PEER] * plan.capacity
+    mine, query_rows = plan.mine, plan.mine * HD
+    for step in range(order_ref.shape[0]):
+        r = lax.broadcasted_iota(jnp.int32, order_ref.shape[1:], 0)
+        c = lax.broadcasted_iota(jnp.int32, order_ref.shape[1:], 1)
+        line, at = (place_ref[LINE] ^ step, c) if plan.direct else (c // plan.line_rows, c % plan.line_rows)
+        part, head, entry = at // (mine * plan.pairs), (at // plan.pairs) % mine, at % plan.pairs
+        goes = jnp.where(at < plan.q_rows, head * HD + part * HALF + line * plan.pairs + entry, -1)
+        tail = at - plan.q_rows
+        goes = jnp.where((tail >= 0) & (tail < 2 * mine), query_rows + tail % mine, goes)
+        order_ref[step] = jnp.where(r == goes, 1.0, 0.0).astype(BF16)
     here = place_ref[SLAB]
     boards, moves = chosen_ref.shape[0], chosen_ref.shape[1]
     move_at = lax.broadcasted_iota(jnp.int32, (moves, plan.slots), 0) + 1
@@ -346,7 +365,7 @@
     lax.fori_loop(0, boards, step, 0)
 
 
-def attend(plan, place_ref, vo_ref, own_ref, other_ref, chosen_ref, fold_ref, *rest):
+def attend(plan, place_ref, vo_ref, own_ref, other_ref, chosen_ref, fold_ref, order_ref, *rest):
     prefix_refs, rest = rest[: plan.slab], rest[plan.slab :]
     *q_refs, out_ref, table, extra, scores, taken_even, taken_odd = rest
     here = place_ref[SLAB]
@@ -355,17 +374,7 @@
     boards = prefix_refs[0].shape[0] - 1
     query_rows = mine * HD
 
-    mixed = None
-    for step, q_ref in enumerate(q_refs):
-        r = lax.broadcasted_iota(jnp.int32, (query_rows + 8, q_ref.shape[0]), 0)
-        c = lax.broadcasted_iota(jnp.int32, (query_rows + 8, q_ref.shape[0]), 1)
-        line, at = (place_ref[LINE] ^ step, c) if plan.direct else (c // plan.line_rows, c % plan.line_rows)
-        part, head, entry = at // (mine * plan.pairs), (at // plan.pairs) % mine, at % plan.pairs
-        goes = jnp.where(at < plan.q_rows, head * HD + part * HALF + line * plan.pairs + entry, -1)
-        tail = at - plan.q_rows
-        goes = jnp.where((tail >= 0) & (tail < 2 * mine), query_rows + tail % mine, goes)
-        term = matmul(jnp.where(r == goes, 1.0, 0.0).astype(BF16), q_ref[...])
-        mixed = term if mixed is None else mixed + term
+    mixed = sum(matmul(order_ref[step], q_ref[...]) for step, q_ref in enumerate(q_refs))
     table[:query_rows] = mixed[:query_rows].astype(BF16)
     extra[...] = jnp.zeros_like(extra)
     for place, value in ((0, mixed[query_rows : query_rows + mine]), (2 * mine, vo_ref[...])):
@@ -391,10 +400,7 @@
             x = taken[:, j * slots : (j + 1) * slots]
             q = jnp.concatenate([x[h * HD : (h + 1) * HD].astype(BF16) for h in range(mine)], axis=1)
             logits = matmul(prefix_refs[j][board], q)
-            if j < plan.slab - 1:
-                fold = fold_ref[j, board]
-            else:
-                fold = fold_columns(plan, here, prefix_refs[j][boards], board, boards, heads)
+            fold = fold_ref[j, board]
             own_logit = per_head(x, query_rows)
             own_value = per_head(x, query_rows + 2 * mine)
             peak = jnp.maximum(jnp.max(logits, axis=0, keepdims=True), own_logit)
@@ -509,23 +515,25 @@
     board_row = move_board.reshape(1, row_count)
 
     half_cols = w_query.shape[1] // groups
-    packed = local_call(
+    packed = pl.pallas_call(
         functools.partial(pack_weights, plan),
-        group_at.reshape(1),
-        (w_query, w_keyval, ws, board_row, move_ids.reshape(1, row_count)),
-        shape((plan.peers, plan.rows, depth), BF16),
-        [
+        out_shape=shape((plan.peers, plan.rows, depth), BF16),
+        in_specs=[pl.BlockSpec(memory_space=pltpu.SMEM)] + [untouched()] * 5,
+        out_specs=untouched(),
+        scratch_shapes=[
             pltpu.VMEM((depth, half_cols), BF16),
             pltpu.VMEM((depth, 2 * HD), BF16),
             pltpu.VMEM((heads, HD), BF16),
             pltpu.VMEM((1, row_count), jnp.int32),
             pltpu.VMEM((1, row_count), jnp.int32),
             pltpu.VMEM((plan.peers * plan.rows, half_cols + 2 * HD), F32),
+            pltpu.VMEM((plan.peers, plan.rows, depth), BF16),
             pltpu.SemaphoreType.DMA((5,)),
+            pltpu.SemaphoreType.DMA((plan.peers,)),
         ],
-        62,
-        range(5),
-    )
+        compiler_params=limits(62),
+        cost_estimate=cost(0, 0),
+    )(group_at.reshape(1), w_query, w_keyval, ws, board_row, move_ids.reshape(1, row_count))
     weights = lax.all_to_all(packed, ("line", "pair"), split_axis=0, concat_axis=0, tiled=True)
 
     payload = pl.pallas_call(
@@ -593,14 +601,15 @@
 
     query_rows = plan.mine * HD
     back = plan.peers * lax.axis_size("tensor")
-    chosen, folds, slot_row = local_call(
+    chosen, folds, slot_row, order = local_call(
         functools.partial(prepare, plan),
         place,
-        (board_row, listed, other, payload, beside, across),
+        (board_row, listed, other, payload, beside, across, diagonal),
         (
             shape((boards_here, moves, plan.slab * plan.slots), BF16),
-            shape((plan.slab - 1, boards_here, prefix_len, plan.mine * plan.slots), F32),
+            shape((plan.slab, boards_here, prefix_len, plan.mine * plan.slots), F32),
             shape((1, row_count), jnp.int32),
+            shape((len(queries), plan.mine * HD + 8, queries[0].shape[0]), BF16),
         ),
         mib=20,
         flops=10**9,
@@ -609,7 +618,7 @@
     parts = local_call(
         functools.partial(attend, plan),
         place,
-        (own_values, listed, other, chosen, folds, payload, beside, across, diagonal, *queries),
+        (own_values, listed, other, chosen, folds, order, payload, beside, across, diagonal, *queries),
         shape((groups, back, plan.share, plan.slots), BF16),
         [
             pltpu.VMEM((query_rows + 16, moves), BF16),

time: 73 us -> 74.1 us (1.015)
  Pallas kernels: 30.9 us -> 32.1 us
    pallas_call x0 -> x1, Pallas kernels: none -> 2.73 us  [per_device(): pl.pallas_call(functools.partial(pack_weights, plan), out_shape=shape((pl...]
    pallas_call x5 -> x4, Pallas kernels: 18.7 us -> 17.2 us  [local_call(): pl.pallas_call(kernel, out_shape=outs, in_specs=[pl.BlockSpec(memory_spac...]
  transfers between devices with their start and end apart: 8 -> 8, of which waited for: 4 -> 3; matrix products, arithmetic and copies ran while one was open for 0% -> 0% of each run, Pallas kernels for 28% -> 28%
where the time goes in v17:
time: 74.1 us; the launch traced here: 73.7 us
  Pallas kernels  32.1 us (43%)
  starting transfers between devices  18.6 us (25%)
  blocking collectives  12.4 us (17%)
  waiting for transfers between devices  7.19 us (10%)
  local copies, waits for them, and re-layouts  3.2 us (4%)
    pallas_call x4, Pallas kernels, local_call(): pl.pallas_call(kernel, out_shape=outs, in_specs=[pl.BlockSpec(memory_spac...  17.2 us
    all_to_all x1, blocking collectives, per_device(): lax.all_to_all(parts.reshape(groups * back, plan.share, plan.slots), ('gr...  12.4 us
    ppermute x7, starting transfers between devices, swap(): return lax.ppermute(x, names, [(at, at ^ step) for at in range(size)])  11.3 us
    pallas_call x1, Pallas kernels, per_device(): pl.pallas_call(normalize, out_shape=[*[shape((moves // 2, width), BF16)]...  8.91 us
    all_to_all x1, starting transfers between devices, per_device(): lax.all_to_all(packed, ('line', 'pair'), split_axis=0, concat_axis=0, til...  7.26 us
    ppermute x7, waiting for transfers between devices, swap(): return lax.ppermute(x, names, [(at, at ^ step) for at in range(size)])  5.4 us
    unnamed x12, local copies, waits for them, and re-layouts  3.2 us
    pallas_call x1, Pallas kernels, per_device(): pl.pallas_call(functools.partial(pack_weights, plan), out_shape=shape((pl...  2.73 us
  transfers between devices with their start and end apart: 8, of which 3 were waited for; matrix products, arithmetic and copies ran while one was open for 0% of the time, Pallas kernels for 28%

profile of v17, /device:TPU:0, one launch (start us, length us, event | category | flops | bytes accessed | tf_op | source)
XLA Modules:
  0.0 73.7 jit_solution(16032194686902704434)
XLA Ops:
  0.0 2.7 %shard_map.91.after_ref = bf16[8,104,512]{2,1,0:T(8,128)(2,1)} custom-call(s32[1]{0:T(128)} %bitcast.place_ref, bf16[512,1024]{1,0:T(8,128)(2,1)} %wq_hbm.1, bf16[512,256]{1,0:T(8,128)(2,1)} %wkv_hbm.1, bf16[8,128]{1,0:T(8,128)(2,1)} %bitcast.17, s32[1,512]{1,0:T(1,128)} %bitcast.13, s32[1,512]{1,0:T(1,128)} %bitcast.19), custom_call_target="tpu_custom_call" | custom-call | tf_op jit(solution)/shard_map/pallas_call | solution.py:518
  2.7 7.3 %all-to-all-start = ((bf16[8,104,512]{2,1,0:T(8,128)(2,1)}), bf16[8,104,512]{2,1,0:T(8,128)(2,1)S(1)}, u32[]{:S(2)}, u32[]{:S(2)}) async-start(bf16[8,104,512]{2,1,0:T(8,128)(2,1)} %shard_map.91.after_ref), calls=%async_computation | async-start | bytes 1703936 | tf_op jit(solution)/shard_map/all_to_all | solution.py:537
  10.0 2.2 %shard_map.93.rest_0_ = bf16[9,256,128]{2,1,0:T(8,128)(2,1)} custom-call(bf16[8,256,256]{2,1,0:T(8,128)(2,1)} %prefix_hbm.1, bf16[8,128]{1,0:T(8,128)(2,1)} %bitcast.18, bf16[8,104,512]{2,1,0:T(8,128)(2,1)} %shard_map.91.after_ref), custom_call_target="tpu_custom_call" | custom-call | tf_op jit(solution)/shard_map/pallas_call | solution.py:539
  12.2 1.6 %collective-permute-start.1 = (bf16[9,256,128]{2,1,0:T(8,128)(2,1)}, bf16[9,256,128]{2,1,0:T(8,128)(2,1)S(1)}, u32[]{:S(2)}, u32[]{:S(2)}) collective-permute-start(bf16[9,256,128]{2,1,0:T(8,128)(2,1)} %shard_map.93.rest_0_), channel_id=1, source_target_pairs={{0,16},{2,18},{16,0},{18,2},{1,17},{3,19},{17,1},{19,3},{4,20},{6,... | collective-permute-start | bytes 1769480 | tf_op jit(solution)/shard_map/ppermute | solution.py:486
  13.8 2.0 %collective-permute-start = (bf16[9,256,128]{2,1,0:T(8,128)(2,1)}, bf16[9,256,128]{2,1,0:T(8,128)(2,1)S(1)}, u32[]{:S(2)}, u32[]{:S(2)}) collective-permute-start(bf16[9,256,128]{2,1,0:T(8,128)(2,1)} %shard_map.93.rest_0_), channel_id=1, source_target_pairs={{0,2},{2,0},{16,18},{18,16},{1,3},{3,1},{17,19},{19,17},{4,6},{6,4... | collective-permute-start | bytes 1769480 | tf_op jit(solution)/shard_map/ppermute | solution.py:486
  15.8 8.9 %shard_map.92 = (bf16[512,4096]{1,0:T(8,128)(2,1)}, bf16[512,4096]{1,0:T(8,128)(2,1)}, bf16[8,4096]{1,0:T(8,128)(2,1)}) custom-call(bf16[1024,4096]{1,0:T(8,128)(2,1)} %table_hbm.1, bf16[32,128]{1,0:T(8,128)(2,1)} %bitcast.16, bf16[8,104,512]{2,1,0:T(8,128)(2,1)} %shard_map.91.after_ref), custom_call_target="tpu_custom_call" | custom-call | flops 4194304 | bytes 1048576 | tf_op jit(solution)/shard_map/pallas_call | solution.py:557
  24.7 0.1 pad_add_fusion.place_ref
  24.8 2.5 %collective-permute-done.1.refs_0_ = bf16[9,256,128]{2,1,0:T(8,128)(2,1)S(1)} collective-permute-done((bf16[9,256,128]{2,1,0:T(8,128)(2,1)}, bf16[9,256,128]{2,1,0:T(8,128)(2,1)S(1)}, u32[]{:S(2)}, u32[]{:S(2)}) %collective-permute-start.1) | collective-permute-done | bytes 589856 | tf_op jit(solution)/shard_map/ppermute | solution.py:486
  27.3 0.8 %copy-done.1 = bf16[8,4096]{1,0:T(8,128)(2,1)S(1)} copy-done((bf16[8,4096]{1,0:T(8,128)(2,1)S(1)}, bf16[8,4096]{1,0:T(8,128)(2,1)}, u32[]{:S(2)}) %copy-start.1) | copy-done | bytes 65560
  28.1 1.7 %collective-permute-start.3 = (bf16[9,256,128]{2,1,0:T(8,128)(2,1)S(1)}, bf16[9,256,128]{2,1,0:T(8,128)(2,1)S(1)}, u32[]{:S(2)}, u32[]{:S(2)}) collective-permute-start(bf16[9,256,128]{2,1,0:T(8,128)(2,1)S(1)} %shard_map.94.after_ref.rest_2_), channel_id=1, source_target_pairs={{0,2},{2,0},{16,18},{18,16},{1,3},{3,1},{17,19},{19,17},{4,6},{6,4... | collective-permute-start | bytes 1769480 | tf_op jit(solution)/shard_map/ppermute | solution.py:486
  29.9 1.8 %all-to-all-done.w_ref = bf16[8,104,512]{2,1,0:T(8,128)(2,1)S(1)} async-done(((bf16[8,104,512]{2,1,0:T(8,128)(2,1)}), bf16[8,104,512]{2,1,0:T(8,128)(2,1)S(1)}, u32[]{:S(2)}, u32[]{:S(2)}) %all-to-all-start) | async-done | bytes 852000 | tf_op jit(solution)/shard_map/all_to_all | solution.py:537
  31.6 2.3 %copy-done.4 = bf16[512,4096]{1,0:T(8,128)(2,1)S(1)} copy-done((bf16[512,4096]{1,0:T(8,128)(2,1)S(1)}, bf16[512,4096]{1,0:T(8,128)(2,1)}, u32[]{:S(2)}) %copy-start.4) | copy-done | bytes 4194328
  34.0 2.1 %shard_map.95 = (bf16[72,1024]{1,0:T(8,128)(2,1)S(1)}, f32[2,1024]{1,0:T(2,128)S(1)}, f32[16,128]{1,0:T(8,128)S(1)}) custom-call(s32[4]{0:T(128)S(1)} %pad_add_fusion.place_ref, bf16[8,104,512]{2,1,0:T(8,128)(2,1)S(1)} %all-to-all-done.w_ref, bf16[512,4096]{1,0:T(8,128)(2,1)S(1)} %copy-done.4, f32[4,32,2]{2,1,0:T(8,128)S(1)} %copy-done.5, ...), custom_call_target="tpu_custom_call" | custom-call | flops 4294967296 | bytes 4194304 | tf_op jit(solution)/shard_map/pallas_call | solution.py:468
  36.1 0.0 copy-start.2
  36.1 2.0 %shard_map.96 = (bf16[72,1024]{1,0:T(8,128)(2,1)S(1)}, f32[2,1024]{1,0:T(2,128)S(1)}) custom-call(s32[4]{0:T(128)S(1)} %pad_add_fusion.place_ref, bf16[8,104,512]{2,1,0:T(8,128)(2,1)S(1)} %all-to-all-done.w_ref, bf16[512,4096]{1,0:T(8,128)(2,1)S(1)} %copy-done.3, f32[4,32,2]{2,1,0:T(8,128)S(1)} %copy-done.5, ...), custom_call_target="tpu_custom_call", output_to_operand_aliasing={{0}: (5, {}), {1}: (6, {})} | custom-call | flops 4294967296 | bytes 4194304 | tf_op jit(solution)/shard_map/pallas_call | solution.py:468
  38.1 2.9 %collective-permute-start.6 = (bf16[72,1024]{1,0:T(8,128)(2,1)S(1)}, bf16[72,1024]{1,0:T(8,128)(2,1)S(1)}, u32[]{:S(2)}, u32[]{:S(2)}) collective-permute-start(bf16[72,1024]{1,0:T(8,128)(2,1)S(1)} %get-tuple-element.27.rest_4_), channel_id=1, source_target_pairs={{0,12},{4,8},{8,4},{12,0},{1,13},{5,9},{9,5},{13,1},{2,14},{6,10},... | collective-permute-start | bytes 442376 | tf_op jit(solution)/shard_map/ppermute | solution.py:486
  41.0 1.6 %collective-permute-start.4 = (bf16[72,1024]{1,0:T(8,128)(2,1)S(1)}, bf16[72,1024]{1,0:T(8,128)(2,1)S(1)}, u32[]{:S(2)}, u32[]{:S(2)}) collective-permute-start(bf16[72,1024]{1,0:T(8,128)(2,1)S(1)} %get-tuple-element.27.rest_4_), channel_id=1, source_target_pairs={{0,4},{4,0},{8,12},{12,8},{1,5},{5,1},{9,13},{13,9},{2,6},{6,2},{1... | collective-permute-start | bytes 442376 | tf_op jit(solution)/shard_map/ppermute | solution.py:486
  42.6 1.5 %collective-permute-start.2 = (f32[16,128]{1,0:T(8,128)S(1)}, f32[16,128]{1,0:T(8,128)S(1)}, u32[]{:S(2)}, u32[]{:S(2)}) collective-permute-start(f32[16,128]{1,0:T(8,128)S(1)} %get-tuple-element.23.own_ref), channel_id=1, source_target_pairs={{0,16},{2,18},{16,0},{18,2},{1,17},{3,19},{17,1},{19,3},{4,20},{6,... | collective-permute-start | bytes 24584 | tf_op jit(solution)/shard_map/ppermute | solution.py:486
  44.1 2.9 %collective-permute-done.3.rest_3_ = bf16[9,256,128]{2,1,0:T(8,128)(2,1)S(1)} collective-permute-done((bf16[9,256,128]{2,1,0:T(8,128)(2,1)S(1)}, bf16[9,256,128]{2,1,0:T(8,128)(2,1)S(1)}, u32[]{:S(2)}, u32[]{:S(2)}) %collective-permute-start.3) | collective-permute-done | bytes 589856 | tf_op jit(solution)/shard_map/ppermute | solution.py:486
  47.0 0.0 collective-permute-done.2.other_ref
  47.1 5.6 %shard_map.97 = (bf16[8,1024,512]{2,1,0:T(8,128)(2,1)S(1)}, f32[4,8,256,256]{3,2,1,0:T(8,128)S(1)}, s32[1,512]{1,0:T(1,128)S(1)}, bf16[4,264,72]{2,1,0:T(8,128)(2,1)S(1)}) custom-call(s32[4]{0:T(128)S(1)} %pad_add_fusion.place_ref, s32[1,512]{1,0:T(1,128)S(1)} %bitcast.14, f32[16,128]{1,0:T(8,128)S(1)} %get-tuple-element.23.own_ref, ...), custom_call_target="tpu_custom_call" | custom-call | flops 1000000000 | bytes 1000000 | tf_op jit(solution)/shard_map/pallas_call | solution.py:468
  52.7 7.5 %shard_map.98 = bf16[2,16,16,128]{3,2,1,0:T(8,128)(2,1)S(1)} custom-call(s32[4]{0:T(128)S(1)} %pad_add_fusion.place_ref, f32[2,1024]{1,0:T(2,128)S(1)} %get-tuple-element.22.vo_ref, f32[16,128]{1,0:T(8,128)S(1)} %get-tuple-element.23.own_ref, f32[16,128]{1,0:T(8,128)S(1)} %collective-permute-done.2.other_ref, ...), custom_call_target="tpu_custom_call" | custom-call | tf_op jit(solution)/shard_map/pallas_call | solution.py:468
  60.2 12.4 %all_to_all.10 = bf16[32,16,128]{2,1,0:T(8,128)(2,1)S(1)} all-to-all(bf16[32,16,128]{2,1,0:T(8,128)(2,1)S(1)} %bitcast.11), channel_id=1, replica_groups=mesh['groups'=2,'line'=4,'pair'=2,'tensor'=2] {'groups','line','pair','t..., dimensions={0} | all-to-all | bytes 262144 | tf_op jit(solution)/shard_map/all_to_all | solution.py:632
  72.6 1.1 %shard_map.99 = f32[1,512]{1,0:T(1,128)} custom-call(bf16[2,4,4,16,128]{4,3,2,1,0:T(8,128)(2,1)S(1)} %bitcast.12, s32[1,512]{1,0:T(1,128)S(1)} %bitcast.15, s32[1,512]{1,0:T(1,128)S(1)} %get-tuple-element.28.slot_ref), custom_call_target="tpu_custom_call" | custom-call | tf_op jit(solution)/shard_map/pallas_call | solution.py:640
  (15 shorter events, 0.0 us)
Async XLA Ops:
  0.0 31.6 %copy-start.5 = (f32[4,32,2]{2,1,0:T(8,128)S(1)}, f32[4,32,2]{2,1,0:T(8,128)}, u32[]{:S(2)}) copy-start(f32[4,32,2]{2,1,0:T(8,128)} %constant.17.clone.turn_ref) | copy-start | bytes 3076
  2.7 28.9 %all-to-all-start = ((bf16[8,104,512]{2,1,0:T(8,128)(2,1)}), bf16[8,104,512]{2,1,0:T(8,128)(2,1)S(1)}, u32[]{:S(2)}, u32[]{:S(2)}) async-start(bf16[8,104,512]{2,1,0:T(8,128)(2,1)} %shard_map.91.after_ref), calls=%async_computation | async-start | bytes 1703936 | tf_op jit(solution)/shard_map/all_to_all | solution.py:537
  12.2 15.1 %collective-permute-start.1 = (bf16[9,256,128]{2,1,0:T(8,128)(2,1)}, bf16[9,256,128]{2,1,0:T(8,128)(2,1)S(1)}, u32[]{:S(2)}, u32[]{:S(2)}) collective-permute-start(bf16[9,256,128]{2,1,0:T(8,128)(2,1)} %shard_map.93.rest_0_), channel_id=1, source_target_pairs={{0,16},{2,18},{16,0},{18,2},{1,17},{3,19},{17,1},{19,3},{4,20},{6,... | collective-permute-start | bytes 1769480 | tf_op jit(solution)/shard_map/ppermute | solution.py:486
  13.8 22.3 %collective-permute-start = (bf16[9,256,128]{2,1,0:T(8,128)(2,1)}, bf16[9,256,128]{2,1,0:T(8,128)(2,1)S(1)}, u32[]{:S(2)}, u32[]{:S(2)}) collective-permute-start(bf16[9,256,128]{2,1,0:T(8,128)(2,1)} %shard_map.93.rest_0_), channel_id=1, source_target_pairs={{0,2},{2,0},{16,18},{18,16},{1,3},{3,1},{17,19},{19,17},{4,6},{6,4... | collective-permute-start | bytes 1769480 | tf_op jit(solution)/shard_map/ppermute | solution.py:486
  27.3 0.8 %copy-start.1 = (bf16[8,4096]{1,0:T(8,128)(2,1)S(1)}, bf16[8,4096]{1,0:T(8,128)(2,1)}, u32[]{:S(2)}) copy-start(bf16[8,4096]{1,0:T(8,128)(2,1)} %get-tuple-element.19.refs_1_) | copy-start | bytes 196612
  28.1 18.9 %collective-permute-start.3 = (bf16[9,256,128]{2,1,0:T(8,128)(2,1)S(1)}, bf16[9,256,128]{2,1,0:T(8,128)(2,1)S(1)}, u32[]{:S(2)}, u32[]{:S(2)}) collective-permute-start(bf16[9,256,128]{2,1,0:T(8,128)(2,1)S(1)} %shard_map.94.after_ref.rest_2_), channel_id=1, source_target_pairs={{0,2},{2,0},{16,18},{18,16},{1,3},{3,1},{17,19},{19,17},{4,6},{6,4... | collective-permute-start | bytes 1769480 | tf_op jit(solution)/shard_map/ppermute | solution.py:486
  31.6 4.4 %copy-start.3 = (bf16[512,4096]{1,0:T(8,128)(2,1)S(1)}, bf16[512,4096]{1,0:T(8,128)(2,1)}, u32[]{:S(2)}) copy-start(bf16[512,4096]{1,0:T(8,128)(2,1)} %get-tuple-element.17.normed_ref) | copy-start | bytes 12582916
  31.6 2.3 %copy-start.4 = (bf16[512,4096]{1,0:T(8,128)(2,1)S(1)}, bf16[512,4096]{1,0:T(8,128)(2,1)}, u32[]{:S(2)}) copy-start(bf16[512,4096]{1,0:T(8,128)(2,1)} %get-tuple-element.18.normed_ref) | copy-start | bytes 12582916
  36.1 11.0 %copy-start = (bf16[9,256,128]{2,1,0:T(8,128)(2,1)S(1)}, bf16[9,256,128]{2,1,0:T(8,128)(2,1)}, u32[]{:S(2)}) copy-start(bf16[9,256,128]{2,1,0:T(8,128)(2,1)} %shard_map.93.rest_0_) | copy-start | bytes 1769476
  36.1 11.0 %copy-start.2 = (s32[512,1]{0,1:T(1,128)S(1)}, s32[512,1]{0,1:T(1,128)}, u32[]{:S(2)}) copy-start(s32[512,1]{0,1:T(1,128)} %param.11) | copy-start | bytes 6148
  38.1 14.5 %collective-permute-start.6 = (bf16[72,1024]{1,0:T(8,128)(2,1)S(1)}, bf16[72,1024]{1,0:T(8,128)(2,1)S(1)}, u32[]{:S(2)}, u32[]{:S(2)}) collective-permute-start(bf16[72,1024]{1,0:T(8,128)(2,1)S(1)} %get-tuple-element.27.rest_4_), channel_id=1, source_target_pairs={{0,12},{4,8},{8,4},{12,0},{1,13},{5,9},{9,5},{13,1},{2,14},{6,10},... | collective-permute-start | bytes 442376 | tf_op jit(solution)/shard_map/ppermute | solution.py:486
  41.0 11.6 %collective-permute-start.5 = (bf16[72,1024]{1,0:T(8,128)(2,1)S(1)}, bf16[72,1024]{1,0:T(8,128)(2,1)S(1)}, u32[]{:S(2)}, u32[]{:S(2)}) collective-permute-start(bf16[72,1024]{1,0:T(8,128)(2,1)S(1)} %get-tuple-element.27.rest_4_), channel_id=1, source_target_pairs={{0,8},{4,12},{8,0},{12,4},{1,9},{5,13},{9,1},{13,5},{2,10},{6,14},... | collective-permute-start | bytes 442376 | tf_op jit(solution)/shard_map/ppermute | solution.py:486
  41.0 11.6 %collective-permute-start.4 = (bf16[72,1024]{1,0:T(8,128)(2,1)S(1)}, bf16[72,1024]{1,0:T(8,128)(2,1)S(1)}, u32[]{:S(2)}, u32[]{:S(2)}) collective-permute-start(bf16[72,1024]{1,0:T(8,128)(2,1)S(1)} %get-tuple-element.27.rest_4_), channel_id=1, source_target_pairs={{0,4},{4,0},{8,12},{12,8},{1,5},{5,1},{9,13},{13,9},{2,6},{6,2},{1... | collective-permute-start | bytes 442376 | tf_op jit(solution)/shard_map/ppermute | solution.py:486
  42.6 4.5 %collective-permute-start.2 = (f32[16,128]{1,0:T(8,128)S(1)}, f32[16,128]{1,0:T(8,128)S(1)}, u32[]{:S(2)}, u32[]{:S(2)}) collective-permute-start(f32[16,128]{1,0:T(8,128)S(1)} %get-tuple-element.23.own_ref), channel_id=1, source_target_pairs={{0,16},{2,18},{16,0},{18,2},{1,17},{3,19},{17,1},{19,3},{4,20},{6,... | collective-permute-start | bytes 24584 | tf_op jit(solution)/shard_map/ppermute | solution.py:486

commit v18 on v16

--- a/solution.py
+++ b/solution.py
@@ -348,7 +348,9 @@
 
 def attend(plan, place_ref, vo_ref, own_ref, other_ref, chosen_ref, fold_ref, *rest):
     prefix_refs, rest = rest[: plan.slab], rest[plan.slab :]
-    *q_refs, out_ref, table, extra, scores, taken_even, taken_odd = rest
+    *q_refs, out_ref, table, extra, scores, taken_even, own_even, taken_odd, own_odd = rest
+    even, odd = (taken_even, own_even), (taken_odd, own_odd)
+    prefix_len = prefix_refs[0].shape[1]
     here = place_ref[SLAB]
     mine, heads, slots = plan.mine, plan.heads, plan.slots
     moves = vo_ref.shape[1]
@@ -383,36 +385,50 @@
         place = ((here ^ j) % plan.pair) * boards + board
         return (own_ref, other_ref)[j // plan.pair][pl.ds(place, 1), :].astype(jnp.int32)
 
-    def gather(board, taken):
-        taken[...] = matmul(table[...], chosen_ref[board])
-
-    def score_board(board, taken):
+    def gather(board, taken, own):
+        found = matmul(table[...], chosen_ref[board])
+        taken[...] = found[:query_rows].astype(BF16)
+        own[...] = found[query_rows:]
+
+    def over(values):
+        return jnp.sum(values, axis=0, keepdims=True)
+
+    half = prefix_len // 2
+
+    def score_board(board, taken, own):
         for j in range(plan.slab):
-            x = taken[:, j * slots : (j + 1) * slots]
-            q = jnp.concatenate([x[h * HD : (h + 1) * HD].astype(BF16) for h in range(mine)], axis=1)
-            logits = matmul(prefix_refs[j][board], q)
-            if j < plan.slab - 1:
-                fold = fold_ref[j, board]
-            else:
-                fold = fold_columns(plan, here, prefix_refs[j][boards], board, boards, heads)
-            own_logit = per_head(x, query_rows)
-            own_value = per_head(x, query_rows + 2 * mine)
-            peak = jnp.maximum(jnp.max(logits, axis=0, keepdims=True), own_logit)
-            weight = jnp.exp2((logits - peak) * scale)
-            own_weight = jnp.exp2((own_logit - peak) * scale)
-            denom = jnp.sum(weight, axis=0, keepdims=True) + own_weight
-            value = (jnp.sum(weight * fold, axis=0, keepdims=True) + own_value * own_weight) / denom
+            at = slice(j * slots, (j + 1) * slots)
+            q = jnp.concatenate([taken[h * HD : (h + 1) * HD, at] for h in range(mine)], axis=1)
+            own_logit = per_head(own[:, at], 0)
+            own_value = per_head(own[:, at], 2 * mine)
+            parts = []
+            for keys in (slice(0, half), slice(half, 2 * half)):
+                logits = matmul(prefix_refs[j][board, keys], q)
+                if j < plan.slab - 1:
+                    fold = fold_ref[j, board, keys]
+                else:
+                    fold = fold_columns(plan, here, prefix_refs[j][boards, keys], board, boards, heads)
+                top = jnp.max(logits, axis=0, keepdims=True)
+                weight = jnp.exp2((logits - top) * scale)
+                parts.append((top, over(weight), over(weight * fold)))
+            parts.append((own_logit, 1.0, own_value))
+            peak = parts[0][0]
+            for top, _, _ in parts[1:]:
+                peak = jnp.maximum(peak, top)
+            shares = [jnp.exp2((top - peak) * scale) for top, _, _ in parts]
+            denom = sum(share * total for share, (_, total, _) in zip(shares, parts))
+            value = sum(share * total for share, (_, _, total) in zip(shares, parts)) / denom
             score = sum(value[:, h * slots : (h + 1) * slots] for h in range(mine))
             scores[here ^ j, pl.ds(board, 1), :] = jnp.where(moves_of(j, board) > 0, score, DEAD)
 
-    gather(0, taken_even)
+    gather(0, *even)
 
     def step(at, carry):
         board = 2 * at
-        gather(jnp.minimum(board + 1, boards - 1), taken_odd)
-        score_board(board, taken_even)
-        gather(jnp.minimum(board + 2, boards - 1), taken_even)
-        score_board(jnp.minimum(board + 1, boards - 1), taken_odd)
+        gather(jnp.minimum(board + 1, boards - 1), *odd)
+        score_board(board, *even)
+        gather(jnp.minimum(board + 2, boards - 1), *even)
+        score_board(jnp.minimum(board + 1, boards - 1), *odd)
         return carry
 
     lax.fori_loop(0, -(-boards // 2), step, 0)
@@ -615,8 +631,7 @@
             pltpu.VMEM((query_rows + 16, moves), BF16),
             pltpu.VMEM((16, moves), F32),
             pltpu.VMEM((plan.slab, boards_here, plan.slots), F32),
-            pltpu.VMEM((query_rows + 16, plan.slab * plan.slots), F32),
-            pltpu.VMEM((query_rows + 16, plan.slab * plan.slots), F32),
+            *[pltpu.VMEM((query_rows, plan.slab * plan.slots), BF16), pltpu.VMEM((16, plan.slab * plan.slots), F32)] * 2,
         ],
         24,
     )

time: 73 us -> 73.4 us (level)
  no operation moved by 1% of the time
where the time goes in v18:
time: 73.4 us; the launch traced here: 73 us
  Pallas kernels  31.3 us (43%)
  starting transfers between devices  18.6 us (25%)
  blocking collectives  12.4 us (17%)
  waiting for transfers between devices  7.33 us (10%)
  local copies, waits for them, and re-layouts  3.15 us (4%)
    pallas_call x5, Pallas kernels, local_call(): pl.pallas_call(kernel, out_shape=outs, in_specs=[pl.BlockSpec(memory_spac...  19.1 us
    all_to_all x1, blocking collectives, per_device(): lax.all_to_all(parts.reshape(groups * back, plan.share, plan.slots), ('gr...  12.4 us
    ppermute x7, starting transfers between devices, swap(): return lax.ppermute(x, names, [(at, at ^ step) for at in range(size)])  11.3 us
    pallas_call x1, Pallas kernels, per_device(): pl.pallas_call(normalize, out_shape=[*[shape((moves // 2, width), BF16)]...  8.91 us
    all_to_all x1, starting transfers between devices, per_device(): lax.all_to_all(packed, ('line', 'pair'), split_axis=0, concat_axis=0, til...  7.26 us
    ppermute x7, waiting for transfers between devices, swap(): return lax.ppermute(x, names, [(at, at ^ step) for at in range(size)])  5.58 us
    unnamed x12, local copies, waits for them, and re-layouts  3.15 us
    pallas_call x1, Pallas kernels, per_device(): pl.pallas_call(functools.partial(pack_prefix, plan), out_shape=shape((boa...  2.22 us
  transfers between devices with their start and end apart: 8, of which 4 were waited for; matrix products, arithmetic and copies ran while one was open for 0% of the time, Pallas kernels for 28%

profile of v18, /device:TPU:0, one launch (start us, length us, event | category | flops | bytes accessed | tf_op | source)
XLA Modules:
  0.0 73.0 jit_solution(5994884992598413205)
XLA Ops:
  0.0 2.6 %shard_map.91.after_ref = bf16[8,104,512]{2,1,0:T(8,128)(2,1)} custom-call(s32[1]{0:T(128)} %bitcast.place_ref, bf16[512,1024]{1,0:T(8,128)(2,1)} %wq_hbm.1, bf16[512,256]{1,0:T(8,128)(2,1)} %wkv_hbm.1, bf16[8,128]{1,0:T(8,128)(2,1)} %bitcast.17, s32[1,512]{1,0:T(1,128)} %bitcast.13, s32[1,512]{1,0:T(1,128)} %bitcast.19), custom_call_target="tpu_custom_call" | custom-call | tf_op jit(solution)/shard_map/pallas_call | solution.py:478
  2.6 7.3 %all-to-all-start = ((bf16[8,104,512]{2,1,0:T(8,128)(2,1)}), bf16[8,104,512]{2,1,0:T(8,128)(2,1)S(1)}, u32[]{:S(2)}, u32[]{:S(2)}) async-start(bf16[8,104,512]{2,1,0:T(8,128)(2,1)} %shard_map.91.after_ref), calls=%async_computation | async-start | bytes 1703936 | tf_op jit(solution)/shard_map/all_to_all | solution.py:545
  9.9 2.2 %shard_map.93.rest_0_ = bf16[9,256,128]{2,1,0:T(8,128)(2,1)} custom-call(bf16[8,256,256]{2,1,0:T(8,128)(2,1)} %prefix_hbm.1, bf16[8,128]{1,0:T(8,128)(2,1)} %bitcast.18, bf16[8,104,512]{2,1,0:T(8,128)(2,1)} %shard_map.91.after_ref), custom_call_target="tpu_custom_call" | custom-call | tf_op jit(solution)/shard_map/pallas_call | solution.py:547
  12.1 1.6 %collective-permute-start.1 = (bf16[9,256,128]{2,1,0:T(8,128)(2,1)}, bf16[9,256,128]{2,1,0:T(8,128)(2,1)S(1)}, u32[]{:S(2)}, u32[]{:S(2)}) collective-permute-start(bf16[9,256,128]{2,1,0:T(8,128)(2,1)} %shard_map.93.rest_0_), channel_id=1, source_target_pairs={{0,16},{2,18},{16,0},{18,2},{1,17},{3,19},{17,1},{19,3},{4,20},{6,... | collective-permute-start | bytes 1769480 | tf_op jit(solution)/shard_map/ppermute | solution.py:496
  13.7 2.0 %collective-permute-start = (bf16[9,256,128]{2,1,0:T(8,128)(2,1)}, bf16[9,256,128]{2,1,0:T(8,128)(2,1)S(1)}, u32[]{:S(2)}, u32[]{:S(2)}) collective-permute-start(bf16[9,256,128]{2,1,0:T(8,128)(2,1)} %shard_map.93.rest_0_), channel_id=1, source_target_pairs={{0,2},{2,0},{16,18},{18,16},{1,3},{3,1},{17,19},{19,17},{4,6},{6,4... | collective-permute-start | bytes 1769480 | tf_op jit(solution)/shard_map/ppermute | solution.py:496
  15.7 8.9 %shard_map.92 = (bf16[512,4096]{1,0:T(8,128)(2,1)}, bf16[512,4096]{1,0:T(8,128)(2,1)}, bf16[8,4096]{1,0:T(8,128)(2,1)}) custom-call(bf16[1024,4096]{1,0:T(8,128)(2,1)} %table_hbm.1, bf16[32,128]{1,0:T(8,128)(2,1)} %bitcast.16, bf16[8,104,512]{2,1,0:T(8,128)(2,1)} %shard_map.91.after_ref), custom_call_target="tpu_custom_call" | custom-call | flops 4194304 | bytes 1048576 | tf_op jit(solution)/shard_map/pallas_call | solution.py:565
  24.7 0.1 pad_add_fusion.place_ref
  24.7 2.5 %collective-permute-done.1.refs_0_ = bf16[9,256,128]{2,1,0:T(8,128)(2,1)S(1)} collective-permute-done((bf16[9,256,128]{2,1,0:T(8,128)(2,1)}, bf16[9,256,128]{2,1,0:T(8,128)(2,1)S(1)}, u32[]{:S(2)}, u32[]{:S(2)}) %collective-permute-start.1) | collective-permute-done | bytes 589856 | tf_op jit(solution)/shard_map/ppermute | solution.py:496
  27.2 0.8 %copy-done.1 = bf16[8,4096]{1,0:T(8,128)(2,1)S(1)} copy-done((bf16[8,4096]{1,0:T(8,128)(2,1)S(1)}, bf16[8,4096]{1,0:T(8,128)(2,1)}, u32[]{:S(2)}) %copy-start.1) | copy-done | bytes 65560
  28.1 1.7 %collective-permute-start.3 = (bf16[9,256,128]{2,1,0:T(8,128)(2,1)S(1)}, bf16[9,256,128]{2,1,0:T(8,128)(2,1)S(1)}, u32[]{:S(2)}, u32[]{:S(2)}) collective-permute-start(bf16[9,256,128]{2,1,0:T(8,128)(2,1)S(1)} %shard_map.94.after_ref.rest_2_), channel_id=1, source_target_pairs={{0,2},{2,0},{16,18},{18,16},{1,3},{3,1},{17,19},{19,17},{4,6},{6,4... | collective-permute-start | bytes 1769480 | tf_op jit(solution)/shard_map/ppermute | solution.py:496
  29.8 1.8 %all-to-all-done.w_ref = bf16[8,104,512]{2,1,0:T(8,128)(2,1)S(1)} async-done(((bf16[8,104,512]{2,1,0:T(8,128)(2,1)}), bf16[8,104,512]{2,1,0:T(8,128)(2,1)S(1)}, u32[]{:S(2)}, u32[]{:S(2)}) %all-to-all-start) | async-done | bytes 852000 | tf_op jit(solution)/shard_map/all_to_all | solution.py:545
  31.5 2.2 %copy-done.4 = bf16[512,4096]{1,0:T(8,128)(2,1)S(1)} copy-done((bf16[512,4096]{1,0:T(8,128)(2,1)S(1)}, bf16[512,4096]{1,0:T(8,128)(2,1)}, u32[]{:S(2)}) %copy-start.4) | copy-done | bytes 4194328
  33.7 2.1 %shard_map.95 = (bf16[72,1024]{1,0:T(8,128)(2,1)S(1)}, f32[2,1024]{1,0:T(2,128)S(1)}, f32[16,128]{1,0:T(8,128)S(1)}) custom-call(s32[4]{0:T(128)S(1)} %pad_add_fusion.place_ref, bf16[8,104,512]{2,1,0:T(8,128)(2,1)S(1)} %all-to-all-done.w_ref, bf16[512,4096]{1,0:T(8,128)(2,1)S(1)} %copy-done.4, f32[4,32,2]{2,1,0:T(8,128)S(1)} %copy-done.5, ...), custom_call_target="tpu_custom_call" | custom-call | flops 4294967296 | bytes 4194304 | tf_op jit(solution)/shard_map/pallas_call | solution.py:478
  35.8 0.1 copy-done.3
  35.9 2.0 %shard_map.96 = (bf16[72,1024]{1,0:T(8,128)(2,1)S(1)}, f32[2,1024]{1,0:T(2,128)S(1)}) custom-call(s32[4]{0:T(128)S(1)} %pad_add_fusion.place_ref, bf16[8,104,512]{2,1,0:T(8,128)(2,1)S(1)} %all-to-all-done.w_ref, bf16[512,4096]{1,0:T(8,128)(2,1)S(1)} %copy-done.3, f32[4,32,2]{2,1,0:T(8,128)S(1)} %copy-done.5, ...), custom_call_target="tpu_custom_call", output_to_operand_aliasing={{0}: (5, {}), {1}: (6, {})} | custom-call | flops 4294967296 | bytes 4194304 | tf_op jit(solution)/shard_map/pallas_call | solution.py:478
  38.0 3.0 %collective-permute-start.6 = (bf16[72,1024]{1,0:T(8,128)(2,1)S(1)}, bf16[72,1024]{1,0:T(8,128)(2,1)S(1)}, u32[]{:S(2)}, u32[]{:S(2)}) collective-permute-start(bf16[72,1024]{1,0:T(8,128)(2,1)S(1)} %get-tuple-element.25.rest_4_), channel_id=1, source_target_pairs={{0,12},{4,8},{8,4},{12,0},{1,13},{5,9},{9,5},{13,1},{2,14},{6,10},... | collective-permute-start | bytes 442376 | tf_op jit(solution)/shard_map/ppermute | solution.py:496
  41.0 1.5 %collective-permute-start.4 = (bf16[72,1024]{1,0:T(8,128)(2,1)S(1)}, bf16[72,1024]{1,0:T(8,128)(2,1)S(1)}, u32[]{:S(2)}, u32[]{:S(2)}) collective-permute-start(bf16[72,1024]{1,0:T(8,128)(2,1)S(1)} %get-tuple-element.25.rest_4_), channel_id=1, source_target_pairs={{0,4},{4,0},{8,12},{12,8},{1,5},{5,1},{9,13},{13,9},{2,6},{6,2},{1... | collective-permute-start | bytes 442376 | tf_op jit(solution)/shard_map/ppermute | solution.py:496
  42.4 1.5 %collective-permute-start.2 = (f32[16,128]{1,0:T(8,128)S(1)}, f32[16,128]{1,0:T(8,128)S(1)}, u32[]{:S(2)}, u32[]{:S(2)}) collective-permute-start(f32[16,128]{1,0:T(8,128)S(1)} %get-tuple-element.22.own_ref), channel_id=1, source_target_pairs={{0,16},{2,18},{16,0},{18,2},{1,17},{3,19},{17,1},{19,3},{4,20},{6,... | collective-permute-start | bytes 24584 | tf_op jit(solution)/shard_map/ppermute | solution.py:496
  43.9 2.1 %collective-permute-done.2.other_ref = f32[16,128]{1,0:T(8,128)S(1)} collective-permute-done((f32[16,128]{1,0:T(8,128)S(1)}, f32[16,128]{1,0:T(8,128)S(1)}, u32[]{:S(2)}, u32[]{:S(2)}) %collective-permute-start.2) | collective-permute-done | bytes 8224 | tf_op jit(solution)/shard_map/ppermute | solution.py:496
  46.1 4.9 %shard_map.97 = (bf16[8,1024,512]{2,1,0:T(8,128)(2,1)S(1)}, f32[3,8,256,256]{3,2,1,0:T(8,128)S(1)}, s32[1,512]{1,0:T(1,128)S(1)}) custom-call(s32[4]{0:T(128)S(1)} %pad_add_fusion.place_ref, s32[1,512]{1,0:T(1,128)S(1)} %bitcast.14, f32[16,128]{1,0:T(8,128)S(1)} %get-tuple-element.22.own_ref, f32[16,128]{1,0:T(8,128)S(1)} %collective-permute-done.2.other_ref, ...), custom_call_target="tpu_custom_call" | custom-call | flops 1000000000 | bytes 1000000 | tf_op jit(solution)/shard_map/pallas_call | solution.py:478
  51.0 1.0 %collective-permute-done.5.rest_6_ = bf16[72,1024]{1,0:T(8,128)(2,1)S(1)} collective-permute-done((bf16[72,1024]{1,0:T(8,128)(2,1)S(1)}, bf16[72,1024]{1,0:T(8,128)(2,1)S(1)}, u32[]{:S(2)}, u32[]{:S(2)}) %collective-permute-start.5) | collective-permute-done | bytes 147488 | tf_op jit(solution)/shard_map/ppermute | solution.py:496
  52.0 7.5 %shard_map.98 = bf16[2,16,16,128]{3,2,1,0:T(8,128)(2,1)S(1)} custom-call(s32[4]{0:T(128)S(1)} %pad_add_fusion.place_ref, f32[2,1024]{1,0:T(2,128)S(1)} %get-tuple-element.21.vo_ref, f32[16,128]{1,0:T(8,128)S(1)} %get-tuple-element.22.own_ref, f32[16,128]{1,0:T(8,128)S(1)} %collective-permute-done.2.other_ref, ...), custom_call_target="tpu_custom_call" | custom-call | tf_op jit(solution)/shard_map/pallas_call | solution.py:478
  59.5 12.4 %all_to_all.10 = bf16[32,16,128]{2,1,0:T(8,128)(2,1)S(1)} all-to-all(bf16[32,16,128]{2,1,0:T(8,128)(2,1)S(1)} %bitcast.11), channel_id=1, replica_groups=mesh['groups'=2,'line'=4,'pair'=2,'tensor'=2] {'groups','line','pair','t..., dimensions={0} | all-to-all | bytes 262144 | tf_op jit(solution)/shard_map/all_to_all | solution.py:638
  71.9 1.1 %shard_map.99 = f32[1,512]{1,0:T(1,128)} custom-call(bf16[2,4,4,16,128]{4,3,2,1,0:T(8,128)(2,1)S(1)} %bitcast.12, s32[1,512]{1,0:T(1,128)S(1)} %bitcast.15, s32[1,512]{1,0:T(1,128)S(1)} %get-tuple-element.26.slot_ref), custom_call_target="tpu_custom_call" | custom-call | tf_op jit(solution)/shard_map/pallas_call | solution.py:646
  (15 shorter events, 0.0 us)
Async XLA Ops:
  2.6 28.9 %all-to-all-start = ((bf16[8,104,512]{2,1,0:T(8,128)(2,1)}), bf16[8,104,512]{2,1,0:T(8,128)(2,1)S(1)}, u32[]{:S(2)}, u32[]{:S(2)}) async-start(bf16[8,104,512]{2,1,0:T(8,128)(2,1)} %shard_map.91.after_ref), calls=%async_computation | async-start | bytes 1703936 | tf_op jit(solution)/shard_map/all_to_all | solution.py:545
  9.9 21.6 %copy-start.5 = (f32[4,32,2]{2,1,0:T(8,128)S(1)}, f32[4,32,2]{2,1,0:T(8,128)}, u32[]{:S(2)}) copy-start(f32[4,32,2]{2,1,0:T(8,128)} %constant.17.clone.turn_ref) | copy-start | bytes 3076
  12.1 15.1 %collective-permute-start.1 = (bf16[9,256,128]{2,1,0:T(8,128)(2,1)}, bf16[9,256,128]{2,1,0:T(8,128)(2,1)S(1)}, u32[]{:S(2)}, u32[]{:S(2)}) collective-permute-start(bf16[9,256,128]{2,1,0:T(8,128)(2,1)} %shard_map.93.rest_0_), channel_id=1, source_target_pairs={{0,16},{2,18},{16,0},{18,2},{1,17},{3,19},{17,1},{19,3},{4,20},{6,... | collective-permute-start | bytes 1769480 | tf_op jit(solution)/shard_map/ppermute | solution.py:496
  13.7 22.1 %collective-permute-start = (bf16[9,256,128]{2,1,0:T(8,128)(2,1)}, bf16[9,256,128]{2,1,0:T(8,128)(2,1)S(1)}, u32[]{:S(2)}, u32[]{:S(2)}) collective-permute-start(bf16[9,256,128]{2,1,0:T(8,128)(2,1)} %shard_map.93.rest_0_), channel_id=1, source_target_pairs={{0,2},{2,0},{16,18},{18,16},{1,3},{3,1},{17,19},{19,17},{4,6},{6,4... | collective-permute-start | bytes 1769480 | tf_op jit(solution)/shard_map/ppermute | solution.py:496
  27.2 0.8 %copy-start.1 = (bf16[8,4096]{1,0:T(8,128)(2,1)S(1)}, bf16[8,4096]{1,0:T(8,128)(2,1)}, u32[]{:S(2)}) copy-start(bf16[8,4096]{1,0:T(8,128)(2,1)} %get-tuple-element.18.refs_1_) | copy-start | bytes 196612
  28.1 22.9 %collective-permute-start.3 = (bf16[9,256,128]{2,1,0:T(8,128)(2,1)S(1)}, bf16[9,256,128]{2,1,0:T(8,128)(2,1)S(1)}, u32[]{:S(2)}, u32[]{:S(2)}) collective-permute-start(bf16[9,256,128]{2,1,0:T(8,128)(2,1)S(1)} %shard_map.94.after_ref.rest_2_), channel_id=1, source_target_pairs={{0,2},{2,0},{16,18},{18,16},{1,3},{3,1},{17,19},{19,17},{4,6},{6,4... | collective-permute-start | bytes 1769480 | tf_op jit(solution)/shard_map/ppermute | solution.py:496
  31.5 2.2 %copy-start.4 = (bf16[512,4096]{1,0:T(8,128)(2,1)S(1)}, bf16[512,4096]{1,0:T(8,128)(2,1)}, u32[]{:S(2)}) copy-start(bf16[512,4096]{1,0:T(8,128)(2,1)} %get-tuple-element.17.normed_ref) | copy-start | bytes 12582916
  33.7 2.2 %copy-start.3 = (bf16[512,4096]{1,0:T(8,128)(2,1)S(1)}, bf16[512,4096]{1,0:T(8,128)(2,1)}, u32[]{:S(2)}) copy-start(bf16[512,4096]{1,0:T(8,128)(2,1)} %get-tuple-element.16.normed_ref) | copy-start | bytes 12582916
  35.9 10.1 %copy-start = (bf16[9,256,128]{2,1,0:T(8,128)(2,1)S(1)}, bf16[9,256,128]{2,1,0:T(8,128)(2,1)}, u32[]{:S(2)}) copy-start(bf16[9,256,128]{2,1,0:T(8,128)(2,1)} %shard_map.93.rest_0_) | copy-start | bytes 1769476
  35.9 10.1 %copy-start.2 = (s32[512,1]{0,1:T(1,128)S(1)}, s32[512,1]{0,1:T(1,128)}, u32[]{:S(2)}) copy-start(s32[512,1]{0,1:T(1,128)} %param.11) | copy-start | bytes 6148
  38.0 13.0 %collective-permute-start.6 = (bf16[72,1024]{1,0:T(8,128)(2,1)S(1)}, bf16[72,1024]{1,0:T(8,128)(2,1)S(1)}, u32[]{:S(2)}, u32[]{:S(2)}) collective-permute-start(bf16[72,1024]{1,0:T(8,128)(2,1)S(1)} %get-tuple-element.25.rest_4_), channel_id=1, source_target_pairs={{0,12},{4,8},{8,4},{12,0},{1,13},{5,9},{9,5},{13,1},{2,14},{6,10},... | collective-permute-start | bytes 442376 | tf_op jit(solution)/shard_map/ppermute | solution.py:496
  41.0 11.0 %collective-permute-start.5 = (bf16[72,1024]{1,0:T(8,128)(2,1)S(1)}, bf16[72,1024]{1,0:T(8,128)(2,1)S(1)}, u32[]{:S(2)}, u32[]{:S(2)}) collective-permute-start(bf16[72,1024]{1,0:T(8,128)(2,1)S(1)} %get-tuple-element.25.rest_4_), channel_id=1, source_target_pairs={{0,8},{4,12},{8,0},{12,4},{1,9},{5,13},{9,1},{13,5},{2,10},{6,14},... | collective-permute-start | bytes 442376 | tf_op jit(solution)/shard_map/ppermute | solution.py:496
  41.0 11.0 %collective-permute-start.4 = (bf16[72,1024]{1,0:T(8,128)(2,1)S(1)}, bf16[72,1024]{1,0:T(8,128)(2,1)S(1)}, u32[]{:S(2)}, u32[]{:S(2)}) collective-permute-start(bf16[72,1024]{1,0:T(8,128)(2,1)S(1)} %get-tuple-element.25.rest_4_), channel_id=1, source_target_pairs={{0,4},{4,0},{8,12},{12,8},{1,5},{5,1},{9,13},{13,9},{2,6},{6,2},{1... | collective-permute-start | bytes 442376 | tf_op jit(solution)/shard_map/ppermute | solution.py:496
  42.4 3.7 %collective-permute-start.2 = (f32[16,128]{1,0:T(8,128)S(1)}, f32[16,128]{1,0:T(8,128)S(1)}, u32[]{:S(2)}, u32[]{:S(2)}) collective-permute-start(f32[16,128]{1,0:T(8,128)S(1)} %get-tuple-element.22.own_ref), channel_id=1, source_target_pairs={{0,16},{2,18},{16,0},{18,2},{1,17},{3,19},{17,1},{19,3},{4,20},{6,... | collective-permute-start | bytes 24584 | tf_op jit(solution)/shard_map/ppermute | solution.py:496

commit v19 on v16

--- a/solution.py
+++ b/solution.py
@@ -172,15 +172,16 @@
     *outs, mark_ref, gain, buffers, made, sems, out_sems = refs
     held, block, _ = buffers.shape
     steps = table_hbm.shape[0] // block
-    each = outs[0].shape[0] // block
+    sizes = (table_hbm.shape[0] - outs[1].shape[0], outs[1].shape[0])
+    places = [(out, at) for out, size in zip(outs, sizes) for at in range(0, size, block)]
 
     def copy(step):
         source = table_hbm.at[pl.ds(step * block, block)]
         return pltpu.make_async_copy(source, buffers.at[step % held], sems.at[step % held])
 
     def store(step):
-        target = outs[step // each].at[pl.ds(step % each * block, block)]
-        return pltpu.make_async_copy(made.at[step % held], target, out_sems.at[step % held])
+        out, at = places[step]
+        return pltpu.make_async_copy(made.at[step % held], out.at[pl.ds(at, block)], out_sems.at[step % held])
 
     for step in range(min(held, steps)):
         copy(step).start()
@@ -230,25 +231,36 @@
 
 def project(plan, place, lists, place_ref, w_ref, normed_ref, turn_ref, after_ref, *refs):
     if lists:
-        *refs, list_ref = refs
+        q_ref, vo_ref, list_ref, table, sems = refs
+        count, _, depth = table.shape
+
+        def copy(part):
+            source = normed_ref.at[pl.ds(0, table.shape[1]), part * depth : (part + 1) * depth]
+            return pltpu.make_async_copy(source, table.at[part], sems.at[part])
+
+        for part in range(count):
+            copy(part).start()
         read_lists(plan, w_ref, list_ref)
-    q_ref, vo_ref = refs[-2:]
+    else:
+        q_ref, vo_ref = refs[-2:]
     turns = turn_ref[place_ref[LINE]]
     half, k_half = plan.q_rows // 2, plan.k_rows // 2
     cosine, sine = turns[:, 0:1], turns[:, 1:2]
     cos_k, sin_k = cosine[:k_half], sine[:k_half]
-    moves = normed_ref.shape[0]
-    block = min(moves, 256)
+    moves = table.shape[1] if lists else normed_ref.shape[0]
+    block = moves if lists else math.gcd(moves, 128)
     for start in range(0, moves, block):
         at, to = slice(start, start + block), slice(place + start, place + start + block)
-        if len(w_ref.shape) == 3:
-            depth = w_ref.shape[2]
-            total = None
-            for s in range(w_ref.shape[0]):
-                term = matmul(w_ref[s], normed_ref[at, s * depth : (s + 1) * depth], NT)
-                total = term if total is None else total + term
-        else:
-            total = matmul(w_ref[...], normed_ref[at, :], NT)
+        total = None
+        for part in range(count if lists else w_ref.shape[0] if len(w_ref.shape) == 3 else 1):
+            w = w_ref[part] if len(w_ref.shape) == 3 else w_ref[...]
+            if lists:
+                copy(part).wait()
+                values = table[part]
+            else:
+                values = normed_ref[at, part * w.shape[1] : (part + 1) * w.shape[1]]
+            term = matmul(w, values, NT)
+            total = term if total is None else total + term
         first, second = total[:half], total[half : 2 * half]
         f_first = (first * cosine - second * sine).astype(BF16).astype(F32)
         f_second = (second * cosine + first * sine).astype(BF16).astype(F32)
@@ -457,13 +469,13 @@
     return pl.BlockSpec(memory_space=pl.ANY)
 
 
-def local_call(kernel, place, args, outs, scratch=(), mib=40, copied=(), flops=0, nbytes=0, aliases=None):
-    vmem = pl.BlockSpec(memory_space=pltpu.VMEM)
+def local_call(kernel, place, args, outs, scratch=(), mib=40, copied=(), flops=0, nbytes=0, aliases=None, fetched=()):
+    vmem, hbm = pl.BlockSpec(memory_space=pltpu.VMEM), pl.BlockSpec(memory_space=pltpu.HBM)
     return pl.pallas_call(
         kernel,
         out_shape=outs,
         in_specs=[pl.BlockSpec(memory_space=pltpu.SMEM)]
-        + [untouched() if at in copied else vmem for at in range(len(args))],
+        + [hbm if at in fetched else untouched() if at in copied else vmem for at in range(len(args))],
         out_specs=jax.tree.map(lambda x: vmem, outs),
         scratch_shapes=scratch,
         input_output_aliases=aliases or {},
@@ -545,10 +557,11 @@
     across = swap(payload, slab_axes, plan.slab, 2)
 
     block = min(moves, 128)
+    blocks = (moves * 3 // 8, moves * 5 // 8)
     vmem = pl.BlockSpec(memory_space=pltpu.VMEM)
     *normed, mark = pl.pallas_call(
         normalize,
-        out_shape=[*[shape((moves // 2, width), BF16)] * 2, pltpu.HBM((8, width), BF16)],
+        out_shape=[shape((moves, width), BF16), shape((blocks[1], width), BF16), pltpu.HBM((8, width), BF16)],
         in_specs=[untouched(), vmem, untouched()],
         out_specs=[untouched()] * 3,
         scratch_shapes=[
@@ -568,22 +581,31 @@
     outs = (shape(sent if plan.direct else (line, *sent), BF16), shape((plan.mine, moves), F32))
     across = tied(across, mark)
     diagonal = swap(across, slab_axes, plan.slab, 1)
-    filled, listed = (), None
-    for step, after in enumerate((across, beside)):
-        made = local_call(
-            functools.partial(project, plan, step * moves // 2, step == 0),
-            place,
-            (flat, normed[step], jnp.asarray(turns), after, *filled),
-            [*outs, *([shape((plan.share, plan.slots), F32)] if step == 0 else [])],
-            (),
-            20,
-            (3,),
-            moves * width * 1024,
-            moves * width,
-            {5: 0, 6: 1} if filled else None,
-        )
-        filled, listed = made[:2], made[2] if step == 0 else listed
-    queries, own_values = filled
+    parts = plan.peers if flat.ndim == 3 else 1
+    queries, own_values, listed = local_call(
+        functools.partial(project, plan, 0, True),
+        place,
+        (flat, normed[0], jnp.asarray(turns), across),
+        (*outs, shape((plan.share, plan.slots), F32)),
+        [pltpu.VMEM((parts, blocks[0], width // parts), BF16), pltpu.SemaphoreType.DMA((parts,))],
+        53,
+        (3,),
+        blocks[0] * width * 2048,
+        blocks[0] * width,
+        fetched=(1,),
+    )
+    queries, own_values = local_call(
+        functools.partial(project, plan, blocks[0], False),
+        place,
+        (flat, normed[1], jnp.asarray(turns), beside, queries, own_values),
+        outs,
+        (),
+        20,
+        (3,),
+        blocks[1] * width * 2048,
+        blocks[1] * width,
+        {5: 0, 6: 1},
+    )
     other = swap(listed, slab_axes, plan.slab, pair)
     if plan.direct:
         queries = [queries] + [swap(queries, "line", line, step) for step in range(1, line)]

time: 73 us -> 74.6 us (1.022)
  Pallas kernels: 30.9 us -> 33.5 us
  blocking collectives: 12.4 us -> 11.6 us
    pallas_call x5, Pallas kernels: 18.7 us -> 21.3 us  [local_call(): pl.pallas_call(kernel, out_shape=outs, in_specs=[pl.BlockSpec(memory_spac...]
    all_to_all x1, blocking collectives: 12.4 us -> 11.6 us  [per_device(): lax.all_to_all(parts.reshape(groups * back, plan.share, plan.slots), ('gr...]
    unnamed x12 -> x16, local copies, waits for them, and re-layouts: 3.15 us -> 2.91 us
  transfers between devices with their start and end apart: 8 -> 8, of which waited for: 4 -> 4; matrix products, arithmetic and copies ran while one was open for 0% -> 0% of each run, Pallas kernels for 28% -> 31%
where the time goes in v19:
time: 74.6 us; the launch traced here: 74.2 us
  Pallas kernels  33.5 us (45%)
  starting transfers between devices  18.6 us (25%)
  blocking collectives  11.6 us (16%)
  waiting for transfers between devices  7.36 us (10%)
  local copies, waits for them, and re-layouts  2.91 us (4%)
    pallas_call x5, Pallas kernels, local_call(): pl.pallas_call(kernel, out_shape=outs, in_specs=[pl.BlockSpec(memory_spac...  21.3 us
    all_to_all x1, blocking collectives, per_device(): lax.all_to_all(parts.reshape(groups * back, plan.share, plan.slots), ('gr...  11.6 us
    ppermute x7, starting transfers between devices, swap(): return lax.ppermute(x, names, [(at, at ^ step) for at in range(size)])  11.3 us
    pallas_call x1, Pallas kernels, per_device(): pl.pallas_call(normalize, out_shape=[shape((moves, width), BF16), shape((...  8.91 us
    all_to_all x1, starting transfers between devices, per_device(): lax.all_to_all(packed, ('line', 'pair'), split_axis=0, concat_axis=0, til...  7.27 us
    ppermute x7, waiting for transfers between devices, swap(): return lax.ppermute(x, names, [(at, at ^ step) for at in range(size)])  5.57 us
    unnamed x16, local copies, waits for them, and re-layouts  2.91 us
    pallas_call x1, Pallas kernels, per_device(): pl.pallas_call(functools.partial(pack_prefix, plan), out_shape=shape((boa...  2.18 us
  transfers between devices with their start and end apart: 8, of which 4 were waited for; matrix products, arithmetic and copies ran while one was open for 0% of the time, Pallas kernels for 31%

profile of v19, /device:TPU:0, one launch (start us, length us, event | category | flops | bytes accessed | tf_op | source)
XLA Modules:
  0.0 74.2 jit_solution(17232297055175981650)
XLA Ops:
  0.0 2.6 %shard_map.91.after_ref = bf16[8,104,512]{2,1,0:T(8,128)(2,1)} custom-call(s32[1]{0:T(128)} %bitcast.place_ref, bf16[512,1024]{1,0:T(8,128)(2,1)} %wq_hbm.1, bf16[512,256]{1,0:T(8,128)(2,1)} %wkv_hbm.1, bf16[8,128]{1,0:T(8,128)(2,1)} %bitcast.19, s32[1,512]{1,0:T(1,128)} %bitcast.13, s32[1,512]{1,0:T(1,128)} %bitcast.21), custom_call_target="tpu_custom_call" | custom-call | tf_op jit(solution)/shard_map/pallas_call | solution.py:474
  2.6 7.3 %all-to-all-start = ((bf16[8,104,512]{2,1,0:T(8,128)(2,1)}), bf16[8,104,512]{2,1,0:T(8,128)(2,1)S(1)}, u32[]{:S(2)}, u32[]{:S(2)}) async-start(bf16[8,104,512]{2,1,0:T(8,128)(2,1)} %shard_map.91.after_ref), calls=%async_computation | async-start | bytes 1703936 | tf_op jit(solution)/shard_map/all_to_all | solution.py:541
  9.9 2.2 %shard_map.93.rest_0_ = bf16[9,256,128]{2,1,0:T(8,128)(2,1)} custom-call(bf16[8,256,256]{2,1,0:T(8,128)(2,1)} %prefix_hbm.1, bf16[8,128]{1,0:T(8,128)(2,1)} %bitcast.20, bf16[8,104,512]{2,1,0:T(8,128)(2,1)} %shard_map.91.after_ref), custom_call_target="tpu_custom_call" | custom-call | tf_op jit(solution)/shard_map/pallas_call | solution.py:543
  12.1 1.6 %collective-permute-start.1 = (bf16[9,256,128]{2,1,0:T(8,128)(2,1)}, bf16[9,256,128]{2,1,0:T(8,128)(2,1)S(1)}, u32[]{:S(2)}, u32[]{:S(2)}) collective-permute-start(bf16[9,256,128]{2,1,0:T(8,128)(2,1)} %shard_map.93.rest_0_), channel_id=1, source_target_pairs={{0,16},{2,18},{16,0},{18,2},{1,17},{3,19},{17,1},{19,3},{4,20},{6,... | collective-permute-start | bytes 1769480 | tf_op jit(solution)/shard_map/ppermute | solution.py:492
  13.6 2.0 %collective-permute-start = (bf16[9,256,128]{2,1,0:T(8,128)(2,1)}, bf16[9,256,128]{2,1,0:T(8,128)(2,1)S(1)}, u32[]{:S(2)}, u32[]{:S(2)}) collective-permute-start(bf16[9,256,128]{2,1,0:T(8,128)(2,1)} %shard_map.93.rest_0_), channel_id=1, source_target_pairs={{0,2},{2,0},{16,18},{18,16},{1,3},{3,1},{17,19},{19,17},{4,6},{6,4... | collective-permute-start | bytes 1769480 | tf_op jit(solution)/shard_map/ppermute | solution.py:492
  15.7 8.9 %shard_map.92 = (bf16[1024,4096]{1,0:T(8,128)(2,1)}, bf16[640,4096]{1,0:T(8,128)(2,1)}, bf16[8,4096]{1,0:T(8,128)(2,1)}) custom-call(bf16[1024,4096]{1,0:T(8,128)(2,1)} %table_hbm.1, bf16[32,128]{1,0:T(8,128)(2,1)} %bitcast.18, bf16[8,104,512]{2,1,0:T(8,128)(2,1)} %shard_map.91.after_ref), custom_call_target="tpu_custom_call" | custom-call | flops 4194304 | bytes 1048576 | tf_op jit(solution)/shard_map/pallas_call | solution.py:562
  24.6 0.1 pad_add_fusion.place_ref
  24.7 2.5 %collective-permute-done.1.refs_0_ = bf16[9,256,128]{2,1,0:T(8,128)(2,1)S(1)} collective-permute-done((bf16[9,256,128]{2,1,0:T(8,128)(2,1)}, bf16[9,256,128]{2,1,0:T(8,128)(2,1)S(1)}, u32[]{:S(2)}, u32[]{:S(2)}) %collective-permute-start.1) | collective-permute-done | bytes 589856 | tf_op jit(solution)/shard_map/ppermute | solution.py:492
  27.1 0.8 %copy-done.3 = bf16[8,4096]{1,0:T(8,128)(2,1)S(1)} copy-done((bf16[8,4096]{1,0:T(8,128)(2,1)S(1)}, bf16[8,4096]{1,0:T(8,128)(2,1)}, u32[]{:S(2)}) %copy-start.3) | copy-done | bytes 65560
  28.0 1.7 %collective-permute-start.3 = (bf16[9,256,128]{2,1,0:T(8,128)(2,1)S(1)}, bf16[9,256,128]{2,1,0:T(8,128)(2,1)S(1)}, u32[]{:S(2)}, u32[]{:S(2)}) collective-permute-start(bf16[9,256,128]{2,1,0:T(8,128)(2,1)S(1)} %shard_map.94.after_ref.rest_2_), channel_id=1, source_target_pairs={{0,2},{2,0},{16,18},{18,16},{1,3},{3,1},{17,19},{19,17},{4,6},{6,4... | collective-permute-start | bytes 1769480 | tf_op jit(solution)/shard_map/ppermute | solution.py:492
  29.7 1.8 %all-to-all-done.w_ref = bf16[8,104,512]{2,1,0:T(8,128)(2,1)S(1)} async-done(((bf16[8,104,512]{2,1,0:T(8,128)(2,1)}), bf16[8,104,512]{2,1,0:T(8,128)(2,1)S(1)}, u32[]{:S(2)}, u32[]{:S(2)}) %all-to-all-start) | async-done | bytes 852000 | tf_op jit(solution)/shard_map/all_to_all | solution.py:541
  31.5 0.9 %copy-done.1 = bf16[8,104,512]{2,1,0:T(8,128)(2,1)} copy-done((bf16[8,104,512]{2,1,0:T(8,128)(2,1)}, bf16[8,104,512]{2,1,0:T(8,128)(2,1)S(1)}, u32[]{:S(2)}) %copy-start.1) | copy-done | bytes 851992
  32.4 4.7 %shard_map.95 = (bf16[72,1024]{1,0:T(8,128)(2,1)S(1)}, f32[2,1024]{1,0:T(2,128)S(1)}, f32[16,128]{1,0:T(8,128)S(1)}) custom-call(s32[4]{0:T(128)S(1)} %pad_add_fusion.place_ref, bf16[8,104,512]{2,1,0:T(8,128)(2,1)} %copy-done.1, bf16[1024,4096]{1,0:T(8,128)(2,1)} %get-tuple-element.17.normed_ref, f32[4,32,2]{2,1,0:T(8,128)S(1)} %copy-done.5, ...), custom_call_target="tpu_custom_call" | custom-call | flops 3221225472 | bytes 1572864 | tf_op jit(solution)/shard_map/pallas_call | solution.py:474
  37.2 1.1 %copy-done.2 = bf16[8,104,512]{2,1,0:T(8,128)(2,1)S(1)} copy-done((bf16[8,104,512]{2,1,0:T(8,128)(2,1)S(1)}, bf16[8,104,512]{2,1,0:T(8,128)(2,1)}, u32[]{:S(2)}) %copy-start.2) | copy-done | bytes 851992
  38.3 2.1 %shard_map.96 = (bf16[72,1024]{1,0:T(8,128)(2,1)S(1)}, f32[2,1024]{1,0:T(2,128)S(1)}) custom-call(s32[4]{0:T(128)S(1)} %pad_add_fusion.place_ref, bf16[8,104,512]{2,1,0:T(8,128)(2,1)S(1)} %copy-done.2, bf16[640,4096]{1,0:T(8,128)(2,1)S(1)} %bitcast.17, f32[4,32,2]{2,1,0:T(8,128)S(1)} %copy-done.5, ...), custom_call_target="tpu_custom_call", output_to_operand_aliasing={{0}: (5, {}), {1}: (6, {})} | custom-call | flops 5368709120 | bytes 2621440 | tf_op jit(solution)/shard_map/pallas_call | solution.py:474
  40.4 1.7 %collective-permute-start.6 = (bf16[72,1024]{1,0:T(8,128)(2,1)S(1)}, bf16[72,1024]{1,0:T(8,128)(2,1)S(1)}, u32[]{:S(2)}, u32[]{:S(2)}) collective-permute-start(bf16[72,1024]{1,0:T(8,128)(2,1)S(1)} %get-tuple-element.25.rest_4_), channel_id=1, source_target_pairs={{0,12},{4,8},{8,4},{12,0},{1,13},{5,9},{9,5},{13,1},{2,14},{6,10},... | collective-permute-start | bytes 442376 | tf_op jit(solution)/shard_map/ppermute | solution.py:492
  42.1 2.7 %collective-permute-start.4 = (bf16[72,1024]{1,0:T(8,128)(2,1)S(1)}, bf16[72,1024]{1,0:T(8,128)(2,1)S(1)}, u32[]{:S(2)}, u32[]{:S(2)}) collective-permute-start(bf16[72,1024]{1,0:T(8,128)(2,1)S(1)} %get-tuple-element.25.rest_4_), channel_id=1, source_target_pairs={{0,4},{4,0},{8,12},{12,8},{1,5},{5,1},{9,13},{13,9},{2,6},{6,2},{1... | collective-permute-start | bytes 442376 | tf_op jit(solution)/shard_map/ppermute | solution.py:492
  44.9 1.5 %collective-permute-start.2 = (f32[16,128]{1,0:T(8,128)S(1)}, f32[16,128]{1,0:T(8,128)S(1)}, u32[]{:S(2)}, u32[]{:S(2)}) collective-permute-start(f32[16,128]{1,0:T(8,128)S(1)} %get-tuple-element.22.own_ref), channel_id=1, source_target_pairs={{0,16},{2,18},{16,0},{18,2},{1,17},{3,19},{17,1},{19,3},{4,20},{6,... | collective-permute-start | bytes 24584 | tf_op jit(solution)/shard_map/ppermute | solution.py:492
  46.4 2.1 %collective-permute-done.2.other_ref = f32[16,128]{1,0:T(8,128)S(1)} collective-permute-done((f32[16,128]{1,0:T(8,128)S(1)}, f32[16,128]{1,0:T(8,128)S(1)}, u32[]{:S(2)}, u32[]{:S(2)}) %collective-permute-start.2) | collective-permute-done | bytes 8224 | tf_op jit(solution)/shard_map/ppermute | solution.py:492
  48.5 4.9 %shard_map.97 = (bf16[8,1024,512]{2,1,0:T(8,128)(2,1)S(1)}, f32[3,8,256,256]{3,2,1,0:T(8,128)S(1)}, s32[1,512]{1,0:T(1,128)S(1)}) custom-call(s32[4]{0:T(128)S(1)} %pad_add_fusion.place_ref, s32[1,512]{1,0:T(1,128)S(1)} %bitcast.14, f32[16,128]{1,0:T(8,128)S(1)} %get-tuple-element.22.own_ref, f32[16,128]{1,0:T(8,128)S(1)} %collective-permute-done.2.other_ref, ...), custom_call_target="tpu_custom_call" | custom-call | flops 1000000000 | bytes 1000000 | tf_op jit(solution)/shard_map/pallas_call | solution.py:474
  53.4 1.0 %collective-permute-done.5.rest_6_ = bf16[72,1024]{1,0:T(8,128)(2,1)S(1)} collective-permute-done((bf16[72,1024]{1,0:T(8,128)(2,1)S(1)}, bf16[72,1024]{1,0:T(8,128)(2,1)S(1)}, u32[]{:S(2)}, u32[]{:S(2)}) %collective-permute-start.5) | collective-permute-done | bytes 147488 | tf_op jit(solution)/shard_map/ppermute | solution.py:492
  54.4 7.1 %shard_map.98 = bf16[2,16,16,128]{3,2,1,0:T(8,128)(2,1)S(1)} custom-call(s32[4]{0:T(128)S(1)} %pad_add_fusion.place_ref, f32[2,1024]{1,0:T(2,128)S(1)} %get-tuple-element.21.vo_ref, f32[16,128]{1,0:T(8,128)S(1)} %get-tuple-element.22.own_ref, f32[16,128]{1,0:T(8,128)S(1)} %collective-permute-done.2.other_ref, ...), custom_call_target="tpu_custom_call" | custom-call | tf_op jit(solution)/shard_map/pallas_call | solution.py:474
  61.5 11.6 %all_to_all.10 = bf16[32,16,128]{2,1,0:T(8,128)(2,1)S(1)} all-to-all(bf16[32,16,128]{2,1,0:T(8,128)(2,1)S(1)} %bitcast.11), channel_id=1, replica_groups=mesh['groups'=2,'line'=4,'pair'=2,'tensor'=2] {'groups','line','pair','t..., dimensions={0} | all-to-all | bytes 262144 | tf_op jit(solution)/shard_map/all_to_all | solution.py:645
  73.1 1.1 %shard_map.99 = f32[1,512]{1,0:T(1,128)} custom-call(bf16[2,4,4,16,128]{4,3,2,1,0:T(8,128)(2,1)S(1)} %bitcast.12, s32[1,512]{1,0:T(1,128)S(1)} %bitcast.15, s32[1,512]{1,0:T(1,128)S(1)} %get-tuple-element.26.slot_ref), custom_call_target="tpu_custom_call" | custom-call | tf_op jit(solution)/shard_map/pallas_call | solution.py:653
  (20 shorter events, 0.0 us)
Async XLA Ops:
  0.0 32.4 %copy-start.5 = (f32[4,32,2]{2,1,0:T(8,128)S(1)}, f32[4,32,2]{2,1,0:T(8,128)}, u32[]{:S(2)}) copy-start(f32[4,32,2]{2,1,0:T(8,128)} %constant.17.clone.turn_ref) | copy-start | bytes 3076
  2.6 28.9 %all-to-all-start = ((bf16[8,104,512]{2,1,0:T(8,128)(2,1)}), bf16[8,104,512]{2,1,0:T(8,128)(2,1)S(1)}, u32[]{:S(2)}, u32[]{:S(2)}) async-start(bf16[8,104,512]{2,1,0:T(8,128)(2,1)} %shard_map.91.after_ref), calls=%async_computation | async-start | bytes 1703936 | tf_op jit(solution)/shard_map/all_to_all | solution.py:541
  12.1 15.1 %collective-permute-start.1 = (bf16[9,256,128]{2,1,0:T(8,128)(2,1)}, bf16[9,256,128]{2,1,0:T(8,128)(2,1)S(1)}, u32[]{:S(2)}, u32[]{:S(2)}) collective-permute-start(bf16[9,256,128]{2,1,0:T(8,128)(2,1)} %shard_map.93.rest_0_), channel_id=1, source_target_pairs={{0,16},{2,18},{16,0},{18,2},{1,17},{3,19},{17,1},{19,3},{4,20},{6,... | collective-permute-start | bytes 1769480 | tf_op jit(solution)/shard_map/ppermute | solution.py:492
  13.6 23.5 %collective-permute-start = (bf16[9,256,128]{2,1,0:T(8,128)(2,1)}, bf16[9,256,128]{2,1,0:T(8,128)(2,1)S(1)}, u32[]{:S(2)}, u32[]{:S(2)}) collective-permute-start(bf16[9,256,128]{2,1,0:T(8,128)(2,1)} %shard_map.93.rest_0_), channel_id=1, source_target_pairs={{0,2},{2,0},{16,18},{18,16},{1,3},{3,1},{17,19},{19,17},{4,6},{6,4... | collective-permute-start | bytes 1769480 | tf_op jit(solution)/shard_map/ppermute | solution.py:492
  27.1 0.8 %copy-start.3 = (bf16[8,4096]{1,0:T(8,128)(2,1)S(1)}, bf16[8,4096]{1,0:T(8,128)(2,1)}, u32[]{:S(2)}) copy-start(bf16[8,4096]{1,0:T(8,128)(2,1)} %get-tuple-element.18.refs_1_) | copy-start | bytes 196612
  28.0 25.4 %collective-permute-start.3 = (bf16[9,256,128]{2,1,0:T(8,128)(2,1)S(1)}, bf16[9,256,128]{2,1,0:T(8,128)(2,1)S(1)}, u32[]{:S(2)}, u32[]{:S(2)}) collective-permute-start(bf16[9,256,128]{2,1,0:T(8,128)(2,1)S(1)} %shard_map.94.after_ref.rest_2_), channel_id=1, source_target_pairs={{0,2},{2,0},{16,18},{18,16},{1,3},{3,1},{17,19},{19,17},{4,6},{6,4... | collective-permute-start | bytes 1769480 | tf_op jit(solution)/shard_map/ppermute | solution.py:492
  31.5 0.9 %copy-start.1 = (bf16[8,104,512]{2,1,0:T(8,128)(2,1)}, bf16[8,104,512]{2,1,0:T(8,128)(2,1)S(1)}, u32[]{:S(2)}) copy-start(bf16[8,104,512]{2,1,0:T(8,128)(2,1)S(1)} %all-to-all-done.w_ref) | copy-start | bytes 2555908
  31.5 5.6 %slice-start = ((s8[5242880]{0:T(1024)(128)(4,1)}), s8[4194304]{0:T(1024)(128)(4,1)S(1)}, s32[]{:S(2)}) async-start(s8[5242880]{0:T(1024)(128)(4,1)} %bitcast.16), calls=%async_computation.2 | async-start | bytes 8388608
  32.4 4.7 %slice-start.1 = ((s8[5242880]{0:T(1024)(128)(4,1)}), s8[1048576]{0:T(1024)(128)(4,1)S(1)}, s32[]{:S(2)}) async-start(s8[5242880]{0:T(1024)(128)(4,1)} %bitcast.16), calls=%async_computation.3 | async-start | bytes 2097152
  37.1 1.2 %copy-start.2 = (bf16[8,104,512]{2,1,0:T(8,128)(2,1)S(1)}, bf16[8,104,512]{2,1,0:T(8,128)(2,1)}, u32[]{:S(2)}) copy-start(bf16[8,104,512]{2,1,0:T(8,128)(2,1)} %copy-done.1) | copy-start | bytes 2555908
  38.3 10.2 %copy-start = (bf16[9,256,128]{2,1,0:T(8,128)(2,1)S(1)}, bf16[9,256,128]{2,1,0:T(8,128)(2,1)}, u32[]{:S(2)}) copy-start(bf16[9,256,128]{2,1,0:T(8,128)(2,1)} %shard_map.93.rest_0_) | copy-start | bytes 1769476
  38.3 10.2 %copy-start.4 = (s32[512,1]{0,1:T(1,128)S(1)}, s32[512,1]{0,1:T(1,128)}, u32[]{:S(2)}) copy-start(s32[512,1]{0,1:T(1,128)} %param.11) | copy-start | bytes 6148
  40.4 13.0 %collective-permute-start.6 = (bf16[72,1024]{1,0:T(8,128)(2,1)S(1)}, bf16[72,1024]{1,0:T(8,128)(2,1)S(1)}, u32[]{:S(2)}, u32[]{:S(2)}) collective-permute-start(bf16[72,1024]{1,0:T(8,128)(2,1)S(1)} %get-tuple-element.25.rest_4_), channel_id=1, source_target_pairs={{0,12},{4,8},{8,4},{12,0},{1,13},{5,9},{9,5},{13,1},{2,14},{6,10},... | collective-permute-start | bytes 442376 | tf_op jit(solution)/shard_map/ppermute | solution.py:492
  42.1 12.3 %collective-permute-start.5 = (bf16[72,1024]{1,0:T(8,128)(2,1)S(1)}, bf16[72,1024]{1,0:T(8,128)(2,1)S(1)}, u32[]{:S(2)}, u32[]{:S(2)}) collective-permute-start(bf16[72,1024]{1,0:T(8,128)(2,1)S(1)} %get-tuple-element.25.rest_4_), channel_id=1, source_target_pairs={{0,8},{4,12},{8,0},{12,4},{1,9},{5,13},{9,1},{13,5},{2,10},{6,14},... | collective-permute-start | bytes 442376 | tf_op jit(solution)/shard_map/ppermute | solution.py:492
  42.1 12.3 %collective-permute-start.4 = (bf16[72,1024]{1,0:T(8,128)(2,1)S(1)}, bf16[72,1024]{1,0:T(8,128)(2,1)S(1)}, u32[]{:S(2)}, u32[]{:S(2)}) collective-permute-start(bf16[72,1024]{1,0:T(8,128)(2,1)S(1)} %get-tuple-element.25.rest_4_), channel_id=1, source_target_pairs={{0,4},{4,0},{8,12},{12,8},{1,5},{5,1},{9,13},{13,9},{2,6},{6,2},{1... | collective-permute-start | bytes 442376 | tf_op jit(solution)/shard_map/ppermute | solution.py:492
  44.9 3.7 %collective-permute-start.2 = (f32[16,128]{1,0:T(8,128)S(1)}, f32[16,128]{1,0:T(8,128)S(1)}, u32[]{:S(2)}, u32[]{:S(2)}) collective-permute-start(f32[16,128]{1,0:T(8,128)S(1)} %get-tuple-element.22.own_ref), channel_id=1, source_target_pairs={{0,16},{2,18},{16,0},{18,2},{1,17},{3,19},{17,1},{19,3},{4,20},{6,... | collective-permute-start | bytes 24584 | tf_op jit(solution)/shard_map/ppermute | solution.py:492

commit v20 on v16

--- a/solution.py
+++ b/solution.py
@@ -238,7 +238,8 @@
     cosine, sine = turns[:, 0:1], turns[:, 1:2]
     cos_k, sin_k = cosine[:k_half], sine[:k_half]
     moves = normed_ref.shape[0]
-    block = min(moves, 256)
+    block = min(moves, HD)
+    every = []
     for start in range(0, moves, block):
         at, to = slice(start, start + block), slice(place + start, place + start + block)
         if len(w_ref.shape) == 3:
@@ -261,17 +262,22 @@
             logit = jnp.sum(f_first[own] * k_first + f_second[own] * k_second, axis=0, keepdims=True)
             logits.append(logit.astype(BF16).astype(F32))
             tails.append(logit - logits[-1])
-        pad = plan.line_rows - plan.q_rows - 2 * plan.mine
-        pieces = [f_first, f_second, *logits, *tails]
-        if pad:
-            pieces.append(jnp.zeros((pad, block), F32))
-        out = jnp.concatenate(pieces, axis=0).astype(BF16)
         if plan.direct:
-            q_ref[:, to] = out
+            chunk = (place + start) // block * plan.q_rows
+            q_ref[chunk : chunk + plan.q_rows] = jnp.concatenate([f_first, f_second], axis=0).astype(BF16)
+            every += [*logits, *tails]
         else:
+            pad = plan.line_rows - plan.q_rows - 2 * plan.mine
+            pieces = [f_first, f_second, *logits, *tails]
+            if pad:
+                pieces.append(jnp.zeros((pad, block), F32))
+            out = jnp.concatenate(pieces, axis=0).astype(BF16)
             for line in range(plan.line):
                 q_ref[line, :, to] = out
         vo_ref[:, to] = total[plan.fold_at : plan.list_at]
+    if plan.direct:
+        first = vo_ref.shape[1] // HD * plan.q_rows + place // block * 2 * plan.mine
+        q_ref[first : first + len(every)] = jnp.concatenate(every, axis=0).astype(BF16)
 
 
 def tied(x, *others):
@@ -355,20 +361,31 @@
     boards = prefix_refs[0].shape[0] - 1
     query_rows = mine * HD
 
-    mixed = None
+    mixed = own_logits = None
     for step, q_ref in enumerate(q_refs):
-        r = lax.broadcasted_iota(jnp.int32, (query_rows + 8, q_ref.shape[0]), 0)
-        c = lax.broadcasted_iota(jnp.int32, (query_rows + 8, q_ref.shape[0]), 1)
+        if plan.direct:
+            chunks = range(moves // HD)
+            values = jnp.concatenate([q_ref[c * plan.q_rows : (c + 1) * plan.q_rows] for c in chunks], axis=1)
+            tails = q_ref[moves // HD * plan.q_rows :].astype(F32)
+            tails = jnp.concatenate([tails[c * 2 * mine : (c + 1) * 2 * mine] for c in chunks], axis=1)
+            tails = tails[:mine] + tails[mine:]
+            own_logits = tails if own_logits is None else own_logits + tails
+        else:
+            values = q_ref[...]
+        r = lax.broadcasted_iota(jnp.int32, (query_rows + 8, values.shape[0]), 0)
+        c = lax.broadcasted_iota(jnp.int32, (query_rows + 8, values.shape[0]), 1)
         line, at = (place_ref[LINE] ^ step, c) if plan.direct else (c // plan.line_rows, c % plan.line_rows)
         part, head, entry = at // (mine * plan.pairs), (at // plan.pairs) % mine, at % plan.pairs
         goes = jnp.where(at < plan.q_rows, head * HD + part * HALF + line * plan.pairs + entry, -1)
         tail = at - plan.q_rows
         goes = jnp.where((tail >= 0) & (tail < 2 * mine), query_rows + tail % mine, goes)
-        term = matmul(jnp.where(r == goes, 1.0, 0.0).astype(BF16), q_ref[...])
+        term = matmul(jnp.where(r == goes, 1.0, 0.0).astype(BF16), values)
         mixed = term if mixed is None else mixed + term
+    if own_logits is None:
+        own_logits = mixed[query_rows : query_rows + mine]
     table[:query_rows] = mixed[:query_rows].astype(BF16)
     extra[...] = jnp.zeros_like(extra)
-    for place, value in ((0, mixed[query_rows : query_rows + mine]), (2 * mine, vo_ref[...])):
+    for place, value in ((0, own_logits), (2 * mine, vo_ref[...])):
         rounded = value.astype(BF16).astype(F32)
         extra[place : place + mine] = rounded
         extra[place + mine : place + 2 * mine] = value - rounded
@@ -564,8 +581,8 @@
     turns = turn_table(prefix_len).reshape(line, 1, plan.pairs, 2)
     turns = np.tile(turns, (1, plan.mine, 1, 1)).reshape(line, plan.mine * plan.pairs, 2)
     flat = weights.transpose(1, 0, 2).reshape(plan.rows, width) if depth % HD else weights
-    sent = (plan.line_rows, moves)
-    outs = (shape(sent if plan.direct else (line, *sent), BF16), shape((plan.mine, moves), F32))
+    sent = (moves // HD * (plan.q_rows + 2 * plan.mine), HD) if plan.direct else (line, plan.line_rows, moves)
+    outs = (shape(sent, BF16), shape((plan.mine, moves), F32))
     across = tied(across, mark)
     diagonal = swap(across, slab_axes, plan.slab, 1)
     filled, listed = (), None

time: 73 us -> 72.2 us (0.989)
  no operation moved by 1% of the time
where the time goes in v20:
time: 72.2 us; the launch traced here: 71.8 us
  Pallas kernels  30.6 us (42%)
  starting transfers between devices  18.6 us (26%)
  blocking collectives  12.4 us (17%)
  waiting for transfers between devices  6.71 us (9%)
  local copies, waits for them, and re-layouts  3.3 us (5%)
    pallas_call x5, Pallas kernels, local_call(): pl.pallas_call(kernel, out_shape=outs, in_specs=[pl.BlockSpec(memory_spac...  18.4 us
    all_to_all x1, blocking collectives, per_device(): lax.all_to_all(parts.reshape(groups * back, plan.share, plan.slots), ('gr...  12.4 us
    ppermute x7, starting transfers between devices, swap(): return lax.ppermute(x, names, [(at, at ^ step) for at in range(size)])  11.3 us
    pallas_call x1, Pallas kernels, per_device(): pl.pallas_call(normalize, out_shape=[*[shape((moves // 2, width), BF16)]...  8.91 us
    all_to_all x1, starting transfers between devices, per_device(): lax.all_to_all(packed, ('line', 'pair'), split_axis=0, concat_axis=0, til...  7.26 us
    ppermute x7, waiting for transfers between devices, swap(): return lax.ppermute(x, names, [(at, at ^ step) for at in range(size)])  4.96 us
    unnamed x12, local copies, waits for them, and re-layouts  3.3 us
    pallas_call x1, Pallas kernels, per_device(): pl.pallas_call(functools.partial(pack_prefix, plan), out_shape=shape((boa...  2.22 us
  transfers between devices with their start and end apart: 8, of which 4 were waited for; matrix products, arithmetic and copies ran while one was open for 0% of the time, Pallas kernels for 28%

profile of v20, /device:TPU:0, one launch (start us, length us, event | category | flops | bytes accessed | tf_op | source)
XLA Modules:
  0.0 71.8 jit_solution(8914577523356532016)
XLA Ops:
  0.0 2.6 %shard_map.91.after_ref = bf16[8,104,512]{2,1,0:T(8,128)(2,1)} custom-call(s32[1]{0:T(128)} %bitcast.place_ref, bf16[512,1024]{1,0:T(8,128)(2,1)} %wq_hbm.1, bf16[512,256]{1,0:T(8,128)(2,1)} %wkv_hbm.1, bf16[8,128]{1,0:T(8,128)(2,1)} %bitcast.17, s32[1,512]{1,0:T(1,128)} %bitcast.13, s32[1,512]{1,0:T(1,128)} %bitcast.19), custom_call_target="tpu_custom_call" | custom-call | tf_op jit(solution)/shard_map/pallas_call | solution.py:479
  2.6 7.3 %all-to-all-start = ((bf16[8,104,512]{2,1,0:T(8,128)(2,1)}), bf16[8,104,512]{2,1,0:T(8,128)(2,1)S(1)}, u32[]{:S(2)}, u32[]{:S(2)}) async-start(bf16[8,104,512]{2,1,0:T(8,128)(2,1)} %shard_map.91.after_ref), calls=%async_computation | async-start | bytes 1703936 | tf_op jit(solution)/shard_map/all_to_all | solution.py:546
  9.9 2.2 %shard_map.93.rest_0_ = bf16[9,256,128]{2,1,0:T(8,128)(2,1)} custom-call(bf16[8,256,256]{2,1,0:T(8,128)(2,1)} %prefix_hbm.1, bf16[8,128]{1,0:T(8,128)(2,1)} %bitcast.18, bf16[8,104,512]{2,1,0:T(8,128)(2,1)} %shard_map.91.after_ref), custom_call_target="tpu_custom_call" | custom-call | tf_op jit(solution)/shard_map/pallas_call | solution.py:548
  12.1 1.6 %collective-permute-start.1 = (bf16[9,256,128]{2,1,0:T(8,128)(2,1)}, bf16[9,256,128]{2,1,0:T(8,128)(2,1)S(1)}, u32[]{:S(2)}, u32[]{:S(2)}) collective-permute-start(bf16[9,256,128]{2,1,0:T(8,128)(2,1)} %shard_map.93.rest_0_), channel_id=1, source_target_pairs={{0,16},{2,18},{16,0},{18,2},{1,17},{3,19},{17,1},{19,3},{4,20},{6,... | collective-permute-start | bytes 1769480 | tf_op jit(solution)/shard_map/ppermute | solution.py:497
  13.7 2.0 %collective-permute-start = (bf16[9,256,128]{2,1,0:T(8,128)(2,1)}, bf16[9,256,128]{2,1,0:T(8,128)(2,1)S(1)}, u32[]{:S(2)}, u32[]{:S(2)}) collective-permute-start(bf16[9,256,128]{2,1,0:T(8,128)(2,1)} %shard_map.93.rest_0_), channel_id=1, source_target_pairs={{0,2},{2,0},{16,18},{18,16},{1,3},{3,1},{17,19},{19,17},{4,6},{6,4... | collective-permute-start | bytes 1769480 | tf_op jit(solution)/shard_map/ppermute | solution.py:497
  15.7 8.9 %shard_map.92 = (bf16[512,4096]{1,0:T(8,128)(2,1)}, bf16[512,4096]{1,0:T(8,128)(2,1)}, bf16[8,4096]{1,0:T(8,128)(2,1)}) custom-call(bf16[1024,4096]{1,0:T(8,128)(2,1)} %table_hbm.1, bf16[32,128]{1,0:T(8,128)(2,1)} %bitcast.16, bf16[8,104,512]{2,1,0:T(8,128)(2,1)} %shard_map.91.after_ref), custom_call_target="tpu_custom_call" | custom-call | flops 4194304 | bytes 1048576 | tf_op jit(solution)/shard_map/pallas_call | solution.py:566
  24.7 0.1 pad_add_fusion.place_ref
  24.7 2.5 %collective-permute-done.1.refs_0_ = bf16[9,256,128]{2,1,0:T(8,128)(2,1)S(1)} collective-permute-done((bf16[9,256,128]{2,1,0:T(8,128)(2,1)}, bf16[9,256,128]{2,1,0:T(8,128)(2,1)S(1)}, u32[]{:S(2)}, u32[]{:S(2)}) %collective-permute-start.1) | collective-permute-done | bytes 589856 | tf_op jit(solution)/shard_map/ppermute | solution.py:497
  27.2 0.8 %copy-done.1 = bf16[8,4096]{1,0:T(8,128)(2,1)S(1)} copy-done((bf16[8,4096]{1,0:T(8,128)(2,1)S(1)}, bf16[8,4096]{1,0:T(8,128)(2,1)}, u32[]{:S(2)}) %copy-start.1) | copy-done | bytes 65560
  28.1 1.7 %collective-permute-start.3 = (bf16[9,256,128]{2,1,0:T(8,128)(2,1)S(1)}, bf16[9,256,128]{2,1,0:T(8,128)(2,1)S(1)}, u32[]{:S(2)}, u32[]{:S(2)}) collective-permute-start(bf16[9,256,128]{2,1,0:T(8,128)(2,1)S(1)} %shard_map.94.after_ref.rest_2_), channel_id=1, source_target_pairs={{0,2},{2,0},{16,18},{18,16},{1,3},{3,1},{17,19},{19,17},{4,6},{6,4... | collective-permute-start | bytes 1769480 | tf_op jit(solution)/shard_map/ppermute | solution.py:497
  29.8 1.8 %all-to-all-done.w_ref = bf16[8,104,512]{2,1,0:T(8,128)(2,1)S(1)} async-done(((bf16[8,104,512]{2,1,0:T(8,128)(2,1)}), bf16[8,104,512]{2,1,0:T(8,128)(2,1)S(1)}, u32[]{:S(2)}, u32[]{:S(2)}) %all-to-all-start) | async-done | bytes 852000 | tf_op jit(solution)/shard_map/all_to_all | solution.py:546
  31.5 2.2 %copy-done.4 = bf16[512,4096]{1,0:T(8,128)(2,1)S(1)} copy-done((bf16[512,4096]{1,0:T(8,128)(2,1)S(1)}, bf16[512,4096]{1,0:T(8,128)(2,1)}, u32[]{:S(2)}) %copy-start.4) | copy-done | bytes 4194328
  33.7 1.9 %shard_map.95 = (bf16[544,128]{1,0:T(8,128)(2,1)S(1)}, f32[2,1024]{1,0:T(2,128)S(1)}, f32[16,128]{1,0:T(8,128)S(1)}) custom-call(s32[4]{0:T(128)S(1)} %pad_add_fusion.place_ref, bf16[8,104,512]{2,1,0:T(8,128)(2,1)S(1)} %all-to-all-done.w_ref, bf16[512,4096]{1,0:T(8,128)(2,1)S(1)} %copy-done.4, f32[4,32,2]{2,1,0:T(8,128)S(1)} %copy-done.5, ...), custom_call_target="tpu_custom_call" | custom-call | flops 4294967296 | bytes 4194304 | tf_op jit(solution)/shard_map/pallas_call | solution.py:479
  35.7 0.3 copy-done.3
  35.9 1.8 %shard_map.96 = (bf16[544,128]{1,0:T(8,128)(2,1)S(1)}, f32[2,1024]{1,0:T(2,128)S(1)}) custom-call(s32[4]{0:T(128)S(1)} %pad_add_fusion.place_ref, bf16[8,104,512]{2,1,0:T(8,128)(2,1)S(1)} %all-to-all-done.w_ref, bf16[512,4096]{1,0:T(8,128)(2,1)S(1)} %copy-done.3, f32[4,32,2]{2,1,0:T(8,128)S(1)} %copy-done.5, ...), custom_call_target="tpu_custom_call", output_to_operand_aliasing={{0}: (5, {}), {1}: (6, {})} | custom-call | flops 4294967296 | bytes 4194304 | tf_op jit(solution)/shard_map/pallas_call | solution.py:479
  37.8 3.0 %collective-permute-start.6 = (bf16[544,128]{1,0:T(8,128)(2,1)S(1)}, bf16[544,128]{1,0:T(8,128)(2,1)S(1)}, u32[]{:S(2)}, u32[]{:S(2)}) collective-permute-start(bf16[544,128]{1,0:T(8,128)(2,1)S(1)} %get-tuple-element.25.rest_4_), channel_id=1, source_target_pairs={{0,12},{4,8},{8,4},{12,0},{1,13},{5,9},{9,5},{13,1},{2,14},{6,10},... | collective-permute-start | bytes 417800 | tf_op jit(solution)/shard_map/ppermute | solution.py:497
  40.8 1.4 %collective-permute-start.4 = (bf16[544,128]{1,0:T(8,128)(2,1)S(1)}, bf16[544,128]{1,0:T(8,128)(2,1)S(1)}, u32[]{:S(2)}, u32[]{:S(2)}) collective-permute-start(bf16[544,128]{1,0:T(8,128)(2,1)S(1)} %get-tuple-element.25.rest_4_), channel_id=1, source_target_pairs={{0,4},{4,0},{8,12},{12,8},{1,5},{5,1},{9,13},{13,9},{2,6},{6,2},{1... | collective-permute-start | bytes 417800 | tf_op jit(solution)/shard_map/ppermute | solution.py:497
  42.2 1.5 %collective-permute-start.2 = (f32[16,128]{1,0:T(8,128)S(1)}, f32[16,128]{1,0:T(8,128)S(1)}, u32[]{:S(2)}, u32[]{:S(2)}) collective-permute-start(f32[16,128]{1,0:T(8,128)S(1)} %get-tuple-element.22.own_ref), channel_id=1, source_target_pairs={{0,16},{2,18},{16,0},{18,2},{1,17},{3,19},{17,1},{19,3},{4,20},{6,... | collective-permute-start | bytes 24584 | tf_op jit(solution)/shard_map/ppermute | solution.py:497
  43.8 2.1 %collective-permute-done.2.other_ref = f32[16,128]{1,0:T(8,128)S(1)} collective-permute-done((f32[16,128]{1,0:T(8,128)S(1)}, f32[16,128]{1,0:T(8,128)S(1)}, u32[]{:S(2)}, u32[]{:S(2)}) %collective-permute-start.2) | collective-permute-done | bytes 8224 | tf_op jit(solution)/shard_map/ppermute | solution.py:497
  45.9 4.9 %shard_map.97 = (bf16[8,1024,512]{2,1,0:T(8,128)(2,1)S(1)}, f32[3,8,256,256]{3,2,1,0:T(8,128)S(1)}, s32[1,512]{1,0:T(1,128)S(1)}) custom-call(s32[4]{0:T(128)S(1)} %pad_add_fusion.place_ref, s32[1,512]{1,0:T(1,128)S(1)} %bitcast.14, f32[16,128]{1,0:T(8,128)S(1)} %get-tuple-element.22.own_ref, f32[16,128]{1,0:T(8,128)S(1)} %collective-permute-done.2.other_ref, ...), custom_call_target="tpu_custom_call" | custom-call | flops 1000000000 | bytes 1000000 | tf_op jit(solution)/shard_map/pallas_call | solution.py:479
  50.8 0.4 collective-permute-done.5.rest_6_
  51.2 7.1 %shard_map.98 = bf16[2,16,16,128]{3,2,1,0:T(8,128)(2,1)S(1)} custom-call(s32[4]{0:T(128)S(1)} %pad_add_fusion.place_ref, f32[2,1024]{1,0:T(2,128)S(1)} %get-tuple-element.21.vo_ref, f32[16,128]{1,0:T(8,128)S(1)} %get-tuple-element.22.own_ref, f32[16,128]{1,0:T(8,128)S(1)} %collective-permute-done.2.other_ref, ...), custom_call_target="tpu_custom_call" | custom-call | tf_op jit(solution)/shard_map/pallas_call | solution.py:479
  58.3 12.4 %all_to_all.10 = bf16[32,16,128]{2,1,0:T(8,128)(2,1)S(1)} all-to-all(bf16[32,16,128]{2,1,0:T(8,128)(2,1)S(1)} %bitcast.11), channel_id=1, replica_groups=mesh['groups'=2,'line'=4,'pair'=2,'tensor'=2] {'groups','line','pair','t..., dimensions={0} | all-to-all | bytes 262144 | tf_op jit(solution)/shard_map/all_to_all | solution.py:640
  70.7 1.1 %shard_map.99 = f32[1,512]{1,0:T(1,128)} custom-call(bf16[2,4,4,16,128]{4,3,2,1,0:T(8,128)(2,1)S(1)} %bitcast.12, s32[1,512]{1,0:T(1,128)S(1)} %bitcast.15, s32[1,512]{1,0:T(1,128)S(1)} %get-tuple-element.26.slot_ref), custom_call_target="tpu_custom_call" | custom-call | tf_op jit(solution)/shard_map/pallas_call | solution.py:648
  (15 shorter events, 0.0 us)
Async XLA Ops:
  2.6 28.9 %all-to-all-start = ((bf16[8,104,512]{2,1,0:T(8,128)(2,1)}), bf16[8,104,512]{2,1,0:T(8,128)(2,1)S(1)}, u32[]{:S(2)}, u32[]{:S(2)}) async-start(bf16[8,104,512]{2,1,0:T(8,128)(2,1)} %shard_map.91.after_ref), calls=%async_computation | async-start | bytes 1703936 | tf_op jit(solution)/shard_map/all_to_all | solution.py:546
  9.9 21.6 %copy-start.5 = (f32[4,32,2]{2,1,0:T(8,128)S(1)}, f32[4,32,2]{2,1,0:T(8,128)}, u32[]{:S(2)}) copy-start(f32[4,32,2]{2,1,0:T(8,128)} %constant.17.clone.turn_ref) | copy-start | bytes 3076
  12.1 15.1 %collective-permute-start.1 = (bf16[9,256,128]{2,1,0:T(8,128)(2,1)}, bf16[9,256,128]{2,1,0:T(8,128)(2,1)S(1)}, u32[]{:S(2)}, u32[]{:S(2)}) collective-permute-start(bf16[9,256,128]{2,1,0:T(8,128)(2,1)} %shard_map.93.rest_0_), channel_id=1, source_target_pairs={{0,16},{2,18},{16,0},{18,2},{1,17},{3,19},{17,1},{19,3},{4,20},{6,... | collective-permute-start | bytes 1769480 | tf_op jit(solution)/shard_map/ppermute | solution.py:497
  13.7 21.9 %collective-permute-start = (bf16[9,256,128]{2,1,0:T(8,128)(2,1)}, bf16[9,256,128]{2,1,0:T(8,128)(2,1)S(1)}, u32[]{:S(2)}, u32[]{:S(2)}) collective-permute-start(bf16[9,256,128]{2,1,0:T(8,128)(2,1)} %shard_map.93.rest_0_), channel_id=1, source_target_pairs={{0,2},{2,0},{16,18},{18,16},{1,3},{3,1},{17,19},{19,17},{4,6},{6,4... | collective-permute-start | bytes 1769480 | tf_op jit(solution)/shard_map/ppermute | solution.py:497
  27.2 0.8 %copy-start.1 = (bf16[8,4096]{1,0:T(8,128)(2,1)S(1)}, bf16[8,4096]{1,0:T(8,128)(2,1)}, u32[]{:S(2)}) copy-start(bf16[8,4096]{1,0:T(8,128)(2,1)} %get-tuple-element.18.refs_1_) | copy-start | bytes 196612
  28.1 22.7 %collective-permute-start.3 = (bf16[9,256,128]{2,1,0:T(8,128)(2,1)S(1)}, bf16[9,256,128]{2,1,0:T(8,128)(2,1)S(1)}, u32[]{:S(2)}, u32[]{:S(2)}) collective-permute-start(bf16[9,256,128]{2,1,0:T(8,128)(2,1)S(1)} %shard_map.94.after_ref.rest_2_), channel_id=1, source_target_pairs={{0,2},{2,0},{16,18},{18,16},{1,3},{3,1},{17,19},{19,17},{4,6},{6,4... | collective-permute-start | bytes 1769480 | tf_op jit(solution)/shard_map/ppermute | solution.py:497
  31.5 2.2 %copy-start.4 = (bf16[512,4096]{1,0:T(8,128)(2,1)S(1)}, bf16[512,4096]{1,0:T(8,128)(2,1)}, u32[]{:S(2)}) copy-start(bf16[512,4096]{1,0:T(8,128)(2,1)} %get-tuple-element.17.normed_ref) | copy-start | bytes 12582916
  33.7 2.2 %copy-start.3 = (bf16[512,4096]{1,0:T(8,128)(2,1)S(1)}, bf16[512,4096]{1,0:T(8,128)(2,1)}, u32[]{:S(2)}) copy-start(bf16[512,4096]{1,0:T(8,128)(2,1)} %get-tuple-element.16.normed_ref) | copy-start | bytes 12582916
  35.9 10.0 %copy-start = (bf16[9,256,128]{2,1,0:T(8,128)(2,1)S(1)}, bf16[9,256,128]{2,1,0:T(8,128)(2,1)}, u32[]{:S(2)}) copy-start(bf16[9,256,128]{2,1,0:T(8,128)(2,1)} %shard_map.93.rest_0_) | copy-start | bytes 1769476
  35.9 10.0 %copy-start.2 = (s32[512,1]{0,1:T(1,128)S(1)}, s32[512,1]{0,1:T(1,128)}, u32[]{:S(2)}) copy-start(s32[512,1]{0,1:T(1,128)} %param.11) | copy-start | bytes 6148
  37.8 13.0 %collective-permute-start.6 = (bf16[544,128]{1,0:T(8,128)(2,1)S(1)}, bf16[544,128]{1,0:T(8,128)(2,1)S(1)}, u32[]{:S(2)}, u32[]{:S(2)}) collective-permute-start(bf16[544,128]{1,0:T(8,128)(2,1)S(1)} %get-tuple-element.25.rest_4_), channel_id=1, source_target_pairs={{0,12},{4,8},{8,4},{12,0},{1,13},{5,9},{9,5},{13,1},{2,14},{6,10},... | collective-permute-start | bytes 417800 | tf_op jit(solution)/shard_map/ppermute | solution.py:497
  40.8 10.4 %collective-permute-start.5 = (bf16[544,128]{1,0:T(8,128)(2,1)S(1)}, bf16[544,128]{1,0:T(8,128)(2,1)S(1)}, u32[]{:S(2)}, u32[]{:S(2)}) collective-permute-start(bf16[544,128]{1,0:T(8,128)(2,1)S(1)} %get-tuple-element.25.rest_4_), channel_id=1, source_target_pairs={{0,8},{4,12},{8,0},{12,4},{1,9},{5,13},{9,1},{13,5},{2,10},{6,14},... | collective-permute-start | bytes 417800 | tf_op jit(solution)/shard_map/ppermute | solution.py:497
  40.8 10.4 %collective-permute-start.4 = (bf16[544,128]{1,0:T(8,128)(2,1)S(1)}, bf16[544,128]{1,0:T(8,128)(2,1)S(1)}, u32[]{:S(2)}, u32[]{:S(2)}) collective-permute-start(bf16[544,128]{1,0:T(8,128)(2,1)S(1)} %get-tuple-element.25.rest_4_), channel_id=1, source_target_pairs={{0,4},{4,0},{8,12},{12,8},{1,5},{5,1},{9,13},{13,9},{2,6},{6,2},{1... | collective-permute-start | bytes 417800 | tf_op jit(solution)/shard_map/ppermute | solution.py:497
  42.2 3.7 %collective-permute-start.2 = (f32[16,128]{1,0:T(8,128)S(1)}, f32[16,128]{1,0:T(8,128)S(1)}, u32[]{:S(2)}, u32[]{:S(2)}) collective-permute-start(f32[16,128]{1,0:T(8,128)S(1)} %get-tuple-element.22.own_ref), channel_id=1, source_target_pairs={{0,16},{2,18},{16,0},{18,2},{1,17},{3,19},{17,1},{19,3},{4,20},{6,... | collective-permute-start | bytes 24584 | tf_op jit(solution)/shard_map/ppermute | solution.py:497

commit v21 on v20

--- a/solution.py
+++ b/solution.py
@@ -172,15 +172,15 @@
     *outs, mark_ref, gain, buffers, made, sems, out_sems = refs
     held, block, _ = buffers.shape
     steps = table_hbm.shape[0] // block
-    each = outs[0].shape[0] // block
+    places = [(out, at) for out in outs for at in range(0, out.shape[0], block)]
 
     def copy(step):
         source = table_hbm.at[pl.ds(step * block, block)]
         return pltpu.make_async_copy(source, buffers.at[step % held], sems.at[step % held])
 
     def store(step):
-        target = outs[step // each].at[pl.ds(step % each * block, block)]
-        return pltpu.make_async_copy(made.at[step % held], target, out_sems.at[step % held])
+        out, at = places[step]
+        return pltpu.make_async_copy(made.at[step % held], out.at[pl.ds(at, block)], out_sems.at[step % held])
 
     for step in range(min(held, steps)):
         copy(step).start()
@@ -230,9 +230,10 @@
 
 def project(plan, place, lists, place_ref, w_ref, normed_ref, turn_ref, after_ref, *refs):
     if lists:
-        *refs, list_ref = refs
+        q_ref, vo_ref, tail_ref, list_ref = refs
         read_lists(plan, w_ref, list_ref)
-    q_ref, vo_ref = refs[-2:]
+    else:
+        tail_ref, q_ref, vo_ref = refs[0], *refs[-2:]
     turns = turn_ref[place_ref[LINE]]
     half, k_half = plan.q_rows // 2, plan.k_rows // 2
     cosine, sine = turns[:, 0:1], turns[:, 1:2]
@@ -275,9 +276,12 @@
             for line in range(plan.line):
                 q_ref[line, :, to] = out
         vo_ref[:, to] = total[plan.fold_at : plan.list_at]
-    if plan.direct:
-        first = vo_ref.shape[1] // HD * plan.q_rows + place // block * 2 * plan.mine
-        q_ref[first : first + len(every)] = jnp.concatenate(every, axis=0).astype(BF16)
+    if plan.direct and lists:
+        tail_ref[: len(every)] = jnp.concatenate(every, axis=0)
+    elif plan.direct:
+        before = place // block * 2 * plan.mine
+        last = q_ref.shape[0] - before - len(every)
+        q_ref[last:] = jnp.concatenate([tail_ref[:before], *every], axis=0).astype(BF16)
 
 
 def tied(x, *others):
@@ -327,7 +331,22 @@
     return matmul(block, pick)
 
 
-def prepare(plan, place_ref, board_ref, own_ref, other_ref, *rest):
+def choose(plan, here, list_ref, chosen_ref):
+    boards, moves = chosen_ref.shape[0], chosen_ref.shape[1]
+    move_at = lax.broadcasted_iota(jnp.int32, (moves, plan.slots), 0) + 1
+
+    def step(board, carry):
+        for j in range(plan.pair):
+            place = ((here ^ j) % plan.pair) * boards + board
+            row = list_ref[pl.ds(place, 1), :].astype(jnp.int32)
+            at = slice(j * plan.slots, (j + 1) * plan.slots)
+            chosen_ref[board, :, at] = jnp.where(move_at == row, 1.0, 0.0).astype(BF16)
+        return carry
+
+    lax.fori_loop(0, boards, step, 0)
+
+
+def prepare(plan, place_ref, board_ref, own_ref, *rest):
     *prefix_refs, chosen_ref, fold_ref, slot_ref = rest
     count = board_ref.shape[1]
     board_row = board_ref[...]
@@ -336,15 +355,10 @@
     rank = jnp.sum(jnp.where((board_col == board_row) & ahead, 1.0, 0.0), axis=0, keepdims=True)
     slot_ref[...] = rank.astype(jnp.int32) + place_ref[PEER] * plan.capacity
     here = place_ref[SLAB]
-    boards, moves = chosen_ref.shape[0], chosen_ref.shape[1]
-    move_at = lax.broadcasted_iota(jnp.int32, (moves, plan.slots), 0) + 1
+    boards = fold_ref.shape[1]
+    choose(plan, here, own_ref, chosen_ref)
 
     def step(board, carry):
-        for j in range(plan.slab):
-            place = ((here ^ j) % plan.pair) * boards + board
-            row = (own_ref, other_ref)[j // plan.pair][pl.ds(place, 1), :].astype(jnp.int32)
-            at = slice(j * plan.slots, (j + 1) * plan.slots)
-            chosen_ref[board, :, at] = jnp.where(move_at == row, 1.0, 0.0).astype(BF16)
         for j, prefix_ref in enumerate(prefix_refs):
             fold_ref[j, board] = fold_columns(plan, here, prefix_ref[boards], board, boards, plan.heads)
         return carry
@@ -352,7 +366,11 @@
     lax.fori_loop(0, boards, step, 0)
 
 
-def attend(plan, place_ref, vo_ref, own_ref, other_ref, chosen_ref, fold_ref, *rest):
+def prepare_other(plan, place_ref, other_ref, chosen_ref):
+    choose(plan, place_ref[SLAB], other_ref, chosen_ref)
+
+
+def attend(plan, place_ref, vo_ref, own_ref, other_ref, own_choice, other_choice, fold_ref, *rest):
     prefix_refs, rest = rest[: plan.slab], rest[plan.slab :]
     *q_refs, out_ref, table, extra, scores, taken_even, taken_odd = rest
     here = place_ref[SLAB]
@@ -401,7 +419,7 @@
         return (own_ref, other_ref)[j // plan.pair][pl.ds(place, 1), :].astype(jnp.int32)
 
     def gather(board, taken):
-        taken[...] = matmul(table[...], chosen_ref[board])
+        taken[...] = matmul(table[...], jnp.concatenate([own_choice[board], other_choice[board]], axis=1))
 
     def score_board(board, taken):
         for j in range(plan.slab):
@@ -562,10 +580,11 @@
     across = swap(payload, slab_axes, plan.slab, 2)
 
     block = min(moves, 128)
+    blocks = (moves * 3 // 8, moves * 5 // 8)
     vmem = pl.BlockSpec(memory_space=pltpu.VMEM)
     *normed, mark = pl.pallas_call(
         normalize,
-        out_shape=[*[shape((moves // 2, width), BF16)] * 2, pltpu.HBM((8, width), BF16)],
+        out_shape=[*[shape((size, width), BF16) for size in blocks], pltpu.HBM((8, width), BF16)],
         in_specs=[untouched(), vmem, untouched()],
         out_specs=[untouched()] * 3,
         scratch_shapes=[
@@ -585,22 +604,29 @@
     outs = (shape(sent, BF16), shape((plan.mine, moves), F32))
     across = tied(across, mark)
     diagonal = swap(across, slab_axes, plan.slab, 1)
-    filled, listed = (), None
-    for step, after in enumerate((across, beside)):
-        made = local_call(
-            functools.partial(project, plan, step * moves // 2, step == 0),
-            place,
-            (flat, normed[step], jnp.asarray(turns), after, *filled),
-            [*outs, *([shape((plan.share, plan.slots), F32)] if step == 0 else [])],
-            (),
-            20,
-            (3,),
-            moves * width * 1024,
-            moves * width,
-            {5: 0, 6: 1} if filled else None,
-        )
-        filled, listed = made[:2], made[2] if step == 0 else listed
-    queries, own_values = filled
+    queries, own_values, tails, listed = local_call(
+        functools.partial(project, plan, 0, True),
+        place,
+        (flat, normed[0], jnp.asarray(turns), across),
+        (*outs, shape((-(-blocks[0] // HD * 2 * plan.mine // 8) * 8, HD), F32), shape((plan.share, plan.slots), F32)),
+        (),
+        20,
+        (3,),
+        blocks[0] * width * 2048,
+        blocks[0] * width,
+    )
+    queries, own_values = local_call(
+        functools.partial(project, plan, blocks[0], False),
+        place,
+        (flat, normed[1], jnp.asarray(turns), beside, tails, queries, own_values),
+        outs,
+        (),
+        20,
+        (3,),
+        blocks[1] * width * 2048,
+        blocks[1] * width,
+        {6: 0, 7: 1},
+    )
     other = swap(listed, slab_axes, plan.slab, pair)
     if plan.direct:
         queries = [queries] + [swap(queries, "line", line, step) for step in range(1, line)]
@@ -610,12 +636,13 @@
 
     query_rows = plan.mine * HD
     back = plan.peers * lax.axis_size("tensor")
-    chosen, folds, slot_row = local_call(
+    choice = shape((boards_here, moves, pair * plan.slots), BF16)
+    own_choice, folds, slot_row = local_call(
         functools.partial(prepare, plan),
         place,
-        (board_row, listed, other, payload, beside, across),
+        (board_row, listed, payload, beside, across),
         (
-            shape((boards_here, moves, plan.slab * plan.slots), BF16),
+            choice,
             shape((plan.slab - 1, boards_here, prefix_len, plan.mine * plan.slots), F32),
             shape((1, row_count), jnp.int32),
         ),
@@ -623,10 +650,13 @@
         flops=10**9,
         nbytes=10**6,
     )
+    other_choice = local_call(
+        functools.partial(prepare_other, plan), place, (other,), choice, mib=20, flops=10**9, nbytes=10**6
+    )
     parts = local_call(
         functools.partial(attend, plan),
         place,
-        (own_values, listed, other, chosen, folds, payload, beside, across, diagonal, *queries),
+        (own_values, listed, other, own_choice, other_choice, folds, payload, beside, across, diagonal, *queries),
         shape((groups, back, plan.share, plan.slots), BF16),
         [
             pltpu.VMEM((query_rows + 16, moves), BF16),

time: 72.2 us -> 72.9 us (level)
  Pallas kernels: 30.6 us -> 31.4 us
    pallas_call x5 -> x6, Pallas kernels: 18.4 us -> 19.2 us  [local_call(): pl.pallas_call(kernel, out_shape=outs, in_specs=[pl.BlockSpec(memory_spac...]
  transfers between devices with their start and end apart: 8 -> 8, of which waited for: 4 -> 3; matrix products, arithmetic and copies ran while one was open for 0% -> 0% of each run, Pallas kernels for 28% -> 28%
where the time goes in v21:
time: 72.9 us; the launch traced here: 72.4 us
  Pallas kernels  31.4 us (43%)
  starting transfers between devices  18.6 us (26%)
  blocking collectives  12.4 us (17%)
  waiting for transfers between devices  6.22 us (9%)
  local copies, waits for them, and re-layouts  3.63 us (5%)
    pallas_call x6, Pallas kernels, local_call(): pl.pallas_call(kernel, out_shape=outs, in_specs=[pl.BlockSpec(memory_spac...  19.2 us
    all_to_all x1, blocking collectives, per_device(): lax.all_to_all(parts.reshape(groups * back, plan.share, plan.slots), ('gr...  12.4 us
    ppermute x7, starting transfers between devices, swap(): return lax.ppermute(x, names, [(at, at ^ step) for at in range(size)])  11.3 us
    pallas_call x1, Pallas kernels, per_device(): pl.pallas_call(normalize, out_shape=[*[shape((size, width), BF16) for siz...  8.89 us
    all_to_all x1, starting transfers between devices, per_device(): lax.all_to_all(packed, ('line', 'pair'), split_axis=0, concat_axis=0, til...  7.26 us
    ppermute x7, waiting for transfers between devices, swap(): return lax.ppermute(x, names, [(at, at ^ step) for at in range(size)])  4.43 us
    unnamed x12, local copies, waits for them, and re-layouts  3.63 us
    pallas_call x1, Pallas kernels, per_device(): pl.pallas_call(functools.partial(pack_prefix, plan), out_shape=shape((boa...  2.19 us
  transfers between devices with their start and end apart: 8, of which 3 were waited for; matrix products, arithmetic and copies ran while one was open for 0% of the time, Pallas kernels for 28%

profile of v21, /device:TPU:0, one launch (start us, length us, event | category | flops | bytes accessed | tf_op | source)
XLA Modules:
  0.0 72.4 jit_solution(14225783441873781682)
XLA Ops:
  0.0 2.6 %shard_map.91.after_ref = bf16[8,104,512]{2,1,0:T(8,128)(2,1)} custom-call(s32[1]{0:T(128)} %bitcast.place_ref, bf16[512,1024]{1,0:T(8,128)(2,1)} %wq_hbm.1, bf16[512,256]{1,0:T(8,128)(2,1)} %wkv_hbm.1, bf16[8,128]{1,0:T(8,128)(2,1)} %bitcast.17, s32[1,512]{1,0:T(1,128)} %bitcast.13, s32[1,512]{1,0:T(1,128)} %bitcast.19), custom_call_target="tpu_custom_call" | custom-call | tf_op jit(solution)/shard_map/pallas_call | solution.py:497
  2.6 7.3 %all-to-all-start = ((bf16[8,104,512]{2,1,0:T(8,128)(2,1)}), bf16[8,104,512]{2,1,0:T(8,128)(2,1)S(1)}, u32[]{:S(2)}, u32[]{:S(2)}) async-start(bf16[8,104,512]{2,1,0:T(8,128)(2,1)} %shard_map.91.after_ref), calls=%async_computation | async-start | bytes 1703936 | tf_op jit(solution)/shard_map/all_to_all | solution.py:564
  9.9 2.2 %shard_map.93.rest_0_ = bf16[9,256,128]{2,1,0:T(8,128)(2,1)} custom-call(bf16[8,256,256]{2,1,0:T(8,128)(2,1)} %prefix_hbm.1, bf16[8,128]{1,0:T(8,128)(2,1)} %bitcast.18, bf16[8,104,512]{2,1,0:T(8,128)(2,1)} %shard_map.91.after_ref), custom_call_target="tpu_custom_call" | custom-call | tf_op jit(solution)/shard_map/pallas_call | solution.py:566
  12.1 1.6 %collective-permute-start.1 = (bf16[9,256,128]{2,1,0:T(8,128)(2,1)}, bf16[9,256,128]{2,1,0:T(8,128)(2,1)S(1)}, u32[]{:S(2)}, u32[]{:S(2)}) collective-permute-start(bf16[9,256,128]{2,1,0:T(8,128)(2,1)} %shard_map.93.rest_0_), channel_id=1, source_target_pairs={{0,16},{2,18},{16,0},{18,2},{1,17},{3,19},{17,1},{19,3},{4,20},{6,... | collective-permute-start | bytes 1769480 | tf_op jit(solution)/shard_map/ppermute | solution.py:515
  13.7 2.0 %collective-permute-start = (bf16[9,256,128]{2,1,0:T(8,128)(2,1)}, bf16[9,256,128]{2,1,0:T(8,128)(2,1)S(1)}, u32[]{:S(2)}, u32[]{:S(2)}) collective-permute-start(bf16[9,256,128]{2,1,0:T(8,128)(2,1)} %shard_map.93.rest_0_), channel_id=1, source_target_pairs={{0,2},{2,0},{16,18},{18,16},{1,3},{3,1},{17,19},{19,17},{4,6},{6,4... | collective-permute-start | bytes 1769480 | tf_op jit(solution)/shard_map/ppermute | solution.py:515
  15.7 8.9 %shard_map.92 = (bf16[384,4096]{1,0:T(8,128)(2,1)}, bf16[640,4096]{1,0:T(8,128)(2,1)}, bf16[8,4096]{1,0:T(8,128)(2,1)}) custom-call(bf16[1024,4096]{1,0:T(8,128)(2,1)} %table_hbm.1, bf16[32,128]{1,0:T(8,128)(2,1)} %bitcast.16, bf16[8,104,512]{2,1,0:T(8,128)(2,1)} %shard_map.91.after_ref), custom_call_target="tpu_custom_call" | custom-call | flops 4194304 | bytes 1048576 | tf_op jit(solution)/shard_map/pallas_call | solution.py:585
  24.6 0.1 pad_add_fusion.place_ref
  24.7 2.5 %collective-permute-done.1.refs_0_ = bf16[9,256,128]{2,1,0:T(8,128)(2,1)S(1)} collective-permute-done((bf16[9,256,128]{2,1,0:T(8,128)(2,1)}, bf16[9,256,128]{2,1,0:T(8,128)(2,1)S(1)}, u32[]{:S(2)}, u32[]{:S(2)}) %collective-permute-start.1) | collective-permute-done | bytes 589856 | tf_op jit(solution)/shard_map/ppermute | solution.py:515
  27.2 0.8 %copy-done.1 = bf16[8,4096]{1,0:T(8,128)(2,1)S(1)} copy-done((bf16[8,4096]{1,0:T(8,128)(2,1)S(1)}, bf16[8,4096]{1,0:T(8,128)(2,1)}, u32[]{:S(2)}) %copy-start.1) | copy-done | bytes 65560
  28.0 1.7 %collective-permute-start.3 = (bf16[9,256,128]{2,1,0:T(8,128)(2,1)S(1)}, bf16[9,256,128]{2,1,0:T(8,128)(2,1)S(1)}, u32[]{:S(2)}, u32[]{:S(2)}) collective-permute-start(bf16[9,256,128]{2,1,0:T(8,128)(2,1)S(1)} %shard_map.94.after_ref.rest_2_), channel_id=1, source_target_pairs={{0,2},{2,0},{16,18},{18,16},{1,3},{3,1},{17,19},{19,17},{4,6},{6,4... | collective-permute-start | bytes 1769480 | tf_op jit(solution)/shard_map/ppermute | solution.py:515
  29.8 1.8 %all-to-all-done.w_ref = bf16[8,104,512]{2,1,0:T(8,128)(2,1)S(1)} async-done(((bf16[8,104,512]{2,1,0:T(8,128)(2,1)}), bf16[8,104,512]{2,1,0:T(8,128)(2,1)S(1)}, u32[]{:S(2)}, u32[]{:S(2)}) %all-to-all-start) | async-done | bytes 852000 | tf_op jit(solution)/shard_map/all_to_all | solution.py:564
  31.5 1.9 %copy-done.4 = bf16[384,4096]{1,0:T(8,128)(2,1)S(1)} copy-done((bf16[384,4096]{1,0:T(8,128)(2,1)S(1)}, bf16[384,4096]{1,0:T(8,128)(2,1)}, u32[]{:S(2)}) %copy-start.4) | copy-done | bytes 3145752
  33.4 1.6 %shard_map.95 = (bf16[544,128]{1,0:T(8,128)(2,1)S(1)}, f32[2,1024]{1,0:T(2,128)S(1)}, f32[16,128]{1,0:T(8,128)S(1)}, f32[16,128]{1,0:T(8,128)S(1)}) custom-call(s32[4]{0:T(128)S(1)} %pad_add_fusion.place_ref, bf16[8,104,512]{2,1,0:T(8,128)(2,1)S(1)} %all-to-all-done.w_ref, bf16[384,4096]{1,0:T(8,128)(2,1)S(1)} %copy-done.4, f32[4,32,2]{2,1,0:T(8,128)S(1)} %copy-done.5, ...), custom_call_target="tpu_custom_call" | custom-call | flops 3221225472 | bytes 1572864 | tf_op jit(solution)/shard_map/pallas_call | solution.py:497
  35.0 0.9 %copy-done.3 = bf16[640,4096]{1,0:T(8,128)(2,1)S(1)} copy-done((bf16[640,4096]{1,0:T(8,128)(2,1)S(1)}, bf16[640,4096]{1,0:T(8,128)(2,1)}, u32[]{:S(2)}) %copy-start.3) | copy-done | bytes 5242904
  35.9 2.1 %shard_map.96 = (bf16[544,128]{1,0:T(8,128)(2,1)S(1)}, f32[2,1024]{1,0:T(2,128)S(1)}) custom-call(s32[4]{0:T(128)S(1)} %pad_add_fusion.place_ref, bf16[8,104,512]{2,1,0:T(8,128)(2,1)S(1)} %all-to-all-done.w_ref, bf16[640,4096]{1,0:T(8,128)(2,1)S(1)} %copy-done.3, f32[4,32,2]{2,1,0:T(8,128)S(1)} %copy-done.5, ...), custom_call_target="tpu_custom_call", output_to_operand_aliasing={{0}: (6, {}), {1}: (7, {})} | custom-call | flops 5368709120 | bytes 2621440 | tf_op jit(solution)/shard_map/pallas_call | solution.py:497
  38.1 3.0 %collective-permute-start.6 = (bf16[544,128]{1,0:T(8,128)(2,1)S(1)}, bf16[544,128]{1,0:T(8,128)(2,1)S(1)}, u32[]{:S(2)}, u32[]{:S(2)}) collective-permute-start(bf16[544,128]{1,0:T(8,128)(2,1)S(1)} %get-tuple-element.27.rest_4_), channel_id=1, source_target_pairs={{0,12},{4,8},{8,4},{12,0},{1,13},{5,9},{9,5},{13,1},{2,14},{6,10},... | collective-permute-start | bytes 417800 | tf_op jit(solution)/shard_map/ppermute | solution.py:515
  41.0 1.5 %collective-permute-start.4 = (bf16[544,128]{1,0:T(8,128)(2,1)S(1)}, bf16[544,128]{1,0:T(8,128)(2,1)S(1)}, u32[]{:S(2)}, u32[]{:S(2)}) collective-permute-start(bf16[544,128]{1,0:T(8,128)(2,1)S(1)} %get-tuple-element.27.rest_4_), channel_id=1, source_target_pairs={{0,4},{4,0},{8,12},{12,8},{1,5},{5,1},{9,13},{13,9},{2,6},{6,2},{1... | collective-permute-start | bytes 417800 | tf_op jit(solution)/shard_map/ppermute | solution.py:515
  42.5 1.5 %collective-permute-start.2 = (f32[16,128]{1,0:T(8,128)S(1)}, f32[16,128]{1,0:T(8,128)S(1)}, u32[]{:S(2)}, u32[]{:S(2)}) collective-permute-start(f32[16,128]{1,0:T(8,128)S(1)} %get-tuple-element.24.own_ref), channel_id=1, source_target_pairs={{0,16},{2,18},{16,0},{18,2},{1,17},{3,19},{17,1},{19,3},{4,20},{6,... | collective-permute-start | bytes 24584 | tf_op jit(solution)/shard_map/ppermute | solution.py:515
  44.0 3.9 %shard_map.97 = (bf16[8,1024,256]{2,1,0:T(8,128)(2,1)S(1)}, f32[3,8,256,256]{3,2,1,0:T(8,128)S(1)}, s32[1,512]{1,0:T(1,128)S(1)}) custom-call(s32[4]{0:T(128)S(1)} %pad_add_fusion.place_ref, s32[1,512]{1,0:T(1,128)S(1)} %bitcast.14, f32[16,128]{1,0:T(8,128)S(1)} %get-tuple-element.24.own_ref, bf16[9,256,128]{2,1,0:T(8,128)(2,1)S(1)} %copy-done, ...), custom_call_target="tpu_custom_call" | custom-call | flops 1000000000 | bytes 1000000 | tf_op jit(solution)/shard_map/pallas_call | solution.py:497
  47.9 1.5 %shard_map.98.other_choice = bf16[8,1024,256]{2,1,0:T(8,128)(2,1)S(1)} custom-call(s32[4]{0:T(128)S(1)} %pad_add_fusion.place_ref, f32[16,128]{1,0:T(8,128)S(1)} %collective-permute-done.2.other_ref), custom_call_target="tpu_custom_call" | custom-call | flops 1000000000 | bytes 1000000 | tf_op jit(solution)/shard_map/pallas_call | solution.py:497
  49.5 1.9 %collective-permute-done.5.rest_6_ = bf16[544,128]{1,0:T(8,128)(2,1)S(1)} collective-permute-done((bf16[544,128]{1,0:T(8,128)(2,1)S(1)}, bf16[544,128]{1,0:T(8,128)(2,1)S(1)}, u32[]{:S(2)}, u32[]{:S(2)}) %collective-permute-start.5) | collective-permute-done | bytes 139296 | tf_op jit(solution)/shard_map/ppermute | solution.py:515
  51.4 7.5 %shard_map.99 = bf16[2,16,16,128]{3,2,1,0:T(8,128)(2,1)S(1)} custom-call(s32[4]{0:T(128)S(1)} %pad_add_fusion.place_ref, f32[2,1024]{1,0:T(2,128)S(1)} %get-tuple-element.23.vo_ref, f32[16,128]{1,0:T(8,128)S(1)} %get-tuple-element.24.own_ref, f32[16,128]{1,0:T(8,128)S(1)} %collective-permute-done.2.other_ref, ...), custom_call_target="tpu_custom_call" | custom-call | tf_op jit(solution)/shard_map/pallas_call | solution.py:497
  58.9 12.4 %all_to_all.10 = bf16[32,16,128]{2,1,0:T(8,128)(2,1)S(1)} all-to-all(bf16[32,16,128]{2,1,0:T(8,128)(2,1)S(1)} %bitcast.11), channel_id=1, replica_groups=mesh['groups'=2,'line'=4,'pair'=2,'tensor'=2] {'groups','line','pair','t..., dimensions={0} | all-to-all | bytes 262144 | tf_op jit(solution)/shard_map/all_to_all | solution.py:670
  71.4 1.1 %shard_map.100 = f32[1,512]{1,0:T(1,128)} custom-call(bf16[2,4,4,16,128]{4,3,2,1,0:T(8,128)(2,1)S(1)} %bitcast.12, s32[1,512]{1,0:T(1,128)S(1)} %bitcast.15, s32[1,512]{1,0:T(1,128)S(1)} %get-tuple-element.28.slot_ref), custom_call_target="tpu_custom_call" | custom-call | tf_op jit(solution)/shard_map/pallas_call | solution.py:678
  (16 shorter events, 0.0 us)
Async XLA Ops:
  2.6 28.9 %all-to-all-start = ((bf16[8,104,512]{2,1,0:T(8,128)(2,1)}), bf16[8,104,512]{2,1,0:T(8,128)(2,1)S(1)}, u32[]{:S(2)}, u32[]{:S(2)}) async-start(bf16[8,104,512]{2,1,0:T(8,128)(2,1)} %shard_map.91.after_ref), calls=%async_computation | async-start | bytes 1703936 | tf_op jit(solution)/shard_map/all_to_all | solution.py:564
  12.1 15.1 %collective-permute-start.1 = (bf16[9,256,128]{2,1,0:T(8,128)(2,1)}, bf16[9,256,128]{2,1,0:T(8,128)(2,1)S(1)}, u32[]{:S(2)}, u32[]{:S(2)}) collective-permute-start(bf16[9,256,128]{2,1,0:T(8,128)(2,1)} %shard_map.93.rest_0_), channel_id=1, source_target_pairs={{0,16},{2,18},{16,0},{18,2},{1,17},{3,19},{17,1},{19,3},{4,20},{6,... | collective-permute-start | bytes 1769480 | tf_op jit(solution)/shard_map/ppermute | solution.py:515
  13.7 21.3 %collective-permute-start = (bf16[9,256,128]{2,1,0:T(8,128)(2,1)}, bf16[9,256,128]{2,1,0:T(8,128)(2,1)S(1)}, u32[]{:S(2)}, u32[]{:S(2)}) collective-permute-start(bf16[9,256,128]{2,1,0:T(8,128)(2,1)} %shard_map.93.rest_0_), channel_id=1, source_target_pairs={{0,2},{2,0},{16,18},{18,16},{1,3},{3,1},{17,19},{19,17},{4,6},{6,4... | collective-permute-start | bytes 1769480 | tf_op jit(solution)/shard_map/ppermute | solution.py:515
  15.7 15.8 %copy-start.5 = (f32[4,32,2]{2,1,0:T(8,128)S(1)}, f32[4,32,2]{2,1,0:T(8,128)}, u32[]{:S(2)}) copy-start(f32[4,32,2]{2,1,0:T(8,128)} %constant.17.clone.turn_ref) | copy-start | bytes 3076
  27.2 0.8 %copy-start.1 = (bf16[8,4096]{1,0:T(8,128)(2,1)S(1)}, bf16[8,4096]{1,0:T(8,128)(2,1)}, u32[]{:S(2)}) copy-start(bf16[8,4096]{1,0:T(8,128)(2,1)} %get-tuple-element.19.refs_1_) | copy-start | bytes 196612
  28.0 21.5 %collective-permute-start.3 = (bf16[9,256,128]{2,1,0:T(8,128)(2,1)S(1)}, bf16[9,256,128]{2,1,0:T(8,128)(2,1)S(1)}, u32[]{:S(2)}, u32[]{:S(2)}) collective-permute-start(bf16[9,256,128]{2,1,0:T(8,128)(2,1)S(1)} %shard_map.94.after_ref.rest_2_), channel_id=1, source_target_pairs={{0,2},{2,0},{16,18},{18,16},{1,3},{3,1},{17,19},{19,17},{4,6},{6,4... | collective-permute-start | bytes 1769480 | tf_op jit(solution)/shard_map/ppermute | solution.py:515
  31.5 1.9 %copy-start.4 = (bf16[384,4096]{1,0:T(8,128)(2,1)S(1)}, bf16[384,4096]{1,0:T(8,128)(2,1)}, u32[]{:S(2)}) copy-start(bf16[384,4096]{1,0:T(8,128)(2,1)} %get-tuple-element.18.normed_ref) | copy-start | bytes 9437188
  33.4 2.5 %copy-start.3 = (bf16[640,4096]{1,0:T(8,128)(2,1)S(1)}, bf16[640,4096]{1,0:T(8,128)(2,1)}, u32[]{:S(2)}) copy-start(bf16[640,4096]{1,0:T(8,128)(2,1)} %get-tuple-element.17.normed_ref) | copy-start | bytes 15728644
  35.9 8.1 %copy-start = (bf16[9,256,128]{2,1,0:T(8,128)(2,1)S(1)}, bf16[9,256,128]{2,1,0:T(8,128)(2,1)}, u32[]{:S(2)}) copy-start(bf16[9,256,128]{2,1,0:T(8,128)(2,1)} %shard_map.93.rest_0_) | copy-start | bytes 1769476
  35.9 8.1 %copy-start.2 = (s32[512,1]{0,1:T(1,128)S(1)}, s32[512,1]{0,1:T(1,128)}, u32[]{:S(2)}) copy-start(s32[512,1]{0,1:T(1,128)} %param.11) | copy-start | bytes 6148
  38.1 11.4 %collective-permute-start.6 = (bf16[544,128]{1,0:T(8,128)(2,1)S(1)}, bf16[544,128]{1,0:T(8,128)(2,1)S(1)}, u32[]{:S(2)}, u32[]{:S(2)}) collective-permute-start(bf16[544,128]{1,0:T(8,128)(2,1)S(1)} %get-tuple-element.27.rest_4_), channel_id=1, source_target_pairs={{0,12},{4,8},{8,4},{12,0},{1,13},{5,9},{9,5},{13,1},{2,14},{6,10},... | collective-permute-start | bytes 417800 | tf_op jit(solution)/shard_map/ppermute | solution.py:515
  41.0 10.4 %collective-permute-start.5 = (bf16[544,128]{1,0:T(8,128)(2,1)S(1)}, bf16[544,128]{1,0:T(8,128)(2,1)S(1)}, u32[]{:S(2)}, u32[]{:S(2)}) collective-permute-start(bf16[544,128]{1,0:T(8,128)(2,1)S(1)} %get-tuple-element.27.rest_4_), channel_id=1, source_target_pairs={{0,8},{4,12},{8,0},{12,4},{1,9},{5,13},{9,1},{13,5},{2,10},{6,14},... | collective-permute-start | bytes 417800 | tf_op jit(solution)/shard_map/ppermute | solution.py:515
  41.0 10.4 %collective-permute-start.4 = (bf16[544,128]{1,0:T(8,128)(2,1)S(1)}, bf16[544,128]{1,0:T(8,128)(2,1)S(1)}, u32[]{:S(2)}, u32[]{:S(2)}) collective-permute-start(bf16[544,128]{1,0:T(8,128)(2,1)S(1)} %get-tuple-element.27.rest_4_), channel_id=1, source_target_pairs={{0,4},{4,0},{8,12},{12,8},{1,5},{5,1},{9,13},{13,9},{2,6},{6,2},{1... | collective-permute-start | bytes 417800 | tf_op jit(solution)/shard_map/ppermute | solution.py:515
  42.5 5.4 %collective-permute-start.2 = (f32[16,128]{1,0:T(8,128)S(1)}, f32[16,128]{1,0:T(8,128)S(1)}, u32[]{:S(2)}, u32[]{:S(2)}) collective-permute-start(f32[16,128]{1,0:T(8,128)S(1)} %get-tuple-element.24.own_ref), channel_id=1, source_target_pairs={{0,16},{2,18},{16,0},{18,2},{1,17},{3,19},{17,1},{19,3},{4,20},{6,... | collective-permute-start | bytes 24584 | tf_op jit(solution)/shard_map/ppermute | solution.py:515

commit v22 on v20

--- a/solution.py
+++ b/solution.py
@@ -35,7 +35,7 @@
 
 
 class Plan:
-    def __init__(self, groups, line, pair, heads, capacity, share):
+    def __init__(self, groups, line, pair, heads, capacity, share, depth):
         self.groups, self.line, self.pair = groups, line, pair
         self.peers = line * pair
         self.slab = groups * pair
@@ -52,6 +52,10 @@
         self.share = share
         self.slots = self.peers * capacity
         self.direct = line <= 4
+        self.tight = self.pairs % 16 == 0 and depth % HD == 0
+        self.chunks = depth // HD
+        last = -(-(self.mine + 1) * self.chunks // 16) * 16
+        self.sent = (self.fold_at * self.chunks + last, HD) if self.tight else (self.rows, depth)
 
 
 def pack_weights(plan, place_ref, wq_hbm, wkv_hbm, ws_hbm, board_hbm, ids_hbm, *rest):
@@ -94,7 +98,7 @@
         both = found[at : at + plan.share] + found[boards + at : boards + at + plan.share]
         lists.append(jnp.sum(both, axis=0, keepdims=True))
 
-    if plan.pairs % 16 == 0:
+    if plan.tight:
         turn_weights(plan, group, lists, copies[3:], wq, wkv, ws_ref, out_ref)
     else:
         pick_weights(plan, group, lists, copies[3:], wq, wkv, ws_ref, out_ref, pick)
@@ -108,22 +112,25 @@
     folds = matmul(ws_ref[...], wkv[:, HD:], NT)
     row = lax.broadcasted_iota(jnp.int32, folds.shape, 0)
     pairs = plan.pairs
-    zeros = jnp.zeros((plan.rows - plan.list_at - 1, folds.shape[1]), F32)
+    lanes = [slice(c * HD, (c + 1) * HD) for c in range(plan.chunks)]
+    first_last = plan.fold_at * plan.chunks
+    zeros = jnp.zeros((plan.sent[0] - first_last - (plan.mine + 1) * plan.chunks, HD), F32)
     for pair in range(plan.pair):
         first = (group * plan.pair + pair) * plan.mine
         mine = [jnp.sum(jnp.where(row == first + h, folds, 0.0), axis=0, keepdims=True) for h in range(plan.mine)]
         for line in range(plan.line):
             peer = line * plan.pair + pair
-            for part in range(2):
-                entry = part * HALF + line * pairs
-                for h in range(plan.mine):
-                    at = (part * plan.mine + h) * pairs
-                    source = (pair * plan.mine + h) * HD + entry
-                    out_ref[peer, at : at + pairs] = q[source : source + pairs]
-                at = plan.q_rows + part * pairs
-                out_ref[peer, at : at + pairs] = k[entry : entry + pairs]
-            last = jnp.concatenate([*mine, lists[line], zeros], axis=0)
-            out_ref[peer, plan.fold_at :] = last.astype(BF16)
+            for c, lane in enumerate(lanes):
+                for part in range(2):
+                    entry = part * HALF + line * pairs
+                    for h in range(plan.mine):
+                        at = c * plan.fold_at + (part * plan.mine + h) * pairs
+                        source = (pair * plan.mine + h) * HD + entry
+                        out_ref[peer, at : at + pairs] = q[source : source + pairs, lane]
+                    at = c * plan.fold_at + plan.q_rows + part * pairs
+                    out_ref[peer, at : at + pairs] = k[entry : entry + pairs, lane]
+            last = [values[:, lane] for values in (*mine, lists[line]) for lane in lanes]
+            out_ref[peer, first_last:] = jnp.concatenate([*last, zeros], axis=0).astype(BF16)
 
 
 def pick_weights(plan, group, lists, copies, wq, wkv, ws_ref, out_ref, pick):
@@ -203,15 +210,36 @@
     mark.wait()
 
 
-def read_lists(plan, w_ref, out_ref):
+def spread_weights(plan, w_ref, full_ref):
+    lists = []
+    for s in range(plan.peers):
+        for c in range(plan.chunks):
+            rows = w_ref[s, c * plan.fold_at : (c + 1) * plan.fold_at]
+            full_ref[s, : plan.fold_at, c * HD : (c + 1) * HD] = rows
+        last = w_ref[s, plan.fold_at * plan.chunks :].astype(F32)
+        last = [
+            jnp.concatenate([last[i * plan.chunks + c : i * plan.chunks + c + 1] for c in range(plan.chunks)], axis=1)
+            for i in range(plan.mine + 1)
+        ]
+        zeros = jnp.zeros((plan.rows - plan.list_at, last[0].shape[1]), F32)
+        full_ref[s, plan.fold_at :] = jnp.concatenate([*last[: plan.mine], zeros], axis=0).astype(BF16)
+        lists.append(last[plan.mine])
+    return jnp.concatenate(lists, axis=0)
+
+
+def list_rows(plan, w_ref):
+    if len(w_ref.shape) == 3:
+        rows = [w_ref[s].astype(F32)[plan.list_at : plan.list_at + 1] for s in range(plan.peers)]
+    else:
+        row = w_ref[...].astype(F32)[plan.list_at : plan.list_at + 1]
+        span = plan.share * plan.capacity
+        rows = [row[:, s * 2 * span : (s + 1) * 2 * span] for s in range(plan.peers)]
+    return jnp.concatenate(rows, axis=0)
+
+
+def read_lists(plan, rows, out_ref):
     share, capacity, peers = plan.share, plan.capacity, plan.peers
     span = share * capacity
-    if len(w_ref.shape) == 3:
-        rows = [w_ref[s].astype(F32)[plan.list_at : plan.list_at + 1] for s in range(peers)]
-    else:
-        row = w_ref[...].astype(F32)[plan.list_at : plan.list_at + 1]
-        rows = [row[:, s * 2 * span : (s + 1) * 2 * span] for s in range(peers)]
-    rows = jnp.concatenate(rows, axis=0)
     lane = lax.broadcasted_iota(jnp.int32, (share * peers, 2 * span), 1)
     row = lax.broadcasted_iota(jnp.int32, (share * peers, 2 * span), 0)
     lane = jnp.where(lane < span, lane, lane - span)
@@ -230,8 +258,14 @@
 
 def project(plan, place, lists, place_ref, w_ref, normed_ref, turn_ref, after_ref, *refs):
     if lists:
-        *refs, list_ref = refs
-        read_lists(plan, w_ref, list_ref)
+        *refs, list_ref, full_ref = refs
+        if plan.tight:
+            rows = spread_weights(plan, w_ref, full_ref)
+            w_ref = full_ref
+        else:
+            rows = list_rows(plan, w_ref)
+            full_ref[...] = w_ref[...]
+        read_lists(plan, rows, list_ref)
     q_ref, vo_ref = refs[-2:]
     turns = turn_ref[place_ref[LINE]]
     half, k_half = plan.q_rows // 2, plan.k_rows // 2
@@ -515,8 +549,8 @@
     board_total = boards_here * line * pair
     capacity = max(2, (2 * row_count + board_total - 1) // board_total)
     heads = w_query.shape[1] // HD
-    plan = Plan(groups, line, pair, heads, capacity, pair * boards_here)
     depth = w_query.shape[0]
+    plan = Plan(groups, line, pair, heads, capacity, pair * boards_here, depth)
     group_at = lax.axis_index("groups").astype(jnp.int32)
     line_at = lax.axis_index("line").astype(jnp.int32)
     pair_at = lax.axis_index("pair").astype(jnp.int32)
@@ -530,7 +564,7 @@
         functools.partial(pack_weights, plan),
         group_at.reshape(1),
         (w_query, w_keyval, ws, board_row, move_ids.reshape(1, row_count)),
-        shape((plan.peers, plan.rows, depth), BF16),
+        shape((plan.peers, *plan.sent), BF16),
         [
             pltpu.VMEM((depth, half_cols), BF16),
             pltpu.VMEM((depth, 2 * HD), BF16),
@@ -585,13 +619,14 @@
     outs = (shape(sent, BF16), shape((plan.mine, moves), F32))
     across = tied(across, mark)
     diagonal = swap(across, slab_axes, plan.slab, 1)
+    full = shape((plan.peers, plan.rows, depth), BF16) if plan.tight else shape(flat.shape, BF16)
     filled, listed = (), None
     for step, after in enumerate((across, beside)):
         made = local_call(
             functools.partial(project, plan, step * moves // 2, step == 0),
             place,
             (flat, normed[step], jnp.asarray(turns), after, *filled),
-            [*outs, *([shape((plan.share, plan.slots), F32)] if step == 0 else [])],
+            [*outs, *([shape((plan.share, plan.slots), F32), full] if step == 0 else [])],
             (),
             20,
             (3,),
@@ -599,7 +634,9 @@
             moves * width,
             {5: 0, 6: 1} if filled else None,
         )
-        filled, listed = made[:2], made[2] if step == 0 else listed
+        filled = made[:2]
+        if step == 0:
+            listed, flat = made[2:]
     queries, own_values = filled
     other = swap(listed, slab_axes, plan.slab, pair)
     if plan.direct:

time: 72.2 us -> 71.9 us (level)
  no operation moved by 1% of the time
where the time goes in v22:
time: 71.9 us; the launch traced here: 71.5 us
  Pallas kernels  30.6 us (43%)
  starting transfers between devices  18.6 us (26%)
  blocking collectives  12.8 us (18%)
  waiting for transfers between devices  5.99 us (8%)
  local copies, waits for them, and re-layouts  3.3 us (5%)
    pallas_call x5, Pallas kernels, local_call(): pl.pallas_call(kernel, out_shape=outs, in_specs=[pl.BlockSpec(memory_spac...  18.4 us
    all_to_all x1, blocking collectives, per_device(): lax.all_to_all(parts.reshape(groups * back, plan.share, plan.slots), ('gr...  12.8 us
    ppermute x7, starting transfers between devices, swap(): return lax.ppermute(x, names, [(at, at ^ step) for at in range(size)])  11.3 us
    pallas_call x1, Pallas kernels, per_device(): pl.pallas_call(normalize, out_shape=[*[shape((moves // 2, width), BF16)]...  8.92 us
    all_to_all x1, starting transfers between devices, per_device(): lax.all_to_all(packed, ('line', 'pair'), split_axis=0, concat_axis=0, til...  7.26 us
    ppermute x7, waiting for transfers between devices, swap(): return lax.ppermute(x, names, [(at, at ^ step) for at in range(size)])  4.95 us
    unnamed x12, local copies, waits for them, and re-layouts  3.3 us
    pallas_call x1, Pallas kernels, per_device(): pl.pallas_call(functools.partial(pack_prefix, plan), out_shape=shape((boa...  2.22 us
  transfers between devices with their start and end apart: 8, of which 4 were waited for; matrix products, arithmetic and copies ran while one was open for 0% of the time, Pallas kernels for 28%

profile of v22, /device:TPU:0, one launch (start us, length us, event | category | flops | bytes accessed | tf_op | source)
XLA Modules:
  0.0 71.5 jit_solution(1566723811927277844)
XLA Ops:
  0.0 2.6 %shard_map.91.after_ref = bf16[8,400,128]{2,1,0:T(8,128)(2,1)} custom-call(s32[1]{0:T(128)} %bitcast.place_ref, bf16[512,1024]{1,0:T(8,128)(2,1)} %wq_hbm.1, bf16[512,256]{1,0:T(8,128)(2,1)} %wkv_hbm.1, bf16[8,128]{1,0:T(8,128)(2,1)} %bitcast.17, s32[1,512]{1,0:T(1,128)} %bitcast.13, s32[1,512]{1,0:T(1,128)} %bitcast.19), custom_call_target="tpu_custom_call" | custom-call | tf_op jit(solution)/shard_map/pallas_call | solution.py:513
  2.6 7.3 %all-to-all-start = ((bf16[8,400,128]{2,1,0:T(8,128)(2,1)}), bf16[8,400,128]{2,1,0:T(8,128)(2,1)S(1)}, u32[]{:S(2)}, u32[]{:S(2)}) async-start(bf16[8,400,128]{2,1,0:T(8,128)(2,1)} %shard_map.91.after_ref), calls=%async_computation | async-start | bytes 1638400 | tf_op jit(solution)/shard_map/all_to_all | solution.py:580
  9.9 2.2 %shard_map.93.rest_0_ = bf16[9,256,128]{2,1,0:T(8,128)(2,1)} custom-call(bf16[8,256,256]{2,1,0:T(8,128)(2,1)} %prefix_hbm.1, bf16[8,128]{1,0:T(8,128)(2,1)} %bitcast.18, bf16[8,400,128]{2,1,0:T(8,128)(2,1)} %shard_map.91.after_ref), custom_call_target="tpu_custom_call" | custom-call | tf_op jit(solution)/shard_map/pallas_call | solution.py:582
  12.1 1.6 %collective-permute-start = (bf16[9,256,128]{2,1,0:T(8,128)(2,1)}, bf16[9,256,128]{2,1,0:T(8,128)(2,1)S(1)}, u32[]{:S(2)}, u32[]{:S(2)}) collective-permute-start(bf16[9,256,128]{2,1,0:T(8,128)(2,1)} %shard_map.93.rest_0_), channel_id=1, source_target_pairs={{0,16},{2,18},{16,0},{18,2},{1,17},{3,19},{17,1},{19,3},{4,20},{6,... | collective-permute-start | bytes 1769480 | tf_op jit(solution)/shard_map/ppermute | solution.py:531
  13.7 2.0 %collective-permute-start.1 = (bf16[9,256,128]{2,1,0:T(8,128)(2,1)}, bf16[9,256,128]{2,1,0:T(8,128)(2,1)S(1)}, u32[]{:S(2)}, u32[]{:S(2)}) collective-permute-start(bf16[9,256,128]{2,1,0:T(8,128)(2,1)} %shard_map.93.rest_0_), channel_id=1, source_target_pairs={{0,2},{2,0},{16,18},{18,16},{1,3},{3,1},{17,19},{19,17},{4,6},{6,4... | collective-permute-start | bytes 1769480 | tf_op jit(solution)/shard_map/ppermute | solution.py:531
  15.7 8.9 %shard_map.92 = (bf16[512,4096]{1,0:T(8,128)(2,1)}, bf16[512,4096]{1,0:T(8,128)(2,1)}, bf16[8,4096]{1,0:T(8,128)(2,1)}) custom-call(bf16[1024,4096]{1,0:T(8,128)(2,1)} %table_hbm.1, bf16[32,128]{1,0:T(8,128)(2,1)} %bitcast.16, bf16[8,400,128]{2,1,0:T(8,128)(2,1)} %shard_map.91.after_ref), custom_call_target="tpu_custom_call" | custom-call | flops 4194304 | bytes 1048576 | tf_op jit(solution)/shard_map/pallas_call | solution.py:600
  24.6 0.1 pad_add_fusion.place_ref
  24.7 2.5 %collective-permute-done.refs_0_ = bf16[9,256,128]{2,1,0:T(8,128)(2,1)S(1)} collective-permute-done((bf16[9,256,128]{2,1,0:T(8,128)(2,1)}, bf16[9,256,128]{2,1,0:T(8,128)(2,1)S(1)}, u32[]{:S(2)}, u32[]{:S(2)}) %collective-permute-start) | collective-permute-done | bytes 589856 | tf_op jit(solution)/shard_map/ppermute | solution.py:531
  27.2 0.8 %copy-done.1 = bf16[8,4096]{1,0:T(8,128)(2,1)S(1)} copy-done((bf16[8,4096]{1,0:T(8,128)(2,1)S(1)}, bf16[8,4096]{1,0:T(8,128)(2,1)}, u32[]{:S(2)}) %copy-start.1) | copy-done | bytes 65560
  28.0 1.7 %collective-permute-start.3 = (bf16[9,256,128]{2,1,0:T(8,128)(2,1)S(1)}, bf16[9,256,128]{2,1,0:T(8,128)(2,1)S(1)}, u32[]{:S(2)}, u32[]{:S(2)}) collective-permute-start(bf16[9,256,128]{2,1,0:T(8,128)(2,1)S(1)} %shard_map.94.after_ref.rest_2_), channel_id=1, source_target_pairs={{0,2},{2,0},{16,18},{18,16},{1,3},{3,1},{17,19},{19,17},{4,6},{6,4... | collective-permute-start | bytes 1769480 | tf_op jit(solution)/shard_map/ppermute | solution.py:531
  29.8 1.0 %all-to-all-done.w_ref = bf16[8,400,128]{2,1,0:T(8,128)(2,1)S(1)} async-done(((bf16[8,400,128]{2,1,0:T(8,128)(2,1)}), bf16[8,400,128]{2,1,0:T(8,128)(2,1)S(1)}, u32[]{:S(2)}, u32[]{:S(2)}) %all-to-all-start) | async-done | bytes 819232 | tf_op jit(solution)/shard_map/all_to_all | solution.py:580
  30.8 2.2 %copy-done.4 = bf16[512,4096]{1,0:T(8,128)(2,1)S(1)} copy-done((bf16[512,4096]{1,0:T(8,128)(2,1)S(1)}, bf16[512,4096]{1,0:T(8,128)(2,1)}, u32[]{:S(2)}) %copy-start.4) | copy-done | bytes 4194328
  33.0 1.9 %shard_map.95 = (bf16[544,128]{1,0:T(8,128)(2,1)S(1)}, f32[2,1024]{1,0:T(2,128)S(1)}, f32[16,128]{1,0:T(8,128)S(1)}, bf16[8,104,512]{2,1,0:T(8,128)(2,1)S(1)}) custom-call(s32[4]{0:T(128)S(1)} %pad_add_fusion.place_ref, bf16[8,400,128]{2,1,0:T(8,128)(2,1)S(1)} %all-to-all-done.w_ref, bf16[512,4096]{1,0:T(8,128)(2,1)S(1)} %copy-done.4, ...), custom_call_target="tpu_custom_call" | custom-call | flops 4294967296 | bytes 4194304 | tf_op jit(solution)/shard_map/pallas_call | solution.py:513
  34.9 0.3 copy-done.3
  35.2 1.8 %shard_map.96 = (bf16[544,128]{1,0:T(8,128)(2,1)S(1)}, f32[2,1024]{1,0:T(2,128)S(1)}) custom-call(s32[4]{0:T(128)S(1)} %pad_add_fusion.place_ref, bf16[8,104,512]{2,1,0:T(8,128)(2,1)S(1)} %get-tuple-element.19.w_ref, bf16[512,4096]{1,0:T(8,128)(2,1)S(1)} %copy-done.3, f32[4,32,2]{2,1,0:T(8,128)S(1)} %copy-done.5, ...), custom_call_target="tpu_custom_call", output_to_operand_aliasing={{0}: (5, {}), {1}: (6, {})} | custom-call | flops 4294967296 | bytes 4194304 | tf_op jit(solution)/shard_map/pallas_call | solution.py:513
  37.0 3.4 %collective-permute-start.6 = (bf16[544,128]{1,0:T(8,128)(2,1)S(1)}, bf16[544,128]{1,0:T(8,128)(2,1)S(1)}, u32[]{:S(2)}, u32[]{:S(2)}) collective-permute-start(bf16[544,128]{1,0:T(8,128)(2,1)S(1)} %get-tuple-element.27.rest_4_), channel_id=1, source_target_pairs={{0,12},{4,8},{8,4},{12,0},{1,13},{5,9},{9,5},{13,1},{2,14},{6,10},... | collective-permute-start | bytes 417800 | tf_op jit(solution)/shard_map/ppermute | solution.py:531
  40.4 1.1 %collective-permute-start.4 = (bf16[544,128]{1,0:T(8,128)(2,1)S(1)}, bf16[544,128]{1,0:T(8,128)(2,1)S(1)}, u32[]{:S(2)}, u32[]{:S(2)}) collective-permute-start(bf16[544,128]{1,0:T(8,128)(2,1)S(1)} %get-tuple-element.27.rest_4_), channel_id=1, source_target_pairs={{0,4},{4,0},{8,12},{12,8},{1,5},{5,1},{9,13},{13,9},{2,6},{6,2},{1... | collective-permute-start | bytes 417800 | tf_op jit(solution)/shard_map/ppermute | solution.py:531
  41.5 1.5 %collective-permute-start.2 = (f32[16,128]{1,0:T(8,128)S(1)}, f32[16,128]{1,0:T(8,128)S(1)}, u32[]{:S(2)}, u32[]{:S(2)}) collective-permute-start(f32[16,128]{1,0:T(8,128)S(1)} %get-tuple-element.24.own_ref), channel_id=1, source_target_pairs={{0,16},{2,18},{16,0},{18,2},{1,17},{3,19},{17,1},{19,3},{4,20},{6,... | collective-permute-start | bytes 24584 | tf_op jit(solution)/shard_map/ppermute | solution.py:531
  43.0 2.1 %collective-permute-done.2.other_ref = f32[16,128]{1,0:T(8,128)S(1)} collective-permute-done((f32[16,128]{1,0:T(8,128)S(1)}, f32[16,128]{1,0:T(8,128)S(1)}, u32[]{:S(2)}, u32[]{:S(2)}) %collective-permute-start.2) | collective-permute-done | bytes 8224 | tf_op jit(solution)/shard_map/ppermute | solution.py:531
  45.1 4.9 %shard_map.97 = (bf16[8,1024,512]{2,1,0:T(8,128)(2,1)S(1)}, f32[3,8,256,256]{3,2,1,0:T(8,128)S(1)}, s32[1,512]{1,0:T(1,128)S(1)}) custom-call(s32[4]{0:T(128)S(1)} %pad_add_fusion.place_ref, s32[1,512]{1,0:T(1,128)S(1)} %bitcast.14, f32[16,128]{1,0:T(8,128)S(1)} %get-tuple-element.24.own_ref, f32[16,128]{1,0:T(8,128)S(1)} %collective-permute-done.2.other_ref, ...), custom_call_target="tpu_custom_call" | custom-call | flops 1000000000 | bytes 1000000 | tf_op jit(solution)/shard_map/pallas_call | solution.py:513
  50.0 0.3 collective-permute-done.5.rest_6_
  50.4 7.2 %shard_map.98 = bf16[2,16,16,128]{3,2,1,0:T(8,128)(2,1)S(1)} custom-call(s32[4]{0:T(128)S(1)} %pad_add_fusion.place_ref, f32[2,1024]{1,0:T(2,128)S(1)} %get-tuple-element.23.vo_ref, f32[16,128]{1,0:T(8,128)S(1)} %get-tuple-element.24.own_ref, f32[16,128]{1,0:T(8,128)S(1)} %collective-permute-done.2.other_ref, ...), custom_call_target="tpu_custom_call" | custom-call | tf_op jit(solution)/shard_map/pallas_call | solution.py:513
  57.6 12.8 %all_to_all.10 = bf16[32,16,128]{2,1,0:T(8,128)(2,1)S(1)} all-to-all(bf16[32,16,128]{2,1,0:T(8,128)(2,1)S(1)} %bitcast.11), channel_id=1, replica_groups=mesh['groups'=2,'line'=4,'pair'=2,'tensor'=2] {'groups','line','pair','t..., dimensions={0} | all-to-all | bytes 262144 | tf_op jit(solution)/shard_map/all_to_all | solution.py:677
  70.4 1.1 %shard_map.99 = f32[1,512]{1,0:T(1,128)} custom-call(bf16[2,4,4,16,128]{4,3,2,1,0:T(8,128)(2,1)S(1)} %bitcast.12, s32[1,512]{1,0:T(1,128)S(1)} %bitcast.15, s32[1,512]{1,0:T(1,128)S(1)} %get-tuple-element.28.slot_ref), custom_call_target="tpu_custom_call" | custom-call | tf_op jit(solution)/shard_map/pallas_call | solution.py:685
  (15 shorter events, 0.0 us)
Async XLA Ops:
  2.6 28.2 %all-to-all-start = ((bf16[8,400,128]{2,1,0:T(8,128)(2,1)}), bf16[8,400,128]{2,1,0:T(8,128)(2,1)S(1)}, u32[]{:S(2)}, u32[]{:S(2)}) async-start(bf16[8,400,128]{2,1,0:T(8,128)(2,1)} %shard_map.91.after_ref), calls=%async_computation | async-start | bytes 1638400 | tf_op jit(solution)/shard_map/all_to_all | solution.py:580
  9.9 20.9 %copy-start.5 = (f32[4,32,2]{2,1,0:T(8,128)S(1)}, f32[4,32,2]{2,1,0:T(8,128)}, u32[]{:S(2)}) copy-start(f32[4,32,2]{2,1,0:T(8,128)} %constant.17.clone.turn_ref) | copy-start | bytes 3076
  12.1 15.1 %collective-permute-start = (bf16[9,256,128]{2,1,0:T(8,128)(2,1)}, bf16[9,256,128]{2,1,0:T(8,128)(2,1)S(1)}, u32[]{:S(2)}, u32[]{:S(2)}) collective-permute-start(bf16[9,256,128]{2,1,0:T(8,128)(2,1)} %shard_map.93.rest_0_), channel_id=1, source_target_pairs={{0,16},{2,18},{16,0},{18,2},{1,17},{3,19},{17,1},{19,3},{4,20},{6,... | collective-permute-start | bytes 1769480 | tf_op jit(solution)/shard_map/ppermute | solution.py:531
  13.7 21.2 %collective-permute-start.1 = (bf16[9,256,128]{2,1,0:T(8,128)(2,1)}, bf16[9,256,128]{2,1,0:T(8,128)(2,1)S(1)}, u32[]{:S(2)}, u32[]{:S(2)}) collective-permute-start(bf16[9,256,128]{2,1,0:T(8,128)(2,1)} %shard_map.93.rest_0_), channel_id=1, source_target_pairs={{0,2},{2,0},{16,18},{18,16},{1,3},{3,1},{17,19},{19,17},{4,6},{6,4... | collective-permute-start | bytes 1769480 | tf_op jit(solution)/shard_map/ppermute | solution.py:531
  27.2 0.8 %copy-start.1 = (bf16[8,4096]{1,0:T(8,128)(2,1)S(1)}, bf16[8,4096]{1,0:T(8,128)(2,1)}, u32[]{:S(2)}) copy-start(bf16[8,4096]{1,0:T(8,128)(2,1)} %get-tuple-element.18.refs_1_) | copy-start | bytes 196612
  28.0 22.0 %collective-permute-start.3 = (bf16[9,256,128]{2,1,0:T(8,128)(2,1)S(1)}, bf16[9,256,128]{2,1,0:T(8,128)(2,1)S(1)}, u32[]{:S(2)}, u32[]{:S(2)}) collective-permute-start(bf16[9,256,128]{2,1,0:T(8,128)(2,1)S(1)} %shard_map.94.after_ref.rest_2_), channel_id=1, source_target_pairs={{0,2},{2,0},{16,18},{18,16},{1,3},{3,1},{17,19},{19,17},{4,6},{6,4... | collective-permute-start | bytes 1769480 | tf_op jit(solution)/shard_map/ppermute | solution.py:531
  30.8 2.2 %copy-start.4 = (bf16[512,4096]{1,0:T(8,128)(2,1)S(1)}, bf16[512,4096]{1,0:T(8,128)(2,1)}, u32[]{:S(2)}) copy-start(bf16[512,4096]{1,0:T(8,128)(2,1)} %get-tuple-element.17.normed_ref) | copy-start | bytes 12582916
  33.0 2.2 %copy-start.3 = (bf16[512,4096]{1,0:T(8,128)(2,1)S(1)}, bf16[512,4096]{1,0:T(8,128)(2,1)}, u32[]{:S(2)}) copy-start(bf16[512,4096]{1,0:T(8,128)(2,1)} %get-tuple-element.20.normed_ref) | copy-start | bytes 12582916
  35.2 9.9 %copy-start = (bf16[9,256,128]{2,1,0:T(8,128)(2,1)S(1)}, bf16[9,256,128]{2,1,0:T(8,128)(2,1)}, u32[]{:S(2)}) copy-start(bf16[9,256,128]{2,1,0:T(8,128)(2,1)} %shard_map.93.rest_0_) | copy-start | bytes 1769476
  35.2 9.9 %copy-start.2 = (s32[512,1]{0,1:T(1,128)S(1)}, s32[512,1]{0,1:T(1,128)}, u32[]{:S(2)}) copy-start(s32[512,1]{0,1:T(1,128)} %param.11) | copy-start | bytes 6148
  37.0 13.0 %collective-permute-start.6 = (bf16[544,128]{1,0:T(8,128)(2,1)S(1)}, bf16[544,128]{1,0:T(8,128)(2,1)S(1)}, u32[]{:S(2)}, u32[]{:S(2)}) collective-permute-start(bf16[544,128]{1,0:T(8,128)(2,1)S(1)} %get-tuple-element.27.rest_4_), channel_id=1, source_target_pairs={{0,12},{4,8},{8,4},{12,0},{1,13},{5,9},{9,5},{13,1},{2,14},{6,10},... | collective-permute-start | bytes 417800 | tf_op jit(solution)/shard_map/ppermute | solution.py:531
  40.4 10.0 %collective-permute-start.5 = (bf16[544,128]{1,0:T(8,128)(2,1)S(1)}, bf16[544,128]{1,0:T(8,128)(2,1)S(1)}, u32[]{:S(2)}, u32[]{:S(2)}) collective-permute-start(bf16[544,128]{1,0:T(8,128)(2,1)S(1)} %get-tuple-element.27.rest_4_), channel_id=1, source_target_pairs={{0,8},{4,12},{8,0},{12,4},{1,9},{5,13},{9,1},{13,5},{2,10},{6,14},... | collective-permute-start | bytes 417800 | tf_op jit(solution)/shard_map/ppermute | solution.py:531
  40.4 10.0 %collective-permute-start.4 = (bf16[544,128]{1,0:T(8,128)(2,1)S(1)}, bf16[544,128]{1,0:T(8,128)(2,1)S(1)}, u32[]{:S(2)}, u32[]{:S(2)}) collective-permute-start(bf16[544,128]{1,0:T(8,128)(2,1)S(1)} %get-tuple-element.27.rest_4_), channel_id=1, source_target_pairs={{0,4},{4,0},{8,12},{12,8},{1,5},{5,1},{9,13},{13,9},{2,6},{6,2},{1... | collective-permute-start | bytes 417800 | tf_op jit(solution)/shard_map/ppermute | solution.py:531
  41.5 3.7 %collective-permute-start.2 = (f32[16,128]{1,0:T(8,128)S(1)}, f32[16,128]{1,0:T(8,128)S(1)}, u32[]{:S(2)}, u32[]{:S(2)}) collective-permute-start(f32[16,128]{1,0:T(8,128)S(1)} %get-tuple-element.24.own_ref), channel_id=1, source_target_pairs={{0,16},{2,18},{16,0},{18,2},{1,17},{3,19},{17,1},{19,3},{4,20},{6,... | collective-permute-start | bytes 24584 | tf_op jit(solution)/shard_map/ppermute | solution.py:531

commit v23 on v22

--- a/solution.py
+++ b/solution.py
@@ -70,7 +70,7 @@
         pltpu.make_async_copy(wq_hbm.at[:, columns_here], wq, sems.at[3]),
         pltpu.make_async_copy(wkv_hbm, wkv, sems.at[4]),
     )
-    for copy in copies:
+    for copy in copies[::-1]:
         copy.start()
     for copy in copies[:3]:
         copy.wait()
@@ -205,9 +205,7 @@
             copy(step + held).start()
     for step in range(max(0, steps - held), steps):
         store(step).wait()
-    mark = pltpu.make_async_copy(made.at[0, pl.ds(0, mark_ref.shape[0])], mark_ref, out_sems.at[0])
-    mark.start()
-    mark.wait()
+    mark_ref[...] = jnp.zeros_like(mark_ref)
 
 
 def spread_weights(plan, w_ref, full_ref):
@@ -318,7 +316,7 @@
     return pl.pallas_call(
         lambda *refs: None,
         out_shape=shape(x.shape, x.dtype),
-        in_specs=[untouched()] + [pl.BlockSpec(memory_space=pltpu.HBM)] * len(others),
+        in_specs=[untouched()] + [pl.BlockSpec(memory_space=pltpu.VMEM)] * len(others),
         out_specs=untouched(),
         input_output_aliases={0: 0},
         compiler_params=limits(1),
@@ -599,9 +597,9 @@
     vmem = pl.BlockSpec(memory_space=pltpu.VMEM)
     *normed, mark = pl.pallas_call(
         normalize,
-        out_shape=[*[shape((moves // 2, width), BF16)] * 2, pltpu.HBM((8, width), BF16)],
+        out_shape=[*[shape((moves // 2, width), BF16)] * 2, pltpu.VMEM((8, HD), F32)],
         in_specs=[untouched(), vmem, untouched()],
-        out_specs=[untouched()] * 3,
+        out_specs=[untouched(), untouched(), vmem],
         scratch_shapes=[
             pltpu.VMEM((1, width), F32),
             pltpu.VMEM((3, block, width), BF16),

time: 71.9 us -> 72.1 us (level)
  waiting for transfers between devices: 5.99 us -> 7.47 us
  local copies, waits for them, and re-layouts: 3.3 us -> 2.45 us
    unnamed x12 -> x10, local copies, waits for them, and re-layouts: 3.3 us -> 2.45 us
    all_to_all x1, waiting for transfers between devices: 1.04 us -> 1.88 us  [per_device(): lax.all_to_all(packed, ('line', 'pair'), split_axis=0, concat_axis=0, til...]
  transfers between devices with their start and end apart: 8 -> 8, of which waited for: 4 -> 4; matrix products, arithmetic and copies ran while one was open for 0% -> 0% of each run, Pallas kernels for 28% -> 27%
where the time goes in v23:
time: 72.1 us; the launch traced here: 71.7 us
  Pallas kernels  30.3 us (42%)
  starting transfers between devices  18.6 us (26%)
  blocking collectives  12.8 us (18%)
  waiting for transfers between devices  7.47 us (10%)
  local copies, waits for them, and re-layouts  2.45 us (3%)
    pallas_call x5, Pallas kernels, local_call(): pl.pallas_call(kernel, out_shape=outs, in_specs=[pl.BlockSpec(memory_spac...  18.7 us
    all_to_all x1, blocking collectives, per_device(): lax.all_to_all(parts.reshape(groups * back, plan.share, plan.slots), ('gr...  12.8 us
    ppermute x7, starting transfers between devices, swap(): return lax.ppermute(x, names, [(at, at ^ step) for at in range(size)])  11.3 us
    pallas_call x1, Pallas kernels, per_device(): pl.pallas_call(normalize, out_shape=[*[shape((moves // 2, width), BF16)]...  8.3 us
    all_to_all x1, starting transfers between devices, per_device(): lax.all_to_all(packed, ('line', 'pair'), split_axis=0, concat_axis=0, til...  7.27 us
    ppermute x7, waiting for transfers between devices, swap(): return lax.ppermute(x, names, [(at, at ^ step) for at in range(size)])  5.59 us
    unnamed x10, local copies, waits for them, and re-layouts  2.45 us
    pallas_call x1, Pallas kernels, per_device(): pl.pallas_call(functools.partial(pack_prefix, plan), out_shape=shape((boa...  2.21 us
  transfers between devices with their start and end apart: 8, of which 4 were waited for; matrix products, arithmetic and copies ran while one was open for 0% of the time, Pallas kernels for 27%

profile of v23, /device:TPU:0, one launch (start us, length us, event | category | flops | bytes accessed | tf_op | source)
XLA Modules:
  0.0 71.7 jit_solution(15008402116719938449)
XLA Ops:
  0.0 2.9 %shard_map.91.after_ref = bf16[8,400,128]{2,1,0:T(8,128)(2,1)} custom-call(s32[1]{0:T(128)} %bitcast.place_ref, bf16[512,1024]{1,0:T(8,128)(2,1)} %wq_hbm.1, bf16[512,256]{1,0:T(8,128)(2,1)} %wkv_hbm.1, bf16[8,128]{1,0:T(8,128)(2,1)} %bitcast.17, s32[1,512]{1,0:T(1,128)} %bitcast.13, s32[1,512]{1,0:T(1,128)} %bitcast.19), custom_call_target="tpu_custom_call" | custom-call | tf_op jit(solution)/shard_map/pallas_call | solution.py:511
  2.9 7.3 %all-to-all-start = ((bf16[8,400,128]{2,1,0:T(8,128)(2,1)}), bf16[8,400,128]{2,1,0:T(8,128)(2,1)S(1)}, u32[]{:S(2)}, u32[]{:S(2)}) async-start(bf16[8,400,128]{2,1,0:T(8,128)(2,1)} %shard_map.91.after_ref), calls=%async_computation | async-start | bytes 1638400 | tf_op jit(solution)/shard_map/all_to_all | solution.py:578
  10.1 2.2 %shard_map.93.rest_0_ = bf16[9,256,128]{2,1,0:T(8,128)(2,1)} custom-call(bf16[8,256,256]{2,1,0:T(8,128)(2,1)} %prefix_hbm.1, bf16[8,128]{1,0:T(8,128)(2,1)} %bitcast.18, bf16[8,400,128]{2,1,0:T(8,128)(2,1)} %shard_map.91.after_ref), custom_call_target="tpu_custom_call" | custom-call | tf_op jit(solution)/shard_map/pallas_call | solution.py:580
  12.4 1.6 %collective-permute-start = (bf16[9,256,128]{2,1,0:T(8,128)(2,1)}, bf16[9,256,128]{2,1,0:T(8,128)(2,1)S(1)}, u32[]{:S(2)}, u32[]{:S(2)}) collective-permute-start(bf16[9,256,128]{2,1,0:T(8,128)(2,1)} %shard_map.93.rest_0_), channel_id=1, source_target_pairs={{0,16},{2,18},{16,0},{18,2},{1,17},{3,19},{17,1},{19,3},{4,20},{6,... | collective-permute-start | bytes 1769480 | tf_op jit(solution)/shard_map/ppermute | solution.py:529
  14.0 2.0 %collective-permute-start.1 = (bf16[9,256,128]{2,1,0:T(8,128)(2,1)}, bf16[9,256,128]{2,1,0:T(8,128)(2,1)S(1)}, u32[]{:S(2)}, u32[]{:S(2)}) collective-permute-start(bf16[9,256,128]{2,1,0:T(8,128)(2,1)} %shard_map.93.rest_0_), channel_id=1, source_target_pairs={{0,2},{2,0},{16,18},{18,16},{1,3},{3,1},{17,19},{19,17},{4,6},{6,4... | collective-permute-start | bytes 1769480 | tf_op jit(solution)/shard_map/ppermute | solution.py:529
  16.0 8.3 %shard_map.92 = (bf16[512,4096]{1,0:T(8,128)(2,1)}, bf16[512,4096]{1,0:T(8,128)(2,1)}, f32[8,128]{1,0:T(8,128)S(1)}) custom-call(bf16[1024,4096]{1,0:T(8,128)(2,1)} %table_hbm.1, bf16[32,128]{1,0:T(8,128)(2,1)} %bitcast.16, bf16[8,400,128]{2,1,0:T(8,128)(2,1)} %shard_map.91.after_ref), custom_call_target="tpu_custom_call" | custom-call | flops 4194304 | bytes 1048576 | tf_op jit(solution)/shard_map/pallas_call | solution.py:598
  24.3 0.1 pad_add_fusion.place_ref
  24.4 3.1 %collective-permute-done.refs_0_ = bf16[9,256,128]{2,1,0:T(8,128)(2,1)S(1)} collective-permute-done((bf16[9,256,128]{2,1,0:T(8,128)(2,1)}, bf16[9,256,128]{2,1,0:T(8,128)(2,1)S(1)}, u32[]{:S(2)}, u32[]{:S(2)}) %collective-permute-start) | collective-permute-done | bytes 589856 | tf_op jit(solution)/shard_map/ppermute | solution.py:529
  27.4 1.7 %collective-permute-start.3 = (bf16[9,256,128]{2,1,0:T(8,128)(2,1)S(1)}, bf16[9,256,128]{2,1,0:T(8,128)(2,1)S(1)}, u32[]{:S(2)}, u32[]{:S(2)}) collective-permute-start(bf16[9,256,128]{2,1,0:T(8,128)(2,1)S(1)} %shard_map.94.after_ref.rest_2_), channel_id=1, source_target_pairs={{0,2},{2,0},{16,18},{18,16},{1,3},{3,1},{17,19},{19,17},{4,6},{6,4... | collective-permute-start | bytes 1769480 | tf_op jit(solution)/shard_map/ppermute | solution.py:529
  29.2 1.9 %all-to-all-done.w_ref = bf16[8,400,128]{2,1,0:T(8,128)(2,1)S(1)} async-done(((bf16[8,400,128]{2,1,0:T(8,128)(2,1)}), bf16[8,400,128]{2,1,0:T(8,128)(2,1)S(1)}, u32[]{:S(2)}, u32[]{:S(2)}) %all-to-all-start) | async-done | bytes 819232 | tf_op jit(solution)/shard_map/all_to_all | solution.py:578
  31.1 2.2 %copy-done.3 = bf16[512,4096]{1,0:T(8,128)(2,1)S(1)} copy-done((bf16[512,4096]{1,0:T(8,128)(2,1)S(1)}, bf16[512,4096]{1,0:T(8,128)(2,1)}, u32[]{:S(2)}) %copy-start.3) | copy-done | bytes 4194328
  33.2 1.9 %shard_map.95 = (bf16[544,128]{1,0:T(8,128)(2,1)S(1)}, f32[2,1024]{1,0:T(2,128)S(1)}, f32[16,128]{1,0:T(8,128)S(1)}, bf16[8,104,512]{2,1,0:T(8,128)(2,1)S(1)}) custom-call(s32[4]{0:T(128)S(1)} %pad_add_fusion.place_ref, bf16[8,400,128]{2,1,0:T(8,128)(2,1)S(1)} %all-to-all-done.w_ref, bf16[512,4096]{1,0:T(8,128)(2,1)S(1)} %copy-done.3, ...), custom_call_target="tpu_custom_call" | custom-call | flops 4294967296 | bytes 4194304 | tf_op jit(solution)/shard_map/pallas_call | solution.py:511
  35.2 0.2 copy-done.2
  35.4 1.8 %shard_map.96 = (bf16[544,128]{1,0:T(8,128)(2,1)S(1)}, f32[2,1024]{1,0:T(2,128)S(1)}) custom-call(s32[4]{0:T(128)S(1)} %pad_add_fusion.place_ref, bf16[8,104,512]{2,1,0:T(8,128)(2,1)S(1)} %get-tuple-element.19.w_ref, bf16[512,4096]{1,0:T(8,128)(2,1)S(1)} %copy-done.2, f32[4,32,2]{2,1,0:T(8,128)S(1)} %copy-done.4, ...), custom_call_target="tpu_custom_call", output_to_operand_aliasing={{0}: (5, {}), {1}: (6, {})} | custom-call | flops 4294967296 | bytes 4194304 | tf_op jit(solution)/shard_map/pallas_call | solution.py:511
  37.2 3.4 %collective-permute-start.6 = (bf16[544,128]{1,0:T(8,128)(2,1)S(1)}, bf16[544,128]{1,0:T(8,128)(2,1)S(1)}, u32[]{:S(2)}, u32[]{:S(2)}) collective-permute-start(bf16[544,128]{1,0:T(8,128)(2,1)S(1)} %get-tuple-element.27.rest_4_), channel_id=1, source_target_pairs={{0,12},{4,8},{8,4},{12,0},{1,13},{5,9},{9,5},{13,1},{2,14},{6,10},... | collective-permute-start | bytes 417800 | tf_op jit(solution)/shard_map/ppermute | solution.py:529
  40.6 0.0 collective-permute-start.5
  40.6 1.1 %collective-permute-start.4 = (bf16[544,128]{1,0:T(8,128)(2,1)S(1)}, bf16[544,128]{1,0:T(8,128)(2,1)S(1)}, u32[]{:S(2)}, u32[]{:S(2)}) collective-permute-start(bf16[544,128]{1,0:T(8,128)(2,1)S(1)} %get-tuple-element.27.rest_4_), channel_id=1, source_target_pairs={{0,4},{4,0},{8,12},{12,8},{1,5},{5,1},{9,13},{13,9},{2,6},{6,2},{1... | collective-permute-start | bytes 417800 | tf_op jit(solution)/shard_map/ppermute | solution.py:529
  41.7 1.5 %collective-permute-start.2 = (f32[16,128]{1,0:T(8,128)S(1)}, f32[16,128]{1,0:T(8,128)S(1)}, u32[]{:S(2)}, u32[]{:S(2)}) collective-permute-start(f32[16,128]{1,0:T(8,128)S(1)} %get-tuple-element.24.own_ref), channel_id=1, source_target_pairs={{0,16},{2,18},{16,0},{18,2},{1,17},{3,19},{17,1},{19,3},{4,20},{6,... | collective-permute-start | bytes 24584 | tf_op jit(solution)/shard_map/ppermute | solution.py:529
  43.2 2.1 %collective-permute-done.2.other_ref = f32[16,128]{1,0:T(8,128)S(1)} collective-permute-done((f32[16,128]{1,0:T(8,128)S(1)}, f32[16,128]{1,0:T(8,128)S(1)}, u32[]{:S(2)}, u32[]{:S(2)}) %collective-permute-start.2) | collective-permute-done | bytes 8224 | tf_op jit(solution)/shard_map/ppermute | solution.py:529
  45.3 4.9 %shard_map.97 = (bf16[8,1024,512]{2,1,0:T(8,128)(2,1)S(1)}, f32[3,8,256,256]{3,2,1,0:T(8,128)S(1)}, s32[1,512]{1,0:T(1,128)S(1)}) custom-call(s32[4]{0:T(128)S(1)} %pad_add_fusion.place_ref, s32[1,512]{1,0:T(1,128)S(1)} %bitcast.14, f32[16,128]{1,0:T(8,128)S(1)} %get-tuple-element.24.own_ref, f32[16,128]{1,0:T(8,128)S(1)} %collective-permute-done.2.other_ref, ...), custom_call_target="tpu_custom_call" | custom-call | flops 1000000000 | bytes 1000000 | tf_op jit(solution)/shard_map/pallas_call | solution.py:511
  50.2 0.4 collective-permute-done.5.rest_6_
  50.6 7.2 %shard_map.98 = bf16[2,16,16,128]{3,2,1,0:T(8,128)(2,1)S(1)} custom-call(s32[4]{0:T(128)S(1)} %pad_add_fusion.place_ref, f32[2,1024]{1,0:T(2,128)S(1)} %get-tuple-element.23.vo_ref, f32[16,128]{1,0:T(8,128)S(1)} %get-tuple-element.24.own_ref, f32[16,128]{1,0:T(8,128)S(1)} %collective-permute-done.2.other_ref, ...), custom_call_target="tpu_custom_call" | custom-call | tf_op jit(solution)/shard_map/pallas_call | solution.py:511
  57.8 12.8 %all_to_all.10 = bf16[32,16,128]{2,1,0:T(8,128)(2,1)S(1)} all-to-all(bf16[32,16,128]{2,1,0:T(8,128)(2,1)S(1)} %bitcast.11), channel_id=1, replica_groups=mesh['groups'=2,'line'=4,'pair'=2,'tensor'=2] {'groups','line','pair','t..., dimensions={0} | all-to-all | bytes 262144 | tf_op jit(solution)/shard_map/all_to_all | solution.py:675
  70.7 1.1 %shard_map.99 = f32[1,512]{1,0:T(1,128)} custom-call(bf16[2,4,4,16,128]{4,3,2,1,0:T(8,128)(2,1)S(1)} %bitcast.12, s32[1,512]{1,0:T(1,128)S(1)} %bitcast.15, s32[1,512]{1,0:T(1,128)S(1)} %get-tuple-element.28.slot_ref), custom_call_target="tpu_custom_call" | custom-call | tf_op jit(solution)/shard_map/pallas_call | solution.py:683
  (13 shorter events, 0.0 us)
Async XLA Ops:
  2.9 28.2 %all-to-all-start = ((bf16[8,400,128]{2,1,0:T(8,128)(2,1)}), bf16[8,400,128]{2,1,0:T(8,128)(2,1)S(1)}, u32[]{:S(2)}, u32[]{:S(2)}) async-start(bf16[8,400,128]{2,1,0:T(8,128)(2,1)} %shard_map.91.after_ref), calls=%async_computation | async-start | bytes 1638400 | tf_op jit(solution)/shard_map/all_to_all | solution.py:578
  10.1 20.9 %copy-start.4 = (f32[4,32,2]{2,1,0:T(8,128)S(1)}, f32[4,32,2]{2,1,0:T(8,128)}, u32[]{:S(2)}) copy-start(f32[4,32,2]{2,1,0:T(8,128)} %constant.17.clone.turn_ref) | copy-start | bytes 3076
  12.4 15.1 %collective-permute-start = (bf16[9,256,128]{2,1,0:T(8,128)(2,1)}, bf16[9,256,128]{2,1,0:T(8,128)(2,1)S(1)}, u32[]{:S(2)}, u32[]{:S(2)}) collective-permute-start(bf16[9,256,128]{2,1,0:T(8,128)(2,1)} %shard_map.93.rest_0_), channel_id=1, source_target_pairs={{0,16},{2,18},{16,0},{18,2},{1,17},{3,19},{17,1},{19,3},{4,20},{6,... | collective-permute-start | bytes 1769480 | tf_op jit(solution)/shard_map/ppermute | solution.py:529
  14.0 21.2 %collective-permute-start.1 = (bf16[9,256,128]{2,1,0:T(8,128)(2,1)}, bf16[9,256,128]{2,1,0:T(8,128)(2,1)S(1)}, u32[]{:S(2)}, u32[]{:S(2)}) collective-permute-start(bf16[9,256,128]{2,1,0:T(8,128)(2,1)} %shard_map.93.rest_0_), channel_id=1, source_target_pairs={{0,2},{2,0},{16,18},{18,16},{1,3},{3,1},{17,19},{19,17},{4,6},{6,4... | collective-permute-start | bytes 1769480 | tf_op jit(solution)/shard_map/ppermute | solution.py:529
  27.4 22.8 %collective-permute-start.3 = (bf16[9,256,128]{2,1,0:T(8,128)(2,1)S(1)}, bf16[9,256,128]{2,1,0:T(8,128)(2,1)S(1)}, u32[]{:S(2)}, u32[]{:S(2)}) collective-permute-start(bf16[9,256,128]{2,1,0:T(8,128)(2,1)S(1)} %shard_map.94.after_ref.rest_2_), channel_id=1, source_target_pairs={{0,2},{2,0},{16,18},{18,16},{1,3},{3,1},{17,19},{19,17},{4,6},{6,4... | collective-permute-start | bytes 1769480 | tf_op jit(solution)/shard_map/ppermute | solution.py:529
  31.1 2.2 %copy-start.3 = (bf16[512,4096]{1,0:T(8,128)(2,1)S(1)}, bf16[512,4096]{1,0:T(8,128)(2,1)}, u32[]{:S(2)}) copy-start(bf16[512,4096]{1,0:T(8,128)(2,1)} %get-tuple-element.17.normed_ref) | copy-start | bytes 12582916
  33.2 2.2 %copy-start.2 = (bf16[512,4096]{1,0:T(8,128)(2,1)S(1)}, bf16[512,4096]{1,0:T(8,128)(2,1)}, u32[]{:S(2)}) copy-start(bf16[512,4096]{1,0:T(8,128)(2,1)} %get-tuple-element.20.normed_ref) | copy-start | bytes 12582916
  35.4 9.9 %copy-start = (bf16[9,256,128]{2,1,0:T(8,128)(2,1)S(1)}, bf16[9,256,128]{2,1,0:T(8,128)(2,1)}, u32[]{:S(2)}) copy-start(bf16[9,256,128]{2,1,0:T(8,128)(2,1)} %shard_map.93.rest_0_) | copy-start | bytes 1769476
  35.4 9.9 %copy-start.1 = (s32[512,1]{0,1:T(1,128)S(1)}, s32[512,1]{0,1:T(1,128)}, u32[]{:S(2)}) copy-start(s32[512,1]{0,1:T(1,128)} %param.11) | copy-start | bytes 6148
  37.2 13.0 %collective-permute-start.6 = (bf16[544,128]{1,0:T(8,128)(2,1)S(1)}, bf16[544,128]{1,0:T(8,128)(2,1)S(1)}, u32[]{:S(2)}, u32[]{:S(2)}) collective-permute-start(bf16[544,128]{1,0:T(8,128)(2,1)S(1)} %get-tuple-element.27.rest_4_), channel_id=1, source_target_pairs={{0,12},{4,8},{8,4},{12,0},{1,13},{5,9},{9,5},{13,1},{2,14},{6,10},... | collective-permute-start | bytes 417800 | tf_op jit(solution)/shard_map/ppermute | solution.py:529
  40.6 10.0 %collective-permute-start.5 = (bf16[544,128]{1,0:T(8,128)(2,1)S(1)}, bf16[544,128]{1,0:T(8,128)(2,1)S(1)}, u32[]{:S(2)}, u32[]{:S(2)}) collective-permute-start(bf16[544,128]{1,0:T(8,128)(2,1)S(1)} %get-tuple-element.27.rest_4_), channel_id=1, source_target_pairs={{0,8},{4,12},{8,0},{12,4},{1,9},{5,13},{9,1},{13,5},{2,10},{6,14},... | collective-permute-start | bytes 417800 | tf_op jit(solution)/shard_map/ppermute | solution.py:529
  40.6 10.0 %collective-permute-start.4 = (bf16[544,128]{1,0:T(8,128)(2,1)S(1)}, bf16[544,128]{1,0:T(8,128)(2,1)S(1)}, u32[]{:S(2)}, u32[]{:S(2)}) collective-permute-start(bf16[544,128]{1,0:T(8,128)(2,1)S(1)} %get-tuple-element.27.rest_4_), channel_id=1, source_target_pairs={{0,4},{4,0},{8,12},{12,8},{1,5},{5,1},{9,13},{13,9},{2,6},{6,2},{1... | collective-permute-start | bytes 417800 | tf_op jit(solution)/shard_map/ppermute | solution.py:529
  41.7 3.7 %collective-permute-start.2 = (f32[16,128]{1,0:T(8,128)S(1)}, f32[16,128]{1,0:T(8,128)S(1)}, u32[]{:S(2)}, u32[]{:S(2)}) collective-permute-start(f32[16,128]{1,0:T(8,128)S(1)} %get-tuple-element.24.own_ref), channel_id=1, source_target_pairs={{0,16},{2,18},{16,0},{18,2},{1,17},{3,19},{17,1},{19,3},{4,20},{6,... | collective-permute-start | bytes 24584 | tf_op jit(solution)/shard_map/ppermute | solution.py:529

commit v24 on v23

--- a/solution.py
+++ b/solution.py
@@ -59,7 +59,7 @@
 
 
 def pack_weights(plan, place_ref, wq_hbm, wkv_hbm, ws_hbm, board_hbm, ids_hbm, *rest):
-    out_ref, wq, wkv, ws_ref, board_ref, ids_ref, pick, sems = rest
+    out_hbm, wq, wkv, ws_ref, board_ref, ids_ref, pick, made, ends, sems, out_sems = rest
     group = place_ref[0]
     half_cols = wq.shape[1]
     columns_here = pl.ds(pl.multiple_of(group * half_cols, HD), half_cols)
@@ -70,8 +70,18 @@
         pltpu.make_async_copy(wq_hbm.at[:, columns_here], wq, sems.at[3]),
         pltpu.make_async_copy(wkv_hbm, wkv, sems.at[4]),
     )
-    for copy in copies[::-1]:
+    for copy in copies:
         copy.start()
+
+    def send(part):
+        source, first = ((made, 0), (ends, made.shape[1]))[part]
+        return pltpu.make_async_copy(source, out_hbm.at[:, pl.ds(first, source.shape[1])], out_sems.at[part])
+
+    if plan.tight:
+        for copy in copies[3:]:
+            copy.wait()
+        turn_weights(plan, wq, wkv, made)
+        send(0).start()
     for copy in copies[:3]:
         copy.wait()
     count, depth = board_ref.shape[1], wq.shape[0]
@@ -99,28 +109,26 @@
         lists.append(jnp.sum(both, axis=0, keepdims=True))
 
     if plan.tight:
-        turn_weights(plan, group, lists, copies[3:], wq, wkv, ws_ref, out_ref)
+        last_rows(plan, group, lists, wkv, ws_ref, ends)
+        send(1).start()
+        send(0).wait()
+        send(1).wait()
     else:
-        pick_weights(plan, group, lists, copies[3:], wq, wkv, ws_ref, out_ref, pick)
-
-
-def turn_weights(plan, group, lists, copies, wq, wkv, ws_ref, out_ref):
-    for copy in copies:
+        pick_weights(plan, group, lists, copies[3:], wq, wkv, ws_ref, made, pick)
+        copy = pltpu.make_async_copy(made, out_hbm, out_sems.at[0])
+        copy.start()
         copy.wait()
+
+
+def turn_weights(plan, wq, wkv, out_ref):
     q = wq[...].T
     k = wkv[:, :HD].T
-    folds = matmul(ws_ref[...], wkv[:, HD:], NT)
-    row = lax.broadcasted_iota(jnp.int32, folds.shape, 0)
     pairs = plan.pairs
-    lanes = [slice(c * HD, (c + 1) * HD) for c in range(plan.chunks)]
-    first_last = plan.fold_at * plan.chunks
-    zeros = jnp.zeros((plan.sent[0] - first_last - (plan.mine + 1) * plan.chunks, HD), F32)
     for pair in range(plan.pair):
-        first = (group * plan.pair + pair) * plan.mine
-        mine = [jnp.sum(jnp.where(row == first + h, folds, 0.0), axis=0, keepdims=True) for h in range(plan.mine)]
         for line in range(plan.line):
             peer = line * plan.pair + pair
-            for c, lane in enumerate(lanes):
+            for c in range(plan.chunks):
+                lane = slice(c * HD, (c + 1) * HD)
                 for part in range(2):
                     entry = part * HALF + line * pairs
                     for h in range(plan.mine):
@@ -129,8 +137,19 @@
                         out_ref[peer, at : at + pairs] = q[source : source + pairs, lane]
                     at = c * plan.fold_at + plan.q_rows + part * pairs
                     out_ref[peer, at : at + pairs] = k[entry : entry + pairs, lane]
+
+
+def last_rows(plan, group, lists, wkv, ws_ref, out_ref):
+    folds = matmul(ws_ref[...], wkv[:, HD:], NT)
+    row = lax.broadcasted_iota(jnp.int32, folds.shape, 0)
+    lanes = [slice(c * HD, (c + 1) * HD) for c in range(plan.chunks)]
+    zeros = jnp.zeros((out_ref.shape[1] - (plan.mine + 1) * plan.chunks, HD), F32)
+    for pair in range(plan.pair):
+        first = (group * plan.pair + pair) * plan.mine
+        mine = [jnp.sum(jnp.where(row == first + h, folds, 0.0), axis=0, keepdims=True) for h in range(plan.mine)]
+        for line in range(plan.line):
             last = [values[:, lane] for values in (*mine, lists[line]) for lane in lanes]
-            out_ref[peer, first_last:] = jnp.concatenate([*last, zeros], axis=0).astype(BF16)
+            out_ref[line * plan.pair + pair] = jnp.concatenate([*last, zeros], axis=0).astype(BF16)
 
 
 def pick_weights(plan, group, lists, copies, wq, wkv, ws_ref, out_ref, pick):
@@ -558,23 +577,27 @@
     board_row = move_board.reshape(1, row_count)
 
     half_cols = w_query.shape[1] // groups
-    packed = local_call(
+    turned = plan.fold_at * plan.chunks if plan.tight else plan.sent[0]
+    made = [pltpu.VMEM((plan.peers, size, plan.sent[1]), BF16) for size in (turned, max(16, plan.sent[0] - turned))]
+    packed = pl.pallas_call(
         functools.partial(pack_weights, plan),
-        group_at.reshape(1),
-        (w_query, w_keyval, ws, board_row, move_ids.reshape(1, row_count)),
-        shape((plan.peers, *plan.sent), BF16),
-        [
+        out_shape=shape((plan.peers, *plan.sent), BF16),
+        in_specs=[pl.BlockSpec(memory_space=pltpu.SMEM)] + [untouched()] * 5,
+        out_specs=untouched(),
+        scratch_shapes=[
             pltpu.VMEM((depth, half_cols), BF16),
             pltpu.VMEM((depth, 2 * HD), BF16),
             pltpu.VMEM((heads, HD), BF16),
             pltpu.VMEM((1, row_count), jnp.int32),
             pltpu.VMEM((1, row_count), jnp.int32),
             pltpu.VMEM((plan.peers * plan.rows, half_cols + 2 * HD), F32),
+            *made,
             pltpu.SemaphoreType.DMA((5,)),
+            pltpu.SemaphoreType.DMA((2,)),
         ],
-        62,
-        range(5),
-    )
+        compiler_params=limits(62),
+        cost_estimate=cost(0, 0),
+    )(group_at.reshape(1), w_query, w_keyval, ws, board_row, move_ids.reshape(1, row_count))
     weights = lax.all_to_all(packed, ("line", "pair"), split_axis=0, concat_axis=0, tiled=True)
 
     payload = pl.pallas_call(

time: 72.1 us -> 72 us (level)
    pallas_call x5 -> x4, Pallas kernels: 18.7 us -> 15.8 us  [local_call(): pl.pallas_call(kernel, out_shape=outs, in_specs=[pl.BlockSpec(memory_spac...]
    pallas_call x0 -> x1, Pallas kernels: none -> 2.76 us  [per_device(): pl.pallas_call(functools.partial(pack_weights, plan), out_shape=shape((pl...]
where the time goes in v24:
time: 72 us; the launch traced here: 71.6 us
  Pallas kernels  30.1 us (42%)
  starting transfers between devices  18.6 us (26%)
  blocking collectives  12.8 us (18%)
  waiting for transfers between devices  7.45 us (10%)
  local copies, waits for them, and re-layouts  2.46 us (3%)
    pallas_call x4, Pallas kernels, local_call(): pl.pallas_call(kernel, out_shape=outs, in_specs=[pl.BlockSpec(memory_spac...  15.8 us
    all_to_all x1, blocking collectives, per_device(): lax.all_to_all(parts.reshape(groups * back, plan.share, plan.slots), ('gr...  12.8 us
    ppermute x7, starting transfers between devices, swap(): return lax.ppermute(x, names, [(at, at ^ step) for at in range(size)])  11.3 us
    pallas_call x1, Pallas kernels, per_device(): pl.pallas_call(normalize, out_shape=[*[shape((moves // 2, width), BF16)]...  8.3 us
    all_to_all x1, starting transfers between devices, per_device(): lax.all_to_all(packed, ('line', 'pair'), split_axis=0, concat_axis=0, til...  7.26 us
    ppermute x7, waiting for transfers between devices, swap(): return lax.ppermute(x, names, [(at, at ^ step) for at in range(size)])  5.57 us
    pallas_call x1, Pallas kernels, per_device(): pl.pallas_call(functools.partial(pack_weights, plan), out_shape=shape((pl...  2.76 us
    unnamed x10, local copies, waits for them, and re-layouts  2.46 us
  transfers between devices with their start and end apart: 8, of which 4 were waited for; matrix products, arithmetic and copies ran while one was open for 0% of the time, Pallas kernels for 27%

profile of v24, /device:TPU:0, one launch (start us, length us, event | category | flops | bytes accessed | tf_op | source)
XLA Modules:
  0.0 71.6 jit_solution(12718851727547708139)
XLA Ops:
  0.0 2.8 %shard_map.91.after_ref = bf16[8,400,128]{2,1,0:T(8,128)(2,1)} custom-call(s32[1]{0:T(128)} %bitcast.place_ref, bf16[512,1024]{1,0:T(8,128)(2,1)} %wq_hbm.1, bf16[512,256]{1,0:T(8,128)(2,1)} %wkv_hbm.1, bf16[8,128]{1,0:T(8,128)(2,1)} %bitcast.17, s32[1,512]{1,0:T(1,128)} %bitcast.13, s32[1,512]{1,0:T(1,128)} %bitcast.19), custom_call_target="tpu_custom_call" | custom-call | tf_op jit(solution)/shard_map/pallas_call | solution.py:582
  2.8 7.3 %all-to-all-start = ((bf16[8,400,128]{2,1,0:T(8,128)(2,1)}), bf16[8,400,128]{2,1,0:T(8,128)(2,1)S(1)}, u32[]{:S(2)}, u32[]{:S(2)}) async-start(bf16[8,400,128]{2,1,0:T(8,128)(2,1)} %shard_map.91.after_ref), calls=%async_computation | async-start | bytes 1638400 | tf_op jit(solution)/shard_map/all_to_all | solution.py:601
  10.0 2.2 %shard_map.93.rest_0_ = bf16[9,256,128]{2,1,0:T(8,128)(2,1)} custom-call(bf16[8,256,256]{2,1,0:T(8,128)(2,1)} %prefix_hbm.1, bf16[8,128]{1,0:T(8,128)(2,1)} %bitcast.18, bf16[8,400,128]{2,1,0:T(8,128)(2,1)} %shard_map.91.after_ref), custom_call_target="tpu_custom_call" | custom-call | tf_op jit(solution)/shard_map/pallas_call | solution.py:603
  12.3 1.6 %collective-permute-start = (bf16[9,256,128]{2,1,0:T(8,128)(2,1)}, bf16[9,256,128]{2,1,0:T(8,128)(2,1)S(1)}, u32[]{:S(2)}, u32[]{:S(2)}) collective-permute-start(bf16[9,256,128]{2,1,0:T(8,128)(2,1)} %shard_map.93.rest_0_), channel_id=1, source_target_pairs={{0,16},{2,18},{16,0},{18,2},{1,17},{3,19},{17,1},{19,3},{4,20},{6,... | collective-permute-start | bytes 1769480 | tf_op jit(solution)/shard_map/ppermute | solution.py:548
  13.8 2.0 %collective-permute-start.1 = (bf16[9,256,128]{2,1,0:T(8,128)(2,1)}, bf16[9,256,128]{2,1,0:T(8,128)(2,1)S(1)}, u32[]{:S(2)}, u32[]{:S(2)}) collective-permute-start(bf16[9,256,128]{2,1,0:T(8,128)(2,1)} %shard_map.93.rest_0_), channel_id=1, source_target_pairs={{0,2},{2,0},{16,18},{18,16},{1,3},{3,1},{17,19},{19,17},{4,6},{6,4... | collective-permute-start | bytes 1769480 | tf_op jit(solution)/shard_map/ppermute | solution.py:548
  15.9 8.3 %shard_map.92 = (bf16[512,4096]{1,0:T(8,128)(2,1)}, bf16[512,4096]{1,0:T(8,128)(2,1)}, f32[8,128]{1,0:T(8,128)S(1)}) custom-call(bf16[1024,4096]{1,0:T(8,128)(2,1)} %table_hbm.1, bf16[32,128]{1,0:T(8,128)(2,1)} %bitcast.16, bf16[8,400,128]{2,1,0:T(8,128)(2,1)} %shard_map.91.after_ref), custom_call_target="tpu_custom_call" | custom-call | flops 4194304 | bytes 1048576 | tf_op jit(solution)/shard_map/pallas_call | solution.py:621
  24.2 0.1 pad_add_fusion.place_ref
  24.2 3.1 %collective-permute-done.refs_0_ = bf16[9,256,128]{2,1,0:T(8,128)(2,1)S(1)} collective-permute-done((bf16[9,256,128]{2,1,0:T(8,128)(2,1)}, bf16[9,256,128]{2,1,0:T(8,128)(2,1)S(1)}, u32[]{:S(2)}, u32[]{:S(2)}) %collective-permute-start) | collective-permute-done | bytes 589856 | tf_op jit(solution)/shard_map/ppermute | solution.py:548
  27.3 1.7 %collective-permute-start.3 = (bf16[9,256,128]{2,1,0:T(8,128)(2,1)S(1)}, bf16[9,256,128]{2,1,0:T(8,128)(2,1)S(1)}, u32[]{:S(2)}, u32[]{:S(2)}) collective-permute-start(bf16[9,256,128]{2,1,0:T(8,128)(2,1)S(1)} %shard_map.94.after_ref.rest_2_), channel_id=1, source_target_pairs={{0,2},{2,0},{16,18},{18,16},{1,3},{3,1},{17,19},{19,17},{4,6},{6,4... | collective-permute-start | bytes 1769480 | tf_op jit(solution)/shard_map/ppermute | solution.py:548
  29.1 1.9 %all-to-all-done.w_ref = bf16[8,400,128]{2,1,0:T(8,128)(2,1)S(1)} async-done(((bf16[8,400,128]{2,1,0:T(8,128)(2,1)}), bf16[8,400,128]{2,1,0:T(8,128)(2,1)S(1)}, u32[]{:S(2)}, u32[]{:S(2)}) %all-to-all-start) | async-done | bytes 819232 | tf_op jit(solution)/shard_map/all_to_all | solution.py:601
  30.9 2.2 %copy-done.3 = bf16[512,4096]{1,0:T(8,128)(2,1)S(1)} copy-done((bf16[512,4096]{1,0:T(8,128)(2,1)S(1)}, bf16[512,4096]{1,0:T(8,128)(2,1)}, u32[]{:S(2)}) %copy-start.3) | copy-done | bytes 4194328
  33.1 1.9 %shard_map.95 = (bf16[544,128]{1,0:T(8,128)(2,1)S(1)}, f32[2,1024]{1,0:T(2,128)S(1)}, f32[16,128]{1,0:T(8,128)S(1)}, bf16[8,104,512]{2,1,0:T(8,128)(2,1)S(1)}) custom-call(s32[4]{0:T(128)S(1)} %pad_add_fusion.place_ref, bf16[8,400,128]{2,1,0:T(8,128)(2,1)S(1)} %all-to-all-done.w_ref, bf16[512,4096]{1,0:T(8,128)(2,1)S(1)} %copy-done.3, ...), custom_call_target="tpu_custom_call" | custom-call | flops 4294967296 | bytes 4194304 | tf_op jit(solution)/shard_map/pallas_call | solution.py:530
  35.1 0.0 collective-permute-done.1.after_ref.rest_1_
  35.1 0.3 copy-done.2
  35.3 1.8 %shard_map.96 = (bf16[544,128]{1,0:T(8,128)(2,1)S(1)}, f32[2,1024]{1,0:T(2,128)S(1)}) custom-call(s32[4]{0:T(128)S(1)} %pad_add_fusion.place_ref, bf16[8,104,512]{2,1,0:T(8,128)(2,1)S(1)} %get-tuple-element.19.w_ref, bf16[512,4096]{1,0:T(8,128)(2,1)S(1)} %copy-done.2, f32[4,32,2]{2,1,0:T(8,128)S(1)} %copy-done.4, ...), custom_call_target="tpu_custom_call", output_to_operand_aliasing={{0}: (5, {}), {1}: (6, {})} | custom-call | flops 4294967296 | bytes 4194304 | tf_op jit(solution)/shard_map/pallas_call | solution.py:530
  37.1 3.4 %collective-permute-start.6 = (bf16[544,128]{1,0:T(8,128)(2,1)S(1)}, bf16[544,128]{1,0:T(8,128)(2,1)S(1)}, u32[]{:S(2)}, u32[]{:S(2)}) collective-permute-start(bf16[544,128]{1,0:T(8,128)(2,1)S(1)} %get-tuple-element.27.rest_4_), channel_id=1, source_target_pairs={{0,12},{4,8},{8,4},{12,0},{1,13},{5,9},{9,5},{13,1},{2,14},{6,10},... | collective-permute-start | bytes 417800 | tf_op jit(solution)/shard_map/ppermute | solution.py:548
  40.5 1.1 %collective-permute-start.4 = (bf16[544,128]{1,0:T(8,128)(2,1)S(1)}, bf16[544,128]{1,0:T(8,128)(2,1)S(1)}, u32[]{:S(2)}, u32[]{:S(2)}) collective-permute-start(bf16[544,128]{1,0:T(8,128)(2,1)S(1)} %get-tuple-element.27.rest_4_), channel_id=1, source_target_pairs={{0,4},{4,0},{8,12},{12,8},{1,5},{5,1},{9,13},{13,9},{2,6},{6,2},{1... | collective-permute-start | bytes 417800 | tf_op jit(solution)/shard_map/ppermute | solution.py:548
  41.6 1.5 %collective-permute-start.2 = (f32[16,128]{1,0:T(8,128)S(1)}, f32[16,128]{1,0:T(8,128)S(1)}, u32[]{:S(2)}, u32[]{:S(2)}) collective-permute-start(f32[16,128]{1,0:T(8,128)S(1)} %get-tuple-element.24.own_ref), channel_id=1, source_target_pairs={{0,16},{2,18},{16,0},{18,2},{1,17},{3,19},{17,1},{19,3},{4,20},{6,... | collective-permute-start | bytes 24584 | tf_op jit(solution)/shard_map/ppermute | solution.py:548
  43.1 2.1 %collective-permute-done.2.other_ref = f32[16,128]{1,0:T(8,128)S(1)} collective-permute-done((f32[16,128]{1,0:T(8,128)S(1)}, f32[16,128]{1,0:T(8,128)S(1)}, u32[]{:S(2)}, u32[]{:S(2)}) %collective-permute-start.2) | collective-permute-done | bytes 8224 | tf_op jit(solution)/shard_map/ppermute | solution.py:548
  45.2 4.9 %shard_map.97 = (bf16[8,1024,512]{2,1,0:T(8,128)(2,1)S(1)}, f32[3,8,256,256]{3,2,1,0:T(8,128)S(1)}, s32[1,512]{1,0:T(1,128)S(1)}) custom-call(s32[4]{0:T(128)S(1)} %pad_add_fusion.place_ref, s32[1,512]{1,0:T(1,128)S(1)} %bitcast.14, f32[16,128]{1,0:T(8,128)S(1)} %get-tuple-element.24.own_ref, f32[16,128]{1,0:T(8,128)S(1)} %collective-permute-done.2.other_ref, ...), custom_call_target="tpu_custom_call" | custom-call | flops 1000000000 | bytes 1000000 | tf_op jit(solution)/shard_map/pallas_call | solution.py:530
  50.1 0.3 collective-permute-done.5.rest_6_
  50.5 7.2 %shard_map.98 = bf16[2,16,16,128]{3,2,1,0:T(8,128)(2,1)S(1)} custom-call(s32[4]{0:T(128)S(1)} %pad_add_fusion.place_ref, f32[2,1024]{1,0:T(2,128)S(1)} %get-tuple-element.23.vo_ref, f32[16,128]{1,0:T(8,128)S(1)} %get-tuple-element.24.own_ref, f32[16,128]{1,0:T(8,128)S(1)} %collective-permute-done.2.other_ref, ...), custom_call_target="tpu_custom_call" | custom-call | tf_op jit(solution)/shard_map/pallas_call | solution.py:530
  57.7 12.8 %all_to_all.10 = bf16[32,16,128]{2,1,0:T(8,128)(2,1)S(1)} all-to-all(bf16[32,16,128]{2,1,0:T(8,128)(2,1)S(1)} %bitcast.11), channel_id=1, replica_groups=mesh['groups'=2,'line'=4,'pair'=2,'tensor'=2] {'groups','line','pair','t..., dimensions={0} | all-to-all | bytes 262144 | tf_op jit(solution)/shard_map/all_to_all | solution.py:698
  70.6 1.1 %shard_map.99 = f32[1,512]{1,0:T(1,128)} custom-call(bf16[2,4,4,16,128]{4,3,2,1,0:T(8,128)(2,1)S(1)} %bitcast.12, s32[1,512]{1,0:T(1,128)S(1)} %bitcast.15, s32[1,512]{1,0:T(1,128)S(1)} %get-tuple-element.28.slot_ref), custom_call_target="tpu_custom_call" | custom-call | tf_op jit(solution)/shard_map/pallas_call | solution.py:706
  (13 shorter events, 0.0 us)
Async XLA Ops:
  2.8 28.2 %all-to-all-start = ((bf16[8,400,128]{2,1,0:T(8,128)(2,1)}), bf16[8,400,128]{2,1,0:T(8,128)(2,1)S(1)}, u32[]{:S(2)}, u32[]{:S(2)}) async-start(bf16[8,400,128]{2,1,0:T(8,128)(2,1)} %shard_map.91.after_ref), calls=%async_computation | async-start | bytes 1638400 | tf_op jit(solution)/shard_map/all_to_all | solution.py:601
  10.0 20.9 %copy-start.4 = (f32[4,32,2]{2,1,0:T(8,128)S(1)}, f32[4,32,2]{2,1,0:T(8,128)}, u32[]{:S(2)}) copy-start(f32[4,32,2]{2,1,0:T(8,128)} %constant.17.clone.turn_ref) | copy-start | bytes 3076
  12.3 15.1 %collective-permute-start = (bf16[9,256,128]{2,1,0:T(8,128)(2,1)}, bf16[9,256,128]{2,1,0:T(8,128)(2,1)S(1)}, u32[]{:S(2)}, u32[]{:S(2)}) collective-permute-start(bf16[9,256,128]{2,1,0:T(8,128)(2,1)} %shard_map.93.rest_0_), channel_id=1, source_target_pairs={{0,16},{2,18},{16,0},{18,2},{1,17},{3,19},{17,1},{19,3},{4,20},{6,... | collective-permute-start | bytes 1769480 | tf_op jit(solution)/shard_map/ppermute | solution.py:548
  13.8 21.2 %collective-permute-start.1 = (bf16[9,256,128]{2,1,0:T(8,128)(2,1)}, bf16[9,256,128]{2,1,0:T(8,128)(2,1)S(1)}, u32[]{:S(2)}, u32[]{:S(2)}) collective-permute-start(bf16[9,256,128]{2,1,0:T(8,128)(2,1)} %shard_map.93.rest_0_), channel_id=1, source_target_pairs={{0,2},{2,0},{16,18},{18,16},{1,3},{3,1},{17,19},{19,17},{4,6},{6,4... | collective-permute-start | bytes 1769480 | tf_op jit(solution)/shard_map/ppermute | solution.py:548
  27.3 22.8 %collective-permute-start.3 = (bf16[9,256,128]{2,1,0:T(8,128)(2,1)S(1)}, bf16[9,256,128]{2,1,0:T(8,128)(2,1)S(1)}, u32[]{:S(2)}, u32[]{:S(2)}) collective-permute-start(bf16[9,256,128]{2,1,0:T(8,128)(2,1)S(1)} %shard_map.94.after_ref.rest_2_), channel_id=1, source_target_pairs={{0,2},{2,0},{16,18},{18,16},{1,3},{3,1},{17,19},{19,17},{4,6},{6,4... | collective-permute-start | bytes 1769480 | tf_op jit(solution)/shard_map/ppermute | solution.py:548
  30.9 2.2 %copy-start.3 = (bf16[512,4096]{1,0:T(8,128)(2,1)S(1)}, bf16[512,4096]{1,0:T(8,128)(2,1)}, u32[]{:S(2)}) copy-start(bf16[512,4096]{1,0:T(8,128)(2,1)} %get-tuple-element.17.normed_ref) | copy-start | bytes 12582916
  33.1 2.2 %copy-start.2 = (bf16[512,4096]{1,0:T(8,128)(2,1)S(1)}, bf16[512,4096]{1,0:T(8,128)(2,1)}, u32[]{:S(2)}) copy-start(bf16[512,4096]{1,0:T(8,128)(2,1)} %get-tuple-element.20.normed_ref) | copy-start | bytes 12582916
  35.3 9.9 %copy-start = (bf16[9,256,128]{2,1,0:T(8,128)(2,1)S(1)}, bf16[9,256,128]{2,1,0:T(8,128)(2,1)}, u32[]{:S(2)}) copy-start(bf16[9,256,128]{2,1,0:T(8,128)(2,1)} %shard_map.93.rest_0_) | copy-start | bytes 1769476
  35.3 9.9 %copy-start.1 = (s32[512,1]{0,1:T(1,128)S(1)}, s32[512,1]{0,1:T(1,128)}, u32[]{:S(2)}) copy-start(s32[512,1]{0,1:T(1,128)} %param.11) | copy-start | bytes 6148
  37.1 13.0 %collective-permute-start.6 = (bf16[544,128]{1,0:T(8,128)(2,1)S(1)}, bf16[544,128]{1,0:T(8,128)(2,1)S(1)}, u32[]{:S(2)}, u32[]{:S(2)}) collective-permute-start(bf16[544,128]{1,0:T(8,128)(2,1)S(1)} %get-tuple-element.27.rest_4_), channel_id=1, source_target_pairs={{0,12},{4,8},{8,4},{12,0},{1,13},{5,9},{9,5},{13,1},{2,14},{6,10},... | collective-permute-start | bytes 417800 | tf_op jit(solution)/shard_map/ppermute | solution.py:548
  40.5 10.0 %collective-permute-start.5 = (bf16[544,128]{1,0:T(8,128)(2,1)S(1)}, bf16[544,128]{1,0:T(8,128)(2,1)S(1)}, u32[]{:S(2)}, u32[]{:S(2)}) collective-permute-start(bf16[544,128]{1,0:T(8,128)(2,1)S(1)} %get-tuple-element.27.rest_4_), channel_id=1, source_target_pairs={{0,8},{4,12},{8,0},{12,4},{1,9},{5,13},{9,1},{13,5},{2,10},{6,14},... | collective-permute-start | bytes 417800 | tf_op jit(solution)/shard_map/ppermute | solution.py:548
  40.5 10.0 %collective-permute-start.4 = (bf16[544,128]{1,0:T(8,128)(2,1)S(1)}, bf16[544,128]{1,0:T(8,128)(2,1)S(1)}, u32[]{:S(2)}, u32[]{:S(2)}) collective-permute-start(bf16[544,128]{1,0:T(8,128)(2,1)S(1)} %get-tuple-element.27.rest_4_), channel_id=1, source_target_pairs={{0,4},{4,0},{8,12},{12,8},{1,5},{5,1},{9,13},{13,9},{2,6},{6,2},{1... | collective-permute-start | bytes 417800 | tf_op jit(solution)/shard_map/ppermute | solution.py:548
  41.6 3.7 %collective-permute-start.2 = (f32[16,128]{1,0:T(8,128)S(1)}, f32[16,128]{1,0:T(8,128)S(1)}, u32[]{:S(2)}, u32[]{:S(2)}) collective-permute-start(f32[16,128]{1,0:T(8,128)S(1)} %get-tuple-element.24.own_ref), channel_id=1, source_target_pairs={{0,16},{2,18},{16,0},{18,2},{1,17},{3,19},{17,1},{19,3},{4,20},{6,... | collective-permute-start | bytes 24584 | tf_op jit(solution)/shard_map/ppermute | solution.py:548

commit v25 on v23

--- a/solution.py
+++ b/solution.py
@@ -70,7 +70,7 @@
         pltpu.make_async_copy(wq_hbm.at[:, columns_here], wq, sems.at[3]),
         pltpu.make_async_copy(wkv_hbm, wkv, sems.at[4]),
     )
-    for copy in copies[::-1]:
+    for copy in copies:
         copy.start()
     for copy in copies[:3]:
         copy.wait()
@@ -316,7 +316,7 @@
     return pl.pallas_call(
         lambda *refs: None,
         out_shape=shape(x.shape, x.dtype),
-        in_specs=[untouched()] + [pl.BlockSpec(memory_space=pltpu.VMEM)] * len(others),
+        in_specs=[untouched()] * (1 + len(others)),
         out_specs=untouched(),
         input_output_aliases={0: 0},
         compiler_params=limits(1),
@@ -619,7 +619,7 @@
     diagonal = swap(across, slab_axes, plan.slab, 1)
     full = shape((plan.peers, plan.rows, depth), BF16) if plan.tight else shape(flat.shape, BF16)
     filled, listed = (), None
-    for step, after in enumerate((across, beside)):
+    for step, after in enumerate((across, across)):
         made = local_call(
             functools.partial(project, plan, step * moves // 2, step == 0),
             place,
@@ -636,6 +636,7 @@
         if step == 0:
             listed, flat = made[2:]
     queries, own_values = filled
+    queries = tied(queries, beside)
     other = swap(listed, slab_axes, plan.slab, pair)
     if plan.direct:
         queries = [queries] + [swap(queries, "line", line, step) for step in range(1, line)]

time: 72.1 us -> 70.8 us (0.982)
  blocking collectives: 12.8 us -> 11.8 us
    all_to_all x1, blocking collectives: 12.8 us -> 11.8 us  [per_device(): lax.all_to_all(parts.reshape(groups * back, plan.share, plan.slots), ('gr...]
where the time goes in v25:
time: 70.8 us; the launch traced here: 70.4 us
  Pallas kernels  30 us (42%)
  starting transfers between devices  18.6 us (26%)
  blocking collectives  11.8 us (17%)
  waiting for transfers between devices  7.45 us (11%)
  local copies, waits for them, and re-layouts  2.46 us (3%)
    pallas_call x5, Pallas kernels, local_call(): pl.pallas_call(kernel, out_shape=outs, in_specs=[pl.BlockSpec(memory_spac...  18.4 us
    all_to_all x1, blocking collectives, per_device(): lax.all_to_all(parts.reshape(groups * back, plan.share, plan.slots), ('gr...  11.8 us
    ppermute x7, starting transfers between devices, swap(): return lax.ppermute(x, names, [(at, at ^ step) for at in range(size)])  11.3 us
    pallas_call x1, Pallas kernels, per_device(): pl.pallas_call(normalize, out_shape=[*[shape((moves // 2, width), BF16)]...  8.3 us
    all_to_all x1, starting transfers between devices, per_device(): lax.all_to_all(packed, ('line', 'pair'), split_axis=0, concat_axis=0, til...  7.26 us
    ppermute x7, waiting for transfers between devices, swap(): return lax.ppermute(x, names, [(at, at ^ step) for at in range(size)])  5.56 us
    unnamed x10, local copies, waits for them, and re-layouts  2.46 us
    pallas_call x1, Pallas kernels, per_device(): pl.pallas_call(functools.partial(pack_prefix, plan), out_shape=shape((boa...  2.21 us
  transfers between devices with their start and end apart: 8, of which 4 were waited for; matrix products, arithmetic and copies ran while one was open for 0% of the time, Pallas kernels for 27%

profile of v25, /device:TPU:0, one launch (start us, length us, event | category | flops | bytes accessed | tf_op | source)
XLA Modules:
  0.0 70.4 jit_solution(16993305492212496694)
XLA Ops:
  0.0 2.6 %shard_map.91.after_ref = bf16[8,400,128]{2,1,0:T(8,128)(2,1)} custom-call(s32[1]{0:T(128)} %bitcast.place_ref, bf16[512,1024]{1,0:T(8,128)(2,1)} %wq_hbm.1, bf16[512,256]{1,0:T(8,128)(2,1)} %wkv_hbm.1, bf16[8,128]{1,0:T(8,128)(2,1)} %bitcast.17, s32[1,512]{1,0:T(1,128)} %bitcast.13, s32[1,512]{1,0:T(1,128)} %bitcast.19), custom_call_target="tpu_custom_call" | custom-call | tf_op jit(solution)/shard_map/pallas_call | solution.py:511
  2.6 7.3 %all-to-all-start = ((bf16[8,400,128]{2,1,0:T(8,128)(2,1)}), bf16[8,400,128]{2,1,0:T(8,128)(2,1)S(1)}, u32[]{:S(2)}, u32[]{:S(2)}) async-start(bf16[8,400,128]{2,1,0:T(8,128)(2,1)} %shard_map.91.after_ref), calls=%async_computation | async-start | bytes 1638400 | tf_op jit(solution)/shard_map/all_to_all | solution.py:578
  9.9 2.2 %shard_map.93.rest_0_ = bf16[9,256,128]{2,1,0:T(8,128)(2,1)} custom-call(bf16[8,256,256]{2,1,0:T(8,128)(2,1)} %prefix_hbm.1, bf16[8,128]{1,0:T(8,128)(2,1)} %bitcast.18, bf16[8,400,128]{2,1,0:T(8,128)(2,1)} %shard_map.91.after_ref), custom_call_target="tpu_custom_call" | custom-call | tf_op jit(solution)/shard_map/pallas_call | solution.py:580
  12.1 1.6 %collective-permute-start = (bf16[9,256,128]{2,1,0:T(8,128)(2,1)}, bf16[9,256,128]{2,1,0:T(8,128)(2,1)S(1)}, u32[]{:S(2)}, u32[]{:S(2)}) collective-permute-start(bf16[9,256,128]{2,1,0:T(8,128)(2,1)} %shard_map.93.rest_0_), channel_id=1, source_target_pairs={{0,16},{2,18},{16,0},{18,2},{1,17},{3,19},{17,1},{19,3},{4,20},{6,... | collective-permute-start | bytes 1769480 | tf_op jit(solution)/shard_map/ppermute | solution.py:529
  13.7 2.0 %collective-permute-start.2 = (bf16[9,256,128]{2,1,0:T(8,128)(2,1)}, bf16[9,256,128]{2,1,0:T(8,128)(2,1)S(1)}, u32[]{:S(2)}, u32[]{:S(2)}) collective-permute-start(bf16[9,256,128]{2,1,0:T(8,128)(2,1)} %shard_map.93.rest_0_), channel_id=1, source_target_pairs={{0,2},{2,0},{16,18},{18,16},{1,3},{3,1},{17,19},{19,17},{4,6},{6,4... | collective-permute-start | bytes 1769480 | tf_op jit(solution)/shard_map/ppermute | solution.py:529
  15.7 8.3 %shard_map.92 = (bf16[512,4096]{1,0:T(8,128)(2,1)}, bf16[512,4096]{1,0:T(8,128)(2,1)}, f32[8,128]{1,0:T(8,128)S(1)}) custom-call(bf16[1024,4096]{1,0:T(8,128)(2,1)} %table_hbm.1, bf16[32,128]{1,0:T(8,128)(2,1)} %bitcast.16, bf16[8,400,128]{2,1,0:T(8,128)(2,1)} %shard_map.91.after_ref), custom_call_target="tpu_custom_call" | custom-call | flops 4194304 | bytes 1048576 | tf_op jit(solution)/shard_map/pallas_call | solution.py:598
  24.0 0.1 pad_add_fusion.place_ref
  24.1 3.1 %collective-permute-done.refs_0_ = bf16[9,256,128]{2,1,0:T(8,128)(2,1)S(1)} collective-permute-done((bf16[9,256,128]{2,1,0:T(8,128)(2,1)}, bf16[9,256,128]{2,1,0:T(8,128)(2,1)S(1)}, u32[]{:S(2)}, u32[]{:S(2)}) %collective-permute-start) | collective-permute-done | bytes 589856 | tf_op jit(solution)/shard_map/ppermute | solution.py:529
  27.2 1.7 %collective-permute-start.3 = (bf16[9,256,128]{2,1,0:T(8,128)(2,1)S(1)}, bf16[9,256,128]{2,1,0:T(8,128)(2,1)S(1)}, u32[]{:S(2)}, u32[]{:S(2)}) collective-permute-start(bf16[9,256,128]{2,1,0:T(8,128)(2,1)S(1)} %shard_map.94.after_ref.rest_2_), channel_id=1, source_target_pairs={{0,2},{2,0},{16,18},{18,16},{1,3},{3,1},{17,19},{19,17},{4,6},{6,4... | collective-permute-start | bytes 1769480 | tf_op jit(solution)/shard_map/ppermute | solution.py:529
  28.9 1.9 %all-to-all-done.w_ref = bf16[8,400,128]{2,1,0:T(8,128)(2,1)S(1)} async-done(((bf16[8,400,128]{2,1,0:T(8,128)(2,1)}), bf16[8,400,128]{2,1,0:T(8,128)(2,1)S(1)}, u32[]{:S(2)}, u32[]{:S(2)}) %all-to-all-start) | async-done | bytes 819232 | tf_op jit(solution)/shard_map/all_to_all | solution.py:578
  30.8 2.2 %copy-done.3 = bf16[512,4096]{1,0:T(8,128)(2,1)S(1)} copy-done((bf16[512,4096]{1,0:T(8,128)(2,1)S(1)}, bf16[512,4096]{1,0:T(8,128)(2,1)}, u32[]{:S(2)}) %copy-start.3) | copy-done | bytes 4194328
  33.0 1.9 %shard_map.95 = (bf16[544,128]{1,0:T(8,128)(2,1)S(1)}, f32[2,1024]{1,0:T(2,128)S(1)}, f32[16,128]{1,0:T(8,128)S(1)}, bf16[8,104,512]{2,1,0:T(8,128)(2,1)S(1)}) custom-call(s32[4]{0:T(128)S(1)} %pad_add_fusion.place_ref, bf16[8,400,128]{2,1,0:T(8,128)(2,1)S(1)} %all-to-all-done.w_ref, bf16[512,4096]{1,0:T(8,128)(2,1)S(1)} %copy-done.3, ...), custom_call_target="tpu_custom_call" | custom-call | flops 4294967296 | bytes 4194304 | tf_op jit(solution)/shard_map/pallas_call | solution.py:511
  34.9 0.3 copy-done.2
  35.2 1.8 %shard_map.96 = (bf16[544,128]{1,0:T(8,128)(2,1)S(1)}, f32[2,1024]{1,0:T(2,128)S(1)}) custom-call(s32[4]{0:T(128)S(1)} %pad_add_fusion.place_ref, bf16[8,104,512]{2,1,0:T(8,128)(2,1)S(1)} %get-tuple-element.19.w_ref, bf16[512,4096]{1,0:T(8,128)(2,1)S(1)} %copy-done.2, f32[4,32,2]{2,1,0:T(8,128)S(1)} %copy-done.4, ...), custom_call_target="tpu_custom_call", output_to_operand_aliasing={{0}: (5, {}), {1}: (6, {})} | custom-call | flops 4294967296 | bytes 4194304 | tf_op jit(solution)/shard_map/pallas_call | solution.py:511
  37.0 1.5 %collective-permute-start.6 = (bf16[544,128]{1,0:T(8,128)(2,1)S(1)}, bf16[544,128]{1,0:T(8,128)(2,1)S(1)}, u32[]{:S(2)}, u32[]{:S(2)}) collective-permute-start(bf16[544,128]{1,0:T(8,128)(2,1)S(1)} %shard_map.98.rest_4_), channel_id=1, source_target_pairs={{0,12},{4,8},{8,4},{12,0},{1,13},{5,9},{9,5},{13,1},{2,14},{6,10},... | collective-permute-start | bytes 417800 | tf_op jit(solution)/shard_map/ppermute | solution.py:529
  38.5 0.3 collective-permute-start.5
  38.8 2.7 %collective-permute-start.4 = (bf16[544,128]{1,0:T(8,128)(2,1)S(1)}, bf16[544,128]{1,0:T(8,128)(2,1)S(1)}, u32[]{:S(2)}, u32[]{:S(2)}) collective-permute-start(bf16[544,128]{1,0:T(8,128)(2,1)S(1)} %shard_map.98.rest_4_), channel_id=1, source_target_pairs={{0,4},{4,0},{8,12},{12,8},{1,5},{5,1},{9,13},{13,9},{2,6},{6,2},{1... | collective-permute-start | bytes 417800 | tf_op jit(solution)/shard_map/ppermute | solution.py:529
  41.5 1.5 %collective-permute-start.1 = (f32[16,128]{1,0:T(8,128)S(1)}, f32[16,128]{1,0:T(8,128)S(1)}, u32[]{:S(2)}, u32[]{:S(2)}) collective-permute-start(f32[16,128]{1,0:T(8,128)S(1)} %get-tuple-element.24.own_ref), channel_id=1, source_target_pairs={{0,16},{2,18},{16,0},{18,2},{1,17},{3,19},{17,1},{19,3},{4,20},{6,... | collective-permute-start | bytes 24584 | tf_op jit(solution)/shard_map/ppermute | solution.py:529
  43.0 2.1 %collective-permute-done.1.other_ref = f32[16,128]{1,0:T(8,128)S(1)} collective-permute-done((f32[16,128]{1,0:T(8,128)S(1)}, f32[16,128]{1,0:T(8,128)S(1)}, u32[]{:S(2)}, u32[]{:S(2)}) %collective-permute-start.1) | collective-permute-done | bytes 8224 | tf_op jit(solution)/shard_map/ppermute | solution.py:529
  45.1 4.9 %shard_map.97 = (bf16[8,1024,512]{2,1,0:T(8,128)(2,1)S(1)}, f32[3,8,256,256]{3,2,1,0:T(8,128)S(1)}, s32[1,512]{1,0:T(1,128)S(1)}) custom-call(s32[4]{0:T(128)S(1)} %pad_add_fusion.place_ref, s32[1,512]{1,0:T(1,128)S(1)} %bitcast.14, f32[16,128]{1,0:T(8,128)S(1)} %get-tuple-element.24.own_ref, f32[16,128]{1,0:T(8,128)S(1)} %collective-permute-done.1.other_ref, ...), custom_call_target="tpu_custom_call" | custom-call | flops 1000000000 | bytes 1000000 | tf_op jit(solution)/shard_map/pallas_call | solution.py:511
  50.0 0.3 collective-permute-done.5.rest_6_
  50.4 7.2 %shard_map.99 = bf16[2,16,16,128]{3,2,1,0:T(8,128)(2,1)S(1)} custom-call(s32[4]{0:T(128)S(1)} %pad_add_fusion.place_ref, f32[2,1024]{1,0:T(2,128)S(1)} %get-tuple-element.23.vo_ref, f32[16,128]{1,0:T(8,128)S(1)} %get-tuple-element.24.own_ref, f32[16,128]{1,0:T(8,128)S(1)} %collective-permute-done.1.other_ref, ...), custom_call_target="tpu_custom_call" | custom-call | tf_op jit(solution)/shard_map/pallas_call | solution.py:511
  57.6 11.8 %all_to_all.10 = bf16[32,16,128]{2,1,0:T(8,128)(2,1)S(1)} all-to-all(bf16[32,16,128]{2,1,0:T(8,128)(2,1)S(1)} %bitcast.11), channel_id=1, replica_groups=mesh['groups'=2,'line'=4,'pair'=2,'tensor'=2] {'groups','line','pair','t..., dimensions={0} | all-to-all | bytes 262144 | tf_op jit(solution)/shard_map/all_to_all | solution.py:676
  69.4 1.1 %shard_map.100 = f32[1,512]{1,0:T(1,128)} custom-call(bf16[2,4,4,16,128]{4,3,2,1,0:T(8,128)(2,1)S(1)} %bitcast.12, s32[1,512]{1,0:T(1,128)S(1)} %bitcast.15, s32[1,512]{1,0:T(1,128)S(1)} %get-tuple-element.28.slot_ref), custom_call_target="tpu_custom_call" | custom-call | tf_op jit(solution)/shard_map/pallas_call | solution.py:684
  (14 shorter events, 0.0 us)
Async XLA Ops:
  2.6 28.2 %all-to-all-start = ((bf16[8,400,128]{2,1,0:T(8,128)(2,1)}), bf16[8,400,128]{2,1,0:T(8,128)(2,1)S(1)}, u32[]{:S(2)}, u32[]{:S(2)}) async-start(bf16[8,400,128]{2,1,0:T(8,128)(2,1)} %shard_map.91.after_ref), calls=%async_computation | async-start | bytes 1638400 | tf_op jit(solution)/shard_map/all_to_all | solution.py:578
  9.9 20.9 %copy-start.4 = (f32[4,32,2]{2,1,0:T(8,128)S(1)}, f32[4,32,2]{2,1,0:T(8,128)}, u32[]{:S(2)}) copy-start(f32[4,32,2]{2,1,0:T(8,128)} %constant.17.clone.turn_ref) | copy-start | bytes 3076
  12.1 15.1 %collective-permute-start = (bf16[9,256,128]{2,1,0:T(8,128)(2,1)}, bf16[9,256,128]{2,1,0:T(8,128)(2,1)S(1)}, u32[]{:S(2)}, u32[]{:S(2)}) collective-permute-start(bf16[9,256,128]{2,1,0:T(8,128)(2,1)} %shard_map.93.rest_0_), channel_id=1, source_target_pairs={{0,16},{2,18},{16,0},{18,2},{1,17},{3,19},{17,1},{19,3},{4,20},{6,... | collective-permute-start | bytes 1769480 | tf_op jit(solution)/shard_map/ppermute | solution.py:529
  13.7 23.3 %collective-permute-start.2 = (bf16[9,256,128]{2,1,0:T(8,128)(2,1)}, bf16[9,256,128]{2,1,0:T(8,128)(2,1)S(1)}, u32[]{:S(2)}, u32[]{:S(2)}) collective-permute-start(bf16[9,256,128]{2,1,0:T(8,128)(2,1)} %shard_map.93.rest_0_), channel_id=1, source_target_pairs={{0,2},{2,0},{16,18},{18,16},{1,3},{3,1},{17,19},{19,17},{4,6},{6,4... | collective-permute-start | bytes 1769480 | tf_op jit(solution)/shard_map/ppermute | solution.py:529
  27.2 22.8 %collective-permute-start.3 = (bf16[9,256,128]{2,1,0:T(8,128)(2,1)S(1)}, bf16[9,256,128]{2,1,0:T(8,128)(2,1)S(1)}, u32[]{:S(2)}, u32[]{:S(2)}) collective-permute-start(bf16[9,256,128]{2,1,0:T(8,128)(2,1)S(1)} %shard_map.94.after_ref.rest_2_), channel_id=1, source_target_pairs={{0,2},{2,0},{16,18},{18,16},{1,3},{3,1},{17,19},{19,17},{4,6},{6,4... | collective-permute-start | bytes 1769480 | tf_op jit(solution)/shard_map/ppermute | solution.py:529
  30.8 2.2 %copy-start.3 = (bf16[512,4096]{1,0:T(8,128)(2,1)S(1)}, bf16[512,4096]{1,0:T(8,128)(2,1)}, u32[]{:S(2)}) copy-start(bf16[512,4096]{1,0:T(8,128)(2,1)} %get-tuple-element.17.normed_ref) | copy-start | bytes 12582916
  33.0 2.2 %copy-start.2 = (bf16[512,4096]{1,0:T(8,128)(2,1)S(1)}, bf16[512,4096]{1,0:T(8,128)(2,1)}, u32[]{:S(2)}) copy-start(bf16[512,4096]{1,0:T(8,128)(2,1)} %get-tuple-element.20.normed_ref) | copy-start | bytes 12582916
  35.2 9.9 %copy-start = (bf16[9,256,128]{2,1,0:T(8,128)(2,1)S(1)}, bf16[9,256,128]{2,1,0:T(8,128)(2,1)}, u32[]{:S(2)}) copy-start(bf16[9,256,128]{2,1,0:T(8,128)(2,1)} %shard_map.93.rest_0_) | copy-start | bytes 1769476
  35.2 9.9 %copy-start.1 = (s32[512,1]{0,1:T(1,128)S(1)}, s32[512,1]{0,1:T(1,128)}, u32[]{:S(2)}) copy-start(s32[512,1]{0,1:T(1,128)} %param.11) | copy-start | bytes 6148
  37.0 13.0 %collective-permute-start.6 = (bf16[544,128]{1,0:T(8,128)(2,1)S(1)}, bf16[544,128]{1,0:T(8,128)(2,1)S(1)}, u32[]{:S(2)}, u32[]{:S(2)}) collective-permute-start(bf16[544,128]{1,0:T(8,128)(2,1)S(1)} %shard_map.98.rest_4_), channel_id=1, source_target_pairs={{0,12},{4,8},{8,4},{12,0},{1,13},{5,9},{9,5},{13,1},{2,14},{6,10},... | collective-permute-start | bytes 417800 | tf_op jit(solution)/shard_map/ppermute | solution.py:529
  38.5 11.9 %collective-permute-start.5 = (bf16[544,128]{1,0:T(8,128)(2,1)S(1)}, bf16[544,128]{1,0:T(8,128)(2,1)S(1)}, u32[]{:S(2)}, u32[]{:S(2)}) collective-permute-start(bf16[544,128]{1,0:T(8,128)(2,1)S(1)} %shard_map.98.rest_4_), channel_id=1, source_target_pairs={{0,8},{4,12},{8,0},{12,4},{1,9},{5,13},{9,1},{13,5},{2,10},{6,14},... | collective-permute-start | bytes 417800 | tf_op jit(solution)/shard_map/ppermute | solution.py:529
  38.8 11.6 %collective-permute-start.4 = (bf16[544,128]{1,0:T(8,128)(2,1)S(1)}, bf16[544,128]{1,0:T(8,128)(2,1)S(1)}, u32[]{:S(2)}, u32[]{:S(2)}) collective-permute-start(bf16[544,128]{1,0:T(8,128)(2,1)S(1)} %shard_map.98.rest_4_), channel_id=1, source_target_pairs={{0,4},{4,0},{8,12},{12,8},{1,5},{5,1},{9,13},{13,9},{2,6},{6,2},{1... | collective-permute-start | bytes 417800 | tf_op jit(solution)/shard_map/ppermute | solution.py:529
  41.5 3.7 %collective-permute-start.1 = (f32[16,128]{1,0:T(8,128)S(1)}, f32[16,128]{1,0:T(8,128)S(1)}, u32[]{:S(2)}, u32[]{:S(2)}) collective-permute-start(f32[16,128]{1,0:T(8,128)S(1)} %get-tuple-element.24.own_ref), channel_id=1, source_target_pairs={{0,16},{2,18},{16,0},{18,2},{1,17},{3,19},{17,1},{19,3},{4,20},{6,... | collective-permute-start | bytes 24584 | tf_op jit(solution)/shard_map/ppermute | solution.py:529

commit v26 on v25

--- a/solution.py
+++ b/solution.py
@@ -360,7 +360,7 @@
 
 
 def prepare(plan, place_ref, board_ref, own_ref, other_ref, *rest):
-    *prefix_refs, chosen_ref, fold_ref, slot_ref = rest
+    chosen_ref, slot_ref = rest
     count = board_ref.shape[1]
     board_row = board_ref[...]
     board_col = jnp.broadcast_to(board_row.astype(F32), (8, count)).T[:, 0:1].astype(jnp.int32)
@@ -377,14 +377,12 @@
             row = (own_ref, other_ref)[j // plan.pair][pl.ds(place, 1), :].astype(jnp.int32)
             at = slice(j * plan.slots, (j + 1) * plan.slots)
             chosen_ref[board, :, at] = jnp.where(move_at == row, 1.0, 0.0).astype(BF16)
-        for j, prefix_ref in enumerate(prefix_refs):
-            fold_ref[j, board] = fold_columns(plan, here, prefix_ref[boards], board, boards, plan.heads)
         return carry
 
     lax.fori_loop(0, boards, step, 0)
 
 
-def attend(plan, place_ref, vo_ref, own_ref, other_ref, chosen_ref, fold_ref, *rest):
+def attend(plan, place_ref, vo_ref, own_ref, other_ref, chosen_ref, *rest):
     prefix_refs, rest = rest[: plan.slab], rest[plan.slab :]
     *q_refs, out_ref, table, extra, scores, taken_even, taken_odd = rest
     here = place_ref[SLAB]
@@ -440,10 +438,7 @@
             x = taken[:, j * slots : (j + 1) * slots]
             q = jnp.concatenate([x[h * HD : (h + 1) * HD].astype(BF16) for h in range(mine)], axis=1)
             logits = matmul(prefix_refs[j][board], q)
-            if j < plan.slab - 1:
-                fold = fold_ref[j, board]
-            else:
-                fold = fold_columns(plan, here, prefix_refs[j][boards], board, boards, heads)
+            fold = fold_columns(plan, here, prefix_refs[j][boards], board, boards, heads)
             own_logit = per_head(x, query_rows)
             own_value = per_head(x, query_rows + 2 * mine)
             peak = jnp.maximum(jnp.max(logits, axis=0, keepdims=True), own_logit)
@@ -646,13 +641,12 @@
 
     query_rows = plan.mine * HD
     back = plan.peers * lax.axis_size("tensor")
-    chosen, folds, slot_row = local_call(
+    chosen, slot_row = local_call(
         functools.partial(prepare, plan),
         place,
-        (board_row, listed, other, payload, beside, across),
+        (board_row, listed, other),
         (
             shape((boards_here, moves, plan.slab * plan.slots), BF16),
-            shape((plan.slab - 1, boards_here, prefix_len, plan.mine * plan.slots), F32),
             shape((1, row_count), jnp.int32),
         ),
         mib=20,
@@ -662,7 +656,7 @@
     parts = local_call(
         functools.partial(attend, plan),
         place,
-        (own_values, listed, other, chosen, folds, payload, beside, across, diagonal, *queries),
+        (own_values, listed, other, chosen, payload, beside, across, diagonal, *queries),
         shape((groups, back, plan.share, plan.slots), BF16),
         [
             pltpu.VMEM((query_rows + 16, moves), BF16),

time: 70.8 us -> 73 us (1.031)
  blocking collectives: 11.8 us -> 13.8 us
  waiting for transfers between devices: 7.45 us -> 8.93 us
  Pallas kernels: 30 us -> 28.8 us
    all_to_all x1, blocking collectives: 11.8 us -> 13.8 us  [per_device(): lax.all_to_all(parts.reshape(groups * back, plan.share, plan.slots), ('gr...]
    ppermute x7, waiting for transfers between devices: 5.56 us -> 7.02 us  [swap(): return lax.ppermute(x, names, [(at, at ^ step) for at in range(size)])]
    pallas_call x5, Pallas kernels: 18.4 us -> 17.3 us  [local_call(): pl.pallas_call(kernel, out_shape=outs, in_specs=[pl.BlockSpec(memory_spac...]
  transfers between devices with their start and end apart: 8 -> 8, of which waited for: 4 -> 4; matrix products, arithmetic and copies ran while one was open for 0% -> 0% of each run, Pallas kernels for 27% -> 23%
where the time goes in v26:
time: 73 us; the launch traced here: 72.7 us
  Pallas kernels  28.8 us (39%)
  starting transfers between devices  18.6 us (25%)
  blocking collectives  13.8 us (19%)
  waiting for transfers between devices  8.93 us (12%)
  local copies, waits for them, and re-layouts  2.36 us (3%)
    pallas_call x5, Pallas kernels, local_call(): pl.pallas_call(kernel, out_shape=outs, in_specs=[pl.BlockSpec(memory_spac...  17.3 us
    all_to_all x1, blocking collectives, per_device(): lax.all_to_all(parts.reshape(groups * back, plan.share, plan.slots), ('gr...  13.8 us
    ppermute x7, starting transfers between devices, swap(): return lax.ppermute(x, names, [(at, at ^ step) for at in range(size)])  11.3 us
    pallas_call x1, Pallas kernels, per_device(): pl.pallas_call(normalize, out_shape=[*[shape((moves // 2, width), BF16)]...  8.3 us
    all_to_all x1, starting transfers between devices, per_device(): lax.all_to_all(packed, ('line', 'pair'), split_axis=0, concat_axis=0, til...  7.27 us
    ppermute x7, waiting for transfers between devices, swap(): return lax.ppermute(x, names, [(at, at ^ step) for at in range(size)])  7.02 us
    unnamed x10, local copies, waits for them, and re-layouts  2.36 us
    pallas_call x1, Pallas kernels, per_device(): pl.pallas_call(functools.partial(pack_prefix, plan), out_shape=shape((boa...  2.17 us
  transfers between devices with their start and end apart: 8, of which 4 were waited for; matrix products, arithmetic and copies ran while one was open for 0% of the time, Pallas kernels for 23%

profile of v26, /device:TPU:0, one launch (start us, length us, event | category | flops | bytes accessed | tf_op | source)
XLA Modules:
  0.0 72.7 jit_solution(4258317960332684930)
XLA Ops:
  0.0 2.7 %shard_map.91.after_ref = bf16[8,400,128]{2,1,0:T(8,128)(2,1)} custom-call(s32[1]{0:T(128)} %bitcast.place_ref, bf16[512,1024]{1,0:T(8,128)(2,1)} %wq_hbm.1, bf16[512,256]{1,0:T(8,128)(2,1)} %wkv_hbm.1, bf16[8,128]{1,0:T(8,128)(2,1)} %bitcast.17, s32[1,512]{1,0:T(1,128)} %bitcast.13, s32[1,512]{1,0:T(1,128)} %bitcast.19), custom_call_target="tpu_custom_call" | custom-call | tf_op jit(solution)/shard_map/pallas_call | solution.py:506
  2.7 7.3 %all-to-all-start = ((bf16[8,400,128]{2,1,0:T(8,128)(2,1)}), bf16[8,400,128]{2,1,0:T(8,128)(2,1)S(1)}, u32[]{:S(2)}, u32[]{:S(2)}) async-start(bf16[8,400,128]{2,1,0:T(8,128)(2,1)} %shard_map.91.after_ref), calls=%async_computation | async-start | bytes 1638400 | tf_op jit(solution)/shard_map/all_to_all | solution.py:573
  9.9 2.2 %shard_map.93.rest_0_ = bf16[9,256,128]{2,1,0:T(8,128)(2,1)} custom-call(bf16[8,256,256]{2,1,0:T(8,128)(2,1)} %prefix_hbm.1, bf16[8,128]{1,0:T(8,128)(2,1)} %bitcast.18, bf16[8,400,128]{2,1,0:T(8,128)(2,1)} %shard_map.91.after_ref), custom_call_target="tpu_custom_call" | custom-call | tf_op jit(solution)/shard_map/pallas_call | solution.py:575
  12.1 1.6 %collective-permute-start = (bf16[9,256,128]{2,1,0:T(8,128)(2,1)}, bf16[9,256,128]{2,1,0:T(8,128)(2,1)S(1)}, u32[]{:S(2)}, u32[]{:S(2)}) collective-permute-start(bf16[9,256,128]{2,1,0:T(8,128)(2,1)} %shard_map.93.rest_0_), channel_id=1, source_target_pairs={{0,16},{2,18},{16,0},{18,2},{1,17},{3,19},{17,1},{19,3},{4,20},{6,... | collective-permute-start | bytes 1769480 | tf_op jit(solution)/shard_map/ppermute | solution.py:524
  13.7 2.0 %collective-permute-start.2 = (bf16[9,256,128]{2,1,0:T(8,128)(2,1)}, bf16[9,256,128]{2,1,0:T(8,128)(2,1)S(1)}, u32[]{:S(2)}, u32[]{:S(2)}) collective-permute-start(bf16[9,256,128]{2,1,0:T(8,128)(2,1)} %shard_map.93.rest_0_), channel_id=1, source_target_pairs={{0,2},{2,0},{16,18},{18,16},{1,3},{3,1},{17,19},{19,17},{4,6},{6,4... | collective-permute-start | bytes 1769480 | tf_op jit(solution)/shard_map/ppermute | solution.py:524
  15.7 8.3 %shard_map.92 = (bf16[512,4096]{1,0:T(8,128)(2,1)}, bf16[512,4096]{1,0:T(8,128)(2,1)}, f32[8,128]{1,0:T(8,128)S(1)}) custom-call(bf16[1024,4096]{1,0:T(8,128)(2,1)} %table_hbm.1, bf16[32,128]{1,0:T(8,128)(2,1)} %bitcast.16, bf16[8,400,128]{2,1,0:T(8,128)(2,1)} %shard_map.91.after_ref), custom_call_target="tpu_custom_call" | custom-call | flops 4194304 | bytes 1048576 | tf_op jit(solution)/shard_map/pallas_call | solution.py:593
  24.0 0.1 pad_add_fusion.place_ref
  24.1 3.1 %collective-permute-done.refs_0_ = bf16[9,256,128]{2,1,0:T(8,128)(2,1)S(1)} collective-permute-done((bf16[9,256,128]{2,1,0:T(8,128)(2,1)}, bf16[9,256,128]{2,1,0:T(8,128)(2,1)S(1)}, u32[]{:S(2)}, u32[]{:S(2)}) %collective-permute-start) | collective-permute-done | bytes 589856 | tf_op jit(solution)/shard_map/ppermute | solution.py:524
  27.2 1.7 %collective-permute-start.3 = (bf16[9,256,128]{2,1,0:T(8,128)(2,1)S(1)}, bf16[9,256,128]{2,1,0:T(8,128)(2,1)S(1)}, u32[]{:S(2)}, u32[]{:S(2)}) collective-permute-start(bf16[9,256,128]{2,1,0:T(8,128)(2,1)S(1)} %shard_map.94.after_ref.rest_2_), channel_id=1, source_target_pairs={{0,2},{2,0},{16,18},{18,16},{1,3},{3,1},{17,19},{19,17},{4,6},{6,4... | collective-permute-start | bytes 1769480 | tf_op jit(solution)/shard_map/ppermute | solution.py:524
  28.9 1.9 %all-to-all-done.w_ref = bf16[8,400,128]{2,1,0:T(8,128)(2,1)S(1)} async-done(((bf16[8,400,128]{2,1,0:T(8,128)(2,1)}), bf16[8,400,128]{2,1,0:T(8,128)(2,1)S(1)}, u32[]{:S(2)}, u32[]{:S(2)}) %all-to-all-start) | async-done | bytes 819232 | tf_op jit(solution)/shard_map/all_to_all | solution.py:573
  30.8 2.3 %copy-done.3 = bf16[512,4096]{1,0:T(8,128)(2,1)S(1)} copy-done((bf16[512,4096]{1,0:T(8,128)(2,1)S(1)}, bf16[512,4096]{1,0:T(8,128)(2,1)}, u32[]{:S(2)}) %copy-start.3) | copy-done | bytes 4194328
  33.2 1.9 %shard_map.95 = (bf16[544,128]{1,0:T(8,128)(2,1)S(1)}, f32[2,1024]{1,0:T(2,128)S(1)}, f32[16,128]{1,0:T(8,128)S(1)}, bf16[8,104,512]{2,1,0:T(8,128)(2,1)S(1)}) custom-call(s32[4]{0:T(128)S(1)} %pad_add_fusion.place_ref, bf16[8,400,128]{2,1,0:T(8,128)(2,1)S(1)} %all-to-all-done.w_ref, bf16[512,4096]{1,0:T(8,128)(2,1)S(1)} %copy-done.3, ...), custom_call_target="tpu_custom_call" | custom-call | flops 4294967296 | bytes 4194304 | tf_op jit(solution)/shard_map/pallas_call | solution.py:506
  35.1 0.0 copy-start.1
  35.2 1.8 %shard_map.96 = (bf16[544,128]{1,0:T(8,128)(2,1)S(1)}, f32[2,1024]{1,0:T(2,128)S(1)}) custom-call(s32[4]{0:T(128)S(1)} %pad_add_fusion.place_ref, bf16[8,104,512]{2,1,0:T(8,128)(2,1)S(1)} %get-tuple-element.18.w_ref, bf16[512,4096]{1,0:T(8,128)(2,1)S(1)} %copy-done.2, f32[4,32,2]{2,1,0:T(8,128)S(1)} %copy-done.4, ...), custom_call_target="tpu_custom_call", output_to_operand_aliasing={{0}: (5, {}), {1}: (6, {})} | custom-call | flops 4294967296 | bytes 4194304 | tf_op jit(solution)/shard_map/pallas_call | solution.py:506
  37.0 0.3 collective-permute-start.4
  37.3 1.8 %collective-permute-start.5 = (bf16[544,128]{1,0:T(8,128)(2,1)S(1)}, bf16[544,128]{1,0:T(8,128)(2,1)S(1)}, u32[]{:S(2)}, u32[]{:S(2)}) collective-permute-start(bf16[544,128]{1,0:T(8,128)(2,1)S(1)} %shard_map.98.rest_4_), channel_id=1, source_target_pairs={{0,8},{4,12},{8,0},{12,4},{1,9},{5,13},{9,1},{13,5},{2,10},{6,14},... | collective-permute-start | bytes 417800 | tf_op jit(solution)/shard_map/ppermute | solution.py:524
  39.1 2.4 %collective-permute-start.6 = (bf16[544,128]{1,0:T(8,128)(2,1)S(1)}, bf16[544,128]{1,0:T(8,128)(2,1)S(1)}, u32[]{:S(2)}, u32[]{:S(2)}) collective-permute-start(bf16[544,128]{1,0:T(8,128)(2,1)S(1)} %shard_map.98.rest_4_), channel_id=1, source_target_pairs={{0,12},{4,8},{8,4},{12,0},{1,13},{5,9},{9,5},{13,1},{2,14},{6,10},... | collective-permute-start | bytes 417800 | tf_op jit(solution)/shard_map/ppermute | solution.py:524
  41.4 1.5 %collective-permute-start.1 = (f32[16,128]{1,0:T(8,128)S(1)}, f32[16,128]{1,0:T(8,128)S(1)}, u32[]{:S(2)}, u32[]{:S(2)}) collective-permute-start(f32[16,128]{1,0:T(8,128)S(1)} %get-tuple-element.23.own_ref), channel_id=1, source_target_pairs={{0,16},{2,18},{16,0},{18,2},{1,17},{3,19},{17,1},{19,3},{4,20},{6,... | collective-permute-start | bytes 24584 | tf_op jit(solution)/shard_map/ppermute | solution.py:524
  43.0 2.1 %collective-permute-done.1.other_ref = f32[16,128]{1,0:T(8,128)S(1)} collective-permute-done((f32[16,128]{1,0:T(8,128)S(1)}, f32[16,128]{1,0:T(8,128)S(1)}, u32[]{:S(2)}, u32[]{:S(2)}) %collective-permute-start.1) | collective-permute-done | bytes 8224 | tf_op jit(solution)/shard_map/ppermute | solution.py:524
  45.1 2.6 %shard_map.97 = (bf16[8,1024,512]{2,1,0:T(8,128)(2,1)S(1)}, s32[1,512]{1,0:T(1,128)S(1)}) custom-call(s32[4]{0:T(128)S(1)} %pad_add_fusion.place_ref, s32[1,512]{1,0:T(1,128)S(1)} %bitcast.14, f32[16,128]{1,0:T(8,128)S(1)} %get-tuple-element.23.own_ref, f32[16,128]{1,0:T(8,128)S(1)} %collective-permute-done.1.other_ref), custom_call_target="tpu_custom_call" | custom-call | flops 1000000000 | bytes 1000000 | tf_op jit(solution)/shard_map/pallas_call | solution.py:506
  47.8 1.8 %collective-permute-done.5.rest_6_ = bf16[544,128]{1,0:T(8,128)(2,1)S(1)} collective-permute-done((bf16[544,128]{1,0:T(8,128)(2,1)S(1)}, bf16[544,128]{1,0:T(8,128)(2,1)S(1)}, u32[]{:S(2)}, u32[]{:S(2)}) %collective-permute-start.5) | collective-permute-done | bytes 139296 | tf_op jit(solution)/shard_map/ppermute | solution.py:524
  49.6 8.2 %shard_map.99 = bf16[2,16,16,128]{3,2,1,0:T(8,128)(2,1)S(1)} custom-call(s32[4]{0:T(128)S(1)} %pad_add_fusion.place_ref, f32[2,1024]{1,0:T(2,128)S(1)} %get-tuple-element.22.vo_ref, f32[16,128]{1,0:T(8,128)S(1)} %get-tuple-element.23.own_ref, f32[16,128]{1,0:T(8,128)S(1)} %collective-permute-done.1.other_ref, ...), custom_call_target="tpu_custom_call" | custom-call | tf_op jit(solution)/shard_map/pallas_call | solution.py:506
  57.8 13.8 %all_to_all.10 = bf16[32,16,128]{2,1,0:T(8,128)(2,1)S(1)} all-to-all(bf16[32,16,128]{2,1,0:T(8,128)(2,1)S(1)} %bitcast.11), channel_id=1, replica_groups=mesh['groups'=2,'line'=4,'pair'=2,'tensor'=2] {'groups','line','pair','t..., dimensions={0} | all-to-all | bytes 262144 | tf_op jit(solution)/shard_map/all_to_all | solution.py:670
  71.7 1.1 %shard_map.100 = f32[1,512]{1,0:T(1,128)} custom-call(bf16[2,4,4,16,128]{4,3,2,1,0:T(8,128)(2,1)S(1)} %bitcast.12, s32[1,512]{1,0:T(1,128)S(1)} %bitcast.15, s32[1,512]{1,0:T(1,128)S(1)} %get-tuple-element.26.slot_ref), custom_call_target="tpu_custom_call" | custom-call | tf_op jit(solution)/shard_map/pallas_call | solution.py:678
  (14 shorter events, 0.0 us)
Async XLA Ops:
  0.0 30.8 %copy-start.4 = (f32[4,32,2]{2,1,0:T(8,128)S(1)}, f32[4,32,2]{2,1,0:T(8,128)}, u32[]{:S(2)}) copy-start(f32[4,32,2]{2,1,0:T(8,128)} %constant.17.clone.turn_ref) | copy-start | bytes 3076
  2.7 28.2 %all-to-all-start = ((bf16[8,400,128]{2,1,0:T(8,128)(2,1)}), bf16[8,400,128]{2,1,0:T(8,128)(2,1)S(1)}, u32[]{:S(2)}, u32[]{:S(2)}) async-start(bf16[8,400,128]{2,1,0:T(8,128)(2,1)} %shard_map.91.after_ref), calls=%async_computation | async-start | bytes 1638400 | tf_op jit(solution)/shard_map/all_to_all | solution.py:573
  12.1 15.1 %collective-permute-start = (bf16[9,256,128]{2,1,0:T(8,128)(2,1)}, bf16[9,256,128]{2,1,0:T(8,128)(2,1)S(1)}, u32[]{:S(2)}, u32[]{:S(2)}) collective-permute-start(bf16[9,256,128]{2,1,0:T(8,128)(2,1)} %shard_map.93.rest_0_), channel_id=1, source_target_pairs={{0,16},{2,18},{16,0},{18,2},{1,17},{3,19},{17,1},{19,3},{4,20},{6,... | collective-permute-start | bytes 1769480 | tf_op jit(solution)/shard_map/ppermute | solution.py:524
  13.7 23.3 %collective-permute-start.2 = (bf16[9,256,128]{2,1,0:T(8,128)(2,1)}, bf16[9,256,128]{2,1,0:T(8,128)(2,1)S(1)}, u32[]{:S(2)}, u32[]{:S(2)}) collective-permute-start(bf16[9,256,128]{2,1,0:T(8,128)(2,1)} %shard_map.93.rest_0_), channel_id=1, source_target_pairs={{0,2},{2,0},{16,18},{18,16},{1,3},{3,1},{17,19},{19,17},{4,6},{6,4... | collective-permute-start | bytes 1769480 | tf_op jit(solution)/shard_map/ppermute | solution.py:524
  27.2 20.6 %collective-permute-start.3 = (bf16[9,256,128]{2,1,0:T(8,128)(2,1)S(1)}, bf16[9,256,128]{2,1,0:T(8,128)(2,1)S(1)}, u32[]{:S(2)}, u32[]{:S(2)}) collective-permute-start(bf16[9,256,128]{2,1,0:T(8,128)(2,1)S(1)} %shard_map.94.after_ref.rest_2_), channel_id=1, source_target_pairs={{0,2},{2,0},{16,18},{18,16},{1,3},{3,1},{17,19},{19,17},{4,6},{6,4... | collective-permute-start | bytes 1769480 | tf_op jit(solution)/shard_map/ppermute | solution.py:524
  30.8 4.3 %copy-start.2 = (bf16[512,4096]{1,0:T(8,128)(2,1)S(1)}, bf16[512,4096]{1,0:T(8,128)(2,1)}, u32[]{:S(2)}) copy-start(bf16[512,4096]{1,0:T(8,128)(2,1)} %get-tuple-element.19.normed_ref) | copy-start | bytes 12582916
  30.8 2.3 %copy-start.3 = (bf16[512,4096]{1,0:T(8,128)(2,1)S(1)}, bf16[512,4096]{1,0:T(8,128)(2,1)}, u32[]{:S(2)}) copy-start(bf16[512,4096]{1,0:T(8,128)(2,1)} %get-tuple-element.16.normed_ref) | copy-start | bytes 12582916
  35.1 10.0 %copy-start.1 = (s32[512,1]{0,1:T(1,128)S(1)}, s32[512,1]{0,1:T(1,128)}, u32[]{:S(2)}) copy-start(s32[512,1]{0,1:T(1,128)} %param.11) | copy-start | bytes 6148
  35.2 14.4 %copy-start = (bf16[9,256,128]{2,1,0:T(8,128)(2,1)S(1)}, bf16[9,256,128]{2,1,0:T(8,128)(2,1)}, u32[]{:S(2)}) copy-start(bf16[9,256,128]{2,1,0:T(8,128)(2,1)} %shard_map.93.rest_0_) | copy-start | bytes 1769476
  37.0 10.8 %collective-permute-start.4 = (bf16[544,128]{1,0:T(8,128)(2,1)S(1)}, bf16[544,128]{1,0:T(8,128)(2,1)S(1)}, u32[]{:S(2)}, u32[]{:S(2)}) collective-permute-start(bf16[544,128]{1,0:T(8,128)(2,1)S(1)} %shard_map.98.rest_4_), channel_id=1, source_target_pairs={{0,4},{4,0},{8,12},{12,8},{1,5},{5,1},{9,13},{13,9},{2,6},{6,2},{1... | collective-permute-start | bytes 417800 | tf_op jit(solution)/shard_map/ppermute | solution.py:524
  37.3 12.3 %collective-permute-start.5 = (bf16[544,128]{1,0:T(8,128)(2,1)S(1)}, bf16[544,128]{1,0:T(8,128)(2,1)S(1)}, u32[]{:S(2)}, u32[]{:S(2)}) collective-permute-start(bf16[544,128]{1,0:T(8,128)(2,1)S(1)} %shard_map.98.rest_4_), channel_id=1, source_target_pairs={{0,8},{4,12},{8,0},{12,4},{1,9},{5,13},{9,1},{13,5},{2,10},{6,14},... | collective-permute-start | bytes 417800 | tf_op jit(solution)/shard_map/ppermute | solution.py:524
  39.1 10.5 %collective-permute-start.6 = (bf16[544,128]{1,0:T(8,128)(2,1)S(1)}, bf16[544,128]{1,0:T(8,128)(2,1)S(1)}, u32[]{:S(2)}, u32[]{:S(2)}) collective-permute-start(bf16[544,128]{1,0:T(8,128)(2,1)S(1)} %shard_map.98.rest_4_), channel_id=1, source_target_pairs={{0,12},{4,8},{8,4},{12,0},{1,13},{5,9},{9,5},{13,1},{2,14},{6,10},... | collective-permute-start | bytes 417800 | tf_op jit(solution)/shard_map/ppermute | solution.py:524
  41.4 3.7 %collective-permute-start.1 = (f32[16,128]{1,0:T(8,128)S(1)}, f32[16,128]{1,0:T(8,128)S(1)}, u32[]{:S(2)}, u32[]{:S(2)}) collective-permute-start(f32[16,128]{1,0:T(8,128)S(1)} %get-tuple-element.23.own_ref), channel_id=1, source_target_pairs={{0,16},{2,18},{16,0},{18,2},{1,17},{3,19},{17,1},{19,3},{4,20},{6,... | collective-permute-start | bytes 24584 | tf_op jit(solution)/shard_map/ppermute | solution.py:524

commit v27 on v26

--- a/solution.py
+++ b/solution.py
@@ -175,8 +175,8 @@
         out_ref[peer] = jnp.where(r == plan.list_at, lists[peer // plan.pair], mine).astype(BF16)
 
 
-def normalize(table_hbm, gain_ref, after_ref, *refs):
-    *outs, mark_ref, gain, buffers, made, sems, out_sems = refs
+def normalize(plan, place_ref, table_hbm, gain_ref, board_ref, after_ref, *refs):
+    *outs, mark_ref, slot_ref, gain, buffers, made, sems, out_sems = refs
     held, block, _ = buffers.shape
     steps = table_hbm.shape[0] // block
     each = outs[0].shape[0] // block
@@ -205,6 +205,12 @@
             copy(step + held).start()
     for step in range(max(0, steps - held), steps):
         store(step).wait()
+    count = board_ref.shape[1]
+    board_row = board_ref[...]
+    board_col = jnp.broadcast_to(board_row.astype(F32), (8, count)).T[:, 0:1].astype(jnp.int32)
+    ahead = lax.broadcasted_iota(jnp.int32, (count, count), 0) < lax.broadcasted_iota(jnp.int32, (count, count), 1)
+    rank = jnp.sum(jnp.where((board_col == board_row) & ahead, 1.0, 0.0), axis=0, keepdims=True)
+    slot_ref[...] = rank.astype(jnp.int32) + place_ref[PEER] * plan.capacity
     mark_ref[...] = jnp.zeros_like(mark_ref)
 
 
@@ -359,14 +365,8 @@
     return matmul(block, pick)
 
 
-def prepare(plan, place_ref, board_ref, own_ref, other_ref, *rest):
-    chosen_ref, slot_ref = rest
-    count = board_ref.shape[1]
-    board_row = board_ref[...]
-    board_col = jnp.broadcast_to(board_row.astype(F32), (8, count)).T[:, 0:1].astype(jnp.int32)
-    ahead = lax.broadcasted_iota(jnp.int32, (count, count), 0) < lax.broadcasted_iota(jnp.int32, (count, count), 1)
-    rank = jnp.sum(jnp.where((board_col == board_row) & ahead, 1.0, 0.0), axis=0, keepdims=True)
-    slot_ref[...] = rank.astype(jnp.int32) + place_ref[PEER] * plan.capacity
+def prepare(plan, place_ref, own_ref, other_ref, *rest):
+    *prefix_refs, chosen_ref, fold_ref = rest
     here = place_ref[SLAB]
     boards, moves = chosen_ref.shape[0], chosen_ref.shape[1]
     move_at = lax.broadcasted_iota(jnp.int32, (moves, plan.slots), 0) + 1
@@ -377,12 +377,24 @@
             row = (own_ref, other_ref)[j // plan.pair][pl.ds(place, 1), :].astype(jnp.int32)
             at = slice(j * plan.slots, (j + 1) * plan.slots)
             chosen_ref[board, :, at] = jnp.where(move_at == row, 1.0, 0.0).astype(BF16)
+        for j, prefix_ref in enumerate(prefix_refs):
+            fold_ref[j, board] = fold_columns(plan, here, prefix_ref[boards], board, boards, plan.heads)
         return carry
 
     lax.fori_loop(0, boards, step, 0)
 
 
-def attend(plan, place_ref, vo_ref, own_ref, other_ref, chosen_ref, *rest):
+def spread_fold(plan, place_ref, prefix_ref, fold_ref):
+    boards = fold_ref.shape[0]
+
+    def step(board, carry):
+        fold_ref[board] = fold_columns(plan, place_ref[SLAB], prefix_ref[boards], board, boards, plan.heads)
+        return carry
+
+    lax.fori_loop(0, boards, step, 0)
+
+
+def attend(plan, place_ref, vo_ref, own_ref, other_ref, chosen_ref, fold_ref, far_ref, *rest):
     prefix_refs, rest = rest[: plan.slab], rest[plan.slab :]
     *q_refs, out_ref, table, extra, scores, taken_even, taken_odd = rest
     here = place_ref[SLAB]
@@ -438,7 +450,7 @@
             x = taken[:, j * slots : (j + 1) * slots]
             q = jnp.concatenate([x[h * HD : (h + 1) * HD].astype(BF16) for h in range(mine)], axis=1)
             logits = matmul(prefix_refs[j][board], q)
-            fold = fold_columns(plan, here, prefix_refs[j][boards], board, boards, heads)
+            fold = fold_ref[j, board] if j < plan.slab - 1 else far_ref[board]
             own_logit = per_head(x, query_rows)
             own_value = per_head(x, query_rows + 2 * mine)
             peak = jnp.maximum(jnp.max(logits, axis=0, keepdims=True), own_logit)
@@ -590,11 +602,11 @@
 
     block = min(moves, 128)
     vmem = pl.BlockSpec(memory_space=pltpu.VMEM)
-    *normed, mark = pl.pallas_call(
-        normalize,
-        out_shape=[*[shape((moves // 2, width), BF16)] * 2, pltpu.VMEM((8, HD), F32)],
-        in_specs=[untouched(), vmem, untouched()],
-        out_specs=[untouched(), untouched(), vmem],
+    *normed, mark, slot_row = pl.pallas_call(
+        functools.partial(normalize, plan),
+        out_shape=[*[shape((moves // 2, width), BF16)] * 2, pltpu.VMEM((8, HD), F32), shape((1, row_count), jnp.int32)],
+        in_specs=[pl.BlockSpec(memory_space=pltpu.SMEM), untouched(), vmem, vmem, untouched()],
+        out_specs=[untouched(), untouched(), vmem, vmem],
         scratch_shapes=[
             pltpu.VMEM((1, width), F32),
             pltpu.VMEM((3, block, width), BF16),
@@ -604,7 +616,7 @@
         ],
         compiler_params=limits(58),
         cost_estimate=cost(moves * width, moves * width // 4),
-    )(move_table, norm_gain.reshape(width // HD, HD), packed)
+    )(place, move_table, norm_gain.reshape(width // HD, HD), board_row, packed)
     turns = turn_table(prefix_len).reshape(line, 1, plan.pairs, 2)
     turns = np.tile(turns, (1, plan.mine, 1, 1)).reshape(line, plan.mine * plan.pairs, 2)
     flat = weights.transpose(1, 0, 2).reshape(plan.rows, width) if depth % HD else weights
@@ -641,29 +653,36 @@
 
     query_rows = plan.mine * HD
     back = plan.peers * lax.axis_size("tensor")
-    chosen, slot_row = local_call(
+    chosen, folds = local_call(
         functools.partial(prepare, plan),
         place,
-        (board_row, listed, other),
+        (listed, other, payload, beside, across),
         (
             shape((boards_here, moves, plan.slab * plan.slots), BF16),
-            shape((1, row_count), jnp.int32),
+            shape((plan.slab - 1, boards_here, prefix_len, plan.mine * plan.slots), F32),
         ),
         mib=20,
         flops=10**9,
         nbytes=10**6,
     )
+    far = local_call(
+        functools.partial(spread_fold, plan),
+        place,
+        (diagonal,),
+        shape((boards_here, prefix_len, plan.mine * plan.slots), F32),
+        mib=20,
+    )
     parts = local_call(
         functools.partial(attend, plan),
         place,
-        (own_values, listed, other, chosen, payload, beside, across, diagonal, *queries),
+        (own_values, listed, other, chosen, folds, far, payload, beside, across, diagonal, *queries),
         shape((groups, back, plan.share, plan.slots), BF16),
         [
-            pltpu.VMEM((query_rows + 16, moves), BF16),
-            pltpu.VMEM((16, moves), F32),
+            pltpu.VMEM((query_rows + 8, moves), BF16),
+            pltpu.VMEM((8, moves), F32),
             pltpu.VMEM((plan.slab, boards_here, plan.slots), F32),
-            pltpu.VMEM((query_rows + 16, plan.slab * plan.slots), F32),
-            pltpu.VMEM((query_rows + 16, plan.slab * plan.slots), F32),
+            pltpu.VMEM((query_rows + 8, plan.slab * plan.slots), F32),
+            pltpu.VMEM((query_rows + 8, plan.slab * plan.slots), F32),
         ],
         24,
     )

time: 73 us -> 74.7 us (1.023)
  Pallas kernels: 28.8 us -> 32.8 us
  waiting for transfers between devices: 8.93 us -> 7.17 us
  blocking collectives: 13.8 us -> 12.4 us
    pallas_call x5 -> x6, Pallas kernels: 17.3 us -> 20.4 us  [local_call(): pl.pallas_call(kernel, out_shape=outs, in_specs=[pl.BlockSpec(memory_spac...]
    ppermute x7, waiting for transfers between devices: 7.02 us -> 5.29 us  [swap(): return lax.ppermute(x, names, [(at, at ^ step) for at in range(size)])]
    all_to_all x1, blocking collectives: 13.8 us -> 12.4 us  [per_device(): lax.all_to_all(parts.reshape(groups * back, plan.share, plan.slots), ('gr...]
    pallas_call x1, Pallas kernels: 8.3 us -> 9.2 us  [per_device(): pl.pallas_call(functools.partial(normalize, plan), out_shape=[*[shape((mo...]
    unnamed x10 -> x14, local copies, waits for them, and re-layouts: 2.36 us -> 2.52 us
  transfers between devices with their start and end apart: 8 -> 8, of which waited for: 4 -> 3; matrix products, arithmetic and copies ran while one was open for 0% -> 1% of each run, Pallas kernels for 23% -> 29%
where the time goes in v27:
time: 74.7 us; the launch traced here: 74.3 us
  Pallas kernels  32.8 us (44%)
  starting transfers between devices  18.6 us (25%)
  blocking collectives  12.4 us (17%)
  waiting for transfers between devices  7.17 us (10%)
  local copies, waits for them, and re-layouts  2.52 us (3%)
    pallas_call x6, Pallas kernels, local_call(): pl.pallas_call(kernel, out_shape=outs, in_specs=[pl.BlockSpec(memory_spac...  20.4 us
    all_to_all x1, blocking collectives, per_device(): lax.all_to_all(parts.reshape(groups * back, plan.share, plan.slots), ('gr...  12.4 us
    ppermute x7, starting transfers between devices, swap(): return lax.ppermute(x, names, [(at, at ^ step) for at in range(size)])  11.3 us
    pallas_call x1, Pallas kernels, per_device(): pl.pallas_call(functools.partial(normalize, plan), out_shape=[*[shape((mo...  9.2 us
    all_to_all x1, starting transfers between devices, per_device(): lax.all_to_all(packed, ('line', 'pair'), split_axis=0, concat_axis=0, til...  7.26 us
    ppermute x7, waiting for transfers between devices, swap(): return lax.ppermute(x, names, [(at, at ^ step) for at in range(size)])  5.29 us
    unnamed x14, local copies, waits for them, and re-layouts  2.52 us
    pallas_call x1, Pallas kernels, per_device(): pl.pallas_call(functools.partial(pack_prefix, plan), out_shape=shape((boa...  2.22 us
  transfers between devices with their start and end apart: 8, of which 3 were waited for; matrix products, arithmetic and copies ran while one was open for 1% of the time, Pallas kernels for 29%

profile of v27, /device:TPU:0, one launch (start us, length us, event | category | flops | bytes accessed | tf_op | source)
XLA Modules:
  0.0 74.3 jit_solution(5445092278688868263)
XLA Ops:
  0.0 2.6 %shard_map.91.after_ref = bf16[8,400,128]{2,1,0:T(8,128)(2,1)} custom-call(s32[1]{0:T(128)} %bitcast.place_ref, bf16[512,1024]{1,0:T(8,128)(2,1)} %wq_hbm.1, bf16[512,256]{1,0:T(8,128)(2,1)} %wkv_hbm.1, bf16[8,128]{1,0:T(8,128)(2,1)} %bitcast.17, s32[1,512]{1,0:T(1,128)} %bitcast.13, s32[1,512]{1,0:T(1,128)} %bitcast.19), custom_call_target="tpu_custom_call" | custom-call | tf_op jit(solution)/shard_map/pallas_call | solution.py:518
  2.6 7.3 %all-to-all-start = ((bf16[8,400,128]{2,1,0:T(8,128)(2,1)}), bf16[8,400,128]{2,1,0:T(8,128)(2,1)S(1)}, u32[]{:S(2)}, u32[]{:S(2)}) async-start(bf16[8,400,128]{2,1,0:T(8,128)(2,1)} %shard_map.91.after_ref), calls=%async_computation | async-start | bytes 1638400 | tf_op jit(solution)/shard_map/all_to_all | solution.py:585
  9.9 2.2 %shard_map.93.rest_0_ = bf16[9,256,128]{2,1,0:T(8,128)(2,1)} custom-call(bf16[8,256,256]{2,1,0:T(8,128)(2,1)} %prefix_hbm.1, bf16[8,128]{1,0:T(8,128)(2,1)} %bitcast.18, bf16[8,400,128]{2,1,0:T(8,128)(2,1)} %shard_map.91.after_ref), custom_call_target="tpu_custom_call" | custom-call | tf_op jit(solution)/shard_map/pallas_call | solution.py:587
  12.1 1.6 %collective-permute-start = (bf16[9,256,128]{2,1,0:T(8,128)(2,1)}, bf16[9,256,128]{2,1,0:T(8,128)(2,1)S(1)}, u32[]{:S(2)}, u32[]{:S(2)}) collective-permute-start(bf16[9,256,128]{2,1,0:T(8,128)(2,1)} %shard_map.93.rest_0_), channel_id=1, source_target_pairs={{0,16},{2,18},{16,0},{18,2},{1,17},{3,19},{17,1},{19,3},{4,20},{6,... | collective-permute-start | bytes 1769480 | tf_op jit(solution)/shard_map/ppermute | solution.py:536
  13.7 2.0 %collective-permute-start.2 = (bf16[9,256,128]{2,1,0:T(8,128)(2,1)}, bf16[9,256,128]{2,1,0:T(8,128)(2,1)S(1)}, u32[]{:S(2)}, u32[]{:S(2)}) collective-permute-start(bf16[9,256,128]{2,1,0:T(8,128)(2,1)} %shard_map.93.rest_0_), channel_id=1, source_target_pairs={{0,2},{2,0},{16,18},{18,16},{1,3},{3,1},{17,19},{19,17},{4,6},{6,4... | collective-permute-start | bytes 1769480 | tf_op jit(solution)/shard_map/ppermute | solution.py:536
  15.7 0.6 pad_add_fusion.place_ref
  16.3 9.2 %shard_map.92 = (bf16[512,4096]{1,0:T(8,128)(2,1)}, bf16[512,4096]{1,0:T(8,128)(2,1)}, f32[8,128]{1,0:T(8,128)S(1)}, s32[1,512]{1,0:T(1,128)}) custom-call(s32[4]{0:T(128)} %pad_add_fusion.place_ref, bf16[1024,4096]{1,0:T(8,128)(2,1)} %table_hbm.1, bf16[32,128]{1,0:T(8,128)(2,1)} %bitcast.16, s32[1,512]{1,0:T(1,128)} %bitcast.14, ...), custom_call_target="tpu_custom_call" | custom-call | flops 4194304 | bytes 1048576 | tf_op jit(solution)/shard_map/pallas_call | solution.py:605
  25.5 1.6 %collective-permute-done.refs_0_ = bf16[9,256,128]{2,1,0:T(8,128)(2,1)S(1)} collective-permute-done((bf16[9,256,128]{2,1,0:T(8,128)(2,1)}, bf16[9,256,128]{2,1,0:T(8,128)(2,1)S(1)}, u32[]{:S(2)}, u32[]{:S(2)}) %collective-permute-start) | collective-permute-done | bytes 589856 | tf_op jit(solution)/shard_map/ppermute | solution.py:536
  27.2 1.7 %collective-permute-start.3 = (bf16[9,256,128]{2,1,0:T(8,128)(2,1)S(1)}, bf16[9,256,128]{2,1,0:T(8,128)(2,1)S(1)}, u32[]{:S(2)}, u32[]{:S(2)}) collective-permute-start(bf16[9,256,128]{2,1,0:T(8,128)(2,1)S(1)} %shard_map.94.after_ref.rest_2_), channel_id=1, source_target_pairs={{0,2},{2,0},{16,18},{18,16},{1,3},{3,1},{17,19},{19,17},{4,6},{6,4... | collective-permute-start | bytes 1769480 | tf_op jit(solution)/shard_map/ppermute | solution.py:536
  28.9 1.9 %all-to-all-done.w_ref = bf16[8,400,128]{2,1,0:T(8,128)(2,1)S(1)} async-done(((bf16[8,400,128]{2,1,0:T(8,128)(2,1)}), bf16[8,400,128]{2,1,0:T(8,128)(2,1)S(1)}, u32[]{:S(2)}, u32[]{:S(2)}) %all-to-all-start) | async-done | bytes 819232 | tf_op jit(solution)/shard_map/all_to_all | solution.py:585
  30.8 2.2 %copy-done.5 = bf16[512,4096]{1,0:T(8,128)(2,1)S(1)} copy-done((bf16[512,4096]{1,0:T(8,128)(2,1)S(1)}, bf16[512,4096]{1,0:T(8,128)(2,1)}, u32[]{:S(2)}) %copy-start.5) | copy-done | bytes 4194328
  33.0 1.9 %shard_map.95 = (bf16[544,128]{1,0:T(8,128)(2,1)S(1)}, f32[2,1024]{1,0:T(2,128)S(1)}, f32[16,128]{1,0:T(8,128)S(1)}, bf16[8,104,512]{2,1,0:T(8,128)(2,1)S(1)}) custom-call(s32[4]{0:T(128)S(1)} %copy-done.2, bf16[8,400,128]{2,1,0:T(8,128)(2,1)S(1)} %all-to-all-done.w_ref, bf16[512,4096]{1,0:T(8,128)(2,1)S(1)} %copy-done.5, f32[4,32,2]{2,1,0:T(8,128)S(1)} %copy-done.6, ...), custom_call_target="tpu_custom_call" | custom-call | flops 4294967296 | bytes 4194304 | tf_op jit(solution)/shard_map/pallas_call | solution.py:518
  34.9 0.3 copy-done.4
  35.2 1.8 %shard_map.96 = (bf16[544,128]{1,0:T(8,128)(2,1)S(1)}, f32[2,1024]{1,0:T(2,128)S(1)}) custom-call(s32[4]{0:T(128)S(1)} %copy-done.2, bf16[8,104,512]{2,1,0:T(8,128)(2,1)S(1)} %get-tuple-element.19.w_ref, bf16[512,4096]{1,0:T(8,128)(2,1)S(1)} %copy-done.4, f32[4,32,2]{2,1,0:T(8,128)S(1)} %copy-done.6, ...), custom_call_target="tpu_custom_call", output_to_operand_aliasing={{0}: (5, {}), {1}: (6, {})} | custom-call | flops 4294967296 | bytes 4194304 | tf_op jit(solution)/shard_map/pallas_call | solution.py:518
  37.0 1.5 %collective-permute-start.6 = (bf16[544,128]{1,0:T(8,128)(2,1)S(1)}, bf16[544,128]{1,0:T(8,128)(2,1)S(1)}, u32[]{:S(2)}, u32[]{:S(2)}) collective-permute-start(bf16[544,128]{1,0:T(8,128)(2,1)S(1)} %shard_map.99.rest_4_), channel_id=1, source_target_pairs={{0,12},{4,8},{8,4},{12,0},{1,13},{5,9},{9,5},{13,1},{2,14},{6,10},... | collective-permute-start | bytes 417800 | tf_op jit(solution)/shard_map/ppermute | solution.py:536
  38.5 0.3 collective-permute-start.5
  38.8 2.7 %collective-permute-start.4 = (bf16[544,128]{1,0:T(8,128)(2,1)S(1)}, bf16[544,128]{1,0:T(8,128)(2,1)S(1)}, u32[]{:S(2)}, u32[]{:S(2)}) collective-permute-start(bf16[544,128]{1,0:T(8,128)(2,1)S(1)} %shard_map.99.rest_4_), channel_id=1, source_target_pairs={{0,4},{4,0},{8,12},{12,8},{1,5},{5,1},{9,13},{13,9},{2,6},{6,2},{1... | collective-permute-start | bytes 417800 | tf_op jit(solution)/shard_map/ppermute | solution.py:536
  41.5 1.5 %collective-permute-start.1 = (f32[16,128]{1,0:T(8,128)S(1)}, f32[16,128]{1,0:T(8,128)S(1)}, u32[]{:S(2)}, u32[]{:S(2)}) collective-permute-start(f32[16,128]{1,0:T(8,128)S(1)} %get-tuple-element.24.own_ref), channel_id=1, source_target_pairs={{0,16},{2,18},{16,0},{18,2},{1,17},{3,19},{17,1},{19,3},{4,20},{6,... | collective-permute-start | bytes 24584 | tf_op jit(solution)/shard_map/ppermute | solution.py:536
  43.0 3.6 %collective-permute-done.3.prefix_ref.rest_3_ = bf16[9,256,128]{2,1,0:T(8,128)(2,1)S(1)} collective-permute-done((bf16[9,256,128]{2,1,0:T(8,128)(2,1)S(1)}, bf16[9,256,128]{2,1,0:T(8,128)(2,1)S(1)}, u32[]{:S(2)}, u32[]{:S(2)}) %collective-permute-start.3) | collective-permute-done | bytes 589856 | tf_op jit(solution)/shard_map/ppermute | solution.py:536
  46.6 2.0 %shard_map.98.far_ref = f32[8,256,256]{2,1,0:T(8,128)S(1)} custom-call(s32[4]{0:T(128)S(1)} %copy-done.2, bf16[9,256,128]{2,1,0:T(8,128)(2,1)S(1)} %collective-permute-done.3.prefix_ref.rest_3_), custom_call_target="tpu_custom_call" | custom-call | tf_op jit(solution)/shard_map/pallas_call | solution.py:518
  48.7 4.7 %shard_map.97 = (bf16[8,1024,512]{2,1,0:T(8,128)(2,1)S(1)}, f32[3,8,256,256]{3,2,1,0:T(8,128)S(1)}) custom-call(s32[4]{0:T(128)S(1)} %copy-done.2, f32[16,128]{1,0:T(8,128)S(1)} %get-tuple-element.24.own_ref, f32[16,128]{1,0:T(8,128)S(1)} %collective-permute-done.1.other_ref, bf16[9,256,128]{2,1,0:T(8,128)(2,1)S(1)} %copy-done, ...), custom_call_target="tpu_custom_call" | custom-call | flops 1000000000 | bytes 1000000 | tf_op jit(solution)/shard_map/pallas_call | solution.py:518
  53.4 7.4 %shard_map.100 = bf16[2,16,16,128]{3,2,1,0:T(8,128)(2,1)S(1)} custom-call(s32[4]{0:T(128)S(1)} %copy-done.2, f32[2,1024]{1,0:T(2,128)S(1)} %get-tuple-element.23.vo_ref, f32[16,128]{1,0:T(8,128)S(1)} %get-tuple-element.24.own_ref, f32[16,128]{1,0:T(8,128)S(1)} %collective-permute-done.1.other_ref, bf16[8,1024,512]{2,1,0:T(8,128)(2,1)S(1)} %get-tuple-element.25.chosen_ref, ...), custom_call_target="tpu_custom_call" | custom-call | tf_op jit(solution)/shard_map/pallas_call | solution.py:518
  60.8 12.4 %all_to_all.10 = bf16[32,16,128]{2,1,0:T(8,128)(2,1)S(1)} all-to-all(bf16[32,16,128]{2,1,0:T(8,128)(2,1)S(1)} %bitcast.11), channel_id=1, replica_groups=mesh['groups'=2,'line'=4,'pair'=2,'tensor'=2] {'groups','line','pair','t..., dimensions={0} | all-to-all | bytes 262144 | tf_op jit(solution)/shard_map/all_to_all | solution.py:689
  73.2 1.1 %shard_map.101 = f32[1,512]{1,0:T(1,128)} custom-call(bf16[2,4,4,16,128]{4,3,2,1,0:T(8,128)(2,1)S(1)} %bitcast.12, s32[1,512]{1,0:T(1,128)S(1)} %bitcast.15, s32[1,512]{1,0:T(1,128)S(1)} %copy-done.3), custom_call_target="tpu_custom_call" | custom-call | tf_op jit(solution)/shard_map/pallas_call | solution.py:697
  (19 shorter events, 0.0 us)
Async XLA Ops:
  2.6 28.2 %all-to-all-start = ((bf16[8,400,128]{2,1,0:T(8,128)(2,1)}), bf16[8,400,128]{2,1,0:T(8,128)(2,1)S(1)}, u32[]{:S(2)}, u32[]{:S(2)}) async-start(bf16[8,400,128]{2,1,0:T(8,128)(2,1)} %shard_map.91.after_ref), calls=%async_computation | async-start | bytes 1638400 | tf_op jit(solution)/shard_map/all_to_all | solution.py:585
  9.9 20.9 %copy-start.6 = (f32[4,32,2]{2,1,0:T(8,128)S(1)}, f32[4,32,2]{2,1,0:T(8,128)}, u32[]{:S(2)}) copy-start(f32[4,32,2]{2,1,0:T(8,128)} %constant.17.clone.turn_ref) | copy-start | bytes 3076
  12.1 15.1 %collective-permute-start = (bf16[9,256,128]{2,1,0:T(8,128)(2,1)}, bf16[9,256,128]{2,1,0:T(8,128)(2,1)S(1)}, u32[]{:S(2)}, u32[]{:S(2)}) collective-permute-start(bf16[9,256,128]{2,1,0:T(8,128)(2,1)} %shard_map.93.rest_0_), channel_id=1, source_target_pairs={{0,16},{2,18},{16,0},{18,2},{1,17},{3,19},{17,1},{19,3},{4,20},{6,... | collective-permute-start | bytes 1769480 | tf_op jit(solution)/shard_map/ppermute | solution.py:536
  13.7 23.3 %collective-permute-start.2 = (bf16[9,256,128]{2,1,0:T(8,128)(2,1)}, bf16[9,256,128]{2,1,0:T(8,128)(2,1)S(1)}, u32[]{:S(2)}, u32[]{:S(2)}) collective-permute-start(bf16[9,256,128]{2,1,0:T(8,128)(2,1)} %shard_map.93.rest_0_), channel_id=1, source_target_pairs={{0,2},{2,0},{16,18},{18,16},{1,3},{3,1},{17,19},{19,17},{4,6},{6,4... | collective-permute-start | bytes 1769480 | tf_op jit(solution)/shard_map/ppermute | solution.py:536
  16.3 14.5 %copy-start.2 = (s32[4]{0:T(128)S(1)}, s32[4]{0:T(128)}, u32[]{:S(2)}) copy-start(s32[4]{0:T(128)} %pad_add_fusion.place_ref) | copy-start | bytes 52
  27.2 19.4 %collective-permute-start.3 = (bf16[9,256,128]{2,1,0:T(8,128)(2,1)S(1)}, bf16[9,256,128]{2,1,0:T(8,128)(2,1)S(1)}, u32[]{:S(2)}, u32[]{:S(2)}) collective-permute-start(bf16[9,256,128]{2,1,0:T(8,128)(2,1)S(1)} %shard_map.94.after_ref.rest_2_), channel_id=1, source_target_pairs={{0,2},{2,0},{16,18},{18,16},{1,3},{3,1},{17,19},{19,17},{4,6},{6,4... | collective-permute-start | bytes 1769480 | tf_op jit(solution)/shard_map/ppermute | solution.py:536
  30.8 2.2 %copy-start.5 = (bf16[512,4096]{1,0:T(8,128)(2,1)S(1)}, bf16[512,4096]{1,0:T(8,128)(2,1)}, u32[]{:S(2)}) copy-start(bf16[512,4096]{1,0:T(8,128)(2,1)} %get-tuple-element.17.normed_ref) | copy-start | bytes 12582916
  33.0 2.2 %copy-start.4 = (bf16[512,4096]{1,0:T(8,128)(2,1)S(1)}, bf16[512,4096]{1,0:T(8,128)(2,1)}, u32[]{:S(2)}) copy-start(bf16[512,4096]{1,0:T(8,128)(2,1)} %get-tuple-element.20.normed_ref) | copy-start | bytes 12582916
  35.2 13.5 %copy-start = (bf16[9,256,128]{2,1,0:T(8,128)(2,1)S(1)}, bf16[9,256,128]{2,1,0:T(8,128)(2,1)}, u32[]{:S(2)}) copy-start(bf16[9,256,128]{2,1,0:T(8,128)(2,1)} %shard_map.93.rest_0_) | copy-start | bytes 1769476
  37.0 16.3 %collective-permute-start.6 = (bf16[544,128]{1,0:T(8,128)(2,1)S(1)}, bf16[544,128]{1,0:T(8,128)(2,1)S(1)}, u32[]{:S(2)}, u32[]{:S(2)}) collective-permute-start(bf16[544,128]{1,0:T(8,128)(2,1)S(1)} %shard_map.99.rest_4_), channel_id=1, source_target_pairs={{0,12},{4,8},{8,4},{12,0},{1,13},{5,9},{9,5},{13,1},{2,14},{6,10},... | collective-permute-start | bytes 417800 | tf_op jit(solution)/shard_map/ppermute | solution.py:536
  38.5 14.8 %collective-permute-start.5 = (bf16[544,128]{1,0:T(8,128)(2,1)S(1)}, bf16[544,128]{1,0:T(8,128)(2,1)S(1)}, u32[]{:S(2)}, u32[]{:S(2)}) collective-permute-start(bf16[544,128]{1,0:T(8,128)(2,1)S(1)} %shard_map.99.rest_4_), channel_id=1, source_target_pairs={{0,8},{4,12},{8,0},{12,4},{1,9},{5,13},{9,1},{13,5},{2,10},{6,14},... | collective-permute-start | bytes 417800 | tf_op jit(solution)/shard_map/ppermute | solution.py:536
  38.8 14.6 %collective-permute-start.4 = (bf16[544,128]{1,0:T(8,128)(2,1)S(1)}, bf16[544,128]{1,0:T(8,128)(2,1)S(1)}, u32[]{:S(2)}, u32[]{:S(2)}) collective-permute-start(bf16[544,128]{1,0:T(8,128)(2,1)S(1)} %shard_map.99.rest_4_), channel_id=1, source_target_pairs={{0,4},{4,0},{8,12},{12,8},{1,5},{5,1},{9,13},{13,9},{2,6},{6,2},{1... | collective-permute-start | bytes 417800 | tf_op jit(solution)/shard_map/ppermute | solution.py:536
  41.5 7.2 %collective-permute-start.1 = (f32[16,128]{1,0:T(8,128)S(1)}, f32[16,128]{1,0:T(8,128)S(1)}, u32[]{:S(2)}, u32[]{:S(2)}) collective-permute-start(f32[16,128]{1,0:T(8,128)S(1)} %get-tuple-element.24.own_ref), channel_id=1, source_target_pairs={{0,16},{2,18},{16,0},{18,2},{1,17},{3,19},{17,1},{19,3},{4,20},{6,... | collective-permute-start | bytes 24584 | tf_op jit(solution)/shard_map/ppermute | solution.py:536
  53.4 19.9 %copy-start.1 = (s32[512,1]{0,1:T(1,128)S(1)}, s32[512,1]{0,1:T(1,128)}, u32[]{:S(2)}) copy-start(s32[512,1]{0,1:T(1,128)} %param.11) | copy-start | bytes 6148
  53.4 19.9 %copy-start.3 = (s32[1,512]{1,0:T(1,128)S(1)}, s32[1,512]{1,0:T(1,128)}, u32[]{:S(2)}) copy-start(s32[1,512]{1,0:T(1,128)} %get-tuple-element.28.slot_ref) | copy-start | bytes 6148

commit v28 on v27

--- a/solution.py
+++ b/solution.py
@@ -384,17 +384,7 @@
     lax.fori_loop(0, boards, step, 0)
 
 
-def spread_fold(plan, place_ref, prefix_ref, fold_ref):
-    boards = fold_ref.shape[0]
-
-    def step(board, carry):
-        fold_ref[board] = fold_columns(plan, place_ref[SLAB], prefix_ref[boards], board, boards, plan.heads)
-        return carry
-
-    lax.fori_loop(0, boards, step, 0)
-
-
-def attend(plan, place_ref, vo_ref, own_ref, other_ref, chosen_ref, fold_ref, far_ref, *rest):
+def attend(plan, place_ref, vo_ref, own_ref, other_ref, chosen_ref, fold_ref, *rest):
     prefix_refs, rest = rest[: plan.slab], rest[plan.slab :]
     *q_refs, out_ref, table, extra, scores, taken_even, taken_odd = rest
     here = place_ref[SLAB]
@@ -450,7 +440,10 @@
             x = taken[:, j * slots : (j + 1) * slots]
             q = jnp.concatenate([x[h * HD : (h + 1) * HD].astype(BF16) for h in range(mine)], axis=1)
             logits = matmul(prefix_refs[j][board], q)
-            fold = fold_ref[j, board] if j < plan.slab - 1 else far_ref[board]
+            if j < plan.slab - 1:
+                fold = fold_ref[j, board]
+            else:
+                fold = fold_columns(plan, here, prefix_refs[j][boards], board, boards, heads)
             own_logit = per_head(x, query_rows)
             own_value = per_head(x, query_rows + 2 * mine)
             peak = jnp.maximum(jnp.max(logits, axis=0, keepdims=True), own_logit)
@@ -500,11 +493,10 @@
     count = board_ref.shape[1]
     member = lax.broadcasted_iota(jnp.int32, (scores.shape[0], count), 0) == board_ref[...]
     member = jnp.where(member, 1.0, 0.0).astype(BF16)
-    found = jnp.zeros((plan.slots, count), F32)
-    for _ in range(3):
-        rounded = logprob.astype(BF16)
-        found = found + matmul(rounded, member, TN)
-        logprob = logprob - rounded.astype(F32)
+    rounded = logprob.astype(BF16)
+    pieces = jnp.concatenate([rounded, (logprob - rounded.astype(F32)).astype(BF16)], axis=1)
+    found = matmul(pieces, member, TN)
+    found = found[: plan.slots] + found[plan.slots :]
     at = lax.broadcasted_iota(jnp.int32, (plan.slots, count), 0) == slot_ref[...]
     out_ref[...] = jnp.sum(jnp.where(at, found, 0.0), axis=0, keepdims=True)
 
@@ -665,24 +657,17 @@
         flops=10**9,
         nbytes=10**6,
     )
-    far = local_call(
-        functools.partial(spread_fold, plan),
-        place,
-        (diagonal,),
-        shape((boards_here, prefix_len, plan.mine * plan.slots), F32),
-        mib=20,
-    )
     parts = local_call(
         functools.partial(attend, plan),
         place,
-        (own_values, listed, other, chosen, folds, far, payload, beside, across, diagonal, *queries),
+        (own_values, listed, other, chosen, folds, payload, beside, across, diagonal, *queries),
         shape((groups, back, plan.share, plan.slots), BF16),
         [
-            pltpu.VMEM((query_rows + 8, moves), BF16),
-            pltpu.VMEM((8, moves), F32),
+            pltpu.VMEM((query_rows + 16, moves), BF16),
+            pltpu.VMEM((16, moves), F32),
             pltpu.VMEM((plan.slab, boards_here, plan.slots), F32),
-            pltpu.VMEM((query_rows + 8, plan.slab * plan.slots), F32),
-            pltpu.VMEM((query_rows + 8, plan.slab * plan.slots), F32),
+            pltpu.VMEM((query_rows + 16, plan.slab * plan.slots), F32),
+            pltpu.VMEM((query_rows + 16, plan.slab * plan.slots), F32),
         ],
         24,
     )

time: 74.7 us -> 70.7 us (0.946)
  Pallas kernels: 32.8 us -> 30.5 us
  waiting for transfers between devices: 7.17 us -> 6.22 us
    pallas_call x6 -> x5, Pallas kernels: 20.4 us -> 18 us  [local_call(): pl.pallas_call(kernel, out_shape=outs, in_specs=[pl.BlockSpec(memory_spac...]
    ppermute x7, waiting for transfers between devices: 5.29 us -> 4.34 us  [swap(): return lax.ppermute(x, names, [(at, at ^ step) for at in range(size)])]
  transfers between devices with their start and end apart: 8 -> 8, of which waited for: 3 -> 4; matrix products, arithmetic and copies ran while one was open for 1% -> 1% of each run, Pallas kernels for 29% -> 28%
where the time goes in v28:
time: 70.7 us; the launch traced here: 70.3 us
  Pallas kernels  30.5 us (43%)
  starting transfers between devices  18.6 us (26%)
  blocking collectives  11.8 us (17%)
  waiting for transfers between devices  6.22 us (9%)
  local copies, waits for them, and re-layouts  2.51 us (4%)
    pallas_call x5, Pallas kernels, local_call(): pl.pallas_call(kernel, out_shape=outs, in_specs=[pl.BlockSpec(memory_spac...  18 us
    all_to_all x1, blocking collectives, per_device(): lax.all_to_all(parts.reshape(groups * back, plan.share, plan.slots), ('gr...  11.8 us
    ppermute x7, starting transfers between devices, swap(): return lax.ppermute(x, names, [(at, at ^ step) for at in range(size)])  11.3 us
    pallas_call x1, Pallas kernels, per_device(): pl.pallas_call(functools.partial(normalize, plan), out_shape=[*[shape((mo...  9.2 us
    all_to_all x1, starting transfers between devices, per_device(): lax.all_to_all(packed, ('line', 'pair'), split_axis=0, concat_axis=0, til...  7.26 us
    ppermute x7, waiting for transfers between devices, swap(): return lax.ppermute(x, names, [(at, at ^ step) for at in range(size)])  4.34 us
    unnamed x14, local copies, waits for them, and re-layouts  2.51 us
    pallas_call x1, Pallas kernels, per_device(): pl.pallas_call(functools.partial(pack_prefix, plan), out_shape=shape((boa...  2.22 us
  transfers between devices with their start and end apart: 8, of which 4 were waited for; matrix products, arithmetic and copies ran while one was open for 1% of the time, Pallas kernels for 28%

profile of v28, /device:TPU:0, one launch (start us, length us, event | category | flops | bytes accessed | tf_op | source)
XLA Modules:
  0.0 70.3 jit_solution(17867130931120139700)
XLA Ops:
  0.0 2.6 %shard_map.91.after_ref = bf16[8,400,128]{2,1,0:T(8,128)(2,1)} custom-call(s32[1]{0:T(128)} %bitcast.place_ref, bf16[512,1024]{1,0:T(8,128)(2,1)} %wq_hbm.1, bf16[512,256]{1,0:T(8,128)(2,1)} %wkv_hbm.1, bf16[8,128]{1,0:T(8,128)(2,1)} %bitcast.17, s32[1,512]{1,0:T(1,128)} %bitcast.13, s32[1,512]{1,0:T(1,128)} %bitcast.19), custom_call_target="tpu_custom_call" | custom-call | tf_op jit(solution)/shard_map/pallas_call | solution.py:510
  2.6 7.3 %all-to-all-start = ((bf16[8,400,128]{2,1,0:T(8,128)(2,1)}), bf16[8,400,128]{2,1,0:T(8,128)(2,1)S(1)}, u32[]{:S(2)}, u32[]{:S(2)}) async-start(bf16[8,400,128]{2,1,0:T(8,128)(2,1)} %shard_map.91.after_ref), calls=%async_computation | async-start | bytes 1638400 | tf_op jit(solution)/shard_map/all_to_all | solution.py:577
  9.9 2.2 %shard_map.93.rest_0_ = bf16[9,256,128]{2,1,0:T(8,128)(2,1)} custom-call(bf16[8,256,256]{2,1,0:T(8,128)(2,1)} %prefix_hbm.1, bf16[8,128]{1,0:T(8,128)(2,1)} %bitcast.18, bf16[8,400,128]{2,1,0:T(8,128)(2,1)} %shard_map.91.after_ref), custom_call_target="tpu_custom_call" | custom-call | tf_op jit(solution)/shard_map/pallas_call | solution.py:579
  12.1 1.6 %collective-permute-start = (bf16[9,256,128]{2,1,0:T(8,128)(2,1)}, bf16[9,256,128]{2,1,0:T(8,128)(2,1)S(1)}, u32[]{:S(2)}, u32[]{:S(2)}) collective-permute-start(bf16[9,256,128]{2,1,0:T(8,128)(2,1)} %shard_map.93.rest_0_), channel_id=1, source_target_pairs={{0,16},{2,18},{16,0},{18,2},{1,17},{3,19},{17,1},{19,3},{4,20},{6,... | collective-permute-start | bytes 1769480 | tf_op jit(solution)/shard_map/ppermute | solution.py:528
  13.7 2.0 %collective-permute-start.2 = (bf16[9,256,128]{2,1,0:T(8,128)(2,1)}, bf16[9,256,128]{2,1,0:T(8,128)(2,1)S(1)}, u32[]{:S(2)}, u32[]{:S(2)}) collective-permute-start(bf16[9,256,128]{2,1,0:T(8,128)(2,1)} %shard_map.93.rest_0_), channel_id=1, source_target_pairs={{0,2},{2,0},{16,18},{18,16},{1,3},{3,1},{17,19},{19,17},{4,6},{6,4... | collective-permute-start | bytes 1769480 | tf_op jit(solution)/shard_map/ppermute | solution.py:528
  15.7 0.6 pad_add_fusion.place_ref
  16.3 9.2 %shard_map.92 = (bf16[512,4096]{1,0:T(8,128)(2,1)}, bf16[512,4096]{1,0:T(8,128)(2,1)}, f32[8,128]{1,0:T(8,128)S(1)}, s32[1,512]{1,0:T(1,128)}) custom-call(s32[4]{0:T(128)} %pad_add_fusion.place_ref, bf16[1024,4096]{1,0:T(8,128)(2,1)} %table_hbm.1, bf16[32,128]{1,0:T(8,128)(2,1)} %bitcast.16, s32[1,512]{1,0:T(1,128)} %bitcast.14, ...), custom_call_target="tpu_custom_call" | custom-call | flops 4194304 | bytes 1048576 | tf_op jit(solution)/shard_map/pallas_call | solution.py:597
  25.5 1.6 %collective-permute-done.refs_0_ = bf16[9,256,128]{2,1,0:T(8,128)(2,1)S(1)} collective-permute-done((bf16[9,256,128]{2,1,0:T(8,128)(2,1)}, bf16[9,256,128]{2,1,0:T(8,128)(2,1)S(1)}, u32[]{:S(2)}, u32[]{:S(2)}) %collective-permute-start) | collective-permute-done | bytes 589856 | tf_op jit(solution)/shard_map/ppermute | solution.py:528
  27.2 1.7 %collective-permute-start.3 = (bf16[9,256,128]{2,1,0:T(8,128)(2,1)S(1)}, bf16[9,256,128]{2,1,0:T(8,128)(2,1)S(1)}, u32[]{:S(2)}, u32[]{:S(2)}) collective-permute-start(bf16[9,256,128]{2,1,0:T(8,128)(2,1)S(1)} %shard_map.94.after_ref.rest_2_), channel_id=1, source_target_pairs={{0,2},{2,0},{16,18},{18,16},{1,3},{3,1},{17,19},{19,17},{4,6},{6,4... | collective-permute-start | bytes 1769480 | tf_op jit(solution)/shard_map/ppermute | solution.py:528
  28.9 1.9 %all-to-all-done.w_ref = bf16[8,400,128]{2,1,0:T(8,128)(2,1)S(1)} async-done(((bf16[8,400,128]{2,1,0:T(8,128)(2,1)}), bf16[8,400,128]{2,1,0:T(8,128)(2,1)S(1)}, u32[]{:S(2)}, u32[]{:S(2)}) %all-to-all-start) | async-done | bytes 819232 | tf_op jit(solution)/shard_map/all_to_all | solution.py:577
  30.8 2.2 %copy-done.5 = bf16[512,4096]{1,0:T(8,128)(2,1)S(1)} copy-done((bf16[512,4096]{1,0:T(8,128)(2,1)S(1)}, bf16[512,4096]{1,0:T(8,128)(2,1)}, u32[]{:S(2)}) %copy-start.5) | copy-done | bytes 4194328
  33.0 1.9 %shard_map.95 = (bf16[544,128]{1,0:T(8,128)(2,1)S(1)}, f32[2,1024]{1,0:T(2,128)S(1)}, f32[16,128]{1,0:T(8,128)S(1)}, bf16[8,104,512]{2,1,0:T(8,128)(2,1)S(1)}) custom-call(s32[4]{0:T(128)S(1)} %copy-done.2, bf16[8,400,128]{2,1,0:T(8,128)(2,1)S(1)} %all-to-all-done.w_ref, bf16[512,4096]{1,0:T(8,128)(2,1)S(1)} %copy-done.5, f32[4,32,2]{2,1,0:T(8,128)S(1)} %copy-done.6, ...), custom_call_target="tpu_custom_call" | custom-call | flops 4294967296 | bytes 4194304 | tf_op jit(solution)/shard_map/pallas_call | solution.py:510
  34.9 0.3 copy-done.4
  35.2 1.8 %shard_map.96 = (bf16[544,128]{1,0:T(8,128)(2,1)S(1)}, f32[2,1024]{1,0:T(2,128)S(1)}) custom-call(s32[4]{0:T(128)S(1)} %copy-done.2, bf16[8,104,512]{2,1,0:T(8,128)(2,1)S(1)} %get-tuple-element.19.w_ref, bf16[512,4096]{1,0:T(8,128)(2,1)S(1)} %copy-done.4, f32[4,32,2]{2,1,0:T(8,128)S(1)} %copy-done.6, ...), custom_call_target="tpu_custom_call", output_to_operand_aliasing={{0}: (5, {}), {1}: (6, {})} | custom-call | flops 4294967296 | bytes 4194304 | tf_op jit(solution)/shard_map/pallas_call | solution.py:510
  37.0 1.5 %collective-permute-start.6 = (bf16[544,128]{1,0:T(8,128)(2,1)S(1)}, bf16[544,128]{1,0:T(8,128)(2,1)S(1)}, u32[]{:S(2)}, u32[]{:S(2)}) collective-permute-start(bf16[544,128]{1,0:T(8,128)(2,1)S(1)} %shard_map.98.rest_4_), channel_id=1, source_target_pairs={{0,12},{4,8},{8,4},{12,0},{1,13},{5,9},{9,5},{13,1},{2,14},{6,10},... | collective-permute-start | bytes 417800 | tf_op jit(solution)/shard_map/ppermute | solution.py:528
  38.5 0.3 collective-permute-start.5
  38.8 2.7 %collective-permute-start.4 = (bf16[544,128]{1,0:T(8,128)(2,1)S(1)}, bf16[544,128]{1,0:T(8,128)(2,1)S(1)}, u32[]{:S(2)}, u32[]{:S(2)}) collective-permute-start(bf16[544,128]{1,0:T(8,128)(2,1)S(1)} %shard_map.98.rest_4_), channel_id=1, source_target_pairs={{0,4},{4,0},{8,12},{12,8},{1,5},{5,1},{9,13},{13,9},{2,6},{6,2},{1... | collective-permute-start | bytes 417800 | tf_op jit(solution)/shard_map/ppermute | solution.py:528
  41.5 1.5 %collective-permute-start.1 = (f32[16,128]{1,0:T(8,128)S(1)}, f32[16,128]{1,0:T(8,128)S(1)}, u32[]{:S(2)}, u32[]{:S(2)}) collective-permute-start(f32[16,128]{1,0:T(8,128)S(1)} %get-tuple-element.24.own_ref), channel_id=1, source_target_pairs={{0,16},{2,18},{16,0},{18,2},{1,17},{3,19},{17,1},{19,3},{4,20},{6,... | collective-permute-start | bytes 24584 | tf_op jit(solution)/shard_map/ppermute | solution.py:528
  43.0 2.1 %collective-permute-done.1.other_ref = f32[16,128]{1,0:T(8,128)S(1)} collective-permute-done((f32[16,128]{1,0:T(8,128)S(1)}, f32[16,128]{1,0:T(8,128)S(1)}, u32[]{:S(2)}, u32[]{:S(2)}) %collective-permute-start.1) | collective-permute-done | bytes 8224 | tf_op jit(solution)/shard_map/ppermute | solution.py:528
  45.1 4.7 %shard_map.97 = (bf16[8,1024,512]{2,1,0:T(8,128)(2,1)S(1)}, f32[3,8,256,256]{3,2,1,0:T(8,128)S(1)}) custom-call(s32[4]{0:T(128)S(1)} %copy-done.2, f32[16,128]{1,0:T(8,128)S(1)} %get-tuple-element.24.own_ref, f32[16,128]{1,0:T(8,128)S(1)} %collective-permute-done.1.other_ref, bf16[9,256,128]{2,1,0:T(8,128)(2,1)S(1)} %copy-done, ...), custom_call_target="tpu_custom_call" | custom-call | flops 1000000000 | bytes 1000000 | tf_op jit(solution)/shard_map/pallas_call | solution.py:510
  49.8 0.6 collective-permute-done.5.rest_6_
  50.4 7.1 %shard_map.99 = bf16[2,16,16,128]{3,2,1,0:T(8,128)(2,1)S(1)} custom-call(s32[4]{0:T(128)S(1)} %copy-done.2, f32[2,1024]{1,0:T(2,128)S(1)} %get-tuple-element.23.vo_ref, f32[16,128]{1,0:T(8,128)S(1)} %get-tuple-element.24.own_ref, f32[16,128]{1,0:T(8,128)S(1)} %collective-permute-done.1.other_ref, bf16[8,1024,512]{2,1,0:T(8,128)(2,1)S(1)} %get-tuple-element.25.chosen_ref, ...), custom_call_target="tpu_custom_call" | custom-call | tf_op jit(solution)/shard_map/pallas_call | solution.py:510
  57.5 11.8 %all_to_all.10 = bf16[32,16,128]{2,1,0:T(8,128)(2,1)S(1)} all-to-all(bf16[32,16,128]{2,1,0:T(8,128)(2,1)S(1)} %bitcast.11), channel_id=1, replica_groups=mesh['groups'=2,'line'=4,'pair'=2,'tensor'=2] {'groups','line','pair','t..., dimensions={0} | all-to-all | bytes 262144 | tf_op jit(solution)/shard_map/all_to_all | solution.py:674
  69.2 1.0 %shard_map.100 = f32[1,512]{1,0:T(1,128)} custom-call(bf16[2,4,4,16,128]{4,3,2,1,0:T(8,128)(2,1)S(1)} %bitcast.12, s32[1,512]{1,0:T(1,128)S(1)} %bitcast.15, s32[1,512]{1,0:T(1,128)S(1)} %copy-done.3), custom_call_target="tpu_custom_call" | custom-call | tf_op jit(solution)/shard_map/pallas_call | solution.py:682
  (18 shorter events, 0.0 us)
Async XLA Ops:
  2.6 28.2 %all-to-all-start = ((bf16[8,400,128]{2,1,0:T(8,128)(2,1)}), bf16[8,400,128]{2,1,0:T(8,128)(2,1)S(1)}, u32[]{:S(2)}, u32[]{:S(2)}) async-start(bf16[8,400,128]{2,1,0:T(8,128)(2,1)} %shard_map.91.after_ref), calls=%async_computation | async-start | bytes 1638400 | tf_op jit(solution)/shard_map/all_to_all | solution.py:577
  9.9 20.9 %copy-start.6 = (f32[4,32,2]{2,1,0:T(8,128)S(1)}, f32[4,32,2]{2,1,0:T(8,128)}, u32[]{:S(2)}) copy-start(f32[4,32,2]{2,1,0:T(8,128)} %constant.17.clone.turn_ref) | copy-start | bytes 3076
  12.1 15.1 %collective-permute-start = (bf16[9,256,128]{2,1,0:T(8,128)(2,1)}, bf16[9,256,128]{2,1,0:T(8,128)(2,1)S(1)}, u32[]{:S(2)}, u32[]{:S(2)}) collective-permute-start(bf16[9,256,128]{2,1,0:T(8,128)(2,1)} %shard_map.93.rest_0_), channel_id=1, source_target_pairs={{0,16},{2,18},{16,0},{18,2},{1,17},{3,19},{17,1},{19,3},{4,20},{6,... | collective-permute-start | bytes 1769480 | tf_op jit(solution)/shard_map/ppermute | solution.py:528
  13.7 23.3 %collective-permute-start.2 = (bf16[9,256,128]{2,1,0:T(8,128)(2,1)}, bf16[9,256,128]{2,1,0:T(8,128)(2,1)S(1)}, u32[]{:S(2)}, u32[]{:S(2)}) collective-permute-start(bf16[9,256,128]{2,1,0:T(8,128)(2,1)} %shard_map.93.rest_0_), channel_id=1, source_target_pairs={{0,2},{2,0},{16,18},{18,16},{1,3},{3,1},{17,19},{19,17},{4,6},{6,4... | collective-permute-start | bytes 1769480 | tf_op jit(solution)/shard_map/ppermute | solution.py:528
  16.3 14.5 %copy-start.2 = (s32[4]{0:T(128)S(1)}, s32[4]{0:T(128)}, u32[]{:S(2)}) copy-start(s32[4]{0:T(128)} %pad_add_fusion.place_ref) | copy-start | bytes 52
  27.2 22.6 %collective-permute-start.3 = (bf16[9,256,128]{2,1,0:T(8,128)(2,1)S(1)}, bf16[9,256,128]{2,1,0:T(8,128)(2,1)S(1)}, u32[]{:S(2)}, u32[]{:S(2)}) collective-permute-start(bf16[9,256,128]{2,1,0:T(8,128)(2,1)S(1)} %shard_map.94.after_ref.rest_2_), channel_id=1, source_target_pairs={{0,2},{2,0},{16,18},{18,16},{1,3},{3,1},{17,19},{19,17},{4,6},{6,4... | collective-permute-start | bytes 1769480 | tf_op jit(solution)/shard_map/ppermute | solution.py:528
  30.8 2.2 %copy-start.5 = (bf16[512,4096]{1,0:T(8,128)(2,1)S(1)}, bf16[512,4096]{1,0:T(8,128)(2,1)}, u32[]{:S(2)}) copy-start(bf16[512,4096]{1,0:T(8,128)(2,1)} %get-tuple-element.17.normed_ref) | copy-start | bytes 12582916
  33.0 2.2 %copy-start.4 = (bf16[512,4096]{1,0:T(8,128)(2,1)S(1)}, bf16[512,4096]{1,0:T(8,128)(2,1)}, u32[]{:S(2)}) copy-start(bf16[512,4096]{1,0:T(8,128)(2,1)} %get-tuple-element.20.normed_ref) | copy-start | bytes 12582916
  35.2 9.9 %copy-start = (bf16[9,256,128]{2,1,0:T(8,128)(2,1)S(1)}, bf16[9,256,128]{2,1,0:T(8,128)(2,1)}, u32[]{:S(2)}) copy-start(bf16[9,256,128]{2,1,0:T(8,128)(2,1)} %shard_map.93.rest_0_) | copy-start | bytes 1769476
  37.0 12.8 %collective-permute-start.6 = (bf16[544,128]{1,0:T(8,128)(2,1)S(1)}, bf16[544,128]{1,0:T(8,128)(2,1)S(1)}, u32[]{:S(2)}, u32[]{:S(2)}) collective-permute-start(bf16[544,128]{1,0:T(8,128)(2,1)S(1)} %shard_map.98.rest_4_), channel_id=1, source_target_pairs={{0,12},{4,8},{8,4},{12,0},{1,13},{5,9},{9,5},{13,1},{2,14},{6,10},... | collective-permute-start | bytes 417800 | tf_op jit(solution)/shard_map/ppermute | solution.py:528
  38.5 11.9 %collective-permute-start.5 = (bf16[544,128]{1,0:T(8,128)(2,1)S(1)}, bf16[544,128]{1,0:T(8,128)(2,1)S(1)}, u32[]{:S(2)}, u32[]{:S(2)}) collective-permute-start(bf16[544,128]{1,0:T(8,128)(2,1)S(1)} %shard_map.98.rest_4_), channel_id=1, source_target_pairs={{0,8},{4,12},{8,0},{12,4},{1,9},{5,13},{9,1},{13,5},{2,10},{6,14},... | collective-permute-start | bytes 417800 | tf_op jit(solution)/shard_map/ppermute | solution.py:528
  38.8 11.6 %collective-permute-start.4 = (bf16[544,128]{1,0:T(8,128)(2,1)S(1)}, bf16[544,128]{1,0:T(8,128)(2,1)S(1)}, u32[]{:S(2)}, u32[]{:S(2)}) collective-permute-start(bf16[544,128]{1,0:T(8,128)(2,1)S(1)} %shard_map.98.rest_4_), channel_id=1, source_target_pairs={{0,4},{4,0},{8,12},{12,8},{1,5},{5,1},{9,13},{13,9},{2,6},{6,2},{1... | collective-permute-start | bytes 417800 | tf_op jit(solution)/shard_map/ppermute | solution.py:528
  41.5 3.7 %collective-permute-start.1 = (f32[16,128]{1,0:T(8,128)S(1)}, f32[16,128]{1,0:T(8,128)S(1)}, u32[]{:S(2)}, u32[]{:S(2)}) collective-permute-start(f32[16,128]{1,0:T(8,128)S(1)} %get-tuple-element.24.own_ref), channel_id=1, source_target_pairs={{0,16},{2,18},{16,0},{18,2},{1,17},{3,19},{17,1},{19,3},{4,20},{6,... | collective-permute-start | bytes 24584 | tf_op jit(solution)/shard_map/ppermute | solution.py:528
  50.4 18.9 %copy-start.1 = (s32[512,1]{0,1:T(1,128)S(1)}, s32[512,1]{0,1:T(1,128)}, u32[]{:S(2)}) copy-start(s32[512,1]{0,1:T(1,128)} %param.11) | copy-start | bytes 6148
  50.4 18.9 %copy-start.3 = (s32[1,512]{1,0:T(1,128)S(1)}, s32[1,512]{1,0:T(1,128)}, u32[]{:S(2)}) copy-start(s32[1,512]{1,0:T(1,128)} %get-tuple-element.28.slot_ref) | copy-start | bytes 6148

commit v29 on v28

--- a/solution.py
+++ b/solution.py
@@ -663,11 +663,11 @@
         (own_values, listed, other, chosen, folds, payload, beside, across, diagonal, *queries),
         shape((groups, back, plan.share, plan.slots), BF16),
         [
-            pltpu.VMEM((query_rows + 16, moves), BF16),
-            pltpu.VMEM((16, moves), F32),
+            pltpu.VMEM((query_rows + 8, moves), BF16),
+            pltpu.VMEM((8, moves), F32),
             pltpu.VMEM((plan.slab, boards_here, plan.slots), F32),
-            pltpu.VMEM((query_rows + 16, plan.slab * plan.slots), F32),
-            pltpu.VMEM((query_rows + 16, plan.slab * plan.slots), F32),
+            pltpu.VMEM((query_rows + 8, plan.slab * plan.slots), F32),
+            pltpu.VMEM((query_rows + 8, plan.slab * plan.slots), F32),
         ],
         24,
     )

time: 70.7 us -> 70.6 us (level)
  no operation moved by 1% of the time
where the time goes in v29:
time: 70.6 us; the launch traced here: 70.2 us
  Pallas kernels  30.4 us (43%)
  starting transfers between devices  18.6 us (26%)
  blocking collectives  11.8 us (17%)
  waiting for transfers between devices  6.22 us (9%)
  local copies, waits for them, and re-layouts  2.51 us (4%)
    pallas_call x5, Pallas kernels, local_call(): pl.pallas_call(kernel, out_shape=outs, in_specs=[pl.BlockSpec(memory_spac...  18 us
    all_to_all x1, blocking collectives, per_device(): lax.all_to_all(parts.reshape(groups * back, plan.share, plan.slots), ('gr...  11.8 us
    ppermute x7, starting transfers between devices, swap(): return lax.ppermute(x, names, [(at, at ^ step) for at in range(size)])  11.3 us
    pallas_call x1, Pallas kernels, per_device(): pl.pallas_call(functools.partial(normalize, plan), out_shape=[*[shape((mo...  9.2 us
    all_to_all x1, starting transfers between devices, per_device(): lax.all_to_all(packed, ('line', 'pair'), split_axis=0, concat_axis=0, til...  7.26 us
    ppermute x7, waiting for transfers between devices, swap(): return lax.ppermute(x, names, [(at, at ^ step) for at in range(size)])  4.34 us
    unnamed x14, local copies, waits for them, and re-layouts  2.51 us
    pallas_call x1, Pallas kernels, per_device(): pl.pallas_call(functools.partial(pack_prefix, plan), out_shape=shape((boa...  2.22 us
  transfers between devices with their start and end apart: 8, of which 4 were waited for; matrix products, arithmetic and copies ran while one was open for 1% of the time, Pallas kernels for 28%

profile of v29, /device:TPU:0, one launch (start us, length us, event | category | flops | bytes accessed | tf_op | source)
XLA Modules:
  0.0 70.2 jit_solution(3970575664394470816)
XLA Ops:
  0.0 2.6 %shard_map.91.after_ref = bf16[8,400,128]{2,1,0:T(8,128)(2,1)} custom-call(s32[1]{0:T(128)} %bitcast.place_ref, bf16[512,1024]{1,0:T(8,128)(2,1)} %wq_hbm.1, bf16[512,256]{1,0:T(8,128)(2,1)} %wkv_hbm.1, bf16[8,128]{1,0:T(8,128)(2,1)} %bitcast.17, s32[1,512]{1,0:T(1,128)} %bitcast.13, s32[1,512]{1,0:T(1,128)} %bitcast.19), custom_call_target="tpu_custom_call" | custom-call | tf_op jit(solution)/shard_map/pallas_call | solution.py:510
  2.6 7.3 %all-to-all-start = ((bf16[8,400,128]{2,1,0:T(8,128)(2,1)}), bf16[8,400,128]{2,1,0:T(8,128)(2,1)S(1)}, u32[]{:S(2)}, u32[]{:S(2)}) async-start(bf16[8,400,128]{2,1,0:T(8,128)(2,1)} %shard_map.91.after_ref), calls=%async_computation | async-start | bytes 1638400 | tf_op jit(solution)/shard_map/all_to_all | solution.py:577
  9.9 2.2 %shard_map.93.rest_0_ = bf16[9,256,128]{2,1,0:T(8,128)(2,1)} custom-call(bf16[8,256,256]{2,1,0:T(8,128)(2,1)} %prefix_hbm.1, bf16[8,128]{1,0:T(8,128)(2,1)} %bitcast.18, bf16[8,400,128]{2,1,0:T(8,128)(2,1)} %shard_map.91.after_ref), custom_call_target="tpu_custom_call" | custom-call | tf_op jit(solution)/shard_map/pallas_call | solution.py:579
  12.1 1.6 %collective-permute-start = (bf16[9,256,128]{2,1,0:T(8,128)(2,1)}, bf16[9,256,128]{2,1,0:T(8,128)(2,1)S(1)}, u32[]{:S(2)}, u32[]{:S(2)}) collective-permute-start(bf16[9,256,128]{2,1,0:T(8,128)(2,1)} %shard_map.93.rest_0_), channel_id=1, source_target_pairs={{0,16},{2,18},{16,0},{18,2},{1,17},{3,19},{17,1},{19,3},{4,20},{6,... | collective-permute-start | bytes 1769480 | tf_op jit(solution)/shard_map/ppermute | solution.py:528
  13.7 2.0 %collective-permute-start.2 = (bf16[9,256,128]{2,1,0:T(8,128)(2,1)}, bf16[9,256,128]{2,1,0:T(8,128)(2,1)S(1)}, u32[]{:S(2)}, u32[]{:S(2)}) collective-permute-start(bf16[9,256,128]{2,1,0:T(8,128)(2,1)} %shard_map.93.rest_0_), channel_id=1, source_target_pairs={{0,2},{2,0},{16,18},{18,16},{1,3},{3,1},{17,19},{19,17},{4,6},{6,4... | collective-permute-start | bytes 1769480 | tf_op jit(solution)/shard_map/ppermute | solution.py:528
  15.7 0.6 pad_add_fusion.place_ref
  16.3 9.2 %shard_map.92 = (bf16[512,4096]{1,0:T(8,128)(2,1)}, bf16[512,4096]{1,0:T(8,128)(2,1)}, f32[8,128]{1,0:T(8,128)S(1)}, s32[1,512]{1,0:T(1,128)}) custom-call(s32[4]{0:T(128)} %pad_add_fusion.place_ref, bf16[1024,4096]{1,0:T(8,128)(2,1)} %table_hbm.1, bf16[32,128]{1,0:T(8,128)(2,1)} %bitcast.16, s32[1,512]{1,0:T(1,128)} %bitcast.14, ...), custom_call_target="tpu_custom_call" | custom-call | flops 4194304 | bytes 1048576 | tf_op jit(solution)/shard_map/pallas_call | solution.py:597
  25.5 1.6 %collective-permute-done.refs_0_ = bf16[9,256,128]{2,1,0:T(8,128)(2,1)S(1)} collective-permute-done((bf16[9,256,128]{2,1,0:T(8,128)(2,1)}, bf16[9,256,128]{2,1,0:T(8,128)(2,1)S(1)}, u32[]{:S(2)}, u32[]{:S(2)}) %collective-permute-start) | collective-permute-done | bytes 589856 | tf_op jit(solution)/shard_map/ppermute | solution.py:528
  27.2 1.7 %collective-permute-start.3 = (bf16[9,256,128]{2,1,0:T(8,128)(2,1)S(1)}, bf16[9,256,128]{2,1,0:T(8,128)(2,1)S(1)}, u32[]{:S(2)}, u32[]{:S(2)}) collective-permute-start(bf16[9,256,128]{2,1,0:T(8,128)(2,1)S(1)} %shard_map.94.after_ref.rest_2_), channel_id=1, source_target_pairs={{0,2},{2,0},{16,18},{18,16},{1,3},{3,1},{17,19},{19,17},{4,6},{6,4... | collective-permute-start | bytes 1769480 | tf_op jit(solution)/shard_map/ppermute | solution.py:528
  28.9 1.9 %all-to-all-done.w_ref = bf16[8,400,128]{2,1,0:T(8,128)(2,1)S(1)} async-done(((bf16[8,400,128]{2,1,0:T(8,128)(2,1)}), bf16[8,400,128]{2,1,0:T(8,128)(2,1)S(1)}, u32[]{:S(2)}, u32[]{:S(2)}) %all-to-all-start) | async-done | bytes 819232 | tf_op jit(solution)/shard_map/all_to_all | solution.py:577
  30.8 2.2 %copy-done.5 = bf16[512,4096]{1,0:T(8,128)(2,1)S(1)} copy-done((bf16[512,4096]{1,0:T(8,128)(2,1)S(1)}, bf16[512,4096]{1,0:T(8,128)(2,1)}, u32[]{:S(2)}) %copy-start.5) | copy-done | bytes 4194328
  33.0 1.9 %shard_map.95 = (bf16[544,128]{1,0:T(8,128)(2,1)S(1)}, f32[2,1024]{1,0:T(2,128)S(1)}, f32[16,128]{1,0:T(8,128)S(1)}, bf16[8,104,512]{2,1,0:T(8,128)(2,1)S(1)}) custom-call(s32[4]{0:T(128)S(1)} %copy-done.2, bf16[8,400,128]{2,1,0:T(8,128)(2,1)S(1)} %all-to-all-done.w_ref, bf16[512,4096]{1,0:T(8,128)(2,1)S(1)} %copy-done.5, f32[4,32,2]{2,1,0:T(8,128)S(1)} %copy-done.6, ...), custom_call_target="tpu_custom_call" | custom-call | flops 4294967296 | bytes 4194304 | tf_op jit(solution)/shard_map/pallas_call | solution.py:510
  34.9 0.3 copy-done.4
  35.2 1.8 %shard_map.96 = (bf16[544,128]{1,0:T(8,128)(2,1)S(1)}, f32[2,1024]{1,0:T(2,128)S(1)}) custom-call(s32[4]{0:T(128)S(1)} %copy-done.2, bf16[8,104,512]{2,1,0:T(8,128)(2,1)S(1)} %get-tuple-element.19.w_ref, bf16[512,4096]{1,0:T(8,128)(2,1)S(1)} %copy-done.4, f32[4,32,2]{2,1,0:T(8,128)S(1)} %copy-done.6, ...), custom_call_target="tpu_custom_call", output_to_operand_aliasing={{0}: (5, {}), {1}: (6, {})} | custom-call | flops 4294967296 | bytes 4194304 | tf_op jit(solution)/shard_map/pallas_call | solution.py:510
  37.0 1.5 %collective-permute-start.6 = (bf16[544,128]{1,0:T(8,128)(2,1)S(1)}, bf16[544,128]{1,0:T(8,128)(2,1)S(1)}, u32[]{:S(2)}, u32[]{:S(2)}) collective-permute-start(bf16[544,128]{1,0:T(8,128)(2,1)S(1)} %shard_map.98.rest_4_), channel_id=1, source_target_pairs={{0,12},{4,8},{8,4},{12,0},{1,13},{5,9},{9,5},{13,1},{2,14},{6,10},... | collective-permute-start | bytes 417800 | tf_op jit(solution)/shard_map/ppermute | solution.py:528
  38.5 0.3 collective-permute-start.5
  38.8 2.7 %collective-permute-start.4 = (bf16[544,128]{1,0:T(8,128)(2,1)S(1)}, bf16[544,128]{1,0:T(8,128)(2,1)S(1)}, u32[]{:S(2)}, u32[]{:S(2)}) collective-permute-start(bf16[544,128]{1,0:T(8,128)(2,1)S(1)} %shard_map.98.rest_4_), channel_id=1, source_target_pairs={{0,4},{4,0},{8,12},{12,8},{1,5},{5,1},{9,13},{13,9},{2,6},{6,2},{1... | collective-permute-start | bytes 417800 | tf_op jit(solution)/shard_map/ppermute | solution.py:528
  41.5 1.5 %collective-permute-start.1 = (f32[16,128]{1,0:T(8,128)S(1)}, f32[16,128]{1,0:T(8,128)S(1)}, u32[]{:S(2)}, u32[]{:S(2)}) collective-permute-start(f32[16,128]{1,0:T(8,128)S(1)} %get-tuple-element.24.own_ref), channel_id=1, source_target_pairs={{0,16},{2,18},{16,0},{18,2},{1,17},{3,19},{17,1},{19,3},{4,20},{6,... | collective-permute-start | bytes 24584 | tf_op jit(solution)/shard_map/ppermute | solution.py:528
  43.0 2.1 %collective-permute-done.1.other_ref = f32[16,128]{1,0:T(8,128)S(1)} collective-permute-done((f32[16,128]{1,0:T(8,128)S(1)}, f32[16,128]{1,0:T(8,128)S(1)}, u32[]{:S(2)}, u32[]{:S(2)}) %collective-permute-start.1) | collective-permute-done | bytes 8224 | tf_op jit(solution)/shard_map/ppermute | solution.py:528
  45.1 4.7 %shard_map.97 = (bf16[8,1024,512]{2,1,0:T(8,128)(2,1)S(1)}, f32[3,8,256,256]{3,2,1,0:T(8,128)S(1)}) custom-call(s32[4]{0:T(128)S(1)} %copy-done.2, f32[16,128]{1,0:T(8,128)S(1)} %get-tuple-element.24.own_ref, f32[16,128]{1,0:T(8,128)S(1)} %collective-permute-done.1.other_ref, bf16[9,256,128]{2,1,0:T(8,128)(2,1)S(1)} %copy-done, ...), custom_call_target="tpu_custom_call" | custom-call | flops 1000000000 | bytes 1000000 | tf_op jit(solution)/shard_map/pallas_call | solution.py:510
  49.8 0.6 collective-permute-done.5.rest_6_
  50.4 7.1 %shard_map.99 = bf16[2,16,16,128]{3,2,1,0:T(8,128)(2,1)S(1)} custom-call(s32[4]{0:T(128)S(1)} %copy-done.2, f32[2,1024]{1,0:T(2,128)S(1)} %get-tuple-element.23.vo_ref, f32[16,128]{1,0:T(8,128)S(1)} %get-tuple-element.24.own_ref, f32[16,128]{1,0:T(8,128)S(1)} %collective-permute-done.1.other_ref, bf16[8,1024,512]{2,1,0:T(8,128)(2,1)S(1)} %get-tuple-element.25.chosen_ref, ...), custom_call_target="tpu_custom_call" | custom-call | tf_op jit(solution)/shard_map/pallas_call | solution.py:510
  57.4 11.8 %all_to_all.10 = bf16[32,16,128]{2,1,0:T(8,128)(2,1)S(1)} all-to-all(bf16[32,16,128]{2,1,0:T(8,128)(2,1)S(1)} %bitcast.11), channel_id=1, replica_groups=mesh['groups'=2,'line'=4,'pair'=2,'tensor'=2] {'groups','line','pair','t..., dimensions={0} | all-to-all | bytes 262144 | tf_op jit(solution)/shard_map/all_to_all | solution.py:674
  69.2 1.0 %shard_map.100 = f32[1,512]{1,0:T(1,128)} custom-call(bf16[2,4,4,16,128]{4,3,2,1,0:T(8,128)(2,1)S(1)} %bitcast.12, s32[1,512]{1,0:T(1,128)S(1)} %bitcast.15, s32[1,512]{1,0:T(1,128)S(1)} %copy-done.3), custom_call_target="tpu_custom_call" | custom-call | tf_op jit(solution)/shard_map/pallas_call | solution.py:682
  (18 shorter events, 0.0 us)
Async XLA Ops:
  2.6 28.2 %all-to-all-start = ((bf16[8,400,128]{2,1,0:T(8,128)(2,1)}), bf16[8,400,128]{2,1,0:T(8,128)(2,1)S(1)}, u32[]{:S(2)}, u32[]{:S(2)}) async-start(bf16[8,400,128]{2,1,0:T(8,128)(2,1)} %shard_map.91.after_ref), calls=%async_computation | async-start | bytes 1638400 | tf_op jit(solution)/shard_map/all_to_all | solution.py:577
  9.9 20.9 %copy-start.6 = (f32[4,32,2]{2,1,0:T(8,128)S(1)}, f32[4,32,2]{2,1,0:T(8,128)}, u32[]{:S(2)}) copy-start(f32[4,32,2]{2,1,0:T(8,128)} %constant.17.clone.turn_ref) | copy-start | bytes 3076
  12.1 15.1 %collective-permute-start = (bf16[9,256,128]{2,1,0:T(8,128)(2,1)}, bf16[9,256,128]{2,1,0:T(8,128)(2,1)S(1)}, u32[]{:S(2)}, u32[]{:S(2)}) collective-permute-start(bf16[9,256,128]{2,1,0:T(8,128)(2,1)} %shard_map.93.rest_0_), channel_id=1, source_target_pairs={{0,16},{2,18},{16,0},{18,2},{1,17},{3,19},{17,1},{19,3},{4,20},{6,... | collective-permute-start | bytes 1769480 | tf_op jit(solution)/shard_map/ppermute | solution.py:528
  13.7 23.3 %collective-permute-start.2 = (bf16[9,256,128]{2,1,0:T(8,128)(2,1)}, bf16[9,256,128]{2,1,0:T(8,128)(2,1)S(1)}, u32[]{:S(2)}, u32[]{:S(2)}) collective-permute-start(bf16[9,256,128]{2,1,0:T(8,128)(2,1)} %shard_map.93.rest_0_), channel_id=1, source_target_pairs={{0,2},{2,0},{16,18},{18,16},{1,3},{3,1},{17,19},{19,17},{4,6},{6,4... | collective-permute-start | bytes 1769480 | tf_op jit(solution)/shard_map/ppermute | solution.py:528
  16.3 14.5 %copy-start.2 = (s32[4]{0:T(128)S(1)}, s32[4]{0:T(128)}, u32[]{:S(2)}) copy-start(s32[4]{0:T(128)} %pad_add_fusion.place_ref) | copy-start | bytes 52
  27.2 22.6 %collective-permute-start.3 = (bf16[9,256,128]{2,1,0:T(8,128)(2,1)S(1)}, bf16[9,256,128]{2,1,0:T(8,128)(2,1)S(1)}, u32[]{:S(2)}, u32[]{:S(2)}) collective-permute-start(bf16[9,256,128]{2,1,0:T(8,128)(2,1)S(1)} %shard_map.94.after_ref.rest_2_), channel_id=1, source_target_pairs={{0,2},{2,0},{16,18},{18,16},{1,3},{3,1},{17,19},{19,17},{4,6},{6,4... | collective-permute-start | bytes 1769480 | tf_op jit(solution)/shard_map/ppermute | solution.py:528
  30.8 2.2 %copy-start.5 = (bf16[512,4096]{1,0:T(8,128)(2,1)S(1)}, bf16[512,4096]{1,0:T(8,128)(2,1)}, u32[]{:S(2)}) copy-start(bf16[512,4096]{1,0:T(8,128)(2,1)} %get-tuple-element.17.normed_ref) | copy-start | bytes 12582916
  33.0 2.2 %copy-start.4 = (bf16[512,4096]{1,0:T(8,128)(2,1)S(1)}, bf16[512,4096]{1,0:T(8,128)(2,1)}, u32[]{:S(2)}) copy-start(bf16[512,4096]{1,0:T(8,128)(2,1)} %get-tuple-element.20.normed_ref) | copy-start | bytes 12582916
  35.2 9.9 %copy-start = (bf16[9,256,128]{2,1,0:T(8,128)(2,1)S(1)}, bf16[9,256,128]{2,1,0:T(8,128)(2,1)}, u32[]{:S(2)}) copy-start(bf16[9,256,128]{2,1,0:T(8,128)(2,1)} %shard_map.93.rest_0_) | copy-start | bytes 1769476
  37.0 12.8 %collective-permute-start.6 = (bf16[544,128]{1,0:T(8,128)(2,1)S(1)}, bf16[544,128]{1,0:T(8,128)(2,1)S(1)}, u32[]{:S(2)}, u32[]{:S(2)}) collective-permute-start(bf16[544,128]{1,0:T(8,128)(2,1)S(1)} %shard_map.98.rest_4_), channel_id=1, source_target_pairs={{0,12},{4,8},{8,4},{12,0},{1,13},{5,9},{9,5},{13,1},{2,14},{6,10},... | collective-permute-start | bytes 417800 | tf_op jit(solution)/shard_map/ppermute | solution.py:528
  38.5 11.9 %collective-permute-start.5 = (bf16[544,128]{1,0:T(8,128)(2,1)S(1)}, bf16[544,128]{1,0:T(8,128)(2,1)S(1)}, u32[]{:S(2)}, u32[]{:S(2)}) collective-permute-start(bf16[544,128]{1,0:T(8,128)(2,1)S(1)} %shard_map.98.rest_4_), channel_id=1, source_target_pairs={{0,8},{4,12},{8,0},{12,4},{1,9},{5,13},{9,1},{13,5},{2,10},{6,14},... | collective-permute-start | bytes 417800 | tf_op jit(solution)/shard_map/ppermute | solution.py:528
  38.8 11.6 %collective-permute-start.4 = (bf16[544,128]{1,0:T(8,128)(2,1)S(1)}, bf16[544,128]{1,0:T(8,128)(2,1)S(1)}, u32[]{:S(2)}, u32[]{:S(2)}) collective-permute-start(bf16[544,128]{1,0:T(8,128)(2,1)S(1)} %shard_map.98.rest_4_), channel_id=1, source_target_pairs={{0,4},{4,0},{8,12},{12,8},{1,5},{5,1},{9,13},{13,9},{2,6},{6,2},{1... | collective-permute-start | bytes 417800 | tf_op jit(solution)/shard_map/ppermute | solution.py:528
  41.5 3.7 %collective-permute-start.1 = (f32[16,128]{1,0:T(8,128)S(1)}, f32[16,128]{1,0:T(8,128)S(1)}, u32[]{:S(2)}, u32[]{:S(2)}) collective-permute-start(f32[16,128]{1,0:T(8,128)S(1)} %get-tuple-element.24.own_ref), channel_id=1, source_target_pairs={{0,16},{2,18},{16,0},{18,2},{1,17},{3,19},{17,1},{19,3},{4,20},{6,... | collective-permute-start | bytes 24584 | tf_op jit(solution)/shard_map/ppermute | solution.py:528
  50.4 18.9 %copy-start.1 = (s32[512,1]{0,1:T(1,128)S(1)}, s32[512,1]{0,1:T(1,128)}, u32[]{:S(2)}) copy-start(s32[512,1]{0,1:T(1,128)} %param.11) | copy-start | bytes 6148
  50.4 18.9 %copy-start.3 = (s32[1,512]{1,0:T(1,128)S(1)}, s32[1,512]{1,0:T(1,128)}, u32[]{:S(2)}) copy-start(s32[1,512]{1,0:T(1,128)} %get-tuple-element.28.slot_ref) | copy-start | bytes 6148
